TPU v7x, 32 devices: a whole 2x2x4 slice. The times are simulated.
32 devices in a mesh: grp: 4 (over y, x), seq: 8 (over z, core).
Axes of the slice: x: 2, y: 2, z: 4, core: 2. Of those that a mesh axis runs over, the one named last changes fastest.
Arguments:
- inputs: bfloat16 [8192, 2560], P(('grp', 'seq')), may hold values from -0.078125 to 0.078125
- out_grad: bfloat16 [8192, 2560], P(('grp', 'seq')), may hold values from -6 to 6
- input_map: bfloat16 [8192, 128], P(('grp', 'seq')), may hold values from -0.09375 to 0.09375
- output_map: bfloat16 [8192, 128], P(('grp', 'seq')), may hold values from -0.09375 to 0.09375
- log_decay: float32 [40, 8192], P(None, ('grp', 'seq')), may hold values from -1 to 0, as said below
Outputs:
- grad_inputs: bfloat16 [8192, 2560], P(('grp', 'seq'))
- grad_input_map: bfloat16 [8192, 128], P(('grp', 'seq'))
- grad_output_map: bfloat16 [8192, 128], P(('grp', 'seq'))
- grad_decay: float32 [40, 8192], P(None, ('grp', 'seq'))
Inputs may be any that keep to these rules, and one draw needn't show every extreme that they name: log_decay is negative everywhere.
All inputs are finite; a program needn't handle non-finite values.
Results may differ from a plain program's by a relative error of at most 0.0081.
Values sent between devices are 32-bit elements; how exact they have to be, the bound alone decides.
No kernel may reach another device: no remote copies, remote signals or barrier semaphores. Data moves between devices by JAX's collectives and lax.ppermute only.
A program may use at most 192 MiB of HBM per device.

v0:
```python
import jax
import jax.numpy as jnp
from jax import lax
from jax.sharding import PartitionSpec as P

STATE = 128
STRETCH = 256


def prefix_2(value, axis, join, neutral, backward):
    count, mine = (lax.axis_size(axis), lax.axis_index(axis))
    pieces = jax.tree.map(lambda part: lax.all_gather(part, axis), value)
    if backward:
        pieces = jax.tree.map(lambda part: part[::-1], pieces)
        mine = count - 1 - mine
    total = jax.tree.map(
        lambda part, zero: jnp.full_like(part, 0) + jnp.asarray(zero, part.dtype), value, neutral
    )

    def lap(position, total):
        longer = join(total, jax.tree.map(lambda part: part[position], pieces))
        return jax.tree.map(lambda new, old: jnp.where(position < mine, new, old), longer, total)

    return lax.fori_loop(0, count - 1, lap, total)


def weigh(values, grads, rates):
    cumulative = jnp.cumsum(rates, axis=1)
    block_decay = cumulative[:, -1]
    decay_tail = jnp.exp(block_decay[:, None] - cumulative)
    decay_lead = jnp.exp(cumulative)
    inputs_tail = (values.astype(jnp.float32) * decay_tail.T[:, :, None]).astype(jnp.bfloat16)
    grads_lead = (grads.astype(jnp.float32) * decay_lead.T[:, :, None]).astype(jnp.bfloat16)
    return (cumulative, block_decay, decay_tail, decay_lead, inputs_tail, grads_lead)


def block_summary(values, grads, write_map, read_map, rates):
    cumulative, block_decay, decay_tail, decay_lead, inputs_tail, grads_lead = weigh(
        values, grads, rates
    )
    own_state = jnp.einsum(
        "khp,kn->hpn", inputs_tail, write_map, preferred_element_type=jnp.float32
    )
    own_back = jnp.einsum("khp,kn->hpn", grads_lead, read_map, preferred_element_type=jnp.float32)
    return (block_decay, own_state, own_back)


def block_intra(values, grads, write_map, read_map, rates):
    head_count = rates.shape[0]
    length = rates.shape[1]
    head_size = values.shape[2]
    group_size = 8
    group_count = head_count // group_size
    cumulative = jnp.cumsum(rates, axis=1)
    row_ids = lax.broadcasted_iota(jnp.int32, (length, length), 0)
    col_ids = lax.broadcasted_iota(jnp.int32, (length, length), 1)
    causal = (row_ids >= col_ids)[None]
    scores = jnp.dot(read_map, write_map.T, preferred_element_type=jnp.float32)
    grouped_values = values.reshape(length, group_count, group_size, head_size).transpose(
        1, 0, 2, 3
    )
    grouped_grads = grads.reshape(length, group_count, group_size, head_size).transpose(1, 0, 2, 3)
    grouped_cumul = cumulative.reshape(group_count, group_size, length)

    def one_group(carry, item):
        group_values, group_grads, group_cumul = item
        log_gap = group_cumul[:, :, None] - group_cumul[:, None, :]
        decay = jnp.where(causal, jnp.exp(jnp.where(causal, log_gap, 0.0)), 0.0)
        mixing = (scores[None] * decay).astype(jnp.bfloat16)
        y_part = jnp.einsum(
            "hij,jhp->ihp", mixing, group_values, preferred_element_type=jnp.float32
        )
        dx_part = jnp.einsum(
            "hij,ihp->jhp", mixing, group_grads, preferred_element_type=jnp.float32
        )
        pair_dots = jnp.einsum(
            "ihp,jhp->hij", group_values, group_grads, preferred_element_type=jnp.float32
        )
        carry = carry + jnp.sum(pair_dots * jnp.swapaxes(decay, 1, 2), axis=0)
        return (carry, (y_part, dx_part))

    summed, (y_parts, dx_parts) = lax.scan(
        one_group,
        jnp.zeros((length, length), jnp.float32),
        (grouped_values, grouped_grads, grouped_cumul),
    )
    y_intra = y_parts.transpose(1, 0, 2, 3).reshape(length, head_count, head_size)
    dx_intra = dx_parts.transpose(1, 0, 2, 3).reshape(length, head_count, head_size)
    head_sum = summed.astype(jnp.bfloat16)
    db_intra = jnp.dot(head_sum, read_map, preferred_element_type=jnp.float32)
    dc_intra = jnp.dot(head_sum.T, write_map, preferred_element_type=jnp.float32)
    return (y_intra, dx_intra, db_intra, dc_intra)


def block_final(
    values,
    grads,
    write_map,
    read_map,
    rates,
    y_intra,
    dx_intra,
    db_intra,
    dc_intra,
    state_in,
    back_in,
):
    cumulative, block_decay, decay_tail, decay_lead, inputs_tail, grads_lead = weigh(
        values, grads, rates
    )
    state_half = state_in.astype(jnp.bfloat16)
    back_half = back_in.astype(jnp.bfloat16)
    outputs_full = (
        y_intra
        + jnp.einsum("kn,hpn->khp", read_map, state_half, preferred_element_type=jnp.float32)
        * decay_lead.T[:, :, None]
    )
    grad_full = (
        dx_intra
        + jnp.einsum("kn,hpn->khp", write_map, back_half, preferred_element_type=jnp.float32)
        * decay_tail.T[:, :, None]
    )
    grad_write = db_intra + jnp.einsum(
        "khp,hpn->kn", inputs_tail, back_half, preferred_element_type=jnp.float32
    )
    grad_read = dc_intra + jnp.einsum(
        "khp,hpn->kn", grads_lead, state_half, preferred_element_type=jnp.float32
    )
    change = jnp.sum(
        grads.astype(jnp.float32) * outputs_full - values.astype(jnp.float32) * grad_full, axis=2
    ).T
    return (
        grad_full.astype(jnp.bfloat16),
        grad_write.astype(jnp.bfloat16),
        grad_read.astype(jnp.bfloat16),
        change,
    )


def apply_first(first_part, second_part):
    return (
        first_part[0] * second_part[0],
        second_part[0][:, None, None] * first_part[1] + second_part[1],
    )


def per_device(inputs, out_grad, input_map, output_map, log_decay):
    head_count = log_decay.shape[0]
    tokens = inputs.shape[0]
    head_size = inputs.shape[1] // head_count
    blocks = tokens // STRETCH
    parts = (
        inputs.reshape(blocks, STRETCH, head_count, head_size),
        out_grad.reshape(blocks, STRETCH, head_count, head_size),
        input_map.reshape(blocks, STRETCH, STATE),
        output_map.reshape(blocks, STRETCH, STATE),
        log_decay.reshape(head_count, blocks, STRETCH).transpose(1, 0, 2),
    )
    decays, own_states, own_backs = lax.map(lambda pieces: block_summary(*pieces), parts)
    empty_state = jnp.zeros((head_count, head_size, STATE), jnp.float32)

    def forward(running, item):
        block_decay, own_state = item
        return (jnp.exp(block_decay)[:, None, None] * running + own_state, running)

    def backward(running, item):
        block_decay, own_back = item
        return (jnp.exp(block_decay)[:, None, None] * running + own_back, running)

    shard_state, shard_local_states = lax.scan(forward, empty_state, (decays, own_states))
    shard_back, local_backs = lax.scan(backward, empty_state, (decays, own_backs), reverse=True)
    shard_log = jnp.sum(decays, axis=0)
    shard_decay = jnp.exp(shard_log)
    identity = (jnp.ones((head_count,), jnp.float32), empty_state)
    intra = lax.map(lambda pieces: block_intra(*pieces), parts)
    prefix = prefix_2((shard_decay, shard_state), "seq", apply_first, identity, False)
    trailing_sum = prefix_2((shard_decay, shard_back), "seq", apply_first, identity, True)
    whole_up = apply_first(prefix, (shard_decay, shard_state))
    whole_down = apply_first(trailing_sum, (shard_decay, shard_back))
    position = lax.axis_index("seq")
    mask_last = (position == lax.axis_size("seq") - 1).astype(jnp.float32)
    mask_first = (position == 0).astype(jnp.float32)
    group_totals = lax.psum(
        (
            whole_up[0] * mask_last,
            whole_up[1] * mask_last,
            whole_down[0] * mask_first,
            whole_down[1] * mask_first,
        ),
        "seq",
    )
    outer_up = prefix_2((group_totals[0], group_totals[1]), "grp", apply_first, identity, False)
    outer_down = prefix_2((group_totals[2], group_totals[3]), "grp", apply_first, identity, True)
    incoming = apply_first(outer_up, prefix)[1]
    outgoing = apply_first(outer_down, trailing_sum)[1]
    running_sum = jnp.cumsum(decays, axis=0)
    before = running_sum - decays
    after = shard_log[None, :] - running_sum
    states_in = shard_local_states + jnp.exp(before)[:, :, None, None] * incoming[None]
    backs_in = local_backs + jnp.exp(after)[:, :, None, None] * outgoing[None]

    def finish(item):
        pieces, intra_part, state_in, back_in = item
        return block_final(*pieces, *intra_part, state_in, back_in)

    grad_values, grad_write, grad_read, change = lax.map(
        finish, (parts, intra, states_in, backs_in)
    )
    change = change.transpose(1, 0, 2).reshape(head_count, tokens)
    suffix_local = jnp.cumsum(change[:, ::-1], axis=1)[:, ::-1]
    shard_total = suffix_local[:, 0]
    every_total = lax.all_gather(shard_total[None, :], ("grp", "seq"), axis=0, tiled=True)
    flat_position = lax.axis_index(("grp", "seq"))
    shard_ranks = lax.broadcasted_iota(jnp.int32, every_total.shape, 0)
    later_sum = jnp.sum(jnp.where(shard_ranks > flat_position, every_total, 0.0), axis=0)
    grad_decay = suffix_local + later_sum[:, None]
    return (
        grad_values.reshape(tokens, head_count * head_size),
        grad_write.reshape(tokens, STATE),
        grad_read.reshape(tokens, STATE),
        grad_decay,
    )


def solution(mesh):
    in_specs = (
        P(("grp", "seq"), None),
        P(("grp", "seq"), None),
        P(("grp", "seq"), None),
        P(("grp", "seq"), None),
        P(None, ("grp", "seq")),
    )
    out_specs = (
        P(("grp", "seq"), None),
        P(("grp", "seq"), None),
        P(("grp", "seq"), None),
        P(None, ("grp", "seq")),
    )
    return jax.shard_map(
        per_device, mesh=mesh, in_specs=in_specs, out_specs=out_specs, check_vma=False
    )
```

profile of v0, /device:TPU:0, one launch (start us, length us, event | category | flops | bytes accessed | tf_op | source)
XLA Modules:
  0.0 494.9 jit_solution(15135910703071199895)
XLA Ops:
  9.2 1.6 copy.57
  10.9 1.6 convolution_add_fusion.1
  12.5 1.2 copy-done.10
  14.4 1.6 convolution_add_fusion
  18.1 18.7 %all-reduce = f32[320]{0:T(512)S(1)} all-reduce(f32[320]{0:T(512)S(1)} %dynamic-update-slice), channel_id=2, replica_groups=mesh['grp'=4,'seq'=8] {'seq'}, use_global_device_ids=true, to_apply=%add | all-reduce | flops 320 | bytes 2560
  36.9 77.9 %all-gather.15.cloned.1.call-done = f32[320,64,128]{2,1,0:T(8,128)} async-done(((f32[40,64,128]{2,1,0:T(8,128)}), f32[320,64,128]{2,1,0:T(8,128)}) %all-gather.15.cloned.1.call-update) | async-done | bytes 10485776 | tf_op jit(solution)/shard_map/all_gather | solution.py:12
  114.9 11.3 %rev.17 = f32[8,40,64,128]{3,2,1,0:T(8,128)} reverse(f32[8,40,64,128]{3,2,1,0:T(8,128)} %bitcast.205), dimensions={0} | reverse | bytes 20971520 | tf_op jit(solution)/shard_map/rev | solution.py:14
  126.2 11.8 %while.59 = (s32[]{:T(128)}, f32[40]{0:T(128)S(1)}, f32[40,64,128]{2,1,0:T(8,128)S(1)}, s32[]{:T(128)}, f32[8,40]{1,0:T(8,128)S(1)}, /*index=5*/f32[8,40,64,128]{3,2,1,0:T(8,128)}, s32[]{:T(128)}, s32[]{:T(128)}) while((s32[]{:T(128)}, f32[40]{0:T(128)S(1)}, f32[40,64,128]{2,1,0:T(8,128)S(1)}, s32[]{:T(128)}, ...), condition=%wide.region_6.7_spmd.clone, body=%wide.region_5.6_spmd.clone.sunk | while | flops 1310844 | bytes 3933075 | solution.py:24
  126.2 1.7 fusion.69
  127.9 1.6 fusion.69
  129.6 1.6 fusion.69
  131.2 1.7 fusion.69
  132.9 1.6 fusion.69
  134.6 1.6 fusion.69
  136.3 1.7 fusion.69
  138.0 77.0 %all-gather.17.cloned.1.call-done = f32[320,64,128]{2,1,0:T(8,128)} async-done(((f32[40,64,128]{2,1,0:T(8,128)}), f32[320,64,128]{2,1,0:T(8,128)}) %all-gather.17.cloned.1.call-update) | async-done | bytes 10485776 | tf_op jit(solution)/shard_map/all_gather | solution.py:12
  214.9 11.6 %while.61 = (s32[]{:T(128)}, f32[40]{0:T(128)S(1)}, f32[40,64,128]{2,1,0:T(8,128)S(1)}, s32[]{:T(128)}, f32[8,40]{1,0:T(8,128)S(1)}, /*index=5*/f32[8,40,64,128]{3,2,1,0:T(8,128)}, s32[]{:T(128)}, s32[]{:T(128)}) while((s32[]{:T(128)}, f32[40]{0:T(128)S(1)}, f32[40,64,128]{2,1,0:T(8,128)S(1)}, s32[]{:T(128)}, ...), condition=%wide.region_12.13_spmd.clone, body=%wide.region_11.12_spmd.clone.sunk | while | flops 1310844 | bytes 3933075 | solution.py:24
  214.9 1.6 fusion.71
  216.6 1.6 fusion.71
  218.3 1.6 fusion.71
  219.9 1.6 fusion.71
  221.6 1.6 fusion.71
  223.3 1.6 fusion.71
  224.9 1.6 fusion.71
  226.6 3.6 multiply_bitcast_fusion
  230.2 67.9 %all-reduce.6.cloned.1.call-done = (f32[1,40,64,128]{3,2,1,0:T(8,128)}, f32[1,40,64,128]{3,2,1,0:T(8,128)}) async-done(((f32[1,40,64,128]{3,2,1,0:T(8,128)}, f32[1,40,64,128]{3,2,1,0:T(8,128)}), (f32[1,40,64,128]{3,2,1,0:T(8,128)}, f32[1,40,64,128]{3,2,1,0:T(8,128)})) %all-reduce.6.cloned.1.call-update) | async-done | bytes 2621456 | tf_op jit(solution)/shard_map/psum | solution.py:183
  298.2 3.7 fusion.26
  302.1 0.9 fusion.41
  303.0 36.5 %while.63 = (s32[]{:T(128)}, f32[256,256]{1,0:T(8,128)S(1)}, f32[5,256,8,64]{1,3,2,0:T(8,128)}, f32[5,256,8,64]{1,3,2,0:T(8,128)}, bf16[5,256,8,64]{1,3,2,0:T(8,...) while((s32[]{:T(128)}, f32[256,256]{1,0:T(8,128)S(1)}, ...), condition=%wide.region_4.5_spmd.clone.clone, body=%wide.region_2.4_spmd.clone.clone.sunk | while | flops 209387520 | bytes 5246095 | solution.py:82
  303.0 1.8 multiply_reduce_fusion.2
  305.2 2.7 fusion.79
  307.8 2.5 fusion.80
  310.4 1.8 multiply_reduce_fusion.2
  312.6 2.6 fusion.79
  315.2 2.5 fusion.80
  317.7 1.8 multiply_reduce_fusion.2
  319.8 2.6 fusion.79
  322.4 2.5 fusion.80
  324.9 1.8 multiply_reduce_fusion.2
  327.0 2.6 fusion.79
  329.7 2.5 fusion.80
  332.2 1.8 multiply_reduce_fusion.2
  334.4 2.6 fusion.79
  337.0 2.5 fusion.80
  339.5 14.6 %all-reduce.2 = (f32[1,40]{1,0:T(1,128)S(1)}, f32[1,40]{1,0:T(1,128)S(1)}) all-reduce(f32[1,40]{1,0:T(1,128)S(1)} %get-tuple-element.841, f32[1,40]{1,0:T(1,128)S(1)} %get-tuple-element.840), channel_id=1, replica_groups=mesh['grp'=4,'seq'=8] {'seq'}, use_global_device_ids=true, to_apply=%region_7.8 | all-reduce | flops 80 | bytes 640 | tf_op jit(solution)/shard_map/psum | solution.py:183
  354.1 7.9 %all-gather.4 = f32[4,1,40]{2,1,0:T(1,128)S(1)} all-gather(f32[1,1,40]{2,1,0:T(1,128)S(1)} %bitcast.214), channel_id=1, replica_groups=mesh['grp'=4,'seq'=8] {'grp'}, dimensions={0}, use_global_device_ids=true | all-gather | bytes 800 | tf_op jit(solution)/shard_map/all_gather | solution.py:12
  362.0 7.9 %all-gather.5 = f32[4,1,40]{2,1,0:T(1,128)S(1)} all-gather(f32[1,1,40]{2,1,0:T(1,128)S(1)} %bitcast.213), channel_id=1, replica_groups=mesh['grp'=4,'seq'=8] {'grp'}, dimensions={0}, use_global_device_ids=true | all-gather | bytes 800 | tf_op jit(solution)/shard_map/all_gather | solution.py:12
  369.9 6.3 %rev.19 = f32[4,40,64,128]{3,2,1,0:T(8,128)} reverse(f32[4,40,64,128]{3,2,1,0:T(8,128)} %all-gather.11.cloned.1.call-done), dimensions={0} | reverse | bytes 10485760 | tf_op jit(solution)/shard_map/rev | solution.py:14
  376.2 8.9 %while.60 = (s32[]{:T(128)}, f32[40,64,128]{2,1,0:T(8,128)}, s32[]{:T(128)}, f32[4,40]{1,0:T(4,128)S(1)}, f32[4,40,64,128]{3,2,1,0:T(8,128)}, /*index=5*/s32[]{:T(128)}, s32[]{:T(128)}) while((s32[]{:T(128)}, f32[40,64,128]{2,1,0:T(8,128)}, s32[]{:T(128)}, f32[4,40]{1,0:T(4,128)S(1)}, f32[4,40,64,128]{3,2,1,0:T(8,128)}, ...), condition=%wide.region_10.11_spmd.clone, body=%wide.region_9.10_spmd.clone.sunk | while | flops 1310724 | bytes 3932745 | solution.py:24
  376.2 2.7 fusion.70
  378.9 3.1 fusion.70
  382.0 3.1 fusion.70
  385.0 38.4 %all-gather.13.cloned.1.call-done = f32[4,40,64,128]{3,2,1,0:T(8,128)} async-done(((f32[1,40,64,128]{3,2,1,0:T(8,128)}), f32[4,40,64,128]{3,2,1,0:T(8,128)}) %all-gather.13.cloned.1.call-update) | async-done | bytes 5242896 | tf_op jit(solution)/shard_map/all_gather | solution.py:12
  423.5 8.6 %while.62 = (s32[]{:T(128)}, f32[40,64,128]{2,1,0:T(8,128)}, s32[]{:T(128)}, f32[4,40]{1,0:T(4,128)S(1)}, f32[4,40,64,128]{3,2,1,0:T(8,128)}, /*index=5*/s32[]{:T(128)}, s32[]{:T(128)}) while((s32[]{:T(128)}, f32[40,64,128]{2,1,0:T(8,128)}, s32[]{:T(128)}, f32[4,40]{1,0:T(4,128)S(1)}, f32[4,40,64,128]{3,2,1,0:T(8,128)}, ...), condition=%wide.region_16.17_spmd.clone, body=%wide.region_15.16_spmd.clone.sunk | while | flops 1310724 | bytes 3932745 | solution.py:24
  423.5 2.6 fusion.72
  426.1 3.0 fusion.72
  429.1 3.0 fusion.72
  432.1 2.2 multiply_convert_fusion.7
  434.3 3.8 fusion.38
  438.1 1.1 fusion.25
  440.8 39.4 %all-reduce.1 = f32[1280]{0:T(1024)S(1)} all-reduce(f32[1280]{0:T(1024)S(1)} %dynamic-update-slice.1), channel_id=5, replica_groups=mesh['grp'=4,'seq'=8] {'grp','seq'}, use_global_device_ids=true, to_apply=%add.1 | all-reduce | flops 1280 | bytes 10240
  480.3 2.0 convolution_bitcast_fusion.2
  482.4 2.0 convolution_bitcast_fusion.3
  486.0 1.6 copy.65
  (137 shorter events, 10.4 us)
Async XLA Ops:
  7.2 7.2 %copy-start = (bf16[256,128]{1,0:T(8,128)(2,1)S(1)}, bf16[256,128]{1,0:T(8,128)(2,1)}, u32[]{:S(2)}) copy-start(bf16[256,128]{1,0:T(8,128)(2,1)} %param.17) | copy-start | bytes 196612
  7.2 107.7 %all-gather.15.cloned.1.call-start = ((), (), s32[]{:S(2)}) async-start(), calls=%async_computation.2 | async-start | bytes 11796480 | tf_op jit(solution)/shard_map/all_gather | solution.py:12
  9.2 1.7 copy-start.11
  10.8 1.6 copy-start.1
  12.4 1.3 copy-start.10
  12.5 202.5 %all-gather.17.cloned.1.call-start = ((), (), s32[]{:S(2)}) async-start(), calls=%async_computation.3 | async-start | bytes 11796480 | tf_op jit(solution)/shard_map/all_gather | solution.py:12
  14.4 1.6 copy-start.3
  16.0 0.7 copy-start.13
  16.0 282.0 %all-reduce.6.cloned.1.call-start = ((), (), s32[]{:S(2)}) async-start(), calls=%async_computation.4 | async-start | bytes 5242880 | tf_op jit(solution)/shard_map/psum | solution.py:183
  230.1 139.7 %all-gather.11.cloned.1.call-start = ((), (), s32[]{:S(2)}) async-start(), calls=%async_computation | async-start | bytes 6553600 | tf_op jit(solution)/shard_map/all_gather | solution.py:12
  298.1 125.4 %all-gather.13.cloned.1.call-start = ((), (), s32[]{:S(2)}) async-start(), calls=%async_computation.1 | async-start | bytes 6553600 | tf_op jit(solution)/shard_map/all_gather | solution.py:12
  305.2 2.7 copy-start.12
  312.5 2.6 copy-start.12
  319.8 2.6 copy-start.12
  327.0 2.6 copy-start.12
  334.4 2.6 copy-start.12
  434.2 3.9 copy-start.8
  434.3 3.9 copy-start.6
  434.3 3.8 copy-start.2
  434.3 3.8 copy-start.4
  434.3 3.8 copy-start.7
  440.2 42.1 %copy-start.9 = (bf16[40,64,128]{2,1,0:T(8,128)(2,1)S(1)}, bf16[40,64,128]{2,1,0:T(8,128)(2,1)}, u32[]{:S(2)}) copy-start(bf16[40,64,128]{2,1,0:T(8,128)(2,1)} %copy-done.8) | copy-start | bytes 1966084
  482.4 3.6 copy-start.5
Sparse Core Ops, SparseCore 0:
  12.6 102.2 all-gather.14
  117.1 97.8 all-gather.16
  230.3 67.7 all-reduce.5
  299.7 60.4 all-gather.10
  361.9 61.5 all-gather.12
where the time goes:
time: 497 us; the launch traced here: 495 us
  waiting for transfers between devices  261 us (53%)
  blocking collectives  88.5 us (18%)
  other arithmetic  53 us (11%)
  matrix products  49.3 us (10%)
  local copies, waits for them, and re-layouts  27.3 us (5%)
  between operations  14.8 us (3%)
    all_gather x4, waiting for transfers between devices, prefix_2(): pieces = jax.tree.map(lambda part: lax.all_gather(part, axis), value)  193 us
    psum x1, waiting for transfers between devices, per_device(): lax.psum((whole_up[0] * mask_last, whole_up[1] * mask_last, whole_down[0]...  67.9 us
    unnamed x2, blocking collectives  58.1 us
    select_n x34, other arithmetic, lap(): jnp.where(position < mine, new, old)  40.5 us
    rev x4, local copies, waits for them, and re-layouts, prefix_2(): pieces = jax.tree.map(lambda part: part[::-1], pieces)  17.6 us
    all_gather x2, blocking collectives, prefix_2(): pieces = jax.tree.map(lambda part: lax.all_gather(part, axis), value)  15.7 us
    psum x1, blocking collectives, per_device(): lax.psum((whole_up[0] * mask_last, whole_up[1] * mask_last, whole_down[0]...  14.6 us
    dot_general x5, matrix products, one_group(): jnp.einsum('hij,jhp->ihp', mixing, group_values, preferred_element_type=j...  13.1 us
  transfers between devices with their start and end apart: 5, of which 4 were waited for; matrix products, arithmetic and copies ran while one was open for 17% of the time, Pallas kernels for 0%

commit v1 on v0

v1 whole, which is shorter than its diff:
```python
import jax
import jax.numpy as jnp
from jax import lax
from jax.experimental import pallas as pl
from jax.experimental.pallas import tpu as pltpu
from jax.sharding import PartitionSpec as P

STATE = 128
STRETCH = 256
LANES = 512
F32 = jnp.float32
BF16 = jnp.bfloat16
HIGHEST = lax.Precision.HIGHEST


def dot(left, right, left_dim, right_dim, precision=None):
    return lax.dot_general(
        left,
        right,
        (((left_dim,), (right_dim,)), ((), ())),
        precision=precision,
        preferred_element_type=F32,
    )


def iota(shape, dim):
    return lax.broadcasted_iota(jnp.int32, shape, dim)


def lower(length):
    return (iota((length, length), 0) >= iota((length, length), 1)).astype(F32)


def thrice(rates):
    heads, length = rates.shape
    spare = jnp.zeros((STATE - 3 * heads, length), F32)
    return jnp.concatenate([rates, rates, rates, spare], axis=0)


def three_terms(value, heads):
    lane = iota(value.shape, 1)
    first = value.astype(BF16)
    rest = value - first.astype(F32)
    second = rest.astype(BF16)
    third = (rest - second.astype(F32)).astype(BF16)
    return jnp.where(lane < heads, first, jnp.where(lane < 2 * heads, second, third))


def spreader(chunk, heads, head_size, lanes):
    row = iota((STATE, lanes), 0)
    head = (iota((STATE, lanes), 1) + chunk * lanes) // head_size
    hit = (row == head) | (row == head + heads) | (row == head + 2 * heads)
    return hit.astype(F32).astype(BF16)


def head_adder(chunk, head_size, lanes):
    head = (iota((lanes, STATE), 0) + chunk * lanes) // head_size
    return (iota((lanes, STATE), 1) == head).astype(F32).astype(BF16)


def head_sums(value, adder):
    first = value.astype(BF16)
    second = (value - first.astype(F32)).astype(BF16)
    return dot(first, adder, 1, 0) + dot(second, adder, 1, 0)


def decay_terms(rates, heads):
    length = rates.shape[1]
    running = dot(lower(length), thrice(rates), 1, 1, HIGHEST)
    last = running[length - 1 : length, :]
    return (
        running,
        three_terms(jnp.exp(last - running), heads),
        three_terms(jnp.exp(running), heads),
    )


def summary_kernel(
    heads, place, x_ref, g_ref, write_ref, read_ref, rates_ref,
    send_ref, keep_ref, decay_ref, total_ref, tail_ref, lead_ref, write_t, read_t,
):
    chunk = pl.program_id(0)
    head_size = x_ref.shape[1] * pl.num_programs(0) // heads

    @pl.when(chunk == 0)
    def _():
        running, tail, lead = decay_terms(rates_ref[...], heads)
        tail_ref[...] = tail
        lead_ref[...] = lead
        total_ref[...] = running[STRETCH - 8 :, :]
        write_t[...] = write_ref[...].astype(F32).T.astype(BF16)
        read_t[...] = read_ref[...].astype(F32).T.astype(BF16)

    spread = spreader(chunk, heads, head_size, x_ref.shape[1])
    tail = dot(tail_ref[...], spread, 1, 0)
    lead = dot(lead_ref[...], spread, 1, 0)
    inputs_tail = (x_ref[...].astype(F32) * tail).astype(BF16)
    grads_lead = (g_ref[...].astype(F32) * lead).astype(BF16)
    state = dot(write_t[...], inputs_tail, 1, 0)
    back = dot(read_t[...], grads_lead, 1, 0)
    decay_ref[...] = lead[STRETCH - 8 :, :]
    first = place[0] == 0
    send_ref[...] = jnp.where(first, state, back)
    keep_ref[...] = jnp.where(first, back, state)


def summary(place, x, g, write_map, read_map, rates):
    tokens, wide = x.shape
    heads = rates.shape[0]
    whole = lambda shape: pl.BlockSpec(shape, lambda c: (0, 0))
    strip = lambda rows: pl.BlockSpec((rows, LANES), lambda c: (0, c))
    return pl.pallas_call(
        lambda *refs: summary_kernel(heads, *refs),
        grid=(wide // LANES,),
        in_specs=[
            pl.BlockSpec(memory_space=pltpu.SMEM),
            strip(tokens),
            strip(tokens),
            whole((tokens, STATE)),
            whole((tokens, STATE)),
            whole((heads, tokens)),
        ],
        out_specs=[strip(STATE), strip(STATE), strip(8), whole((8, STATE))],
        out_shape=[
            jax.ShapeDtypeStruct((STATE, wide), F32),
            jax.ShapeDtypeStruct((STATE, wide), F32),
            jax.ShapeDtypeStruct((8, wide), F32),
            jax.ShapeDtypeStruct((8, STATE), F32),
        ],
        scratch_shapes=[
            pltpu.VMEM((tokens, STATE), BF16),
            pltpu.VMEM((tokens, STATE), BF16),
            pltpu.VMEM((STATE, tokens), BF16),
            pltpu.VMEM((STATE, tokens), BF16),
        ],
        compiler_params=pltpu.CompilerParams(vmem_limit_bytes=32 << 20),
        name="summary",
    )(place, x, g, write_map, read_map, rates)


def intra_kernel(
    heads, x_ref, g_ref, write_ref, read_ref, rates_ref,
    dx_ref, db_ref, dc_ref, change_ref, column_ref, row_ref, scores_ref, mask_ref, pairs_ref,
):
    chunk = pl.program_id(0)
    lanes = x_ref.shape[1]
    head_size = lanes * pl.num_programs(0) // heads
    per_chunk = lanes // head_size

    @pl.when(chunk == 0)
    def _():
        rates = rates_ref[...]
        triangle = lower(STRETCH)
        column_ref[...] = dot(triangle, thrice(rates), 1, 1, HIGHEST)
        row_ref[...] = dot(rates, triangle, 1, 1, HIGHEST)
        mask_ref[...] = triangle
        scores_ref[...] = dot(read_ref[...], write_ref[...], 1, 1)
        pairs_ref[...] = jnp.zeros_like(pairs_ref)
        change_ref[...] = jnp.zeros_like(change_ref)

    columns = pltpu.roll(column_ref[...], STATE - chunk * per_chunk, 1)
    rows = row_ref[pl.ds(pl.multiple_of(chunk * per_chunk, per_chunk), per_chunk), :]
    causal = mask_ref[...] > 0.5
    scores = scores_ref[...]
    pairs = pairs_ref[...]
    low_half = iota((STRETCH, 2 * head_size), 1) < head_size
    adder = head_adder(chunk, head_size, lanes)
    for pair in range(per_chunk // 2):
        strip = slice(pair * 2 * head_size, (pair + 1) * 2 * head_size)
        x = x_ref[:, strip]
        g = g_ref[:, strip]
        ys, dxs = [], []
        for half in range(2):
            head = 2 * pair + half
            gap = columns[:, head : head + 1] - rows[head : head + 1, :]
            decay = jnp.where(causal, jnp.exp(gap), 0.0)
            mixing = (scores * decay).astype(BF16)
            ys.append(dot(mixing, x, 1, 0))
            dxs.append(dot(mixing, g, 0, 0))
            mine = low_half if half == 0 else jnp.logical_not(low_half)
            pairs = pairs + dot(jnp.where(mine, g, jnp.zeros_like(g)), x, 1, 1) * decay
        y = jnp.where(low_half, ys[0], ys[1])
        dx = jnp.where(low_half, dxs[0], dxs[1])
        dx_ref[:, strip] = dx
        change_ref[...] += head_sums(
            g.astype(F32) * y - x.astype(F32) * dx, adder[strip, :]
        )
    pairs_ref[...] = pairs

    @pl.when(chunk == pl.num_programs(0) - 1)
    def _():
        summed = pairs_ref[...].astype(BF16)
        db_ref[...] = dot(summed, read_ref[...], 0, 0)
        dc_ref[...] = dot(summed, write_ref[...], 1, 0)


def intra(x, g, write_map, read_map, rates):
    tokens, wide = x.shape
    heads = rates.shape[0]
    whole = lambda shape: pl.BlockSpec(shape, lambda c: (0, 0))
    strip = lambda rows: pl.BlockSpec((rows, LANES), lambda c: (0, c))
    return pl.pallas_call(
        lambda *refs: intra_kernel(heads, *refs),
        grid=(wide // LANES,),
        in_specs=[
            strip(tokens),
            strip(tokens),
            whole((tokens, STATE)),
            whole((tokens, STATE)),
            whole((heads, tokens)),
        ],
        out_specs=[strip(tokens)] + [whole((tokens, STATE))] * 3,
        out_shape=[
            jax.ShapeDtypeStruct((tokens, wide), F32),
            jax.ShapeDtypeStruct((tokens, STATE), F32),
            jax.ShapeDtypeStruct((tokens, STATE), F32),
            jax.ShapeDtypeStruct((tokens, STATE), F32),
        ],
        scratch_shapes=[
            pltpu.VMEM((tokens, STATE), F32),
            pltpu.VMEM((heads, tokens), F32),
            pltpu.VMEM((tokens, tokens), F32),
            pltpu.VMEM((tokens, tokens), F32),
            pltpu.VMEM((tokens, tokens), F32),
        ],
        compiler_params=pltpu.CompilerParams(vmem_limit_bytes=32 << 20),
        cost_estimate=pl.CostEstimate(
            flops=30_000_000_000, bytes_accessed=6_000_000, transcendentals=heads * tokens * tokens
        ),
        name="intra",
    )(x, g, write_map, read_map, rates)


def finish_kernel(
    heads, pieces, place, x_ref, g_ref, write_ref, read_ref, rates_ref,
    dx_ref, db_ref, dc_ref, change_ref, first_ref, other_decay_ref, *rest,
):
    own_pieces = rest[:pieces]
    far_pieces = rest[pieces : 2 * pieces]
    (grad_ref, write_out, read_out, suffix_ref, tail_ref, lead_ref, own_ref, far_ref, sum_ref,
     db_sum, dc_sum) = rest[2 * pieces :]
    chunk = pl.program_id(0)
    lanes = x_ref.shape[1]
    head_size = lanes * pl.num_programs(0) // heads
    part = STATE // pieces

    @pl.when(chunk == 0)
    def _():
        _, tail, lead = decay_terms(rates_ref[...], heads)
        tail_ref[...] = tail
        lead_ref[...] = lead
        sum_ref[...] = change_ref[...]
        db_sum[...] = db_ref[...]
        dc_sum[...] = dc_ref[...]

    for step in range(pieces):
        rows = pl.ds(pl.multiple_of((place[1] ^ step) * part, part), part)
        own_ref[rows, :] = own_pieces[step][...]
        far_ref[rows, :] = far_pieces[step][...]
    own = own_ref[...] * other_decay_ref[0:1, :] + first_ref[...]
    far = far_ref[...]
    is_first = place[0] == 0
    state = jnp.where(is_first, far, own).astype(BF16)
    back = jnp.where(is_first, own, far).astype(BF16)
    spread = spreader(chunk, heads, head_size, lanes)
    tail = dot(tail_ref[...], spread, 1, 0)
    lead = dot(lead_ref[...], spread, 1, 0)
    x = x_ref[...].astype(F32)
    g = g_ref[...].astype(F32)
    y = dot(read_ref[...], state, 1, 0) * lead
    dx = dot(write_ref[...], back, 1, 0) * tail
    grad_ref[...] = (dx_ref[...] + dx).astype(BF16)
    sum_ref[...] += head_sums(g * y - x * dx, head_adder(chunk, head_size, lanes))
    db_sum[...] += dot((x * tail).astype(BF16), back, 1, 1)
    dc_sum[...] += dot((g * lead).astype(BF16), state, 1, 1)

    @pl.when(chunk == pl.num_programs(0) - 1)
    def _():
        write_out[...] = db_sum[...].astype(BF16)
        read_out[...] = dc_sum[...].astype(BF16)
        suffix_ref[...] = dot(sum_ref[...], lower(STRETCH), 0, 0, HIGHEST)[:heads, :]


def finish(place, x, g, write_map, read_map, rates, parts, first, other_decay, own, far):
    tokens, wide = x.shape
    heads = rates.shape[0]
    pieces = len(own)
    whole = lambda shape: pl.BlockSpec(shape, lambda c: (0, 0))
    strip = lambda rows: pl.BlockSpec((rows, LANES), lambda c: (0, c))
    return pl.pallas_call(
        lambda *refs: finish_kernel(heads, pieces, *refs),
        grid=(wide // LANES,),
        in_specs=[
            pl.BlockSpec(memory_space=pltpu.SMEM),
            strip(tokens),
            strip(tokens),
            whole((tokens, STATE)),
            whole((tokens, STATE)),
            whole((heads, tokens)),
            strip(tokens),
            whole((tokens, STATE)),
            whole((tokens, STATE)),
            whole((tokens, STATE)),
            strip(STATE),
            strip(1),
        ]
        + [strip(STATE // pieces)] * (2 * pieces),
        out_specs=[
            strip(tokens),
            whole((tokens, STATE)),
            whole((tokens, STATE)),
            whole((heads, tokens)),
        ],
        out_shape=[
            jax.ShapeDtypeStruct((tokens, wide), BF16),
            jax.ShapeDtypeStruct((tokens, STATE), BF16),
            jax.ShapeDtypeStruct((tokens, STATE), BF16),
            jax.ShapeDtypeStruct((heads, tokens), F32),
        ],
        scratch_shapes=[
            pltpu.VMEM((tokens, STATE), BF16),
            pltpu.VMEM((tokens, STATE), BF16),
            pltpu.VMEM((STATE, LANES), F32),
            pltpu.VMEM((STATE, LANES), F32),
            pltpu.VMEM((tokens, STATE), F32),
            pltpu.VMEM((tokens, STATE), F32),
            pltpu.VMEM((tokens, STATE), F32),
        ],
        compiler_params=pltpu.CompilerParams(vmem_limit_bytes=32 << 20),
        name="finish",
    )(place, x, g, write_map, read_map, rates, *parts, first, other_decay, *own, *far)


def chain_weights(logs, order, target):
    rank = order * jnp.arange(logs.shape[0])
    goal = order * target
    between = (rank[None, :] > rank[:, None]) & (rank[None, :] < goal)
    passed = jnp.sum(jnp.where(between[:, :, None], logs[None], 0.0), axis=1)
    return jnp.where((rank < goal)[:, None], jnp.exp(passed), 0.0)


def per_device(inputs, out_grad, input_map, output_map, log_decay):
    heads = log_decay.shape[0]
    head_size = inputs.shape[1] // heads
    groups, shards = lax.axis_size("grp"), lax.axis_size("seq")
    chips = shards // 2
    part = STATE // chips
    group, shard = lax.axis_index("grp"), lax.axis_index("seq")
    chip, core = shard // 2, shard % 2
    order = 2 * core - 1
    place = jnp.stack([core, chip]).astype(jnp.int32)
    everyone = [(a, z, c) for a in range(groups) for z in range(chips) for c in range(2)]

    def move(value, target):
        pairs = []
        for a, z, c in everyone:
            to = target(a, z, c)
            if to is not None:
                pairs.append((a * shards + 2 * z + c, to[0] * shards + 2 * to[1] + to[2]))
        return lax.ppermute(value, ("grp", "seq"), pairs)

    def widen(value):
        return jnp.repeat(value, head_size, axis=-1)

    send, keep, own_decay, totals = summary(place, inputs, out_grad, input_map, output_map, log_decay)
    every_log = lax.all_gather(totals[7:8, :heads], ("grp", "seq"), axis=0, tiled=True)
    parts = intra(inputs, out_grad, input_map, output_map, log_decay)

    first = move(send, lambda a, z, c: (a, z, 1 - c))
    chip_total = own_decay[7:8] * first + keep

    logs = every_log.reshape(groups, chips, 2, heads)
    chip_logs = jnp.sum(logs, axis=2)
    my_logs = lax.dynamic_index_in_dim(chip_logs, group, 0, keepdims=False)
    group_logs = jnp.sum(chip_logs, axis=1)

    def piece(index):
        return lax.dynamic_slice_in_dim(chip_total, index * part, part, 0)

    at = [piece(chip)] + [
        move(piece(chip ^ step), lambda a, z, c: (a, z ^ step, c)) for step in range(1, chips)
    ]

    def weighted(weights, values):
        total = None
        for step, value in enumerate(values):
            row = lax.dynamic_index_in_dim(weights, chip ^ step, 0, keepdims=True)
            total = value * row if total is None else total + value * row
        return total

    end = jnp.where(core == 1, chips, -1)
    group_total = weighted(widen(chain_weights(my_logs, order, end)), at)
    group_weights = widen(chain_weights(group_logs, order, group))
    incoming = jnp.zeros_like(group_total)
    for step in range(1, groups):

        def later(a, z, c):
            to = a + step if c == 1 else a - step
            return (to, z, c) if 0 <= to < groups else None

        got = move(group_total, later)
        source = jnp.clip(group - order * step, 0, groups - 1)
        valid = (group - order * step == source).astype(F32)
        row = lax.dynamic_index_in_dim(group_weights, source, 0, keepdims=True)
        incoming = incoming + got * (row * valid)

    def entering(step):
        target = chip ^ step
        rank = order * jnp.arange(chips)
        ahead = jnp.exp(
            jnp.sum(jnp.where((rank < order * target)[:, None], my_logs, 0.0), axis=0)
        )
        return widen(ahead)[None] * incoming + weighted(
            widen(chain_weights(my_logs, order, target)), at
        )

    own = [
        entering(step) if step == 0 else move(entering(step), lambda a, z, c: (a, z ^ step, c))
        for step in range(chips)
    ]
    far = [move(value, lambda a, z, c: (a, z, 1 - c)) for value in own]
    other_log = lax.dynamic_index_in_dim(
        every_log, group * shards + (shard ^ 1), 0, keepdims=True
    )
    grad_inputs, grad_write, grad_read, suffix = finish(
        place,
        inputs,
        out_grad,
        input_map,
        output_map,
        log_decay,
        parts,
        first,
        widen(jnp.exp(other_log)),
        own,
        far,
    )
    every_total = lax.all_gather(suffix[:, :1].T, ("grp", "seq"), axis=0, tiled=True)
    ranks = lax.broadcasted_iota(jnp.int32, every_total.shape, 0)
    later_sum = jnp.sum(jnp.where(ranks > group * shards + shard, every_total, 0.0), axis=0)
    return (grad_inputs, grad_write, grad_read, suffix + later_sum[:, None])


def solution(mesh):
    tokens = P(("grp", "seq"), None)
    in_specs = (tokens, tokens, tokens, tokens, P(None, ("grp", "seq")))
    out_specs = (tokens, tokens, tokens, P(None, ("grp", "seq")))
    return jax.shard_map(
        per_device, mesh=mesh, in_specs=in_specs, out_specs=out_specs, check_vma=False
    )
```

time: 497 us -> 207 us (0.42)
  waiting for transfers between devices: 261 us -> 45.4 us
  matrix products: 49.3 us -> 0 us
  other arithmetic: 53 us -> 8.58 us
  Pallas kernels: 0 us -> 24.4 us
  starting transfers between devices: 0.2 us -> 18.6 us
  between operations: 14.8 us -> 1.17 us
  local copies, waits for them, and re-layouts: 27.3 us -> 21.6 us
    all_gather x4 -> x0, waiting for transfers between devices: 193 us -> none  [prefix_2(): pieces = jax.tree.map(lambda part: lax.all_gather(part, axis), value)]
    psum x1 -> x0, waiting for transfers between devices: 67.9 us -> none  [per_device(): lax.psum((whole_up[0] * mask_last, whole_up[1] * mask_last, whole_down[0]...]
    dot_general x24 -> x0, matrix products: 49.3 us -> none  [the longest x5 13.1 us: one_group(): jnp.einsum('hij,jhp->ihp', mixing, group_values, preferred_element_type=j...]
    ppermute x0 -> x14, waiting for transfers between devices: none -> 45.4 us  [move(): return lax.ppermute(value, ('grp', 'seq'), pairs)]
    select_n x34 -> x6, other arithmetic: 40.5 us -> 0.4 us  [chain_weights(): return jnp.where((rank < goal)[:, None], jnp.exp(passed), 0.0)]
    all_gather x2 -> x1, blocking collectives: 15.7 us -> 42.6 us  [per_device(): lax.all_gather(totals[7:8, :heads], ('grp', 'seq'), axis=0, tiled=True)]
    pallas_call x0 -> x3, Pallas kernels: none -> 24.4 us  [the longest x1 10.7 us: intra(): pl.pallas_call(lambda *refs: intra_kernel(heads, *refs), grid=(wide // LA...]
    ppermute x0 -> x14, starting transfers between devices: none -> 18.6 us  [move(): return lax.ppermute(value, ('grp', 'seq'), pairs)]
  transfers between devices with their start and end apart: 5 -> 14, of which waited for: 4 -> 6; matrix products, arithmetic and copies ran while one was open for 17% -> 4% of each run, Pallas kernels for 0% -> 5%
where the time goes in v1:
time: 207 us; the launch traced here: 206 us
  blocking collectives  86.1 us (42%)
  waiting for transfers between devices  45.4 us (22%)
  Pallas kernels  24.4 us (12%)
  local copies, waits for them, and re-layouts  21.6 us (10%)
  starting transfers between devices  18.6 us (9%)
  other arithmetic  8.58 us (4%)
    ppermute x14, waiting for transfers between devices, move(): return lax.ppermute(value, ('grp', 'seq'), pairs)  45.4 us
    unnamed x1, blocking collectives  43.5 us
    all_gather x1, blocking collectives, per_device(): lax.all_gather(totals[7:8, :heads], ('grp', 'seq'), axis=0, tiled=True)  42.6 us
    ppermute x14, starting transfers between devices, move(): return lax.ppermute(value, ('grp', 'seq'), pairs)  18.6 us
    unnamed x59, local copies, waits for them, and re-layouts  16.5 us
    pallas_call x1, Pallas kernels, intra(): pl.pallas_call(lambda *refs: intra_kernel(heads, *refs), grid=(wide // LA...  10.7 us
    pallas_call x1, Pallas kernels, finish(): pl.pallas_call(lambda *refs: finish_kernel(heads, pieces, *refs), grid=(w...  8.9 us
    pallas_call x1, Pallas kernels, summary(): pl.pallas_call(lambda *refs: summary_kernel(heads, *refs), grid=(wide //...  4.82 us
  transfers between devices with their start and end apart: 14, of which 6 were waited for; matrix products, arithmetic and copies ran while one was open for 4% of the time, Pallas kernels for 5%

profile of v1, /device:TPU:0, one launch (start us, length us, event | category | flops | bytes accessed | tf_op | source)
XLA Modules:
  0.0 205.9 jit_solution(7194830890189118862)
XLA Ops:
  0.7 1.3 copy-done
  2.0 1.3 copy-done.2
  3.4 0.8 copy-done.8
  4.2 0.8 copy-done.10
  5.0 0.8 copy-done.12
  5.8 4.8 %summary.1 = (f32[128,2560]{1,0:T(8,128)}, f32[128,2560]{1,0:T(8,128)S(1)}, f32[8,2560]{1,0:T(8,128)S(1)}, f32[8,128]{1,0:T(8,128)S(1)}) custom-call(s32[2]{0:T(128)S(1)} %pad_add_fusion.refs_0_, bf16[256,2560]{1,0:T(8,128)(2,1)S(1)} %copy-done, bf16[256,2560]{1,0:T(8,128)(2,1)S(1)} %copy-done.2, bf16[256,128]{1,0:T(8,128)(2,1)S(1)} %copy-done.8, ...), custom_call_target="tpu_custom_call" | custom-call | tf_op jit(solution)/shard_map/summary/pallas_call | solution.py:112
  10.6 0.5 collective-permute-start
  11.1 42.6 %all-gather.1 = f32[32,1,40]{2,1,0:T(1,128)S(1)} all-gather(f32[1,1,40]{2,1,0:T(1,128)S(1)} %slice_bitcast_fusion), channel_id=1, replica_groups=mesh['grp'=4,'seq'=8] {'grp','seq'}, dimensions={0}, use_global_device_ids=true | all-gather | bytes 5280 | tf_op jit(solution)/shard_map/all_gather | solution.py:366
  53.9 0.1 select_reduce_fusion.5
  54.0 0.1 select_reduce_fusion.7
  54.1 0.1 select_reduce_fusion.1
  54.4 0.2 multiply_add_fusion
  54.6 0.9 copy-done.4
  55.5 1.0 copy-done.20
  56.5 4.4 %collective-permute-start.3 = (f32[32,2560]{1,0:T(8,128)S(1)}, f32[32,2560]{1,0:T(8,128)S(1)}, u32[]{:S(2)}, u32[]{:S(2)}) collective-permute-start(f32[32,2560]{1,0:T(8,128)S(1)} %get-tuple-element.68), channel_id=1, source_target_pairs={{0,6},{1,7},{2,4},{3,5},{4,2},{5,3},{6,0},{7,1},{8,14},{9,15},{10,... | collective-permute-start | bytes 983048 | tf_op jit(solution)/shard_map/ppermute | solution.py:360
  61.1 0.1 reshape.326
  61.2 0.1 dynamic-slice_reduce_fusion.19
  61.4 8.5 %collective-permute-done.1 = f32[32,2560]{1,0:T(8,128)S(1)} collective-permute-done((f32[32,2560]{1,0:T(8,128)S(1)}, f32[32,2560]{1,0:T(8,128)S(1)}, u32[]{:S(2)}, u32[]{:S(2)}) %collective-permute-start.1) | collective-permute-done | bytes 327712 | tf_op jit(solution)/shard_map/ppermute | solution.py:360
  69.9 12.1 %collective-permute-done.2 = f32[32,2560]{1,0:T(8,128)S(1)} collective-permute-done((f32[32,2560]{1,0:T(8,128)S(1)}, f32[32,2560]{1,0:T(8,128)S(1)}, u32[]{:S(2)}, u32[]{:S(2)}) %collective-permute-start.2) | collective-permute-done | bytes 327712 | tf_op jit(solution)/shard_map/ppermute | solution.py:360
  82.1 2.1 %multiply_add_fusion.2 = f32[32,2560]{1,0:T(8,128)} fusion(f32[32,2560]{1,0:T(8,128)S(1)} %collective-permute-done.3, f32[32,2560]{1,0:T(8,128)S(1)} %collective-permute-done.2, f32[32,2560]{1,0:T(8,128)S(1)} %collective-permute-done.1, f32[128,2560]{1,0:T(8,128)} %copy-done.20, s32[]{:T(128)S(6)} %select_n.126, f32[2560]{0:T(1024)S(1)} %get-tuple-element.48, ...), kind=kLoop, calls=%fused_computation.6 | loop fusion | flops 573440 | bytes 1679364 | tf_op jit(solution)/shard_map/add | solution.py:388
  84.2 1.3 collective-permute-start.4
  85.4 1.3 collective-permute-start.5
  86.7 1.3 collective-permute-start.6
  88.2 0.1 reshape.331
  88.4 0.7 reshape.327
  89.2 0.7 mul.506
  89.9 0.1 reshape.330
  90.1 0.1 reshape.329
  90.3 0.7 mul.474
  91.0 0.7 mul.490
  91.8 0.1 broadcast_in_dim.220
  91.9 0.1 reshape.328
  92.1 0.1 dynamic-slice_reduce_fusion.3
  92.3 0.1 dynamic-slice_reduce_fusion.7
  92.4 0.1 dynamic-slice_reduce_fusion.11
  92.5 0.1 dynamic-slice_reduce_fusion.15
  92.6 1.0 multiply_reduce_fusion.2
  93.6 1.0 collective-permute-done.4
  94.7 3.4 %collective-permute-done.5 = f32[32,2560]{1,0:T(8,128)S(1)} collective-permute-done((f32[32,2560]{1,0:T(8,128)}, f32[32,2560]{1,0:T(8,128)S(1)}, u32[]{:S(2)}, u32[]{:S(2)}) %collective-permute-start.5) | collective-permute-done | bytes 327712 | tf_op jit(solution)/shard_map/ppermute | solution.py:360
  98.2 0.9 add_add_fusion
  99.2 1.3 add_add_fusion.1
  100.6 6.9 %collective-permute-start.7 = (f32[32,2560]{1,0:T(8,128)S(1)}, f32[32,2560]{1,0:T(8,128)S(1)}, u32[]{:S(2)}, u32[]{:S(2)}) collective-permute-start(f32[32,2560]{1,0:T(8,128)S(1)} %get-tuple-element.66), channel_id=1, source_target_pairs={{0,2},{1,3},{2,0},{3,1},{4,6},{5,7},{6,4},{7,5},{8,10},{9,11},{10,... | collective-permute-start | bytes 983048 | tf_op jit(solution)/shard_map/ppermute | solution.py:360
  107.5 2.4 %collective-permute-start.9 = (f32[32,2560]{1,0:T(8,128)S(1)}, f32[32,2560]{1,0:T(8,128)}, u32[]{:S(2)}, u32[]{:S(2)}) collective-permute-start(f32[32,2560]{1,0:T(8,128)S(1)} %get-tuple-element.62), channel_id=1, source_target_pairs={{0,6},{1,7},{2,4},{3,5},{4,2},{5,3},{6,0},{7,1},{8,14},{9,15},{10,... | collective-permute-start | bytes 983048 | tf_op jit(solution)/shard_map/ppermute | solution.py:360
  109.9 1.3 add_add_fusion.3.refs_12_
  111.3 6.6 %collective-permute-done.7.refs_13_ = f32[32,2560]{1,0:T(8,128)S(1)} collective-permute-done((f32[32,2560]{1,0:T(8,128)S(1)}, f32[32,2560]{1,0:T(8,128)S(1)}, u32[]{:S(2)}, u32[]{:S(2)}) %collective-permute-start.7) | collective-permute-done | bytes 327712 | tf_op jit(solution)/shard_map/ppermute | solution.py:360
  117.9 13.6 %collective-permute-done.8.refs_14_ = f32[32,2560]{1,0:T(8,128)} collective-permute-done((f32[32,2560]{1,0:T(8,128)S(1)}, f32[32,2560]{1,0:T(8,128)}, u32[]{:S(2)}, u32[]{:S(2)}) %collective-permute-start.8) | collective-permute-done | bytes 327712 | tf_op jit(solution)/shard_map/ppermute | solution.py:360
  131.5 0.5 collective-permute-start.13
  132.0 10.7 %intra.1 = (f32[256,2560]{1,0:T(8,128)S(1)}, f32[256,128]{1,0:T(8,128)S(1)}, f32[256,128]{1,0:T(8,128)S(1)}, f32[256,128]{1,0:T(8,128)S(1)}) custom-call(bf16[256,2560]{1,0:T(8,128)(2,1)S(1)} %copy-done.1, bf16[256,2560]{1,0:T(8,128)(2,1)S(1)} %copy-done.3, bf16[256,128]{1,0:T(8,128)(2,1)S(1)} %copy-done.9, bf16[256,128]{1,0:T(8,128)(2,1)S(1)} %copy-done.11, ...), custom_call_target="tpu_custom_call" | custom-call | flops 30000001024 | bytes 6000000 | tf_op jit(solution)/shard_map/intra/pallas_call | solution.py:202
  142.8 1.5 copy-done.6
  144.3 0.7 copy-done.14
  144.9 0.7 copy-done.16
  145.6 0.6 copy-done.18
  146.3 0.1 broadcast_in_dim.206.refs_11_
  146.5 1.3 copy-done.5
  147.8 1.7 copy-done.7
  149.5 0.9 copy-done.15
  150.4 0.9 copy-done.17
  151.3 0.9 copy-done.19
  152.2 8.9 %finish.1 = (bf16[256,2560]{1,0:T(8,128)(2,1)}, bf16[256,128]{1,0:T(8,128)(2,1)}, bf16[256,128]{1,0:T(8,128)(2,1)}, f32[40,256]{1,0:T(8,128)S(1)}) custom-call(s32[2]{0:T(128)S(1)} %pad_add_fusion.refs_0_, bf16[256,2560]{1,0:T(8,128)(2,1)S(1)} %copy-done.1, bf16[256,2560]{1,0:T(8,128)(2,1)S(1)} %copy-done.3, bf16[256,128]{1,0:T(8,128)(2,1)S(1)} %copy-done.9, ...), custom_call_target="tpu_custom_call" | custom-call | tf_op jit(solution)/shard_map/finish/pallas_call | solution.py:290
  161.2 0.1 slice_reduce_fusion
  161.3 0.3 dynamic-update-slice
  161.5 43.5 %all-reduce = f32[1280]{0:T(1024)S(1)} all-reduce(f32[1280]{0:T(1024)S(1)} %dynamic-update-slice), channel_id=2, replica_groups=mesh['grp'=4,'seq'=8] {'grp','seq'}, use_global_device_ids=true, to_apply=%add | all-reduce | flops 1280 | bytes 10240
  205.1 0.1 select_reduce_fusion
  205.2 0.7 broadcast_add_fusion
  (89 shorter events, 1.9 us)
Async XLA Ops:
  0.7 1.3 copy-start
  2.0 1.3 copy-start.2
  3.4 0.8 copy-start.8
  4.2 0.8 copy-start.10
  5.0 0.8 copy-start.12
  10.6 43.8 %collective-permute-start = (f32[128,2560]{1,0:T(8,128)}, f32[128,2560]{1,0:T(8,128)S(1)}, u32[]{:S(2)}, u32[]{:S(2)}) collective-permute-start(f32[128,2560]{1,0:T(8,128)} %get-tuple-element.20), channel_id=1, source_target_pairs={{0,1},{1,0},{2,3},{3,2},{4,5},{5,4},{6,7},{7,6},{8,9},{9,8},{10,11... | collective-permute-start | bytes 3932168 | tf_op jit(solution)/shard_map/ppermute | solution.py:360
  54.4 1.1 copy-start.4
  55.5 1.1 copy-start.20
  56.5 13.4 %collective-permute-start.1 = (f32[32,2560]{1,0:T(8,128)S(1)}, f32[32,2560]{1,0:T(8,128)S(1)}, u32[]{:S(2)}, u32[]{:S(2)}) collective-permute-start(f32[32,2560]{1,0:T(8,128)S(1)} %get-tuple-element.67), channel_id=1, source_target_pairs={{0,2},{1,3},{2,0},{3,1},{4,6},{5,7},{6,4},{7,5},{8,10},{9,11},{10,... | collective-permute-start | bytes 983048 | tf_op jit(solution)/shard_map/ppermute | solution.py:360
  56.5 25.5 %collective-permute-start.2 = (f32[32,2560]{1,0:T(8,128)S(1)}, f32[32,2560]{1,0:T(8,128)S(1)}, u32[]{:S(2)}, u32[]{:S(2)}) collective-permute-start(f32[32,2560]{1,0:T(8,128)S(1)} %get-tuple-element.69), channel_id=1, source_target_pairs={{0,4},{1,5},{2,6},{3,7},{4,0},{5,1},{6,2},{7,3},{8,12},{9,13},{10,... | collective-permute-start | bytes 983048 | tf_op jit(solution)/shard_map/ppermute | solution.py:360
  56.5 25.5 %collective-permute-start.3 = (f32[32,2560]{1,0:T(8,128)S(1)}, f32[32,2560]{1,0:T(8,128)S(1)}, u32[]{:S(2)}, u32[]{:S(2)}) collective-permute-start(f32[32,2560]{1,0:T(8,128)S(1)} %get-tuple-element.68), channel_id=1, source_target_pairs={{0,6},{1,7},{2,4},{3,5},{4,2},{5,3},{6,0},{7,1},{8,14},{9,15},{10,... | collective-permute-start | bytes 983048 | tf_op jit(solution)/shard_map/ppermute | solution.py:360
  69.9 29.2 %copy-start.22 = (f32[32,2560]{1,0:T(8,128)}, f32[32,2560]{1,0:T(8,128)S(1)}, u32[]{:S(2)}) copy-start(f32[32,2560]{1,0:T(8,128)S(1)} %collective-permute-done.1) | copy-start | bytes 983044
  82.1 18.4 %copy-start.23 = (f32[32,2560]{1,0:T(8,128)}, f32[32,2560]{1,0:T(8,128)S(1)}, u32[]{:S(2)}) copy-start(f32[32,2560]{1,0:T(8,128)S(1)} %collective-permute-done.2) | copy-start | bytes 983044
  82.1 17.0 %copy-start.24 = (f32[32,2560]{1,0:T(8,128)}, f32[32,2560]{1,0:T(8,128)S(1)}, u32[]{:S(2)}) copy-start(f32[32,2560]{1,0:T(8,128)S(1)} %collective-permute-done.3) | copy-start | bytes 983044
  82.1 16.1 %copy-start.21 = (f32[128,2560]{1,0:T(8,128)S(1)}, f32[128,2560]{1,0:T(8,128)}, u32[]{:S(2)}) copy-start(f32[128,2560]{1,0:T(8,128)} %copy-done.20) | copy-start | bytes 3932164
  84.2 10.5 %collective-permute-start.4 = (f32[32,2560]{1,0:T(8,128)}, f32[32,2560]{1,0:T(8,128)S(1)}, u32[]{:S(2)}, u32[]{:S(2)}) collective-permute-start(f32[32,2560]{1,0:T(8,128)} %multiply_add_fusion.2), channel_id=1, source_target_pairs={{1,9},{3,11},{5,13},{7,15},{8,0},{9,17},{10,2},{11,19},{12,4},{13,... | collective-permute-start | bytes 983048 | tf_op jit(solution)/shard_map/ppermute | solution.py:360
  85.4 12.7 %collective-permute-start.5 = (f32[32,2560]{1,0:T(8,128)}, f32[32,2560]{1,0:T(8,128)S(1)}, u32[]{:S(2)}, u32[]{:S(2)}) collective-permute-start(f32[32,2560]{1,0:T(8,128)} %multiply_add_fusion.2), channel_id=1, source_target_pairs={{1,17},{3,19},{5,21},{7,23},{9,25},{11,27},{13,29},{15,31},{16,0},... | collective-permute-start | bytes 983048 | tf_op jit(solution)/shard_map/ppermute | solution.py:360
  86.7 11.4 %collective-permute-start.6 = (f32[32,2560]{1,0:T(8,128)}, f32[32,2560]{1,0:T(8,128)S(1)}, u32[]{:S(2)}, u32[]{:S(2)}) collective-permute-start(f32[32,2560]{1,0:T(8,128)} %multiply_add_fusion.2), channel_id=1, source_target_pairs={{1,25},{3,27},{5,29},{7,31},{24,0},{26,2},{28,4},{30,6}} | collective-permute-start | bytes 983048 | tf_op jit(solution)/shard_map/ppermute | solution.py:360
  98.1 1.0 copy-start.26
  98.1 1.0 copy-start.27
  99.1 10.8 %copy-start.25 = (f32[32,2560]{1,0:T(8,128)S(1)}, f32[32,2560]{1,0:T(8,128)}, u32[]{:S(2)}) copy-start(f32[32,2560]{1,0:T(8,128)} %copy-done.24) | copy-start | bytes 983044
  99.1 32.9 %copy-start.3 = (bf16[256,2560]{1,0:T(8,128)(2,1)S(1)}, bf16[256,2560]{1,0:T(8,128)(2,1)}, u32[]{:S(2)}) copy-start(bf16[256,2560]{1,0:T(8,128)(2,1)} %refs_2_.5) | copy-start | bytes 3932164
  100.5 31.5 %copy-start.1 = (bf16[256,2560]{1,0:T(8,128)(2,1)S(1)}, bf16[256,2560]{1,0:T(8,128)(2,1)}, u32[]{:S(2)}) copy-start(bf16[256,2560]{1,0:T(8,128)(2,1)} %refs_1_.5) | copy-start | bytes 3932164
  100.5 31.5 %copy-start.9 = (bf16[256,128]{1,0:T(8,128)(2,1)S(1)}, bf16[256,128]{1,0:T(8,128)(2,1)}, u32[]{:S(2)}) copy-start(bf16[256,128]{1,0:T(8,128)(2,1)} %refs_3_.5) | copy-start | bytes 196612
  100.5 31.5 %copy-start.11 = (bf16[256,128]{1,0:T(8,128)(2,1)S(1)}, bf16[256,128]{1,0:T(8,128)(2,1)}, u32[]{:S(2)}) copy-start(bf16[256,128]{1,0:T(8,128)(2,1)} %refs_4_.5) | copy-start | bytes 196612
  100.5 31.5 %copy-start.13 = (f32[40,256]{1,0:T(8,128)S(1)}, f32[40,256]{1,0:T(8,128)}, u32[]{:S(2)}) copy-start(f32[40,256]{1,0:T(8,128)} %refs_5_.3) | copy-start | bytes 122884
  100.6 17.4 %collective-permute-start.7 = (f32[32,2560]{1,0:T(8,128)S(1)}, f32[32,2560]{1,0:T(8,128)S(1)}, u32[]{:S(2)}, u32[]{:S(2)}) collective-permute-start(f32[32,2560]{1,0:T(8,128)S(1)} %get-tuple-element.66), channel_id=1, source_target_pairs={{0,2},{1,3},{2,0},{3,1},{4,6},{5,7},{6,4},{7,5},{8,10},{9,11},{10,... | collective-permute-start | bytes 983048 | tf_op jit(solution)/shard_map/ppermute | solution.py:360
  107.5 24.0 %collective-permute-start.8 = (f32[32,2560]{1,0:T(8,128)S(1)}, f32[32,2560]{1,0:T(8,128)}, u32[]{:S(2)}, u32[]{:S(2)}) collective-permute-start(f32[32,2560]{1,0:T(8,128)S(1)} %get-tuple-element.65), channel_id=1, source_target_pairs={{0,4},{1,5},{2,6},{3,7},{4,0},{5,1},{6,2},{7,3},{8,12},{9,13},{10,... | collective-permute-start | bytes 983048 | tf_op jit(solution)/shard_map/ppermute | solution.py:360
  107.5 24.0 %collective-permute-start.9 = (f32[32,2560]{1,0:T(8,128)S(1)}, f32[32,2560]{1,0:T(8,128)}, u32[]{:S(2)}, u32[]{:S(2)}) collective-permute-start(f32[32,2560]{1,0:T(8,128)S(1)} %get-tuple-element.62), channel_id=1, source_target_pairs={{0,6},{1,7},{2,4},{3,5},{4,2},{5,3},{6,0},{7,1},{8,14},{9,15},{10,... | collective-permute-start | bytes 983048 | tf_op jit(solution)/shard_map/ppermute | solution.py:360
  111.2 35.2 %collective-permute-start.10 = (f32[32,2560]{1,0:T(8,128)S(1)}, f32[32,2560]{1,0:T(8,128)}, u32[]{:S(2)}, u32[]{:S(2)}) collective-permute-start(f32[32,2560]{1,0:T(8,128)S(1)} %add_add_fusion.3.refs_12_), channel_id=1, source_target_pairs={{0,1},{1,0},{2,3},{3,2},{4,5},{5,4},{6,7},{7,6},{8,9},{9,8},{10,11... | collective-permute-start | bytes 983048 | tf_op jit(solution)/shard_map/ppermute | solution.py:360
  117.9 28.5 %collective-permute-start.11 = (f32[32,2560]{1,0:T(8,128)S(1)}, f32[32,2560]{1,0:T(8,128)}, u32[]{:S(2)}, u32[]{:S(2)}) collective-permute-start(f32[32,2560]{1,0:T(8,128)S(1)} %collective-permute-done.7.refs_13_), channel_id=1, source_target_pairs={{0,1},{1,0},{2,3},{3,2},{4,5},{5,4},{6,7},{7,6},{8,9},{9,8},{10,11... | collective-permute-start | bytes 983048 | tf_op jit(solution)/shard_map/ppermute | solution.py:360
  131.5 14.9 %collective-permute-start.12 = (f32[32,2560]{1,0:T(8,128)}, f32[32,2560]{1,0:T(8,128)}, u32[]{:S(2)}, u32[]{:S(2)}) collective-permute-start(f32[32,2560]{1,0:T(8,128)} %collective-permute-done.8.refs_14_), channel_id=1, source_target_pairs={{0,1},{1,0},{2,3},{3,2},{4,5},{5,4},{6,7},{7,6},{8,9},{9,8},{10,11... | collective-permute-start | bytes 983048 | tf_op jit(solution)/shard_map/ppermute | solution.py:360
  131.5 14.9 %collective-permute-start.13 = (f32[32,2560]{1,0:T(8,128)}, f32[32,2560]{1,0:T(8,128)}, u32[]{:S(2)}, u32[]{:S(2)}) collective-permute-start(f32[32,2560]{1,0:T(8,128)} %collective-permute-done.9.refs_15_), channel_id=1, source_target_pairs={{0,1},{1,0},{2,3},{3,2},{4,5},{5,4},{6,7},{7,6},{8,9},{9,8},{10,11... | collective-permute-start | bytes 983048 | tf_op jit(solution)/shard_map/ppermute | solution.py:360
  142.8 1.5 copy-start.6
  144.3 0.7 copy-start.14
  144.9 0.7 copy-start.16
  145.6 0.7 copy-start.18
  146.5 1.3 copy-start.5
  147.8 1.7 copy-start.7
  149.5 0.9 copy-start.15
  150.4 0.9 copy-start.17
  151.3 0.9 copy-start.19

commit v2 on v1

v2 whole, which is shorter than its diff:
```python
import jax
import jax.numpy as jnp
from jax import lax
from jax.experimental import pallas as pl
from jax.experimental.pallas import tpu as pltpu
from jax.sharding import PartitionSpec as P

STATE = 128
STRETCH = 256
LANES = 512
STRIP = 128
META = 8
BIG_VMEM = 56 << 20
SMALL_VMEM = 24 << 20
F32 = jnp.float32
BF16 = jnp.bfloat16
HIGHEST = lax.Precision.HIGHEST


def dot(left, right, left_dim, right_dim, precision=None):
    return lax.dot_general(
        left,
        right,
        (((left_dim,), (right_dim,)), ((), ())),
        precision=precision,
        preferred_element_type=F32,
    )


def iota(shape, dim):
    return lax.broadcasted_iota(jnp.int32, shape, dim)


def lower(length):
    return (iota((length, length), 0) >= iota((length, length), 1)).astype(F32)


def thrice(rates):
    heads, length = rates.shape
    spare = jnp.zeros((STATE - 3 * heads, length), F32)
    return jnp.concatenate([rates, rates, rates, spare], axis=0)


def three_terms(value, heads):
    lane = iota(value.shape, 1)
    first = value.astype(BF16)
    rest = value - first.astype(F32)
    second = rest.astype(BF16)
    third = (rest - second.astype(F32)).astype(BF16)
    return jnp.where(lane < heads, first, jnp.where(lane < 2 * heads, second, third))


def spreader(chunk, heads, head_size, lanes):
    row = iota((STATE, lanes), 0)
    head = (iota((STATE, lanes), 1) + chunk * lanes) // head_size
    hit = (row == head) | (row == head + heads) | (row == head + 2 * heads)
    return hit.astype(F32).astype(BF16)


def head_adder(chunk, head_size, lanes):
    head = (iota((lanes, STATE), 0) + chunk * lanes) // head_size
    return (iota((lanes, STATE), 1) == head).astype(F32).astype(BF16)


def head_sums(value, adder):
    first = value.astype(BF16)
    second = (value - first.astype(F32)).astype(BF16)
    return dot(first, adder, 1, 0) + dot(second, adder, 1, 0)


def decay_terms(rates, heads):
    length = rates.shape[1]
    running = dot(lower(length), thrice(rates), 1, 1, HIGHEST)
    last = running[length - 1 : length, :]
    return (
        running,
        three_terms(jnp.exp(last - running), heads),
        three_terms(jnp.exp(running), heads),
    )


def term_pair(value):
    first = value.astype(BF16)
    return first, (value - first.astype(F32)).astype(BF16)


def spread_rows(rows, strips, head_size):
    per_strip = STRIP // head_size
    lane = iota((strips, STRIP), 1)
    row = iota((strips, STRIP), 0)
    picked = [jnp.where(lane // per_strip == row, value, 0.0) for value in rows]
    spread = lane_spread(per_strip, head_size)
    stacked = jnp.concatenate(picked, axis=0) if len(picked) > 1 else picked[0]
    wide = dot(stacked, spread, 1, 0, HIGHEST)
    return [wide[i * strips : (i + 1) * strips, :] for i in range(len(rows))]


def lane_spread(per_strip, head_size):
    head = iota((STRIP, STRIP), 0) % per_strip
    return (iota((STRIP, STRIP), 1) // head_size == head).astype(F32)


def whole(*shape):
    return pl.BlockSpec(shape, lambda *_: (0,) * len(shape))


def lanes_of(rows):
    return pl.BlockSpec((rows, LANES), lambda c: (0, c))


SCALARS = pl.BlockSpec(memory_space=pltpu.SMEM)


def summary_kernel(
    heads, chips, place, x_ref, g_ref, write_ref, read_ref, rates_ref,
    send_ref, keep_ref, decay_ref, tail_ref, lead_ref, write_t, read_t,
):
    chunk = pl.program_id(0)
    lanes = x_ref.shape[1]
    strips = lanes // STRIP
    all_strips = strips * pl.num_programs(0)
    head_size = lanes * pl.num_programs(0) // heads
    part = STATE // chips

    @pl.when(chunk == 0)
    def _():
        running, tail, lead = decay_terms(rates_ref[...], heads)
        tail_ref[...] = tail
        lead_ref[...] = lead
        send_ref[pl.ds(all_strips * STATE, META), :] = jnp.broadcast_to(
            running[STRETCH - 1 :, :], (META, STRIP)
        )
        write_t[...] = write_ref[...].astype(F32).T.astype(BF16)
        read_t[...] = read_ref[...].astype(F32).T.astype(BF16)

    spread = spreader(chunk, heads, head_size, lanes)
    tail = dot(tail_ref[...], spread, 1, 0)
    lead = dot(lead_ref[...], spread, 1, 0)
    inputs_tail = (x_ref[...].astype(F32) * tail).astype(BF16)
    grads_lead = (g_ref[...].astype(F32) * lead).astype(BF16)
    state = dot(write_t[...], inputs_tail, 1, 0)
    back = dot(read_t[...], grads_lead, 1, 0)
    first = place[0] == 0
    send = jnp.where(first, state, back)
    keep = jnp.where(first, back, state)
    for strip in range(strips):
        at = chunk * strips + strip
        wide = slice(strip * STRIP, (strip + 1) * STRIP)
        decay_ref[pl.ds(at, 1), :] = lead[STRETCH - 1 :, wide]
        for quarter in range(chips):
            rows = pl.ds(pl.multiple_of((quarter * all_strips + at) * part, part), part)
            mine = slice(quarter * part, (quarter + 1) * part)
            send_ref[rows, :] = send[mine, wide]
            keep_ref[rows, :] = keep[mine, wide]


def summary(chips, place, x, g, write_map, read_map, rates):
    tokens, wide = x.shape
    heads = rates.shape[0]
    strips = wide // STRIP
    return pl.pallas_call(
        lambda *refs: summary_kernel(heads, chips, *refs),
        grid=(wide // LANES,),
        in_specs=[
            SCALARS,
            lanes_of(tokens),
            lanes_of(tokens),
            whole(tokens, STATE),
            whole(tokens, STATE),
            whole(heads, tokens),
        ],
        out_specs=[
            whole(strips * STATE + META, STRIP),
            whole(strips * STATE, STRIP),
            whole(strips, STRIP),
        ],
        out_shape=[
            jax.ShapeDtypeStruct((strips * STATE + META, STRIP), F32),
            jax.ShapeDtypeStruct((strips * STATE, STRIP), F32),
            jax.ShapeDtypeStruct((strips, STRIP), F32),
        ],
        scratch_shapes=[
            pltpu.VMEM((tokens, STATE), BF16),
            pltpu.VMEM((tokens, STATE), BF16),
            pltpu.VMEM((STATE, tokens), BF16),
            pltpu.VMEM((STATE, tokens), BF16),
        ],
        compiler_params=pltpu.CompilerParams(vmem_limit_bytes=BIG_VMEM),
        name="summary",
    )(place, x, g, write_map, read_map, rates)


def combine_kernel(chips, place, first_ref, keep_ref, decay_ref, rates_ref, *out_refs):
    strips = decay_ref.shape[0]
    part = STATE // chips
    size = strips * part
    own_log = jnp.sum(rates_ref[...], axis=1, keepdims=True)
    heads = own_log.shape[0]
    lane = iota((heads, STRIP), 1)
    row = iota((heads, STRIP), 0)
    own_log = jnp.sum(jnp.where(lane == row, own_log, 0.0), axis=0, keepdims=True)
    meta = first_ref[pl.ds(chips * size, META), :]
    meta = jnp.where(iota((META, STRIP), 1) < heads, meta + own_log, 0.0)
    for step, out_ref in enumerate(out_refs):
        base = (place[1] ^ step) * size
        for strip in range(strips):
            rows = pl.ds(pl.multiple_of(base + strip * part, part), part)
            out_ref[strip * part : (strip + 1) * part, :] = (
                first_ref[rows, :] * decay_ref[strip : strip + 1, :] + keep_ref[rows, :]
            )
        out_ref[size:, :] = meta


def combine(chips, place, first, keep, decay, rates):
    strips = decay.shape[0]
    size = strips * (STATE // chips)
    return pl.pallas_call(
        lambda *refs: combine_kernel(chips, *refs),
        in_specs=[
            SCALARS,
            whole(*first.shape),
            whole(*keep.shape),
            whole(*decay.shape),
            whole(*rates.shape),
        ],
        out_specs=[whole(size + META, STRIP)] * chips,
        out_shape=[jax.ShapeDtypeStruct((size + META, STRIP), F32)] * chips,
        compiler_params=pltpu.CompilerParams(vmem_limit_bytes=SMALL_VMEM),
        name="combine",
    )(place, first, keep, decay, rates)


def rank_of(place, step):
    chip = place[1] ^ step
    return jnp.where(place[0] == 1, chip, -chip)


def masked_sum(terms):
    total = None
    for hit, value in terms:
        value = jnp.where(hit, value, 0.0)
        total = value if total is None else total + value
    return total


def total_kernel(strips, head_size, place, after_ref, *refs):
    at_refs, out_ref = refs[:-1], refs[-1]
    chips = len(at_refs)
    part = STATE // chips
    size = strips * part
    rank = [rank_of(place, step) for step in range(chips)]
    logs = [ref[size : size + 1, :] for ref in at_refs]
    weights = [
        jnp.exp(masked_sum([(rank[b] > rank[a], logs[b]) for b in range(chips)]))
        for a in range(chips)
    ]
    wide = spread_rows(weights, strips, head_size)
    for strip in range(strips):
        rows = slice(strip * part, (strip + 1) * part)
        total = at_refs[0][rows, :] * wide[0][strip : strip + 1, :]
        for a in range(1, chips):
            total = total + at_refs[a][rows, :] * wide[a][strip : strip + 1, :]
        out_ref[rows, :] = total
    out_ref[size:, :] = jnp.broadcast_to(sum(logs[1:], logs[0]), (META, STRIP))


def group_total(head_size, place, after, at):
    strips = (at[0].shape[0] - META) * len(at) // STATE
    return pl.pallas_call(
        lambda *refs: total_kernel(strips, head_size, *refs),
        in_specs=[SCALARS, whole(*after.shape)] + [whole(*at[0].shape)] * len(at),
        out_specs=whole(*at[0].shape),
        out_shape=jax.ShapeDtypeStruct(at[0].shape, F32),
        compiler_params=pltpu.CompilerParams(vmem_limit_bytes=SMALL_VMEM),
        name="group_total",
    )(place, after, *at)


def enter_kernel(chips, strips, head_size, place, *refs):
    at_refs, got_refs, out_refs = refs[:chips], refs[chips:-chips], refs[-chips:]
    part = STATE // chips
    size = strips * part
    rank = [rank_of(place, step) for step in range(chips)]
    logs = [ref[size : size + 1, :] for ref in at_refs]
    zero = jnp.zeros_like(logs[0])
    rows_of = []
    passed = zero
    for ref in got_refs:
        rows_of.append(jnp.exp(passed))
        passed = passed + ref[size : size + 1, :]
    for to in range(chips):
        rows_of.append(
            jnp.exp(masked_sum([(rank[m] < rank[to], logs[m]) for m in range(chips)]))
        )
    pairs = [(to, a) for to in range(chips) for a in range(chips) if a != to]
    for to, a in pairs:
        between = masked_sum(
            [((rank[m] > rank[a]) & (rank[m] < rank[to]), logs[m]) for m in range(chips)]
        )
        rows_of.append(jnp.where(rank[a] < rank[to], jnp.exp(between), 0.0))
    wide = spread_rows(rows_of, strips, head_size)
    groups_wide = wide[: len(got_refs)]
    ahead_wide = wide[len(got_refs) : len(got_refs) + chips]
    pair_wide = dict(zip(pairs, wide[len(got_refs) + chips :]))
    for strip in range(strips):
        rows = slice(strip * part, (strip + 1) * part)
        one = slice(strip, strip + 1)
        incoming = jnp.zeros((part, STRIP), F32)
        for ref, weight in zip(got_refs, groups_wide):
            incoming = incoming + ref[rows, :] * weight[one, :]
        values = [ref[rows, :] for ref in at_refs]
        for to in range(chips):
            entering = incoming * ahead_wide[to][one, :]
            for a in range(chips):
                if a != to:
                    entering = entering + values[a] * pair_wide[to, a][one, :]
            out_refs[to][rows, :] = entering


def enter(head_size, place, at, got):
    chips = len(at)
    strips = (at[0].shape[0] - META) * chips // STATE
    size = strips * (STATE // chips)
    return pl.pallas_call(
        lambda *refs: enter_kernel(chips, strips, head_size, *refs),
        in_specs=[SCALARS] + [whole(*at[0].shape)] * (chips + len(got)),
        out_specs=[whole(size, STRIP)] * chips,
        out_shape=[jax.ShapeDtypeStruct((size, STRIP), F32)] * chips,
        compiler_params=pltpu.CompilerParams(vmem_limit_bytes=SMALL_VMEM),
        name="enter",
    )(place, *at, *got)


def intra_kernel(
    heads, after_ref, x_ref, g_ref, write_ref, read_ref, rates_ref,
    dx_ref, db_ref, dc_ref, change_ref, state_ref, back_ref,
    column_ref, row_ref, scores_ref, mask_ref, pairs_ref, tail_ref, lead_ref, write_t, read_t,
):
    chunk = pl.program_id(0)
    lanes = x_ref.shape[1]
    head_size = lanes * pl.num_programs(0) // heads
    per_chunk = lanes // head_size

    @pl.when(chunk == 0)
    def _():
        rates = rates_ref[...]
        triangle = lower(STRETCH)
        running, tail, lead = decay_terms(rates, heads)
        column_ref[...] = running
        tail_ref[...] = tail
        lead_ref[...] = lead
        row_ref[...] = dot(rates, triangle, 1, 1, HIGHEST)
        mask_ref[...] = triangle
        scores_ref[...] = dot(read_ref[...], write_ref[...], 1, 1)
        pairs_ref[...] = jnp.zeros_like(pairs_ref)
        change_ref[...] = jnp.zeros_like(change_ref)
        write_t[...] = write_ref[...].astype(F32).T.astype(BF16)
        read_t[...] = read_ref[...].astype(F32).T.astype(BF16)

    columns = pltpu.roll(column_ref[...], STATE - chunk * per_chunk, 1)
    rows = row_ref[pl.ds(pl.multiple_of(chunk * per_chunk, per_chunk), per_chunk), :]
    causal = mask_ref[...] > 0.5
    scores = scores_ref[...]
    pairs = pairs_ref[...]
    low_half = iota((STRETCH, 2 * head_size), 1) < head_size
    adder = head_adder(chunk, head_size, lanes)
    spread = spreader(chunk, heads, head_size, lanes)
    high, low = term_pair(x_ref[...].astype(F32) * dot(tail_ref[...], spread, 1, 0))
    state_ref[...] = dot(write_t[...], high, 1, 0) + dot(write_t[...], low, 1, 0)
    high, low = term_pair(g_ref[...].astype(F32) * dot(lead_ref[...], spread, 1, 0))
    back_ref[...] = dot(read_t[...], high, 1, 0) + dot(read_t[...], low, 1, 0)
    for pair in range(per_chunk // 2):
        strip = slice(pair * 2 * head_size, (pair + 1) * 2 * head_size)
        x = x_ref[:, strip]
        g = g_ref[:, strip]
        ys, dxs = [], []
        for half in range(2):
            head = 2 * pair + half
            gap = columns[:, head : head + 1] - rows[head : head + 1, :]
            decay = jnp.where(causal, jnp.exp(gap), 0.0)
            mixing = (scores * decay).astype(BF16)
            ys.append(dot(mixing, x, 1, 0))
            dxs.append(dot(mixing, g, 0, 0))
            mine = low_half if half == 0 else jnp.logical_not(low_half)
            pairs = pairs + dot(jnp.where(mine, g, jnp.zeros_like(g)), x, 1, 1) * decay
        y = jnp.where(low_half, ys[0], ys[1])
        dx = jnp.where(low_half, dxs[0], dxs[1])
        dx_ref[:, strip] = dx
        change_ref[...] += head_sums(
            g.astype(F32) * y - x.astype(F32) * dx, adder[strip, :]
        )
    pairs_ref[...] = pairs

    @pl.when(chunk == pl.num_programs(0) - 1)
    def _():
        summed = pairs_ref[...].astype(BF16)
        db_ref[...] = dot(summed, read_ref[...], 0, 0)
        dc_ref[...] = dot(summed, write_ref[...], 1, 0)


def intra(after, x, g, write_map, read_map, rates):
    tokens, wide = x.shape
    heads = rates.shape[0]
    return pl.pallas_call(
        lambda *refs: intra_kernel(heads, *refs),
        grid=(wide // LANES,),
        in_specs=[
            whole(META, STRIP),
            lanes_of(tokens),
            lanes_of(tokens),
            whole(tokens, STATE),
            whole(tokens, STATE),
            whole(heads, tokens),
        ],
        out_specs=[lanes_of(tokens)] + [whole(tokens, STATE)] * 3 + [lanes_of(STATE)] * 2,
        out_shape=[
            jax.ShapeDtypeStruct((tokens, wide), F32),
            jax.ShapeDtypeStruct((tokens, STATE), F32),
            jax.ShapeDtypeStruct((tokens, STATE), F32),
            jax.ShapeDtypeStruct((tokens, STATE), F32),
            jax.ShapeDtypeStruct((STATE, wide), F32),
            jax.ShapeDtypeStruct((STATE, wide), F32),
        ],
        scratch_shapes=[
            pltpu.VMEM((tokens, STATE), F32),
            pltpu.VMEM((heads, tokens), F32),
            pltpu.VMEM((tokens, tokens), F32),
            pltpu.VMEM((tokens, tokens), F32),
            pltpu.VMEM((tokens, tokens), F32),
            pltpu.VMEM((tokens, STATE), BF16),
            pltpu.VMEM((tokens, STATE), BF16),
            pltpu.VMEM((STATE, tokens), BF16),
            pltpu.VMEM((STATE, tokens), BF16),
        ],
        compiler_params=pltpu.CompilerParams(vmem_limit_bytes=BIG_VMEM),
        cost_estimate=pl.CostEstimate(
            flops=12_000_000_000, bytes_accessed=8_000_000, transcendentals=heads * tokens * tokens
        ),
        name="intra",
    )(after, x, g, write_map, read_map, rates)


def assemble_kernel(
    heads, chips, place, first_log, state_own, back_own, *refs,
):
    first_refs, own_refs, far_refs = (refs[i * chips : (i + 1) * chips] for i in range(3))
    state_ref, back_ref, total_ref = refs[3 * chips :]
    chunk = pl.program_id(0)
    lanes = state_ref.shape[1]
    strips = lanes // STRIP
    head_size = lanes * pl.num_programs(0) // heads
    per_strip = STRIP // head_size
    part = STATE // chips

    @pl.when(chunk == 0)
    def _():
        total_ref[...] = jnp.zeros_like(total_ref)

    lane = iota((META, STRIP), 1)
    row = iota((META, STRIP), 0) + chunk * strips
    picked = jnp.where(lane // per_strip == row, jnp.exp(first_log[...]), 0.0)
    decay = dot(picked, lane_spread(per_strip, head_size), 1, 0, HIGHEST)
    is_first = place[0] == 0
    for step in range(chips):
        quarter = place[1] ^ step
        rows = pl.ds(pl.multiple_of(quarter * part, part), part)
        for strip in range(strips):
            wide = slice(strip * STRIP, (strip + 1) * STRIP)
            here = slice(strip * part, (strip + 1) * part)
            own = own_refs[step][here, :] * decay[strip : strip + 1, :]
            own = own + first_refs[step][here, :]
            far = far_refs[step][here, :]
            state_ref[rows, wide] = jnp.where(is_first, far, own).astype(BF16)
            back_ref[rows, wide] = jnp.where(is_first, own, far).astype(BF16)
    state = state_ref[...].astype(F32)
    back = back_ref[...].astype(F32)
    row_sum = jnp.sum(state * back_own[...] - back * state_own[...], axis=0, keepdims=True)
    total_ref[...] += head_sums(
        jnp.broadcast_to(row_sum, (META, lanes)), head_adder(chunk, head_size, lanes)
    )


def assemble(heads, chips, place, first, state_own, back_own, own, far):
    wide = state_own.shape[1]
    strips = wide // STRIP
    steps = wide // LANES
    part = STATE // chips
    block = LANES // STRIP * part
    meta_at = strips * STATE // META
    piece = pl.BlockSpec((block, STRIP), lambda c, place: (c, 0))
    lanes = pl.BlockSpec((STATE, LANES), lambda c, place: (0, c))

    def quarter(step):
        return pl.BlockSpec((block, STRIP), lambda c, place: ((place[1] ^ step) * steps + c, 0))

    return pl.pallas_call(
        lambda *refs: assemble_kernel(heads, chips, *refs),
        grid_spec=pltpu.PrefetchScalarGridSpec(
            num_scalar_prefetch=1,
            grid=(steps,),
            in_specs=[pl.BlockSpec((META, STRIP), lambda c, place: (meta_at, 0)), lanes, lanes]
            + [quarter(step) for step in range(chips)]
            + [piece] * (2 * chips),
            out_specs=[lanes, lanes, whole(META, STRIP)],
        ),
        out_shape=[
            jax.ShapeDtypeStruct((STATE, wide), BF16),
            jax.ShapeDtypeStruct((STATE, wide), BF16),
            jax.ShapeDtypeStruct((META, STRIP), F32),
        ],
        compiler_params=pltpu.CompilerParams(vmem_limit_bytes=BIG_VMEM),
        name="assemble",
    )(place, first, state_own, back_own, *([first] * chips), *own, *far)


def finish_kernel(
    heads, x_ref, g_ref, write_ref, read_ref, rates_ref,
    dx_ref, db_ref, dc_ref, change_ref, state_ref, back_ref,
    grad_ref, write_out, read_out, suffix_ref, tail_ref, lead_ref, sum_ref, db_sum, dc_sum,
):
    chunk = pl.program_id(0)
    lanes = x_ref.shape[1]
    head_size = lanes * pl.num_programs(0) // heads

    @pl.when(chunk == 0)
    def _():
        _, tail, lead = decay_terms(rates_ref[...], heads)
        tail_ref[...] = tail
        lead_ref[...] = lead
        sum_ref[...] = change_ref[...]
        db_sum[...] = db_ref[...]
        dc_sum[...] = dc_ref[...]

    state = state_ref[...]
    back = back_ref[...]
    spread = spreader(chunk, heads, head_size, lanes)
    tail = dot(tail_ref[...], spread, 1, 0)
    lead = dot(lead_ref[...], spread, 1, 0)
    x = x_ref[...].astype(F32)
    g = g_ref[...].astype(F32)
    y = dot(read_ref[...], state, 1, 0) * lead
    dx = dot(write_ref[...], back, 1, 0) * tail
    grad_ref[...] = (dx_ref[...] + dx).astype(BF16)
    sum_ref[...] += head_sums(g * y - x * dx, head_adder(chunk, head_size, lanes))
    db_sum[...] += dot((x * tail).astype(BF16), back, 1, 1)
    dc_sum[...] += dot((g * lead).astype(BF16), state, 1, 1)

    @pl.when(chunk == pl.num_programs(0) - 1)
    def _():
        write_out[...] = db_sum[...].astype(BF16)
        read_out[...] = dc_sum[...].astype(BF16)
        suffix_ref[...] = dot(sum_ref[...], lower(STRETCH), 0, 0, HIGHEST)[:heads, :]


def finish(x, g, write_map, read_map, rates, parts, state, back):
    tokens, wide = x.shape
    heads = rates.shape[0]
    return pl.pallas_call(
        lambda *refs: finish_kernel(heads, *refs),
        grid=(wide // LANES,),
        in_specs=[
            lanes_of(tokens),
            lanes_of(tokens),
            whole(tokens, STATE),
            whole(tokens, STATE),
            whole(heads, tokens),
            lanes_of(tokens),
            whole(tokens, STATE),
            whole(tokens, STATE),
            whole(tokens, STATE),
            lanes_of(STATE),
            lanes_of(STATE),
        ],
        out_specs=[
            lanes_of(tokens),
            whole(tokens, STATE),
            whole(tokens, STATE),
            whole(heads, tokens),
        ],
        out_shape=[
            jax.ShapeDtypeStruct((tokens, wide), BF16),
            jax.ShapeDtypeStruct((tokens, STATE), BF16),
            jax.ShapeDtypeStruct((tokens, STATE), BF16),
            jax.ShapeDtypeStruct((heads, tokens), F32),
        ],
        scratch_shapes=[
            pltpu.VMEM((tokens, STATE), BF16),
            pltpu.VMEM((tokens, STATE), BF16),
            pltpu.VMEM((tokens, STATE), F32),
            pltpu.VMEM((tokens, STATE), F32),
            pltpu.VMEM((tokens, STATE), F32),
        ],
        compiler_params=pltpu.CompilerParams(vmem_limit_bytes=BIG_VMEM),
        cost_estimate=pl.CostEstimate(
            flops=6_000_000_000, bytes_accessed=9_000_000, transcendentals=tokens * STATE * 2
        ),
        name="finish",
    )(x, g, write_map, read_map, rates, *parts, state, back)


def per_device(inputs, out_grad, input_map, output_map, log_decay):
    heads = log_decay.shape[0]
    head_size = inputs.shape[1] // heads
    groups, shards = lax.axis_size("grp"), lax.axis_size("seq")
    chips = shards // 2
    shard = lax.axis_index("seq")
    chip, core = shard // 2, shard % 2
    place = jnp.stack([core, chip]).astype(jnp.int32)
    everyone = [(a, z, c) for a in range(groups) for z in range(chips) for c in range(2)]

    def move(value, target):
        pairs = []
        for a, z, c in everyone:
            to = target(a, z, c)
            if to is not None:
                pairs.append((a * shards + 2 * z + c, to[0] * shards + 2 * to[1] + to[2]))
        return lax.ppermute(value, ("grp", "seq"), pairs)

    def to_core(value):
        return move(value, lambda a, z, c: (a, z, 1 - c))

    def to_chip(value, step):
        return move(value, lambda a, z, c: (a, z ^ step, c)) if step else value

    def to_group(value, step, ahead):
        def target(a, z, c):
            to = a + step if ahead(c) else a - step
            return (to, z, c) if 0 <= to < groups else None

        return move(value, target)

    send, keep, decay = summary(
        chips, place, inputs, out_grad, input_map, output_map, log_decay
    )
    first = to_core(send)
    at = combine(chips, place, first, keep, decay, log_decay)
    parts = intra(at[0][-META:], inputs, out_grad, input_map, output_map, log_decay)
    at = [to_chip(value, step) for step, value in enumerate(at)]
    total = group_total(head_size, place, parts[3][:META], at)
    got = [to_group(total, step, lambda c: c == 1) for step in range(1, groups)]
    own = [to_chip(value, step) for step, value in enumerate(enter(head_size, place, at, got))]
    far = [to_core(value) for value in own]
    state, back, tally = assemble(heads, chips, place, first, parts[4], parts[5], own, far)
    grad_inputs, grad_write, grad_read, suffix = finish(
        inputs, out_grad, input_map, output_map, log_decay, parts[:4], state, back
    )

    other = to_core(tally)
    later = jnp.where(core == 0, other, 0.0)
    tally = tally + other
    steps = [to_chip(tally, step) for step in range(1, chips)]
    for step, value in enumerate(steps, 1):
        later = later + jnp.where((chip ^ step) > chip, value, 0.0)
        tally = tally + value
    for step in range(1, groups):
        later = later + to_group(tally, step, lambda c: False)
    return (grad_inputs, grad_write, grad_read, suffix + later[0, :heads][:, None])


def solution(mesh):
    tokens = P(("grp", "seq"), None)
    in_specs = (tokens, tokens, tokens, tokens, P(None, ("grp", "seq")))
    out_specs = (tokens, tokens, tokens, P(None, ("grp", "seq")))
    return jax.shard_map(
        per_device, mesh=mesh, in_specs=in_specs, out_specs=out_specs, check_vma=False
    )
```

time: 207 us -> 129 us (0.62)
  blocking collectives: 86.1 us -> 0 us
  local copies, waits for them, and re-layouts: 21.6 us -> 4.48 us
  Pallas kernels: 24.4 us -> 40.1 us
  starting transfers between devices: 18.6 us -> 28.8 us
  other arithmetic: 8.58 us -> 2.79 us
  waiting for transfers between devices: 45.4 us -> 50.4 us
    unnamed x1 -> x0, blocking collectives: 43.5 us -> none
    all_gather x1 -> x0, blocking collectives: 42.6 us -> none  [per_device(): lax.all_gather(totals[7:8, :heads], ('grp', 'seq'), axis=0, tiled=True)]
    unnamed x59 -> x26, local copies, waits for them, and re-layouts: 16.5 us -> 3.21 us
    pallas_call x2 -> x6, Pallas kernels: 13.7 us -> 26.1 us  [the longest x1 9.26 us: finish(): pl.pallas_call(lambda *refs: finish_kernel(heads, *refs), grid=(wide // L...]
    ppermute x14 -> x21, starting transfers between devices: 18.6 us -> 28.8 us  [move(): return lax.ppermute(value, ('grp', 'seq'), pairs)]
    ppermute x14 -> x21, waiting for transfers between devices: 45.4 us -> 50.4 us  [move(): return lax.ppermute(value, ('grp', 'seq'), pairs)]
    add x6 -> x4, other arithmetic: 6.55 us -> 2.19 us  [the longest x1 1.47 us: per_device(): suffix + later[0, :heads][:, None]]
    pallas_call x1, Pallas kernels: 10.7 us -> 14.1 us  [intra(): pl.pallas_call(lambda *refs: intra_kernel(heads, *refs), grid=(wide // LA...]
  transfers between devices with their start and end apart: 14 -> 21, of which waited for: 6 -> 12; matrix products, arithmetic and copies ran while one was open for 4% -> 1% of each run, Pallas kernels for 5% -> 18%
where the time goes in v2:
time: 129 us; the launch traced here: 127 us
  waiting for transfers between devices  50.4 us (39%)
  Pallas kernels  40.1 us (31%)
  starting transfers between devices  28.8 us (22%)
  local copies, waits for them, and re-layouts  4.48 us (3%)
  other arithmetic  2.79 us (2%)
    ppermute x21, waiting for transfers between devices, move(): return lax.ppermute(value, ('grp', 'seq'), pairs)  50.4 us
    ppermute x21, starting transfers between devices, move(): return lax.ppermute(value, ('grp', 'seq'), pairs)  28.8 us
    pallas_call x1, Pallas kernels, intra(): pl.pallas_call(lambda *refs: intra_kernel(heads, *refs), grid=(wide // LA...  14.1 us
    pallas_call x1, Pallas kernels, finish(): pl.pallas_call(lambda *refs: finish_kernel(heads, *refs), grid=(wide // L...  9.26 us
    pallas_call x1, Pallas kernels, assemble(): pl.pallas_call(lambda *refs: assemble_kernel(heads, chips, *refs), grid_s...  7.08 us
    pallas_call x1, Pallas kernels, summary(): pl.pallas_call(lambda *refs: summary_kernel(heads, chips, *refs), grid=(w...  6.81 us
    unnamed x26, local copies, waits for them, and re-layouts  3.21 us
  transfers between devices with their start and end apart: 21, of which 12 were waited for; matrix products, arithmetic and copies ran while one was open for 1% of the time, Pallas kernels for 18%

profile of v2, /device:TPU:0, one launch (start us, length us, event | category | flops | bytes accessed | tf_op | source)
XLA Modules:
  0.0 127.4 jit_solution(17426939390217960627)
XLA Ops:
  0.6 0.6 pad_add_fusion.refs_0_
  1.3 6.8 %summary.1 = (f32[2568,128]{1,0:T(8,128)}, f32[2560,128]{1,0:T(8,128)}, f32[20,128]{1,0:T(8,128)}) custom-call(s32[2]{0:T(128)} %pad_add_fusion.refs_0_, bf16[256,2560]{1,0:T(8,128)(2,1)} %refs_0_.1, bf16[256,2560]{1,0:T(8,128)(2,1)} %refs_1_.5, bf16[256,128]{1,0:T(8,128)(2,1)} %refs_2_.5, bf16[256,128]{1,0:T(8,128)(2,1)} %refs_3_.5, f32[40,256]{1,0:T(8,128)} %refs_4_.7), custom_call_target="tpu_custom_call" | custom-call | tf_op jit(solution)/shard_map/summary/pallas_call | solution.py:161
  8.1 0.5 collective-permute-start
  8.5 2.9 %collective-permute-done.refs_1_.refs_4_.refs_5_.refs_6_.refs_7_ = f32[2568,128]{1,0:T(8,128)S(1)} collective-permute-done((f32[2568,128]{1,0:T(8,128)}, f32[2568,128]{1,0:T(8,128)S(1)}, u32[]{:S(2)}, u32[]{:S(2)}) %collective-permute-start) | collective-permute-done | bytes 1314848 | tf_op jit(solution)/shard_map/ppermute | solution.py:617
  11.4 0.0 copy-done.3
  11.4 0.0 copy-done.4
  11.4 1.8 %copy-done.1 = f32[2560,128]{1,0:T(8,128)S(1)} copy-done((f32[2560,128]{1,0:T(8,128)S(1)}, f32[2560,128]{1,0:T(8,128)}, u32[]{:S(2)}) %copy-start.1) | copy-done | bytes 1310744
  13.2 0.7 copy-done.5
  13.9 0.7 combine.1
  14.6 0.0 copy-done
  14.6 0.6 slice.9.refs_0_
  15.2 2.9 %collective-permute-start.1 = (f32[648,128]{1,0:T(8,128)S(1)}, f32[648,128]{1,0:T(8,128)S(1)}, u32[]{:S(2)}, u32[]{:S(2)}) collective-permute-start(f32[648,128]{1,0:T(8,128)S(1)} %get-tuple-element.38), channel_id=1, source_target_pairs={{0,2},{1,3},{2,0},{3,1},{4,6},{5,7},{6,4},{7,5},{8,10},{9,11},{10,... | collective-permute-start | bytes 995336 | tf_op jit(solution)/shard_map/ppermute | solution.py:617
  18.2 2.6 %collective-permute-start.2 = (f32[648,128]{1,0:T(8,128)S(1)}, f32[648,128]{1,0:T(8,128)S(1)}, u32[]{:S(2)}, u32[]{:S(2)}) collective-permute-start(f32[648,128]{1,0:T(8,128)S(1)} %get-tuple-element.39), channel_id=1, source_target_pairs={{0,4},{1,5},{2,6},{3,7},{4,0},{5,1},{6,2},{7,3},{8,12},{9,13},{10,... | collective-permute-start | bytes 995336 | tf_op jit(solution)/shard_map/ppermute | solution.py:617
  20.8 0.0 collective-permute-start.3
  20.8 14.1 %intra.1 = (f32[256,2560]{1,0:T(8,128)}, f32[256,128]{1,0:T(8,128)}, f32[256,128]{1,0:T(8,128)}, f32[256,128]{1,0:T(8,128)}, f32[128,2560]{1,0:T(8,128)}, /*index=5*/f32[128,2560]{1,0:T(8,128)}) custom-call(f32[8,128]{1,0:T(8,128)} %slice.9.refs_0_, bf16[256,2560]{1,0:T(8,128)(2,1)} %refs_0_.1, bf16[256,2560]{1,0:T(8,128)(2,1)} %refs_1_.5, ...), custom_call_target="tpu_custom_call" | custom-call | flops 12000000000 | bytes 8000000 | tf_op jit(solution)/shard_map/intra/pallas_call | solution.py:404
  34.8 0.7 slice.10.refs_1_
  35.5 0.0 collective-permute-done.1.refs_3_.refs_2_
  35.5 8.5 %collective-permute-done.2.refs_4_.refs_3_ = f32[648,128]{1,0:T(8,128)S(1)} collective-permute-done((f32[648,128]{1,0:T(8,128)S(1)}, f32[648,128]{1,0:T(8,128)S(1)}, u32[]{:S(2)}, u32[]{:S(2)}) %collective-permute-start.2) | collective-permute-done | bytes 331808 | tf_op jit(solution)/shard_map/ppermute | solution.py:617
  44.0 0.0 collective-permute-done.3.refs_5_.refs_4_
  44.0 0.8 group_total.1
  44.8 1.3 %collective-permute-start.4 = (f32[648,128]{1,0:T(8,128)S(1)}, f32[648,128]{1,0:T(8,128)S(1)}, u32[]{:S(2)}, u32[]{:S(2)}) collective-permute-start(f32[648,128]{1,0:T(8,128)S(1)} %group_total.1), channel_id=1, source_target_pairs={{1,9},{3,11},{5,13},{7,15},{8,0},{9,17},{10,2},{11,19},{12,4},{13,... | collective-permute-start | bytes 995336 | tf_op jit(solution)/shard_map/ppermute | solution.py:617
  46.1 1.3 %collective-permute-start.5 = (f32[648,128]{1,0:T(8,128)S(1)}, f32[648,128]{1,0:T(8,128)S(1)}, u32[]{:S(2)}, u32[]{:S(2)}) collective-permute-start(f32[648,128]{1,0:T(8,128)S(1)} %group_total.1), channel_id=1, source_target_pairs={{1,17},{3,19},{5,21},{7,23},{9,25},{11,27},{13,29},{15,31},{16,0},... | collective-permute-start | bytes 995336 | tf_op jit(solution)/shard_map/ppermute | solution.py:617
  47.4 1.3 %collective-permute-start.6 = (f32[648,128]{1,0:T(8,128)S(1)}, f32[648,128]{1,0:T(8,128)S(1)}, u32[]{:S(2)}, u32[]{:S(2)}) collective-permute-start(f32[648,128]{1,0:T(8,128)S(1)} %group_total.1), channel_id=1, source_target_pairs={{1,25},{3,27},{5,29},{7,31},{24,0},{26,2},{28,4},{30,6}} | collective-permute-start | bytes 995336 | tf_op jit(solution)/shard_map/ppermute | solution.py:617
  48.7 6.7 %collective-permute-done.4.refs_5_ = f32[648,128]{1,0:T(8,128)S(1)} collective-permute-done((f32[648,128]{1,0:T(8,128)S(1)}, f32[648,128]{1,0:T(8,128)S(1)}, u32[]{:S(2)}, u32[]{:S(2)}) %collective-permute-start.4) | collective-permute-done | bytes 331808 | tf_op jit(solution)/shard_map/ppermute | solution.py:617
  55.4 4.2 %collective-permute-done.5.refs_6_ = f32[648,128]{1,0:T(8,128)S(1)} collective-permute-done((f32[648,128]{1,0:T(8,128)S(1)}, f32[648,128]{1,0:T(8,128)S(1)}, u32[]{:S(2)}, u32[]{:S(2)}) %collective-permute-start.5) | collective-permute-done | bytes 331808 | tf_op jit(solution)/shard_map/ppermute | solution.py:617
  59.6 0.0 collective-permute-done.6.refs_7_
  59.6 1.4 %enter.1 = (f32[640,128]{1,0:T(8,128)S(1)}, f32[640,128]{1,0:T(8,128)S(1)}, f32[640,128]{1,0:T(8,128)S(1)}, f32[640,128]{1,0:T(8,128)S(1)}) custom-call(s32[2]{0:T(128)S(1)} %copy-done.4, f32[648,128]{1,0:T(8,128)S(1)} %get-tuple-element.31.refs_2_.refs_1_, f32[648,128]{1,0:T(8,128)S(1)} %collective-permute-done.1.refs_3_.refs_2_, ...), custom_call_target="tpu_custom_call" | custom-call | tf_op jit(solution)/shard_map/enter/pallas_call | solution.py:324
  61.0 6.7 %collective-permute-start.7 = (f32[640,128]{1,0:T(8,128)S(1)}, f32[640,128]{1,0:T(8,128)S(1)}, u32[]{:S(2)}, u32[]{:S(2)}) collective-permute-start(f32[640,128]{1,0:T(8,128)S(1)} %get-tuple-element.42), channel_id=1, source_target_pairs={{0,2},{1,3},{2,0},{3,1},{4,6},{5,7},{6,4},{7,5},{8,10},{9,11},{10,... | collective-permute-start | bytes 983048 | tf_op jit(solution)/shard_map/ppermute | solution.py:617
  67.7 1.1 collective-permute-start.8
  68.8 1.4 %collective-permute-start.9 = (f32[640,128]{1,0:T(8,128)S(1)}, f32[640,128]{1,0:T(8,128)S(1)}, u32[]{:S(2)}, u32[]{:S(2)}) collective-permute-start(f32[640,128]{1,0:T(8,128)S(1)} %get-tuple-element.44), channel_id=1, source_target_pairs={{0,6},{1,7},{2,4},{3,5},{4,2},{5,3},{6,0},{7,1},{8,14},{9,15},{10,... | collective-permute-start | bytes 983048 | tf_op jit(solution)/shard_map/ppermute | solution.py:617
  70.2 0.0 collective-permute-start.10
  70.2 6.5 %collective-permute-done.7.refs_9_ = f32[640,128]{1,0:T(8,128)S(1)} collective-permute-done((f32[640,128]{1,0:T(8,128)S(1)}, f32[640,128]{1,0:T(8,128)S(1)}, u32[]{:S(2)}, u32[]{:S(2)}) %collective-permute-start.7) | collective-permute-done | bytes 327712 | tf_op jit(solution)/shard_map/ppermute | solution.py:617
  76.7 0.0 collective-permute-start.11
  76.7 15.3 %collective-permute-done.8.refs_10_ = f32[640,128]{1,0:T(8,128)S(1)} collective-permute-done((f32[640,128]{1,0:T(8,128)S(1)}, f32[640,128]{1,0:T(8,128)S(1)}, u32[]{:S(2)}, u32[]{:S(2)}) %collective-permute-start.8) | collective-permute-done | bytes 327712 | tf_op jit(solution)/shard_map/ppermute | solution.py:617
  92.0 0.0 collective-permute-start.12
  92.0 0.0 collective-permute-done.9.refs_11_
  92.1 0.5 collective-permute-start.13
  92.6 0.0 collective-permute-done.10.refs_12_
  92.6 0.0 collective-permute-done.11.refs_13_
  92.6 1.1 collective-permute-done.12.refs_14_
  93.7 0.5 collective-permute-done.13.refs_15_
  94.1 0.0 copy-done.8
  94.2 0.0 copy-done.9
  94.2 0.0 copy-done.10
  94.2 0.2 copy-done.11
  94.4 0.4 copy-done.12
  94.8 7.1 %assemble.1 = (bf16[128,2560]{1,0:T(8,128)(2,1)}, bf16[128,2560]{1,0:T(8,128)(2,1)}, f32[8,128]{1,0:T(8,128)}) custom-call(s32[2]{0:T(128)} %pad_add_fusion.refs_0_, f32[2568,128]{1,0:T(8,128)} %copy-done, f32[128,2560]{1,0:T(8,128)} %get-tuple-element.36.refs_2_, f32[128,2560]{1,0:T(8,128)} %get-tuple-element.37.refs_3_, f32[2568,128]{1,0:T(8,128)} %copy-done, ...), custom_call_target="tpu_custom_call" | custom-call | tf_op jit(solution)/shard_map/assemble/pallas_call | solution.py:496
  101.9 0.2 collective-permute-start.14
  102.1 1.2 collective-permute-done.14
  103.4 0.7 add.46
  104.1 2.0 %collective-permute-start.17 = (f32[8,128]{1,0:T(8,128)S(1)}, f32[8,128]{1,0:T(8,128)S(1)}, u32[]{:S(2)}, u32[]{:S(2)}) collective-permute-start(f32[8,128]{1,0:T(8,128)S(1)} %add.46), channel_id=1, source_target_pairs={{0,6},{1,7},{2,4},{3,5},{4,2},{5,3},{6,0},{7,1},{8,14},{9,15},{10,... | collective-permute-start | bytes 12296 | tf_op jit(solution)/shard_map/ppermute | solution.py:617
  106.0 3.1 %collective-permute-start.16 = (f32[8,128]{1,0:T(8,128)S(1)}, f32[8,128]{1,0:T(8,128)S(1)}, u32[]{:S(2)}, u32[]{:S(2)}) collective-permute-start(f32[8,128]{1,0:T(8,128)S(1)} %add.46), channel_id=1, source_target_pairs={{0,4},{1,5},{2,6},{3,7},{4,0},{5,1},{6,2},{7,3},{8,12},{9,13},{10,... | collective-permute-start | bytes 12296 | tf_op jit(solution)/shard_map/ppermute | solution.py:617
  109.1 0.1 collective-permute-start.15
  109.2 0.2 collective-permute-done.17
  109.5 1.3 %collective-permute-done.16 = f32[8,128]{1,0:T(8,128)S(1)} collective-permute-done((f32[8,128]{1,0:T(8,128)S(1)}, f32[8,128]{1,0:T(8,128)S(1)}, u32[]{:S(2)}, u32[]{:S(2)}) %collective-permute-start.16) | collective-permute-done | bytes 4128 | tf_op jit(solution)/shard_map/ppermute | solution.py:617
  110.8 2.0 %collective-permute-done.15 = f32[8,128]{1,0:T(8,128)S(1)} collective-permute-done((f32[8,128]{1,0:T(8,128)S(1)}, f32[8,128]{1,0:T(8,128)S(1)}, u32[]{:S(2)}, u32[]{:S(2)}) %collective-permute-start.15) | collective-permute-done | bytes 4128 | tf_op jit(solution)/shard_map/ppermute | solution.py:617
  112.7 1.3 %collective-permute-start.20 = (f32[8,128]{1,0:T(8,128)S(1)}, f32[8,128]{1,0:T(8,128)S(1)}, u32[]{:S(2)}, u32[]{:S(2)}) collective-permute-start(f32[8,128]{1,0:T(8,128)S(1)} %add_add_fusion.1), channel_id=1, source_target_pairs={{24,0},{25,1},{26,2},{27,3},{28,4},{29,5},{30,6},{31,7}} | collective-permute-start | bytes 12296 | tf_op jit(solution)/shard_map/ppermute | solution.py:617
  114.0 1.3 %collective-permute-start.19 = (f32[8,128]{1,0:T(8,128)S(1)}, f32[8,128]{1,0:T(8,128)S(1)}, u32[]{:S(2)}, u32[]{:S(2)}) collective-permute-start(f32[8,128]{1,0:T(8,128)S(1)} %add_add_fusion.1), channel_id=1, source_target_pairs={{16,0},{17,1},{18,2},{19,3},{20,4},{21,5},{22,6},{23,7},{24,8},{25... | collective-permute-start | bytes 12296 | tf_op jit(solution)/shard_map/ppermute | solution.py:617
  115.3 1.3 %collective-permute-start.18 = (f32[8,128]{1,0:T(8,128)S(1)}, f32[8,128]{1,0:T(8,128)S(1)}, u32[]{:S(2)}, u32[]{:S(2)}) collective-permute-start(f32[8,128]{1,0:T(8,128)S(1)} %add_add_fusion.1), channel_id=1, source_target_pairs={{8,0},{9,1},{10,2},{11,3},{12,4},{13,5},{14,6},{15,7},{16,8},{17,9... | collective-permute-start | bytes 12296 | tf_op jit(solution)/shard_map/ppermute | solution.py:617
  116.6 9.3 %finish.1 = (bf16[256,2560]{1,0:T(8,128)(2,1)}, bf16[256,128]{1,0:T(8,128)(2,1)}, bf16[256,128]{1,0:T(8,128)(2,1)}, f32[40,256]{1,0:T(8,128)}) custom-call(bf16[256,2560]{1,0:T(8,128)(2,1)} %refs_0_.1, bf16[256,2560]{1,0:T(8,128)(2,1)} %refs_1_.5, bf16[256,128]{1,0:T(8,128)(2,1)} %refs_2_.5, bf16[256,128]{1,0:T(8,128)(2,1)} %refs_3_.5, f32[40,256]{1,0:T(8,128)} %refs_4_.7, ...), custom_call_target="tpu_custom_call" | custom-call | flops 6000000000 | bytes 9000000 | tf_op jit(solution)/shard_map/finish/pallas_call | solution.py:558
  125.9 0.0 collective-permute-done.20
  125.9 0.0 collective-permute-done.19
  125.9 0.0 collective-permute-done.18
  126.0 1.5 %broadcast_add_fusion = f32[40,256]{1,0:T(8,128)} fusion(f32[40,256]{1,0:T(8,128)} %get-tuple-element.50, f32[40]{0:T(128)S(1)} %slice_bitcast_fusion), kind=kLoop, calls=%fused_computation | loop fusion | flops 10240 | bytes 82080 | tf_op jit(solution)/shard_map/add | solution.py:657
  (19 shorter events, 0.1 us)
Async XLA Ops:
  1.3 10.2 %copy-start.3 = (f32[40,256]{1,0:T(8,128)S(1)}, f32[40,256]{1,0:T(8,128)}, u32[]{:S(2)}) copy-start(f32[40,256]{1,0:T(8,128)} %refs_4_.7) | copy-start | bytes 122884
  1.3 10.2 %copy-start.4 = (s32[2]{0:T(128)S(1)}, s32[2]{0:T(128)}, u32[]{:S(2)}) copy-start(s32[2]{0:T(128)} %pad_add_fusion.refs_0_) | copy-start | bytes 28
  8.1 3.3 %collective-permute-start = (f32[2568,128]{1,0:T(8,128)}, f32[2568,128]{1,0:T(8,128)S(1)}, u32[]{:S(2)}, u32[]{:S(2)}) collective-permute-start(f32[2568,128]{1,0:T(8,128)} %get-tuple-element.28), channel_id=1, source_target_pairs={{0,1},{1,0},{2,3},{3,2},{4,5},{5,4},{6,7},{7,6},{8,9},{9,8},{10,11... | collective-permute-start | bytes 3944456 | tf_op jit(solution)/shard_map/ppermute | solution.py:617
  11.4 3.2 %copy-start = (f32[2568,128]{1,0:T(8,128)}, f32[2568,128]{1,0:T(8,128)S(1)}, u32[]{:S(2)}) copy-start(f32[2568,128]{1,0:T(8,128)S(1)} %collective-permute-done.refs_1_.refs_4_.refs_5_.refs_6_.refs_7_) | copy-start | bytes 3944452
  11.4 1.8 %copy-start.1 = (f32[2560,128]{1,0:T(8,128)S(1)}, f32[2560,128]{1,0:T(8,128)}, u32[]{:S(2)}) copy-start(f32[2560,128]{1,0:T(8,128)} %get-tuple-element.29.refs_2_) | copy-start | bytes 3932164
  13.2 0.7 copy-start.5
  15.2 20.3 %collective-permute-start.1 = (f32[648,128]{1,0:T(8,128)S(1)}, f32[648,128]{1,0:T(8,128)S(1)}, u32[]{:S(2)}, u32[]{:S(2)}) collective-permute-start(f32[648,128]{1,0:T(8,128)S(1)} %get-tuple-element.38), channel_id=1, source_target_pairs={{0,2},{1,3},{2,0},{3,1},{4,6},{5,7},{6,4},{7,5},{8,10},{9,11},{10,... | collective-permute-start | bytes 995336 | tf_op jit(solution)/shard_map/ppermute | solution.py:617
  18.2 25.8 %collective-permute-start.2 = (f32[648,128]{1,0:T(8,128)S(1)}, f32[648,128]{1,0:T(8,128)S(1)}, u32[]{:S(2)}, u32[]{:S(2)}) collective-permute-start(f32[648,128]{1,0:T(8,128)S(1)} %get-tuple-element.39), channel_id=1, source_target_pairs={{0,4},{1,5},{2,6},{3,7},{4,0},{5,1},{6,2},{7,3},{8,12},{9,13},{10,... | collective-permute-start | bytes 995336 | tf_op jit(solution)/shard_map/ppermute | solution.py:617
  20.8 23.2 %collective-permute-start.3 = (f32[648,128]{1,0:T(8,128)S(1)}, f32[648,128]{1,0:T(8,128)S(1)}, u32[]{:S(2)}, u32[]{:S(2)}) collective-permute-start(f32[648,128]{1,0:T(8,128)S(1)} %get-tuple-element.40), channel_id=1, source_target_pairs={{0,6},{1,7},{2,4},{3,5},{4,2},{5,3},{6,0},{7,1},{8,14},{9,15},{10,... | collective-permute-start | bytes 995336 | tf_op jit(solution)/shard_map/ppermute | solution.py:617
  44.8 10.6 %collective-permute-start.4 = (f32[648,128]{1,0:T(8,128)S(1)}, f32[648,128]{1,0:T(8,128)S(1)}, u32[]{:S(2)}, u32[]{:S(2)}) collective-permute-start(f32[648,128]{1,0:T(8,128)S(1)} %group_total.1), channel_id=1, source_target_pairs={{1,9},{3,11},{5,13},{7,15},{8,0},{9,17},{10,2},{11,19},{12,4},{13,... | collective-permute-start | bytes 995336 | tf_op jit(solution)/shard_map/ppermute | solution.py:617
  46.1 13.5 %collective-permute-start.5 = (f32[648,128]{1,0:T(8,128)S(1)}, f32[648,128]{1,0:T(8,128)S(1)}, u32[]{:S(2)}, u32[]{:S(2)}) collective-permute-start(f32[648,128]{1,0:T(8,128)S(1)} %group_total.1), channel_id=1, source_target_pairs={{1,17},{3,19},{5,21},{7,23},{9,25},{11,27},{13,29},{15,31},{16,0},... | collective-permute-start | bytes 995336 | tf_op jit(solution)/shard_map/ppermute | solution.py:617
  47.4 12.2 %collective-permute-start.6 = (f32[648,128]{1,0:T(8,128)S(1)}, f32[648,128]{1,0:T(8,128)S(1)}, u32[]{:S(2)}, u32[]{:S(2)}) collective-permute-start(f32[648,128]{1,0:T(8,128)S(1)} %group_total.1), channel_id=1, source_target_pairs={{1,25},{3,27},{5,29},{7,31},{24,0},{26,2},{28,4},{30,6}} | collective-permute-start | bytes 995336 | tf_op jit(solution)/shard_map/ppermute | solution.py:617
  61.0 33.1 %copy-start.2 = (f32[640,128]{1,0:T(8,128)}, f32[640,128]{1,0:T(8,128)S(1)}, u32[]{:S(2)}) copy-start(f32[640,128]{1,0:T(8,128)S(1)} %get-tuple-element.41.refs_8_) | copy-start | bytes 983044
  61.0 15.7 %collective-permute-start.7 = (f32[640,128]{1,0:T(8,128)S(1)}, f32[640,128]{1,0:T(8,128)S(1)}, u32[]{:S(2)}, u32[]{:S(2)}) collective-permute-start(f32[640,128]{1,0:T(8,128)S(1)} %get-tuple-element.42), channel_id=1, source_target_pairs={{0,2},{1,3},{2,0},{3,1},{4,6},{5,7},{6,4},{7,5},{8,10},{9,11},{10,... | collective-permute-start | bytes 983048 | tf_op jit(solution)/shard_map/ppermute | solution.py:617
  67.7 24.4 %collective-permute-start.8 = (f32[640,128]{1,0:T(8,128)S(1)}, f32[640,128]{1,0:T(8,128)S(1)}, u32[]{:S(2)}, u32[]{:S(2)}) collective-permute-start(f32[640,128]{1,0:T(8,128)S(1)} %get-tuple-element.43), channel_id=1, source_target_pairs={{0,4},{1,5},{2,6},{3,7},{4,0},{5,1},{6,2},{7,3},{8,12},{9,13},{10,... | collective-permute-start | bytes 983048 | tf_op jit(solution)/shard_map/ppermute | solution.py:617
  68.8 23.3 %collective-permute-start.9 = (f32[640,128]{1,0:T(8,128)S(1)}, f32[640,128]{1,0:T(8,128)S(1)}, u32[]{:S(2)}, u32[]{:S(2)}) collective-permute-start(f32[640,128]{1,0:T(8,128)S(1)} %get-tuple-element.44), channel_id=1, source_target_pairs={{0,6},{1,7},{2,4},{3,5},{4,2},{5,3},{6,0},{7,1},{8,14},{9,15},{10,... | collective-permute-start | bytes 983048 | tf_op jit(solution)/shard_map/ppermute | solution.py:617
  70.2 22.4 %collective-permute-start.10 = (f32[640,128]{1,0:T(8,128)S(1)}, f32[640,128]{1,0:T(8,128)S(1)}, u32[]{:S(2)}, u32[]{:S(2)}) collective-permute-start(f32[640,128]{1,0:T(8,128)S(1)} %get-tuple-element.41.refs_8_), channel_id=1, source_target_pairs={{0,1},{1,0},{2,3},{3,2},{4,5},{5,4},{6,7},{7,6},{8,9},{9,8},{10,11... | collective-permute-start | bytes 983048 | tf_op jit(solution)/shard_map/ppermute | solution.py:617
  76.7 17.5 %copy-start.6 = (f32[640,128]{1,0:T(8,128)}, f32[640,128]{1,0:T(8,128)S(1)}, u32[]{:S(2)}) copy-start(f32[640,128]{1,0:T(8,128)S(1)} %collective-permute-done.7.refs_9_) | copy-start | bytes 983044
  76.7 15.9 %collective-permute-start.11 = (f32[640,128]{1,0:T(8,128)S(1)}, f32[640,128]{1,0:T(8,128)S(1)}, u32[]{:S(2)}, u32[]{:S(2)}) collective-permute-start(f32[640,128]{1,0:T(8,128)S(1)} %collective-permute-done.7.refs_9_), channel_id=1, source_target_pairs={{0,1},{1,0},{2,3},{3,2},{4,5},{5,4},{6,7},{7,6},{8,9},{9,8},{10,11... | collective-permute-start | bytes 983048 | tf_op jit(solution)/shard_map/ppermute | solution.py:617
  92.0 2.1 %copy-start.7 = (f32[640,128]{1,0:T(8,128)}, f32[640,128]{1,0:T(8,128)S(1)}, u32[]{:S(2)}) copy-start(f32[640,128]{1,0:T(8,128)S(1)} %collective-permute-done.8.refs_10_) | copy-start | bytes 983044
  92.0 1.6 %collective-permute-start.12 = (f32[640,128]{1,0:T(8,128)S(1)}, f32[640,128]{1,0:T(8,128)S(1)}, u32[]{:S(2)}, u32[]{:S(2)}) collective-permute-start(f32[640,128]{1,0:T(8,128)S(1)} %collective-permute-done.8.refs_10_), channel_id=1, source_target_pairs={{0,1},{1,0},{2,3},{3,2},{4,5},{5,4},{6,7},{7,6},{8,9},{9,8},{10,11... | collective-permute-start | bytes 983048 | tf_op jit(solution)/shard_map/ppermute | solution.py:617
  92.0 2.1 %copy-start.8 = (f32[640,128]{1,0:T(8,128)}, f32[640,128]{1,0:T(8,128)S(1)}, u32[]{:S(2)}) copy-start(f32[640,128]{1,0:T(8,128)S(1)} %collective-permute-done.9.refs_11_) | copy-start | bytes 983044
  92.1 2.1 %collective-permute-start.13 = (f32[640,128]{1,0:T(8,128)S(1)}, f32[640,128]{1,0:T(8,128)S(1)}, u32[]{:S(2)}, u32[]{:S(2)}) collective-permute-start(f32[640,128]{1,0:T(8,128)S(1)} %collective-permute-done.9.refs_11_), channel_id=1, source_target_pairs={{0,1},{1,0},{2,3},{3,2},{4,5},{5,4},{6,7},{7,6},{8,9},{9,8},{10,11... | collective-permute-start | bytes 983048 | tf_op jit(solution)/shard_map/ppermute | solution.py:617
  92.6 1.6 %copy-start.9 = (f32[640,128]{1,0:T(8,128)}, f32[640,128]{1,0:T(8,128)S(1)}, u32[]{:S(2)}) copy-start(f32[640,128]{1,0:T(8,128)S(1)} %collective-permute-done.10.refs_12_) | copy-start | bytes 983044
  92.6 1.6 %copy-start.10 = (f32[640,128]{1,0:T(8,128)}, f32[640,128]{1,0:T(8,128)S(1)}, u32[]{:S(2)}) copy-start(f32[640,128]{1,0:T(8,128)S(1)} %collective-permute-done.11.refs_13_) | copy-start | bytes 983044
  93.7 0.7 copy-start.11
  94.1 0.7 copy-start.12
  101.9 1.4 %collective-permute-start.14 = (f32[8,128]{1,0:T(8,128)}, f32[8,128]{1,0:T(8,128)S(1)}, u32[]{:S(2)}, u32[]{:S(2)}) collective-permute-start(f32[8,128]{1,0:T(8,128)} %get-tuple-element.51), channel_id=1, source_target_pairs={{0,1},{1,0},{2,3},{3,2},{4,5},{5,4},{6,7},{7,6},{8,9},{9,8},{10,11... | collective-permute-start | bytes 12296 | tf_op jit(solution)/shard_map/ppermute | solution.py:617
  104.1 5.4 %collective-permute-start.17 = (f32[8,128]{1,0:T(8,128)S(1)}, f32[8,128]{1,0:T(8,128)S(1)}, u32[]{:S(2)}, u32[]{:S(2)}) collective-permute-start(f32[8,128]{1,0:T(8,128)S(1)} %add.46), channel_id=1, source_target_pairs={{0,6},{1,7},{2,4},{3,5},{4,2},{5,3},{6,0},{7,1},{8,14},{9,15},{10,... | collective-permute-start | bytes 12296 | tf_op jit(solution)/shard_map/ppermute | solution.py:617
  106.0 4.7 %collective-permute-start.16 = (f32[8,128]{1,0:T(8,128)S(1)}, f32[8,128]{1,0:T(8,128)S(1)}, u32[]{:S(2)}, u32[]{:S(2)}) collective-permute-start(f32[8,128]{1,0:T(8,128)S(1)} %add.46), channel_id=1, source_target_pairs={{0,4},{1,5},{2,6},{3,7},{4,0},{5,1},{6,2},{7,3},{8,12},{9,13},{10,... | collective-permute-start | bytes 12296 | tf_op jit(solution)/shard_map/ppermute | solution.py:617
  109.1 3.6 %collective-permute-start.15 = (f32[8,128]{1,0:T(8,128)S(1)}, f32[8,128]{1,0:T(8,128)S(1)}, u32[]{:S(2)}, u32[]{:S(2)}) collective-permute-start(f32[8,128]{1,0:T(8,128)S(1)} %add.46), channel_id=1, source_target_pairs={{0,2},{1,3},{2,0},{3,1},{4,6},{5,7},{6,4},{7,5},{8,10},{9,11},{10,... | collective-permute-start | bytes 12296 | tf_op jit(solution)/shard_map/ppermute | solution.py:617
  112.7 13.2 %collective-permute-start.20 = (f32[8,128]{1,0:T(8,128)S(1)}, f32[8,128]{1,0:T(8,128)S(1)}, u32[]{:S(2)}, u32[]{:S(2)}) collective-permute-start(f32[8,128]{1,0:T(8,128)S(1)} %add_add_fusion.1), channel_id=1, source_target_pairs={{24,0},{25,1},{26,2},{27,3},{28,4},{29,5},{30,6},{31,7}} | collective-permute-start | bytes 12296 | tf_op jit(solution)/shard_map/ppermute | solution.py:617
  114.0 11.9 %collective-permute-start.19 = (f32[8,128]{1,0:T(8,128)S(1)}, f32[8,128]{1,0:T(8,128)S(1)}, u32[]{:S(2)}, u32[]{:S(2)}) collective-permute-start(f32[8,128]{1,0:T(8,128)S(1)} %add_add_fusion.1), channel_id=1, source_target_pairs={{16,0},{17,1},{18,2},{19,3},{20,4},{21,5},{22,6},{23,7},{24,8},{25... | collective-permute-start | bytes 12296 | tf_op jit(solution)/shard_map/ppermute | solution.py:617
  115.3 10.6 %collective-permute-start.18 = (f32[8,128]{1,0:T(8,128)S(1)}, f32[8,128]{1,0:T(8,128)S(1)}, u32[]{:S(2)}, u32[]{:S(2)}) collective-permute-start(f32[8,128]{1,0:T(8,128)S(1)} %add_add_fusion.1), channel_id=1, source_target_pairs={{8,0},{9,1},{10,2},{11,3},{12,4},{13,5},{14,6},{15,7},{16,8},{17,9... | collective-permute-start | bytes 12296 | tf_op jit(solution)/shard_map/ppermute | solution.py:617

commit v3 on v2

v3 whole, which is shorter than its diff:
```python
import jax
import jax.numpy as jnp
from jax import lax
from jax.experimental import pallas as pl
from jax.experimental.pallas import tpu as pltpu
from jax.sharding import PartitionSpec as P

STATE = 128
STRETCH = 256
LANES = 512
HALVES = 2
STRIP = 128
META = 8
BIG_VMEM = 56 << 20
SMALL_VMEM = 24 << 20
F32 = jnp.float32
BF16 = jnp.bfloat16
HIGHEST = lax.Precision.HIGHEST


def dot(left, right, left_dim, right_dim, precision=None):
    return lax.dot_general(
        left,
        right,
        (((left_dim,), (right_dim,)), ((), ())),
        precision=precision,
        preferred_element_type=F32,
    )


def iota(shape, dim):
    return lax.broadcasted_iota(jnp.int32, shape, dim)


def lower(length):
    return (iota((length, length), 0) >= iota((length, length), 1)).astype(F32)


def thrice(rates):
    heads, length = rates.shape
    spare = jnp.zeros((STATE - 3 * heads, length), F32)
    return jnp.concatenate([rates, rates, rates, spare], axis=0)


def three_terms(value, heads):
    lane = iota(value.shape, 1)
    first = value.astype(BF16)
    rest = value - first.astype(F32)
    second = rest.astype(BF16)
    third = (rest - second.astype(F32)).astype(BF16)
    return jnp.where(lane < heads, first, jnp.where(lane < 2 * heads, second, third))


def spreader(chunk, heads, head_size, lanes):
    row = iota((STATE, lanes), 0)
    head = (iota((STATE, lanes), 1) + chunk * lanes) // head_size
    hit = (row == head) | (row == head + heads) | (row == head + 2 * heads)
    return hit.astype(F32).astype(BF16)


def head_adder(chunk, head_size, lanes):
    head = (iota((lanes, STATE), 0) + chunk * lanes) // head_size
    return (iota((lanes, STATE), 1) == head).astype(F32).astype(BF16)


def head_sums(value, adder):
    first = value.astype(BF16)
    second = (value - first.astype(F32)).astype(BF16)
    return dot(first, adder, 1, 0) + dot(second, adder, 1, 0)


def decay_terms(rates, heads):
    length = rates.shape[1]
    running = dot(lower(length), thrice(rates), 1, 1, HIGHEST)
    last = running[length - 1 : length, :]
    return (
        running,
        three_terms(jnp.exp(last - running), heads),
        three_terms(jnp.exp(running), heads),
    )


def term_pair(value):
    first = value.astype(BF16)
    return first, (value - first.astype(F32)).astype(BF16)


def lane_spread(per_strip, head_size):
    head = iota((STRIP, STRIP), 0) % per_strip
    return (iota((STRIP, STRIP), 1) // head_size == head).astype(F32)


def spread_rows(rows, offset, strips, head_size):
    per_strip = STRIP // head_size
    lane = iota((strips, STRIP), 1)
    row = iota((strips, STRIP), 0) + offset
    picked = [jnp.where(lane // per_strip == row, value, 0.0) for value in rows]
    stacked = jnp.concatenate(picked, axis=0) if len(picked) > 1 else picked[0]
    wide = dot(stacked, lane_spread(per_strip, head_size), 1, 0, HIGHEST)
    return [wide[i * strips : (i + 1) * strips, :] for i in range(len(rows))]


def whole(*shape):
    return pl.BlockSpec(shape, lambda *_: (0,) * len(shape))


def lanes_of(rows):
    return pl.BlockSpec((rows, LANES), lambda c: (0, c))


def half_lanes(rows, lanes, half, steps):
    return pl.BlockSpec((rows, lanes), lambda c: (0, half * steps + c))


SCALARS = pl.BlockSpec(memory_space=pltpu.SMEM)
STEPS = 2


def summary_kernel(heads, chips, half, place, x_ref, g_ref, write_ref, read_ref, *refs):
    chunk = pl.program_id(0)
    lanes = x_ref.shape[1]
    strips = lanes // STRIP
    half_strips = strips * STEPS
    head_size = lanes * STEPS * HALVES // heads
    part = STATE // chips
    if half == 0:
        rates_ref, send_ref, keep_ref, decay_ref, log_ref, run_ref, tail_ref, lead_ref = refs[:8]
    else:
        log_ref, tail_ref, lead_ref, send_ref, keep_ref, decay_ref = refs[:6]
    write_t, read_t = refs[-2:]

    @pl.when(chunk == 0)
    def _():
        if half == 0:
            running, tail, lead = decay_terms(rates_ref[...], heads)
            run_ref[...] = running
            tail_ref[...] = tail
            lead_ref[...] = lead
            log_ref[...] = jnp.broadcast_to(running[STRETCH - 1 :, :], (META, STRIP))
        send_ref[pl.ds(half_strips * STATE, META), :] = log_ref[...]
        write_t[...] = write_ref[...].astype(F32).T.astype(BF16)
        read_t[...] = read_ref[...].astype(F32).T.astype(BF16)

    spread = spreader(half * STEPS + chunk, heads, head_size, lanes)
    tail = dot(tail_ref[...], spread, 1, 0)
    lead = dot(lead_ref[...], spread, 1, 0)
    inputs_tail = (x_ref[...].astype(F32) * tail).astype(BF16)
    grads_lead = (g_ref[...].astype(F32) * lead).astype(BF16)
    state = dot(write_t[...], inputs_tail, 1, 0)
    back = dot(read_t[...], grads_lead, 1, 0)
    first = place[0] == 0
    send = jnp.where(first, state, back)
    keep = jnp.where(first, back, state)
    for strip in range(strips):
        at = chunk * strips + strip
        wide = slice(strip * STRIP, (strip + 1) * STRIP)
        decay_ref[pl.ds(at, 1), :] = lead[STRETCH - 1 :, wide]
        for quarter in range(chips):
            rows = pl.ds(pl.multiple_of((quarter * half_strips + at) * part, part), part)
            mine = slice(quarter * part, (quarter + 1) * part)
            send_ref[rows, :] = send[mine, wide]
            keep_ref[rows, :] = keep[mine, wide]


def summary(chips, half, place, x, g, write_map, read_map, rates, shared):
    tokens, wide = x.shape
    heads = rates.shape[0]
    lanes = wide // (STEPS * HALVES)
    strips = wide // STRIP // HALVES
    terms = [
        jax.ShapeDtypeStruct((META, STRIP), F32),
        jax.ShapeDtypeStruct((tokens, STRIP), F32),
        jax.ShapeDtypeStruct((tokens, STRIP), BF16),
        jax.ShapeDtypeStruct((tokens, STRIP), BF16),
    ]
    out_shape = [
        jax.ShapeDtypeStruct((strips * STATE + META, STRIP), F32),
        jax.ShapeDtypeStruct((strips * STATE, STRIP), F32),
        jax.ShapeDtypeStruct((strips, STRIP), F32),
    ]
    if half == 0:
        extra = [rates]
        out_shape = out_shape + terms
    else:
        extra = [shared[0], shared[2], shared[3]]
    return pl.pallas_call(
        lambda *refs: summary_kernel(heads, chips, half, *refs),
        grid=(STEPS,),
        in_specs=[
            SCALARS,
            half_lanes(tokens, lanes, half, STEPS),
            half_lanes(tokens, lanes, half, STEPS),
            whole(tokens, STATE),
            whole(tokens, STATE),
        ]
        + [whole(*value.shape) for value in extra],
        out_specs=[whole(*out.shape) for out in out_shape],
        out_shape=out_shape,
        scratch_shapes=[
            pltpu.VMEM((STATE, tokens), BF16),
            pltpu.VMEM((STATE, tokens), BF16),
        ],
        compiler_params=pltpu.CompilerParams(vmem_limit_bytes=BIG_VMEM),
        cost_estimate=pl.CostEstimate(
            flops=1_000_000_000, bytes_accessed=3_000_000, transcendentals=0
        ),
        name="summary",
    )(place, x, g, write_map, read_map, *extra)


def combine_kernel(chips, place, after, first_ref, keep_ref, decay_ref, log_ref, *out_refs):
    strips = decay_ref.shape[0]
    part = STATE // chips
    size = strips * part
    meta = first_ref[pl.ds(chips * size, META), :] + log_ref[...]
    for step, out_ref in enumerate(out_refs):
        base = (place[1] ^ step) * size
        for strip in range(strips):
            rows = pl.ds(pl.multiple_of(base + strip * part, part), part)
            out_ref[strip * part : (strip + 1) * part, :] = (
                first_ref[rows, :] * decay_ref[strip : strip + 1, :] + keep_ref[rows, :]
            )
        out_ref[size:, :] = meta


def combine(chips, place, after, first, keep, decay, log):
    strips = decay.shape[0]
    size = strips * (STATE // chips)
    return pl.pallas_call(
        lambda *refs: combine_kernel(chips, *refs),
        in_specs=[SCALARS]
        + [whole(*value.shape) for value in (after, first, keep, decay, log)],
        out_specs=[whole(size + META, STRIP)] * chips,
        out_shape=[jax.ShapeDtypeStruct((size + META, STRIP), F32)] * chips,
        compiler_params=pltpu.CompilerParams(vmem_limit_bytes=SMALL_VMEM),
        name="combine",
    )(place, after, first, keep, decay, log)


def rank_of(place, step):
    chip = place[1] ^ step
    return jnp.where(place[0] == 1, chip, -chip)


def masked_sum(terms):
    total = None
    for hit, value in terms:
        value = jnp.where(hit, value, 0.0)
        total = value if total is None else total + value
    return total


def total_kernel(offset, strips, head_size, place, after_ref, *refs):
    at_refs, out_ref = refs[:-1], refs[-1]
    chips = len(at_refs)
    part = STATE // chips
    size = strips * part
    rank = [rank_of(place, step) for step in range(chips)]
    logs = [ref[size : size + 1, :] for ref in at_refs]
    weights = [
        jnp.exp(masked_sum([(rank[b] > rank[a], logs[b]) for b in range(chips)]))
        for a in range(chips)
    ]
    wide = spread_rows(weights, offset, strips, head_size)
    for strip in range(strips):
        rows = slice(strip * part, (strip + 1) * part)
        total = at_refs[0][rows, :] * wide[0][strip : strip + 1, :]
        for a in range(1, chips):
            total = total + at_refs[a][rows, :] * wide[a][strip : strip + 1, :]
        out_ref[rows, :] = total
    out_ref[size:, :] = jnp.broadcast_to(sum(logs[1:], logs[0]), (META, STRIP))


def group_total(half, head_size, place, after, at):
    strips = (at[0].shape[0] - META) * len(at) // STATE
    return pl.pallas_call(
        lambda *refs: total_kernel(half * strips, strips, head_size, *refs),
        in_specs=[SCALARS, whole(*after.shape)] + [whole(*at[0].shape)] * len(at),
        out_specs=whole(*at[0].shape),
        out_shape=jax.ShapeDtypeStruct(at[0].shape, F32),
        compiler_params=pltpu.CompilerParams(vmem_limit_bytes=SMALL_VMEM),
        name="group_total",
    )(place, after, *at)


def enter_kernel(chips, offset, strips, head_size, place, *refs):
    at_refs, got_refs, out_refs = refs[:chips], refs[chips:-chips], refs[-chips:]
    part = STATE // chips
    size = strips * part
    rank = [rank_of(place, step) for step in range(chips)]
    logs = [ref[size : size + 1, :] for ref in at_refs]
    zero = jnp.zeros_like(logs[0])
    rows_of = []
    passed = zero
    for ref in got_refs:
        rows_of.append(jnp.exp(passed))
        passed = passed + ref[size : size + 1, :]
    for to in range(chips):
        rows_of.append(
            jnp.exp(masked_sum([(rank[m] < rank[to], logs[m]) for m in range(chips)]))
        )
    pairs = [(to, a) for to in range(chips) for a in range(chips) if a != to]
    for to, a in pairs:
        between = masked_sum(
            [((rank[m] > rank[a]) & (rank[m] < rank[to]), logs[m]) for m in range(chips)]
        )
        rows_of.append(jnp.where(rank[a] < rank[to], jnp.exp(between), 0.0))
    wide = spread_rows(rows_of, offset, strips, head_size)
    groups_wide = wide[: len(got_refs)]
    ahead_wide = wide[len(got_refs) : len(got_refs) + chips]
    pair_wide = dict(zip(pairs, wide[len(got_refs) + chips :]))
    for strip in range(strips):
        rows = slice(strip * part, (strip + 1) * part)
        one = slice(strip, strip + 1)
        incoming = jnp.zeros((part, STRIP), F32)
        for ref, weight in zip(got_refs, groups_wide):
            incoming = incoming + ref[rows, :] * weight[one, :]
        values = [ref[rows, :] for ref in at_refs]
        for to in range(chips):
            entering = incoming * ahead_wide[to][one, :]
            for a in range(chips):
                if a != to:
                    entering = entering + values[a] * pair_wide[to, a][one, :]
            out_refs[to][rows, :] = entering


def enter(half, head_size, place, at, got):
    chips = len(at)
    strips = (at[0].shape[0] - META) * chips // STATE
    size = strips * (STATE // chips)
    return pl.pallas_call(
        lambda *refs: enter_kernel(chips, half * strips, strips, head_size, *refs),
        in_specs=[SCALARS] + [whole(*at[0].shape)] * (chips + len(got)),
        out_specs=[whole(size, STRIP)] * chips,
        out_shape=[jax.ShapeDtypeStruct((size, STRIP), F32)] * chips,
        compiler_params=pltpu.CompilerParams(vmem_limit_bytes=SMALL_VMEM),
        name="enter",
    )(place, *at, *got)


def intra_kernel(
    heads, after_ref, x_ref, g_ref, write_ref, read_ref, rates_ref, column_ref, tail_ref, lead_ref,
    dx_ref, db_ref, dc_ref, change_ref, state_ref, back_ref,
    row_ref, scores_ref, mask_ref, pairs_ref, write_t, read_t,
):
    chunk = pl.program_id(0)
    lanes = x_ref.shape[1]
    head_size = lanes * pl.num_programs(0) // heads
    per_chunk = lanes // head_size

    @pl.when(chunk == 0)
    def _():
        rates = rates_ref[...]
        triangle = lower(STRETCH)
        row_ref[...] = dot(rates, triangle, 1, 1, HIGHEST)
        mask_ref[...] = triangle
        scores_ref[...] = dot(read_ref[...], write_ref[...], 1, 1)
        pairs_ref[...] = jnp.zeros_like(pairs_ref)
        change_ref[...] = jnp.zeros_like(change_ref)
        write_t[...] = write_ref[...].astype(F32).T.astype(BF16)
        read_t[...] = read_ref[...].astype(F32).T.astype(BF16)

    columns = pltpu.roll(column_ref[...], STATE - chunk * per_chunk, 1)
    rows = row_ref[pl.ds(pl.multiple_of(chunk * per_chunk, per_chunk), per_chunk), :]
    causal = mask_ref[...] > 0.5
    scores = scores_ref[...]
    pairs = pairs_ref[...]
    low_half = iota((STRETCH, 2 * head_size), 1) < head_size
    adder = head_adder(chunk, head_size, lanes)
    spread = spreader(chunk, heads, head_size, lanes)
    high, low = term_pair(x_ref[...].astype(F32) * dot(tail_ref[...], spread, 1, 0))
    state_ref[...] = dot(write_t[...], high, 1, 0) + dot(write_t[...], low, 1, 0)
    high, low = term_pair(g_ref[...].astype(F32) * dot(lead_ref[...], spread, 1, 0))
    back_ref[...] = dot(read_t[...], high, 1, 0) + dot(read_t[...], low, 1, 0)
    for pair in range(per_chunk // 2):
        strip = slice(pair * 2 * head_size, (pair + 1) * 2 * head_size)
        x = x_ref[:, strip]
        g = g_ref[:, strip]
        ys, dxs = [], []
        for half in range(2):
            head = 2 * pair + half
            gap = columns[:, head : head + 1] - rows[head : head + 1, :]
            decay = jnp.where(causal, jnp.exp(gap), 0.0)
            mixing = (scores * decay).astype(BF16)
            ys.append(dot(mixing, x, 1, 0))
            dxs.append(dot(mixing, g, 0, 0))
            mine = low_half if half == 0 else jnp.logical_not(low_half)
            pairs = pairs + dot(jnp.where(mine, g, jnp.zeros_like(g)), x, 1, 1) * decay
        y = jnp.where(low_half, ys[0], ys[1])
        dx = jnp.where(low_half, dxs[0], dxs[1])
        dx_ref[:, strip] = dx
        change_ref[...] += head_sums(
            g.astype(F32) * y - x.astype(F32) * dx, adder[strip, :]
        )
    pairs_ref[...] = pairs

    @pl.when(chunk == pl.num_programs(0) - 1)
    def _():
        summed = pairs_ref[...].astype(BF16)
        db_ref[...] = dot(summed, read_ref[...], 0, 0)
        dc_ref[...] = dot(summed, write_ref[...], 1, 0)


def intra(after, x, g, write_map, read_map, rates, shared):
    tokens, wide = x.shape
    heads = rates.shape[0]
    return pl.pallas_call(
        lambda *refs: intra_kernel(heads, *refs),
        grid=(wide // LANES,),
        in_specs=[
            whole(META, STRIP),
            lanes_of(tokens),
            lanes_of(tokens),
            whole(tokens, STATE),
            whole(tokens, STATE),
            whole(heads, tokens),
        ]
        + [whole(tokens, STRIP)] * 3,
        out_specs=[lanes_of(tokens)] + [whole(tokens, STATE)] * 3 + [lanes_of(STATE)] * 2,
        out_shape=[
            jax.ShapeDtypeStruct((tokens, wide), F32),
            jax.ShapeDtypeStruct((tokens, STATE), F32),
            jax.ShapeDtypeStruct((tokens, STATE), F32),
            jax.ShapeDtypeStruct((tokens, STATE), F32),
            jax.ShapeDtypeStruct((STATE, wide), F32),
            jax.ShapeDtypeStruct((STATE, wide), F32),
        ],
        scratch_shapes=[
            pltpu.VMEM((heads, tokens), F32),
            pltpu.VMEM((tokens, tokens), F32),
            pltpu.VMEM((tokens, tokens), F32),
            pltpu.VMEM((tokens, tokens), F32),
            pltpu.VMEM((STATE, tokens), BF16),
            pltpu.VMEM((STATE, tokens), BF16),
        ],
        compiler_params=pltpu.CompilerParams(vmem_limit_bytes=BIG_VMEM),
        cost_estimate=pl.CostEstimate(
            flops=12_000_000_000, bytes_accessed=8_000_000, transcendentals=heads * tokens * tokens
        ),
        name="intra",
    )(after, x, g, write_map, read_map, rates, *shared[1:])


def assemble_kernel(
    heads, chips, half, head_size, place, after, first_ref, state_own, back_own, *refs,
):
    own_refs, far_refs = refs[:chips], refs[chips : 2 * chips]
    state_ref, back_ref, total_ref = refs[2 * chips :]
    lanes = state_ref.shape[1]
    strips = lanes // STRIP
    part = STATE // chips
    size = strips * part
    log = first_ref[chips * size : chips * size + 1, :]
    decay = spread_rows([jnp.exp(log)], half * strips, strips, head_size)[0]
    is_first = place[0] == 0
    sums = [None] * strips
    for step in range(chips):
        quarter = place[1] ^ step
        rows = pl.ds(pl.multiple_of(quarter * part, part), part)
        for strip in range(strips):
            wide = slice(strip * STRIP, (strip + 1) * STRIP)
            here = slice(strip * part, (strip + 1) * part)
            there = pl.ds(pl.multiple_of(quarter * size + strip * part, part), part)
            own = own_refs[step][here, :] * decay[strip : strip + 1, :] + first_ref[there, :]
            far = far_refs[step][here, :]
            state = jnp.where(is_first, far, own).astype(BF16)
            back = jnp.where(is_first, own, far).astype(BF16)
            state_ref[rows, wide] = state
            back_ref[rows, wide] = back
            gain = state.astype(F32) * back_own[rows, wide]
            gain = gain - back.astype(F32) * state_own[rows, wide]
            sums[strip] = gain if sums[strip] is None else sums[strip] + gain
    row_sum = [
        jnp.broadcast_to(jnp.sum(value, axis=0, keepdims=True), (META, STRIP)) for value in sums
    ]
    total_ref[...] = head_sums(
        jnp.concatenate(row_sum, axis=1), head_adder(half, head_size, lanes)
    )


def assemble(heads, half, place, after, first, state_own, back_own, own, far):
    chips = len(own)
    wide = state_own.shape[1]
    lanes = wide // HALVES
    mine = pl.BlockSpec((STATE, lanes), lambda c: (0, half))
    return pl.pallas_call(
        lambda *refs: assemble_kernel(heads, chips, half, wide // heads, *refs),
        grid=(1,),
        in_specs=[SCALARS, whole(*after.shape), whole(*first.shape), mine, mine]
        + [whole(*value.shape) for value in (*own, *far)],
        out_specs=[whole(STATE, lanes), whole(STATE, lanes), whole(META, STRIP)],
        out_shape=[
            jax.ShapeDtypeStruct((STATE, lanes), BF16),
            jax.ShapeDtypeStruct((STATE, lanes), BF16),
            jax.ShapeDtypeStruct((META, STRIP), F32),
        ],
        compiler_params=pltpu.CompilerParams(vmem_limit_bytes=SMALL_VMEM),
        name="assemble",
    )(place, after, first, state_own, back_own, *own, *far)


def finish_kernel(
    heads, half, x_ref, g_ref, write_ref, read_ref, tail_ref, lead_ref,
    dx_ref, db_ref, dc_ref, change_ref, state_ref, back_ref, *refs,
):
    grad_ref, db_out, dc_out, sum_out, db_sum, dc_sum = refs[-6:]
    chunk = pl.program_id(0)
    lanes = x_ref.shape[1]
    head_size = lanes * STEPS * HALVES // heads

    @pl.when(chunk == 0)
    def _():
        sum_out[...] = change_ref[...]
        db_sum[...] = db_ref[...]
        dc_sum[...] = dc_ref[...]

    state = state_ref[...]
    back = back_ref[...]
    spread = spreader(half * STEPS + chunk, heads, head_size, lanes)
    tail = dot(tail_ref[...], spread, 1, 0)
    lead = dot(lead_ref[...], spread, 1, 0)
    x = x_ref[...].astype(F32)
    g = g_ref[...].astype(F32)
    y = dot(read_ref[...], state, 1, 0) * lead
    dx = dot(write_ref[...], back, 1, 0) * tail
    grad_ref[...] = (dx_ref[...] + dx).astype(BF16)
    adder = head_adder(half * STEPS + chunk, head_size, lanes)
    sum_out[...] += head_sums(g * y - x * dx, adder)
    db_sum[...] += dot((x * tail).astype(BF16), back, 1, 1)
    dc_sum[...] += dot((g * lead).astype(BF16), state, 1, 1)

    @pl.when(chunk == STEPS - 1)
    def _():
        db_out[...] = db_sum[...].astype(db_out.dtype)
        dc_out[...] = dc_sum[...].astype(dc_out.dtype)


def finish(heads, half, x, g, write_map, read_map, shared, dx, sums, state, back, grad):
    tokens, wide = x.shape
    lanes = wide // (STEPS * HALVES)
    strip = half_lanes(tokens, lanes, half, STEPS)
    own = pl.BlockSpec((STATE, lanes), lambda c: (0, c))
    kind = BF16 if half == HALVES - 1 else F32
    earlier = [] if grad is None else [grad]
    return pl.pallas_call(
        lambda *refs: finish_kernel(heads, half, *refs),
        grid=(STEPS,),
        in_specs=[strip, strip]
        + [whole(tokens, STATE)] * 4
        + [strip]
        + [whole(tokens, STATE)] * 3
        + [own, own]
        + [pl.BlockSpec(memory_space=pl.ANY)] * len(earlier),
        out_specs=[strip] + [whole(tokens, STATE)] * 3,
        out_shape=[
            jax.ShapeDtypeStruct((tokens, wide), BF16),
            jax.ShapeDtypeStruct((tokens, STATE), kind),
            jax.ShapeDtypeStruct((tokens, STATE), kind),
            jax.ShapeDtypeStruct((tokens, STATE), F32),
        ],
        scratch_shapes=[pltpu.VMEM((tokens, STATE), F32)] * 2,
        input_output_aliases={12: 0} if earlier else {},
        compiler_params=pltpu.CompilerParams(vmem_limit_bytes=BIG_VMEM),
        cost_estimate=pl.CostEstimate(
            flops=3_000_000_000, bytes_accessed=5_000_000, transcendentals=0
        ),
        name="finish",
    )(x, g, write_map, read_map, *shared[2:], dx, *sums, state, back, *earlier)


def suffix_kernel(change_ref, later_ref, out_ref):
    heads = out_ref.shape[0]
    last = iota((STRETCH, STATE), 0) == STRETCH - 1
    change = change_ref[...] + jnp.where(last, later_ref[0:1, :], 0.0)
    out_ref[...] = dot(change, lower(STRETCH), 0, 0, HIGHEST)[:heads, :]


def suffix(heads, change, later):
    return pl.pallas_call(
        suffix_kernel,
        in_specs=[whole(*change.shape), whole(*later.shape)],
        out_specs=whole(heads, STRETCH),
        out_shape=jax.ShapeDtypeStruct((heads, STRETCH), F32),
        name="suffix",
    )(change, later)


def per_device(inputs, out_grad, input_map, output_map, log_decay):
    heads = log_decay.shape[0]
    head_size = inputs.shape[1] // heads
    groups, shards = lax.axis_size("grp"), lax.axis_size("seq")
    chips = shards // 2
    shard = lax.axis_index("seq")
    chip, core = shard // 2, shard % 2
    place = jnp.stack([core, chip]).astype(jnp.int32)
    everyone = [(a, z, c) for a in range(groups) for z in range(chips) for c in range(2)]

    def move(value, target):
        pairs = []
        for a, z, c in everyone:
            to = target(a, z, c)
            if to is not None:
                pairs.append((a * shards + 2 * z + c, to[0] * shards + 2 * to[1] + to[2]))
        return lax.ppermute(value, ("grp", "seq"), pairs)

    def to_core(value):
        return move(value, lambda a, z, c: (a, z, 1 - c))

    def to_chip(value, step):
        return move(value, lambda a, z, c: (a, z ^ step, c)) if step else value

    def to_group(value, step, ahead):
        def target(a, z, c):
            to = a + step if ahead(c) else a - step
            return (to, z, c) if 0 <= to < groups else None

        return move(value, target)

    def scan_half(half, after, at):
        at = [to_chip(value, step) for step, value in enumerate(at)]
        total = group_total(half, head_size, place, after, at)
        got = [to_group(total, step, lambda c: c == 1) for step in range(1, groups)]
        inside = enter(half, head_size, place, at, got)
        own = [to_chip(value, step) for step, value in enumerate(inside)]
        return own, [to_core(value) for value in own]

    def later_total(tally):
        other = to_core(tally)
        later = jnp.where(core == 0, other, 0.0)
        tally = tally + other
        steps = [to_chip(tally, step) for step in range(1, chips)]
        for step, value in enumerate(steps, 1):
            later = later + jnp.where((chip ^ step) > chip, value, 0.0)
            tally = tally + value
        for step in range(1, groups):
            later = later + to_group(tally, step, lambda c: False)
        return later

    maps = (inputs, out_grad, input_map, output_map)
    send, keep, decay, *shared = summary(chips, 0, place, *maps, log_decay, None)
    first = [to_core(send)]
    pieces = [combine(chips, place, shared[0], first[0], keep, decay, shared[0])]
    send, keep, decay = summary(chips, 1, place, *maps, log_decay, shared)
    first.append(to_core(send))
    dx, db, dc, change, state_own, back_own = intra(
        pieces[0][0][-META:], *maps, log_decay, shared
    )
    token = change[:META]
    pieces.append(combine(chips, place, token, first[1], keep, decay, shared[0]))
    sums, grad, later = (db, dc, change), None, None
    for half in range(HALVES):
        own, far = scan_half(half, token, pieces[half])
        state, back, tally = assemble(
            heads, half, place, sums[2][:META], first[half], state_own, back_own, own, far
        )
        grad, *sums = finish(heads, half, *maps, shared, dx, sums, state, back, grad)
        found = later_total(tally)
        later = found if later is None else later + found
    return (grad, sums[0], sums[1], suffix(heads, sums[2], later))


def solution(mesh):
    tokens = P(("grp", "seq"), None)
    in_specs = (tokens, tokens, tokens, tokens, P(None, ("grp", "seq")))
    out_specs = (tokens, tokens, tokens, P(None, ("grp", "seq")))
    return jax.shard_map(
        per_device, mesh=mesh, in_specs=in_specs, out_specs=out_specs, check_vma=False
    )
```

time: 129 us -> 126 us (0.977)
  waiting for transfers between devices: 50.4 us -> 18.6 us
  starting transfers between devices: 28.8 us -> 57.4 us
  other arithmetic: 2.79 us -> 1.28 us
  Pallas kernels: 40.1 us -> 41.5 us
    ppermute x21 -> x42, waiting for transfers between devices: 50.4 us -> 18.6 us  [move(): return lax.ppermute(value, ('grp', 'seq'), pairs)]
    ppermute x21 -> x42, starting transfers between devices: 28.8 us -> 57.4 us  [move(): return lax.ppermute(value, ('grp', 'seq'), pairs)]
    add x4 -> x5, other arithmetic: 2.19 us -> 0.63 us  [the longest x1 0.61 us: per_device(): later = found if later is None else later + found]
    pallas_call x5 -> x11, Pallas kernels: 25.4 us -> 26.2 us  [the longest x2 10.8 us: finish(): pl.pallas_call(lambda *refs: finish_kernel(heads, half, *refs), grid=(STE...]
    unnamed x26 -> x24, local copies, waits for them, and re-layouts: 3.21 us -> 2.92 us
  transfers between devices with their start and end apart: 21 -> 42, of which waited for: 12 -> 5; matrix products, arithmetic and copies ran while one was open for 1% -> 2% of each run, Pallas kernels for 18% -> 28%
where the time goes in v3:
time: 126 us; the launch traced here: 125 us
  starting transfers between devices  57.4 us (46%)
  Pallas kernels  41.5 us (33%)
  waiting for transfers between devices  18.6 us (15%)
  local copies, waits for them, and re-layouts  4.88 us (4%)
  other arithmetic  1.28 us (1%)
    ppermute x42, starting transfers between devices, move(): return lax.ppermute(value, ('grp', 'seq'), pairs)  57.4 us
    ppermute x42, waiting for transfers between devices, move(): return lax.ppermute(value, ('grp', 'seq'), pairs)  18.6 us
    pallas_call x1, Pallas kernels, intra(): pl.pallas_call(lambda *refs: intra_kernel(heads, *refs), grid=(wide // LA...  14 us
    pallas_call x2, Pallas kernels, finish(): pl.pallas_call(lambda *refs: finish_kernel(heads, half, *refs), grid=(STE...  10.8 us
    pallas_call x2, Pallas kernels, summary(): pl.pallas_call(lambda *refs: summary_kernel(heads, chips, half, *refs), g...  7.31 us
    unnamed x24, local copies, waits for them, and re-layouts  2.92 us
    pallas_call x2, Pallas kernels, assemble(): pl.pallas_call(lambda *refs: assemble_kernel(heads, chips, half, wide //...  2.7 us
  transfers between devices with their start and end apart: 42, of which 5 were waited for; matrix products, arithmetic and copies ran while one was open for 2% of the time, Pallas kernels for 28%

profile of v3, /device:TPU:0, one launch (start us, length us, event | category | flops | bytes accessed | tf_op | source)
XLA Modules:
  0.0 124.7 jit_solution(13728865102344579228)
XLA Ops:
  0.6 0.7 pad_add_fusion.refs_0_
  1.3 3.8 %summary.2 = (f32[1288,128]{1,0:T(8,128)}, f32[1280,128]{1,0:T(8,128)}, f32[10,128]{1,0:T(8,128)}, f32[8,128]{1,0:T(8,128)}, f32[256,128]{1,0:T(8,128)}, /*index...) custom-call(s32[2]{0:T(128)} %pad_add_fusion.refs_0_, bf16[256,2560]{1,0:T(8,128)(2,1)} %refs_0_.3, ...), custom_call_target="tpu_custom_call" | custom-call | flops 1000000000 | bytes 3000000 | tf_op jit(solution)/shard_map/summary/pallas_call | solution.py:186
  5.1 0.5 collective-permute-start
  5.6 3.6 %summary.3 = (f32[1288,128]{1,0:T(8,128)}, f32[1280,128]{1,0:T(8,128)}, f32[10,128]{1,0:T(8,128)}) custom-call(s32[2]{0:T(128)} %pad_add_fusion.refs_0_, bf16[256,2560]{1,0:T(8,128)(2,1)} %refs_0_.3, bf16[256,2560]{1,0:T(8,128)(2,1)} %refs_1_.9, bf16[256,128]{1,0:T(8,128)(2,1)} %refs_2_.9, bf16[256,128]{1,0:T(8,128)(2,1)} %refs_3_.9, ...), custom_call_target="tpu_custom_call" | custom-call | flops 1000000000 | bytes 3000000 | tf_op jit(solution)/shard_map/summary/pallas_call | solution.py:186
  9.2 0.6 combine.2
  9.9 0.6 slice.10.refs_0_
  10.5 3.0 %collective-permute-start.1 = (f32[328,128]{1,0:T(8,128)S(1)}, f32[328,128]{1,0:T(8,128)S(1)}, u32[]{:S(2)}, u32[]{:S(2)}) collective-permute-start(f32[328,128]{1,0:T(8,128)S(1)} %get-tuple-element.64), channel_id=1, source_target_pairs={{0,2},{1,3},{2,0},{3,1},{4,6},{5,7},{6,4},{7,5},{8,10},{9,11},{10,... | collective-permute-start | bytes 503816 | tf_op jit(solution)/shard_map/ppermute | solution.py:604
  13.5 2.6 %collective-permute-start.2 = (f32[328,128]{1,0:T(8,128)S(1)}, f32[328,128]{1,0:T(8,128)S(1)}, u32[]{:S(2)}, u32[]{:S(2)}) collective-permute-start(f32[328,128]{1,0:T(8,128)S(1)} %get-tuple-element.65), channel_id=1, source_target_pairs={{0,4},{1,5},{2,6},{3,7},{4,0},{5,1},{6,2},{7,3},{8,12},{9,13},{10,... | collective-permute-start | bytes 503816 | tf_op jit(solution)/shard_map/ppermute | solution.py:604
  16.1 14.0 %intra.1 = (f32[256,2560]{1,0:T(8,128)}, f32[256,128]{1,0:T(8,128)}, f32[256,128]{1,0:T(8,128)}, f32[256,128]{1,0:T(8,128)}, f32[128,2560]{1,0:T(8,128)}, /*index=5*/f32[128,2560]{1,0:T(8,128)}) custom-call(f32[8,128]{1,0:T(8,128)} %slice.10.refs_0_, bf16[256,2560]{1,0:T(8,128)(2,1)} %refs_0_.3, bf16[256,2560]{1,0:T(8,128)(2,1)} %refs_1_.9, ...), custom_call_target="tpu_custom_call" | custom-call | flops 12000000000 | bytes 8000000 | tf_op jit(solution)/shard_map/intra/pallas_call | solution.py:407
  30.1 0.7 slice.11.refs_1_
  30.8 0.6 combine.3
  31.4 1.0 collective-permute-start.15
  32.4 3.5 %collective-permute-start.16 = (f32[328,128]{1,0:T(8,128)S(1)}, f32[328,128]{1,0:T(8,128)S(1)}, u32[]{:S(2)}, u32[]{:S(2)}) collective-permute-start(f32[328,128]{1,0:T(8,128)S(1)} %get-tuple-element.81), channel_id=1, source_target_pairs={{0,4},{1,5},{2,6},{3,7},{4,0},{5,1},{6,2},{7,3},{8,12},{9,13},{10,... | collective-permute-start | bytes 503816 | tf_op jit(solution)/shard_map/ppermute | solution.py:604
  35.9 0.8 group_total.2
  36.7 1.3 %collective-permute-start.4 = (f32[328,128]{1,0:T(8,128)S(1)}, f32[328,128]{1,0:T(8,128)S(1)}, u32[]{:S(2)}, u32[]{:S(2)}) collective-permute-start(f32[328,128]{1,0:T(8,128)S(1)} %group_total.2), channel_id=1, source_target_pairs={{1,9},{3,11},{5,13},{7,15},{8,0},{9,17},{10,2},{11,19},{12,4},{13,... | collective-permute-start | bytes 503816 | tf_op jit(solution)/shard_map/ppermute | solution.py:604
  38.0 1.3 %collective-permute-start.5 = (f32[328,128]{1,0:T(8,128)S(1)}, f32[328,128]{1,0:T(8,128)S(1)}, u32[]{:S(2)}, u32[]{:S(2)}) collective-permute-start(f32[328,128]{1,0:T(8,128)S(1)} %group_total.2), channel_id=1, source_target_pairs={{1,17},{3,19},{5,21},{7,23},{9,25},{11,27},{13,29},{15,31},{16,0},... | collective-permute-start | bytes 503816 | tf_op jit(solution)/shard_map/ppermute | solution.py:604
  39.3 0.1 collective-permute-done.15.refs_3_.refs_2_
  39.4 1.3 %collective-permute-start.6 = (f32[328,128]{1,0:T(8,128)S(1)}, f32[328,128]{1,0:T(8,128)S(1)}, u32[]{:S(2)}, u32[]{:S(2)}) collective-permute-start(f32[328,128]{1,0:T(8,128)S(1)} %group_total.2), channel_id=1, source_target_pairs={{1,25},{3,27},{5,29},{7,31},{24,0},{26,2},{28,4},{30,6}} | collective-permute-start | bytes 503816 | tf_op jit(solution)/shard_map/ppermute | solution.py:604
  40.7 7.6 %collective-permute-done.16.refs_4_.refs_3_ = f32[328,128]{1,0:T(8,128)S(1)} collective-permute-done((f32[328,128]{1,0:T(8,128)S(1)}, f32[328,128]{1,0:T(8,128)S(1)}, u32[]{:S(2)}, u32[]{:S(2)}) %collective-permute-start.16) | collective-permute-done | bytes 167968 | tf_op jit(solution)/shard_map/ppermute | solution.py:604
  48.3 0.8 group_total.3
  49.1 1.4 %collective-permute-start.18 = (f32[328,128]{1,0:T(8,128)S(1)}, f32[328,128]{1,0:T(8,128)S(1)}, u32[]{:S(2)}, u32[]{:S(2)}) collective-permute-start(f32[328,128]{1,0:T(8,128)S(1)} %group_total.3), channel_id=1, source_target_pairs={{1,9},{3,11},{5,13},{7,15},{8,0},{9,17},{10,2},{11,19},{12,4},{13,... | collective-permute-start | bytes 503816 | tf_op jit(solution)/shard_map/ppermute | solution.py:604
  50.5 1.3 %collective-permute-start.19 = (f32[328,128]{1,0:T(8,128)S(1)}, f32[328,128]{1,0:T(8,128)S(1)}, u32[]{:S(2)}, u32[]{:S(2)}) collective-permute-start(f32[328,128]{1,0:T(8,128)S(1)} %group_total.3), channel_id=1, source_target_pairs={{1,17},{3,19},{5,21},{7,23},{9,25},{11,27},{13,29},{15,31},{16,0},... | collective-permute-start | bytes 503816 | tf_op jit(solution)/shard_map/ppermute | solution.py:604
  51.8 1.3 %collective-permute-start.20 = (f32[328,128]{1,0:T(8,128)S(1)}, f32[328,128]{1,0:T(8,128)S(1)}, u32[]{:S(2)}, u32[]{:S(2)}) collective-permute-start(f32[328,128]{1,0:T(8,128)S(1)} %group_total.3), channel_id=1, source_target_pairs={{1,25},{3,27},{5,29},{7,31},{24,0},{26,2},{28,4},{30,6}} | collective-permute-start | bytes 503816 | tf_op jit(solution)/shard_map/ppermute | solution.py:604
  53.2 1.0 enter.2
  54.2 2.4 %collective-permute-start.7 = (f32[320,128]{1,0:T(8,128)S(1)}, f32[320,128]{1,0:T(8,128)S(1)}, u32[]{:S(2)}, u32[]{:S(2)}) collective-permute-start(f32[320,128]{1,0:T(8,128)S(1)} %get-tuple-element.68), channel_id=1, source_target_pairs={{0,2},{1,3},{2,0},{3,1},{4,6},{5,7},{6,4},{7,5},{8,10},{9,11},{10,... | collective-permute-start | bytes 491528 | tf_op jit(solution)/shard_map/ppermute | solution.py:604
  56.6 1.1 collective-permute-start.8
  57.7 1.4 %collective-permute-start.9 = (f32[320,128]{1,0:T(8,128)S(1)}, f32[320,128]{1,0:T(8,128)S(1)}, u32[]{:S(2)}, u32[]{:S(2)}) collective-permute-start(f32[320,128]{1,0:T(8,128)S(1)} %get-tuple-element.70), channel_id=1, source_target_pairs={{0,6},{1,7},{2,4},{3,5},{4,2},{5,3},{6,0},{7,1},{8,14},{9,15},{10,... | collective-permute-start | bytes 491528 | tf_op jit(solution)/shard_map/ppermute | solution.py:604
  59.1 1.8 %collective-permute-start.10 = (f32[320,128]{1,0:T(8,128)S(1)}, f32[320,128]{1,0:T(8,128)S(1)}, u32[]{:S(2)}, u32[]{:S(2)}) collective-permute-start(f32[320,128]{1,0:T(8,128)S(1)} %get-tuple-element.67.refs_5_), channel_id=1, source_target_pairs={{0,1},{1,0},{2,3},{3,2},{4,5},{5,4},{6,7},{7,6},{8,9},{9,8},{10,11... | collective-permute-start | bytes 491528 | tf_op jit(solution)/shard_map/ppermute | solution.py:604
  60.8 0.3 collective-permute-done.20.refs_7_
  61.2 1.0 enter.3
  62.2 2.4 %collective-permute-start.21 = (f32[320,128]{1,0:T(8,128)S(1)}, f32[320,128]{1,0:T(8,128)S(1)}, u32[]{:S(2)}, u32[]{:S(2)}) collective-permute-start(f32[320,128]{1,0:T(8,128)S(1)} %get-tuple-element.84), channel_id=1, source_target_pairs={{0,2},{1,3},{2,0},{3,1},{4,6},{5,7},{6,4},{7,5},{8,10},{9,11},{10,... | collective-permute-start | bytes 491528 | tf_op jit(solution)/shard_map/ppermute | solution.py:604
  64.7 1.1 collective-permute-start.22
  65.7 6.9 %collective-permute-start.23 = (f32[320,128]{1,0:T(8,128)S(1)}, f32[320,128]{1,0:T(8,128)S(1)}, u32[]{:S(2)}, u32[]{:S(2)}) collective-permute-start(f32[320,128]{1,0:T(8,128)S(1)} %get-tuple-element.86), channel_id=1, source_target_pairs={{0,6},{1,7},{2,4},{3,5},{4,2},{5,3},{6,0},{7,1},{8,14},{9,15},{10,... | collective-permute-start | bytes 491528 | tf_op jit(solution)/shard_map/ppermute | solution.py:604
  72.7 2.1 %collective-permute-start.11 = (f32[320,128]{1,0:T(8,128)S(1)}, f32[320,128]{1,0:T(8,128)S(1)}, u32[]{:S(2)}, u32[]{:S(2)}) collective-permute-start(f32[320,128]{1,0:T(8,128)S(1)} %collective-permute-done.7.refs_6_), channel_id=1, source_target_pairs={{0,1},{1,0},{2,3},{3,2},{4,5},{5,4},{6,7},{7,6},{8,9},{9,8},{10,11... | collective-permute-start | bytes 491528 | tf_op jit(solution)/shard_map/ppermute | solution.py:604
  74.7 0.1 collective-permute-start.12
  74.8 0.4 collective-permute-start.13
  75.2 9.7 %collective-permute-done.22.refs_7_ = f32[320,128]{1,0:T(8,128)S(1)} collective-permute-done((f32[320,128]{1,0:T(8,128)S(1)}, f32[320,128]{1,0:T(8,128)S(1)}, u32[]{:S(2)}, u32[]{:S(2)}) %collective-permute-start.22) | collective-permute-done | bytes 163872 | tf_op jit(solution)/shard_map/ppermute | solution.py:604
  85.0 1.3 %collective-permute-start.24 = (f32[320,128]{1,0:T(8,128)S(1)}, f32[320,128]{1,0:T(8,128)S(1)}, u32[]{:S(2)}, u32[]{:S(2)}) collective-permute-start(f32[320,128]{1,0:T(8,128)S(1)} %get-tuple-element.83.refs_5_), channel_id=1, source_target_pairs={{0,1},{1,0},{2,3},{3,2},{4,5},{5,4},{6,7},{7,6},{8,9},{9,8},{10,11... | collective-permute-start | bytes 491528 | tf_op jit(solution)/shard_map/ppermute | solution.py:604
  86.3 0.5 collective-permute-start.26
  86.9 1.3 %assemble.2 = (bf16[128,1280]{1,0:T(8,128)(2,1)S(1)}, bf16[128,1280]{1,0:T(8,128)(2,1)S(1)}, f32[8,128]{1,0:T(8,128)S(1)}) custom-call(s32[2]{0:T(128)S(1)} %copy-done.5, f32[8,128]{1,0:T(8,128)S(1)} %slice.11.refs_1_, f32[1288,128]{1,0:T(8,128)S(1)} %collective-permute-done.refs_2_, f32[128,2560]{1,0:T(8,128)S(1)} %copy-done, f32[128,2560]{1,0:T(8,128)S(1)} %copy-done.1, ...), custom_call_target="tpu_custom_call" | custom-call | tf_op jit(solution)/shard_map/assemble/pallas_call | solution.py:486
  88.2 0.7 copy-done.10
  89.0 0.7 copy-done.11
  89.7 5.4 %finish.2 = (bf16[256,2560]{1,0:T(8,128)(2,1)}, f32[256,128]{1,0:T(8,128)}, f32[256,128]{1,0:T(8,128)}, f32[256,128]{1,0:T(8,128)}) custom-call(bf16[256,2560]{1,0:T(8,128)(2,1)} %refs_0_.3, bf16[256,2560]{1,0:T(8,128)(2,1)} %refs_1_.9, bf16[256,128]{1,0:T(8,128)(2,1)} %refs_2_.9, bf16[256,128]{1,0:T(8,128)(2,1)} %refs_3_.9, ...), custom_call_target="tpu_custom_call" | custom-call | flops 3000000000 | bytes 5000000 | tf_op jit(solution)/shard_map/finish/pallas_call | solution.py:545
  95.0 0.7 slice.12.refs_1_
  95.7 1.4 %assemble.3 = (bf16[128,1280]{1,0:T(8,128)(2,1)S(1)}, bf16[128,1280]{1,0:T(8,128)(2,1)S(1)}, f32[8,128]{1,0:T(8,128)S(1)}) custom-call(s32[2]{0:T(128)S(1)} %copy-done.5, f32[8,128]{1,0:T(8,128)S(1)} %slice.12.refs_1_, f32[1288,128]{1,0:T(8,128)S(1)} %collective-permute-done.14.refs_2_, f32[128,2560]{1,0:T(8,128)S(1)} %copy-done, f32[128,2560]{1,0:T(8,128)S(1)} %copy-done.1, ...), custom_call_target="tpu_custom_call" | custom-call | tf_op jit(solution)/shard_map/assemble/pallas_call | solution.py:486
  97.1 0.7 copy-done.8
  97.8 0.7 copy-done.9
  98.5 0.4 collective-permute-start.35
  99.1 0.8 collective-permute-done.35
  99.8 2.7 %collective-permute-start.38 = (f32[8,128]{1,0:T(8,128)S(1)}, f32[8,128]{1,0:T(8,128)S(1)}, u32[]{:S(2)}, u32[]{:S(2)}) collective-permute-start(f32[8,128]{1,0:T(8,128)S(1)} %add.79), channel_id=1, source_target_pairs={{0,6},{1,7},{2,4},{3,5},{4,2},{5,3},{6,0},{7,1},{8,14},{9,15},{10,... | collective-permute-start | bytes 12296 | tf_op jit(solution)/shard_map/ppermute | solution.py:604
  102.5 1.9 %collective-permute-start.37 = (f32[8,128]{1,0:T(8,128)S(1)}, f32[8,128]{1,0:T(8,128)S(1)}, u32[]{:S(2)}, u32[]{:S(2)}) collective-permute-start(f32[8,128]{1,0:T(8,128)S(1)} %add.79), channel_id=1, source_target_pairs={{0,4},{1,5},{2,6},{3,7},{4,0},{5,1},{6,2},{7,3},{8,12},{9,13},{10,... | collective-permute-start | bytes 12296 | tf_op jit(solution)/shard_map/ppermute | solution.py:604
  104.4 0.1 collective-permute-start.36
  104.5 2.4 %collective-permute-start.31 = (f32[8,128]{1,0:T(8,128)S(1)}, f32[8,128]{1,0:T(8,128)S(1)}, u32[]{:S(2)}, u32[]{:S(2)}) collective-permute-start(f32[8,128]{1,0:T(8,128)S(1)} %add.69), channel_id=1, source_target_pairs={{0,6},{1,7},{2,4},{3,5},{4,2},{5,3},{6,0},{7,1},{8,14},{9,15},{10,... | collective-permute-start | bytes 12296 | tf_op jit(solution)/shard_map/ppermute | solution.py:604
  107.0 1.0 collective-permute-start.30
  107.9 1.0 collective-permute-start.29
  108.9 1.3 %collective-permute-start.41 = (f32[8,128]{1,0:T(8,128)S(1)}, f32[8,128]{1,0:T(8,128)S(1)}, u32[]{:S(2)}, u32[]{:S(2)}) collective-permute-start(f32[8,128]{1,0:T(8,128)S(1)} %add_add_fusion.1), channel_id=1, source_target_pairs={{24,0},{25,1},{26,2},{27,3},{28,4},{29,5},{30,6},{31,7}} | collective-permute-start | bytes 12296 | tf_op jit(solution)/shard_map/ppermute | solution.py:604
  110.2 1.3 %collective-permute-start.40 = (f32[8,128]{1,0:T(8,128)S(1)}, f32[8,128]{1,0:T(8,128)S(1)}, u32[]{:S(2)}, u32[]{:S(2)}) collective-permute-start(f32[8,128]{1,0:T(8,128)S(1)} %add_add_fusion.1), channel_id=1, source_target_pairs={{16,0},{17,1},{18,2},{19,3},{20,4},{21,5},{22,6},{23,7},{24,8},{25... | collective-permute-start | bytes 12296 | tf_op jit(solution)/shard_map/ppermute | solution.py:604
  111.6 1.3 %collective-permute-start.39 = (f32[8,128]{1,0:T(8,128)S(1)}, f32[8,128]{1,0:T(8,128)S(1)}, u32[]{:S(2)}, u32[]{:S(2)}) collective-permute-start(f32[8,128]{1,0:T(8,128)S(1)} %add_add_fusion.1), channel_id=1, source_target_pairs={{8,0},{9,1},{10,2},{11,3},{12,4},{13,5},{14,6},{15,7},{16,8},{17,9... | collective-permute-start | bytes 12296 | tf_op jit(solution)/shard_map/ppermute | solution.py:604
  112.9 1.3 %collective-permute-start.34 = (f32[8,128]{1,0:T(8,128)S(1)}, f32[8,128]{1,0:T(8,128)S(1)}, u32[]{:S(2)}, u32[]{:S(2)}) collective-permute-start(f32[8,128]{1,0:T(8,128)S(1)} %add_add_fusion.2), channel_id=1, source_target_pairs={{24,0},{25,1},{26,2},{27,3},{28,4},{29,5},{30,6},{31,7}} | collective-permute-start | bytes 12296 | tf_op jit(solution)/shard_map/ppermute | solution.py:604
  114.2 1.3 %collective-permute-start.33 = (f32[8,128]{1,0:T(8,128)S(1)}, f32[8,128]{1,0:T(8,128)S(1)}, u32[]{:S(2)}, u32[]{:S(2)}) collective-permute-start(f32[8,128]{1,0:T(8,128)S(1)} %add_add_fusion.2), channel_id=1, source_target_pairs={{16,0},{17,1},{18,2},{19,3},{20,4},{21,5},{22,6},{23,7},{24,8},{25... | collective-permute-start | bytes 12296 | tf_op jit(solution)/shard_map/ppermute | solution.py:604
  115.5 1.3 %collective-permute-start.32 = (f32[8,128]{1,0:T(8,128)S(1)}, f32[8,128]{1,0:T(8,128)S(1)}, u32[]{:S(2)}, u32[]{:S(2)}) collective-permute-start(f32[8,128]{1,0:T(8,128)S(1)} %add_add_fusion.2), channel_id=1, source_target_pairs={{8,0},{9,1},{10,2},{11,3},{12,4},{13,5},{14,6},{15,7},{16,8},{17,9... | collective-permute-start | bytes 12296 | tf_op jit(solution)/shard_map/ppermute | solution.py:604
  116.8 5.4 %finish.3 = (bf16[256,2560]{1,0:T(8,128)(2,1)}, bf16[256,128]{1,0:T(8,128)(2,1)}, bf16[256,128]{1,0:T(8,128)(2,1)}, f32[256,128]{1,0:T(8,128)}) custom-call(bf16[256,2560]{1,0:T(8,128)(2,1)} %refs_0_.3, bf16[256,2560]{1,0:T(8,128)(2,1)} %refs_1_.9, bf16[256,128]{1,0:T(8,128)(2,1)} %refs_2_.9, ...), custom_call_target="tpu_custom_call", output_to_operand_aliasing={{0}: (12, {})} | custom-call | flops 3000000000 | bytes 5000000 | tf_op jit(solution)/shard_map/finish/pallas_call | solution.py:545
  122.3 0.6 add_add_fusion.later_ref
  122.9 1.8 %suffix.1 = f32[40,256]{1,0:T(8,128)} custom-call(f32[256,128]{1,0:T(8,128)} %get-tuple-element.93.change_ref, f32[8,128]{1,0:T(8,128)} %add_add_fusion.later_ref), custom_call_target="tpu_custom_call" | custom-call | tf_op jit(solution)/shard_map/suffix/pallas_call | solution.py:579
  (67 shorter events, 0.3 us)
Async XLA Ops:
  5.1 4.1 %collective-permute-start = (f32[1288,128]{1,0:T(8,128)}, f32[1288,128]{1,0:T(8,128)S(1)}, u32[]{:S(2)}, u32[]{:S(2)}) collective-permute-start(f32[1288,128]{1,0:T(8,128)} %get-tuple-element.53), channel_id=1, source_target_pairs={{0,1},{1,0},{2,3},{3,2},{4,5},{5,4},{6,7},{7,6},{8,9},{9,8},{10,11... | collective-permute-start | bytes 1978376 | tf_op jit(solution)/shard_map/ppermute | solution.py:604
  5.6 3.6 %copy-start.3 = (f32[1280,128]{1,0:T(8,128)S(1)}, f32[1280,128]{1,0:T(8,128)}, u32[]{:S(2)}) copy-start(f32[1280,128]{1,0:T(8,128)} %get-tuple-element.54.refs_3_) | copy-start | bytes 1966084
  5.6 3.6 %copy-start.4 = (f32[8,128]{1,0:T(8,128)S(1)}, f32[8,128]{1,0:T(8,128)}, u32[]{:S(2)}) copy-start(f32[8,128]{1,0:T(8,128)} %get-tuple-element.52.refs_1_.refs_5_) | copy-start | bytes 12292
  5.6 3.6 %copy-start.5 = (s32[2]{0:T(128)S(1)}, s32[2]{0:T(128)}, u32[]{:S(2)}) copy-start(s32[2]{0:T(128)} %pad_add_fusion.refs_0_) | copy-start | bytes 28
  5.6 3.6 %copy-start.7 = (f32[10,128]{1,0:T(8,128)S(1)}, f32[10,128]{1,0:T(8,128)}, u32[]{:S(2)}) copy-start(f32[10,128]{1,0:T(8,128)} %get-tuple-element.55.refs_4_) | copy-start | bytes 15364
  9.2 21.6 %collective-permute-start.14 = (f32[1288,128]{1,0:T(8,128)}, f32[1288,128]{1,0:T(8,128)S(1)}, u32[]{:S(2)}, u32[]{:S(2)}) collective-permute-start(f32[1288,128]{1,0:T(8,128)} %get-tuple-element.76), channel_id=1, source_target_pairs={{0,1},{1,0},{2,3},{3,2},{4,5},{5,4},{6,7},{7,6},{8,9},{9,8},{10,11... | collective-permute-start | bytes 1978376 | tf_op jit(solution)/shard_map/ppermute | solution.py:604
  10.5 25.4 %collective-permute-start.1 = (f32[328,128]{1,0:T(8,128)S(1)}, f32[328,128]{1,0:T(8,128)S(1)}, u32[]{:S(2)}, u32[]{:S(2)}) collective-permute-start(f32[328,128]{1,0:T(8,128)S(1)} %get-tuple-element.64), channel_id=1, source_target_pairs={{0,2},{1,3},{2,0},{3,1},{4,6},{5,7},{6,4},{7,5},{8,10},{9,11},{10,... | collective-permute-start | bytes 503816 | tf_op jit(solution)/shard_map/ppermute | solution.py:604
  13.5 22.4 %collective-permute-start.2 = (f32[328,128]{1,0:T(8,128)S(1)}, f32[328,128]{1,0:T(8,128)S(1)}, u32[]{:S(2)}, u32[]{:S(2)}) collective-permute-start(f32[328,128]{1,0:T(8,128)S(1)} %get-tuple-element.65), channel_id=1, source_target_pairs={{0,4},{1,5},{2,6},{3,7},{4,0},{5,1},{6,2},{7,3},{8,12},{9,13},{10,... | collective-permute-start | bytes 503816 | tf_op jit(solution)/shard_map/ppermute | solution.py:604
  16.1 19.8 %collective-permute-start.3 = (f32[328,128]{1,0:T(8,128)S(1)}, f32[328,128]{1,0:T(8,128)S(1)}, u32[]{:S(2)}, u32[]{:S(2)}) collective-permute-start(f32[328,128]{1,0:T(8,128)S(1)} %get-tuple-element.66), channel_id=1, source_target_pairs={{0,6},{1,7},{2,4},{3,5},{4,2},{5,3},{6,0},{7,1},{8,14},{9,15},{10,... | collective-permute-start | bytes 503816 | tf_op jit(solution)/shard_map/ppermute | solution.py:604
  16.1 14.7 %copy-start.2 = (f32[1280,128]{1,0:T(8,128)S(1)}, f32[1280,128]{1,0:T(8,128)}, u32[]{:S(2)}) copy-start(f32[1280,128]{1,0:T(8,128)} %get-tuple-element.77.refs_3_) | copy-start | bytes 1966084
  16.1 14.7 %copy-start.6 = (f32[10,128]{1,0:T(8,128)S(1)}, f32[10,128]{1,0:T(8,128)}, u32[]{:S(2)}) copy-start(f32[10,128]{1,0:T(8,128)} %get-tuple-element.78.refs_4_) | copy-start | bytes 15364
  31.4 8.0 %collective-permute-start.15 = (f32[328,128]{1,0:T(8,128)S(1)}, f32[328,128]{1,0:T(8,128)S(1)}, u32[]{:S(2)}, u32[]{:S(2)}) collective-permute-start(f32[328,128]{1,0:T(8,128)S(1)} %get-tuple-element.80), channel_id=1, source_target_pairs={{0,2},{1,3},{2,0},{3,1},{4,6},{5,7},{6,4},{7,5},{8,10},{9,11},{10,... | collective-permute-start | bytes 503816 | tf_op jit(solution)/shard_map/ppermute | solution.py:604
  32.4 15.9 %collective-permute-start.16 = (f32[328,128]{1,0:T(8,128)S(1)}, f32[328,128]{1,0:T(8,128)S(1)}, u32[]{:S(2)}, u32[]{:S(2)}) collective-permute-start(f32[328,128]{1,0:T(8,128)S(1)} %get-tuple-element.81), channel_id=1, source_target_pairs={{0,4},{1,5},{2,6},{3,7},{4,0},{5,1},{6,2},{7,3},{8,12},{9,13},{10,... | collective-permute-start | bytes 503816 | tf_op jit(solution)/shard_map/ppermute | solution.py:604
  35.9 12.4 %collective-permute-start.17 = (f32[328,128]{1,0:T(8,128)S(1)}, f32[328,128]{1,0:T(8,128)S(1)}, u32[]{:S(2)}, u32[]{:S(2)}) collective-permute-start(f32[328,128]{1,0:T(8,128)S(1)} %get-tuple-element.82), channel_id=1, source_target_pairs={{0,6},{1,7},{2,4},{3,5},{4,2},{5,3},{6,0},{7,1},{8,14},{9,15},{10,... | collective-permute-start | bytes 503816 | tf_op jit(solution)/shard_map/ppermute | solution.py:604
  36.7 15.1 %collective-permute-start.4 = (f32[328,128]{1,0:T(8,128)S(1)}, f32[328,128]{1,0:T(8,128)S(1)}, u32[]{:S(2)}, u32[]{:S(2)}) collective-permute-start(f32[328,128]{1,0:T(8,128)S(1)} %group_total.2), channel_id=1, source_target_pairs={{1,9},{3,11},{5,13},{7,15},{8,0},{9,17},{10,2},{11,19},{12,4},{13,... | collective-permute-start | bytes 503816 | tf_op jit(solution)/shard_map/ppermute | solution.py:604
  38.0 15.1 %collective-permute-start.5 = (f32[328,128]{1,0:T(8,128)S(1)}, f32[328,128]{1,0:T(8,128)S(1)}, u32[]{:S(2)}, u32[]{:S(2)}) collective-permute-start(f32[328,128]{1,0:T(8,128)S(1)} %group_total.2), channel_id=1, source_target_pairs={{1,17},{3,19},{5,21},{7,23},{9,25},{11,27},{13,29},{15,31},{16,0},... | collective-permute-start | bytes 503816 | tf_op jit(solution)/shard_map/ppermute | solution.py:604
  39.4 13.7 %collective-permute-start.6 = (f32[328,128]{1,0:T(8,128)S(1)}, f32[328,128]{1,0:T(8,128)S(1)}, u32[]{:S(2)}, u32[]{:S(2)}) collective-permute-start(f32[328,128]{1,0:T(8,128)S(1)} %group_total.2), channel_id=1, source_target_pairs={{1,25},{3,27},{5,29},{7,31},{24,0},{26,2},{28,4},{30,6}} | collective-permute-start | bytes 503816 | tf_op jit(solution)/shard_map/ppermute | solution.py:604
  48.3 38.6 %copy-start.1 = (f32[128,2560]{1,0:T(8,128)S(1)}, f32[128,2560]{1,0:T(8,128)}, u32[]{:S(2)}) copy-start(f32[128,2560]{1,0:T(8,128)} %get-tuple-element.63.refs_4_) | copy-start | bytes 3932164
  49.1 37.8 %copy-start = (f32[128,2560]{1,0:T(8,128)S(1)}, f32[128,2560]{1,0:T(8,128)}, u32[]{:S(2)}) copy-start(f32[128,2560]{1,0:T(8,128)} %get-tuple-element.62.refs_3_) | copy-start | bytes 3932164
  49.1 8.6 %collective-permute-start.18 = (f32[328,128]{1,0:T(8,128)S(1)}, f32[328,128]{1,0:T(8,128)S(1)}, u32[]{:S(2)}, u32[]{:S(2)}) collective-permute-start(f32[328,128]{1,0:T(8,128)S(1)} %group_total.3), channel_id=1, source_target_pairs={{1,9},{3,11},{5,13},{7,15},{8,0},{9,17},{10,2},{11,19},{12,4},{13,... | collective-permute-start | bytes 503816 | tf_op jit(solution)/shard_map/ppermute | solution.py:604
  50.5 8.6 %collective-permute-start.19 = (f32[328,128]{1,0:T(8,128)S(1)}, f32[328,128]{1,0:T(8,128)S(1)}, u32[]{:S(2)}, u32[]{:S(2)}) collective-permute-start(f32[328,128]{1,0:T(8,128)S(1)} %group_total.3), channel_id=1, source_target_pairs={{1,17},{3,19},{5,21},{7,23},{9,25},{11,27},{13,29},{15,31},{16,0},... | collective-permute-start | bytes 503816 | tf_op jit(solution)/shard_map/ppermute | solution.py:604
  51.8 9.3 %collective-permute-start.20 = (f32[328,128]{1,0:T(8,128)S(1)}, f32[328,128]{1,0:T(8,128)S(1)}, u32[]{:S(2)}, u32[]{:S(2)}) collective-permute-start(f32[328,128]{1,0:T(8,128)S(1)} %group_total.3), channel_id=1, source_target_pairs={{1,25},{3,27},{5,29},{7,31},{24,0},{26,2},{28,4},{30,6}} | collective-permute-start | bytes 503816 | tf_op jit(solution)/shard_map/ppermute | solution.py:604
  54.2 10.5 %collective-permute-start.7 = (f32[320,128]{1,0:T(8,128)S(1)}, f32[320,128]{1,0:T(8,128)S(1)}, u32[]{:S(2)}, u32[]{:S(2)}) collective-permute-start(f32[320,128]{1,0:T(8,128)S(1)} %get-tuple-element.68), channel_id=1, source_target_pairs={{0,2},{1,3},{2,0},{3,1},{4,6},{5,7},{6,4},{7,5},{8,10},{9,11},{10,... | collective-permute-start | bytes 491528 | tf_op jit(solution)/shard_map/ppermute | solution.py:604
  56.6 9.1 %collective-permute-start.8 = (f32[320,128]{1,0:T(8,128)S(1)}, f32[320,128]{1,0:T(8,128)S(1)}, u32[]{:S(2)}, u32[]{:S(2)}) collective-permute-start(f32[320,128]{1,0:T(8,128)S(1)} %get-tuple-element.69), channel_id=1, source_target_pairs={{0,4},{1,5},{2,6},{3,7},{4,0},{5,1},{6,2},{7,3},{8,12},{9,13},{10,... | collective-permute-start | bytes 491528 | tf_op jit(solution)/shard_map/ppermute | solution.py:604
  57.7 15.0 %collective-permute-start.9 = (f32[320,128]{1,0:T(8,128)S(1)}, f32[320,128]{1,0:T(8,128)S(1)}, u32[]{:S(2)}, u32[]{:S(2)}) collective-permute-start(f32[320,128]{1,0:T(8,128)S(1)} %get-tuple-element.70), channel_id=1, source_target_pairs={{0,6},{1,7},{2,4},{3,5},{4,2},{5,3},{6,0},{7,1},{8,14},{9,15},{10,... | collective-permute-start | bytes 491528 | tf_op jit(solution)/shard_map/ppermute | solution.py:604
  59.1 15.6 %collective-permute-start.10 = (f32[320,128]{1,0:T(8,128)S(1)}, f32[320,128]{1,0:T(8,128)S(1)}, u32[]{:S(2)}, u32[]{:S(2)}) collective-permute-start(f32[320,128]{1,0:T(8,128)S(1)} %get-tuple-element.67.refs_5_), channel_id=1, source_target_pairs={{0,1},{1,0},{2,3},{3,2},{4,5},{5,4},{6,7},{7,6},{8,9},{9,8},{10,11... | collective-permute-start | bytes 491528 | tf_op jit(solution)/shard_map/ppermute | solution.py:604
  62.2 12.6 %collective-permute-start.21 = (f32[320,128]{1,0:T(8,128)S(1)}, f32[320,128]{1,0:T(8,128)S(1)}, u32[]{:S(2)}, u32[]{:S(2)}) collective-permute-start(f32[320,128]{1,0:T(8,128)S(1)} %get-tuple-element.84), channel_id=1, source_target_pairs={{0,2},{1,3},{2,0},{3,1},{4,6},{5,7},{6,4},{7,5},{8,10},{9,11},{10,... | collective-permute-start | bytes 491528 | tf_op jit(solution)/shard_map/ppermute | solution.py:604
  64.7 20.3 %collective-permute-start.22 = (f32[320,128]{1,0:T(8,128)S(1)}, f32[320,128]{1,0:T(8,128)S(1)}, u32[]{:S(2)}, u32[]{:S(2)}) collective-permute-start(f32[320,128]{1,0:T(8,128)S(1)} %get-tuple-element.85), channel_id=1, source_target_pairs={{0,4},{1,5},{2,6},{3,7},{4,0},{5,1},{6,2},{7,3},{8,12},{9,13},{10,... | collective-permute-start | bytes 491528 | tf_op jit(solution)/shard_map/ppermute | solution.py:604
  65.7 20.6 %collective-permute-start.23 = (f32[320,128]{1,0:T(8,128)S(1)}, f32[320,128]{1,0:T(8,128)S(1)}, u32[]{:S(2)}, u32[]{:S(2)}) collective-permute-start(f32[320,128]{1,0:T(8,128)S(1)} %get-tuple-element.86), channel_id=1, source_target_pairs={{0,6},{1,7},{2,4},{3,5},{4,2},{5,3},{6,0},{7,1},{8,14},{9,15},{10,... | collective-permute-start | bytes 491528 | tf_op jit(solution)/shard_map/ppermute | solution.py:604
  72.7 13.6 %collective-permute-start.11 = (f32[320,128]{1,0:T(8,128)S(1)}, f32[320,128]{1,0:T(8,128)S(1)}, u32[]{:S(2)}, u32[]{:S(2)}) collective-permute-start(f32[320,128]{1,0:T(8,128)S(1)} %collective-permute-done.7.refs_6_), channel_id=1, source_target_pairs={{0,1},{1,0},{2,3},{3,2},{4,5},{5,4},{6,7},{7,6},{8,9},{9,8},{10,11... | collective-permute-start | bytes 491528 | tf_op jit(solution)/shard_map/ppermute | solution.py:604
  74.7 12.1 %collective-permute-start.12 = (f32[320,128]{1,0:T(8,128)S(1)}, f32[320,128]{1,0:T(8,128)S(1)}, u32[]{:S(2)}, u32[]{:S(2)}) collective-permute-start(f32[320,128]{1,0:T(8,128)S(1)} %collective-permute-done.8.refs_7_), channel_id=1, source_target_pairs={{0,1},{1,0},{2,3},{3,2},{4,5},{5,4},{6,7},{7,6},{8,9},{9,8},{10,11... | collective-permute-start | bytes 491528 | tf_op jit(solution)/shard_map/ppermute | solution.py:604
  74.8 12.1 %collective-permute-start.13 = (f32[320,128]{1,0:T(8,128)S(1)}, f32[320,128]{1,0:T(8,128)S(1)}, u32[]{:S(2)}, u32[]{:S(2)}) collective-permute-start(f32[320,128]{1,0:T(8,128)S(1)} %collective-permute-done.9.refs_8_), channel_id=1, source_target_pairs={{0,1},{1,0},{2,3},{3,2},{4,5},{5,4},{6,7},{7,6},{8,9},{9,8},{10,11... | collective-permute-start | bytes 491528 | tf_op jit(solution)/shard_map/ppermute | solution.py:604
  85.0 10.7 %collective-permute-start.24 = (f32[320,128]{1,0:T(8,128)S(1)}, f32[320,128]{1,0:T(8,128)S(1)}, u32[]{:S(2)}, u32[]{:S(2)}) collective-permute-start(f32[320,128]{1,0:T(8,128)S(1)} %get-tuple-element.83.refs_5_), channel_id=1, source_target_pairs={{0,1},{1,0},{2,3},{3,2},{4,5},{5,4},{6,7},{7,6},{8,9},{9,8},{10,11... | collective-permute-start | bytes 491528 | tf_op jit(solution)/shard_map/ppermute | solution.py:604
  86.3 9.4 %collective-permute-start.25 = (f32[320,128]{1,0:T(8,128)S(1)}, f32[320,128]{1,0:T(8,128)S(1)}, u32[]{:S(2)}, u32[]{:S(2)}) collective-permute-start(f32[320,128]{1,0:T(8,128)S(1)} %collective-permute-done.21.refs_6_), channel_id=1, source_target_pairs={{0,1},{1,0},{2,3},{3,2},{4,5},{5,4},{6,7},{7,6},{8,9},{9,8},{10,11... | collective-permute-start | bytes 491528 | tf_op jit(solution)/shard_map/ppermute | solution.py:604
  86.3 9.4 %collective-permute-start.26 = (f32[320,128]{1,0:T(8,128)S(1)}, f32[320,128]{1,0:T(8,128)S(1)}, u32[]{:S(2)}, u32[]{:S(2)}) collective-permute-start(f32[320,128]{1,0:T(8,128)S(1)} %collective-permute-done.22.refs_7_), channel_id=1, source_target_pairs={{0,1},{1,0},{2,3},{3,2},{4,5},{5,4},{6,7},{7,6},{8,9},{9,8},{10,11... | collective-permute-start | bytes 491528 | tf_op jit(solution)/shard_map/ppermute | solution.py:604
  86.8 8.9 %collective-permute-start.27 = (f32[320,128]{1,0:T(8,128)S(1)}, f32[320,128]{1,0:T(8,128)S(1)}, u32[]{:S(2)}, u32[]{:S(2)}) collective-permute-start(f32[320,128]{1,0:T(8,128)S(1)} %collective-permute-done.23.refs_8_), channel_id=1, source_target_pairs={{0,1},{1,0},{2,3},{3,2},{4,5},{5,4},{6,7},{7,6},{8,9},{9,8},{10,11... | collective-permute-start | bytes 491528 | tf_op jit(solution)/shard_map/ppermute | solution.py:604
  88.2 0.7 copy-start.10
  89.0 0.7 copy-start.11
  97.1 0.7 copy-start.8
  97.8 0.7 copy-start.9
  98.5 1.3 %collective-permute-start.35 = (f32[8,128]{1,0:T(8,128)S(1)}, f32[8,128]{1,0:T(8,128)S(1)}, u32[]{:S(2)}, u32[]{:S(2)}) collective-permute-start(f32[8,128]{1,0:T(8,128)S(1)} %get-tuple-element.95), channel_id=1, source_target_pairs={{0,1},{1,0},{2,3},{3,2},{4,5},{5,4},{6,7},{7,6},{8,9},{9,8},{10,11... | collective-permute-start | bytes 12296 | tf_op jit(solution)/shard_map/ppermute | solution.py:604
  99.0 5.5 %collective-permute-start.28 = (f32[8,128]{1,0:T(8,128)S(1)}, f32[8,128]{1,0:T(8,128)S(1)}, u32[]{:S(2)}, u32[]{:S(2)}) collective-permute-start(f32[8,128]{1,0:T(8,128)S(1)} %get-tuple-element.94), channel_id=1, source_target_pairs={{0,1},{1,0},{2,3},{3,2},{4,5},{5,4},{6,7},{7,6},{8,9},{9,8},{10,11... | collective-permute-start | bytes 12296 | tf_op jit(solution)/shard_map/ppermute | solution.py:604
  99.8 8.1 %collective-permute-start.38 = (f32[8,128]{1,0:T(8,128)S(1)}, f32[8,128]{1,0:T(8,128)S(1)}, u32[]{:S(2)}, u32[]{:S(2)}) collective-permute-start(f32[8,128]{1,0:T(8,128)S(1)} %add.79), channel_id=1, source_target_pairs={{0,6},{1,7},{2,4},{3,5},{4,2},{5,3},{6,0},{7,1},{8,14},{9,15},{10,... | collective-permute-start | bytes 12296 | tf_op jit(solution)/shard_map/ppermute | solution.py:604
  102.5 6.4 %collective-permute-start.37 = (f32[8,128]{1,0:T(8,128)S(1)}, f32[8,128]{1,0:T(8,128)S(1)}, u32[]{:S(2)}, u32[]{:S(2)}) collective-permute-start(f32[8,128]{1,0:T(8,128)S(1)} %add.79), channel_id=1, source_target_pairs={{0,4},{1,5},{2,6},{3,7},{4,0},{5,1},{6,2},{7,3},{8,12},{9,13},{10,... | collective-permute-start | bytes 12296 | tf_op jit(solution)/shard_map/ppermute | solution.py:604
  104.4 4.5 %collective-permute-start.36 = (f32[8,128]{1,0:T(8,128)S(1)}, f32[8,128]{1,0:T(8,128)S(1)}, u32[]{:S(2)}, u32[]{:S(2)}) collective-permute-start(f32[8,128]{1,0:T(8,128)S(1)} %add.79), channel_id=1, source_target_pairs={{0,2},{1,3},{2,0},{3,1},{4,6},{5,7},{6,4},{7,5},{8,10},{9,11},{10,... | collective-permute-start | bytes 12296 | tf_op jit(solution)/shard_map/ppermute | solution.py:604
  104.5 7.0 %collective-permute-start.31 = (f32[8,128]{1,0:T(8,128)S(1)}, f32[8,128]{1,0:T(8,128)S(1)}, u32[]{:S(2)}, u32[]{:S(2)}) collective-permute-start(f32[8,128]{1,0:T(8,128)S(1)} %add.69), channel_id=1, source_target_pairs={{0,6},{1,7},{2,4},{3,5},{4,2},{5,3},{6,0},{7,1},{8,14},{9,15},{10,... | collective-permute-start | bytes 12296 | tf_op jit(solution)/shard_map/ppermute | solution.py:604
  107.0 5.9 %collective-permute-start.30 = (f32[8,128]{1,0:T(8,128)S(1)}, f32[8,128]{1,0:T(8,128)S(1)}, u32[]{:S(2)}, u32[]{:S(2)}) collective-permute-start(f32[8,128]{1,0:T(8,128)S(1)} %add.69), channel_id=1, source_target_pairs={{0,4},{1,5},{2,6},{3,7},{4,0},{5,1},{6,2},{7,3},{8,12},{9,13},{10,... | collective-permute-start | bytes 12296 | tf_op jit(solution)/shard_map/ppermute | solution.py:604
  107.9 4.9 %collective-permute-start.29 = (f32[8,128]{1,0:T(8,128)S(1)}, f32[8,128]{1,0:T(8,128)S(1)}, u32[]{:S(2)}, u32[]{:S(2)}) collective-permute-start(f32[8,128]{1,0:T(8,128)S(1)} %add.69), channel_id=1, source_target_pairs={{0,2},{1,3},{2,0},{3,1},{4,6},{5,7},{6,4},{7,5},{8,10},{9,11},{10,... | collective-permute-start | bytes 12296 | tf_op jit(solution)/shard_map/ppermute | solution.py:604
  108.9 6.5 %collective-permute-start.41 = (f32[8,128]{1,0:T(8,128)S(1)}, f32[8,128]{1,0:T(8,128)S(1)}, u32[]{:S(2)}, u32[]{:S(2)}) collective-permute-start(f32[8,128]{1,0:T(8,128)S(1)} %add_add_fusion.1), channel_id=1, source_target_pairs={{24,0},{25,1},{26,2},{27,3},{28,4},{29,5},{30,6},{31,7}} | collective-permute-start | bytes 12296 | tf_op jit(solution)/shard_map/ppermute | solution.py:604
  110.2 12.0 %collective-permute-start.40 = (f32[8,128]{1,0:T(8,128)S(1)}, f32[8,128]{1,0:T(8,128)S(1)}, u32[]{:S(2)}, u32[]{:S(2)}) collective-permute-start(f32[8,128]{1,0:T(8,128)S(1)} %add_add_fusion.1), channel_id=1, source_target_pairs={{16,0},{17,1},{18,2},{19,3},{20,4},{21,5},{22,6},{23,7},{24,8},{25... | collective-permute-start | bytes 12296 | tf_op jit(solution)/shard_map/ppermute | solution.py:604
  111.6 10.7 %collective-permute-start.39 = (f32[8,128]{1,0:T(8,128)S(1)}, f32[8,128]{1,0:T(8,128)S(1)}, u32[]{:S(2)}, u32[]{:S(2)}) collective-permute-start(f32[8,128]{1,0:T(8,128)S(1)} %add_add_fusion.1), channel_id=1, source_target_pairs={{8,0},{9,1},{10,2},{11,3},{12,4},{13,5},{14,6},{15,7},{16,8},{17,9... | collective-permute-start | bytes 12296 | tf_op jit(solution)/shard_map/ppermute | solution.py:604
  112.9 9.3 %collective-permute-start.34 = (f32[8,128]{1,0:T(8,128)S(1)}, f32[8,128]{1,0:T(8,128)S(1)}, u32[]{:S(2)}, u32[]{:S(2)}) collective-permute-start(f32[8,128]{1,0:T(8,128)S(1)} %add_add_fusion.2), channel_id=1, source_target_pairs={{24,0},{25,1},{26,2},{27,3},{28,4},{29,5},{30,6},{31,7}} | collective-permute-start | bytes 12296 | tf_op jit(solution)/shard_map/ppermute | solution.py:604
  114.2 8.1 %collective-permute-start.33 = (f32[8,128]{1,0:T(8,128)S(1)}, f32[8,128]{1,0:T(8,128)S(1)}, u32[]{:S(2)}, u32[]{:S(2)}) collective-permute-start(f32[8,128]{1,0:T(8,128)S(1)} %add_add_fusion.2), channel_id=1, source_target_pairs={{16,0},{17,1},{18,2},{19,3},{20,4},{21,5},{22,6},{23,7},{24,8},{25... | collective-permute-start | bytes 12296 | tf_op jit(solution)/shard_map/ppermute | solution.py:604
  115.5 6.8 %collective-permute-start.32 = (f32[8,128]{1,0:T(8,128)S(1)}, f32[8,128]{1,0:T(8,128)S(1)}, u32[]{:S(2)}, u32[]{:S(2)}) collective-permute-start(f32[8,128]{1,0:T(8,128)S(1)} %add_add_fusion.2), channel_id=1, source_target_pairs={{8,0},{9,1},{10,2},{11,3},{12,4},{13,5},{14,6},{15,7},{16,8},{17,9... | collective-permute-start | bytes 12296 | tf_op jit(solution)/shard_map/ppermute | solution.py:604

commit v4 on v3

--- a/solution.py
+++ b/solution.py
@@ -228,8 +228,10 @@
     size = strips * (STATE // chips)
     return pl.pallas_call(
         lambda *refs: combine_kernel(chips, *refs),
+        grid=(1,),
         in_specs=[SCALARS]
-        + [whole(*value.shape) for value in (after, first, keep, decay, log)],
+        + [whole(META, STRIP)]
+        + [whole(*value.shape) for value in (first, keep, decay, log)],
         out_specs=[whole(size + META, STRIP)] * chips,
         out_shape=[jax.ShapeDtypeStruct((size + META, STRIP), F32)] * chips,
         compiler_params=pltpu.CompilerParams(vmem_limit_bytes=SMALL_VMEM),
@@ -275,7 +277,8 @@
     strips = (at[0].shape[0] - META) * len(at) // STATE
     return pl.pallas_call(
         lambda *refs: total_kernel(half * strips, strips, head_size, *refs),
-        in_specs=[SCALARS, whole(*after.shape)] + [whole(*at[0].shape)] * len(at),
+        grid=(1,),
+        in_specs=[SCALARS, whole(META, STRIP)] + [whole(*at[0].shape)] * len(at),
         out_specs=whole(*at[0].shape),
         out_shape=jax.ShapeDtypeStruct(at[0].shape, F32),
         compiler_params=pltpu.CompilerParams(vmem_limit_bytes=SMALL_VMEM),
@@ -486,7 +489,7 @@
     return pl.pallas_call(
         lambda *refs: assemble_kernel(heads, chips, half, wide // heads, *refs),
         grid=(1,),
-        in_specs=[SCALARS, whole(*after.shape), whole(*first.shape), mine, mine]
+        in_specs=[SCALARS, whole(META, STRIP), whole(*first.shape), mine, mine]
         + [whole(*value.shape) for value in (*own, *far)],
         out_specs=[whole(STATE, lanes), whole(STATE, lanes), whole(META, STRIP)],
         out_shape=[
@@ -500,13 +503,14 @@
 
 
 def finish_kernel(
-    heads, half, x_ref, g_ref, write_ref, read_ref, tail_ref, lead_ref,
+    heads, start, steps, x_ref, g_ref, write_ref, read_ref, tail_ref, lead_ref,
     dx_ref, db_ref, dc_ref, change_ref, state_ref, back_ref, *refs,
 ):
     grad_ref, db_out, dc_out, sum_out, db_sum, dc_sum = refs[-6:]
     chunk = pl.program_id(0)
     lanes = x_ref.shape[1]
     head_size = lanes * STEPS * HALVES // heads
+    wide = start + chunk
 
     @pl.when(chunk == 0)
     def _():
@@ -516,7 +520,7 @@
 
     state = state_ref[...]
     back = back_ref[...]
-    spread = spreader(half * STEPS + chunk, heads, head_size, lanes)
+    spread = spreader(wide, heads, head_size, lanes)
     tail = dot(tail_ref[...], spread, 1, 0)
     lead = dot(lead_ref[...], spread, 1, 0)
     x = x_ref[...].astype(F32)
@@ -524,27 +528,27 @@
     y = dot(read_ref[...], state, 1, 0) * lead
     dx = dot(write_ref[...], back, 1, 0) * tail
     grad_ref[...] = (dx_ref[...] + dx).astype(BF16)
-    adder = head_adder(half * STEPS + chunk, head_size, lanes)
+    adder = head_adder(wide, head_size, lanes)
     sum_out[...] += head_sums(g * y - x * dx, adder)
     db_sum[...] += dot((x * tail).astype(BF16), back, 1, 1)
     dc_sum[...] += dot((g * lead).astype(BF16), state, 1, 1)
 
-    @pl.when(chunk == STEPS - 1)
+    @pl.when(chunk == steps - 1)
     def _():
         db_out[...] = db_sum[...].astype(db_out.dtype)
         dc_out[...] = dc_sum[...].astype(dc_out.dtype)
 
 
-def finish(heads, half, x, g, write_map, read_map, shared, dx, sums, state, back, grad):
+def finish(heads, start, steps, x, g, write_map, read_map, shared, dx, sums, state, back, grad):
     tokens, wide = x.shape
     lanes = wide // (STEPS * HALVES)
-    strip = half_lanes(tokens, lanes, half, STEPS)
-    own = pl.BlockSpec((STATE, lanes), lambda c: (0, c))
-    kind = BF16 if half == HALVES - 1 else F32
+    strip = pl.BlockSpec((tokens, lanes), lambda c: (0, start + c))
+    own = pl.BlockSpec((STATE, lanes), lambda c: (0, start % STEPS + c))
+    kind = BF16 if start + steps == STEPS * HALVES else F32
     earlier = [] if grad is None else [grad]
     return pl.pallas_call(
-        lambda *refs: finish_kernel(heads, half, *refs),
-        grid=(STEPS,),
+        lambda *refs: finish_kernel(heads, start, steps, *refs),
+        grid=(steps,),
         in_specs=[strip, strip]
         + [whole(tokens, STATE)] * 4
         + [strip]
@@ -560,7 +564,7 @@
         ],
         scratch_shapes=[pltpu.VMEM((tokens, STATE), F32)] * 2,
         input_output_aliases={12: 0} if earlier else {},
-        compiler_params=pltpu.CompilerParams(vmem_limit_bytes=BIG_VMEM),
+        compiler_params=pltpu.CompilerParams(vmem_limit_bytes=SMALL_VMEM),
         cost_estimate=pl.CostEstimate(
             flops=3_000_000_000, bytes_accessed=5_000_000, transcendentals=0
         ),
@@ -616,25 +620,8 @@
 
         return move(value, target)
 
-    def scan_half(half, after, at):
-        at = [to_chip(value, step) for step, value in enumerate(at)]
-        total = group_total(half, head_size, place, after, at)
-        got = [to_group(total, step, lambda c: c == 1) for step in range(1, groups)]
-        inside = enter(half, head_size, place, at, got)
-        own = [to_chip(value, step) for step, value in enumerate(inside)]
-        return own, [to_core(value) for value in own]
-
-    def later_total(tally):
-        other = to_core(tally)
-        later = jnp.where(core == 0, other, 0.0)
-        tally = tally + other
-        steps = [to_chip(tally, step) for step in range(1, chips)]
-        for step, value in enumerate(steps, 1):
-            later = later + jnp.where((chip ^ step) > chip, value, 0.0)
-            tally = tally + value
-        for step in range(1, groups):
-            later = later + to_group(tally, step, lambda c: False)
-        return later
+    def hold(value, *tokens):
+        return lax.optimization_barrier((value, tokens))[0]
 
     maps = (inputs, out_grad, input_map, output_map)
     send, keep, decay, *shared = summary(chips, 0, place, *maps, log_decay, None)
@@ -642,20 +629,44 @@
     pieces = [combine(chips, place, shared[0], first[0], keep, decay, shared[0])]
     send, keep, decay = summary(chips, 1, place, *maps, log_decay, shared)
     first.append(to_core(send))
-    dx, db, dc, change, state_own, back_own = intra(
-        pieces[0][0][-META:], *maps, log_decay, shared
-    )
-    token = change[:META]
-    pieces.append(combine(chips, place, token, first[1], keep, decay, shared[0]))
-    sums, grad, later = (db, dc, change), None, None
+    dx, db, dc, change, state_own, back_own = intra(pieces[0][0], *maps, log_decay, shared)
+    pieces.append(combine(chips, place, change, first[1], keep, decay, shared[0]))
+
+    own, token = [], pieces[1][0]
     for half in range(HALVES):
-        own, far = scan_half(half, token, pieces[half])
-        state, back, tally = assemble(
-            heads, half, place, sums[2][:META], first[half], state_own, back_own, own, far
+        at = [to_chip(value, step) for step, value in enumerate(pieces[half])]
+        total = group_total(half, head_size, place, token, at)
+        got = [to_group(total, step, lambda c: c == 1) for step in range(1, groups)]
+        inside = enter(half, head_size, place, at, got)
+        own.append([to_chip(value, step) for step, value in enumerate(inside)])
+        token = inside[0]
+
+    def entering(half, token):
+        far = [to_core(value) for value in own[half]]
+        return assemble(
+            heads, half, place, token, first[half], state_own, back_own, own[half], far
         )
-        grad, *sums = finish(heads, half, *maps, shared, dx, sums, state, back, grad)
-        found = later_total(tally)
-        later = found if later is None else later + found
+
+    state, back, tally = entering(0, token)
+    grad, *sums = finish(heads, 0, STEPS, *maps, shared, dx, (db, dc, change), state, back, None)
+    own[1] = hold(own[1], sums[2])
+    state, back, tally_b = entering(1, sums[2])
+    tally = tally + tally_b
+
+    other = to_core(tally)
+    grad, *sums = finish(heads, STEPS, 1, *maps, shared, dx, sums, state, back, grad)
+    other = hold(other, sums[2])
+    later = jnp.where(core == 0, other, 0.0)
+    tally = tally + other
+    steps = [to_chip(tally, step) for step in range(1, chips)]
+    sums = hold(sums, tally)
+    grad, *sums = finish(heads, STEPS + 1, 1, *maps, shared, dx, sums, state, back, grad)
+    steps = hold(steps, sums[2])
+    for step, value in enumerate(steps, 1):
+        later = later + jnp.where((chip ^ step) > chip, value, 0.0)
+        tally = tally + value
+    for step in range(1, groups):
+        later = later + to_group(tally, step, lambda c: False)
     return (grad, sums[0], sums[1], suffix(heads, sums[2], later))
 
 

time: 126 us -> 122 us (0.968)
  Pallas kernels: 41.5 us -> 38.1 us
  waiting for transfers between devices: 18.6 us -> 21.6 us
  local copies, waits for them, and re-layouts: 4.88 us -> 2.68 us
    pallas_call x4 -> x5, Pallas kernels: 12 us -> 8.64 us  [the longest x3 7.33 us: finish(): pl.pallas_call(lambda *refs: finish_kernel(heads, start, steps, *refs), g...]
    ppermute x42 -> x35, waiting for transfers between devices: 18.6 us -> 21.6 us  [move(): return lax.ppermute(value, ('grp', 'seq'), pairs)]
    slice x3 -> x0, local copies, waits for them, and re-layouts: 1.96 us -> none  [the longest x2 1.36 us: per_device(): sums[2][:META]]
    ppermute x42 -> x35, starting transfers between devices: 57.4 us -> 56.6 us  [move(): return lax.ppermute(value, ('grp', 'seq'), pairs)]
    unnamed x24 -> x44, local copies, waits for them, and re-layouts: 2.92 us -> 2.68 us
  transfers between devices with their start and end apart: 42 -> 35, of which waited for: 5 -> 12; matrix products, arithmetic and copies ran while one was open for 2% -> 0% of each run, Pallas kernels for 28% -> 25%
where the time goes in v4:
time: 122 us; the launch traced here: 121 us
  starting transfers between devices  56.6 us (46%)
  Pallas kernels  38.1 us (31%)
  waiting for transfers between devices  21.6 us (18%)
  local copies, waits for them, and re-layouts  2.68 us (2%)
  other arithmetic  1.22 us (1%)
    ppermute x35, starting transfers between devices, move(): return lax.ppermute(value, ('grp', 'seq'), pairs)  56.6 us
    ppermute x35, waiting for transfers between devices, move(): return lax.ppermute(value, ('grp', 'seq'), pairs)  21.6 us
    pallas_call x1, Pallas kernels, intra(): pl.pallas_call(lambda *refs: intra_kernel(heads, *refs), grid=(wide // LA...  14 us
    pallas_call x3, Pallas kernels, finish(): pl.pallas_call(lambda *refs: finish_kernel(heads, start, steps, *refs), g...  7.33 us
    pallas_call x2, Pallas kernels, summary(): pl.pallas_call(lambda *refs: summary_kernel(heads, chips, half, *refs), g...  7.31 us
    unnamed x44, local copies, waits for them, and re-layouts  2.68 us
    pallas_call x2, Pallas kernels, assemble(): pl.pallas_call(lambda *refs: assemble_kernel(heads, chips, half, wide //...  2.67 us
  transfers between devices with their start and end apart: 35, of which 12 were waited for; matrix products, arithmetic and copies ran while one was open for 0% of the time, Pallas kernels for 25%

profile of v4, /device:TPU:0, one launch (start us, length us, event | category | flops | bytes accessed | tf_op | source)
XLA Modules:
  0.0 121.3 jit_solution(18354448515849081702)
XLA Ops:
  0.6 0.6 pad_add_fusion.refs_0_
  1.3 3.8 %summary.2 = (f32[1288,128]{1,0:T(8,128)}, f32[1280,128]{1,0:T(8,128)}, f32[10,128]{1,0:T(8,128)}, f32[8,128]{1,0:T(8,128)}, f32[256,128]{1,0:T(8,128)}, /*index...) custom-call(s32[2]{0:T(128)} %pad_add_fusion.refs_0_, bf16[256,2560]{1,0:T(8,128)(2,1)} %refs_0_.5, ...), custom_call_target="tpu_custom_call" | custom-call | flops 1000000000 | bytes 3000000 | tf_op jit(solution)/shard_map/summary/pallas_call | solution.py:186
  5.0 0.5 collective-permute-start
  5.6 3.5 %summary.3 = (f32[1288,128]{1,0:T(8,128)}, f32[1280,128]{1,0:T(8,128)}, f32[10,128]{1,0:T(8,128)}) custom-call(s32[2]{0:T(128)} %pad_add_fusion.refs_0_, bf16[256,2560]{1,0:T(8,128)(2,1)} %refs_0_.5, bf16[256,2560]{1,0:T(8,128)(2,1)} %refs_1_.11, bf16[256,128]{1,0:T(8,128)(2,1)} %refs_2_.11, bf16[256,128]{1,0:T(8,128)(2,1)} %refs_3_.11, ...), custom_call_target="tpu_custom_call" | custom-call | flops 1000000000 | bytes 3000000 | tf_op jit(solution)/shard_map/summary/pallas_call | solution.py:186
  9.1 0.1 collective-permute-start.1
  9.2 0.7 combine.2
  9.9 0.7 copy-done.2
  10.5 3.0 %collective-permute-start.5 = (f32[328,128]{1,0:T(8,128)S(1)}, f32[328,128]{1,0:T(8,128)S(1)}, u32[]{:S(2)}, u32[]{:S(2)}) collective-permute-start(f32[328,128]{1,0:T(8,128)S(1)} %get-tuple-element.84), channel_id=1, source_target_pairs={{0,2},{1,3},{2,0},{3,1},{4,6},{5,7},{6,4},{7,5},{8,10},{9,11},{10,... | collective-permute-start | bytes 503816 | tf_op jit(solution)/shard_map/ppermute | solution.py:608
  13.6 2.6 %collective-permute-start.6 = (f32[328,128]{1,0:T(8,128)S(1)}, f32[328,128]{1,0:T(8,128)S(1)}, u32[]{:S(2)}, u32[]{:S(2)}) collective-permute-start(f32[328,128]{1,0:T(8,128)S(1)} %get-tuple-element.85), channel_id=1, source_target_pairs={{0,4},{1,5},{2,6},{3,7},{4,0},{5,1},{6,2},{7,3},{8,12},{9,13},{10,... | collective-permute-start | bytes 503816 | tf_op jit(solution)/shard_map/ppermute | solution.py:608
  16.1 14.0 %intra.1 = (f32[256,2560]{1,0:T(8,128)}, f32[256,128]{1,0:T(8,128)}, f32[256,128]{1,0:T(8,128)}, f32[256,128]{1,0:T(8,128)}, f32[128,2560]{1,0:T(8,128)}, /*index=5*/f32[128,2560]{1,0:T(8,128)}) custom-call(f32[328,128]{1,0:T(8,128)} %copy-done.2, bf16[256,2560]{1,0:T(8,128)(2,1)} %refs_0_.5, bf16[256,2560]{1,0:T(8,128)(2,1)} %refs_1_.11, ...), custom_call_target="tpu_custom_call" | custom-call | flops 12000000000 | bytes 8000000 | tf_op jit(solution)/shard_map/intra/pallas_call | solution.py:410
  30.2 0.9 copy-done.7
  31.2 0.7 combine.3
  31.9 0.8 group_total.2
  32.7 1.3 %collective-permute-start.10 = (f32[328,128]{1,0:T(8,128)S(1)}, f32[328,128]{1,0:T(8,128)S(1)}, u32[]{:S(2)}, u32[]{:S(2)}) collective-permute-start(f32[328,128]{1,0:T(8,128)S(1)} %group_total.2), channel_id=1, source_target_pairs={{1,25},{3,27},{5,29},{7,31},{24,0},{26,2},{28,4},{30,6}} | collective-permute-start | bytes 503816 | tf_op jit(solution)/shard_map/ppermute | solution.py:608
  34.0 1.3 %collective-permute-start.8 = (f32[328,128]{1,0:T(8,128)S(1)}, f32[328,128]{1,0:T(8,128)S(1)}, u32[]{:S(2)}, u32[]{:S(2)}) collective-permute-start(f32[328,128]{1,0:T(8,128)S(1)} %group_total.2), channel_id=1, source_target_pairs={{1,9},{3,11},{5,13},{7,15},{8,0},{9,17},{10,2},{11,19},{12,4},{13,... | collective-permute-start | bytes 503816 | tf_op jit(solution)/shard_map/ppermute | solution.py:608
  35.3 1.3 %collective-permute-start.9 = (f32[328,128]{1,0:T(8,128)S(1)}, f32[328,128]{1,0:T(8,128)S(1)}, u32[]{:S(2)}, u32[]{:S(2)}) collective-permute-start(f32[328,128]{1,0:T(8,128)S(1)} %group_total.2), channel_id=1, source_target_pairs={{1,17},{3,19},{5,21},{7,23},{9,25},{11,27},{13,29},{15,31},{16,0},... | collective-permute-start | bytes 503816 | tf_op jit(solution)/shard_map/ppermute | solution.py:608
  36.6 1.0 collective-permute-start.2
  37.6 3.5 %collective-permute-start.3 = (f32[328,128]{1,0:T(8,128)S(1)}, f32[328,128]{1,0:T(8,128)S(1)}, u32[]{:S(2)}, u32[]{:S(2)}) collective-permute-start(f32[328,128]{1,0:T(8,128)S(1)} %get-tuple-element.82), channel_id=1, source_target_pairs={{0,4},{1,5},{2,6},{3,7},{4,0},{5,1},{6,2},{7,3},{8,12},{9,13},{10,... | collective-permute-start | bytes 503816 | tf_op jit(solution)/shard_map/ppermute | solution.py:608
  41.0 3.6 %collective-permute-start.4 = (f32[328,128]{1,0:T(8,128)S(1)}, f32[328,128]{1,0:T(8,128)S(1)}, u32[]{:S(2)}, u32[]{:S(2)}) collective-permute-start(f32[328,128]{1,0:T(8,128)S(1)} %get-tuple-element.83), channel_id=1, source_target_pairs={{0,6},{1,7},{2,4},{3,5},{4,2},{5,3},{6,0},{7,1},{8,14},{9,15},{10,... | collective-permute-start | bytes 503816 | tf_op jit(solution)/shard_map/ppermute | solution.py:608
  44.7 1.0 enter.2
  45.7 0.1 collective-permute-start.14
  45.8 0.6 collective-permute-done.3.refs_4_.refs_3_
  46.4 4.2 %collective-permute-done.4.refs_5_.refs_4_ = f32[328,128]{1,0:T(8,128)S(1)} collective-permute-done((f32[328,128]{1,0:T(8,128)S(1)}, f32[328,128]{1,0:T(8,128)S(1)}, u32[]{:S(2)}, u32[]{:S(2)}) %collective-permute-start.4) | collective-permute-done | bytes 167968 | tf_op jit(solution)/shard_map/ppermute | solution.py:608
  50.5 0.8 group_total.3
  51.3 1.3 %collective-permute-start.11 = (f32[328,128]{1,0:T(8,128)S(1)}, f32[328,128]{1,0:T(8,128)S(1)}, u32[]{:S(2)}, u32[]{:S(2)}) collective-permute-start(f32[328,128]{1,0:T(8,128)S(1)} %group_total.3), channel_id=1, source_target_pairs={{1,9},{3,11},{5,13},{7,15},{8,0},{9,17},{10,2},{11,19},{12,4},{13,... | collective-permute-start | bytes 503816 | tf_op jit(solution)/shard_map/ppermute | solution.py:608
  52.6 1.3 %collective-permute-start.12 = (f32[328,128]{1,0:T(8,128)S(1)}, f32[328,128]{1,0:T(8,128)S(1)}, u32[]{:S(2)}, u32[]{:S(2)}) collective-permute-start(f32[328,128]{1,0:T(8,128)S(1)} %group_total.3), channel_id=1, source_target_pairs={{1,17},{3,19},{5,21},{7,23},{9,25},{11,27},{13,29},{15,31},{16,0},... | collective-permute-start | bytes 503816 | tf_op jit(solution)/shard_map/ppermute | solution.py:608
  53.9 6.4 %collective-permute-start.15 = (f32[320,128]{1,0:T(8,128)S(1)}, f32[320,128]{1,0:T(8,128)S(1)}, u32[]{:S(2)}, u32[]{:S(2)}) collective-permute-start(f32[320,128]{1,0:T(8,128)S(1)} %get-tuple-element.92), channel_id=1, source_target_pairs={{0,4},{1,5},{2,6},{3,7},{4,0},{5,1},{6,2},{7,3},{8,12},{9,13},{10,... | collective-permute-start | bytes 491528 | tf_op jit(solution)/shard_map/ppermute | solution.py:608
  60.3 1.7 %collective-permute-start.16 = (f32[320,128]{1,0:T(8,128)S(1)}, f32[320,128]{1,0:T(8,128)S(1)}, u32[]{:S(2)}, u32[]{:S(2)}) collective-permute-start(f32[320,128]{1,0:T(8,128)S(1)} %get-tuple-element.93), channel_id=1, source_target_pairs={{0,6},{1,7},{2,4},{3,5},{4,2},{5,3},{6,0},{7,1},{8,14},{9,15},{10,... | collective-permute-start | bytes 491528 | tf_op jit(solution)/shard_map/ppermute | solution.py:608
  62.0 1.5 %collective-permute-start.13 = (f32[328,128]{1,0:T(8,128)S(1)}, f32[328,128]{1,0:T(8,128)S(1)}, u32[]{:S(2)}, u32[]{:S(2)}) collective-permute-start(f32[328,128]{1,0:T(8,128)S(1)} %group_total.3), channel_id=1, source_target_pairs={{1,25},{3,27},{5,29},{7,31},{24,0},{26,2},{28,4},{30,6}} | collective-permute-start | bytes 503816 | tf_op jit(solution)/shard_map/ppermute | solution.py:608
  63.5 0.1 collective-permute-done.15.refs_7_
  63.6 10.3 %collective-permute-start.17 = (f32[320,128]{1,0:T(8,128)S(1)}, f32[320,128]{1,0:T(8,128)S(1)}, u32[]{:S(2)}, u32[]{:S(2)}) collective-permute-start(f32[320,128]{1,0:T(8,128)S(1)} %get-tuple-element.87.refs_1_.refs_5_), channel_id=1, source_target_pairs={{0,1},{1,0},{2,3},{3,2},{4,5},{5,4},{6,7},{7,6},{8,9},{9,8},{10,11... | collective-permute-start | bytes 491528 | tf_op jit(solution)/shard_map/ppermute | solution.py:608
  74.0 0.5 collective-permute-start.19
  74.5 0.1 collective-permute-start.20
  74.5 1.0 enter.3
  75.6 2.3 %collective-permute-start.21 = (f32[320,128]{1,0:T(8,128)S(1)}, f32[320,128]{1,0:T(8,128)S(1)}, u32[]{:S(2)}, u32[]{:S(2)}) collective-permute-start(f32[320,128]{1,0:T(8,128)S(1)} %get-tuple-element.99), channel_id=1, source_target_pairs={{0,2},{1,3},{2,0},{3,1},{4,6},{5,7},{6,4},{7,5},{8,10},{9,11},{10,... | collective-permute-start | bytes 491528 | tf_op jit(solution)/shard_map/ppermute | solution.py:608
  77.9 0.4 collective-permute-start.22
  78.2 2.1 %collective-permute-start.23 = (f32[320,128]{1,0:T(8,128)S(1)}, f32[320,128]{1,0:T(8,128)S(1)}, u32[]{:S(2)}, u32[]{:S(2)}) collective-permute-start(f32[320,128]{1,0:T(8,128)S(1)} %get-tuple-element.101), channel_id=1, source_target_pairs={{0,6},{1,7},{2,4},{3,5},{4,2},{5,3},{6,0},{7,1},{8,14},{9,15},{10,... | collective-permute-start | bytes 491528 | tf_op jit(solution)/shard_map/ppermute | solution.py:608
  80.4 1.3 %assemble.2 = (bf16[128,1280]{1,0:T(8,128)(2,1)S(1)}, bf16[128,1280]{1,0:T(8,128)(2,1)S(1)}, f32[8,128]{1,0:T(8,128)S(1)}) custom-call(s32[2]{0:T(128)S(1)} %copy-done.10, f32[320,128]{1,0:T(8,128)S(1)} %get-tuple-element.102.refs_1_.refs_5_, f32[1288,128]{1,0:T(8,128)S(1)} %collective-permute-done.refs_2_, f32[128,2560]{1,0:T(8,128)S(1)} %copy-done, ...), custom_call_target="tpu_custom_call" | custom-call | tf_op jit(solution)/shard_map/assemble/pallas_call | solution.py:489
  81.8 0.3 copy-done.14
  82.2 3.8 %finish.3 = (bf16[256,2560]{1,0:T(8,128)(2,1)}, f32[256,128]{1,0:T(8,128)S(1)}, f32[256,128]{1,0:T(8,128)S(1)}, f32[256,128]{1,0:T(8,128)S(1)}) custom-call(bf16[256,2560]{1,0:T(8,128)(2,1)S(1)} %copy-done.13, bf16[256,2560]{1,0:T(8,128)(2,1)S(1)} %copy-done.14, bf16[256,128]{1,0:T(8,128)(2,1)S(1)} %copy-done.15, bf16[256,128]{1,0:T(8,128)(2,1)S(1)} %copy-done.16, ...), custom_call_target="tpu_custom_call" | custom-call | flops 3000000000 | bytes 5000000 | tf_op jit(solution)/shard_map/finish/pallas_call | solution.py:549
  85.9 7.0 %collective-permute-done.22.refs_7_ = f32[320,128]{1,0:T(8,128)S(1)} collective-permute-done((f32[320,128]{1,0:T(8,128)S(1)}, f32[320,128]{1,0:T(8,128)S(1)}, u32[]{:S(2)}, u32[]{:S(2)}) %collective-permute-start.22) | collective-permute-done | bytes 163872 | tf_op jit(solution)/shard_map/ppermute | solution.py:608
  92.9 0.5 collective-permute-start.25
  93.4 0.5 collective-permute-start.27
  93.9 0.4 collective-permute-done.24.refs_9_
  94.3 0.2 collective-permute-done.25.refs_10_
  94.5 0.3 collective-permute-done.26.refs_11_
  94.8 0.2 collective-permute-done.27.refs_12_
  95.0 1.3 %assemble.3 = (bf16[128,1280]{1,0:T(8,128)(2,1)S(1)}, bf16[128,1280]{1,0:T(8,128)(2,1)S(1)}, f32[8,128]{1,0:T(8,128)S(1)}) custom-call(s32[2]{0:T(128)S(1)} %copy-done.10, f32[256,128]{1,0:T(8,128)S(1)} %get-tuple-element.98.refs_1_.refs_9_, f32[1288,128]{1,0:T(8,128)S(1)} %collective-permute-done.1.refs_2_, f32[128,2560]{1,0:T(8,128)S(1)} %copy-done, ...), custom_call_target="tpu_custom_call" | custom-call | tf_op jit(solution)/shard_map/assemble/pallas_call | solution.py:489
  96.4 0.3 collective-permute-start.28
  96.7 1.7 %finish.4 = (bf16[256,2560]{1,0:T(8,128)(2,1)}, f32[256,128]{1,0:T(8,128)S(1)}, f32[256,128]{1,0:T(8,128)S(1)}, f32[256,128]{1,0:T(8,128)S(1)}) custom-call(bf16[256,2560]{1,0:T(8,128)(2,1)S(1)} %copy-done.13, bf16[256,2560]{1,0:T(8,128)(2,1)S(1)} %copy-done.14, bf16[256,128]{1,0:T(8,128)(2,1)S(1)} %copy-done.15, ...), custom_call_target="tpu_custom_call", output_to_operand_aliasing={{0}: (12, {})} | custom-call | flops 3000000000 | bytes 5000000 | tf_op jit(solution)/shard_map/finish/pallas_call | solution.py:549
  98.5 2.9 %collective-permute-start.29 = (f32[8,128]{1,0:T(8,128)S(1)}, f32[8,128]{1,0:T(8,128)S(1)}, u32[]{:S(2)}, u32[]{:S(2)}) collective-permute-start(f32[8,128]{1,0:T(8,128)S(1)} %add.40), channel_id=1, source_target_pairs={{0,2},{1,3},{2,0},{3,1},{4,6},{5,7},{6,4},{7,5},{8,10},{9,11},{10,... | collective-permute-start | bytes 12296 | tf_op jit(solution)/shard_map/ppermute | solution.py:608
  101.4 0.3 collective-permute-start.30
  101.7 2.1 %collective-permute-start.31 = (f32[8,128]{1,0:T(8,128)S(1)}, f32[8,128]{1,0:T(8,128)S(1)}, u32[]{:S(2)}, u32[]{:S(2)}) collective-permute-start(f32[8,128]{1,0:T(8,128)S(1)} %add.40), channel_id=1, source_target_pairs={{0,6},{1,7},{2,4},{3,5},{4,2},{5,3},{6,0},{7,1},{8,14},{9,15},{10,... | collective-permute-start | bytes 12296 | tf_op jit(solution)/shard_map/ppermute | solution.py:608
  103.8 1.8 %finish.5 = (bf16[256,2560]{1,0:T(8,128)(2,1)}, bf16[256,128]{1,0:T(8,128)(2,1)}, bf16[256,128]{1,0:T(8,128)(2,1)}, f32[256,128]{1,0:T(8,128)S(1)}) custom-call(bf16[256,2560]{1,0:T(8,128)(2,1)S(1)} %copy-done.13, bf16[256,2560]{1,0:T(8,128)(2,1)S(1)} %copy-done.14, bf16[256,128]{1,0:T(8,128)(2,1)S(1)} %copy-done.15, ...), custom_call_target="tpu_custom_call", output_to_operand_aliasing={{0}: (12, {})} | custom-call | flops 3000000000 | bytes 5000000 | tf_op jit(solution)/shard_map/finish/pallas_call | solution.py:549
  105.7 0.6 copy-done.6
  106.3 0.8 collective-permute-done.31
  107.2 1.3 %collective-permute-start.32 = (f32[8,128]{1,0:T(8,128)S(1)}, f32[8,128]{1,0:T(8,128)S(1)}, u32[]{:S(2)}, u32[]{:S(2)}) collective-permute-start(f32[8,128]{1,0:T(8,128)S(1)} %add_add_fusion.1), channel_id=1, source_target_pairs={{8,0},{9,1},{10,2},{11,3},{12,4},{13,5},{14,6},{15,7},{16,8},{17,9... | collective-permute-start | bytes 12296 | tf_op jit(solution)/shard_map/ppermute | solution.py:608
  108.4 1.3 %collective-permute-start.33 = (f32[8,128]{1,0:T(8,128)S(1)}, f32[8,128]{1,0:T(8,128)S(1)}, u32[]{:S(2)}, u32[]{:S(2)}) collective-permute-start(f32[8,128]{1,0:T(8,128)S(1)} %add_add_fusion.1), channel_id=1, source_target_pairs={{16,0},{17,1},{18,2},{19,3},{20,4},{21,5},{22,6},{23,7},{24,8},{25... | collective-permute-start | bytes 12296 | tf_op jit(solution)/shard_map/ppermute | solution.py:608
  109.7 1.3 %collective-permute-start.34 = (f32[8,128]{1,0:T(8,128)S(1)}, f32[8,128]{1,0:T(8,128)S(1)}, u32[]{:S(2)}, u32[]{:S(2)}) collective-permute-start(f32[8,128]{1,0:T(8,128)S(1)} %add_add_fusion.1), channel_id=1, source_target_pairs={{24,0},{25,1},{26,2},{27,3},{28,4},{29,5},{30,6},{31,7}} | collective-permute-start | bytes 12296 | tf_op jit(solution)/shard_map/ppermute | solution.py:608
  111.1 3.1 %collective-permute-done.32 = f32[8,128]{1,0:T(8,128)S(1)} collective-permute-done((f32[8,128]{1,0:T(8,128)S(1)}, f32[8,128]{1,0:T(8,128)S(1)}, u32[]{:S(2)}, u32[]{:S(2)}) %collective-permute-start.32) | collective-permute-done | bytes 4128 | tf_op jit(solution)/shard_map/ppermute | solution.py:608
  114.2 2.8 %collective-permute-done.33 = f32[8,128]{1,0:T(8,128)S(1)} collective-permute-done((f32[8,128]{1,0:T(8,128)S(1)}, f32[8,128]{1,0:T(8,128)S(1)}, u32[]{:S(2)}, u32[]{:S(2)}) %collective-permute-start.33) | collective-permute-done | bytes 4128 | tf_op jit(solution)/shard_map/ppermute | solution.py:608
  116.9 1.9 %collective-permute-done.34 = f32[8,128]{1,0:T(8,128)S(1)} collective-permute-done((f32[8,128]{1,0:T(8,128)S(1)}, f32[8,128]{1,0:T(8,128)S(1)}, u32[]{:S(2)}, u32[]{:S(2)}) %collective-permute-start.34) | collective-permute-done | bytes 4128 | tf_op jit(solution)/shard_map/ppermute | solution.py:608
  118.9 0.6 add_add_fusion.later_ref
  119.5 1.8 %suffix.1 = f32[40,256]{1,0:T(8,128)} custom-call(f32[256,128]{1,0:T(8,128)} %copy-done.6, f32[8,128]{1,0:T(8,128)} %add_add_fusion.later_ref), custom_call_target="tpu_custom_call" | custom-call | tf_op jit(solution)/shard_map/suffix/pallas_call | solution.py:583
  (70 shorter events, 0.2 us)
Async XLA Ops:
  5.0 4.1 %collective-permute-start = (f32[1288,128]{1,0:T(8,128)}, f32[1288,128]{1,0:T(8,128)S(1)}, u32[]{:S(2)}, u32[]{:S(2)}) collective-permute-start(f32[1288,128]{1,0:T(8,128)} %get-tuple-element.68), channel_id=1, source_target_pairs={{0,1},{1,0},{2,3},{3,2},{4,5},{5,4},{6,7},{7,6},{8,9},{9,8},{10,11... | collective-permute-start | bytes 1978376 | tf_op jit(solution)/shard_map/ppermute | solution.py:608
  5.5 3.6 %copy-start.5 = (f32[1280,128]{1,0:T(8,128)S(1)}, f32[1280,128]{1,0:T(8,128)}, u32[]{:S(2)}) copy-start(f32[1280,128]{1,0:T(8,128)} %get-tuple-element.69.refs_3_) | copy-start | bytes 1966084
  5.5 3.6 %copy-start.9 = (f32[8,128]{1,0:T(8,128)S(1)}, f32[8,128]{1,0:T(8,128)}, u32[]{:S(2)}) copy-start(f32[8,128]{1,0:T(8,128)} %get-tuple-element.67.refs_1_.refs_5_) | copy-start | bytes 12292
  5.5 3.6 %copy-start.10 = (s32[2]{0:T(128)S(1)}, s32[2]{0:T(128)}, u32[]{:S(2)}) copy-start(s32[2]{0:T(128)} %pad_add_fusion.refs_0_) | copy-start | bytes 28
  5.6 3.6 %copy-start.12 = (f32[10,128]{1,0:T(8,128)S(1)}, f32[10,128]{1,0:T(8,128)}, u32[]{:S(2)}) copy-start(f32[10,128]{1,0:T(8,128)} %get-tuple-element.70.refs_4_) | copy-start | bytes 15364
  9.1 21.1 %collective-permute-start.1 = (f32[1288,128]{1,0:T(8,128)}, f32[1288,128]{1,0:T(8,128)S(1)}, u32[]{:S(2)}, u32[]{:S(2)}) collective-permute-start(f32[1288,128]{1,0:T(8,128)} %get-tuple-element.77), channel_id=1, source_target_pairs={{0,1},{1,0},{2,3},{3,2},{4,5},{5,4},{6,7},{7,6},{8,9},{9,8},{10,11... | collective-permute-start | bytes 1978376 | tf_op jit(solution)/shard_map/ppermute | solution.py:608
  9.9 0.7 copy-start.2
  10.5 21.3 %collective-permute-start.5 = (f32[328,128]{1,0:T(8,128)S(1)}, f32[328,128]{1,0:T(8,128)S(1)}, u32[]{:S(2)}, u32[]{:S(2)}) collective-permute-start(f32[328,128]{1,0:T(8,128)S(1)} %get-tuple-element.84), channel_id=1, source_target_pairs={{0,2},{1,3},{2,0},{3,1},{4,6},{5,7},{6,4},{7,5},{8,10},{9,11},{10,... | collective-permute-start | bytes 503816 | tf_op jit(solution)/shard_map/ppermute | solution.py:608
  13.6 18.3 %collective-permute-start.6 = (f32[328,128]{1,0:T(8,128)S(1)}, f32[328,128]{1,0:T(8,128)S(1)}, u32[]{:S(2)}, u32[]{:S(2)}) collective-permute-start(f32[328,128]{1,0:T(8,128)S(1)} %get-tuple-element.85), channel_id=1, source_target_pairs={{0,4},{1,5},{2,6},{3,7},{4,0},{5,1},{6,2},{7,3},{8,12},{9,13},{10,... | collective-permute-start | bytes 503816 | tf_op jit(solution)/shard_map/ppermute | solution.py:608
  16.1 15.7 %collective-permute-start.7 = (f32[328,128]{1,0:T(8,128)S(1)}, f32[328,128]{1,0:T(8,128)S(1)}, u32[]{:S(2)}, u32[]{:S(2)}) collective-permute-start(f32[328,128]{1,0:T(8,128)S(1)} %get-tuple-element.86), channel_id=1, source_target_pairs={{0,6},{1,7},{2,4},{3,5},{4,2},{5,3},{6,0},{7,1},{8,14},{9,15},{10,... | collective-permute-start | bytes 503816 | tf_op jit(solution)/shard_map/ppermute | solution.py:608
  16.1 14.1 %copy-start.4 = (f32[1280,128]{1,0:T(8,128)S(1)}, f32[1280,128]{1,0:T(8,128)}, u32[]{:S(2)}) copy-start(f32[1280,128]{1,0:T(8,128)} %get-tuple-element.78.refs_3_) | copy-start | bytes 1966084
  16.1 14.1 %copy-start.11 = (f32[10,128]{1,0:T(8,128)S(1)}, f32[10,128]{1,0:T(8,128)}, u32[]{:S(2)}) copy-start(f32[10,128]{1,0:T(8,128)} %get-tuple-element.79.refs_4_) | copy-start | bytes 15364
  30.2 1.7 %copy-start.3 = (f32[328,128]{1,0:T(8,128)S(1)}, f32[328,128]{1,0:T(8,128)}, u32[]{:S(2)}) copy-start(f32[328,128]{1,0:T(8,128)} %copy-done.2) | copy-start | bytes 503812
  30.2 0.9 copy-start.7
  31.9 49.9 %copy-start.18 = (bf16[256,128]{1,0:T(8,128)(2,1)S(1)}, bf16[256,128]{1,0:T(8,128)(2,1)}, u32[]{:S(2)}) copy-start(bf16[256,128]{1,0:T(8,128)(2,1)} %get-tuple-element.65.refs_7_.refs_6_.refs_4_) | copy-start | bytes 196612
  31.9 49.9 %copy-start.19 = (bf16[256,128]{1,0:T(8,128)(2,1)S(1)}, bf16[256,128]{1,0:T(8,128)(2,1)}, u32[]{:S(2)}) copy-start(bf16[256,128]{1,0:T(8,128)(2,1)} %get-tuple-element.66.refs_8_.refs_7_.refs_5_) | copy-start | bytes 196612
  31.9 49.9 %copy-start.20 = (f32[256,128]{1,0:T(8,128)S(1)}, f32[256,128]{1,0:T(8,128)}, u32[]{:S(2)}) copy-start(f32[256,128]{1,0:T(8,128)} %get-tuple-element.74.refs_7_) | copy-start | bytes 393220
  31.9 49.9 %copy-start.21 = (f32[256,128]{1,0:T(8,128)S(1)}, f32[256,128]{1,0:T(8,128)}, u32[]{:S(2)}) copy-start(f32[256,128]{1,0:T(8,128)} %get-tuple-element.75.refs_8_) | copy-start | bytes 393220
  32.7 8.3 %collective-permute-start.10 = (f32[328,128]{1,0:T(8,128)S(1)}, f32[328,128]{1,0:T(8,128)S(1)}, u32[]{:S(2)}, u32[]{:S(2)}) collective-permute-start(f32[328,128]{1,0:T(8,128)S(1)} %group_total.2), channel_id=1, source_target_pairs={{1,25},{3,27},{5,29},{7,31},{24,0},{26,2},{28,4},{30,6}} | collective-permute-start | bytes 503816 | tf_op jit(solution)/shard_map/ppermute | solution.py:608
  34.0 10.7 %collective-permute-start.8 = (f32[328,128]{1,0:T(8,128)S(1)}, f32[328,128]{1,0:T(8,128)S(1)}, u32[]{:S(2)}, u32[]{:S(2)}) collective-permute-start(f32[328,128]{1,0:T(8,128)S(1)} %group_total.2), channel_id=1, source_target_pairs={{1,9},{3,11},{5,13},{7,15},{8,0},{9,17},{10,2},{11,19},{12,4},{13,... | collective-permute-start | bytes 503816 | tf_op jit(solution)/shard_map/ppermute | solution.py:608
  35.3 9.4 %collective-permute-start.9 = (f32[328,128]{1,0:T(8,128)S(1)}, f32[328,128]{1,0:T(8,128)S(1)}, u32[]{:S(2)}, u32[]{:S(2)}) collective-permute-start(f32[328,128]{1,0:T(8,128)S(1)} %group_total.2), channel_id=1, source_target_pairs={{1,17},{3,19},{5,21},{7,23},{9,25},{11,27},{13,29},{15,31},{16,0},... | collective-permute-start | bytes 503816 | tf_op jit(solution)/shard_map/ppermute | solution.py:608
  36.6 9.2 %collective-permute-start.2 = (f32[328,128]{1,0:T(8,128)S(1)}, f32[328,128]{1,0:T(8,128)S(1)}, u32[]{:S(2)}, u32[]{:S(2)}) collective-permute-start(f32[328,128]{1,0:T(8,128)S(1)} %get-tuple-element.81), channel_id=1, source_target_pairs={{0,2},{1,3},{2,0},{3,1},{4,6},{5,7},{6,4},{7,5},{8,10},{9,11},{10,... | collective-permute-start | bytes 503816 | tf_op jit(solution)/shard_map/ppermute | solution.py:608
  37.6 8.8 %collective-permute-start.3 = (f32[328,128]{1,0:T(8,128)S(1)}, f32[328,128]{1,0:T(8,128)S(1)}, u32[]{:S(2)}, u32[]{:S(2)}) collective-permute-start(f32[328,128]{1,0:T(8,128)S(1)} %get-tuple-element.82), channel_id=1, source_target_pairs={{0,4},{1,5},{2,6},{3,7},{4,0},{5,1},{6,2},{7,3},{8,12},{9,13},{10,... | collective-permute-start | bytes 503816 | tf_op jit(solution)/shard_map/ppermute | solution.py:608
  41.0 9.5 %collective-permute-start.4 = (f32[328,128]{1,0:T(8,128)S(1)}, f32[328,128]{1,0:T(8,128)S(1)}, u32[]{:S(2)}, u32[]{:S(2)}) collective-permute-start(f32[328,128]{1,0:T(8,128)S(1)} %get-tuple-element.83), channel_id=1, source_target_pairs={{0,6},{1,7},{2,4},{3,5},{4,2},{5,3},{6,0},{7,1},{8,14},{9,15},{10,... | collective-permute-start | bytes 503816 | tf_op jit(solution)/shard_map/ppermute | solution.py:608
  44.7 35.7 %copy-start.1 = (f32[128,2560]{1,0:T(8,128)S(1)}, f32[128,2560]{1,0:T(8,128)}, u32[]{:S(2)}) copy-start(f32[128,2560]{1,0:T(8,128)} %get-tuple-element.90.refs_4_) | copy-start | bytes 3932164
  45.7 34.7 %copy-start = (f32[128,2560]{1,0:T(8,128)S(1)}, f32[128,2560]{1,0:T(8,128)}, u32[]{:S(2)}) copy-start(f32[128,2560]{1,0:T(8,128)} %get-tuple-element.89.refs_3_) | copy-start | bytes 3932164
  45.7 16.3 %collective-permute-start.14 = (f32[320,128]{1,0:T(8,128)S(1)}, f32[320,128]{1,0:T(8,128)S(1)}, u32[]{:S(2)}, u32[]{:S(2)}) collective-permute-start(f32[320,128]{1,0:T(8,128)S(1)} %get-tuple-element.91), channel_id=1, source_target_pairs={{0,2},{1,3},{2,0},{3,1},{4,6},{5,7},{6,4},{7,5},{8,10},{9,11},{10,... | collective-permute-start | bytes 491528 | tf_op jit(solution)/shard_map/ppermute | solution.py:608
  51.3 22.6 %collective-permute-start.11 = (f32[328,128]{1,0:T(8,128)S(1)}, f32[328,128]{1,0:T(8,128)S(1)}, u32[]{:S(2)}, u32[]{:S(2)}) collective-permute-start(f32[328,128]{1,0:T(8,128)S(1)} %group_total.3), channel_id=1, source_target_pairs={{1,9},{3,11},{5,13},{7,15},{8,0},{9,17},{10,2},{11,19},{12,4},{13,... | collective-permute-start | bytes 503816 | tf_op jit(solution)/shard_map/ppermute | solution.py:608
  52.6 21.8 %collective-permute-start.12 = (f32[328,128]{1,0:T(8,128)S(1)}, f32[328,128]{1,0:T(8,128)S(1)}, u32[]{:S(2)}, u32[]{:S(2)}) collective-permute-start(f32[328,128]{1,0:T(8,128)S(1)} %group_total.3), channel_id=1, source_target_pairs={{1,17},{3,19},{5,21},{7,23},{9,25},{11,27},{13,29},{15,31},{16,0},... | collective-permute-start | bytes 503816 | tf_op jit(solution)/shard_map/ppermute | solution.py:608
  53.9 9.7 %collective-permute-start.15 = (f32[320,128]{1,0:T(8,128)S(1)}, f32[320,128]{1,0:T(8,128)S(1)}, u32[]{:S(2)}, u32[]{:S(2)}) collective-permute-start(f32[320,128]{1,0:T(8,128)S(1)} %get-tuple-element.92), channel_id=1, source_target_pairs={{0,4},{1,5},{2,6},{3,7},{4,0},{5,1},{6,2},{7,3},{8,12},{9,13},{10,... | collective-permute-start | bytes 491528 | tf_op jit(solution)/shard_map/ppermute | solution.py:608
  60.3 13.7 %collective-permute-start.16 = (f32[320,128]{1,0:T(8,128)S(1)}, f32[320,128]{1,0:T(8,128)S(1)}, u32[]{:S(2)}, u32[]{:S(2)}) collective-permute-start(f32[320,128]{1,0:T(8,128)S(1)} %get-tuple-element.93), channel_id=1, source_target_pairs={{0,6},{1,7},{2,4},{3,5},{4,2},{5,3},{6,0},{7,1},{8,14},{9,15},{10,... | collective-permute-start | bytes 491528 | tf_op jit(solution)/shard_map/ppermute | solution.py:608
  62.0 12.5 %collective-permute-start.13 = (f32[328,128]{1,0:T(8,128)S(1)}, f32[328,128]{1,0:T(8,128)S(1)}, u32[]{:S(2)}, u32[]{:S(2)}) collective-permute-start(f32[328,128]{1,0:T(8,128)S(1)} %group_total.3), channel_id=1, source_target_pairs={{1,25},{3,27},{5,29},{7,31},{24,0},{26,2},{28,4},{30,6}} | collective-permute-start | bytes 503816 | tf_op jit(solution)/shard_map/ppermute | solution.py:608
  63.6 14.3 %collective-permute-start.17 = (f32[320,128]{1,0:T(8,128)S(1)}, f32[320,128]{1,0:T(8,128)S(1)}, u32[]{:S(2)}, u32[]{:S(2)}) collective-permute-start(f32[320,128]{1,0:T(8,128)S(1)} %get-tuple-element.87.refs_1_.refs_5_), channel_id=1, source_target_pairs={{0,1},{1,0},{2,3},{3,2},{4,5},{5,4},{6,7},{7,6},{8,9},{9,8},{10,11... | collective-permute-start | bytes 491528 | tf_op jit(solution)/shard_map/ppermute | solution.py:608
  73.9 4.3 %collective-permute-start.18 = (f32[320,128]{1,0:T(8,128)S(1)}, f32[320,128]{1,0:T(8,128)S(1)}, u32[]{:S(2)}, u32[]{:S(2)}) collective-permute-start(f32[320,128]{1,0:T(8,128)S(1)} %collective-permute-done.14.refs_6_), channel_id=1, source_target_pairs={{0,1},{1,0},{2,3},{3,2},{4,5},{5,4},{6,7},{7,6},{8,9},{9,8},{10,11... | collective-permute-start | bytes 491528 | tf_op jit(solution)/shard_map/ppermute | solution.py:608
  74.0 6.4 %collective-permute-start.19 = (f32[320,128]{1,0:T(8,128)S(1)}, f32[320,128]{1,0:T(8,128)S(1)}, u32[]{:S(2)}, u32[]{:S(2)}) collective-permute-start(f32[320,128]{1,0:T(8,128)S(1)} %collective-permute-done.15.refs_7_), channel_id=1, source_target_pairs={{0,1},{1,0},{2,3},{3,2},{4,5},{5,4},{6,7},{7,6},{8,9},{9,8},{10,11... | collective-permute-start | bytes 491528 | tf_op jit(solution)/shard_map/ppermute | solution.py:608
  74.5 5.9 %collective-permute-start.20 = (f32[320,128]{1,0:T(8,128)S(1)}, f32[320,128]{1,0:T(8,128)S(1)}, u32[]{:S(2)}, u32[]{:S(2)}) collective-permute-start(f32[320,128]{1,0:T(8,128)S(1)} %collective-permute-done.16.refs_8_), channel_id=1, source_target_pairs={{0,1},{1,0},{2,3},{3,2},{4,5},{5,4},{6,7},{7,6},{8,9},{9,8},{10,11... | collective-permute-start | bytes 491528 | tf_op jit(solution)/shard_map/ppermute | solution.py:608
  74.5 7.2 %copy-start.17 = (f32[256,2560]{1,0:T(8,128)S(1)}, f32[256,2560]{1,0:T(8,128)}, u32[]{:S(2)}) copy-start(f32[256,2560]{1,0:T(8,128)} %get-tuple-element.73.refs_6_) | copy-start | bytes 7864324
  75.6 10.4 %collective-permute-start.21 = (f32[320,128]{1,0:T(8,128)S(1)}, f32[320,128]{1,0:T(8,128)S(1)}, u32[]{:S(2)}, u32[]{:S(2)}) collective-permute-start(f32[320,128]{1,0:T(8,128)S(1)} %get-tuple-element.99), channel_id=1, source_target_pairs={{0,2},{1,3},{2,0},{3,1},{4,6},{5,7},{6,4},{7,5},{8,10},{9,11},{10,... | collective-permute-start | bytes 491528 | tf_op jit(solution)/shard_map/ppermute | solution.py:608
  77.9 15.0 %collective-permute-start.22 = (f32[320,128]{1,0:T(8,128)S(1)}, f32[320,128]{1,0:T(8,128)S(1)}, u32[]{:S(2)}, u32[]{:S(2)}) collective-permute-start(f32[320,128]{1,0:T(8,128)S(1)} %get-tuple-element.100), channel_id=1, source_target_pairs={{0,4},{1,5},{2,6},{3,7},{4,0},{5,1},{6,2},{7,3},{8,12},{9,13},{10,... | collective-permute-start | bytes 491528 | tf_op jit(solution)/shard_map/ppermute | solution.py:608
  78.2 14.7 %collective-permute-start.23 = (f32[320,128]{1,0:T(8,128)S(1)}, f32[320,128]{1,0:T(8,128)S(1)}, u32[]{:S(2)}, u32[]{:S(2)}) collective-permute-start(f32[320,128]{1,0:T(8,128)S(1)} %get-tuple-element.101), channel_id=1, source_target_pairs={{0,6},{1,7},{2,4},{3,5},{4,2},{5,3},{6,0},{7,1},{8,14},{9,15},{10,... | collective-permute-start | bytes 491528 | tf_op jit(solution)/shard_map/ppermute | solution.py:608
  80.4 1.4 %copy-start.8 = (f32[256,128]{1,0:T(8,128)S(1)}, f32[256,128]{1,0:T(8,128)}, u32[]{:S(2)}) copy-start(f32[256,128]{1,0:T(8,128)} %get-tuple-element.76.refs_1_.refs_9_) | copy-start | bytes 393220
  80.4 1.4 %copy-start.13 = (bf16[256,2560]{1,0:T(8,128)(2,1)S(1)}, bf16[256,2560]{1,0:T(8,128)(2,1)}, u32[]{:S(2)}) copy-start(bf16[256,2560]{1,0:T(8,128)(2,1)} %refs_0_.5) | copy-start | bytes 3932164
  80.4 1.8 %copy-start.14 = (bf16[256,2560]{1,0:T(8,128)(2,1)S(1)}, bf16[256,2560]{1,0:T(8,128)(2,1)}, u32[]{:S(2)}) copy-start(bf16[256,2560]{1,0:T(8,128)(2,1)} %refs_1_.11) | copy-start | bytes 3932164
  80.4 1.8 %copy-start.15 = (bf16[256,128]{1,0:T(8,128)(2,1)S(1)}, bf16[256,128]{1,0:T(8,128)(2,1)}, u32[]{:S(2)}) copy-start(bf16[256,128]{1,0:T(8,128)(2,1)} %refs_2_.11) | copy-start | bytes 196612
  80.4 1.7 %copy-start.16 = (bf16[256,128]{1,0:T(8,128)(2,1)S(1)}, bf16[256,128]{1,0:T(8,128)(2,1)}, u32[]{:S(2)}) copy-start(bf16[256,128]{1,0:T(8,128)(2,1)} %refs_3_.11) | copy-start | bytes 196612
  92.9 1.4 %collective-permute-start.24 = (f32[320,128]{1,0:T(8,128)S(1)}, f32[320,128]{1,0:T(8,128)S(1)}, u32[]{:S(2)}, u32[]{:S(2)}) collective-permute-start(f32[320,128]{1,0:T(8,128)S(1)} %get-tuple-element.102.refs_1_.refs_5_), channel_id=1, source_target_pairs={{0,1},{1,0},{2,3},{3,2},{4,5},{5,4},{6,7},{7,6},{8,9},{9,8},{10,11... | collective-permute-start | bytes 491528 | tf_op jit(solution)/shard_map/ppermute | solution.py:608
  92.9 1.6 %collective-permute-start.25 = (f32[320,128]{1,0:T(8,128)S(1)}, f32[320,128]{1,0:T(8,128)S(1)}, u32[]{:S(2)}, u32[]{:S(2)}) collective-permute-start(f32[320,128]{1,0:T(8,128)S(1)} %collective-permute-done.21.refs_6_), channel_id=1, source_target_pairs={{0,1},{1,0},{2,3},{3,2},{4,5},{5,4},{6,7},{7,6},{8,9},{9,8},{10,11... | collective-permute-start | bytes 491528 | tf_op jit(solution)/shard_map/ppermute | solution.py:608
  93.4 1.4 %collective-permute-start.26 = (f32[320,128]{1,0:T(8,128)S(1)}, f32[320,128]{1,0:T(8,128)S(1)}, u32[]{:S(2)}, u32[]{:S(2)}) collective-permute-start(f32[320,128]{1,0:T(8,128)S(1)} %collective-permute-done.22.refs_7_), channel_id=1, source_target_pairs={{0,1},{1,0},{2,3},{3,2},{4,5},{5,4},{6,7},{7,6},{8,9},{9,8},{10,11... | collective-permute-start | bytes 491528 | tf_op jit(solution)/shard_map/ppermute | solution.py:608
  93.4 1.6 %collective-permute-start.27 = (f32[320,128]{1,0:T(8,128)S(1)}, f32[320,128]{1,0:T(8,128)S(1)}, u32[]{:S(2)}, u32[]{:S(2)}) collective-permute-start(f32[320,128]{1,0:T(8,128)S(1)} %collective-permute-done.23.refs_8_), channel_id=1, source_target_pairs={{0,1},{1,0},{2,3},{3,2},{4,5},{5,4},{6,7},{7,6},{8,9},{9,8},{10,11... | collective-permute-start | bytes 491528 | tf_op jit(solution)/shard_map/ppermute | solution.py:608
  96.4 2.1 %collective-permute-start.28 = (f32[8,128]{1,0:T(8,128)S(1)}, f32[8,128]{1,0:T(8,128)S(1)}, u32[]{:S(2)}, u32[]{:S(2)}) collective-permute-start(f32[8,128]{1,0:T(8,128)S(1)} %add.39), channel_id=1, source_target_pairs={{0,1},{1,0},{2,3},{3,2},{4,5},{5,4},{6,7},{7,6},{8,9},{9,8},{10,11... | collective-permute-start | bytes 12296 | tf_op jit(solution)/shard_map/ppermute | solution.py:608
  98.5 7.8 %collective-permute-start.29 = (f32[8,128]{1,0:T(8,128)S(1)}, f32[8,128]{1,0:T(8,128)S(1)}, u32[]{:S(2)}, u32[]{:S(2)}) collective-permute-start(f32[8,128]{1,0:T(8,128)S(1)} %add.40), channel_id=1, source_target_pairs={{0,2},{1,3},{2,0},{3,1},{4,6},{5,7},{6,4},{7,5},{8,10},{9,11},{10,... | collective-permute-start | bytes 12296 | tf_op jit(solution)/shard_map/ppermute | solution.py:608
  101.4 4.9 %collective-permute-start.30 = (f32[8,128]{1,0:T(8,128)S(1)}, f32[8,128]{1,0:T(8,128)S(1)}, u32[]{:S(2)}, u32[]{:S(2)}) collective-permute-start(f32[8,128]{1,0:T(8,128)S(1)} %add.40), channel_id=1, source_target_pairs={{0,4},{1,5},{2,6},{3,7},{4,0},{5,1},{6,2},{7,3},{8,12},{9,13},{10,... | collective-permute-start | bytes 12296 | tf_op jit(solution)/shard_map/ppermute | solution.py:608
  101.7 5.4 %collective-permute-start.31 = (f32[8,128]{1,0:T(8,128)S(1)}, f32[8,128]{1,0:T(8,128)S(1)}, u32[]{:S(2)}, u32[]{:S(2)}) collective-permute-start(f32[8,128]{1,0:T(8,128)S(1)} %add.40), channel_id=1, source_target_pairs={{0,6},{1,7},{2,4},{3,5},{4,2},{5,3},{6,0},{7,1},{8,14},{9,15},{10,... | collective-permute-start | bytes 12296 | tf_op jit(solution)/shard_map/ppermute | solution.py:608
  105.7 0.6 copy-start.6
  107.2 7.0 %collective-permute-start.32 = (f32[8,128]{1,0:T(8,128)S(1)}, f32[8,128]{1,0:T(8,128)S(1)}, u32[]{:S(2)}, u32[]{:S(2)}) collective-permute-start(f32[8,128]{1,0:T(8,128)S(1)} %add_add_fusion.1), channel_id=1, source_target_pairs={{8,0},{9,1},{10,2},{11,3},{12,4},{13,5},{14,6},{15,7},{16,8},{17,9... | collective-permute-start | bytes 12296 | tf_op jit(solution)/shard_map/ppermute | solution.py:608
  108.4 8.5 %collective-permute-start.33 = (f32[8,128]{1,0:T(8,128)S(1)}, f32[8,128]{1,0:T(8,128)S(1)}, u32[]{:S(2)}, u32[]{:S(2)}) collective-permute-start(f32[8,128]{1,0:T(8,128)S(1)} %add_add_fusion.1), channel_id=1, source_target_pairs={{16,0},{17,1},{18,2},{19,3},{20,4},{21,5},{22,6},{23,7},{24,8},{25... | collective-permute-start | bytes 12296 | tf_op jit(solution)/shard_map/ppermute | solution.py:608
  109.7 9.1 %collective-permute-start.34 = (f32[8,128]{1,0:T(8,128)S(1)}, f32[8,128]{1,0:T(8,128)S(1)}, u32[]{:S(2)}, u32[]{:S(2)}) collective-permute-start(f32[8,128]{1,0:T(8,128)S(1)} %add_add_fusion.1), channel_id=1, source_target_pairs={{24,0},{25,1},{26,2},{27,3},{28,4},{29,5},{30,6},{31,7}} | collective-permute-start | bytes 12296 | tf_op jit(solution)/shard_map/ppermute | solution.py:608

commit v5 on v4

--- a/solution.py
+++ b/solution.py
@@ -112,6 +112,7 @@
     return pl.BlockSpec((rows, lanes), lambda c: (0, half * steps + c))
 
 
+LITTLE = pl.CostEstimate(flops=1, bytes_accessed=1, transcendentals=0)
 SCALARS = pl.BlockSpec(memory_space=pltpu.SMEM)
 STEPS = 2
 
@@ -201,9 +202,7 @@
             pltpu.VMEM((STATE, tokens), BF16),
         ],
         compiler_params=pltpu.CompilerParams(vmem_limit_bytes=BIG_VMEM),
-        cost_estimate=pl.CostEstimate(
-            flops=1_000_000_000, bytes_accessed=3_000_000, transcendentals=0
-        ),
+        cost_estimate=LITTLE,
         name="summary",
     )(place, x, g, write_map, read_map, *extra)
 
@@ -235,6 +234,7 @@
         out_specs=[whole(size + META, STRIP)] * chips,
         out_shape=[jax.ShapeDtypeStruct((size + META, STRIP), F32)] * chips,
         compiler_params=pltpu.CompilerParams(vmem_limit_bytes=SMALL_VMEM),
+        cost_estimate=LITTLE,
         name="combine",
     )(place, after, first, keep, decay, log)
 
@@ -242,6 +242,38 @@
 def rank_of(place, step):
     chip = place[1] ^ step
     return jnp.where(place[0] == 1, chip, -chip)
+
+
+def is_ahead(place, bit):
+    return ((place[2] >> bit) & 1) == place[0]
+
+
+def join_kernel(bit, offset, strips, head_size, place, mine_ref, got_ref, out_ref):
+    size = mine_ref.shape[0] - META
+    part = size // strips
+    ahead = is_ahead(place, bit)
+    mine_log = mine_ref[size : size + 1, :]
+    got_log = got_ref[size : size + 1, :]
+    mine_row = jnp.where(ahead, 1.0, jnp.exp(got_log))
+    got_row = jnp.where(ahead, jnp.exp(mine_log), 1.0)
+    mine_wide, got_wide = spread_rows([mine_row, got_row], offset, strips, head_size)
+    for strip in range(strips):
+        rows = slice(strip * part, (strip + 1) * part)
+        one = slice(strip, strip + 1)
+        out_ref[rows, :] = mine_ref[rows, :] * mine_wide[one, :] + got_ref[rows, :] * got_wide[one, :]
+    out_ref[size:, :] = jnp.broadcast_to(mine_log + got_log, (META, STRIP))
+
+
+def join(half, bit, strips, head_size, place, mine, got):
+    return pl.pallas_call(
+        lambda *refs: join_kernel(bit, half * strips, strips, head_size, *refs),
+        in_specs=[SCALARS, whole(*mine.shape), whole(*got.shape)],
+        out_specs=whole(*mine.shape),
+        out_shape=jax.ShapeDtypeStruct(mine.shape, F32),
+        compiler_params=pltpu.CompilerParams(vmem_limit_bytes=SMALL_VMEM),
+        cost_estimate=LITTLE,
+        name="join",
+    )(place, mine, got)
 
 
 def masked_sum(terms):
@@ -282,11 +314,12 @@
         out_specs=whole(*at[0].shape),
         out_shape=jax.ShapeDtypeStruct(at[0].shape, F32),
         compiler_params=pltpu.CompilerParams(vmem_limit_bytes=SMALL_VMEM),
+        cost_estimate=LITTLE,
         name="group_total",
     )(place, after, *at)
 
 
-def enter_kernel(chips, offset, strips, head_size, place, *refs):
+def enter_kernel(chips, offset, strips, head_size, place, after_ref, *refs):
     at_refs, got_refs, out_refs = refs[:chips], refs[chips:-chips], refs[-chips:]
     part = STATE // chips
     size = strips * part
@@ -295,9 +328,10 @@
     zero = jnp.zeros_like(logs[0])
     rows_of = []
     passed = zero
-    for ref in got_refs:
-        rows_of.append(jnp.exp(passed))
-        passed = passed + ref[size : size + 1, :]
+    for bit, ref in enumerate(got_refs):
+        ahead = is_ahead(place, bit)
+        rows_of.append(jnp.where(ahead, jnp.exp(passed), 0.0))
+        passed = passed + jnp.where(ahead, ref[size : size + 1, :], 0.0)
     for to in range(chips):
         rows_of.append(
             jnp.exp(masked_sum([(rank[m] < rank[to], logs[m]) for m in range(chips)]))
@@ -327,18 +361,20 @@
             out_refs[to][rows, :] = entering
 
 
-def enter(half, head_size, place, at, got):
+def enter(half, head_size, place, after, at, got):
     chips = len(at)
     strips = (at[0].shape[0] - META) * chips // STATE
     size = strips * (STATE // chips)
     return pl.pallas_call(
         lambda *refs: enter_kernel(chips, half * strips, strips, head_size, *refs),
-        in_specs=[SCALARS] + [whole(*at[0].shape)] * (chips + len(got)),
+        grid=(1,),
+        in_specs=[SCALARS, whole(META, STRIP)] + [whole(*at[0].shape)] * (chips + len(got)),
         out_specs=[whole(size, STRIP)] * chips,
         out_shape=[jax.ShapeDtypeStruct((size, STRIP), F32)] * chips,
         compiler_params=pltpu.CompilerParams(vmem_limit_bytes=SMALL_VMEM),
+        cost_estimate=LITTLE,
         name="enter",
-    )(place, *at, *got)
+    )(place, after, *at, *got)
 
 
 def intra_kernel(
@@ -437,18 +473,36 @@
             pltpu.VMEM((STATE, tokens), BF16),
         ],
         compiler_params=pltpu.CompilerParams(vmem_limit_bytes=BIG_VMEM),
-        cost_estimate=pl.CostEstimate(
-            flops=12_000_000_000, bytes_accessed=8_000_000, transcendentals=heads * tokens * tokens
-        ),
+        cost_estimate=LITTLE,
         name="intra",
     )(after, x, g, write_map, read_map, rates, *shared[1:])
 
 
+def order_kernel(place, *refs):
+    pieces, out_ref = refs[:-1], refs[-1]
+    size = pieces[0].shape[0]
+    for step, ref in enumerate(pieces):
+        rows = pl.ds(pl.multiple_of((place[1] ^ step) * size, size), size)
+        out_ref[rows, :] = ref[...]
+
+
+def order(place, pieces):
+    shape = (len(pieces) * pieces[0].shape[0], STRIP)
+    return pl.pallas_call(
+        order_kernel,
+        in_specs=[SCALARS] + [whole(*value.shape) for value in pieces],
+        out_specs=whole(*shape),
+        out_shape=jax.ShapeDtypeStruct(shape, F32),
+        compiler_params=pltpu.CompilerParams(vmem_limit_bytes=SMALL_VMEM),
+        cost_estimate=LITTLE,
+        name="order",
+    )(place, *pieces)
+
+
 def assemble_kernel(
-    heads, chips, half, head_size, place, after, first_ref, state_own, back_own, *refs,
+    heads, chips, half, head_size, place, after, first_ref, state_own, back_own, own_ref, far_ref,
+    state_ref, back_ref, total_ref,
 ):
-    own_refs, far_refs = refs[:chips], refs[chips : 2 * chips]
-    state_ref, back_ref, total_ref = refs[2 * chips :]
     lanes = state_ref.shape[1]
     strips = lanes // STRIP
     part = STATE // chips
@@ -457,15 +511,13 @@
     decay = spread_rows([jnp.exp(log)], half * strips, strips, head_size)[0]
     is_first = place[0] == 0
     sums = [None] * strips
-    for step in range(chips):
-        quarter = place[1] ^ step
-        rows = pl.ds(pl.multiple_of(quarter * part, part), part)
+    for quarter in range(chips):
+        rows = slice(quarter * part, (quarter + 1) * part)
         for strip in range(strips):
             wide = slice(strip * STRIP, (strip + 1) * STRIP)
-            here = slice(strip * part, (strip + 1) * part)
-            there = pl.ds(pl.multiple_of(quarter * size + strip * part, part), part)
-            own = own_refs[step][here, :] * decay[strip : strip + 1, :] + first_ref[there, :]
-            far = far_refs[step][here, :]
+            here = slice(quarter * size + strip * part, quarter * size + (strip + 1) * part)
+            own = own_ref[here, :] * decay[strip : strip + 1, :] + first_ref[here, :]
+            far = far_ref[here, :]
             state = jnp.where(is_first, far, own).astype(BF16)
             back = jnp.where(is_first, own, far).astype(BF16)
             state_ref[rows, wide] = state
@@ -481,8 +533,7 @@
     )
 
 
-def assemble(heads, half, place, after, first, state_own, back_own, own, far):
-    chips = len(own)
+def assemble(heads, chips, half, place, after, first, state_own, back_own, own, far):
     wide = state_own.shape[1]
     lanes = wide // HALVES
     mine = pl.BlockSpec((STATE, lanes), lambda c: (0, half))
@@ -490,7 +541,7 @@
         lambda *refs: assemble_kernel(heads, chips, half, wide // heads, *refs),
         grid=(1,),
         in_specs=[SCALARS, whole(META, STRIP), whole(*first.shape), mine, mine]
-        + [whole(*value.shape) for value in (*own, *far)],
+        + [whole(*own.shape), whole(*far.shape)],
         out_specs=[whole(STATE, lanes), whole(STATE, lanes), whole(META, STRIP)],
         out_shape=[
             jax.ShapeDtypeStruct((STATE, lanes), BF16),
@@ -498,15 +549,16 @@
             jax.ShapeDtypeStruct((META, STRIP), F32),
         ],
         compiler_params=pltpu.CompilerParams(vmem_limit_bytes=SMALL_VMEM),
+        cost_estimate=LITTLE,
         name="assemble",
-    )(place, after, first, state_own, back_own, *own, *far)
+    )(place, after, first, state_own, back_own, own, far)
 
 
 def finish_kernel(
-    heads, start, steps, x_ref, g_ref, write_ref, read_ref, tail_ref, lead_ref,
+    heads, start, steps, last, x_ref, g_ref, write_ref, read_ref, tail_ref, lead_ref,
     dx_ref, db_ref, dc_ref, change_ref, state_ref, back_ref, *refs,
 ):
-    grad_ref, db_out, dc_out, sum_out, db_sum, dc_sum = refs[-6:]
+    grad_ref, db_out, dc_out, change_out, db_sum, dc_sum, sum_out = refs[-7:]
     chunk = pl.program_id(0)
     lanes = x_ref.shape[1]
     head_size = lanes * STEPS * HALVES // heads
@@ -537,6 +589,10 @@
     def _():
         db_out[...] = db_sum[...].astype(db_out.dtype)
         dc_out[...] = dc_sum[...].astype(dc_out.dtype)
+        if last:
+            change_out[...] = dot(sum_out[...], lower(STRETCH), 0, 0, HIGHEST)[:heads, :]
+        else:
+            change_out[...] = sum_out[...]
 
 
 def finish(heads, start, steps, x, g, write_map, read_map, shared, dx, sums, state, back, grad):
@@ -544,10 +600,12 @@
     lanes = wide // (STEPS * HALVES)
     strip = pl.BlockSpec((tokens, lanes), lambda c: (0, start + c))
     own = pl.BlockSpec((STATE, lanes), lambda c: (0, start % STEPS + c))
-    kind = BF16 if start + steps == STEPS * HALVES else F32
+    last = start + steps == STEPS * HALVES
+    kind = BF16 if last else F32
+    change = (heads, tokens) if last else (tokens, STATE)
     earlier = [] if grad is None else [grad]
     return pl.pallas_call(
-        lambda *refs: finish_kernel(heads, start, steps, *refs),
+        lambda *refs: finish_kernel(heads, start, steps, last, *refs),
         grid=(steps,),
         in_specs=[strip, strip]
         + [whole(tokens, STATE)] * 4
@@ -555,38 +613,35 @@
         + [whole(tokens, STATE)] * 3
         + [own, own]
         + [pl.BlockSpec(memory_space=pl.ANY)] * len(earlier),
-        out_specs=[strip] + [whole(tokens, STATE)] * 3,
+        out_specs=[strip] + [whole(tokens, STATE)] * 2 + [whole(*change)],
         out_shape=[
             jax.ShapeDtypeStruct((tokens, wide), BF16),
             jax.ShapeDtypeStruct((tokens, STATE), kind),
             jax.ShapeDtypeStruct((tokens, STATE), kind),
-            jax.ShapeDtypeStruct((tokens, STATE), F32),
+            jax.ShapeDtypeStruct(change, F32),
         ],
-        scratch_shapes=[pltpu.VMEM((tokens, STATE), F32)] * 2,
+        scratch_shapes=[pltpu.VMEM((tokens, STATE), F32)] * 3,
         input_output_aliases={12: 0} if earlier else {},
         compiler_params=pltpu.CompilerParams(vmem_limit_bytes=SMALL_VMEM),
-        cost_estimate=pl.CostEstimate(
-            flops=3_000_000_000, bytes_accessed=5_000_000, transcendentals=0
-        ),
+        cost_estimate=LITTLE,
         name="finish",
     )(x, g, write_map, read_map, *shared[2:], dx, *sums, state, back, *earlier)
 
 
-def suffix_kernel(change_ref, later_ref, out_ref):
+def add_later_kernel(suffix_ref, later_ref, out_ref):
     heads = out_ref.shape[0]
-    last = iota((STRETCH, STATE), 0) == STRETCH - 1
-    change = change_ref[...] + jnp.where(last, later_ref[0:1, :], 0.0)
-    out_ref[...] = dot(change, lower(STRETCH), 0, 0, HIGHEST)[:heads, :]
-
-
-def suffix(heads, change, later):
-    return pl.pallas_call(
-        suffix_kernel,
-        in_specs=[whole(*change.shape), whole(*later.shape)],
-        out_specs=whole(heads, STRETCH),
-        out_shape=jax.ShapeDtypeStruct((heads, STRETCH), F32),
-        name="suffix",
-    )(change, later)
+    out_ref[...] = suffix_ref[...] + later_ref[...].T[:heads, 0:1]
+
+
+def add_later(suffix, later):
+    return pl.pallas_call(
+        add_later_kernel,
+        in_specs=[whole(*suffix.shape), whole(*later.shape)],
+        out_specs=whole(*suffix.shape),
+        out_shape=jax.ShapeDtypeStruct(suffix.shape, F32),
+        cost_estimate=LITTLE,
+        name="add_later",
+    )(suffix, later)
 
 
 def per_device(inputs, out_grad, input_map, output_map, log_decay):
@@ -594,9 +649,11 @@
     head_size = inputs.shape[1] // heads
     groups, shards = lax.axis_size("grp"), lax.axis_size("seq")
     chips = shards // 2
-    shard = lax.axis_index("seq")
-    chip, core = shard // 2, shard % 2
-    place = jnp.stack([core, chip]).astype(jnp.int32)
+    shard, group = lax.axis_index("seq"), lax.axis_index("grp")
+    chip, core = shard >> 1, shard & 1
+    place = jnp.stack([core, chip, group]).astype(jnp.int32)
+    strips = inputs.shape[1] // STRIP // HALVES
+    bits = groups.bit_length() - 1
     everyone = [(a, z, c) for a in range(groups) for z in range(chips) for c in range(2)]
 
     def move(value, target):
@@ -613,12 +670,8 @@
     def to_chip(value, step):
         return move(value, lambda a, z, c: (a, z ^ step, c)) if step else value
 
-    def to_group(value, step, ahead):
-        def target(a, z, c):
-            to = a + step if ahead(c) else a - step
-            return (to, z, c) if 0 <= to < groups else None
-
-        return move(value, target)
+    def to_group(value, step):
+        return move(value, lambda a, z, c: (a ^ step, z, c))
 
     def hold(value, *tokens):
         return lax.optimization_barrier((value, tokens))[0]
@@ -632,19 +685,28 @@
     dx, db, dc, change, state_own, back_own = intra(pieces[0][0], *maps, log_decay, shared)
     pieces.append(combine(chips, place, change, first[1], keep, decay, shared[0]))
 
-    own, token = [], pieces[1][0]
+    at, total, token = [], [], pieces[1][0]
     for half in range(HALVES):
-        at = [to_chip(value, step) for step, value in enumerate(pieces[half])]
-        total = group_total(half, head_size, place, token, at)
-        got = [to_group(total, step, lambda c: c == 1) for step in range(1, groups)]
-        inside = enter(half, head_size, place, at, got)
+        at.append([to_chip(value, step) for step, value in enumerate(pieces[half])])
+        total.append(group_total(half, head_size, place, token, at[half]))
+        token = total[half]
+    own = []
+    for half in range(HALVES):
+        block, got = total[half], []
+        for bit in range(bits):
+            got.append(to_group(block, 1 << bit))
+            if bit < bits - 1:
+                block = join(half, bit, strips, head_size, place, block, got[bit])
+        inside = enter(half, head_size, place, token, at[half], got)
+        token = inside[0]
         own.append([to_chip(value, step) for step, value in enumerate(inside)])
-        token = inside[0]
+
+    own[0] = hold(own[0], token)
 
     def entering(half, token):
-        far = [to_core(value) for value in own[half]]
+        mine = order(place, own[half])
         return assemble(
-            heads, half, place, token, first[half], state_own, back_own, own[half], far
+            heads, chips, half, place, token, first[half], state_own, back_own, mine, to_core(mine)
         )
 
     state, back, tally = entering(0, token)
@@ -653,21 +715,21 @@
     state, back, tally_b = entering(1, sums[2])
     tally = tally + tally_b
 
-    other = to_core(tally)
+    def count(later, tally, got, bit, index):
+        return later + jnp.where((index >> bit) & 1 == 0, got, 0.0), tally + got
+
+    got = to_core(tally)
     grad, *sums = finish(heads, STEPS, 1, *maps, shared, dx, sums, state, back, grad)
-    other = hold(other, sums[2])
-    later = jnp.where(core == 0, other, 0.0)
-    tally = tally + other
-    steps = [to_chip(tally, step) for step in range(1, chips)]
+    later, tally = count(0.0, tally, hold(got, sums[2]), 0, core)
+    got = to_chip(tally, 1)
     sums = hold(sums, tally)
     grad, *sums = finish(heads, STEPS + 1, 1, *maps, shared, dx, sums, state, back, grad)
-    steps = hold(steps, sums[2])
-    for step, value in enumerate(steps, 1):
-        later = later + jnp.where((chip ^ step) > chip, value, 0.0)
-        tally = tally + value
-    for step in range(1, groups):
-        later = later + to_group(tally, step, lambda c: False)
-    return (grad, sums[0], sums[1], suffix(heads, sums[2], later))
+    later, tally = count(later, tally, hold(got, sums[2]), 0, chip)
+    for bit in range(1, chips.bit_length() - 1):
+        later, tally = count(later, tally, to_chip(tally, 1 << bit), bit, chip)
+    for bit in range(bits):
+        later, tally = count(later, tally, to_group(tally, 1 << bit), bit, group)
+    return (grad, sums[0], sums[1], add_later(sums[2], later))
 
 
 def solution(mesh):

time: 122 us -> 117 us (0.959)
  starting transfers between devices: 56.6 us -> 37.8 us
  waiting for transfers between devices: 21.6 us -> 34.1 us
  Pallas kernels: 38.1 us -> 40.4 us
    ppermute x35 -> x25, starting transfers between devices: 56.6 us -> 37.8 us  [move(): return lax.ppermute(value, ('grp', 'seq'), pairs)]
    ppermute x35 -> x25, waiting for transfers between devices: 21.6 us -> 34.1 us  [move(): return lax.ppermute(value, ('grp', 'seq'), pairs)]
    pallas_call x4 -> x8, Pallas kernels: 9.15 us -> 11.5 us  [the longest x3 7.3 us: finish(): pl.pallas_call(lambda *refs: finish_kernel(heads, start, steps, last, *re...]
  transfers between devices with their start and end apart: 35 -> 25, of which waited for: 12 -> 10; matrix products, arithmetic and copies ran while one was open for 0% -> 0% of each run, Pallas kernels for 25% -> 28%
where the time goes in v5:
time: 117 us
  Pallas kernels  40.4 us (35%)
  starting transfers between devices  37.8 us (32%)
  waiting for transfers between devices  34.1 us (29%)
  local copies, waits for them, and re-layouts  2.65 us (2%)
  other arithmetic  1.28 us (1%)
    ppermute x25, starting transfers between devices, move(): return lax.ppermute(value, ('grp', 'seq'), pairs)  37.8 us
    ppermute x25, waiting for transfers between devices, move(): return lax.ppermute(value, ('grp', 'seq'), pairs)  34.1 us
    pallas_call x1, Pallas kernels, intra(): pl.pallas_call(lambda *refs: intra_kernel(heads, *refs), grid=(wide // LA...  14 us
    pallas_call x2, Pallas kernels, summary(): pl.pallas_call(lambda *refs: summary_kernel(heads, chips, half, *refs), g...  7.35 us
    pallas_call x3, Pallas kernels, finish(): pl.pallas_call(lambda *refs: finish_kernel(heads, start, steps, last, *re...  7.3 us
    unnamed x44, local copies, waits for them, and re-layouts  2.65 us
    pallas_call x2, Pallas kernels, assemble(): pl.pallas_call(lambda *refs: assemble_kernel(heads, chips, half, wide //...  2.64 us
  transfers between devices with their start and end apart: 25, of which 10 were waited for; matrix products, arithmetic and copies ran while one was open for 0% of the time, Pallas kernels for 28%

profile of v5, /device:TPU:0, one launch (start us, length us, event | category | flops | bytes accessed | tf_op | source)
XLA Modules:
  0.0 117.1 jit_solution(5742003156518259686)
XLA Ops:
  0.6 0.7 pad_add_fusion.refs_0_.place
  1.3 3.8 %summary.2 = (f32[1288,128]{1,0:T(8,128)}, f32[1280,128]{1,0:T(8,128)}, f32[10,128]{1,0:T(8,128)}, f32[8,128]{1,0:T(8,128)}, f32[256,128]{1,0:T(8,128)}, /*index...) custom-call(s32[3]{0:T(128)} %pad_add_fusion.refs_0_.place, bf16[256,2560]{1,0:T(8,128)(2,1)} %refs_0_.5, ...), custom_call_target="tpu_custom_call" | custom-call | flops 1 | bytes 1 | tf_op jit(solution)/shard_map/summary/pallas_call | solution.py:187
  5.1 0.5 collective-permute-start
  5.6 3.6 %summary.3 = (f32[1288,128]{1,0:T(8,128)}, f32[1280,128]{1,0:T(8,128)}, f32[10,128]{1,0:T(8,128)}) custom-call(s32[3]{0:T(128)} %pad_add_fusion.refs_0_.place, bf16[256,2560]{1,0:T(8,128)(2,1)} %refs_0_.5, bf16[256,2560]{1,0:T(8,128)(2,1)} %refs_1_.11, bf16[256,128]{1,0:T(8,128)(2,1)} %refs_2_.11, bf16[256,128]{1,0:T(8,128)(2,1)} %refs_3_.11, ...), custom_call_target="tpu_custom_call" | custom-call | flops 1 | bytes 1 | tf_op jit(solution)/shard_map/summary/pallas_call | solution.py:187
  9.2 0.1 collective-permute-start.1
  9.3 0.7 combine.2
  9.9 0.6 copy-done.9
  10.6 3.0 %collective-permute-start.2 = (f32[328,128]{1,0:T(8,128)S(1)}, f32[328,128]{1,0:T(8,128)S(1)}, u32[]{:S(2)}, u32[]{:S(2)}) collective-permute-start(f32[328,128]{1,0:T(8,128)S(1)} %get-tuple-element.83), channel_id=1, source_target_pairs={{0,2},{1,3},{2,0},{3,1},{4,6},{5,7},{6,4},{7,5},{8,10},{9,11},{10,... | collective-permute-start | bytes 503816 | tf_op jit(solution)/shard_map/ppermute | solution.py:665
  13.6 2.6 %collective-permute-start.3 = (f32[328,128]{1,0:T(8,128)S(1)}, f32[328,128]{1,0:T(8,128)S(1)}, u32[]{:S(2)}, u32[]{:S(2)}) collective-permute-start(f32[328,128]{1,0:T(8,128)S(1)} %get-tuple-element.84), channel_id=1, source_target_pairs={{0,4},{1,5},{2,6},{3,7},{4,0},{5,1},{6,2},{7,3},{8,12},{9,13},{10,... | collective-permute-start | bytes 503816 | tf_op jit(solution)/shard_map/ppermute | solution.py:665
  16.2 14.0 %intra.1 = (f32[256,2560]{1,0:T(8,128)}, f32[256,128]{1,0:T(8,128)}, f32[256,128]{1,0:T(8,128)}, f32[256,128]{1,0:T(8,128)}, f32[128,2560]{1,0:T(8,128)}, /*index=5*/f32[128,2560]{1,0:T(8,128)}) custom-call(f32[328,128]{1,0:T(8,128)} %copy-done.9, bf16[256,2560]{1,0:T(8,128)(2,1)} %refs_0_.5, bf16[256,2560]{1,0:T(8,128)(2,1)} %refs_1_.11, ...), custom_call_target="tpu_custom_call" | custom-call | flops 1 | bytes 1 | tf_op jit(solution)/shard_map/intra/pallas_call | solution.py:446
  30.3 0.9 copy-done.13
  31.2 0.7 combine.3
  31.8 1.0 collective-permute-start.5
  32.8 3.5 %collective-permute-start.6 = (f32[328,128]{1,0:T(8,128)S(1)}, f32[328,128]{1,0:T(8,128)S(1)}, u32[]{:S(2)}, u32[]{:S(2)}) collective-permute-start(f32[328,128]{1,0:T(8,128)S(1)} %get-tuple-element.87), channel_id=1, source_target_pairs={{0,4},{1,5},{2,6},{3,7},{4,0},{5,1},{6,2},{7,3},{8,12},{9,13},{10,... | collective-permute-start | bytes 503816 | tf_op jit(solution)/shard_map/ppermute | solution.py:665
  36.3 0.8 group_total.2.refs_1_
  37.1 1.8 %collective-permute-start.8 = (f32[328,128]{1,0:T(8,128)S(1)}, f32[328,128]{1,0:T(8,128)S(1)}, u32[]{:S(2)}, u32[]{:S(2)}) collective-permute-start(f32[328,128]{1,0:T(8,128)S(1)} %group_total.2.refs_1_), channel_id=1, source_target_pairs={{0,8},{1,9},{2,10},{3,11},{4,12},{5,13},{6,14},{7,15},{8,0},{9,1},... | collective-permute-start | bytes 503816 | tf_op jit(solution)/shard_map/ppermute | solution.py:665
  38.9 1.0 collective-permute-done.5.refs_3_
  39.9 8.8 %collective-permute-done.6.refs_4_ = f32[328,128]{1,0:T(8,128)S(1)} collective-permute-done((f32[328,128]{1,0:T(8,128)S(1)}, f32[328,128]{1,0:T(8,128)S(1)}, u32[]{:S(2)}, u32[]{:S(2)}) %collective-permute-start.6) | collective-permute-done | bytes 167968 | tf_op jit(solution)/shard_map/ppermute | solution.py:665
  48.7 0.8 group_total.3.refs_1_
  49.5 1.6 %collective-permute-start.10 = (f32[328,128]{1,0:T(8,128)S(1)}, f32[328,128]{1,0:T(8,128)S(1)}, u32[]{:S(2)}, u32[]{:S(2)}) collective-permute-start(f32[328,128]{1,0:T(8,128)S(1)} %group_total.3.refs_1_), channel_id=1, source_target_pairs={{0,8},{1,9},{2,10},{3,11},{4,12},{5,13},{6,14},{7,15},{8,0},{9,1},... | collective-permute-start | bytes 503816 | tf_op jit(solution)/shard_map/ppermute | solution.py:665
  51.0 0.7 join.2
  51.8 1.6 %collective-permute-start.9 = (f32[328,128]{1,0:T(8,128)S(1)}, f32[328,128]{1,0:T(8,128)S(1)}, u32[]{:S(2)}, u32[]{:S(2)}) collective-permute-start(f32[328,128]{1,0:T(8,128)S(1)} %join.2), channel_id=1, source_target_pairs={{0,16},{1,17},{2,18},{3,19},{4,20},{5,21},{6,22},{7,23},{8,24},{9,... | collective-permute-start | bytes 503816 | tf_op jit(solution)/shard_map/ppermute | solution.py:665
  53.4 1.5 %collective-permute-done.10.refs_2_.refs_6_ = f32[328,128]{1,0:T(8,128)S(1)} collective-permute-done((f32[328,128]{1,0:T(8,128)S(1)}, f32[328,128]{1,0:T(8,128)S(1)}, u32[]{:S(2)}, u32[]{:S(2)}) %collective-permute-start.10) | collective-permute-done | bytes 167968 | tf_op jit(solution)/shard_map/ppermute | solution.py:665
  54.9 0.7 join.3
  55.6 1.6 %collective-permute-start.11 = (f32[328,128]{1,0:T(8,128)S(1)}, f32[328,128]{1,0:T(8,128)S(1)}, u32[]{:S(2)}, u32[]{:S(2)}) collective-permute-start(f32[328,128]{1,0:T(8,128)S(1)} %join.3), channel_id=1, source_target_pairs={{0,16},{1,17},{2,18},{3,19},{4,20},{5,21},{6,22},{7,23},{8,24},{9,... | collective-permute-start | bytes 503816 | tf_op jit(solution)/shard_map/ppermute | solution.py:665
  57.2 1.0 enter.2
  58.3 0.0 copy-start.3
  58.3 4.2 %collective-permute-start.12 = (f32[320,128]{1,0:T(8,128)S(1)}, f32[320,128]{1,0:T(8,128)S(1)}, u32[]{:S(2)}, u32[]{:S(2)}) collective-permute-start(f32[320,128]{1,0:T(8,128)S(1)} %get-tuple-element.93), channel_id=1, source_target_pairs={{0,2},{1,3},{2,0},{3,1},{4,6},{5,7},{6,4},{7,5},{8,10},{9,11},{10,... | collective-permute-start | bytes 491528 | tf_op jit(solution)/shard_map/ppermute | solution.py:665
  62.4 0.9 collective-permute-start.13
  63.3 1.6 %collective-permute-start.14 = (f32[320,128]{1,0:T(8,128)S(1)}, f32[320,128]{1,0:T(8,128)S(1)}, u32[]{:S(2)}, u32[]{:S(2)}) collective-permute-start(f32[320,128]{1,0:T(8,128)S(1)} %get-tuple-element.95), channel_id=1, source_target_pairs={{0,6},{1,7},{2,4},{3,5},{4,2},{5,3},{6,0},{7,1},{8,14},{9,15},{10,... | collective-permute-start | bytes 491528 | tf_op jit(solution)/shard_map/ppermute | solution.py:665
  64.9 1.0 enter.3
  65.9 2.1 %collective-permute-done.12.refs_1_ = f32[320,128]{1,0:T(8,128)S(1)} collective-permute-done((f32[320,128]{1,0:T(8,128)S(1)}, f32[320,128]{1,0:T(8,128)S(1)}, u32[]{:S(2)}, u32[]{:S(2)}) %collective-permute-start.12) | collective-permute-done | bytes 163872 | tf_op jit(solution)/shard_map/ppermute | solution.py:665
  68.0 5.4 %collective-permute-done.13.refs_2_ = f32[320,128]{1,0:T(8,128)S(1)} collective-permute-done((f32[320,128]{1,0:T(8,128)S(1)}, f32[320,128]{1,0:T(8,128)S(1)}, u32[]{:S(2)}, u32[]{:S(2)}) %collective-permute-start.13) | collective-permute-done | bytes 163872 | tf_op jit(solution)/shard_map/ppermute | solution.py:665
  73.4 0.6 order.2.refs_5_
  74.0 0.1 collective-permute-start.15
  74.1 2.4 %collective-permute-start.16 = (f32[320,128]{1,0:T(8,128)S(1)}, f32[320,128]{1,0:T(8,128)S(1)}, u32[]{:S(2)}, u32[]{:S(2)}) collective-permute-start(f32[320,128]{1,0:T(8,128)S(1)} %get-tuple-element.105), channel_id=1, source_target_pairs={{0,2},{1,3},{2,0},{3,1},{4,6},{5,7},{6,4},{7,5},{8,10},{9,11},{10,... | collective-permute-start | bytes 491528 | tf_op jit(solution)/shard_map/ppermute | solution.py:665
  76.5 1.4 %collective-permute-start.17 = (f32[320,128]{1,0:T(8,128)S(1)}, f32[320,128]{1,0:T(8,128)S(1)}, u32[]{:S(2)}, u32[]{:S(2)}) collective-permute-start(f32[320,128]{1,0:T(8,128)S(1)} %get-tuple-element.106), channel_id=1, source_target_pairs={{0,4},{1,5},{2,6},{3,7},{4,0},{5,1},{6,2},{7,3},{8,12},{9,13},{10,... | collective-permute-start | bytes 491528 | tf_op jit(solution)/shard_map/ppermute | solution.py:665
  77.9 1.4 %collective-permute-start.18 = (f32[320,128]{1,0:T(8,128)S(1)}, f32[320,128]{1,0:T(8,128)S(1)}, u32[]{:S(2)}, u32[]{:S(2)}) collective-permute-start(f32[320,128]{1,0:T(8,128)S(1)} %get-tuple-element.107), channel_id=1, source_target_pairs={{0,6},{1,7},{2,4},{3,5},{4,2},{5,3},{6,0},{7,1},{8,14},{9,15},{10,... | collective-permute-start | bytes 491528 | tf_op jit(solution)/shard_map/ppermute | solution.py:665
  79.3 0.0 copy-start
  79.3 0.0 copy-start.6
  79.4 1.3 %assemble.2 = (bf16[128,1280]{1,0:T(8,128)(2,1)S(1)}, bf16[128,1280]{1,0:T(8,128)(2,1)S(1)}, f32[8,128]{1,0:T(8,128)S(1)}) custom-call(s32[3]{0:T(128)S(1)} %copy-done.17, f32[320,128]{1,0:T(8,128)S(1)} %get-tuple-element.108.refs_1_.refs_0_, f32[1288,128]{1,0:T(8,128)S(1)} %collective-permute-done.refs_2_, f32[128,2560]{1,0:T(8,128)S(1)} %copy-done.3, ...), custom_call_target="tpu_custom_call" | custom-call | flops 1 | bytes 1 | tf_op jit(solution)/shard_map/assemble/pallas_call | solution.py:540
  80.7 0.0 copy-done
  80.7 0.3 copy-done.1
  81.0 0.0 copy-done.14
  81.0 0.0 copy-done.15
  81.1 3.8 %finish.3 = (bf16[256,2560]{1,0:T(8,128)(2,1)}, f32[256,128]{1,0:T(8,128)S(1)}, f32[256,128]{1,0:T(8,128)S(1)}, f32[256,128]{1,0:T(8,128)S(1)}) custom-call(bf16[256,2560]{1,0:T(8,128)(2,1)S(1)} %copy-done, bf16[256,2560]{1,0:T(8,128)(2,1)S(1)} %copy-done.1, bf16[256,128]{1,0:T(8,128)(2,1)S(1)} %copy-done.5, bf16[256,128]{1,0:T(8,128)(2,1)S(1)} %copy-done.6, ...), custom_call_target="tpu_custom_call" | custom-call | flops 1 | bytes 1 | tf_op jit(solution)/shard_map/finish/pallas_call | solution.py:607
  84.8 6.6 %collective-permute-done.17.refs_2_ = f32[320,128]{1,0:T(8,128)S(1)} collective-permute-done((f32[320,128]{1,0:T(8,128)S(1)}, f32[320,128]{1,0:T(8,128)S(1)}, u32[]{:S(2)}, u32[]{:S(2)}) %collective-permute-start.17) | collective-permute-done | bytes 163872 | tf_op jit(solution)/shard_map/ppermute | solution.py:665
  91.5 0.6 order.3.refs_5_
  92.1 0.1 collective-permute-start.19
  92.2 2.1 %collective-permute-done.19.refs_6_ = f32[1280,128]{1,0:T(8,128)S(1)} collective-permute-done((f32[1280,128]{1,0:T(8,128)S(1)}, f32[1280,128]{1,0:T(8,128)S(1)}, u32[]{:S(2)}, u32[]{:S(2)}) %collective-permute-start.19) | collective-permute-done | bytes 655392 | tf_op jit(solution)/shard_map/ppermute | solution.py:665
  94.2 1.3 %assemble.3 = (bf16[128,1280]{1,0:T(8,128)(2,1)S(1)}, bf16[128,1280]{1,0:T(8,128)(2,1)S(1)}, f32[8,128]{1,0:T(8,128)S(1)}) custom-call(s32[3]{0:T(128)S(1)} %copy-done.17, f32[256,128]{1,0:T(8,128)S(1)} %get-tuple-element.104.refs_1_.refs_9_, f32[1288,128]{1,0:T(8,128)S(1)} %collective-permute-done.1.refs_2_, f32[128,2560]{1,0:T(8,128)S(1)} %copy-done.3, ...), custom_call_target="tpu_custom_call" | custom-call | flops 1 | bytes 1 | tf_op jit(solution)/shard_map/assemble/pallas_call | solution.py:540
  95.6 0.2 collective-permute-start.20
  95.8 1.7 %finish.4 = (bf16[256,2560]{1,0:T(8,128)(2,1)}, f32[256,128]{1,0:T(8,128)S(1)}, f32[256,128]{1,0:T(8,128)S(1)}, f32[256,128]{1,0:T(8,128)S(1)}) custom-call(bf16[256,2560]{1,0:T(8,128)(2,1)S(1)} %copy-done, bf16[256,2560]{1,0:T(8,128)(2,1)S(1)} %copy-done.1, bf16[256,128]{1,0:T(8,128)(2,1)S(1)} %copy-done.5, ...), custom_call_target="tpu_custom_call", output_to_operand_aliasing={{0}: (12, {})} | custom-call | flops 1 | bytes 1 | tf_op jit(solution)/shard_map/finish/pallas_call | solution.py:607
  97.5 3.3 %collective-permute-start.21 = (f32[8,128]{1,0:T(8,128)S(1)}, f32[8,128]{1,0:T(8,128)S(1)}, u32[]{:S(2)}, u32[]{:S(2)}) collective-permute-start(f32[8,128]{1,0:T(8,128)S(1)} %add.28), channel_id=1, source_target_pairs={{0,2},{1,3},{2,0},{3,1},{4,6},{5,7},{6,4},{7,5},{8,10},{9,11},{10,... | collective-permute-start | bytes 12296 | tf_op jit(solution)/shard_map/ppermute | solution.py:665
  100.9 1.8 %finish.5 = (bf16[256,2560]{1,0:T(8,128)(2,1)}, bf16[256,128]{1,0:T(8,128)(2,1)}, bf16[256,128]{1,0:T(8,128)(2,1)}, f32[40,256]{1,0:T(8,128)S(1)}) custom-call(bf16[256,2560]{1,0:T(8,128)(2,1)S(1)} %copy-done, bf16[256,2560]{1,0:T(8,128)(2,1)S(1)} %copy-done.1, bf16[256,128]{1,0:T(8,128)(2,1)S(1)} %copy-done.5, ...), custom_call_target="tpu_custom_call", output_to_operand_aliasing={{0}: (12, {})} | custom-call | flops 1 | bytes 1 | tf_op jit(solution)/shard_map/finish/pallas_call | solution.py:607
  102.6 0.6 copy-done.19
  103.3 2.5 %collective-permute-start.22 = (f32[8,128]{1,0:T(8,128)S(1)}, f32[8,128]{1,0:T(8,128)S(1)}, u32[]{:S(2)}, u32[]{:S(2)}) collective-permute-start(f32[8,128]{1,0:T(8,128)S(1)} %add.30), channel_id=1, source_target_pairs={{0,4},{1,5},{2,6},{3,7},{4,0},{5,1},{6,2},{7,3},{8,12},{9,13},{10,... | collective-permute-start | bytes 12296 | tf_op jit(solution)/shard_map/ppermute | solution.py:665
  105.8 2.0 %collective-permute-done.22 = f32[8,128]{1,0:T(8,128)S(1)} collective-permute-done((f32[8,128]{1,0:T(8,128)S(1)}, f32[8,128]{1,0:T(8,128)S(1)}, u32[]{:S(2)}, u32[]{:S(2)}) %collective-permute-start.22) | collective-permute-done | bytes 4128 | tf_op jit(solution)/shard_map/ppermute | solution.py:665
  107.8 1.2 %collective-permute-start.23 = (f32[8,128]{1,0:T(8,128)S(1)}, f32[8,128]{1,0:T(8,128)S(1)}, u32[]{:S(2)}, u32[]{:S(2)}) collective-permute-start(f32[8,128]{1,0:T(8,128)S(1)} %add.32), channel_id=1, source_target_pairs={{0,8},{1,9},{2,10},{3,11},{4,12},{5,13},{6,14},{7,15},{8,0},{9,1},... | collective-permute-start | bytes 12296 | tf_op jit(solution)/shard_map/ppermute | solution.py:665
  109.0 2.4 %collective-permute-done.23 = f32[8,128]{1,0:T(8,128)S(1)} collective-permute-done((f32[8,128]{1,0:T(8,128)S(1)}, f32[8,128]{1,0:T(8,128)S(1)}, u32[]{:S(2)}, u32[]{:S(2)}) %collective-permute-start.23) | collective-permute-done | bytes 4128 | tf_op jit(solution)/shard_map/ppermute | solution.py:665
  111.4 1.5 %collective-permute-start.24 = (f32[8,128]{1,0:T(8,128)S(1)}, f32[8,128]{1,0:T(8,128)S(1)}, u32[]{:S(2)}, u32[]{:S(2)}) collective-permute-start(f32[8,128]{1,0:T(8,128)S(1)} %add.34), channel_id=1, source_target_pairs={{0,16},{1,17},{2,18},{3,19},{4,20},{5,21},{6,22},{7,23},{8,24},{9,... | collective-permute-start | bytes 12296 | tf_op jit(solution)/shard_map/ppermute | solution.py:665
  112.9 2.1 %collective-permute-done.24 = f32[8,128]{1,0:T(8,128)S(1)} collective-permute-done((f32[8,128]{1,0:T(8,128)S(1)}, f32[8,128]{1,0:T(8,128)S(1)}, u32[]{:S(2)}, u32[]{:S(2)}) %collective-permute-start.24) | collective-permute-done | bytes 4128 | tf_op jit(solution)/shard_map/ppermute | solution.py:665
  115.0 0.6 select_add_fusion.later_ref
  115.6 1.5 %add_later.1 = f32[40,256]{1,0:T(8,128)} custom-call(f32[40,256]{1,0:T(8,128)} %copy-done.19, f32[8,128]{1,0:T(8,128)} %select_add_fusion.later_ref), custom_call_target="tpu_custom_call" | custom-call | flops 1 | bytes 1 | tf_op jit(solution)/shard_map/add_later/pallas_call | solution.py:637
  (56 shorter events, 0.1 us)
Async XLA Ops:
  5.1 4.2 %collective-permute-start = (f32[1288,128]{1,0:T(8,128)}, f32[1288,128]{1,0:T(8,128)S(1)}, u32[]{:S(2)}, u32[]{:S(2)}) collective-permute-start(f32[1288,128]{1,0:T(8,128)} %get-tuple-element.70), channel_id=1, source_target_pairs={{0,1},{1,0},{2,3},{3,2},{4,5},{5,4},{6,7},{7,6},{8,9},{9,8},{10,11... | collective-permute-start | bytes 1978376 | tf_op jit(solution)/shard_map/ppermute | solution.py:665
  5.6 3.7 %copy-start.12 = (f32[1280,128]{1,0:T(8,128)S(1)}, f32[1280,128]{1,0:T(8,128)}, u32[]{:S(2)}) copy-start(f32[1280,128]{1,0:T(8,128)} %get-tuple-element.71.refs_3_) | copy-start | bytes 1966084
  5.6 3.7 %copy-start.17 = (s32[3]{0:T(128)S(1)}, s32[3]{0:T(128)}, u32[]{:S(2)}) copy-start(s32[3]{0:T(128)} %pad_add_fusion.refs_0_.place) | copy-start | bytes 40
  5.6 3.7 %copy-start.18 = (f32[8,128]{1,0:T(8,128)S(1)}, f32[8,128]{1,0:T(8,128)}, u32[]{:S(2)}) copy-start(f32[8,128]{1,0:T(8,128)} %get-tuple-element.69.refs_1_.refs_5_) | copy-start | bytes 12292
  5.6 3.7 %copy-start.21 = (f32[10,128]{1,0:T(8,128)S(1)}, f32[10,128]{1,0:T(8,128)}, u32[]{:S(2)}) copy-start(f32[10,128]{1,0:T(8,128)} %get-tuple-element.72.refs_4_) | copy-start | bytes 15364
  9.2 21.0 %collective-permute-start.1 = (f32[1288,128]{1,0:T(8,128)}, f32[1288,128]{1,0:T(8,128)S(1)}, u32[]{:S(2)}, u32[]{:S(2)}) collective-permute-start(f32[1288,128]{1,0:T(8,128)} %get-tuple-element.79), channel_id=1, source_target_pairs={{0,1},{1,0},{2,3},{3,2},{4,5},{5,4},{6,7},{7,6},{8,9},{9,8},{10,11... | collective-permute-start | bytes 1978376 | tf_op jit(solution)/shard_map/ppermute | solution.py:665
  9.9 0.7 copy-start.9
  10.6 25.7 %collective-permute-start.2 = (f32[328,128]{1,0:T(8,128)S(1)}, f32[328,128]{1,0:T(8,128)S(1)}, u32[]{:S(2)}, u32[]{:S(2)}) collective-permute-start(f32[328,128]{1,0:T(8,128)S(1)} %get-tuple-element.83), channel_id=1, source_target_pairs={{0,2},{1,3},{2,0},{3,1},{4,6},{5,7},{6,4},{7,5},{8,10},{9,11},{10,... | collective-permute-start | bytes 503816 | tf_op jit(solution)/shard_map/ppermute | solution.py:665
  13.6 22.7 %collective-permute-start.3 = (f32[328,128]{1,0:T(8,128)S(1)}, f32[328,128]{1,0:T(8,128)S(1)}, u32[]{:S(2)}, u32[]{:S(2)}) collective-permute-start(f32[328,128]{1,0:T(8,128)S(1)} %get-tuple-element.84), channel_id=1, source_target_pairs={{0,4},{1,5},{2,6},{3,7},{4,0},{5,1},{6,2},{7,3},{8,12},{9,13},{10,... | collective-permute-start | bytes 503816 | tf_op jit(solution)/shard_map/ppermute | solution.py:665
  16.2 20.1 %collective-permute-start.4 = (f32[328,128]{1,0:T(8,128)S(1)}, f32[328,128]{1,0:T(8,128)S(1)}, u32[]{:S(2)}, u32[]{:S(2)}) collective-permute-start(f32[328,128]{1,0:T(8,128)S(1)} %get-tuple-element.85), channel_id=1, source_target_pairs={{0,6},{1,7},{2,4},{3,5},{4,2},{5,3},{6,0},{7,1},{8,14},{9,15},{10,... | collective-permute-start | bytes 503816 | tf_op jit(solution)/shard_map/ppermute | solution.py:665
  16.2 14.0 %copy-start.11 = (f32[1280,128]{1,0:T(8,128)S(1)}, f32[1280,128]{1,0:T(8,128)}, u32[]{:S(2)}) copy-start(f32[1280,128]{1,0:T(8,128)} %get-tuple-element.80.refs_3_) | copy-start | bytes 1966084
  16.2 14.0 %copy-start.20 = (f32[10,128]{1,0:T(8,128)S(1)}, f32[10,128]{1,0:T(8,128)}, u32[]{:S(2)}) copy-start(f32[10,128]{1,0:T(8,128)} %get-tuple-element.81.refs_4_) | copy-start | bytes 15364
  30.2 6.1 %copy-start.10 = (f32[328,128]{1,0:T(8,128)S(1)}, f32[328,128]{1,0:T(8,128)}, u32[]{:S(2)}) copy-start(f32[328,128]{1,0:T(8,128)} %copy-done.9) | copy-start | bytes 503812
  30.2 0.9 copy-start.13
  31.8 8.0 %collective-permute-start.5 = (f32[328,128]{1,0:T(8,128)S(1)}, f32[328,128]{1,0:T(8,128)S(1)}, u32[]{:S(2)}, u32[]{:S(2)}) collective-permute-start(f32[328,128]{1,0:T(8,128)S(1)} %get-tuple-element.86), channel_id=1, source_target_pairs={{0,2},{1,3},{2,0},{3,1},{4,6},{5,7},{6,4},{7,5},{8,10},{9,11},{10,... | collective-permute-start | bytes 503816 | tf_op jit(solution)/shard_map/ppermute | solution.py:665
  32.8 15.9 %collective-permute-start.6 = (f32[328,128]{1,0:T(8,128)S(1)}, f32[328,128]{1,0:T(8,128)S(1)}, u32[]{:S(2)}, u32[]{:S(2)}) collective-permute-start(f32[328,128]{1,0:T(8,128)S(1)} %get-tuple-element.87), channel_id=1, source_target_pairs={{0,4},{1,5},{2,6},{3,7},{4,0},{5,1},{6,2},{7,3},{8,12},{9,13},{10,... | collective-permute-start | bytes 503816 | tf_op jit(solution)/shard_map/ppermute | solution.py:665
  36.3 12.4 %collective-permute-start.7 = (f32[328,128]{1,0:T(8,128)S(1)}, f32[328,128]{1,0:T(8,128)S(1)}, u32[]{:S(2)}, u32[]{:S(2)}) collective-permute-start(f32[328,128]{1,0:T(8,128)S(1)} %get-tuple-element.88), channel_id=1, source_target_pairs={{0,6},{1,7},{2,4},{3,5},{4,2},{5,3},{6,0},{7,1},{8,14},{9,15},{10,... | collective-permute-start | bytes 503816 | tf_op jit(solution)/shard_map/ppermute | solution.py:665
  37.1 13.9 %collective-permute-start.8 = (f32[328,128]{1,0:T(8,128)S(1)}, f32[328,128]{1,0:T(8,128)S(1)}, u32[]{:S(2)}, u32[]{:S(2)}) collective-permute-start(f32[328,128]{1,0:T(8,128)S(1)} %group_total.2.refs_1_), channel_id=1, source_target_pairs={{0,8},{1,9},{2,10},{3,11},{4,12},{5,13},{6,14},{7,15},{8,0},{9,1},... | collective-permute-start | bytes 503816 | tf_op jit(solution)/shard_map/ppermute | solution.py:665
  49.5 5.4 %collective-permute-start.10 = (f32[328,128]{1,0:T(8,128)S(1)}, f32[328,128]{1,0:T(8,128)S(1)}, u32[]{:S(2)}, u32[]{:S(2)}) collective-permute-start(f32[328,128]{1,0:T(8,128)S(1)} %group_total.3.refs_1_), channel_id=1, source_target_pairs={{0,8},{1,9},{2,10},{3,11},{4,12},{5,13},{6,14},{7,15},{8,0},{9,1},... | collective-permute-start | bytes 503816 | tf_op jit(solution)/shard_map/ppermute | solution.py:665
  51.8 5.5 %collective-permute-start.9 = (f32[328,128]{1,0:T(8,128)S(1)}, f32[328,128]{1,0:T(8,128)S(1)}, u32[]{:S(2)}, u32[]{:S(2)}) collective-permute-start(f32[328,128]{1,0:T(8,128)S(1)} %join.2), channel_id=1, source_target_pairs={{0,16},{1,17},{2,18},{3,19},{4,20},{5,21},{6,22},{7,23},{8,24},{9,... | collective-permute-start | bytes 503816 | tf_op jit(solution)/shard_map/ppermute | solution.py:665
  54.9 25.8 %copy-start.16 = (f32[256,128]{1,0:T(8,128)S(1)}, f32[256,128]{1,0:T(8,128)}, u32[]{:S(2)}) copy-start(f32[256,128]{1,0:T(8,128)} %get-tuple-element.77.refs_8_) | copy-start | bytes 393220
  55.6 9.2 %collective-permute-start.11 = (f32[328,128]{1,0:T(8,128)S(1)}, f32[328,128]{1,0:T(8,128)S(1)}, u32[]{:S(2)}, u32[]{:S(2)}) collective-permute-start(f32[328,128]{1,0:T(8,128)S(1)} %join.3), channel_id=1, source_target_pairs={{0,16},{1,17},{2,18},{3,19},{4,20},{5,21},{6,22},{7,23},{8,24},{9,... | collective-permute-start | bytes 503816 | tf_op jit(solution)/shard_map/ppermute | solution.py:665
  57.2 22.0 %copy-start.4 = (f32[128,2560]{1,0:T(8,128)S(1)}, f32[128,2560]{1,0:T(8,128)}, u32[]{:S(2)}) copy-start(f32[128,2560]{1,0:T(8,128)} %get-tuple-element.92.refs_4_) | copy-start | bytes 3932164
  58.3 21.0 %copy-start.3 = (f32[128,2560]{1,0:T(8,128)S(1)}, f32[128,2560]{1,0:T(8,128)}, u32[]{:S(2)}) copy-start(f32[128,2560]{1,0:T(8,128)} %get-tuple-element.91.refs_3_) | copy-start | bytes 3932164
  58.3 9.7 %collective-permute-start.12 = (f32[320,128]{1,0:T(8,128)S(1)}, f32[320,128]{1,0:T(8,128)S(1)}, u32[]{:S(2)}, u32[]{:S(2)}) collective-permute-start(f32[320,128]{1,0:T(8,128)S(1)} %get-tuple-element.93), channel_id=1, source_target_pairs={{0,2},{1,3},{2,0},{3,1},{4,6},{5,7},{6,4},{7,5},{8,10},{9,11},{10,... | collective-permute-start | bytes 491528 | tf_op jit(solution)/shard_map/ppermute | solution.py:665
  62.4 11.0 %collective-permute-start.13 = (f32[320,128]{1,0:T(8,128)S(1)}, f32[320,128]{1,0:T(8,128)S(1)}, u32[]{:S(2)}, u32[]{:S(2)}) collective-permute-start(f32[320,128]{1,0:T(8,128)S(1)} %get-tuple-element.94), channel_id=1, source_target_pairs={{0,4},{1,5},{2,6},{3,7},{4,0},{5,1},{6,2},{7,3},{8,12},{9,13},{10,... | collective-permute-start | bytes 491528 | tf_op jit(solution)/shard_map/ppermute | solution.py:665
  63.3 10.1 %collective-permute-start.14 = (f32[320,128]{1,0:T(8,128)S(1)}, f32[320,128]{1,0:T(8,128)S(1)}, u32[]{:S(2)}, u32[]{:S(2)}) collective-permute-start(f32[320,128]{1,0:T(8,128)S(1)} %get-tuple-element.95), channel_id=1, source_target_pairs={{0,6},{1,7},{2,4},{3,5},{4,2},{5,3},{6,0},{7,1},{8,14},{9,15},{10,... | collective-permute-start | bytes 491528 | tf_op jit(solution)/shard_map/ppermute | solution.py:665
  73.4 7.3 %copy-start.2 = (f32[256,2560]{1,0:T(8,128)S(1)}, f32[256,2560]{1,0:T(8,128)}, u32[]{:S(2)}) copy-start(f32[256,2560]{1,0:T(8,128)} %get-tuple-element.75.refs_6_) | copy-start | bytes 7864324
  74.0 5.2 %collective-permute-start.15 = (f32[1280,128]{1,0:T(8,128)S(1)}, f32[1280,128]{1,0:T(8,128)S(1)}, u32[]{:S(2)}, u32[]{:S(2)}) collective-permute-start(f32[1280,128]{1,0:T(8,128)S(1)} %order.2.refs_5_), channel_id=1, source_target_pairs={{0,1},{1,0},{2,3},{3,2},{4,5},{5,4},{6,7},{7,6},{8,9},{9,8},{10,11... | collective-permute-start | bytes 1966088 | tf_op jit(solution)/shard_map/ppermute | solution.py:665
  74.1 10.8 %collective-permute-start.16 = (f32[320,128]{1,0:T(8,128)S(1)}, f32[320,128]{1,0:T(8,128)S(1)}, u32[]{:S(2)}, u32[]{:S(2)}) collective-permute-start(f32[320,128]{1,0:T(8,128)S(1)} %get-tuple-element.105), channel_id=1, source_target_pairs={{0,2},{1,3},{2,0},{3,1},{4,6},{5,7},{6,4},{7,5},{8,10},{9,11},{10,... | collective-permute-start | bytes 491528 | tf_op jit(solution)/shard_map/ppermute | solution.py:665
  76.5 15.0 %collective-permute-start.17 = (f32[320,128]{1,0:T(8,128)S(1)}, f32[320,128]{1,0:T(8,128)S(1)}, u32[]{:S(2)}, u32[]{:S(2)}) collective-permute-start(f32[320,128]{1,0:T(8,128)S(1)} %get-tuple-element.106), channel_id=1, source_target_pairs={{0,4},{1,5},{2,6},{3,7},{4,0},{5,1},{6,2},{7,3},{8,12},{9,13},{10,... | collective-permute-start | bytes 491528 | tf_op jit(solution)/shard_map/ppermute | solution.py:665
  77.9 13.6 %collective-permute-start.18 = (f32[320,128]{1,0:T(8,128)S(1)}, f32[320,128]{1,0:T(8,128)S(1)}, u32[]{:S(2)}, u32[]{:S(2)}) collective-permute-start(f32[320,128]{1,0:T(8,128)S(1)} %get-tuple-element.107), channel_id=1, source_target_pairs={{0,6},{1,7},{2,4},{3,5},{4,2},{5,3},{6,0},{7,1},{8,14},{9,15},{10,... | collective-permute-start | bytes 491528 | tf_op jit(solution)/shard_map/ppermute | solution.py:665
  79.3 1.4 %copy-start = (bf16[256,2560]{1,0:T(8,128)(2,1)S(1)}, bf16[256,2560]{1,0:T(8,128)(2,1)}, u32[]{:S(2)}) copy-start(bf16[256,2560]{1,0:T(8,128)(2,1)} %refs_0_.5) | copy-start | bytes 3932164
  79.3 1.7 %copy-start.1 = (bf16[256,2560]{1,0:T(8,128)(2,1)S(1)}, bf16[256,2560]{1,0:T(8,128)(2,1)}, u32[]{:S(2)}) copy-start(bf16[256,2560]{1,0:T(8,128)(2,1)} %refs_1_.11) | copy-start | bytes 3932164
  79.3 1.7 %copy-start.5 = (bf16[256,128]{1,0:T(8,128)(2,1)S(1)}, bf16[256,128]{1,0:T(8,128)(2,1)}, u32[]{:S(2)}) copy-start(bf16[256,128]{1,0:T(8,128)(2,1)} %refs_2_.11) | copy-start | bytes 196612
  79.3 1.7 %copy-start.6 = (bf16[256,128]{1,0:T(8,128)(2,1)S(1)}, bf16[256,128]{1,0:T(8,128)(2,1)}, u32[]{:S(2)}) copy-start(bf16[256,128]{1,0:T(8,128)(2,1)} %refs_3_.11) | copy-start | bytes 196612
  79.3 1.7 %copy-start.7 = (bf16[256,128]{1,0:T(8,128)(2,1)S(1)}, bf16[256,128]{1,0:T(8,128)(2,1)}, u32[]{:S(2)}) copy-start(bf16[256,128]{1,0:T(8,128)(2,1)} %get-tuple-element.67.refs_7_.refs_6_.refs_4_) | copy-start | bytes 196612
  79.3 1.7 %copy-start.8 = (bf16[256,128]{1,0:T(8,128)(2,1)S(1)}, bf16[256,128]{1,0:T(8,128)(2,1)}, u32[]{:S(2)}) copy-start(bf16[256,128]{1,0:T(8,128)(2,1)} %get-tuple-element.68.refs_8_.refs_7_.refs_5_) | copy-start | bytes 196612
  79.3 1.7 %copy-start.14 = (f32[256,128]{1,0:T(8,128)S(1)}, f32[256,128]{1,0:T(8,128)}, u32[]{:S(2)}) copy-start(f32[256,128]{1,0:T(8,128)} %get-tuple-element.78.refs_1_.refs_9_) | copy-start | bytes 393220
  79.3 1.7 %copy-start.15 = (f32[256,128]{1,0:T(8,128)S(1)}, f32[256,128]{1,0:T(8,128)}, u32[]{:S(2)}) copy-start(f32[256,128]{1,0:T(8,128)} %get-tuple-element.76.refs_7_) | copy-start | bytes 393220
  92.1 2.2 %collective-permute-start.19 = (f32[1280,128]{1,0:T(8,128)S(1)}, f32[1280,128]{1,0:T(8,128)S(1)}, u32[]{:S(2)}, u32[]{:S(2)}) collective-permute-start(f32[1280,128]{1,0:T(8,128)S(1)} %order.3.refs_5_), channel_id=1, source_target_pairs={{0,1},{1,0},{2,3},{3,2},{4,5},{5,4},{6,7},{7,6},{8,9},{9,8},{10,11... | collective-permute-start | bytes 1966088 | tf_op jit(solution)/shard_map/ppermute | solution.py:665
  95.6 2.0 %collective-permute-start.20 = (f32[8,128]{1,0:T(8,128)S(1)}, f32[8,128]{1,0:T(8,128)S(1)}, u32[]{:S(2)}, u32[]{:S(2)}) collective-permute-start(f32[8,128]{1,0:T(8,128)S(1)} %add.27), channel_id=1, source_target_pairs={{0,1},{1,0},{2,3},{3,2},{4,5},{5,4},{6,7},{7,6},{8,9},{9,8},{10,11... | collective-permute-start | bytes 12296 | tf_op jit(solution)/shard_map/ppermute | solution.py:665
  97.5 5.7 %collective-permute-start.21 = (f32[8,128]{1,0:T(8,128)S(1)}, f32[8,128]{1,0:T(8,128)S(1)}, u32[]{:S(2)}, u32[]{:S(2)}) collective-permute-start(f32[8,128]{1,0:T(8,128)S(1)} %add.28), channel_id=1, source_target_pairs={{0,2},{1,3},{2,0},{3,1},{4,6},{5,7},{6,4},{7,5},{8,10},{9,11},{10,... | collective-permute-start | bytes 12296 | tf_op jit(solution)/shard_map/ppermute | solution.py:665
  102.6 0.6 copy-start.19
  103.3 4.5 %collective-permute-start.22 = (f32[8,128]{1,0:T(8,128)S(1)}, f32[8,128]{1,0:T(8,128)S(1)}, u32[]{:S(2)}, u32[]{:S(2)}) collective-permute-start(f32[8,128]{1,0:T(8,128)S(1)} %add.30), channel_id=1, source_target_pairs={{0,4},{1,5},{2,6},{3,7},{4,0},{5,1},{6,2},{7,3},{8,12},{9,13},{10,... | collective-permute-start | bytes 12296 | tf_op jit(solution)/shard_map/ppermute | solution.py:665
  107.8 3.6 %collective-permute-start.23 = (f32[8,128]{1,0:T(8,128)S(1)}, f32[8,128]{1,0:T(8,128)S(1)}, u32[]{:S(2)}, u32[]{:S(2)}) collective-permute-start(f32[8,128]{1,0:T(8,128)S(1)} %add.32), channel_id=1, source_target_pairs={{0,8},{1,9},{2,10},{3,11},{4,12},{5,13},{6,14},{7,15},{8,0},{9,1},... | collective-permute-start | bytes 12296 | tf_op jit(solution)/shard_map/ppermute | solution.py:665
  111.4 3.6 %collective-permute-start.24 = (f32[8,128]{1,0:T(8,128)S(1)}, f32[8,128]{1,0:T(8,128)S(1)}, u32[]{:S(2)}, u32[]{:S(2)}) collective-permute-start(f32[8,128]{1,0:T(8,128)S(1)} %add.34), channel_id=1, source_target_pairs={{0,16},{1,17},{2,18},{3,19},{4,20},{5,21},{6,22},{7,23},{8,24},{9,... | collective-permute-start | bytes 12296 | tf_op jit(solution)/shard_map/ppermute | solution.py:665

commit v6 on v5

--- a/solution.py
+++ b/solution.py
@@ -244,38 +244,6 @@
     return jnp.where(place[0] == 1, chip, -chip)
 
 
-def is_ahead(place, bit):
-    return ((place[2] >> bit) & 1) == place[0]
-
-
-def join_kernel(bit, offset, strips, head_size, place, mine_ref, got_ref, out_ref):
-    size = mine_ref.shape[0] - META
-    part = size // strips
-    ahead = is_ahead(place, bit)
-    mine_log = mine_ref[size : size + 1, :]
-    got_log = got_ref[size : size + 1, :]
-    mine_row = jnp.where(ahead, 1.0, jnp.exp(got_log))
-    got_row = jnp.where(ahead, jnp.exp(mine_log), 1.0)
-    mine_wide, got_wide = spread_rows([mine_row, got_row], offset, strips, head_size)
-    for strip in range(strips):
-        rows = slice(strip * part, (strip + 1) * part)
-        one = slice(strip, strip + 1)
-        out_ref[rows, :] = mine_ref[rows, :] * mine_wide[one, :] + got_ref[rows, :] * got_wide[one, :]
-    out_ref[size:, :] = jnp.broadcast_to(mine_log + got_log, (META, STRIP))
-
-
-def join(half, bit, strips, head_size, place, mine, got):
-    return pl.pallas_call(
-        lambda *refs: join_kernel(bit, half * strips, strips, head_size, *refs),
-        in_specs=[SCALARS, whole(*mine.shape), whole(*got.shape)],
-        out_specs=whole(*mine.shape),
-        out_shape=jax.ShapeDtypeStruct(mine.shape, F32),
-        compiler_params=pltpu.CompilerParams(vmem_limit_bytes=SMALL_VMEM),
-        cost_estimate=LITTLE,
-        name="join",
-    )(place, mine, got)
-
-
 def masked_sum(terms):
     total = None
     for hit, value in terms:
@@ -328,10 +296,9 @@
     zero = jnp.zeros_like(logs[0])
     rows_of = []
     passed = zero
-    for bit, ref in enumerate(got_refs):
-        ahead = is_ahead(place, bit)
-        rows_of.append(jnp.where(ahead, jnp.exp(passed), 0.0))
-        passed = passed + jnp.where(ahead, ref[size : size + 1, :], 0.0)
+    for ref in got_refs:
+        rows_of.append(jnp.exp(passed))
+        passed = passed + ref[size : size + 1, :]
     for to in range(chips):
         rows_of.append(
             jnp.exp(masked_sum([(rank[m] < rank[to], logs[m]) for m in range(chips)]))
@@ -673,6 +640,13 @@
     def to_group(value, step):
         return move(value, lambda a, z, c: (a ^ step, z, c))
 
+    def to_later(value, step):
+        def target(a, z, c):
+            to = a + step if c == 1 else a - step
+            return (to, z, c) if 0 <= to < groups else None
+
+        return move(value, target)
+
     def hold(value, *tokens):
         return lax.optimization_barrier((value, tokens))[0]
 
@@ -685,34 +659,32 @@
     dx, db, dc, change, state_own, back_own = intra(pieces[0][0], *maps, log_decay, shared)
     pieces.append(combine(chips, place, change, first[1], keep, decay, shared[0]))
 
-    at, total, token = [], [], pieces[1][0]
-    for half in range(HALVES):
-        at.append([to_chip(value, step) for step, value in enumerate(pieces[half])])
-        total.append(group_total(half, head_size, place, token, at[half]))
-        token = total[half]
-    own = []
-    for half in range(HALVES):
-        block, got = total[half], []
-        for bit in range(bits):
-            got.append(to_group(block, 1 << bit))
-            if bit < bits - 1:
-                block = join(half, bit, strips, head_size, place, block, got[bit])
-        inside = enter(half, head_size, place, token, at[half], got)
-        token = inside[0]
-        own.append([to_chip(value, step) for step, value in enumerate(inside)])
-
-    own[0] = hold(own[0], token)
-
-    def entering(half, token):
-        mine = order(place, own[half])
+    def trade(values):
+        return [to_chip(value, step) for step, value in enumerate(values)]
+
+    def to_groups(half, token, at):
+        total = group_total(half, head_size, place, token, at)
+        return [to_later(total, step) for step in range(1, groups)]
+
+    at_a = trade(pieces[0])
+    at_b = trade(pieces[1])
+    got_a = to_groups(0, pieces[1][0], at_a)
+    got_a, at_b = lax.optimization_barrier((got_a, at_b))
+    own_a = trade(enter(0, head_size, place, change, at_a, got_a))
+    got_b = to_groups(1, change, at_b)
+    own_a, got_b = lax.optimization_barrier((own_a, got_b))
+    own_b = trade(enter(1, head_size, place, change, at_b, got_b))
+
+    def entering(half, token, own):
+        mine = order(place, own)
         return assemble(
             heads, chips, half, place, token, first[half], state_own, back_own, mine, to_core(mine)
         )
 
-    state, back, tally = entering(0, token)
+    state, back, tally = entering(0, change, own_a)
     grad, *sums = finish(heads, 0, STEPS, *maps, shared, dx, (db, dc, change), state, back, None)
-    own[1] = hold(own[1], sums[2])
-    state, back, tally_b = entering(1, sums[2])
+    own_b = hold(own_b, sums[2])
+    state, back, tally_b = entering(1, sums[2], own_b)
     tally = tally + tally_b
 
     def count(later, tally, got, bit, index):

time: 117 us -> 119 us (1.017)
  waiting for transfers between devices: 34.1 us -> 35.8 us
  Pallas kernels: 40.4 us -> 39 us
    ppermute x25 -> x27, waiting for transfers between devices: 34.1 us -> 35.8 us  [move(): return lax.ppermute(value, ('grp', 'seq'), pairs)]
    pallas_call x2 -> x0, Pallas kernels: 1.46 us -> none  [join(): pl.pallas_call(lambda *refs: join_kernel(bit, half * strips, strips, head...]
    ppermute x25 -> x27, starting transfers between devices: 37.8 us -> 38.5 us  [move(): return lax.ppermute(value, ('grp', 'seq'), pairs)]
  transfers between devices with their start and end apart: 25 -> 27, of which waited for: 10 -> 8; matrix products, arithmetic and copies ran while one was open for 0% -> 0% of each run, Pallas kernels for 28% -> 26%
where the time goes in v6:
time: 119 us; the launch traced here: 118 us
  Pallas kernels  39 us (33%)
  starting transfers between devices  38.5 us (32%)
  waiting for transfers between devices  35.8 us (30%)
  local copies, waits for them, and re-layouts  2.63 us (2%)
  other arithmetic  1.26 us (1%)
    ppermute x27, starting transfers between devices, move(): return lax.ppermute(value, ('grp', 'seq'), pairs)  38.5 us
    ppermute x27, waiting for transfers between devices, move(): return lax.ppermute(value, ('grp', 'seq'), pairs)  35.8 us
    pallas_call x1, Pallas kernels, intra(): pl.pallas_call(lambda *refs: intra_kernel(heads, *refs), grid=(wide // LA...  14.1 us
    pallas_call x3, Pallas kernels, finish(): pl.pallas_call(lambda *refs: finish_kernel(heads, start, steps, last, *re...  7.32 us
    pallas_call x2, Pallas kernels, summary(): pl.pallas_call(lambda *refs: summary_kernel(heads, chips, half, *refs), g...  7.32 us
    unnamed x44, local copies, waits for them, and re-layouts  2.63 us
    pallas_call x2, Pallas kernels, assemble(): pl.pallas_call(lambda *refs: assemble_kernel(heads, chips, half, wide //...  2.62 us
  transfers between devices with their start and end apart: 27, of which 8 were waited for; matrix products, arithmetic and copies ran while one was open for 0% of the time, Pallas kernels for 26%

profile of v6, /device:TPU:0, one launch (start us, length us, event | category | flops | bytes accessed | tf_op | source)
XLA Modules:
  0.0 118.2 jit_solution(9630213135660759024)
XLA Ops:
  0.6 0.6 pad_add_fusion.refs_0_.place
  1.3 3.8 %summary.2 = (f32[1288,128]{1,0:T(8,128)}, f32[1280,128]{1,0:T(8,128)}, f32[10,128]{1,0:T(8,128)}, f32[8,128]{1,0:T(8,128)}, f32[256,128]{1,0:T(8,128)}, /*index...) custom-call(s32[3]{0:T(128)} %pad_add_fusion.refs_0_.place, bf16[256,2560]{1,0:T(8,128)(2,1)} %refs_0_.5, ...), custom_call_target="tpu_custom_call" | custom-call | flops 1 | bytes 1 | tf_op jit(solution)/shard_map/summary/pallas_call | solution.py:187
  5.0 0.5 collective-permute-start
  5.6 3.6 %summary.3 = (f32[1288,128]{1,0:T(8,128)}, f32[1280,128]{1,0:T(8,128)}, f32[10,128]{1,0:T(8,128)}) custom-call(s32[3]{0:T(128)} %pad_add_fusion.refs_0_.place, bf16[256,2560]{1,0:T(8,128)(2,1)} %refs_0_.5, bf16[256,2560]{1,0:T(8,128)(2,1)} %refs_1_.11, bf16[256,128]{1,0:T(8,128)(2,1)} %refs_2_.11, bf16[256,128]{1,0:T(8,128)(2,1)} %refs_3_.11, ...), custom_call_target="tpu_custom_call" | custom-call | flops 1 | bytes 1 | tf_op jit(solution)/shard_map/summary/pallas_call | solution.py:187
  9.1 0.1 collective-permute-start.4
  9.2 0.7 combine.2
  9.9 0.7 copy-done.11
  10.6 3.0 %collective-permute-start.1 = (f32[328,128]{1,0:T(8,128)S(1)}, f32[328,128]{1,0:T(8,128)S(1)}, u32[]{:S(2)}, u32[]{:S(2)}) collective-permute-start(f32[328,128]{1,0:T(8,128)S(1)} %get-tuple-element.91), channel_id=1, source_target_pairs={{0,2},{1,3},{2,0},{3,1},{4,6},{5,7},{6,4},{7,5},{8,10},{9,11},{10,... | collective-permute-start | bytes 503816 | tf_op jit(solution)/shard_map/ppermute | solution.py:632
  13.6 2.6 %collective-permute-start.2 = (f32[328,128]{1,0:T(8,128)S(1)}, f32[328,128]{1,0:T(8,128)S(1)}, u32[]{:S(2)}, u32[]{:S(2)}) collective-permute-start(f32[328,128]{1,0:T(8,128)S(1)} %get-tuple-element.92), channel_id=1, source_target_pairs={{0,4},{1,5},{2,6},{3,7},{4,0},{5,1},{6,2},{7,3},{8,12},{9,13},{10,... | collective-permute-start | bytes 503816 | tf_op jit(solution)/shard_map/ppermute | solution.py:632
  16.2 14.1 %intra.1 = (f32[256,2560]{1,0:T(8,128)}, f32[256,128]{1,0:T(8,128)}, f32[256,128]{1,0:T(8,128)}, f32[256,128]{1,0:T(8,128)}, f32[128,2560]{1,0:T(8,128)}, /*index=5*/f32[128,2560]{1,0:T(8,128)}) custom-call(f32[328,128]{1,0:T(8,128)} %copy-done.11, bf16[256,2560]{1,0:T(8,128)(2,1)} %refs_0_.5, bf16[256,2560]{1,0:T(8,128)(2,1)} %refs_1_.11, ...), custom_call_target="tpu_custom_call" | custom-call | flops 1 | bytes 1 | tf_op jit(solution)/shard_map/intra/pallas_call | solution.py:413
  30.3 0.9 copy-done.5
  31.2 0.6 combine.3
  31.9 0.9 collective-permute-start.8
  32.8 3.5 %collective-permute-start.9 = (f32[328,128]{1,0:T(8,128)S(1)}, f32[328,128]{1,0:T(8,128)S(1)}, u32[]{:S(2)}, u32[]{:S(2)}) collective-permute-start(f32[328,128]{1,0:T(8,128)S(1)} %get-tuple-element.99), channel_id=1, source_target_pairs={{0,4},{1,5},{2,6},{3,7},{4,0},{5,1},{6,2},{7,3},{8,12},{9,13},{10,... | collective-permute-start | bytes 503816 | tf_op jit(solution)/shard_map/ppermute | solution.py:632
  36.3 0.0 collective-permute-start.10
  36.3 0.8 group_total.2
  37.1 1.3 %collective-permute-start.7 = (f32[328,128]{1,0:T(8,128)S(1)}, f32[328,128]{1,0:T(8,128)S(1)}, u32[]{:S(2)}, u32[]{:S(2)}) collective-permute-start(f32[328,128]{1,0:T(8,128)S(1)} %group_total.2), channel_id=1, source_target_pairs={{1,25},{3,27},{5,29},{7,31},{24,0},{26,2},{28,4},{30,6}} | collective-permute-start | bytes 503816 | tf_op jit(solution)/shard_map/ppermute | solution.py:632
  38.4 1.3 %collective-permute-start.6 = (f32[328,128]{1,0:T(8,128)S(1)}, f32[328,128]{1,0:T(8,128)S(1)}, u32[]{:S(2)}, u32[]{:S(2)}) collective-permute-start(f32[328,128]{1,0:T(8,128)S(1)} %group_total.2), channel_id=1, source_target_pairs={{1,17},{3,19},{5,21},{7,23},{9,25},{11,27},{13,29},{15,31},{16,0},... | collective-permute-start | bytes 503816 | tf_op jit(solution)/shard_map/ppermute | solution.py:632
  39.7 0.1 collective-permute-done.8.refs_3_
  39.9 1.3 %collective-permute-start.5 = (f32[328,128]{1,0:T(8,128)S(1)}, f32[328,128]{1,0:T(8,128)S(1)}, u32[]{:S(2)}, u32[]{:S(2)}) collective-permute-start(f32[328,128]{1,0:T(8,128)S(1)} %group_total.2), channel_id=1, source_target_pairs={{1,9},{3,11},{5,13},{7,15},{8,0},{9,17},{10,2},{11,19},{12,4},{13,... | collective-permute-start | bytes 503816 | tf_op jit(solution)/shard_map/ppermute | solution.py:632
  41.1 7.5 %collective-permute-done.9.refs_4_ = f32[328,128]{1,0:T(8,128)S(1)} collective-permute-done((f32[328,128]{1,0:T(8,128)S(1)}, f32[328,128]{1,0:T(8,128)S(1)}, u32[]{:S(2)}, u32[]{:S(2)}) %collective-permute-start.9) | collective-permute-done | bytes 167968 | tf_op jit(solution)/shard_map/ppermute | solution.py:632
  48.7 1.0 enter.2
  49.8 2.4 %collective-permute-start.11 = (f32[320,128]{1,0:T(8,128)S(1)}, f32[320,128]{1,0:T(8,128)S(1)}, u32[]{:S(2)}, u32[]{:S(2)}) collective-permute-start(f32[320,128]{1,0:T(8,128)S(1)} %get-tuple-element.105), channel_id=1, source_target_pairs={{0,2},{1,3},{2,0},{3,1},{4,6},{5,7},{6,4},{7,5},{8,10},{9,11},{10,... | collective-permute-start | bytes 491528 | tf_op jit(solution)/shard_map/ppermute | solution.py:632
  52.2 0.8 group_total.3
  53.0 1.3 %collective-permute-start.16 = (f32[328,128]{1,0:T(8,128)S(1)}, f32[328,128]{1,0:T(8,128)S(1)}, u32[]{:S(2)}, u32[]{:S(2)}) collective-permute-start(f32[328,128]{1,0:T(8,128)S(1)} %group_total.3), channel_id=1, source_target_pairs={{1,25},{3,27},{5,29},{7,31},{24,0},{26,2},{28,4},{30,6}} | collective-permute-start | bytes 503816 | tf_op jit(solution)/shard_map/ppermute | solution.py:632
  54.3 1.3 %collective-permute-start.15 = (f32[328,128]{1,0:T(8,128)S(1)}, f32[328,128]{1,0:T(8,128)S(1)}, u32[]{:S(2)}, u32[]{:S(2)}) collective-permute-start(f32[328,128]{1,0:T(8,128)S(1)} %group_total.3), channel_id=1, source_target_pairs={{1,17},{3,19},{5,21},{7,23},{9,25},{11,27},{13,29},{15,31},{16,0},... | collective-permute-start | bytes 503816 | tf_op jit(solution)/shard_map/ppermute | solution.py:632
  55.6 1.5 %collective-permute-start.14 = (f32[328,128]{1,0:T(8,128)S(1)}, f32[328,128]{1,0:T(8,128)S(1)}, u32[]{:S(2)}, u32[]{:S(2)}) collective-permute-start(f32[328,128]{1,0:T(8,128)S(1)} %group_total.3), channel_id=1, source_target_pairs={{1,9},{3,11},{5,13},{7,15},{8,0},{9,17},{10,2},{11,19},{12,4},{13,... | collective-permute-start | bytes 503816 | tf_op jit(solution)/shard_map/ppermute | solution.py:632
  57.1 1.1 collective-permute-start.12
  58.2 1.5 %collective-permute-start.13 = (f32[320,128]{1,0:T(8,128)S(1)}, f32[320,128]{1,0:T(8,128)S(1)}, u32[]{:S(2)}, u32[]{:S(2)}) collective-permute-start(f32[320,128]{1,0:T(8,128)S(1)} %get-tuple-element.107), channel_id=1, source_target_pairs={{0,6},{1,7},{2,4},{3,5},{4,2},{5,3},{6,0},{7,1},{8,14},{9,15},{10,... | collective-permute-start | bytes 491528 | tf_op jit(solution)/shard_map/ppermute | solution.py:632
  59.6 11.9 %collective-permute-done.12.refs_2_ = f32[320,128]{1,0:T(8,128)S(1)} collective-permute-done((f32[320,128]{1,0:T(8,128)S(1)}, f32[320,128]{1,0:T(8,128)S(1)}, u32[]{:S(2)}, u32[]{:S(2)}) %collective-permute-start.12) | collective-permute-done | bytes 163872 | tf_op jit(solution)/shard_map/ppermute | solution.py:632
  71.6 0.0 copy-start.3
  71.6 0.6 order.2.refs_5_
  72.2 0.2 collective-permute-start.17
  72.4 1.0 enter.3
  73.4 4.1 %collective-permute-start.18 = (f32[320,128]{1,0:T(8,128)S(1)}, f32[320,128]{1,0:T(8,128)S(1)}, u32[]{:S(2)}, u32[]{:S(2)}) collective-permute-start(f32[320,128]{1,0:T(8,128)S(1)} %get-tuple-element.125), channel_id=1, source_target_pairs={{0,2},{1,3},{2,0},{3,1},{4,6},{5,7},{6,4},{7,5},{8,10},{9,11},{10,... | collective-permute-start | bytes 491528 | tf_op jit(solution)/shard_map/ppermute | solution.py:632
  77.5 1.0 collective-permute-start.19
  78.6 1.4 %collective-permute-start.20 = (f32[320,128]{1,0:T(8,128)S(1)}, f32[320,128]{1,0:T(8,128)S(1)}, u32[]{:S(2)}, u32[]{:S(2)}) collective-permute-start(f32[320,128]{1,0:T(8,128)S(1)} %get-tuple-element.127), channel_id=1, source_target_pairs={{0,6},{1,7},{2,4},{3,5},{4,2},{5,3},{6,0},{7,1},{8,14},{9,15},{10,... | collective-permute-start | bytes 491528 | tf_op jit(solution)/shard_map/ppermute | solution.py:632
  80.0 0.0 copy-start
  80.0 0.0 copy-start.1
  80.0 0.0 copy-start.8
  80.0 0.0 copy-start.9
  80.1 1.3 %assemble.2 = (bf16[128,1280]{1,0:T(8,128)(2,1)S(1)}, bf16[128,1280]{1,0:T(8,128)(2,1)S(1)}, f32[8,128]{1,0:T(8,128)S(1)}) custom-call(s32[3]{0:T(128)S(1)} %copy-done.17, f32[256,128]{1,0:T(8,128)S(1)} %copy-done.6, f32[1288,128]{1,0:T(8,128)S(1)} %collective-permute-done.refs_2_, f32[128,2560]{1,0:T(8,128)S(1)} %copy-done.3, f32[128,2560]{1,0:T(8,128)S(1)} %copy-done.4, ...), custom_call_target="tpu_custom_call" | custom-call | flops 1 | bytes 1 | tf_op jit(solution)/shard_map/assemble/pallas_call | solution.py:507
  81.4 0.0 copy-done
  81.4 0.3 copy-done.1
  81.7 0.0 copy-done.15
  81.8 3.8 %finish.3 = (bf16[256,2560]{1,0:T(8,128)(2,1)}, f32[256,128]{1,0:T(8,128)S(1)}, f32[256,128]{1,0:T(8,128)S(1)}, f32[256,128]{1,0:T(8,128)S(1)}) custom-call(bf16[256,2560]{1,0:T(8,128)(2,1)S(1)} %copy-done, bf16[256,2560]{1,0:T(8,128)(2,1)S(1)} %copy-done.1, bf16[256,128]{1,0:T(8,128)(2,1)S(1)} %copy-done.7, bf16[256,128]{1,0:T(8,128)(2,1)S(1)} %copy-done.8, ...), custom_call_target="tpu_custom_call" | custom-call | flops 1 | bytes 1 | tf_op jit(solution)/shard_map/finish/pallas_call | solution.py:574
  85.5 7.0 %collective-permute-done.19.refs_2_ = f32[320,128]{1,0:T(8,128)S(1)} collective-permute-done((f32[320,128]{1,0:T(8,128)S(1)}, f32[320,128]{1,0:T(8,128)S(1)}, u32[]{:S(2)}, u32[]{:S(2)}) %collective-permute-start.19) | collective-permute-done | bytes 163872 | tf_op jit(solution)/shard_map/ppermute | solution.py:632
  92.6 0.6 order.3.refs_5_
  93.1 0.1 collective-permute-start.21
  93.2 2.1 %collective-permute-done.21.refs_6_ = f32[1280,128]{1,0:T(8,128)S(1)} collective-permute-done((f32[1280,128]{1,0:T(8,128)S(1)}, f32[1280,128]{1,0:T(8,128)S(1)}, u32[]{:S(2)}, u32[]{:S(2)}) %collective-permute-start.21) | collective-permute-done | bytes 655392 | tf_op jit(solution)/shard_map/ppermute | solution.py:632
  95.3 1.3 %assemble.3 = (bf16[128,1280]{1,0:T(8,128)(2,1)S(1)}, bf16[128,1280]{1,0:T(8,128)(2,1)S(1)}, f32[8,128]{1,0:T(8,128)S(1)}) custom-call(s32[3]{0:T(128)S(1)} %copy-done.17, f32[256,128]{1,0:T(8,128)S(1)} %get-tuple-element.120.refs_1_.refs_9_, f32[1288,128]{1,0:T(8,128)S(1)} %collective-permute-done.4.refs_2_, f32[128,2560]{1,0:T(8,128)S(1)} %copy-done.3, ...), custom_call_target="tpu_custom_call" | custom-call | flops 1 | bytes 1 | tf_op jit(solution)/shard_map/assemble/pallas_call | solution.py:507
  96.6 0.2 collective-permute-start.22
  96.8 1.8 %finish.4 = (bf16[256,2560]{1,0:T(8,128)(2,1)}, f32[256,128]{1,0:T(8,128)S(1)}, f32[256,128]{1,0:T(8,128)S(1)}, f32[256,128]{1,0:T(8,128)S(1)}) custom-call(bf16[256,2560]{1,0:T(8,128)(2,1)S(1)} %copy-done, bf16[256,2560]{1,0:T(8,128)(2,1)S(1)} %copy-done.1, bf16[256,128]{1,0:T(8,128)(2,1)S(1)} %copy-done.7, ...), custom_call_target="tpu_custom_call", output_to_operand_aliasing={{0}: (12, {})} | custom-call | flops 1 | bytes 1 | tf_op jit(solution)/shard_map/finish/pallas_call | solution.py:574
  98.6 3.3 %collective-permute-start.23 = (f32[8,128]{1,0:T(8,128)S(1)}, f32[8,128]{1,0:T(8,128)S(1)}, u32[]{:S(2)}, u32[]{:S(2)}) collective-permute-start(f32[8,128]{1,0:T(8,128)S(1)} %add.28), channel_id=1, source_target_pairs={{0,2},{1,3},{2,0},{3,1},{4,6},{5,7},{6,4},{7,5},{8,10},{9,11},{10,... | collective-permute-start | bytes 12296 | tf_op jit(solution)/shard_map/ppermute | solution.py:632
  101.9 1.8 %finish.5 = (bf16[256,2560]{1,0:T(8,128)(2,1)}, bf16[256,128]{1,0:T(8,128)(2,1)}, bf16[256,128]{1,0:T(8,128)(2,1)}, f32[40,256]{1,0:T(8,128)S(1)}) custom-call(bf16[256,2560]{1,0:T(8,128)(2,1)S(1)} %copy-done, bf16[256,2560]{1,0:T(8,128)(2,1)S(1)} %copy-done.1, bf16[256,128]{1,0:T(8,128)(2,1)S(1)} %copy-done.7, ...), custom_call_target="tpu_custom_call", output_to_operand_aliasing={{0}: (12, {})} | custom-call | flops 1 | bytes 1 | tf_op jit(solution)/shard_map/finish/pallas_call | solution.py:574
  103.7 0.6 copy-done.19
  104.4 2.1 %collective-permute-start.24 = (f32[8,128]{1,0:T(8,128)S(1)}, f32[8,128]{1,0:T(8,128)S(1)}, u32[]{:S(2)}, u32[]{:S(2)}) collective-permute-start(f32[8,128]{1,0:T(8,128)S(1)} %add.30), channel_id=1, source_target_pairs={{0,4},{1,5},{2,6},{3,7},{4,0},{5,1},{6,2},{7,3},{8,12},{9,13},{10,... | collective-permute-start | bytes 12296 | tf_op jit(solution)/shard_map/ppermute | solution.py:632
  106.5 2.4 %collective-permute-done.24 = f32[8,128]{1,0:T(8,128)S(1)} collective-permute-done((f32[8,128]{1,0:T(8,128)S(1)}, f32[8,128]{1,0:T(8,128)S(1)}, u32[]{:S(2)}, u32[]{:S(2)}) %collective-permute-start.24) | collective-permute-done | bytes 4128 | tf_op jit(solution)/shard_map/ppermute | solution.py:632
  108.9 1.6 %collective-permute-start.25 = (f32[8,128]{1,0:T(8,128)S(1)}, f32[8,128]{1,0:T(8,128)S(1)}, u32[]{:S(2)}, u32[]{:S(2)}) collective-permute-start(f32[8,128]{1,0:T(8,128)S(1)} %add.32), channel_id=1, source_target_pairs={{0,8},{1,9},{2,10},{3,11},{4,12},{5,13},{6,14},{7,15},{8,0},{9,1},... | collective-permute-start | bytes 12296 | tf_op jit(solution)/shard_map/ppermute | solution.py:632
  110.4 2.0 %collective-permute-done.25 = f32[8,128]{1,0:T(8,128)S(1)} collective-permute-done((f32[8,128]{1,0:T(8,128)S(1)}, f32[8,128]{1,0:T(8,128)S(1)}, u32[]{:S(2)}, u32[]{:S(2)}) %collective-permute-start.25) | collective-permute-done | bytes 4128 | tf_op jit(solution)/shard_map/ppermute | solution.py:632
  112.5 0.9 collective-permute-start.26
  113.4 2.7 %collective-permute-done.26 = f32[8,128]{1,0:T(8,128)S(1)} collective-permute-done((f32[8,128]{1,0:T(8,128)S(1)}, f32[8,128]{1,0:T(8,128)S(1)}, u32[]{:S(2)}, u32[]{:S(2)}) %collective-permute-start.26) | collective-permute-done | bytes 4128 | tf_op jit(solution)/shard_map/ppermute | solution.py:632
  116.1 0.6 select_add_fusion.later_ref
  116.7 1.5 %add_later.1 = f32[40,256]{1,0:T(8,128)} custom-call(f32[40,256]{1,0:T(8,128)} %copy-done.19, f32[8,128]{1,0:T(8,128)} %select_add_fusion.later_ref), custom_call_target="tpu_custom_call" | custom-call | flops 1 | bytes 1 | tf_op jit(solution)/shard_map/add_later/pallas_call | solution.py:604
  (58 shorter events, 0.1 us)
Async XLA Ops:
  5.0 4.2 %collective-permute-start = (f32[1288,128]{1,0:T(8,128)}, f32[1288,128]{1,0:T(8,128)S(1)}, u32[]{:S(2)}, u32[]{:S(2)}) collective-permute-start(f32[1288,128]{1,0:T(8,128)} %get-tuple-element.80), channel_id=1, source_target_pairs={{0,1},{1,0},{2,3},{3,2},{4,5},{5,4},{6,7},{7,6},{8,9},{9,8},{10,11... | collective-permute-start | bytes 1978376 | tf_op jit(solution)/shard_map/ppermute | solution.py:632
  5.6 3.6 %copy-start.14 = (f32[1280,128]{1,0:T(8,128)S(1)}, f32[1280,128]{1,0:T(8,128)}, u32[]{:S(2)}) copy-start(f32[1280,128]{1,0:T(8,128)} %get-tuple-element.81.refs_3_) | copy-start | bytes 1966084
  5.6 3.6 %copy-start.17 = (s32[3]{0:T(128)S(1)}, s32[3]{0:T(128)}, u32[]{:S(2)}) copy-start(s32[3]{0:T(128)} %pad_add_fusion.refs_0_.place) | copy-start | bytes 40
  5.6 3.6 %copy-start.18 = (f32[8,128]{1,0:T(8,128)S(1)}, f32[8,128]{1,0:T(8,128)}, u32[]{:S(2)}) copy-start(f32[8,128]{1,0:T(8,128)} %get-tuple-element.79.refs_1_.refs_5_) | copy-start | bytes 12292
  5.6 3.6 %copy-start.21 = (f32[10,128]{1,0:T(8,128)S(1)}, f32[10,128]{1,0:T(8,128)}, u32[]{:S(2)}) copy-start(f32[10,128]{1,0:T(8,128)} %get-tuple-element.82.refs_4_) | copy-start | bytes 15364
  9.1 21.2 %collective-permute-start.4 = (f32[1288,128]{1,0:T(8,128)}, f32[1288,128]{1,0:T(8,128)S(1)}, u32[]{:S(2)}, u32[]{:S(2)}) collective-permute-start(f32[1288,128]{1,0:T(8,128)} %get-tuple-element.94), channel_id=1, source_target_pairs={{0,1},{1,0},{2,3},{3,2},{4,5},{5,4},{6,7},{7,6},{8,9},{9,8},{10,11... | collective-permute-start | bytes 1978376 | tf_op jit(solution)/shard_map/ppermute | solution.py:632
  9.9 0.7 copy-start.11
  10.6 25.7 %collective-permute-start.1 = (f32[328,128]{1,0:T(8,128)S(1)}, f32[328,128]{1,0:T(8,128)S(1)}, u32[]{:S(2)}, u32[]{:S(2)}) collective-permute-start(f32[328,128]{1,0:T(8,128)S(1)} %get-tuple-element.91), channel_id=1, source_target_pairs={{0,2},{1,3},{2,0},{3,1},{4,6},{5,7},{6,4},{7,5},{8,10},{9,11},{10,... | collective-permute-start | bytes 503816 | tf_op jit(solution)/shard_map/ppermute | solution.py:632
  13.6 22.7 %collective-permute-start.2 = (f32[328,128]{1,0:T(8,128)S(1)}, f32[328,128]{1,0:T(8,128)S(1)}, u32[]{:S(2)}, u32[]{:S(2)}) collective-permute-start(f32[328,128]{1,0:T(8,128)S(1)} %get-tuple-element.92), channel_id=1, source_target_pairs={{0,4},{1,5},{2,6},{3,7},{4,0},{5,1},{6,2},{7,3},{8,12},{9,13},{10,... | collective-permute-start | bytes 503816 | tf_op jit(solution)/shard_map/ppermute | solution.py:632
  16.2 20.2 %collective-permute-start.3 = (f32[328,128]{1,0:T(8,128)S(1)}, f32[328,128]{1,0:T(8,128)S(1)}, u32[]{:S(2)}, u32[]{:S(2)}) collective-permute-start(f32[328,128]{1,0:T(8,128)S(1)} %get-tuple-element.93), channel_id=1, source_target_pairs={{0,6},{1,7},{2,4},{3,5},{4,2},{5,3},{6,0},{7,1},{8,14},{9,15},{10,... | collective-permute-start | bytes 503816 | tf_op jit(solution)/shard_map/ppermute | solution.py:632
  16.2 14.1 %copy-start.13 = (f32[1280,128]{1,0:T(8,128)S(1)}, f32[1280,128]{1,0:T(8,128)}, u32[]{:S(2)}) copy-start(f32[1280,128]{1,0:T(8,128)} %get-tuple-element.95.refs_3_) | copy-start | bytes 1966084
  16.2 14.1 %copy-start.20 = (f32[10,128]{1,0:T(8,128)S(1)}, f32[10,128]{1,0:T(8,128)}, u32[]{:S(2)}) copy-start(f32[10,128]{1,0:T(8,128)} %get-tuple-element.96.refs_4_) | copy-start | bytes 15364
  16.2 20.2 %copy-start.12 = (f32[328,128]{1,0:T(8,128)S(1)}, f32[328,128]{1,0:T(8,128)}, u32[]{:S(2)}) copy-start(f32[328,128]{1,0:T(8,128)} %copy-done.11) | copy-start | bytes 503812
  30.3 0.9 copy-start.5
  31.2 17.5 %copy-start.6 = (f32[256,128]{1,0:T(8,128)S(1)}, f32[256,128]{1,0:T(8,128)}, u32[]{:S(2)}) copy-start(f32[256,128]{1,0:T(8,128)} %get-tuple-element.88.refs_1_.refs_9_) | copy-start | bytes 393220
  31.9 8.0 %collective-permute-start.8 = (f32[328,128]{1,0:T(8,128)S(1)}, f32[328,128]{1,0:T(8,128)S(1)}, u32[]{:S(2)}, u32[]{:S(2)}) collective-permute-start(f32[328,128]{1,0:T(8,128)S(1)} %get-tuple-element.98), channel_id=1, source_target_pairs={{0,2},{1,3},{2,0},{3,1},{4,6},{5,7},{6,4},{7,5},{8,10},{9,11},{10,... | collective-permute-start | bytes 503816 | tf_op jit(solution)/shard_map/ppermute | solution.py:632
  32.8 15.9 %collective-permute-start.9 = (f32[328,128]{1,0:T(8,128)S(1)}, f32[328,128]{1,0:T(8,128)S(1)}, u32[]{:S(2)}, u32[]{:S(2)}) collective-permute-start(f32[328,128]{1,0:T(8,128)S(1)} %get-tuple-element.99), channel_id=1, source_target_pairs={{0,4},{1,5},{2,6},{3,7},{4,0},{5,1},{6,2},{7,3},{8,12},{9,13},{10,... | collective-permute-start | bytes 503816 | tf_op jit(solution)/shard_map/ppermute | solution.py:632
  36.3 12.4 %collective-permute-start.10 = (f32[328,128]{1,0:T(8,128)S(1)}, f32[328,128]{1,0:T(8,128)S(1)}, u32[]{:S(2)}, u32[]{:S(2)}) collective-permute-start(f32[328,128]{1,0:T(8,128)S(1)} %get-tuple-element.100), channel_id=1, source_target_pairs={{0,6},{1,7},{2,4},{3,5},{4,2},{5,3},{6,0},{7,1},{8,14},{9,15},{10,... | collective-permute-start | bytes 503816 | tf_op jit(solution)/shard_map/ppermute | solution.py:632
  37.1 11.6 %collective-permute-start.7 = (f32[328,128]{1,0:T(8,128)S(1)}, f32[328,128]{1,0:T(8,128)S(1)}, u32[]{:S(2)}, u32[]{:S(2)}) collective-permute-start(f32[328,128]{1,0:T(8,128)S(1)} %group_total.2), channel_id=1, source_target_pairs={{1,25},{3,27},{5,29},{7,31},{24,0},{26,2},{28,4},{30,6}} | collective-permute-start | bytes 503816 | tf_op jit(solution)/shard_map/ppermute | solution.py:632
  38.4 10.3 %collective-permute-start.6 = (f32[328,128]{1,0:T(8,128)S(1)}, f32[328,128]{1,0:T(8,128)S(1)}, u32[]{:S(2)}, u32[]{:S(2)}) collective-permute-start(f32[328,128]{1,0:T(8,128)S(1)} %group_total.2), channel_id=1, source_target_pairs={{1,17},{3,19},{5,21},{7,23},{9,25},{11,27},{13,29},{15,31},{16,0},... | collective-permute-start | bytes 503816 | tf_op jit(solution)/shard_map/ppermute | solution.py:632
  39.9 8.8 %collective-permute-start.5 = (f32[328,128]{1,0:T(8,128)S(1)}, f32[328,128]{1,0:T(8,128)S(1)}, u32[]{:S(2)}, u32[]{:S(2)}) collective-permute-start(f32[328,128]{1,0:T(8,128)S(1)} %group_total.2), channel_id=1, source_target_pairs={{1,9},{3,11},{5,13},{7,15},{8,0},{9,17},{10,2},{11,19},{12,4},{13,... | collective-permute-start | bytes 503816 | tf_op jit(solution)/shard_map/ppermute | solution.py:632
  48.7 32.7 %copy-start.16 = (f32[256,128]{1,0:T(8,128)S(1)}, f32[256,128]{1,0:T(8,128)}, u32[]{:S(2)}) copy-start(f32[256,128]{1,0:T(8,128)} %get-tuple-element.87.refs_8_) | copy-start | bytes 393220
  49.8 8.4 %collective-permute-start.11 = (f32[320,128]{1,0:T(8,128)S(1)}, f32[320,128]{1,0:T(8,128)S(1)}, u32[]{:S(2)}, u32[]{:S(2)}) collective-permute-start(f32[320,128]{1,0:T(8,128)S(1)} %get-tuple-element.105), channel_id=1, source_target_pairs={{0,2},{1,3},{2,0},{3,1},{4,6},{5,7},{6,4},{7,5},{8,10},{9,11},{10,... | collective-permute-start | bytes 491528 | tf_op jit(solution)/shard_map/ppermute | solution.py:632
  52.2 27.8 %copy-start.4 = (f32[128,2560]{1,0:T(8,128)S(1)}, f32[128,2560]{1,0:T(8,128)}, u32[]{:S(2)}) copy-start(f32[128,2560]{1,0:T(8,128)} %get-tuple-element.90.refs_4_) | copy-start | bytes 3932164
  53.0 18.6 %collective-permute-start.16 = (f32[328,128]{1,0:T(8,128)S(1)}, f32[328,128]{1,0:T(8,128)S(1)}, u32[]{:S(2)}, u32[]{:S(2)}) collective-permute-start(f32[328,128]{1,0:T(8,128)S(1)} %group_total.3), channel_id=1, source_target_pairs={{1,25},{3,27},{5,29},{7,31},{24,0},{26,2},{28,4},{30,6}} | collective-permute-start | bytes 503816 | tf_op jit(solution)/shard_map/ppermute | solution.py:632
  54.3 17.3 %collective-permute-start.15 = (f32[328,128]{1,0:T(8,128)S(1)}, f32[328,128]{1,0:T(8,128)S(1)}, u32[]{:S(2)}, u32[]{:S(2)}) collective-permute-start(f32[328,128]{1,0:T(8,128)S(1)} %group_total.3), channel_id=1, source_target_pairs={{1,17},{3,19},{5,21},{7,23},{9,25},{11,27},{13,29},{15,31},{16,0},... | collective-permute-start | bytes 503816 | tf_op jit(solution)/shard_map/ppermute | solution.py:632
  55.6 16.0 %collective-permute-start.14 = (f32[328,128]{1,0:T(8,128)S(1)}, f32[328,128]{1,0:T(8,128)S(1)}, u32[]{:S(2)}, u32[]{:S(2)}) collective-permute-start(f32[328,128]{1,0:T(8,128)S(1)} %group_total.3), channel_id=1, source_target_pairs={{1,9},{3,11},{5,13},{7,15},{8,0},{9,17},{10,2},{11,19},{12,4},{13,... | collective-permute-start | bytes 503816 | tf_op jit(solution)/shard_map/ppermute | solution.py:632
  57.1 14.5 %collective-permute-start.12 = (f32[320,128]{1,0:T(8,128)S(1)}, f32[320,128]{1,0:T(8,128)S(1)}, u32[]{:S(2)}, u32[]{:S(2)}) collective-permute-start(f32[320,128]{1,0:T(8,128)S(1)} %get-tuple-element.106), channel_id=1, source_target_pairs={{0,4},{1,5},{2,6},{3,7},{4,0},{5,1},{6,2},{7,3},{8,12},{9,13},{10,... | collective-permute-start | bytes 491528 | tf_op jit(solution)/shard_map/ppermute | solution.py:632
  58.2 13.4 %collective-permute-start.13 = (f32[320,128]{1,0:T(8,128)S(1)}, f32[320,128]{1,0:T(8,128)S(1)}, u32[]{:S(2)}, u32[]{:S(2)}) collective-permute-start(f32[320,128]{1,0:T(8,128)S(1)} %get-tuple-element.107), channel_id=1, source_target_pairs={{0,6},{1,7},{2,4},{3,5},{4,2},{5,3},{6,0},{7,1},{8,14},{9,15},{10,... | collective-permute-start | bytes 491528 | tf_op jit(solution)/shard_map/ppermute | solution.py:632
  71.6 8.4 %copy-start.3 = (f32[128,2560]{1,0:T(8,128)S(1)}, f32[128,2560]{1,0:T(8,128)}, u32[]{:S(2)}) copy-start(f32[128,2560]{1,0:T(8,128)} %get-tuple-element.89.refs_3_) | copy-start | bytes 3932164
  72.2 7.8 %collective-permute-start.17 = (f32[1280,128]{1,0:T(8,128)S(1)}, f32[1280,128]{1,0:T(8,128)S(1)}, u32[]{:S(2)}, u32[]{:S(2)}) collective-permute-start(f32[1280,128]{1,0:T(8,128)S(1)} %order.2.refs_5_), channel_id=1, source_target_pairs={{0,1},{1,0},{2,3},{3,2},{4,5},{5,4},{6,7},{7,6},{8,9},{9,8},{10,11... | collective-permute-start | bytes 1966088 | tf_op jit(solution)/shard_map/ppermute | solution.py:632
  72.4 9.0 %copy-start.2 = (f32[256,2560]{1,0:T(8,128)S(1)}, f32[256,2560]{1,0:T(8,128)}, u32[]{:S(2)}) copy-start(f32[256,2560]{1,0:T(8,128)} %get-tuple-element.85.refs_6_) | copy-start | bytes 7864324
  73.4 12.1 %collective-permute-start.18 = (f32[320,128]{1,0:T(8,128)S(1)}, f32[320,128]{1,0:T(8,128)S(1)}, u32[]{:S(2)}, u32[]{:S(2)}) collective-permute-start(f32[320,128]{1,0:T(8,128)S(1)} %get-tuple-element.125), channel_id=1, source_target_pairs={{0,2},{1,3},{2,0},{3,1},{4,6},{5,7},{6,4},{7,5},{8,10},{9,11},{10,... | collective-permute-start | bytes 491528 | tf_op jit(solution)/shard_map/ppermute | solution.py:632
  77.5 15.0 %collective-permute-start.19 = (f32[320,128]{1,0:T(8,128)S(1)}, f32[320,128]{1,0:T(8,128)S(1)}, u32[]{:S(2)}, u32[]{:S(2)}) collective-permute-start(f32[320,128]{1,0:T(8,128)S(1)} %get-tuple-element.126), channel_id=1, source_target_pairs={{0,4},{1,5},{2,6},{3,7},{4,0},{5,1},{6,2},{7,3},{8,12},{9,13},{10,... | collective-permute-start | bytes 491528 | tf_op jit(solution)/shard_map/ppermute | solution.py:632
  78.6 14.0 %collective-permute-start.20 = (f32[320,128]{1,0:T(8,128)S(1)}, f32[320,128]{1,0:T(8,128)S(1)}, u32[]{:S(2)}, u32[]{:S(2)}) collective-permute-start(f32[320,128]{1,0:T(8,128)S(1)} %get-tuple-element.127), channel_id=1, source_target_pairs={{0,6},{1,7},{2,4},{3,5},{4,2},{5,3},{6,0},{7,1},{8,14},{9,15},{10,... | collective-permute-start | bytes 491528 | tf_op jit(solution)/shard_map/ppermute | solution.py:632
  80.0 1.4 %copy-start = (bf16[256,2560]{1,0:T(8,128)(2,1)S(1)}, bf16[256,2560]{1,0:T(8,128)(2,1)}, u32[]{:S(2)}) copy-start(bf16[256,2560]{1,0:T(8,128)(2,1)} %refs_0_.5) | copy-start | bytes 3932164
  80.0 1.7 %copy-start.1 = (bf16[256,2560]{1,0:T(8,128)(2,1)S(1)}, bf16[256,2560]{1,0:T(8,128)(2,1)}, u32[]{:S(2)}) copy-start(bf16[256,2560]{1,0:T(8,128)(2,1)} %refs_1_.11) | copy-start | bytes 3932164
  80.0 1.7 %copy-start.7 = (bf16[256,128]{1,0:T(8,128)(2,1)S(1)}, bf16[256,128]{1,0:T(8,128)(2,1)}, u32[]{:S(2)}) copy-start(bf16[256,128]{1,0:T(8,128)(2,1)} %refs_2_.11) | copy-start | bytes 196612
  80.0 1.7 %copy-start.8 = (bf16[256,128]{1,0:T(8,128)(2,1)S(1)}, bf16[256,128]{1,0:T(8,128)(2,1)}, u32[]{:S(2)}) copy-start(bf16[256,128]{1,0:T(8,128)(2,1)} %refs_3_.11) | copy-start | bytes 196612
  80.0 1.7 %copy-start.9 = (bf16[256,128]{1,0:T(8,128)(2,1)S(1)}, bf16[256,128]{1,0:T(8,128)(2,1)}, u32[]{:S(2)}) copy-start(bf16[256,128]{1,0:T(8,128)(2,1)} %get-tuple-element.77.refs_7_.refs_6_.refs_4_) | copy-start | bytes 196612
  80.0 1.7 %copy-start.10 = (bf16[256,128]{1,0:T(8,128)(2,1)S(1)}, bf16[256,128]{1,0:T(8,128)(2,1)}, u32[]{:S(2)}) copy-start(bf16[256,128]{1,0:T(8,128)(2,1)} %get-tuple-element.78.refs_8_.refs_7_.refs_5_) | copy-start | bytes 196612
  80.1 1.7 %copy-start.15 = (f32[256,128]{1,0:T(8,128)S(1)}, f32[256,128]{1,0:T(8,128)}, u32[]{:S(2)}) copy-start(f32[256,128]{1,0:T(8,128)} %get-tuple-element.86.refs_7_) | copy-start | bytes 393220
  93.1 2.2 %collective-permute-start.21 = (f32[1280,128]{1,0:T(8,128)S(1)}, f32[1280,128]{1,0:T(8,128)S(1)}, u32[]{:S(2)}, u32[]{:S(2)}) collective-permute-start(f32[1280,128]{1,0:T(8,128)S(1)} %order.3.refs_5_), channel_id=1, source_target_pairs={{0,1},{1,0},{2,3},{3,2},{4,5},{5,4},{6,7},{7,6},{8,9},{9,8},{10,11... | collective-permute-start | bytes 1966088 | tf_op jit(solution)/shard_map/ppermute | solution.py:632
  96.6 2.0 %collective-permute-start.22 = (f32[8,128]{1,0:T(8,128)S(1)}, f32[8,128]{1,0:T(8,128)S(1)}, u32[]{:S(2)}, u32[]{:S(2)}) collective-permute-start(f32[8,128]{1,0:T(8,128)S(1)} %add.27), channel_id=1, source_target_pairs={{0,1},{1,0},{2,3},{3,2},{4,5},{5,4},{6,7},{7,6},{8,9},{9,8},{10,11... | collective-permute-start | bytes 12296 | tf_op jit(solution)/shard_map/ppermute | solution.py:632
  98.6 5.7 %collective-permute-start.23 = (f32[8,128]{1,0:T(8,128)S(1)}, f32[8,128]{1,0:T(8,128)S(1)}, u32[]{:S(2)}, u32[]{:S(2)}) collective-permute-start(f32[8,128]{1,0:T(8,128)S(1)} %add.28), channel_id=1, source_target_pairs={{0,2},{1,3},{2,0},{3,1},{4,6},{5,7},{6,4},{7,5},{8,10},{9,11},{10,... | collective-permute-start | bytes 12296 | tf_op jit(solution)/shard_map/ppermute | solution.py:632
  103.7 0.6 copy-start.19
  104.4 4.5 %collective-permute-start.24 = (f32[8,128]{1,0:T(8,128)S(1)}, f32[8,128]{1,0:T(8,128)S(1)}, u32[]{:S(2)}, u32[]{:S(2)}) collective-permute-start(f32[8,128]{1,0:T(8,128)S(1)} %add.30), channel_id=1, source_target_pairs={{0,4},{1,5},{2,6},{3,7},{4,0},{5,1},{6,2},{7,3},{8,12},{9,13},{10,... | collective-permute-start | bytes 12296 | tf_op jit(solution)/shard_map/ppermute | solution.py:632
  108.9 3.6 %collective-permute-start.25 = (f32[8,128]{1,0:T(8,128)S(1)}, f32[8,128]{1,0:T(8,128)S(1)}, u32[]{:S(2)}, u32[]{:S(2)}) collective-permute-start(f32[8,128]{1,0:T(8,128)S(1)} %add.32), channel_id=1, source_target_pairs={{0,8},{1,9},{2,10},{3,11},{4,12},{5,13},{6,14},{7,15},{8,0},{9,1},... | collective-permute-start | bytes 12296 | tf_op jit(solution)/shard_map/ppermute | solution.py:632
  112.5 3.6 %collective-permute-start.26 = (f32[8,128]{1,0:T(8,128)S(1)}, f32[8,128]{1,0:T(8,128)S(1)}, u32[]{:S(2)}, u32[]{:S(2)}) collective-permute-start(f32[8,128]{1,0:T(8,128)S(1)} %add.34), channel_id=1, source_target_pairs={{0,16},{1,17},{2,18},{3,19},{4,20},{5,21},{6,22},{7,23},{8,24},{9,... | collective-permute-start | bytes 12296 | tf_op jit(solution)/shard_map/ppermute | solution.py:632

commit v7 on v6

--- a/solution.py
+++ b/solution.py
@@ -207,162 +207,172 @@
     )(place, x, g, write_map, read_map, *extra)
 
 
-def combine_kernel(chips, place, after, first_ref, keep_ref, decay_ref, log_ref, *out_refs):
+def combine_kernel(chips, place, first_ref, keep_ref, decay_ref, log_ref, mine_ref, send_ref):
     strips = decay_ref.shape[0]
     part = STATE // chips
-    size = strips * part
-    meta = first_ref[pl.ds(chips * size, META), :] + log_ref[...]
-    for step, out_ref in enumerate(out_refs):
-        base = (place[1] ^ step) * size
+    size = mine_ref.shape[0]
+    bit = place[1] & 1
+    for base, out_ref in ((bit * size, mine_ref), ((1 - bit) * size, send_ref)):
         for strip in range(strips):
-            rows = pl.ds(pl.multiple_of(base + strip * part, part), part)
-            out_ref[strip * part : (strip + 1) * part, :] = (
-                first_ref[rows, :] * decay_ref[strip : strip + 1, :] + keep_ref[rows, :]
-            )
-        out_ref[size:, :] = meta
-
-
-def combine(chips, place, after, first, keep, decay, log):
-    strips = decay.shape[0]
-    size = strips * (STATE // chips)
+            decay = decay_ref[strip : strip + 1, :]
+            for at in range(strip * part, size, strips * part):
+                rows = pl.ds(pl.multiple_of(base + at, part), part)
+                out_ref[at : at + part, :] = first_ref[rows, :] * decay + keep_ref[rows, :]
+    send_ref[size:, :] = first_ref[2 * size :, :] + log_ref[...]
+
+
+def halves(size):
+    return (
+        [whole(size, STRIP), whole(size + META, STRIP)],
+        [
+            jax.ShapeDtypeStruct((size, STRIP), F32),
+            jax.ShapeDtypeStruct((size + META, STRIP), F32),
+        ],
+    )
+
+
+def combine(chips, place, first, keep, decay, log):
+    out_specs, out_shape = halves(keep.shape[0] // 2)
     return pl.pallas_call(
         lambda *refs: combine_kernel(chips, *refs),
+        in_specs=[SCALARS] + [whole(*value.shape) for value in (first, keep, decay, log)],
+        out_specs=out_specs,
+        out_shape=out_shape,
+        compiler_params=pltpu.CompilerParams(vmem_limit_bytes=SMALL_VMEM),
+        cost_estimate=LITTLE,
+        name="combine",
+    )(place, first, keep, decay, log)
+
+
+def is_ahead(place, level):
+    return ((place[1] >> level) & 1) == place[0]
+
+
+def tail_block(value):
+    return pl.BlockSpec((META, STRIP), lambda c: (value.shape[0] // META - 1, 0))
+
+
+def up_kernel(level, last, part, offset, strips, head_size, place, mine_ref, log_ref, got_ref, *outs):
+    size = mine_ref.shape[0]
+    ahead = is_ahead(place, level)
+    mine_log, got_log = log_ref[0:1, :], got_ref[size : size + 1, :]
+    mine_wide, got_wide = spread_rows(
+        [jnp.where(ahead, 1.0, jnp.exp(got_log)), jnp.where(ahead, jnp.exp(mine_log), 1.0)],
+        offset,
+        strips,
+        head_size,
+    )
+    bit = (place[1] >> (level + 1)) & 1
+    half = size if last else size // 2
+    targets = ((0, outs[0]),) if last else ((bit * half, outs[0]), ((1 - bit) * half, outs[1]))
+    for base, out_ref in targets:
+        for strip in range(strips):
+            one = slice(strip, strip + 1)
+            for at in range(strip * part, half, strips * part):
+                rows = slice(at, at + part)
+                if not last:
+                    rows = pl.ds(pl.multiple_of(base + at, part), part)
+                out_ref[at : at + part, :] = (
+                    mine_ref[rows, :] * mine_wide[one, :] + got_ref[rows, :] * got_wide[one, :]
+                )
+    outs[-1][half:, :] = jnp.broadcast_to(mine_log + got_log, (META, STRIP))
+
+
+def up(level, chips, half, strips, head_size, place, mine, send, got):
+    size = mine.shape[0]
+    last = 2 << level == chips
+    out_specs, out_shape = halves(size if last else size // 2)
+    if last:
+        out_specs, out_shape = out_specs[1:], out_shape[1:]
+    return pl.pallas_call(
+        lambda *refs: up_kernel(
+            level, last, STATE // chips, half * strips, strips, head_size, *refs
+        ),
         grid=(1,),
-        in_specs=[SCALARS]
-        + [whole(META, STRIP)]
-        + [whole(*value.shape) for value in (first, keep, decay, log)],
-        out_specs=[whole(size + META, STRIP)] * chips,
-        out_shape=[jax.ShapeDtypeStruct((size + META, STRIP), F32)] * chips,
+        in_specs=[SCALARS, whole(size, STRIP), tail_block(send), whole(size + META, STRIP)],
+        out_specs=out_specs,
+        out_shape=out_shape,
         compiler_params=pltpu.CompilerParams(vmem_limit_bytes=SMALL_VMEM),
         cost_estimate=LITTLE,
-        name="combine",
-    )(place, after, first, keep, decay, log)
-
-
-def rank_of(place, step):
-    chip = place[1] ^ step
-    return jnp.where(place[0] == 1, chip, -chip)
-
-
-def masked_sum(terms):
-    total = None
-    for hit, value in terms:
-        value = jnp.where(hit, value, 0.0)
-        total = value if total is None else total + value
-    return total
-
-
-def total_kernel(offset, strips, head_size, place, after_ref, *refs):
-    at_refs, out_ref = refs[:-1], refs[-1]
-    chips = len(at_refs)
-    part = STATE // chips
-    size = strips * part
-    rank = [rank_of(place, step) for step in range(chips)]
-    logs = [ref[size : size + 1, :] for ref in at_refs]
-    weights = [
-        jnp.exp(masked_sum([(rank[b] > rank[a], logs[b]) for b in range(chips)]))
-        for a in range(chips)
+        name="up",
+    )(place, mine, send, got)
+
+
+def down_kernel(level, top, part, offset, strips, head_size, place, mine_ref, log_ref, got_ref, *refs):
+    sources, (here_ref, there_ref) = refs[:-2], refs[-2:]
+    size = mine_ref.shape[0]
+    ahead = is_ahead(place, level)
+    rows_of = [
+        jnp.where(ahead, jnp.exp(got_ref[size : size + 1, :]), 1.0),
+        jnp.where(ahead, 1.0, jnp.exp(log_ref[0:1, :])),
     ]
-    wide = spread_rows(weights, offset, strips, head_size)
-    for strip in range(strips):
-        rows = slice(strip * part, (strip + 1) * part)
-        total = at_refs[0][rows, :] * wide[0][strip : strip + 1, :]
-        for a in range(1, chips):
-            total = total + at_refs[a][rows, :] * wide[a][strip : strip + 1, :]
-        out_ref[rows, :] = total
-    out_ref[size:, :] = jnp.broadcast_to(sum(logs[1:], logs[0]), (META, STRIP))
-
-
-def group_total(half, head_size, place, after, at):
-    strips = (at[0].shape[0] - META) * len(at) // STATE
-    return pl.pallas_call(
-        lambda *refs: total_kernel(half * strips, strips, head_size, *refs),
+    if top:
+        passed = jnp.zeros_like(rows_of[0])
+        for ref in sources:
+            rows_of.append(jnp.exp(passed))
+            passed = passed + ref[size : size + 1, :]
+        bases, length = (0,), size
+    else:
+        length = size // 2
+        bit = (place[1] >> (level + 1)) & 1
+        bases = (bit * length, (1 - bit) * length)
+    here_wide, there_wide, *group_wide = spread_rows(rows_of, offset, strips, head_size)
+    for index, base in enumerate(bases):
+        for strip in range(strips):
+            one = slice(strip, strip + 1)
+            for at in range(strip * part, length, strips * part):
+                rows = slice(at, at + part)
+                if top:
+                    entering = sources[0][rows, :] * group_wide[0][one, :]
+                    for ref, wide in zip(sources[1:], group_wide[1:]):
+                        entering = entering + ref[rows, :] * wide[one, :]
+                else:
+                    entering = sources[index][rows, :]
+                    rows = pl.ds(pl.multiple_of(base + at, part), part)
+                got = jnp.where(ahead, got_ref[rows, :], 0.0)
+                mine = jnp.where(ahead, 0.0, mine_ref[rows, :])
+                here_ref[rows, :] = entering * here_wide[one, :] + got
+                there_ref[rows, :] = entering * there_wide[one, :] + mine
+
+
+def down(level, chips, half, strips, head_size, place, mine, send, got, sources):
+    size = mine.shape[0]
+    top = 2 << level == chips
+    return pl.pallas_call(
+        lambda *refs: down_kernel(
+            level, top, STATE // chips, half * strips, strips, head_size, *refs
+        ),
         grid=(1,),
-        in_specs=[SCALARS, whole(META, STRIP)] + [whole(*at[0].shape)] * len(at),
-        out_specs=whole(*at[0].shape),
-        out_shape=jax.ShapeDtypeStruct(at[0].shape, F32),
+        in_specs=[SCALARS, whole(size, STRIP), tail_block(send), whole(size + META, STRIP)]
+        + [whole(*value.shape) for value in sources],
+        out_specs=[whole(size, STRIP)] * 2,
+        out_shape=[jax.ShapeDtypeStruct((size, STRIP), F32)] * 2,
         compiler_params=pltpu.CompilerParams(vmem_limit_bytes=SMALL_VMEM),
         cost_estimate=LITTLE,
-        name="group_total",
-    )(place, after, *at)
-
-
-def enter_kernel(chips, offset, strips, head_size, place, after_ref, *refs):
-    at_refs, got_refs, out_refs = refs[:chips], refs[chips:-chips], refs[-chips:]
-    part = STATE // chips
-    size = strips * part
-    rank = [rank_of(place, step) for step in range(chips)]
-    logs = [ref[size : size + 1, :] for ref in at_refs]
-    zero = jnp.zeros_like(logs[0])
-    rows_of = []
-    passed = zero
-    for ref in got_refs:
-        rows_of.append(jnp.exp(passed))
-        passed = passed + ref[size : size + 1, :]
-    for to in range(chips):
-        rows_of.append(
-            jnp.exp(masked_sum([(rank[m] < rank[to], logs[m]) for m in range(chips)]))
-        )
-    pairs = [(to, a) for to in range(chips) for a in range(chips) if a != to]
-    for to, a in pairs:
-        between = masked_sum(
-            [((rank[m] > rank[a]) & (rank[m] < rank[to]), logs[m]) for m in range(chips)]
-        )
-        rows_of.append(jnp.where(rank[a] < rank[to], jnp.exp(between), 0.0))
-    wide = spread_rows(rows_of, offset, strips, head_size)
-    groups_wide = wide[: len(got_refs)]
-    ahead_wide = wide[len(got_refs) : len(got_refs) + chips]
-    pair_wide = dict(zip(pairs, wide[len(got_refs) + chips :]))
-    for strip in range(strips):
-        rows = slice(strip * part, (strip + 1) * part)
-        one = slice(strip, strip + 1)
-        incoming = jnp.zeros((part, STRIP), F32)
-        for ref, weight in zip(got_refs, groups_wide):
-            incoming = incoming + ref[rows, :] * weight[one, :]
-        values = [ref[rows, :] for ref in at_refs]
-        for to in range(chips):
-            entering = incoming * ahead_wide[to][one, :]
-            for a in range(chips):
-                if a != to:
-                    entering = entering + values[a] * pair_wide[to, a][one, :]
-            out_refs[to][rows, :] = entering
-
-
-def enter(half, head_size, place, after, at, got):
-    chips = len(at)
-    strips = (at[0].shape[0] - META) * chips // STATE
-    size = strips * (STATE // chips)
-    return pl.pallas_call(
-        lambda *refs: enter_kernel(chips, half * strips, strips, head_size, *refs),
-        grid=(1,),
-        in_specs=[SCALARS, whole(META, STRIP)] + [whole(*at[0].shape)] * (chips + len(got)),
-        out_specs=[whole(size, STRIP)] * chips,
-        out_shape=[jax.ShapeDtypeStruct((size, STRIP), F32)] * chips,
-        compiler_params=pltpu.CompilerParams(vmem_limit_bytes=SMALL_VMEM),
-        cost_estimate=LITTLE,
-        name="enter",
-    )(place, after, *at, *got)
+        name="down",
+    )(place, mine, send, got, *sources)
 
 
 def intra_kernel(
-    heads, after_ref, x_ref, g_ref, write_ref, read_ref, rates_ref, column_ref, tail_ref, lead_ref,
-    dx_ref, db_ref, dc_ref, change_ref, state_ref, back_ref,
-    row_ref, scores_ref, mask_ref, pairs_ref, write_t, read_t,
+    heads, head_size, start, last,
+    after_ref, x_ref, g_ref, write_ref, read_ref, rates_ref, column_ref, tail_ref, lead_ref, *refs,
 ):
-    chunk = pl.program_id(0)
+    dx_ref, state_ref, back_ref, change_ref, *sums, row_ref, scores_ref, mask_ref, pairs_ref, \
+        write_t, read_t = refs[5 if start else 0 :]
+    step = pl.program_id(0)
+    chunk = start + step
     lanes = x_ref.shape[1]
-    head_size = lanes * pl.num_programs(0) // heads
     per_chunk = lanes // head_size
 
-    @pl.when(chunk == 0)
+    @pl.when(step == 0)
     def _():
         rates = rates_ref[...]
         triangle = lower(STRETCH)
         row_ref[...] = dot(rates, triangle, 1, 1, HIGHEST)
         mask_ref[...] = triangle
         scores_ref[...] = dot(read_ref[...], write_ref[...], 1, 1)
-        pairs_ref[...] = jnp.zeros_like(pairs_ref)
-        change_ref[...] = jnp.zeros_like(change_ref)
+        pairs_ref[...] = refs[4][...] if start else jnp.zeros_like(pairs_ref)
+        change_ref[...] = refs[3][...] if start else jnp.zeros_like(change_ref)
         write_t[...] = write_ref[...].astype(F32).T.astype(BF16)
         read_t[...] = read_ref[...].astype(F32).T.astype(BF16)
 
@@ -400,37 +410,45 @@
         )
     pairs_ref[...] = pairs
 
-    @pl.when(chunk == pl.num_programs(0) - 1)
+    @pl.when(step == pl.num_programs(0) - 1)
     def _():
-        summed = pairs_ref[...].astype(BF16)
-        db_ref[...] = dot(summed, read_ref[...], 0, 0)
-        dc_ref[...] = dot(summed, write_ref[...], 1, 0)
-
-
-def intra(after, x, g, write_map, read_map, rates, shared):
+        if last:
+            summed = pairs_ref[...].astype(BF16)
+            sums[0][...] = dot(summed, read_ref[...], 0, 0)
+            sums[1][...] = dot(summed, write_ref[...], 1, 0)
+        else:
+            sums[0][...] = pairs_ref[...]
+
+
+def intra(start, steps, after, x, g, write_map, read_map, rates, shared, earlier):
     tokens, wide = x.shape
     heads = rates.shape[0]
-    return pl.pallas_call(
-        lambda *refs: intra_kernel(heads, *refs),
-        grid=(wide // LANES,),
+    last = (start + steps) * LANES == wide
+    lanes = lambda rows: pl.BlockSpec((rows, LANES), lambda c: (0, start + c))
+    anywhere = pl.BlockSpec(memory_space=pl.ANY)
+    sums = [(tokens, STATE)] * 2 if last else [(tokens, tokens)]
+    return pl.pallas_call(
+        lambda *refs: intra_kernel(heads, wide // heads, start, last, *refs),
+        grid=(steps,),
         in_specs=[
             whole(META, STRIP),
-            lanes_of(tokens),
-            lanes_of(tokens),
+            lanes(tokens),
+            lanes(tokens),
             whole(tokens, STATE),
             whole(tokens, STATE),
             whole(heads, tokens),
         ]
-        + [whole(tokens, STRIP)] * 3,
-        out_specs=[lanes_of(tokens)] + [whole(tokens, STATE)] * 3 + [lanes_of(STATE)] * 2,
+        + [whole(tokens, STRIP)] * 3
+        + ([anywhere] * 3 + [whole(tokens, STATE), whole(tokens, tokens)] if earlier else []),
+        out_specs=[lanes(tokens), lanes(STATE), lanes(STATE), whole(tokens, STATE)]
+        + [whole(*shape) for shape in sums],
         out_shape=[
             jax.ShapeDtypeStruct((tokens, wide), F32),
-            jax.ShapeDtypeStruct((tokens, STATE), F32),
-            jax.ShapeDtypeStruct((tokens, STATE), F32),
-            jax.ShapeDtypeStruct((tokens, STATE), F32),
             jax.ShapeDtypeStruct((STATE, wide), F32),
             jax.ShapeDtypeStruct((STATE, wide), F32),
-        ],
+            jax.ShapeDtypeStruct((tokens, STATE), F32),
+        ]
+        + [jax.ShapeDtypeStruct(shape, F32) for shape in sums],
         scratch_shapes=[
             pltpu.VMEM((heads, tokens), F32),
             pltpu.VMEM((tokens, tokens), F32),
@@ -439,31 +457,31 @@
             pltpu.VMEM((STATE, tokens), BF16),
             pltpu.VMEM((STATE, tokens), BF16),
         ],
-        compiler_params=pltpu.CompilerParams(vmem_limit_bytes=BIG_VMEM),
+        input_output_aliases={9: 0, 10: 1, 11: 2} if earlier else {},
+        compiler_params=pltpu.CompilerParams(vmem_limit_bytes=SMALL_VMEM),
         cost_estimate=LITTLE,
         name="intra",
-    )(after, x, g, write_map, read_map, rates, *shared[1:])
-
-
-def order_kernel(place, *refs):
-    pieces, out_ref = refs[:-1], refs[-1]
-    size = pieces[0].shape[0]
-    for step, ref in enumerate(pieces):
-        rows = pl.ds(pl.multiple_of((place[1] ^ step) * size, size), size)
-        out_ref[rows, :] = ref[...]
-
-
-def order(place, pieces):
-    shape = (len(pieces) * pieces[0].shape[0], STRIP)
+    )(after, x, g, write_map, read_map, rates, *shared[1:], *earlier)
+
+
+def order_kernel(place, here_ref, got_ref, out_ref):
+    size = here_ref.shape[0]
+    bit = place[1] & 1
+    out_ref[pl.ds(pl.multiple_of(bit * size, size), size), :] = here_ref[...]
+    out_ref[pl.ds(pl.multiple_of((1 - bit) * size, size), size), :] = got_ref[...]
+
+
+def order(place, here, got):
+    shape = (2 * here.shape[0], STRIP)
     return pl.pallas_call(
         order_kernel,
-        in_specs=[SCALARS] + [whole(*value.shape) for value in pieces],
+        in_specs=[SCALARS, whole(*here.shape), whole(*got.shape)],
         out_specs=whole(*shape),
         out_shape=jax.ShapeDtypeStruct(shape, F32),
         compiler_params=pltpu.CompilerParams(vmem_limit_bytes=SMALL_VMEM),
         cost_estimate=LITTLE,
         name="order",
-    )(place, *pieces)
+    )(place, here, got)
 
 
 def assemble_kernel(
@@ -653,38 +671,75 @@
     maps = (inputs, out_grad, input_map, output_map)
     send, keep, decay, *shared = summary(chips, 0, place, *maps, log_decay, None)
     first = [to_core(send)]
-    pieces = [combine(chips, place, shared[0], first[0], keep, decay, shared[0])]
+    kept, decays = [keep], [decay]
     send, keep, decay = summary(chips, 1, place, *maps, log_decay, shared)
     first.append(to_core(send))
-    dx, db, dc, change, state_own, back_own = intra(pieces[0][0], *maps, log_decay, shared)
-    pieces.append(combine(chips, place, change, first[1], keep, decay, shared[0]))
-
-    def trade(values):
-        return [to_chip(value, step) for step, value in enumerate(values)]
-
-    def to_groups(half, token, at):
-        total = group_total(half, head_size, place, token, at)
-        return [to_later(total, step) for step in range(1, groups)]
-
-    at_a = trade(pieces[0])
-    at_b = trade(pieces[1])
-    got_a = to_groups(0, pieces[1][0], at_a)
-    got_a, at_b = lax.optimization_barrier((got_a, at_b))
-    own_a = trade(enter(0, head_size, place, change, at_a, got_a))
-    got_b = to_groups(1, change, at_b)
-    own_a, got_b = lax.optimization_barrier((own_a, got_b))
-    own_b = trade(enter(1, head_size, place, change, at_b, got_b))
-
-    def entering(half, token, own):
-        mine = order(place, own)
+    kept.append(keep)
+    decays.append(decay)
+
+    levels = chips.bit_length() - 1
+    held = [[], []]
+    waiting = [None, None]
+
+    def advance(half, step):
+        fixed = (chips, half, strips, head_size, place)
+        if step == 0:
+            mine, send = combine(
+                chips, place, first[half], kept[half], decays[half], shared[0]
+            )
+        elif step < levels:
+            held[half][-1] += (waiting[half],)
+            mine, send = up(step - 1, *fixed, *held[half][-1])
+        elif step == levels:
+            held[half][-1] += (waiting[half],)
+            (send,) = up(step - 1, *fixed, *held[half][-1])
+            waiting[half] = [to_later(send, far) for far in range(1, groups)]
+            return send
+        elif step <= 2 * levels:
+            level = 2 * levels - step
+            if level < levels - 1:
+                waiting[half] = (held[half][level + 1], waiting[half])
+            mine, send = down(level, *fixed, *held[half][level], waiting[half])
+            held[half][level] = mine
+            waiting[half] = to_chip(send, 1 << level)
+            return send
+        else:
+            send = order(place, held[half][0], waiting[half])
+            held[half] = send
+            waiting[half] = to_core(send)
+            return send
+        held[half].append((mine, send))
+        waiting[half] = to_chip(send, 1 << step)
+        return send
+
+    def entering(half, token):
         return assemble(
-            heads, chips, half, place, token, first[half], state_own, back_own, mine, to_core(mine)
+            heads, chips, half, place, token, first[half], state_own, back_own,
+            held[half], waiting[half],
         )
 
-    state, back, tally = entering(0, change, own_a)
+    chunks = inputs.shape[1] // LANES
+    rounds = 2 * levels + 2
+    block, ready = (), 0
+    for step in range(rounds):
+        token = advance(0, step)
+        if step:
+            advance(1, step - 1)
+        if step < 3:
+            more = pl.cdiv(chunks - ready, 3 - step)
+            block = intra(ready, more, token, *maps, log_decay, shared, block)
+            ready += more
+            waiting[0], waiting[1], first[1], block = lax.optimization_barrier(
+                (waiting[0], waiting[1], first[1], block)
+            )
+        elif step < rounds - 1:
+            waiting[0], waiting[1] = lax.optimization_barrier((waiting[0], waiting[1]))
+    dx, state_own, back_own, change, db, dc = block
+    state, back, tally = entering(0, change)
     grad, *sums = finish(heads, 0, STEPS, *maps, shared, dx, (db, dc, change), state, back, None)
-    own_b = hold(own_b, sums[2])
-    state, back, tally_b = entering(1, sums[2], own_b)
+    waiting[1] = hold(waiting[1], sums[2])
+    advance(1, rounds - 1)
+    state, back, tally_b = entering(1, sums[2])
     tally = tally + tally_b
 
     def count(later, tally, got, bit, index):

time: 119 us -> 116 us (0.975)
  starting transfers between devices: 38.5 us -> 26.5 us
  waiting for transfers between devices: 35.8 us -> 45.8 us
  local copies, waits for them, and re-layouts: 2.63 us -> 0.68 us
    ppermute x27 -> x23, starting transfers between devices: 38.5 us -> 26.5 us  [move(): return lax.ppermute(value, ('grp', 'seq'), pairs)]
    ppermute x27 -> x23, waiting for transfers between devices: 35.8 us -> 45.8 us  [move(): return lax.ppermute(value, ('grp', 'seq'), pairs)]
    unnamed x44 -> x30, local copies, waits for them, and re-layouts: 2.63 us -> 0.68 us
    pallas_call x9 -> x15, Pallas kernels: 20.2 us -> 21.1 us  [the longest x3 12.5 us: intra(): pl.pallas_call(lambda *refs: intra_kernel(heads, wide // heads, start, la...]
  transfers between devices with their start and end apart: 27 -> 23, of which waited for: 8 -> 14; matrix products, arithmetic and copies ran while one was open for 0% -> 0% of each run, Pallas kernels for 26% -> 25%
where the time goes in v7:
time: 116 us; the launch traced here: 115 us
  waiting for transfers between devices  45.8 us (39%)
  Pallas kernels  40 us (34%)
  starting transfers between devices  26.5 us (23%)
  other arithmetic  1.28 us (1%)
    ppermute x23, waiting for transfers between devices, move(): return lax.ppermute(value, ('grp', 'seq'), pairs)  45.8 us
    ppermute x23, starting transfers between devices, move(): return lax.ppermute(value, ('grp', 'seq'), pairs)  26.5 us
    pallas_call x3, Pallas kernels, intra(): pl.pallas_call(lambda *refs: intra_kernel(heads, wide // heads, start, la...  12.5 us
    pallas_call x2, Pallas kernels, summary(): pl.pallas_call(lambda *refs: summary_kernel(heads, chips, half, *refs), g...  7.41 us
    pallas_call x3, Pallas kernels, finish(): pl.pallas_call(lambda *refs: finish_kernel(heads, start, steps, last, *re...  7.38 us
    pallas_call x4, Pallas kernels, down(): pl.pallas_call(lambda *refs: down_kernel(level, top, STATE // chips, half...  3.16 us
    pallas_call x4, Pallas kernels, up(): pl.pallas_call(lambda *refs: up_kernel(level, last, STATE // chips, half...  2.96 us
    pallas_call x2, Pallas kernels, assemble(): pl.pallas_call(lambda *refs: assemble_kernel(heads, chips, half, wide //...  2.62 us
  transfers between devices with their start and end apart: 23, of which 14 were waited for; matrix products, arithmetic and copies ran while one was open for 0% of the time, Pallas kernels for 25%

profile of v7, /device:TPU:0, one launch (start us, length us, event | category | flops | bytes accessed | tf_op | source)
XLA Modules:
  0.0 115.3 jit_solution(11557707384677652582)
XLA Ops:
  0.6 0.7 pad_add_fusion.refs_0_.place
  1.3 3.8 %summary.2 = (f32[1288,128]{1,0:T(8,128)}, f32[1280,128]{1,0:T(8,128)}, f32[10,128]{1,0:T(8,128)}, f32[8,128]{1,0:T(8,128)}, f32[256,128]{1,0:T(8,128)}, /*index...) custom-call(s32[3]{0:T(128)} %pad_add_fusion.refs_0_.place, bf16[256,2560]{1,0:T(8,128)(2,1)} %refs_0_.5, ...), custom_call_target="tpu_custom_call" | custom-call | flops 1 | bytes 1 | tf_op jit(solution)/shard_map/summary/pallas_call | solution.py:187
  5.1 0.5 collective-permute-start
  5.6 0.0 copy-start.1
  5.6 0.0 copy-start.3
  5.6 0.0 copy-start.4
  5.7 3.7 %summary.3 = (f32[1288,128]{1,0:T(8,128)}, f32[1280,128]{1,0:T(8,128)}, f32[10,128]{1,0:T(8,128)}) custom-call(s32[3]{0:T(128)} %pad_add_fusion.refs_0_.place, bf16[256,2560]{1,0:T(8,128)(2,1)} %refs_0_.5, bf16[256,2560]{1,0:T(8,128)(2,1)} %refs_1_.15, bf16[256,128]{1,0:T(8,128)(2,1)} %refs_2_.15, bf16[256,128]{1,0:T(8,128)(2,1)} %refs_3_.15, ...), custom_call_target="tpu_custom_call" | custom-call | flops 1 | bytes 1 | tf_op jit(solution)/shard_map/summary/pallas_call | solution.py:187
  9.3 0.1 collective-permute-start.2
  9.5 0.6 combine.2
  10.1 3.1 %collective-permute-start.1 = (f32[648,128]{1,0:T(8,128)S(1)}, f32[648,128]{1,0:T(8,128)S(1)}, u32[]{:S(2)}, u32[]{:S(2)}) collective-permute-start(f32[648,128]{1,0:T(8,128)S(1)} %get-tuple-element.109.refs_0_.refs_2_), channel_id=1, source_target_pairs={{0,2},{1,3},{2,0},{3,1},{4,6},{5,7},{6,4},{7,5},{8,10},{9,11},{10,... | collective-permute-start | bytes 995336 | tf_op jit(solution)/shard_map/ppermute | solution.py:650
  13.3 5.1 %intra.3 = (f32[256,2560]{1,0:T(8,128)S(1)}, f32[128,2560]{1,0:T(8,128)S(1)}, f32[128,2560]{1,0:T(8,128)S(1)}, f32[256,128]{1,0:T(8,128)S(1)}, f32[256,256]{1,0:T(8,128)S(1)}) custom-call(f32[648,128]{1,0:T(8,128)S(1)} %get-tuple-element.109.refs_0_.refs_2_, bf16[256,2560]{1,0:T(8,128)(2,1)S(1)} %copy-done, bf16[256,2560]{1,0:T(8,128)(2,1)S(1)} %copy-done.1, ...), custom_call_target="tpu_custom_call" | custom-call | flops 1 | bytes 1 | tf_op jit(solution)/shard_map/intra/pallas_call | solution.py:430
  18.4 2.9 %collective-permute-done.1.refs_3_ = f32[648,128]{1,0:T(8,128)S(1)} collective-permute-done((f32[648,128]{1,0:T(8,128)S(1)}, f32[648,128]{1,0:T(8,128)S(1)}, u32[]{:S(2)}, u32[]{:S(2)}) %collective-permute-start.1) | collective-permute-done | bytes 331808 | tf_op jit(solution)/shard_map/ppermute | solution.py:650
  21.2 0.6 combine.3
  21.9 1.8 %collective-permute-start.4 = (f32[648,128]{1,0:T(8,128)S(1)}, f32[648,128]{1,0:T(8,128)S(1)}, u32[]{:S(2)}, u32[]{:S(2)}) collective-permute-start(f32[648,128]{1,0:T(8,128)S(1)} %get-tuple-element.123.refs_2_), channel_id=1, source_target_pairs={{0,2},{1,3},{2,0},{3,1},{4,6},{5,7},{6,4},{7,5},{8,10},{9,11},{10,... | collective-permute-start | bytes 995336 | tf_op jit(solution)/shard_map/ppermute | solution.py:650
  23.7 0.8 up.4
  24.4 2.7 %collective-permute-start.3 = (f32[328,128]{1,0:T(8,128)S(1)}, f32[328,128]{1,0:T(8,128)S(1)}, u32[]{:S(2)}, u32[]{:S(2)}) collective-permute-start(f32[328,128]{1,0:T(8,128)S(1)} %get-tuple-element.119.refs_0_.refs_2_), channel_id=1, source_target_pairs={{0,4},{1,5},{2,6},{3,7},{4,0},{5,1},{6,2},{7,3},{8,12},{9,13},{10,... | collective-permute-start | bytes 503816 | tf_op jit(solution)/shard_map/ppermute | solution.py:650
  27.1 5.0 %intra.4 = (f32[256,2560]{1,0:T(8,128)S(1)}, f32[128,2560]{1,0:T(8,128)S(1)}, f32[128,2560]{1,0:T(8,128)S(1)}, f32[256,128]{1,0:T(8,128)S(1)}, f32[256,256]{1,0:T(8,128)S(1)}) custom-call(f32[328,128]{1,0:T(8,128)S(1)} %get-tuple-element.119.refs_0_.refs_2_, ...), custom_call_target="tpu_custom_call", output_to_operand_aliasing={{0}: (9, {}), {1}: (10, {}), {2}: (11, {})} | custom-call | flops 1 | bytes 1 | tf_op jit(solution)/shard_map/intra/pallas_call | solution.py:430
  32.1 1.6 %collective-permute-done.3.refs_3_ = f32[328,128]{1,0:T(8,128)S(1)} collective-permute-done((f32[328,128]{1,0:T(8,128)S(1)}, f32[328,128]{1,0:T(8,128)S(1)}, u32[]{:S(2)}, u32[]{:S(2)}) %collective-permute-start.3) | collective-permute-done | bytes 167968 | tf_op jit(solution)/shard_map/ppermute | solution.py:650
  33.7 1.1 collective-permute-done.4.refs_3_
  34.7 0.8 up.6
  35.5 2.4 %collective-permute-start.8 = (f32[328,128]{1,0:T(8,128)S(1)}, f32[328,128]{1,0:T(8,128)S(1)}, u32[]{:S(2)}, u32[]{:S(2)}) collective-permute-start(f32[328,128]{1,0:T(8,128)S(1)} %get-tuple-element.137.refs_2_), channel_id=1, source_target_pairs={{0,4},{1,5},{2,6},{3,7},{4,0},{5,1},{6,2},{7,3},{8,12},{9,13},{10,... | collective-permute-start | bytes 503816 | tf_op jit(solution)/shard_map/ppermute | solution.py:650
  37.9 0.7 up.5.refs_0_
  38.6 1.3 %collective-permute-start.5 = (f32[328,128]{1,0:T(8,128)S(1)}, f32[328,128]{1,0:T(8,128)S(1)}, u32[]{:S(2)}, u32[]{:S(2)}) collective-permute-start(f32[328,128]{1,0:T(8,128)S(1)} %up.5.refs_0_), channel_id=1, source_target_pairs={{1,9},{3,11},{5,13},{7,15},{8,0},{9,17},{10,2},{11,19},{12,4},{13,... | collective-permute-start | bytes 503816 | tf_op jit(solution)/shard_map/ppermute | solution.py:650
  39.9 1.3 %collective-permute-start.6 = (f32[328,128]{1,0:T(8,128)S(1)}, f32[328,128]{1,0:T(8,128)S(1)}, u32[]{:S(2)}, u32[]{:S(2)}) collective-permute-start(f32[328,128]{1,0:T(8,128)S(1)} %up.5.refs_0_), channel_id=1, source_target_pairs={{1,17},{3,19},{5,21},{7,23},{9,25},{11,27},{13,29},{15,31},{16,0},... | collective-permute-start | bytes 503816 | tf_op jit(solution)/shard_map/ppermute | solution.py:650
  41.2 1.3 %collective-permute-start.7 = (f32[328,128]{1,0:T(8,128)S(1)}, f32[328,128]{1,0:T(8,128)S(1)}, u32[]{:S(2)}, u32[]{:S(2)}) collective-permute-start(f32[328,128]{1,0:T(8,128)S(1)} %up.5.refs_0_), channel_id=1, source_target_pairs={{1,25},{3,27},{5,29},{7,31},{24,0},{26,2},{28,4},{30,6}} | collective-permute-start | bytes 503816 | tf_op jit(solution)/shard_map/ppermute | solution.py:650
  42.5 2.5 %intra.5 = (f32[256,2560]{1,0:T(8,128)S(1)}, f32[128,2560]{1,0:T(8,128)S(1)}, f32[128,2560]{1,0:T(8,128)S(1)}, f32[256,128]{1,0:T(8,128)S(1)}, f32[256,128]{1,0:T(8,128)S(1)}, /*index=5*/f32[256,128]{1,0:T(8,128)S(1)}) custom-call(f32[328,128]{1,0:T(8,128)S(1)} %up.5.refs_0_, ...), custom_call_target="tpu_custom_call", output_to_operand_aliasing={{0}: (9, {}), {1}: (10, {}), {2}: (11, {})} | custom-call | flops 1 | bytes 1 | tf_op jit(solution)/shard_map/intra/pallas_call | solution.py:430
  45.0 0.9 collective-permute-done.5.refs_4_
  45.9 2.2 %collective-permute-done.6.refs_5_ = f32[328,128]{1,0:T(8,128)S(1)} collective-permute-done((f32[328,128]{1,0:T(8,128)S(1)}, f32[328,128]{1,0:T(8,128)S(1)}, u32[]{:S(2)}, u32[]{:S(2)}) %collective-permute-start.6) | collective-permute-done | bytes 167968 | tf_op jit(solution)/shard_map/ppermute | solution.py:650
  48.1 2.5 %collective-permute-done.7.refs_6_ = f32[328,128]{1,0:T(8,128)S(1)} collective-permute-done((f32[328,128]{1,0:T(8,128)S(1)}, f32[328,128]{1,0:T(8,128)S(1)}, u32[]{:S(2)}, u32[]{:S(2)}) %collective-permute-start.7) | collective-permute-done | bytes 167968 | tf_op jit(solution)/shard_map/ppermute | solution.py:650
  50.6 0.7 up.7
  51.3 1.3 %collective-permute-start.10 = (f32[328,128]{1,0:T(8,128)S(1)}, f32[328,128]{1,0:T(8,128)S(1)}, u32[]{:S(2)}, u32[]{:S(2)}) collective-permute-start(f32[328,128]{1,0:T(8,128)S(1)} %up.7), channel_id=1, source_target_pairs={{1,9},{3,11},{5,13},{7,15},{8,0},{9,17},{10,2},{11,19},{12,4},{13,... | collective-permute-start | bytes 503816 | tf_op jit(solution)/shard_map/ppermute | solution.py:650
  52.6 1.3 %collective-permute-start.11 = (f32[328,128]{1,0:T(8,128)S(1)}, f32[328,128]{1,0:T(8,128)S(1)}, u32[]{:S(2)}, u32[]{:S(2)}) collective-permute-start(f32[328,128]{1,0:T(8,128)S(1)} %up.7), channel_id=1, source_target_pairs={{1,17},{3,19},{5,21},{7,23},{9,25},{11,27},{13,29},{15,31},{16,0},... | collective-permute-start | bytes 503816 | tf_op jit(solution)/shard_map/ppermute | solution.py:650
  53.9 1.5 %collective-permute-start.12 = (f32[328,128]{1,0:T(8,128)S(1)}, f32[328,128]{1,0:T(8,128)S(1)}, u32[]{:S(2)}, u32[]{:S(2)}) collective-permute-start(f32[328,128]{1,0:T(8,128)S(1)} %up.7), channel_id=1, source_target_pairs={{1,25},{3,27},{5,29},{7,31},{24,0},{26,2},{28,4},{30,6}} | collective-permute-start | bytes 503816 | tf_op jit(solution)/shard_map/ppermute | solution.py:650
  55.4 0.8 down.4
  56.2 0.7 collective-permute-start.9
  56.9 9.9 %collective-permute-done.9.refs_5_ = f32[320,128]{1,0:T(8,128)S(1)} collective-permute-done((f32[320,128]{1,0:T(8,128)S(1)}, f32[320,128]{1,0:T(8,128)S(1)}, u32[]{:S(2)}, u32[]{:S(2)}) %collective-permute-start.9) | collective-permute-done | bytes 163872 | tf_op jit(solution)/shard_map/ppermute | solution.py:650
  66.7 0.8 down.5
  67.5 0.1 collective-permute-start.13
  67.6 0.8 down.6
  68.4 2.3 %collective-permute-start.14 = (f32[320,128]{1,0:T(8,128)S(1)}, f32[320,128]{1,0:T(8,128)S(1)}, u32[]{:S(2)}, u32[]{:S(2)}) collective-permute-start(f32[320,128]{1,0:T(8,128)S(1)} %get-tuple-element.169), channel_id=1, source_target_pairs={{0,4},{1,5},{2,6},{3,7},{4,0},{5,1},{6,2},{7,3},{8,12},{9,13},{10,... | collective-permute-start | bytes 491528 | tf_op jit(solution)/shard_map/ppermute | solution.py:650
  70.7 7.0 %collective-permute-done.14.refs_5_ = f32[320,128]{1,0:T(8,128)S(1)} collective-permute-done((f32[320,128]{1,0:T(8,128)S(1)}, f32[320,128]{1,0:T(8,128)S(1)}, u32[]{:S(2)}, u32[]{:S(2)}) %collective-permute-start.14) | collective-permute-done | bytes 163872 | tf_op jit(solution)/shard_map/ppermute | solution.py:650
  77.6 2.2 %collective-permute-done.13.got_ref = f32[640,128]{1,0:T(8,128)S(1)} collective-permute-done((f32[640,128]{1,0:T(8,128)S(1)}, f32[640,128]{1,0:T(8,128)S(1)}, u32[]{:S(2)}, u32[]{:S(2)}) %collective-permute-start.13) | collective-permute-done | bytes 327712 | tf_op jit(solution)/shard_map/ppermute | solution.py:650
  79.8 0.6 order.2.refs_5_
  80.4 0.1 collective-permute-start.15
  80.5 0.8 down.7
  81.3 1.4 %collective-permute-start.16 = (f32[640,128]{1,0:T(8,128)S(1)}, f32[640,128]{1,0:T(8,128)S(1)}, u32[]{:S(2)}, u32[]{:S(2)}) collective-permute-start(f32[640,128]{1,0:T(8,128)S(1)} %get-tuple-element.180), channel_id=1, source_target_pairs={{0,2},{1,3},{2,0},{3,1},{4,6},{5,7},{6,4},{7,5},{8,10},{9,11},{10,... | collective-permute-start | bytes 983048 | tf_op jit(solution)/shard_map/ppermute | solution.py:650
  82.7 1.3 %assemble.2 = (bf16[128,1280]{1,0:T(8,128)(2,1)S(1)}, bf16[128,1280]{1,0:T(8,128)(2,1)S(1)}, f32[8,128]{1,0:T(8,128)S(1)}) custom-call(s32[3]{0:T(128)S(1)} %copy-done.10, f32[256,128]{1,0:T(8,128)S(1)} %get-tuple-element.153.refs_1_.refs_9_, f32[1288,128]{1,0:T(8,128)S(1)} %collective-permute-done.refs_1_.refs_2_, ...), custom_call_target="tpu_custom_call" | custom-call | flops 1 | bytes 1 | tf_op jit(solution)/shard_map/assemble/pallas_call | solution.py:525
  84.0 3.8 %finish.3 = (bf16[256,2560]{1,0:T(8,128)(2,1)}, f32[256,128]{1,0:T(8,128)S(1)}, f32[256,128]{1,0:T(8,128)S(1)}, f32[256,128]{1,0:T(8,128)S(1)}) custom-call(bf16[256,2560]{1,0:T(8,128)(2,1)S(1)} %copy-done, bf16[256,2560]{1,0:T(8,128)(2,1)S(1)} %copy-done.1, bf16[256,128]{1,0:T(8,128)(2,1)S(1)} %copy-done.2, bf16[256,128]{1,0:T(8,128)(2,1)S(1)} %copy-done.3, ...), custom_call_target="tpu_custom_call" | custom-call | flops 1 | bytes 1 | tf_op jit(solution)/shard_map/finish/pallas_call | solution.py:592
  87.8 3.6 %collective-permute-done.16.got_ref = f32[640,128]{1,0:T(8,128)S(1)} collective-permute-done((f32[640,128]{1,0:T(8,128)S(1)}, f32[640,128]{1,0:T(8,128)S(1)}, u32[]{:S(2)}, u32[]{:S(2)}) %collective-permute-start.16) | collective-permute-done | bytes 327712 | tf_op jit(solution)/shard_map/ppermute | solution.py:650
  91.5 0.6 order.3.refs_5_
  92.1 0.1 collective-permute-start.17
  92.1 2.1 %collective-permute-done.17.refs_6_ = f32[1280,128]{1,0:T(8,128)S(1)} collective-permute-done((f32[1280,128]{1,0:T(8,128)S(1)}, f32[1280,128]{1,0:T(8,128)S(1)}, u32[]{:S(2)}, u32[]{:S(2)}) %collective-permute-start.17) | collective-permute-done | bytes 655392 | tf_op jit(solution)/shard_map/ppermute | solution.py:650
  94.2 1.3 %assemble.3 = (bf16[128,1280]{1,0:T(8,128)(2,1)S(1)}, bf16[128,1280]{1,0:T(8,128)(2,1)S(1)}, f32[8,128]{1,0:T(8,128)S(1)}) custom-call(s32[3]{0:T(128)S(1)} %copy-done.10, f32[256,128]{1,0:T(8,128)S(1)} %get-tuple-element.175.refs_1_.refs_9_, f32[1288,128]{1,0:T(8,128)S(1)} %collective-permute-done.2.refs_1_.refs_2_, ...), custom_call_target="tpu_custom_call" | custom-call | flops 1 | bytes 1 | tf_op jit(solution)/shard_map/assemble/pallas_call | solution.py:525
  95.6 0.2 collective-permute-start.18
  95.8 1.8 %finish.4 = (bf16[256,2560]{1,0:T(8,128)(2,1)}, f32[256,128]{1,0:T(8,128)S(1)}, f32[256,128]{1,0:T(8,128)S(1)}, f32[256,128]{1,0:T(8,128)S(1)}) custom-call(bf16[256,2560]{1,0:T(8,128)(2,1)S(1)} %copy-done, bf16[256,2560]{1,0:T(8,128)(2,1)S(1)} %copy-done.1, bf16[256,128]{1,0:T(8,128)(2,1)S(1)} %copy-done.2, ...), custom_call_target="tpu_custom_call", output_to_operand_aliasing={{0}: (12, {})} | custom-call | flops 1 | bytes 1 | tf_op jit(solution)/shard_map/finish/pallas_call | solution.py:592
  97.5 1.4 %collective-permute-start.19 = (f32[8,128]{1,0:T(8,128)S(1)}, f32[8,128]{1,0:T(8,128)S(1)}, u32[]{:S(2)}, u32[]{:S(2)}) collective-permute-start(f32[8,128]{1,0:T(8,128)S(1)} %add.28), channel_id=1, source_target_pairs={{0,2},{1,3},{2,0},{3,1},{4,6},{5,7},{6,4},{7,5},{8,10},{9,11},{10,... | collective-permute-start | bytes 12296 | tf_op jit(solution)/shard_map/ppermute | solution.py:650
  98.9 1.8 %finish.5 = (bf16[256,2560]{1,0:T(8,128)(2,1)}, bf16[256,128]{1,0:T(8,128)(2,1)}, bf16[256,128]{1,0:T(8,128)(2,1)}, f32[40,256]{1,0:T(8,128)S(1)}) custom-call(bf16[256,2560]{1,0:T(8,128)(2,1)S(1)} %copy-done, bf16[256,2560]{1,0:T(8,128)(2,1)S(1)} %copy-done.1, bf16[256,128]{1,0:T(8,128)(2,1)S(1)} %copy-done.2, ...), custom_call_target="tpu_custom_call", output_to_operand_aliasing={{0}: (12, {})} | custom-call | flops 1 | bytes 1 | tf_op jit(solution)/shard_map/finish/pallas_call | solution.py:592
  100.8 0.6 copy-done.11
  101.4 1.7 %collective-permute-start.20 = (f32[8,128]{1,0:T(8,128)S(1)}, f32[8,128]{1,0:T(8,128)S(1)}, u32[]{:S(2)}, u32[]{:S(2)}) collective-permute-start(f32[8,128]{1,0:T(8,128)S(1)} %add.30), channel_id=1, source_target_pairs={{0,4},{1,5},{2,6},{3,7},{4,0},{5,1},{6,2},{7,3},{8,12},{9,13},{10,... | collective-permute-start | bytes 12296 | tf_op jit(solution)/shard_map/ppermute | solution.py:650
  103.1 2.8 %collective-permute-done.20 = f32[8,128]{1,0:T(8,128)S(1)} collective-permute-done((f32[8,128]{1,0:T(8,128)S(1)}, f32[8,128]{1,0:T(8,128)S(1)}, u32[]{:S(2)}, u32[]{:S(2)}) %collective-permute-start.20) | collective-permute-done | bytes 4128 | tf_op jit(solution)/shard_map/ppermute | solution.py:650
  105.9 3.6 %collective-permute-done.21 = f32[8,128]{1,0:T(8,128)S(1)} collective-permute-done((f32[8,128]{1,0:T(8,128)S(1)}, f32[8,128]{1,0:T(8,128)S(1)}, u32[]{:S(2)}, u32[]{:S(2)}) %collective-permute-start.21) | collective-permute-done | bytes 4128 | tf_op jit(solution)/shard_map/ppermute | solution.py:650
  109.5 3.6 %collective-permute-done.22 = f32[8,128]{1,0:T(8,128)S(1)} collective-permute-done((f32[8,128]{1,0:T(8,128)S(1)}, f32[8,128]{1,0:T(8,128)S(1)}, u32[]{:S(2)}, u32[]{:S(2)}) %collective-permute-start.22) | collective-permute-done | bytes 4128 | tf_op jit(solution)/shard_map/ppermute | solution.py:650
  113.1 0.6 select_add_fusion.later_ref
  113.7 1.5 %add_later.1 = f32[40,256]{1,0:T(8,128)} custom-call(f32[40,256]{1,0:T(8,128)} %copy-done.11, f32[8,128]{1,0:T(8,128)} %select_add_fusion.later_ref), custom_call_target="tpu_custom_call" | custom-call | flops 1 | bytes 1 | tf_op jit(solution)/shard_map/add_later/pallas_call | solution.py:622
  (42 shorter events, 0.1 us)
Async XLA Ops:
  5.1 4.4 %collective-permute-start = (f32[1288,128]{1,0:T(8,128)}, f32[1288,128]{1,0:T(8,128)S(1)}, u32[]{:S(2)}, u32[]{:S(2)}) collective-permute-start(f32[1288,128]{1,0:T(8,128)} %get-tuple-element.104), channel_id=1, source_target_pairs={{0,1},{1,0},{2,3},{3,2},{4,5},{5,4},{6,7},{7,6},{8,9},{9,8},{10,11... | collective-permute-start | bytes 1978376 | tf_op jit(solution)/shard_map/ppermute | solution.py:650
  5.6 3.9 %copy-start.9 = (f32[1280,128]{1,0:T(8,128)S(1)}, f32[1280,128]{1,0:T(8,128)}, u32[]{:S(2)}) copy-start(f32[1280,128]{1,0:T(8,128)} %get-tuple-element.105.refs_2_) | copy-start | bytes 1966084
  5.6 3.9 %copy-start.10 = (s32[3]{0:T(128)S(1)}, s32[3]{0:T(128)}, u32[]{:S(2)}) copy-start(s32[3]{0:T(128)} %pad_add_fusion.refs_0_.place) | copy-start | bytes 40
  5.6 3.9 %copy-start.12 = (f32[8,128]{1,0:T(8,128)S(1)}, f32[8,128]{1,0:T(8,128)}, u32[]{:S(2)}) copy-start(f32[8,128]{1,0:T(8,128)} %get-tuple-element.107.refs_4_.refs_5_) | copy-start | bytes 12292
  5.6 3.9 %copy-start.14 = (f32[10,128]{1,0:T(8,128)S(1)}, f32[10,128]{1,0:T(8,128)}, u32[]{:S(2)}) copy-start(f32[10,128]{1,0:T(8,128)} %get-tuple-element.106.refs_3_) | copy-start | bytes 15364
  5.6 7.6 %copy-start.1 = (bf16[256,2560]{1,0:T(8,128)(2,1)S(1)}, bf16[256,2560]{1,0:T(8,128)(2,1)}, u32[]{:S(2)}) copy-start(bf16[256,2560]{1,0:T(8,128)(2,1)} %refs_1_.15) | copy-start | bytes 3932164
  5.6 7.6 %copy-start.2 = (bf16[256,128]{1,0:T(8,128)(2,1)S(1)}, bf16[256,128]{1,0:T(8,128)(2,1)}, u32[]{:S(2)}) copy-start(bf16[256,128]{1,0:T(8,128)(2,1)} %refs_2_.15) | copy-start | bytes 196612
  5.6 7.6 %copy-start.3 = (bf16[256,128]{1,0:T(8,128)(2,1)S(1)}, bf16[256,128]{1,0:T(8,128)(2,1)}, u32[]{:S(2)}) copy-start(bf16[256,128]{1,0:T(8,128)(2,1)} %refs_3_.15) | copy-start | bytes 196612
  5.6 7.6 %copy-start.4 = (bf16[256,128]{1,0:T(8,128)(2,1)S(1)}, bf16[256,128]{1,0:T(8,128)(2,1)}, u32[]{:S(2)}) copy-start(bf16[256,128]{1,0:T(8,128)(2,1)} %get-tuple-element.102.refs_6_.refs_7_.refs_4_) | copy-start | bytes 196612
  5.6 7.6 %copy-start.5 = (bf16[256,128]{1,0:T(8,128)(2,1)S(1)}, bf16[256,128]{1,0:T(8,128)(2,1)}, u32[]{:S(2)}) copy-start(bf16[256,128]{1,0:T(8,128)(2,1)} %get-tuple-element.103.refs_7_.refs_8_.refs_5_) | copy-start | bytes 196612
  5.7 7.6 %copy-start.6 = (f32[256,128]{1,0:T(8,128)S(1)}, f32[256,128]{1,0:T(8,128)}, u32[]{:S(2)}) copy-start(f32[256,128]{1,0:T(8,128)} %get-tuple-element.111.refs_6_) | copy-start | bytes 393220
  5.7 7.6 %copy-start.7 = (f32[40,256]{1,0:T(8,128)S(1)}, f32[40,256]{1,0:T(8,128)}, u32[]{:S(2)}) copy-start(f32[40,256]{1,0:T(8,128)} %refs_5_.7) | copy-start | bytes 122884
  9.3 3.9 %copy-start = (bf16[256,2560]{1,0:T(8,128)(2,1)S(1)}, bf16[256,2560]{1,0:T(8,128)(2,1)}, u32[]{:S(2)}) copy-start(bf16[256,2560]{1,0:T(8,128)(2,1)} %refs_0_.5) | copy-start | bytes 3932164
  9.3 9.0 %collective-permute-start.2 = (f32[1288,128]{1,0:T(8,128)}, f32[1288,128]{1,0:T(8,128)S(1)}, u32[]{:S(2)}, u32[]{:S(2)}) collective-permute-start(f32[1288,128]{1,0:T(8,128)} %get-tuple-element.110), channel_id=1, source_target_pairs={{0,1},{1,0},{2,3},{3,2},{4,5},{5,4},{6,7},{7,6},{8,9},{9,8},{10,11... | collective-permute-start | bytes 1978376 | tf_op jit(solution)/shard_map/ppermute | solution.py:650
  10.1 11.1 %collective-permute-start.1 = (f32[648,128]{1,0:T(8,128)S(1)}, f32[648,128]{1,0:T(8,128)S(1)}, u32[]{:S(2)}, u32[]{:S(2)}) collective-permute-start(f32[648,128]{1,0:T(8,128)S(1)} %get-tuple-element.109.refs_0_.refs_2_), channel_id=1, source_target_pairs={{0,2},{1,3},{2,0},{3,1},{4,6},{5,7},{6,4},{7,5},{8,10},{9,11},{10,... | collective-permute-start | bytes 995336 | tf_op jit(solution)/shard_map/ppermute | solution.py:650
  13.3 8.0 %copy-start.8 = (f32[1280,128]{1,0:T(8,128)S(1)}, f32[1280,128]{1,0:T(8,128)}, u32[]{:S(2)}) copy-start(f32[1280,128]{1,0:T(8,128)} %get-tuple-element.121.refs_2_) | copy-start | bytes 1966084
  13.3 7.9 %copy-start.13 = (f32[10,128]{1,0:T(8,128)S(1)}, f32[10,128]{1,0:T(8,128)}, u32[]{:S(2)}) copy-start(f32[10,128]{1,0:T(8,128)} %get-tuple-element.122.refs_3_) | copy-start | bytes 15364
  21.9 12.9 %collective-permute-start.4 = (f32[648,128]{1,0:T(8,128)S(1)}, f32[648,128]{1,0:T(8,128)S(1)}, u32[]{:S(2)}, u32[]{:S(2)}) collective-permute-start(f32[648,128]{1,0:T(8,128)S(1)} %get-tuple-element.123.refs_2_), channel_id=1, source_target_pairs={{0,2},{1,3},{2,0},{3,1},{4,6},{5,7},{6,4},{7,5},{8,10},{9,11},{10,... | collective-permute-start | bytes 995336 | tf_op jit(solution)/shard_map/ppermute | solution.py:650
  24.4 9.3 %collective-permute-start.3 = (f32[328,128]{1,0:T(8,128)S(1)}, f32[328,128]{1,0:T(8,128)S(1)}, u32[]{:S(2)}, u32[]{:S(2)}) collective-permute-start(f32[328,128]{1,0:T(8,128)S(1)} %get-tuple-element.119.refs_0_.refs_2_), channel_id=1, source_target_pairs={{0,4},{1,5},{2,6},{3,7},{4,0},{5,1},{6,2},{7,3},{8,12},{9,13},{10,... | collective-permute-start | bytes 503816 | tf_op jit(solution)/shard_map/ppermute | solution.py:650
  35.5 9.5 %collective-permute-start.8 = (f32[328,128]{1,0:T(8,128)S(1)}, f32[328,128]{1,0:T(8,128)S(1)}, u32[]{:S(2)}, u32[]{:S(2)}) collective-permute-start(f32[328,128]{1,0:T(8,128)S(1)} %get-tuple-element.137.refs_2_), channel_id=1, source_target_pairs={{0,4},{1,5},{2,6},{3,7},{4,0},{5,1},{6,2},{7,3},{8,12},{9,13},{10,... | collective-permute-start | bytes 503816 | tf_op jit(solution)/shard_map/ppermute | solution.py:650
  38.6 7.3 %collective-permute-start.5 = (f32[328,128]{1,0:T(8,128)S(1)}, f32[328,128]{1,0:T(8,128)S(1)}, u32[]{:S(2)}, u32[]{:S(2)}) collective-permute-start(f32[328,128]{1,0:T(8,128)S(1)} %up.5.refs_0_), channel_id=1, source_target_pairs={{1,9},{3,11},{5,13},{7,15},{8,0},{9,17},{10,2},{11,19},{12,4},{13,... | collective-permute-start | bytes 503816 | tf_op jit(solution)/shard_map/ppermute | solution.py:650
  39.9 8.2 %collective-permute-start.6 = (f32[328,128]{1,0:T(8,128)S(1)}, f32[328,128]{1,0:T(8,128)S(1)}, u32[]{:S(2)}, u32[]{:S(2)}) collective-permute-start(f32[328,128]{1,0:T(8,128)S(1)} %up.5.refs_0_), channel_id=1, source_target_pairs={{1,17},{3,19},{5,21},{7,23},{9,25},{11,27},{13,29},{15,31},{16,0},... | collective-permute-start | bytes 503816 | tf_op jit(solution)/shard_map/ppermute | solution.py:650
  41.2 9.3 %collective-permute-start.7 = (f32[328,128]{1,0:T(8,128)S(1)}, f32[328,128]{1,0:T(8,128)S(1)}, u32[]{:S(2)}, u32[]{:S(2)}) collective-permute-start(f32[328,128]{1,0:T(8,128)S(1)} %up.5.refs_0_), channel_id=1, source_target_pairs={{1,25},{3,27},{5,29},{7,31},{24,0},{26,2},{28,4},{30,6}} | collective-permute-start | bytes 503816 | tf_op jit(solution)/shard_map/ppermute | solution.py:650
  51.3 15.4 %collective-permute-start.10 = (f32[328,128]{1,0:T(8,128)S(1)}, f32[328,128]{1,0:T(8,128)S(1)}, u32[]{:S(2)}, u32[]{:S(2)}) collective-permute-start(f32[328,128]{1,0:T(8,128)S(1)} %up.7), channel_id=1, source_target_pairs={{1,9},{3,11},{5,13},{7,15},{8,0},{9,17},{10,2},{11,19},{12,4},{13,... | collective-permute-start | bytes 503816 | tf_op jit(solution)/shard_map/ppermute | solution.py:650
  52.6 14.1 %collective-permute-start.11 = (f32[328,128]{1,0:T(8,128)S(1)}, f32[328,128]{1,0:T(8,128)S(1)}, u32[]{:S(2)}, u32[]{:S(2)}) collective-permute-start(f32[328,128]{1,0:T(8,128)S(1)} %up.7), channel_id=1, source_target_pairs={{1,17},{3,19},{5,21},{7,23},{9,25},{11,27},{13,29},{15,31},{16,0},... | collective-permute-start | bytes 503816 | tf_op jit(solution)/shard_map/ppermute | solution.py:650
  53.9 12.8 %collective-permute-start.12 = (f32[328,128]{1,0:T(8,128)S(1)}, f32[328,128]{1,0:T(8,128)S(1)}, u32[]{:S(2)}, u32[]{:S(2)}) collective-permute-start(f32[328,128]{1,0:T(8,128)S(1)} %up.7), channel_id=1, source_target_pairs={{1,25},{3,27},{5,29},{7,31},{24,0},{26,2},{28,4},{30,6}} | collective-permute-start | bytes 503816 | tf_op jit(solution)/shard_map/ppermute | solution.py:650
  56.2 10.5 %collective-permute-start.9 = (f32[320,128]{1,0:T(8,128)S(1)}, f32[320,128]{1,0:T(8,128)S(1)}, u32[]{:S(2)}, u32[]{:S(2)}) collective-permute-start(f32[320,128]{1,0:T(8,128)S(1)} %get-tuple-element.160), channel_id=1, source_target_pairs={{0,4},{1,5},{2,6},{3,7},{4,0},{5,1},{6,2},{7,3},{8,12},{9,13},{10,... | collective-permute-start | bytes 491528 | tf_op jit(solution)/shard_map/ppermute | solution.py:650
  67.5 12.3 %collective-permute-start.13 = (f32[640,128]{1,0:T(8,128)S(1)}, f32[640,128]{1,0:T(8,128)S(1)}, u32[]{:S(2)}, u32[]{:S(2)}) collective-permute-start(f32[640,128]{1,0:T(8,128)S(1)} %get-tuple-element.165), channel_id=1, source_target_pairs={{0,2},{1,3},{2,0},{3,1},{4,6},{5,7},{6,4},{7,5},{8,10},{9,11},{10,... | collective-permute-start | bytes 983048 | tf_op jit(solution)/shard_map/ppermute | solution.py:650
  68.4 9.2 %collective-permute-start.14 = (f32[320,128]{1,0:T(8,128)S(1)}, f32[320,128]{1,0:T(8,128)S(1)}, u32[]{:S(2)}, u32[]{:S(2)}) collective-permute-start(f32[320,128]{1,0:T(8,128)S(1)} %get-tuple-element.169), channel_id=1, source_target_pairs={{0,4},{1,5},{2,6},{3,7},{4,0},{5,1},{6,2},{7,3},{8,12},{9,13},{10,... | collective-permute-start | bytes 491528 | tf_op jit(solution)/shard_map/ppermute | solution.py:650
  80.4 2.3 %collective-permute-start.15 = (f32[1280,128]{1,0:T(8,128)S(1)}, f32[1280,128]{1,0:T(8,128)S(1)}, u32[]{:S(2)}, u32[]{:S(2)}) collective-permute-start(f32[1280,128]{1,0:T(8,128)S(1)} %order.2.refs_5_), channel_id=1, source_target_pairs={{0,1},{1,0},{2,3},{3,2},{4,5},{5,4},{6,7},{7,6},{8,9},{9,8},{10,11... | collective-permute-start | bytes 1966088 | tf_op jit(solution)/shard_map/ppermute | solution.py:650
  81.3 10.2 %collective-permute-start.16 = (f32[640,128]{1,0:T(8,128)S(1)}, f32[640,128]{1,0:T(8,128)S(1)}, u32[]{:S(2)}, u32[]{:S(2)}) collective-permute-start(f32[640,128]{1,0:T(8,128)S(1)} %get-tuple-element.180), channel_id=1, source_target_pairs={{0,2},{1,3},{2,0},{3,1},{4,6},{5,7},{6,4},{7,5},{8,10},{9,11},{10,... | collective-permute-start | bytes 983048 | tf_op jit(solution)/shard_map/ppermute | solution.py:650
  92.1 2.2 %collective-permute-start.17 = (f32[1280,128]{1,0:T(8,128)S(1)}, f32[1280,128]{1,0:T(8,128)S(1)}, u32[]{:S(2)}, u32[]{:S(2)}) collective-permute-start(f32[1280,128]{1,0:T(8,128)S(1)} %order.3.refs_5_), channel_id=1, source_target_pairs={{0,1},{1,0},{2,3},{3,2},{4,5},{5,4},{6,7},{7,6},{8,9},{9,8},{10,11... | collective-permute-start | bytes 1966088 | tf_op jit(solution)/shard_map/ppermute | solution.py:650
  95.6 2.0 %collective-permute-start.18 = (f32[8,128]{1,0:T(8,128)S(1)}, f32[8,128]{1,0:T(8,128)S(1)}, u32[]{:S(2)}, u32[]{:S(2)}) collective-permute-start(f32[8,128]{1,0:T(8,128)S(1)} %add.27), channel_id=1, source_target_pairs={{0,1},{1,0},{2,3},{3,2},{4,5},{5,4},{6,7},{7,6},{8,9},{9,8},{10,11... | collective-permute-start | bytes 12296 | tf_op jit(solution)/shard_map/ppermute | solution.py:650
  97.5 3.8 %collective-permute-start.19 = (f32[8,128]{1,0:T(8,128)S(1)}, f32[8,128]{1,0:T(8,128)S(1)}, u32[]{:S(2)}, u32[]{:S(2)}) collective-permute-start(f32[8,128]{1,0:T(8,128)S(1)} %add.28), channel_id=1, source_target_pairs={{0,2},{1,3},{2,0},{3,1},{4,6},{5,7},{6,4},{7,5},{8,10},{9,11},{10,... | collective-permute-start | bytes 12296 | tf_op jit(solution)/shard_map/ppermute | solution.py:650
  100.8 0.6 copy-start.11
  101.4 4.5 %collective-permute-start.20 = (f32[8,128]{1,0:T(8,128)S(1)}, f32[8,128]{1,0:T(8,128)S(1)}, u32[]{:S(2)}, u32[]{:S(2)}) collective-permute-start(f32[8,128]{1,0:T(8,128)S(1)} %add.30), channel_id=1, source_target_pairs={{0,4},{1,5},{2,6},{3,7},{4,0},{5,1},{6,2},{7,3},{8,12},{9,13},{10,... | collective-permute-start | bytes 12296 | tf_op jit(solution)/shard_map/ppermute | solution.py:650
  105.9 3.6 %collective-permute-start.21 = (f32[8,128]{1,0:T(8,128)S(1)}, f32[8,128]{1,0:T(8,128)S(1)}, u32[]{:S(2)}, u32[]{:S(2)}) collective-permute-start(f32[8,128]{1,0:T(8,128)S(1)} %add.32), channel_id=1, source_target_pairs={{0,8},{1,9},{2,10},{3,11},{4,12},{5,13},{6,14},{7,15},{8,0},{9,1},... | collective-permute-start | bytes 12296 | tf_op jit(solution)/shard_map/ppermute | solution.py:650
  109.5 3.6 %collective-permute-start.22 = (f32[8,128]{1,0:T(8,128)S(1)}, f32[8,128]{1,0:T(8,128)S(1)}, u32[]{:S(2)}, u32[]{:S(2)}) collective-permute-start(f32[8,128]{1,0:T(8,128)S(1)} %add.34), channel_id=1, source_target_pairs={{0,16},{1,17},{2,18},{3,19},{4,20},{5,21},{6,22},{7,23},{8,24},{9,... | collective-permute-start | bytes 12296 | tf_op jit(solution)/shard_map/ppermute | solution.py:650

commit v8 on v7

--- a/solution.py
+++ b/solution.py
@@ -355,9 +355,9 @@
 
 def intra_kernel(
     heads, head_size, start, last,
-    after_ref, x_ref, g_ref, write_ref, read_ref, rates_ref, column_ref, tail_ref, lead_ref, *refs,
+    place, after_ref, x_ref, g_ref, write_ref, read_ref, rates_ref, column_ref, tail_ref, lead_ref, *refs,
 ):
-    dx_ref, state_ref, back_ref, change_ref, *sums, row_ref, scores_ref, mask_ref, pairs_ref, \
+    dx_ref, mine_ref, other_ref, change_ref, *sums, row_ref, scores_ref, mask_ref, pairs_ref, \
         write_t, read_t = refs[5 if start else 0 :]
     step = pl.program_id(0)
     chunk = start + step
@@ -385,9 +385,12 @@
     adder = head_adder(chunk, head_size, lanes)
     spread = spreader(chunk, heads, head_size, lanes)
     high, low = term_pair(x_ref[...].astype(F32) * dot(tail_ref[...], spread, 1, 0))
-    state_ref[...] = dot(write_t[...], high, 1, 0) + dot(write_t[...], low, 1, 0)
+    state = dot(write_t[...], high, 1, 0) + dot(write_t[...], low, 1, 0)
     high, low = term_pair(g_ref[...].astype(F32) * dot(lead_ref[...], spread, 1, 0))
-    back_ref[...] = dot(read_t[...], high, 1, 0) + dot(read_t[...], low, 1, 0)
+    back = dot(read_t[...], high, 1, 0) + dot(read_t[...], low, 1, 0)
+    is_first = place[0] == 0
+    mine_ref[...] = jnp.where(is_first, state, back)
+    other_ref[...] = jnp.where(is_first, back, state)
     for pair in range(per_chunk // 2):
         strip = slice(pair * 2 * head_size, (pair + 1) * 2 * head_size)
         x = x_ref[:, strip]
@@ -420,7 +423,7 @@
             sums[0][...] = pairs_ref[...]
 
 
-def intra(start, steps, after, x, g, write_map, read_map, rates, shared, earlier):
+def intra(start, steps, place, after, x, g, write_map, read_map, rates, shared, earlier):
     tokens, wide = x.shape
     heads = rates.shape[0]
     last = (start + steps) * LANES == wide
@@ -431,6 +434,7 @@
         lambda *refs: intra_kernel(heads, wide // heads, start, last, *refs),
         grid=(steps,),
         in_specs=[
+            SCALARS,
             whole(META, STRIP),
             lanes(tokens),
             lanes(tokens),
@@ -457,11 +461,11 @@
             pltpu.VMEM((STATE, tokens), BF16),
             pltpu.VMEM((STATE, tokens), BF16),
         ],
-        input_output_aliases={9: 0, 10: 1, 11: 2} if earlier else {},
+        input_output_aliases={10: 0, 11: 1, 12: 2} if earlier else {},
         compiler_params=pltpu.CompilerParams(vmem_limit_bytes=SMALL_VMEM),
         cost_estimate=LITTLE,
         name="intra",
-    )(after, x, g, write_map, read_map, rates, *shared[1:], *earlier)
+    )(place, after, x, g, write_map, read_map, rates, *shared[1:], *earlier)
 
 
 def order_kernel(place, here_ref, got_ref, out_ref):
@@ -484,18 +488,62 @@
     )(place, here, got)
 
 
-def assemble_kernel(
-    heads, chips, half, head_size, place, after, first_ref, state_own, back_own, own_ref, far_ref,
-    state_ref, back_ref, total_ref,
+def tally_kernel(
+    heads, chips, half, head_size, place, first_ref, enter_ref, mine_ref, other_ref, out_ref
 ):
-    lanes = state_ref.shape[1]
+    lanes = mine_ref.shape[1]
     strips = lanes // STRIP
     part = STATE // chips
     size = strips * part
     log = first_ref[chips * size : chips * size + 1, :]
     decay = spread_rows([jnp.exp(log)], half * strips, strips, head_size)[0]
+    sums = [[], []]
+    for strip in range(strips):
+        wide = slice(strip * STRIP, (strip + 1) * STRIP)
+        near_sum = far_sum = None
+        for quarter in range(chips):
+            rows = slice(quarter * part, (quarter + 1) * part)
+            here = slice(quarter * size + strip * part, quarter * size + (strip + 1) * part)
+            far = enter_ref[here, :]
+            near = far * decay[strip : strip + 1, :] + first_ref[here, :]
+            near = near.astype(BF16).astype(F32) * mine_ref[rows, wide]
+            far = far.astype(BF16).astype(F32) * other_ref[rows, wide]
+            near_sum = near if near_sum is None else near_sum + near
+            far_sum = far if far_sum is None else far_sum + far
+        for found, value in zip(sums, (near_sum, far_sum)):
+            found.append(jnp.sum(value, axis=0, keepdims=True))
+    near, far = (jnp.concatenate(found, axis=1) for found in sums)
+    sign = jnp.where(place[0] == 1, 1.0, -1.0)
+    second = jnp.where(place[0] == 1, near, far) * sign
+    chip = (near + far) * sign
+    both = jnp.where(iota((META, lanes), 0) < META // 2, chip, second)
+    out_ref[...] = head_sums(both, head_adder(half, head_size, lanes))
+
+
+def tally(heads, chips, half, place, first, entering, mine, other):
+    wide = mine.shape[1]
+    ours = pl.BlockSpec((STATE, wide // HALVES), lambda c: (0, half))
+    return pl.pallas_call(
+        lambda *refs: tally_kernel(heads, chips, half, wide // heads, *refs),
+        grid=(1,),
+        in_specs=[SCALARS, whole(*first.shape), whole(*entering.shape), ours, ours],
+        out_specs=whole(META, STRIP),
+        out_shape=jax.ShapeDtypeStruct((META, STRIP), F32),
+        compiler_params=pltpu.CompilerParams(vmem_limit_bytes=SMALL_VMEM),
+        cost_estimate=LITTLE,
+        name="tally",
+    )(place, first, entering, mine, other)
+
+
+def assemble_kernel(
+    chips, half, head_size, place, after, first_ref, own_ref, far_ref, state_ref, back_ref
+):
+    strips = state_ref.shape[1] // STRIP
+    part = STATE // chips
+    size = strips * part
+    log = first_ref[chips * size : chips * size + 1, :]
+    decay = spread_rows([jnp.exp(log)], half * strips, strips, head_size)[0]
     is_first = place[0] == 0
-    sums = [None] * strips
     for quarter in range(chips):
         rows = slice(quarter * part, (quarter + 1) * part)
         for strip in range(strips):
@@ -503,40 +551,24 @@
             here = slice(quarter * size + strip * part, quarter * size + (strip + 1) * part)
             own = own_ref[here, :] * decay[strip : strip + 1, :] + first_ref[here, :]
             far = far_ref[here, :]
-            state = jnp.where(is_first, far, own).astype(BF16)
-            back = jnp.where(is_first, own, far).astype(BF16)
-            state_ref[rows, wide] = state
-            back_ref[rows, wide] = back
-            gain = state.astype(F32) * back_own[rows, wide]
-            gain = gain - back.astype(F32) * state_own[rows, wide]
-            sums[strip] = gain if sums[strip] is None else sums[strip] + gain
-    row_sum = [
-        jnp.broadcast_to(jnp.sum(value, axis=0, keepdims=True), (META, STRIP)) for value in sums
-    ]
-    total_ref[...] = head_sums(
-        jnp.concatenate(row_sum, axis=1), head_adder(half, head_size, lanes)
-    )
-
-
-def assemble(heads, chips, half, place, after, first, state_own, back_own, own, far):
-    wide = state_own.shape[1]
-    lanes = wide // HALVES
-    mine = pl.BlockSpec((STATE, lanes), lambda c: (0, half))
-    return pl.pallas_call(
-        lambda *refs: assemble_kernel(heads, chips, half, wide // heads, *refs),
+            state_ref[rows, wide] = jnp.where(is_first, far, own).astype(BF16)
+            back_ref[rows, wide] = jnp.where(is_first, own, far).astype(BF16)
+
+
+def assemble(heads, chips, half, place, after, first, own, far):
+    strips = own.shape[0] // STATE
+    lanes = strips * STRIP
+    return pl.pallas_call(
+        lambda *refs: assemble_kernel(chips, half, lanes * HALVES // heads, *refs),
         grid=(1,),
-        in_specs=[SCALARS, whole(META, STRIP), whole(*first.shape), mine, mine]
-        + [whole(*own.shape), whole(*far.shape)],
-        out_specs=[whole(STATE, lanes), whole(STATE, lanes), whole(META, STRIP)],
-        out_shape=[
-            jax.ShapeDtypeStruct((STATE, lanes), BF16),
-            jax.ShapeDtypeStruct((STATE, lanes), BF16),
-            jax.ShapeDtypeStruct((META, STRIP), F32),
-        ],
+        in_specs=[SCALARS, whole(META, STRIP)]
+        + [whole(*value.shape) for value in (first, own, far)],
+        out_specs=[whole(STATE, lanes), whole(STATE, lanes)],
+        out_shape=[jax.ShapeDtypeStruct((STATE, lanes), BF16)] * 2,
         compiler_params=pltpu.CompilerParams(vmem_limit_bytes=SMALL_VMEM),
         cost_estimate=LITTLE,
         name="assemble",
-    )(place, after, first, state_own, back_own, own, far)
+    )(place, after, first, own, far)
 
 
 def finish_kernel(
@@ -613,20 +645,22 @@
     )(x, g, write_map, read_map, *shared[2:], dx, *sums, state, back, *earlier)
 
 
-def add_later_kernel(suffix_ref, later_ref, out_ref):
+def add_later_kernel(place, suffix_ref, mine_ref, other_ref, out_ref):
     heads = out_ref.shape[0]
-    out_ref[...] = suffix_ref[...] + later_ref[...].T[:heads, 0:1]
-
-
-def add_later(suffix, later):
+    later = (mine_ref[...] + other_ref[...]).T[:heads, :]
+    second = later[:, META // 2 : META // 2 + 1]
+    out_ref[...] = suffix_ref[...] + later[:, 0:1] + jnp.where(place[0] == 0, second, 0.0)
+
+
+def add_later(place, suffix, mine, other):
     return pl.pallas_call(
         add_later_kernel,
-        in_specs=[whole(*suffix.shape), whole(*later.shape)],
+        in_specs=[SCALARS] + [whole(*value.shape) for value in (suffix, mine, other)],
         out_specs=whole(*suffix.shape),
         out_shape=jax.ShapeDtypeStruct(suffix.shape, F32),
         cost_estimate=LITTLE,
         name="add_later",
-    )(suffix, later)
+    )(place, suffix, mine, other)
 
 
 def per_device(inputs, out_grad, input_map, output_map, log_decay):
@@ -638,7 +672,6 @@
     chip, core = shard >> 1, shard & 1
     place = jnp.stack([core, chip, group]).astype(jnp.int32)
     strips = inputs.shape[1] // STRIP // HALVES
-    bits = groups.bit_length() - 1
     everyone = [(a, z, c) for a in range(groups) for z in range(chips) for c in range(2)]
 
     def move(value, target):
@@ -655,8 +688,8 @@
     def to_chip(value, step):
         return move(value, lambda a, z, c: (a, z ^ step, c)) if step else value
 
-    def to_group(value, step):
-        return move(value, lambda a, z, c: (a ^ step, z, c))
+    def to_earlier(value, step):
+        return move(value, lambda a, z, c: (a - step, z, c) if a >= step else None)
 
     def to_later(value, step):
         def target(a, z, c):
@@ -714,49 +747,60 @@
 
     def entering(half, token):
         return assemble(
-            heads, chips, half, place, token, first[half], state_own, back_own,
-            held[half], waiting[half],
+            heads, chips, half, place, token, first[half], held[half], waiting[half]
         )
 
     chunks = inputs.shape[1] // LANES
     rounds = 2 * levels + 2
     block, ready = (), 0
     for step in range(rounds):
+        if step == rounds - 1:
+            waiting[0] = hold(waiting[0], advance(1, step - 1))
+            advance(0, step)
+            continue
         token = advance(0, step)
+        if step == levels + 1:
+            waiting[1] = hold(waiting[1], token)
         if step:
             advance(1, step - 1)
         if step < 3:
             more = pl.cdiv(chunks - ready, 3 - step)
-            block = intra(ready, more, token, *maps, log_decay, shared, block)
+            block = intra(ready, more, place, token, *maps, log_decay, shared, block)
             ready += more
             waiting[0], waiting[1], first[1], block = lax.optimization_barrier(
                 (waiting[0], waiting[1], first[1], block)
             )
-        elif step < rounds - 1:
+        else:
             waiting[0], waiting[1] = lax.optimization_barrier((waiting[0], waiting[1]))
-    dx, state_own, back_own, change, db, dc = block
-    state, back, tally = entering(0, change)
+    dx, mine, other, change, db, dc = block
+    other = to_core(other)
+
+    def count(half):
+        return tally(heads, chips, half, place, first[half], held[half], mine, other)
+
+    state, back = entering(0, change)
     grad, *sums = finish(heads, 0, STEPS, *maps, shared, dx, (db, dc, change), state, back, None)
-    waiting[1] = hold(waiting[1], sums[2])
+    counted = count(0)
+    waiting[1] = hold(waiting[1], sums[2], counted)
     advance(1, rounds - 1)
-    state, back, tally_b = entering(1, sums[2])
-    tally = tally + tally_b
-
-    def count(later, tally, got, bit, index):
-        return later + jnp.where((index >> bit) & 1 == 0, got, 0.0), tally + got
-
-    got = to_core(tally)
+    counted = counted + count(1)
+
+    reached = [to_chip(counted, step) for step in range(1, chips)]
+    state, back = entering(1, counted)
     grad, *sums = finish(heads, STEPS, 1, *maps, shared, dx, sums, state, back, grad)
-    later, tally = count(0.0, tally, hold(got, sums[2]), 0, core)
-    got = to_chip(tally, 1)
-    sums = hold(sums, tally)
+    reached = hold(reached, sums[2])
+    later, whole_group = jnp.zeros_like(counted), counted
+    for step, value in enumerate(reached, 1):
+        later = later + jnp.where((chip ^ step) > chip, value, 0.0)
+        whole_group = whole_group + value
+    reached = [to_earlier(whole_group, step) for step in range(1, groups)]
+    sums = hold(sums, whole_group)
     grad, *sums = finish(heads, STEPS + 1, 1, *maps, shared, dx, sums, state, back, grad)
-    later, tally = count(later, tally, hold(got, sums[2]), 0, chip)
-    for bit in range(1, chips.bit_length() - 1):
-        later, tally = count(later, tally, to_chip(tally, 1 << bit), bit, chip)
-    for bit in range(bits):
-        later, tally = count(later, tally, to_group(tally, 1 << bit), bit, group)
-    return (grad, sums[0], sums[1], add_later(sums[2], later))
+    reached = hold(reached, sums[2])
+    later = sum(reached, later)
+    row = lax.broadcasted_iota(jnp.int32, later.shape, 0)
+    counted = jnp.where(row < META // 2, later, counted)
+    return (grad, sums[0], sums[1], add_later(place, sums[2], counted, to_core(counted)))
 
 
 def solution(mesh):

time: 116 us -> 124 us (1.069)
  the two profiles are of different devices: /device:TPU:0 before, /device:TPU:7 now
where the time goes in v8:
time: 124 us; the launch traced here: 123 us
  starting transfers between devices  44.8 us (36%)
  Pallas kernels  43.1 us (35%)
  waiting for transfers between devices  23.3 us (19%)
  local copies, waits for them, and re-layouts  8.27 us (7%)
  other arithmetic  2.52 us (2%)
    ppermute x26, starting transfers between devices, move(): return lax.ppermute(value, ('grp', 'seq'), pairs)  44.8 us
    ppermute x26, waiting for transfers between devices, move(): return lax.ppermute(value, ('grp', 'seq'), pairs)  23.3 us
    pallas_call x3, Pallas kernels, intra(): pl.pallas_call(lambda *refs: intra_kernel(heads, wide // heads, start, la...  14.1 us
    unnamed x56, local copies, waits for them, and re-layouts  8.27 us
    pallas_call x2, Pallas kernels, summary(): pl.pallas_call(lambda *refs: summary_kernel(heads, chips, half, *refs), g...  7.42 us
    pallas_call x3, Pallas kernels, finish(): pl.pallas_call(lambda *refs: finish_kernel(heads, start, steps, last, *re...  7.32 us
    pallas_call x4, Pallas kernels, down(): pl.pallas_call(lambda *refs: down_kernel(level, top, STATE // chips, half...  3.16 us
    pallas_call x4, Pallas kernels, up(): pl.pallas_call(lambda *refs: up_kernel(level, last, STATE // chips, half...  2.96 us
  transfers between devices with their start and end apart: 26, of which 11 were waited for; matrix products, arithmetic and copies ran while one was open for 0% of the time, Pallas kernels for 29%

profile of v8, /device:TPU:7, one launch (start us, length us, event | category | flops | bytes accessed | tf_op | source)
XLA Modules:
  0.0 123.0 jit_solution(3183826578506377292)
XLA Ops:
  1.2 3.8 %summary.2 = (f32[1288,128]{1,0:T(8,128)}, f32[1280,128]{1,0:T(8,128)}, f32[10,128]{1,0:T(8,128)}, f32[8,128]{1,0:T(8,128)}, f32[256,128]{1,0:T(8,128)}, /*index...) custom-call(s32[3]{0:T(128)} %pad_add_fusion.refs_0_.place, bf16[256,2560]{1,0:T(8,128)(2,1)} %refs_0_.5, ...), custom_call_target="tpu_custom_call" | custom-call | flops 1 | bytes 1 | tf_op jit(solution)/shard_map/summary/pallas_call | solution.py:187
  5.0 0.7 collective-permute-start
  5.8 3.7 %summary.3 = (f32[1288,128]{1,0:T(8,128)}, f32[1280,128]{1,0:T(8,128)}, f32[10,128]{1,0:T(8,128)}) custom-call(s32[3]{0:T(128)} %pad_add_fusion.refs_0_.place, bf16[256,2560]{1,0:T(8,128)(2,1)} %refs_0_.5, bf16[256,2560]{1,0:T(8,128)(2,1)} %refs_1_.9, bf16[256,128]{1,0:T(8,128)(2,1)} %refs_2_.15, bf16[256,128]{1,0:T(8,128)(2,1)} %refs_3_.15, ...), custom_call_target="tpu_custom_call" | custom-call | flops 1 | bytes 1 | tf_op jit(solution)/shard_map/summary/pallas_call | solution.py:187
  9.6 0.7 combine.2
  10.3 1.4 %collective-permute-start.1 = (f32[648,128]{1,0:T(8,128)S(1)}, f32[648,128]{1,0:T(8,128)S(1)}, u32[]{:S(2)}, u32[]{:S(2)}) collective-permute-start(f32[648,128]{1,0:T(8,128)S(1)} %get-tuple-element.113.refs_1_.refs_2_), channel_id=1, source_target_pairs={{0,2},{1,3},{2,0},{3,1},{4,6},{5,7},{6,4},{7,5},{8,10},{9,11},{10,... | collective-permute-start | bytes 995336 | tf_op jit(solution)/shard_map/ppermute | solution.py:683
  11.7 5.6 %intra.3 = (f32[256,2560]{1,0:T(8,128)S(1)}, f32[128,2560]{1,0:T(8,128)S(1)}, f32[128,2560]{1,0:T(8,128)S(1)}, f32[256,128]{1,0:T(8,128)S(1)}, f32[256,256]{1,0:T(8,128)S(1)}) custom-call(s32[3]{0:T(128)S(1)} %copy-done.12, f32[648,128]{1,0:T(8,128)S(1)} %get-tuple-element.113.refs_1_.refs_2_, bf16[256,2560]{1,0:T(8,128)(2,1)S(1)} %copy-done, ...), custom_call_target="tpu_custom_call" | custom-call | flops 1 | bytes 1 | tf_op jit(solution)/shard_map/intra/pallas_call | solution.py:433
  17.3 1.9 %collective-permute-done.1.refs_3_ = f32[648,128]{1,0:T(8,128)S(1)} collective-permute-done((f32[648,128]{1,0:T(8,128)S(1)}, f32[648,128]{1,0:T(8,128)S(1)}, u32[]{:S(2)}, u32[]{:S(2)}) %collective-permute-start.1) | collective-permute-done | bytes 331808 | tf_op jit(solution)/shard_map/ppermute | solution.py:683
  19.3 0.7 combine.3
  19.9 1.4 %collective-permute-start.4 = (f32[648,128]{1,0:T(8,128)S(1)}, f32[648,128]{1,0:T(8,128)S(1)}, u32[]{:S(2)}, u32[]{:S(2)}) collective-permute-start(f32[648,128]{1,0:T(8,128)S(1)} %get-tuple-element.127.refs_2_), channel_id=1, source_target_pairs={{0,2},{1,3},{2,0},{3,1},{4,6},{5,7},{6,4},{7,5},{8,10},{9,11},{10,... | collective-permute-start | bytes 995336 | tf_op jit(solution)/shard_map/ppermute | solution.py:683
  21.3 0.8 up.4
  22.0 2.4 %collective-permute-start.3 = (f32[328,128]{1,0:T(8,128)S(1)}, f32[328,128]{1,0:T(8,128)S(1)}, u32[]{:S(2)}, u32[]{:S(2)}) collective-permute-start(f32[328,128]{1,0:T(8,128)S(1)} %get-tuple-element.123.refs_1_.refs_2_), channel_id=1, source_target_pairs={{0,4},{1,5},{2,6},{3,7},{4,0},{5,1},{6,2},{7,3},{8,12},{9,13},{10,... | collective-permute-start | bytes 503816 | tf_op jit(solution)/shard_map/ppermute | solution.py:683
  24.4 5.5 %intra.4 = (f32[256,2560]{1,0:T(8,128)S(1)}, f32[128,2560]{1,0:T(8,128)S(1)}, f32[128,2560]{1,0:T(8,128)S(1)}, f32[256,128]{1,0:T(8,128)S(1)}, f32[256,256]{1,0:T(8,128)S(1)}) custom-call(s32[3]{0:T(128)S(1)} %copy-done.12, f32[328,128]{1,0:T(8,128)S(1)} %get-tuple-element.123.refs_1_.refs_2_, ...), custom_call_target="tpu_custom_call", output_to_operand_aliasing={{0}: (10, {}), {1}: (11, {}), {2}: (12, {})} | custom-call | flops 1 | bytes 1 | tf_op jit(solution)/shard_map/intra/pallas_call | solution.py:433
  29.9 0.7 collective-permute-done.3.refs_3_
  30.6 0.9 collective-permute-done.4.refs_3_
  31.5 0.8 up.6
  32.3 2.0 %collective-permute-start.8 = (f32[328,128]{1,0:T(8,128)S(1)}, f32[328,128]{1,0:T(8,128)S(1)}, u32[]{:S(2)}, u32[]{:S(2)}) collective-permute-start(f32[328,128]{1,0:T(8,128)S(1)} %get-tuple-element.141.refs_2_), channel_id=1, source_target_pairs={{0,4},{1,5},{2,6},{3,7},{4,0},{5,1},{6,2},{7,3},{8,12},{9,13},{10,... | collective-permute-start | bytes 503816 | tf_op jit(solution)/shard_map/ppermute | solution.py:683
  34.3 0.7 up.5.refs_1_
  35.0 1.3 %collective-permute-start.5 = (f32[328,128]{1,0:T(8,128)S(1)}, f32[328,128]{1,0:T(8,128)S(1)}, u32[]{:S(2)}, u32[]{:S(2)}) collective-permute-start(f32[328,128]{1,0:T(8,128)S(1)} %up.5.refs_1_), channel_id=1, source_target_pairs={{1,9},{3,11},{5,13},{7,15},{8,0},{9,17},{10,2},{11,19},{12,4},{13,... | collective-permute-start | bytes 503816 | tf_op jit(solution)/shard_map/ppermute | solution.py:683
  36.3 1.3 %collective-permute-start.6 = (f32[328,128]{1,0:T(8,128)S(1)}, f32[328,128]{1,0:T(8,128)S(1)}, u32[]{:S(2)}, u32[]{:S(2)}) collective-permute-start(f32[328,128]{1,0:T(8,128)S(1)} %up.5.refs_1_), channel_id=1, source_target_pairs={{1,17},{3,19},{5,21},{7,23},{9,25},{11,27},{13,29},{15,31},{16,0},... | collective-permute-start | bytes 503816 | tf_op jit(solution)/shard_map/ppermute | solution.py:683
  37.6 1.3 %collective-permute-start.7 = (f32[328,128]{1,0:T(8,128)S(1)}, f32[328,128]{1,0:T(8,128)S(1)}, u32[]{:S(2)}, u32[]{:S(2)}) collective-permute-start(f32[328,128]{1,0:T(8,128)S(1)} %up.5.refs_1_), channel_id=1, source_target_pairs={{1,25},{3,27},{5,29},{7,31},{24,0},{26,2},{28,4},{30,6}} | collective-permute-start | bytes 503816 | tf_op jit(solution)/shard_map/ppermute | solution.py:683
  38.9 3.0 %intra.5 = (f32[256,2560]{1,0:T(8,128)S(1)}, f32[128,2560]{1,0:T(8,128)S(1)}, f32[128,2560]{1,0:T(8,128)S(1)}, f32[256,128]{1,0:T(8,128)S(1)}, f32[256,128]{1,0:T(8,128)S(1)}, /*index=5*/f32[256,128]{1,0:T(8,128)S(1)}) custom-call(s32[3]{0:T(128)S(1)} %copy-done.12, ...), custom_call_target="tpu_custom_call", output_to_operand_aliasing={{0}: (10, {}), {1}: (11, {}), {2}: (12, {})} | custom-call | flops 1 | bytes 1 | tf_op jit(solution)/shard_map/intra/pallas_call | solution.py:433
  41.9 0.7 collective-permute-done.6.refs_5_
  42.7 2.8 %collective-permute-done.7.refs_6_ = f32[328,128]{1,0:T(8,128)S(1)} collective-permute-done((f32[328,128]{1,0:T(8,128)S(1)}, f32[328,128]{1,0:T(8,128)S(1)}, u32[]{:S(2)}, u32[]{:S(2)}) %collective-permute-start.7) | collective-permute-done | bytes 167968 | tf_op jit(solution)/shard_map/ppermute | solution.py:683
  45.5 1.6 %collective-permute-start.16 = (f32[128,2560]{1,0:T(8,128)S(1)}, f32[128,2560]{1,0:T(8,128)S(1)}, u32[]{:S(2)}, u32[]{:S(2)}) collective-permute-start(f32[128,2560]{1,0:T(8,128)S(1)} %get-tuple-element.184), channel_id=1, source_target_pairs={{0,1},{1,0},{2,3},{3,2},{4,5},{5,4},{6,7},{7,6},{8,9},{9,8},{10,11... | collective-permute-start | bytes 3932168 | tf_op jit(solution)/shard_map/ppermute | solution.py:683
  47.1 0.8 down.4
  47.9 0.7 up.7
  48.7 1.3 %collective-permute-start.10 = (f32[328,128]{1,0:T(8,128)S(1)}, f32[328,128]{1,0:T(8,128)S(1)}, u32[]{:S(2)}, u32[]{:S(2)}) collective-permute-start(f32[328,128]{1,0:T(8,128)S(1)} %up.7), channel_id=1, source_target_pairs={{1,9},{3,11},{5,13},{7,15},{8,0},{9,17},{10,2},{11,19},{12,4},{13,... | collective-permute-start | bytes 503816 | tf_op jit(solution)/shard_map/ppermute | solution.py:683
  50.0 1.3 %collective-permute-start.11 = (f32[328,128]{1,0:T(8,128)S(1)}, f32[328,128]{1,0:T(8,128)S(1)}, u32[]{:S(2)}, u32[]{:S(2)}) collective-permute-start(f32[328,128]{1,0:T(8,128)S(1)} %up.7), channel_id=1, source_target_pairs={{1,17},{3,19},{5,21},{7,23},{9,25},{11,27},{13,29},{15,31},{16,0},... | collective-permute-start | bytes 503816 | tf_op jit(solution)/shard_map/ppermute | solution.py:683
  51.3 1.5 %collective-permute-start.12 = (f32[328,128]{1,0:T(8,128)S(1)}, f32[328,128]{1,0:T(8,128)S(1)}, u32[]{:S(2)}, u32[]{:S(2)}) collective-permute-start(f32[328,128]{1,0:T(8,128)S(1)} %up.7), channel_id=1, source_target_pairs={{1,25},{3,27},{5,29},{7,31},{24,0},{26,2},{28,4},{30,6}} | collective-permute-start | bytes 503816 | tf_op jit(solution)/shard_map/ppermute | solution.py:683
  53.2 6.5 %collective-permute-done.9.refs_5_ = f32[320,128]{1,0:T(8,128)S(1)} collective-permute-done((f32[320,128]{1,0:T(8,128)S(1)}, f32[320,128]{1,0:T(8,128)S(1)}, u32[]{:S(2)}, u32[]{:S(2)}) %collective-permute-start.9) | collective-permute-done | bytes 163872 | tf_op jit(solution)/shard_map/ppermute | solution.py:683
  59.7 0.8 down.5
  60.5 1.0 collective-permute-start.13
  61.5 0.8 down.6
  62.3 1.1 collective-permute-start.14
  63.4 4.1 %collective-permute-done.14.refs_5_ = f32[320,128]{1,0:T(8,128)S(1)} collective-permute-done((f32[320,128]{1,0:T(8,128)S(1)}, f32[320,128]{1,0:T(8,128)S(1)}, u32[]{:S(2)}, u32[]{:S(2)}) %collective-permute-start.14) | collective-permute-done | bytes 163872 | tf_op jit(solution)/shard_map/ppermute | solution.py:683
  67.5 1.2 %collective-permute-done.13.got_ref = f32[640,128]{1,0:T(8,128)S(1)} collective-permute-done((f32[640,128]{1,0:T(8,128)S(1)}, f32[640,128]{1,0:T(8,128)S(1)}, u32[]{:S(2)}, u32[]{:S(2)}) %collective-permute-start.13) | collective-permute-done | bytes 327712 | tf_op jit(solution)/shard_map/ppermute | solution.py:683
  68.7 0.8 down.7
  70.1 7.9 %collective-permute-start.15 = (f32[1280,128]{1,0:T(8,128)S(1)}, f32[1280,128]{1,0:T(8,128)S(1)}, u32[]{:S(2)}, u32[]{:S(2)}) collective-permute-start(f32[1280,128]{1,0:T(8,128)S(1)} %order.2.refs_3_.refs_2_), channel_id=1, source_target_pairs={{0,1},{1,0},{2,3},{3,2},{4,5},{5,4},{6,7},{7,6},{8,9},{9,8},{10,11... | collective-permute-start | bytes 1966088 | tf_op jit(solution)/shard_map/ppermute | solution.py:683
  78.1 1.7 %collective-permute-done.15.refs_4_ = f32[1280,128]{1,0:T(8,128)S(1)} collective-permute-done((f32[1280,128]{1,0:T(8,128)S(1)}, f32[1280,128]{1,0:T(8,128)S(1)}, u32[]{:S(2)}, u32[]{:S(2)}) %collective-permute-start.15) | collective-permute-done | bytes 655392 | tf_op jit(solution)/shard_map/ppermute | solution.py:683
  79.8 0.9 assemble.2
  80.7 3.8 %finish.3 = (bf16[256,2560]{1,0:T(8,128)(2,1)}, f32[256,128]{1,0:T(8,128)S(1)}, f32[256,128]{1,0:T(8,128)S(1)}, f32[256,128]{1,0:T(8,128)S(1)}) custom-call(bf16[256,2560]{1,0:T(8,128)(2,1)S(1)} %copy-done, bf16[256,2560]{1,0:T(8,128)(2,1)S(1)} %copy-done.1, bf16[256,128]{1,0:T(8,128)(2,1)S(1)} %copy-done.4, bf16[256,128]{1,0:T(8,128)(2,1)S(1)} %copy-done.5, ...), custom_call_target="tpu_custom_call" | custom-call | flops 1 | bytes 1 | tf_op jit(solution)/shard_map/finish/pallas_call | solution.py:624
  84.5 1.2 tally.2
  85.6 1.7 %collective-permute-done.17.got_ref = f32[640,128]{1,0:T(8,128)S(1)} collective-permute-done((f32[640,128]{1,0:T(8,128)S(1)}, f32[640,128]{1,0:T(8,128)S(1)}, u32[]{:S(2)}, u32[]{:S(2)}) %collective-permute-start.17) | collective-permute-done | bytes 327712 | tf_op jit(solution)/shard_map/ppermute | solution.py:683
  87.9 0.9 collective-permute-start.18
  88.9 1.2 tally.3
  90.2 1.1 collective-permute-start.20
  91.3 2.4 %collective-permute-start.21 = (f32[8,128]{1,0:T(8,128)S(1)}, f32[8,128]{1,0:T(8,128)S(1)}, u32[]{:S(2)}, u32[]{:S(2)}) collective-permute-start(f32[8,128]{1,0:T(8,128)S(1)} %add.27.refs_1_), channel_id=1, source_target_pairs={{0,6},{1,7},{2,4},{3,5},{4,2},{5,3},{6,0},{7,1},{8,14},{9,15},{10,... | collective-permute-start | bytes 12296 | tf_op jit(solution)/shard_map/ppermute | solution.py:683
  93.7 0.9 assemble.3
  94.6 1.8 %finish.4 = (bf16[256,2560]{1,0:T(8,128)(2,1)}, f32[256,128]{1,0:T(8,128)S(1)}, f32[256,128]{1,0:T(8,128)S(1)}, f32[256,128]{1,0:T(8,128)S(1)}) custom-call(bf16[256,2560]{1,0:T(8,128)(2,1)S(1)} %copy-done, bf16[256,2560]{1,0:T(8,128)(2,1)S(1)} %copy-done.1, bf16[256,128]{1,0:T(8,128)(2,1)S(1)} %copy-done.4, ...), custom_call_target="tpu_custom_call", output_to_operand_aliasing={{0}: (12, {})} | custom-call | flops 1 | bytes 1 | tf_op jit(solution)/shard_map/finish/pallas_call | solution.py:624
  96.4 0.6 copy-done.13
  97.0 0.6 copy-done.15
  97.6 0.7 copy-done.17
  99.5 4.0 %collective-permute-start.22 = (f32[8,128]{1,0:T(8,128)}, f32[8,128]{1,0:T(8,128)}, u32[]{:S(2)}, u32[]{:S(2)}) collective-permute-start(f32[8,128]{1,0:T(8,128)} %add_add_fusion), channel_id=1, source_target_pairs={{8,0},{9,1},{10,2},{11,3},{12,4},{13,5},{14,6},{15,7},{16,8},{17,9... | collective-permute-start | bytes 12296 | tf_op jit(solution)/shard_map/ppermute | solution.py:683
  103.5 5.0 %collective-permute-start.23 = (f32[8,128]{1,0:T(8,128)}, f32[8,128]{1,0:T(8,128)}, u32[]{:S(2)}, u32[]{:S(2)}) collective-permute-start(f32[8,128]{1,0:T(8,128)} %add_add_fusion), channel_id=1, source_target_pairs={{16,0},{17,1},{18,2},{19,3},{20,4},{21,5},{22,6},{23,7},{24,8},{25... | collective-permute-start | bytes 12296 | tf_op jit(solution)/shard_map/ppermute | solution.py:683
  108.5 1.9 %collective-permute-start.24 = (f32[8,128]{1,0:T(8,128)}, f32[8,128]{1,0:T(8,128)}, u32[]{:S(2)}, u32[]{:S(2)}) collective-permute-start(f32[8,128]{1,0:T(8,128)} %add_add_fusion), channel_id=1, source_target_pairs={{24,0},{25,1},{26,2},{27,3},{28,4},{29,5},{30,6},{31,7}} | collective-permute-start | bytes 12296 | tf_op jit(solution)/shard_map/ppermute | solution.py:683
  110.9 1.7 %copy-done.3 = f32[256,2560]{1,0:T(8,128)S(1)} copy-done((f32[256,2560]{1,0:T(8,128)S(1)}, f32[256,2560]{1,0:T(8,128)}, u32[]{:S(2)}) %copy-start.3) | copy-done | bytes 2621464
  112.7 0.9 copy-done.14
  113.6 0.9 copy-done.16
  114.5 0.9 copy-done.18
  115.4 1.8 %finish.5 = (bf16[256,2560]{1,0:T(8,128)(2,1)}, bf16[256,128]{1,0:T(8,128)(2,1)}, bf16[256,128]{1,0:T(8,128)(2,1)}, f32[40,256]{1,0:T(8,128)S(1)}) custom-call(bf16[256,2560]{1,0:T(8,128)(2,1)S(1)} %copy-done, bf16[256,2560]{1,0:T(8,128)(2,1)S(1)} %copy-done.1, bf16[256,128]{1,0:T(8,128)(2,1)S(1)} %copy-done.4, ...), custom_call_target="tpu_custom_call", output_to_operand_aliasing={{0}: (12, {})} | custom-call | flops 1 | bytes 1 | tf_op jit(solution)/shard_map/finish/pallas_call | solution.py:624
  117.8 0.8 add_select_fusion.mine_ref
  118.6 1.4 %collective-permute-start.25 = (f32[8,128]{1,0:T(8,128)S(1)}, f32[8,128]{1,0:T(8,128)S(1)}, u32[]{:S(2)}, u32[]{:S(2)}) collective-permute-start(f32[8,128]{1,0:T(8,128)S(1)} %add_select_fusion.mine_ref), channel_id=1, source_target_pairs={{0,1},{1,0},{2,3},{3,2},{4,5},{5,4},{6,7},{7,6},{8,9},{9,8},{10,11... | collective-permute-start | bytes 12296 | tf_op jit(solution)/shard_map/ppermute | solution.py:683
  120.0 0.8 collective-permute-done.25.other_ref
  121.5 1.6 %add_later.1 = f32[40,256]{1,0:T(8,128)} custom-call(s32[3]{0:T(128)} %pad_add_fusion.refs_0_.place, f32[40,256]{1,0:T(8,128)} %copy-done.19, f32[8,128]{1,0:T(8,128)} %copy-done.25, f32[8,128]{1,0:T(8,128)} %copy-done.26), custom_call_target="tpu_custom_call" | custom-call | flops 1 | bytes 1 | tf_op jit(solution)/shard_map/add_later/pallas_call | solution.py:656
  (74 shorter events, 5.4 us)
Async XLA Ops:
  5.0 4.6 %collective-permute-start = (f32[1288,128]{1,0:T(8,128)}, f32[1288,128]{1,0:T(8,128)S(1)}, u32[]{:S(2)}, u32[]{:S(2)}) collective-permute-start(f32[1288,128]{1,0:T(8,128)} %get-tuple-element.108), channel_id=1, source_target_pairs={{0,1},{1,0},{2,3},{3,2},{4,5},{5,4},{6,7},{7,6},{8,9},{9,8},{10,11... | collective-permute-start | bytes 1978376 | tf_op jit(solution)/shard_map/ppermute | solution.py:683
  5.7 3.9 %copy-start.11 = (f32[1280,128]{1,0:T(8,128)S(1)}, f32[1280,128]{1,0:T(8,128)}, u32[]{:S(2)}) copy-start(f32[1280,128]{1,0:T(8,128)} %get-tuple-element.109.refs_2_) | copy-start | bytes 1966084
  5.7 3.9 %copy-start.12 = (s32[3]{0:T(128)S(1)}, s32[3]{0:T(128)}, u32[]{:S(2)}) copy-start(s32[3]{0:T(128)} %pad_add_fusion.refs_0_.place) | copy-start | bytes 40
  5.7 3.9 %copy-start.20 = (f32[8,128]{1,0:T(8,128)S(1)}, f32[8,128]{1,0:T(8,128)}, u32[]{:S(2)}) copy-start(f32[8,128]{1,0:T(8,128)} %get-tuple-element.111.refs_4_.refs_5_) | copy-start | bytes 12292
  5.7 3.9 %copy-start.22 = (f32[10,128]{1,0:T(8,128)S(1)}, f32[10,128]{1,0:T(8,128)}, u32[]{:S(2)}) copy-start(f32[10,128]{1,0:T(8,128)} %get-tuple-element.110.refs_3_) | copy-start | bytes 15364
  5.7 5.9 %copy-start.1 = (bf16[256,2560]{1,0:T(8,128)(2,1)S(1)}, bf16[256,2560]{1,0:T(8,128)(2,1)}, u32[]{:S(2)}) copy-start(bf16[256,2560]{1,0:T(8,128)(2,1)} %refs_1_.9) | copy-start | bytes 3932164
  5.7 5.9 %copy-start.4 = (bf16[256,128]{1,0:T(8,128)(2,1)S(1)}, bf16[256,128]{1,0:T(8,128)(2,1)}, u32[]{:S(2)}) copy-start(bf16[256,128]{1,0:T(8,128)(2,1)} %refs_2_.15) | copy-start | bytes 196612
  5.8 5.9 %copy-start.5 = (bf16[256,128]{1,0:T(8,128)(2,1)S(1)}, bf16[256,128]{1,0:T(8,128)(2,1)}, u32[]{:S(2)}) copy-start(bf16[256,128]{1,0:T(8,128)(2,1)} %refs_3_.15) | copy-start | bytes 196612
  5.8 5.9 %copy-start.6 = (bf16[256,128]{1,0:T(8,128)(2,1)S(1)}, bf16[256,128]{1,0:T(8,128)(2,1)}, u32[]{:S(2)}) copy-start(bf16[256,128]{1,0:T(8,128)(2,1)} %get-tuple-element.106.refs_6_.refs_8_.refs_4_) | copy-start | bytes 196612
  5.8 5.9 %copy-start.7 = (bf16[256,128]{1,0:T(8,128)(2,1)S(1)}, bf16[256,128]{1,0:T(8,128)(2,1)}, u32[]{:S(2)}) copy-start(bf16[256,128]{1,0:T(8,128)(2,1)} %get-tuple-element.107.refs_7_.refs_9_.refs_5_) | copy-start | bytes 196612
  5.8 5.9 %copy-start.8 = (f32[256,128]{1,0:T(8,128)S(1)}, f32[256,128]{1,0:T(8,128)}, u32[]{:S(2)}) copy-start(f32[256,128]{1,0:T(8,128)} %get-tuple-element.115.refs_7_) | copy-start | bytes 393220
  5.8 5.9 %copy-start.9 = (f32[40,256]{1,0:T(8,128)S(1)}, f32[40,256]{1,0:T(8,128)}, u32[]{:S(2)}) copy-start(f32[40,256]{1,0:T(8,128)} %refs_6_.5) | copy-start | bytes 122884
  9.5 2.2 %copy-start = (bf16[256,2560]{1,0:T(8,128)(2,1)S(1)}, bf16[256,2560]{1,0:T(8,128)(2,1)}, u32[]{:S(2)}) copy-start(bf16[256,2560]{1,0:T(8,128)(2,1)} %refs_0_.5) | copy-start | bytes 3932164
  9.5 7.8 %collective-permute-start.2 = (f32[1288,128]{1,0:T(8,128)}, f32[1288,128]{1,0:T(8,128)S(1)}, u32[]{:S(2)}, u32[]{:S(2)}) collective-permute-start(f32[1288,128]{1,0:T(8,128)} %get-tuple-element.114), channel_id=1, source_target_pairs={{0,1},{1,0},{2,3},{3,2},{4,5},{5,4},{6,7},{7,6},{8,9},{9,8},{10,11... | collective-permute-start | bytes 1978376 | tf_op jit(solution)/shard_map/ppermute | solution.py:683
  10.3 9.0 %collective-permute-start.1 = (f32[648,128]{1,0:T(8,128)S(1)}, f32[648,128]{1,0:T(8,128)S(1)}, u32[]{:S(2)}, u32[]{:S(2)}) collective-permute-start(f32[648,128]{1,0:T(8,128)S(1)} %get-tuple-element.113.refs_1_.refs_2_), channel_id=1, source_target_pairs={{0,2},{1,3},{2,0},{3,1},{4,6},{5,7},{6,4},{7,5},{8,10},{9,11},{10,... | collective-permute-start | bytes 995336 | tf_op jit(solution)/shard_map/ppermute | solution.py:683
  11.7 7.6 %copy-start.10 = (f32[1280,128]{1,0:T(8,128)S(1)}, f32[1280,128]{1,0:T(8,128)}, u32[]{:S(2)}) copy-start(f32[1280,128]{1,0:T(8,128)} %get-tuple-element.125.refs_2_) | copy-start | bytes 1966084
  11.7 7.5 %copy-start.21 = (f32[10,128]{1,0:T(8,128)S(1)}, f32[10,128]{1,0:T(8,128)}, u32[]{:S(2)}) copy-start(f32[10,128]{1,0:T(8,128)} %get-tuple-element.126.refs_3_) | copy-start | bytes 15364
  19.9 11.6 %collective-permute-start.4 = (f32[648,128]{1,0:T(8,128)S(1)}, f32[648,128]{1,0:T(8,128)S(1)}, u32[]{:S(2)}, u32[]{:S(2)}) collective-permute-start(f32[648,128]{1,0:T(8,128)S(1)} %get-tuple-element.127.refs_2_), channel_id=1, source_target_pairs={{0,2},{1,3},{2,0},{3,1},{4,6},{5,7},{6,4},{7,5},{8,10},{9,11},{10,... | collective-permute-start | bytes 995336 | tf_op jit(solution)/shard_map/ppermute | solution.py:683
  22.0 8.6 %collective-permute-start.3 = (f32[328,128]{1,0:T(8,128)S(1)}, f32[328,128]{1,0:T(8,128)S(1)}, u32[]{:S(2)}, u32[]{:S(2)}) collective-permute-start(f32[328,128]{1,0:T(8,128)S(1)} %get-tuple-element.123.refs_1_.refs_2_), channel_id=1, source_target_pairs={{0,4},{1,5},{2,6},{3,7},{4,0},{5,1},{6,2},{7,3},{8,12},{9,13},{10,... | collective-permute-start | bytes 503816 | tf_op jit(solution)/shard_map/ppermute | solution.py:683
  32.3 9.6 %collective-permute-start.8 = (f32[328,128]{1,0:T(8,128)S(1)}, f32[328,128]{1,0:T(8,128)S(1)}, u32[]{:S(2)}, u32[]{:S(2)}) collective-permute-start(f32[328,128]{1,0:T(8,128)S(1)} %get-tuple-element.141.refs_2_), channel_id=1, source_target_pairs={{0,4},{1,5},{2,6},{3,7},{4,0},{5,1},{6,2},{7,3},{8,12},{9,13},{10,... | collective-permute-start | bytes 503816 | tf_op jit(solution)/shard_map/ppermute | solution.py:683
  35.0 6.9 %collective-permute-start.5 = (f32[328,128]{1,0:T(8,128)S(1)}, f32[328,128]{1,0:T(8,128)S(1)}, u32[]{:S(2)}, u32[]{:S(2)}) collective-permute-start(f32[328,128]{1,0:T(8,128)S(1)} %up.5.refs_1_), channel_id=1, source_target_pairs={{1,9},{3,11},{5,13},{7,15},{8,0},{9,17},{10,2},{11,19},{12,4},{13,... | collective-permute-start | bytes 503816 | tf_op jit(solution)/shard_map/ppermute | solution.py:683
  36.3 6.4 %collective-permute-start.6 = (f32[328,128]{1,0:T(8,128)S(1)}, f32[328,128]{1,0:T(8,128)S(1)}, u32[]{:S(2)}, u32[]{:S(2)}) collective-permute-start(f32[328,128]{1,0:T(8,128)S(1)} %up.5.refs_1_), channel_id=1, source_target_pairs={{1,17},{3,19},{5,21},{7,23},{9,25},{11,27},{13,29},{15,31},{16,0},... | collective-permute-start | bytes 503816 | tf_op jit(solution)/shard_map/ppermute | solution.py:683
  37.6 7.9 %collective-permute-start.7 = (f32[328,128]{1,0:T(8,128)S(1)}, f32[328,128]{1,0:T(8,128)S(1)}, u32[]{:S(2)}, u32[]{:S(2)}) collective-permute-start(f32[328,128]{1,0:T(8,128)S(1)} %up.5.refs_1_), channel_id=1, source_target_pairs={{1,25},{3,27},{5,29},{7,31},{24,0},{26,2},{28,4},{30,6}} | collective-permute-start | bytes 503816 | tf_op jit(solution)/shard_map/ppermute | solution.py:683
  41.9 52.7 %copy-start.2 = (f32[256,2560]{1,0:T(8,128)}, f32[256,2560]{1,0:T(8,128)S(1)}, u32[]{:S(2)}) copy-start(f32[256,2560]{1,0:T(8,128)S(1)} %get-tuple-element.154.refs_6_) | copy-start | bytes 7864324
  45.5 38.9 %collective-permute-start.16 = (f32[128,2560]{1,0:T(8,128)S(1)}, f32[128,2560]{1,0:T(8,128)S(1)}, u32[]{:S(2)}, u32[]{:S(2)}) collective-permute-start(f32[128,2560]{1,0:T(8,128)S(1)} %get-tuple-element.184), channel_id=1, source_target_pairs={{0,1},{1,0},{2,3},{3,2},{4,5},{5,4},{6,7},{7,6},{8,9},{9,8},{10,11... | collective-permute-start | bytes 3932168 | tf_op jit(solution)/shard_map/ppermute | solution.py:683
  48.7 11.0 %collective-permute-start.10 = (f32[328,128]{1,0:T(8,128)S(1)}, f32[328,128]{1,0:T(8,128)S(1)}, u32[]{:S(2)}, u32[]{:S(2)}) collective-permute-start(f32[328,128]{1,0:T(8,128)S(1)} %up.7), channel_id=1, source_target_pairs={{1,9},{3,11},{5,13},{7,15},{8,0},{9,17},{10,2},{11,19},{12,4},{13,... | collective-permute-start | bytes 503816 | tf_op jit(solution)/shard_map/ppermute | solution.py:683
  50.0 9.7 %collective-permute-start.11 = (f32[328,128]{1,0:T(8,128)S(1)}, f32[328,128]{1,0:T(8,128)S(1)}, u32[]{:S(2)}, u32[]{:S(2)}) collective-permute-start(f32[328,128]{1,0:T(8,128)S(1)} %up.7), channel_id=1, source_target_pairs={{1,17},{3,19},{5,21},{7,23},{9,25},{11,27},{13,29},{15,31},{16,0},... | collective-permute-start | bytes 503816 | tf_op jit(solution)/shard_map/ppermute | solution.py:683
  51.3 8.4 %collective-permute-start.12 = (f32[328,128]{1,0:T(8,128)S(1)}, f32[328,128]{1,0:T(8,128)S(1)}, u32[]{:S(2)}, u32[]{:S(2)}) collective-permute-start(f32[328,128]{1,0:T(8,128)S(1)} %up.7), channel_id=1, source_target_pairs={{1,25},{3,27},{5,29},{7,31},{24,0},{26,2},{28,4},{30,6}} | collective-permute-start | bytes 503816 | tf_op jit(solution)/shard_map/ppermute | solution.py:683
  52.8 6.9 %collective-permute-start.9 = (f32[320,128]{1,0:T(8,128)S(1)}, f32[320,128]{1,0:T(8,128)S(1)}, u32[]{:S(2)}, u32[]{:S(2)}) collective-permute-start(f32[320,128]{1,0:T(8,128)S(1)} %get-tuple-element.162), channel_id=1, source_target_pairs={{0,4},{1,5},{2,6},{3,7},{4,0},{5,1},{6,2},{7,3},{8,12},{9,13},{10,... | collective-permute-start | bytes 491528 | tf_op jit(solution)/shard_map/ppermute | solution.py:683
  60.5 8.3 %collective-permute-start.13 = (f32[640,128]{1,0:T(8,128)S(1)}, f32[640,128]{1,0:T(8,128)S(1)}, u32[]{:S(2)}, u32[]{:S(2)}) collective-permute-start(f32[640,128]{1,0:T(8,128)S(1)} %get-tuple-element.168), channel_id=1, source_target_pairs={{0,2},{1,3},{2,0},{3,1},{4,6},{5,7},{6,4},{7,5},{8,10},{9,11},{10,... | collective-permute-start | bytes 983048 | tf_op jit(solution)/shard_map/ppermute | solution.py:683
  62.3 5.2 %collective-permute-start.14 = (f32[320,128]{1,0:T(8,128)S(1)}, f32[320,128]{1,0:T(8,128)S(1)}, u32[]{:S(2)}, u32[]{:S(2)}) collective-permute-start(f32[320,128]{1,0:T(8,128)S(1)} %get-tuple-element.172), channel_id=1, source_target_pairs={{0,4},{1,5},{2,6},{3,7},{4,0},{5,1},{6,2},{7,3},{8,12},{9,13},{10,... | collective-permute-start | bytes 491528 | tf_op jit(solution)/shard_map/ppermute | solution.py:683
  70.1 9.7 %collective-permute-start.15 = (f32[1280,128]{1,0:T(8,128)S(1)}, f32[1280,128]{1,0:T(8,128)S(1)}, u32[]{:S(2)}, u32[]{:S(2)}) collective-permute-start(f32[1280,128]{1,0:T(8,128)S(1)} %order.2.refs_3_.refs_2_), channel_id=1, source_target_pairs={{0,1},{1,0},{2,3},{3,2},{4,5},{5,4},{6,7},{7,6},{8,9},{9,8},{10,11... | collective-permute-start | bytes 1966088 | tf_op jit(solution)/shard_map/ppermute | solution.py:683
  78.1 9.3 %collective-permute-start.17 = (f32[640,128]{1,0:T(8,128)S(1)}, f32[640,128]{1,0:T(8,128)S(1)}, u32[]{:S(2)}, u32[]{:S(2)}) collective-permute-start(f32[640,128]{1,0:T(8,128)S(1)} %get-tuple-element.176), channel_id=1, source_target_pairs={{0,2},{1,3},{2,0},{3,1},{4,6},{5,7},{6,4},{7,5},{8,10},{9,11},{10,... | collective-permute-start | bytes 983048 | tf_op jit(solution)/shard_map/ppermute | solution.py:683
  87.9 5.8 %collective-permute-start.18 = (f32[1280,128]{1,0:T(8,128)S(1)}, f32[1280,128]{1,0:T(8,128)S(1)}, u32[]{:S(2)}, u32[]{:S(2)}) collective-permute-start(f32[1280,128]{1,0:T(8,128)S(1)} %order.3.refs_2_.refs_3_), channel_id=1, source_target_pairs={{0,1},{1,0},{2,3},{3,2},{4,5},{5,4},{6,7},{7,6},{8,9},{9,8},{10,11... | collective-permute-start | bytes 1966088 | tf_op jit(solution)/shard_map/ppermute | solution.py:683
  90.1 8.2 %collective-permute-start.19 = (f32[8,128]{1,0:T(8,128)S(1)}, f32[8,128]{1,0:T(8,128)S(1)}, u32[]{:S(2)}, u32[]{:S(2)}) collective-permute-start(f32[8,128]{1,0:T(8,128)S(1)} %add.27.refs_1_), channel_id=1, source_target_pairs={{0,2},{1,3},{2,0},{3,1},{4,6},{5,7},{6,4},{7,5},{8,10},{9,11},{10,... | collective-permute-start | bytes 12296 | tf_op jit(solution)/shard_map/ppermute | solution.py:683
  90.2 8.1 %collective-permute-start.20 = (f32[8,128]{1,0:T(8,128)S(1)}, f32[8,128]{1,0:T(8,128)S(1)}, u32[]{:S(2)}, u32[]{:S(2)}) collective-permute-start(f32[8,128]{1,0:T(8,128)S(1)} %add.27.refs_1_), channel_id=1, source_target_pairs={{0,4},{1,5},{2,6},{3,7},{4,0},{5,1},{6,2},{7,3},{8,12},{9,13},{10,... | collective-permute-start | bytes 12296 | tf_op jit(solution)/shard_map/ppermute | solution.py:683
  91.3 7.0 %collective-permute-start.21 = (f32[8,128]{1,0:T(8,128)S(1)}, f32[8,128]{1,0:T(8,128)S(1)}, u32[]{:S(2)}, u32[]{:S(2)}) collective-permute-start(f32[8,128]{1,0:T(8,128)S(1)} %add.27.refs_1_), channel_id=1, source_target_pairs={{0,6},{1,7},{2,4},{3,5},{4,2},{5,3},{6,0},{7,1},{8,14},{9,15},{10,... | collective-permute-start | bytes 12296 | tf_op jit(solution)/shard_map/ppermute | solution.py:683
  96.3 0.6 copy-start.13
  97.0 0.6 copy-start.15
  97.6 0.7 copy-start.17
  98.3 0.6 copy-start.23
  99.5 18.3 %collective-permute-start.22 = (f32[8,128]{1,0:T(8,128)}, f32[8,128]{1,0:T(8,128)}, u32[]{:S(2)}, u32[]{:S(2)}) collective-permute-start(f32[8,128]{1,0:T(8,128)} %add_add_fusion), channel_id=1, source_target_pairs={{8,0},{9,1},{10,2},{11,3},{12,4},{13,5},{14,6},{15,7},{16,8},{17,9... | collective-permute-start | bytes 12296 | tf_op jit(solution)/shard_map/ppermute | solution.py:683
  103.5 14.3 %collective-permute-start.23 = (f32[8,128]{1,0:T(8,128)}, f32[8,128]{1,0:T(8,128)}, u32[]{:S(2)}, u32[]{:S(2)}) collective-permute-start(f32[8,128]{1,0:T(8,128)} %add_add_fusion), channel_id=1, source_target_pairs={{16,0},{17,1},{18,2},{19,3},{20,4},{21,5},{22,6},{23,7},{24,8},{25... | collective-permute-start | bytes 12296 | tf_op jit(solution)/shard_map/ppermute | solution.py:683
  108.5 9.3 %collective-permute-start.24 = (f32[8,128]{1,0:T(8,128)}, f32[8,128]{1,0:T(8,128)}, u32[]{:S(2)}, u32[]{:S(2)}) collective-permute-start(f32[8,128]{1,0:T(8,128)} %add_add_fusion), channel_id=1, source_target_pairs={{24,0},{25,1},{26,2},{27,3},{28,4},{29,5},{30,6},{31,7}} | collective-permute-start | bytes 12296 | tf_op jit(solution)/shard_map/ppermute | solution.py:683
  110.9 1.7 %copy-start.3 = (f32[256,2560]{1,0:T(8,128)S(1)}, f32[256,2560]{1,0:T(8,128)}, u32[]{:S(2)}) copy-start(f32[256,2560]{1,0:T(8,128)} %copy-done.2) | copy-start | bytes 7864324
  112.7 0.9 copy-start.14
  113.6 0.9 copy-start.16
  114.5 0.9 copy-start.18
  115.4 2.4 %copy-start.24 = (f32[8,128]{1,0:T(8,128)S(1)}, f32[8,128]{1,0:T(8,128)}, u32[]{:S(2)}) copy-start(f32[8,128]{1,0:T(8,128)} %copy-done.23) | copy-start | bytes 12292
  115.4 2.4 %copy-start.27 = (pred[8]{0:T(512)(128)(4,1)S(1)}, pred[8]{0:T(512)(128)(4,1)}, u32[]{:S(2)}) copy-start(pred[8]{0:T(512)(128)(4,1)} %iota_compare_fusion) | copy-start | bytes 28
  117.2 0.6 copy-start.19
  118.6 2.2 %copy-start.25 = (f32[8,128]{1,0:T(8,128)}, f32[8,128]{1,0:T(8,128)S(1)}, u32[]{:S(2)}) copy-start(f32[8,128]{1,0:T(8,128)S(1)} %add_select_fusion.mine_ref) | copy-start | bytes 12292
  118.6 2.2 %collective-permute-start.25 = (f32[8,128]{1,0:T(8,128)S(1)}, f32[8,128]{1,0:T(8,128)S(1)}, u32[]{:S(2)}, u32[]{:S(2)}) collective-permute-start(f32[8,128]{1,0:T(8,128)S(1)} %add_select_fusion.mine_ref), channel_id=1, source_target_pairs={{0,1},{1,0},{2,3},{3,2},{4,5},{5,4},{6,7},{7,6},{8,9},{9,8},{10,11... | collective-permute-start | bytes 12296 | tf_op jit(solution)/shard_map/ppermute | solution.py:683
  120.9 0.6 copy-start.26

commit v9 on v8

--- a/solution.py
+++ b/solution.py
@@ -468,24 +468,24 @@
     )(place, after, x, g, write_map, read_map, rates, *shared[1:], *earlier)
 
 
-def order_kernel(place, here_ref, got_ref, out_ref):
+def order_kernel(place, after_ref, here_ref, got_ref, out_ref):
     size = here_ref.shape[0]
     bit = place[1] & 1
     out_ref[pl.ds(pl.multiple_of(bit * size, size), size), :] = here_ref[...]
     out_ref[pl.ds(pl.multiple_of((1 - bit) * size, size), size), :] = got_ref[...]
 
 
-def order(place, here, got):
+def order(place, after, here, got):
     shape = (2 * here.shape[0], STRIP)
     return pl.pallas_call(
         order_kernel,
-        in_specs=[SCALARS, whole(*here.shape), whole(*got.shape)],
+        in_specs=[SCALARS, whole(META, STRIP), whole(*here.shape), whole(*got.shape)],
         out_specs=whole(*shape),
         out_shape=jax.ShapeDtypeStruct(shape, F32),
         compiler_params=pltpu.CompilerParams(vmem_limit_bytes=SMALL_VMEM),
         cost_estimate=LITTLE,
         name="order",
-    )(place, here, got)
+    )(place, after, here, got)
 
 
 def tally_kernel(
@@ -572,10 +572,10 @@
 
 
 def finish_kernel(
-    heads, start, steps, last, x_ref, g_ref, write_ref, read_ref, tail_ref, lead_ref,
+    heads, start, steps, last, after_ref, x_ref, g_ref, write_ref, read_ref, tail_ref, lead_ref,
     dx_ref, db_ref, dc_ref, change_ref, state_ref, back_ref, *refs,
 ):
-    grad_ref, db_out, dc_out, change_out, db_sum, dc_sum, sum_out = refs[-7:]
+    grad_ref, db_out, dc_out, change_out, token_ref, db_sum, dc_sum, sum_out = refs[-8:]
     chunk = pl.program_id(0)
     lanes = x_ref.shape[1]
     head_size = lanes * STEPS * HALVES // heads
@@ -604,6 +604,7 @@
 
     @pl.when(chunk == steps - 1)
     def _():
+        token_ref[...] = jnp.zeros_like(token_ref)
         db_out[...] = db_sum[...].astype(db_out.dtype)
         dc_out[...] = dc_sum[...].astype(dc_out.dtype)
         if last:
@@ -612,7 +613,7 @@
             change_out[...] = sum_out[...]
 
 
-def finish(heads, start, steps, x, g, write_map, read_map, shared, dx, sums, state, back, grad):
+def finish(heads, start, steps, after, x, g, write_map, read_map, shared, dx, sums, state, back, grad):
     tokens, wide = x.shape
     lanes = wide // (STEPS * HALVES)
     strip = pl.BlockSpec((tokens, lanes), lambda c: (0, start + c))
@@ -624,25 +625,26 @@
     return pl.pallas_call(
         lambda *refs: finish_kernel(heads, start, steps, last, *refs),
         grid=(steps,),
-        in_specs=[strip, strip]
+        in_specs=[whole(META, STRIP), strip, strip]
         + [whole(tokens, STATE)] * 4
         + [strip]
         + [whole(tokens, STATE)] * 3
         + [own, own]
         + [pl.BlockSpec(memory_space=pl.ANY)] * len(earlier),
-        out_specs=[strip] + [whole(tokens, STATE)] * 2 + [whole(*change)],
+        out_specs=[strip] + [whole(tokens, STATE)] * 2 + [whole(*change), whole(META, STRIP)],
         out_shape=[
             jax.ShapeDtypeStruct((tokens, wide), BF16),
             jax.ShapeDtypeStruct((tokens, STATE), kind),
             jax.ShapeDtypeStruct((tokens, STATE), kind),
             jax.ShapeDtypeStruct(change, F32),
+            jax.ShapeDtypeStruct((META, STRIP), F32),
         ],
         scratch_shapes=[pltpu.VMEM((tokens, STATE), F32)] * 3,
-        input_output_aliases={12: 0} if earlier else {},
+        input_output_aliases={13: 0} if earlier else {},
         compiler_params=pltpu.CompilerParams(vmem_limit_bytes=SMALL_VMEM),
         cost_estimate=LITTLE,
         name="finish",
-    )(x, g, write_map, read_map, *shared[2:], dx, *sums, state, back, *earlier)
+    )(after, x, g, write_map, read_map, *shared[2:], dx, *sums, state, back, *earlier)
 
 
 def add_later_kernel(place, suffix_ref, mine_ref, other_ref, out_ref):
@@ -698,9 +700,6 @@
 
         return move(value, target)
 
-    def hold(value, *tokens):
-        return lax.optimization_barrier((value, tokens))[0]
-
     maps = (inputs, out_grad, input_map, output_map)
     send, keep, decay, *shared = summary(chips, 0, place, *maps, log_decay, None)
     first = [to_core(send)]
@@ -714,7 +713,7 @@
     held = [[], []]
     waiting = [None, None]
 
-    def advance(half, step):
+    def advance(half, step, after=None):
         fixed = (chips, half, strips, head_size, place)
         if step == 0:
             mine, send = combine(
@@ -737,7 +736,7 @@
             waiting[half] = to_chip(send, 1 << level)
             return send
         else:
-            send = order(place, held[half][0], waiting[half])
+            send = order(place, after, held[half][0], waiting[half])
             held[half] = send
             waiting[half] = to_core(send)
             return send
@@ -752,25 +751,21 @@
 
     chunks = inputs.shape[1] // LANES
     rounds = 2 * levels + 2
+    spare = chunks - 3
+    parts = {0: spare - spare // 2, 1: 1 + spare // 2, levels: 1, levels + 1: 1}
     block, ready = (), 0
     for step in range(rounds):
-        if step == rounds - 1:
-            waiting[0] = hold(waiting[0], advance(1, step - 1))
-            advance(0, step)
-            continue
-        token = advance(0, step)
-        if step == levels + 1:
-            waiting[1] = hold(waiting[1], token)
+        token = advance(0, step, shared[0])
         if step:
-            advance(1, step - 1)
-        if step < 3:
-            more = pl.cdiv(chunks - ready, 3 - step)
-            block = intra(ready, more, place, token, *maps, log_decay, shared, block)
-            ready += more
+            behind = advance(1, step - 1)
+            token = behind if step == levels + 1 else token
+        if step in parts:
+            block = intra(ready, parts[step], place, token, *maps, log_decay, shared, block)
+            ready += parts[step]
             waiting[0], waiting[1], first[1], block = lax.optimization_barrier(
                 (waiting[0], waiting[1], first[1], block)
             )
-        else:
+        elif step < rounds - 1:
             waiting[0], waiting[1] = lax.optimization_barrier((waiting[0], waiting[1]))
     dx, mine, other, change, db, dc = block
     other = to_core(other)
@@ -778,26 +773,28 @@
     def count(half):
         return tally(heads, chips, half, place, first[half], held[half], mine, other)
 
-    state, back = entering(0, change)
-    grad, *sums = finish(heads, 0, STEPS, *maps, shared, dx, (db, dc, change), state, back, None)
     counted = count(0)
-    waiting[1] = hold(waiting[1], sums[2], counted)
-    advance(1, rounds - 1)
+    state, back = entering(0, counted)
+    grad, *sums, token = finish(
+        heads, 0, STEPS, counted, *maps, shared, dx, (db, dc, change), state, back, None
+    )
+    advance(1, rounds - 1, token)
     counted = counted + count(1)
 
     reached = [to_chip(counted, step) for step in range(1, chips)]
     state, back = entering(1, counted)
-    grad, *sums = finish(heads, STEPS, 1, *maps, shared, dx, sums, state, back, grad)
-    reached = hold(reached, sums[2])
-    later, whole_group = jnp.zeros_like(counted), counted
+    grad, *sums, token = finish(
+        heads, STEPS, 1, counted, *maps, shared, dx, sums, state, back, grad
+    )
+    later, whole_group = jnp.zeros_like(counted), counted + token
     for step, value in enumerate(reached, 1):
         later = later + jnp.where((chip ^ step) > chip, value, 0.0)
         whole_group = whole_group + value
     reached = [to_earlier(whole_group, step) for step in range(1, groups)]
-    sums = hold(sums, whole_group)
-    grad, *sums = finish(heads, STEPS + 1, 1, *maps, shared, dx, sums, state, back, grad)
-    reached = hold(reached, sums[2])
-    later = sum(reached, later)
+    grad, *sums, token = finish(
+        heads, STEPS + 1, 1, whole_group, *maps, shared, dx, sums, state, back, grad
+    )
+    later = sum(reached, later + token)
     row = lax.broadcasted_iota(jnp.int32, later.shape, 0)
     counted = jnp.where(row < META // 2, later, counted)
     return (grad, sums[0], sums[1], add_later(place, sums[2], counted, to_core(counted)))

time: 124 us -> 123 us (level)
    pallas_call x3 -> x4, Pallas kernels: 14.1 us -> 14.8 us  [intra(): pl.pallas_call(lambda *refs: intra_kernel(heads, wide // heads, start, la...]
  transfers between devices with their start and end apart: 26 -> 26, of which waited for: 11 -> 10; matrix products, arithmetic and copies ran while one was open for 0% -> 0% of each run, Pallas kernels for 29% -> 29%
where the time goes in v9:
time: 123 us
  starting transfers between devices  45.5 us (37%)
  Pallas kernels  43.8 us (36%)
  waiting for transfers between devices  22.8 us (19%)
  local copies, waits for them, and re-layouts  7.67 us (6%)
  other arithmetic  1.93 us (2%)
    ppermute x26, starting transfers between devices, move(): return lax.ppermute(value, ('grp', 'seq'), pairs)  45.5 us
    ppermute x26, waiting for transfers between devices, move(): return lax.ppermute(value, ('grp', 'seq'), pairs)  22.8 us
    pallas_call x4, Pallas kernels, intra(): pl.pallas_call(lambda *refs: intra_kernel(heads, wide // heads, start, la...  14.8 us
    unnamed x56, local copies, waits for them, and re-layouts  7.67 us
    pallas_call x2, Pallas kernels, summary(): pl.pallas_call(lambda *refs: summary_kernel(heads, chips, half, *refs), g...  7.41 us
    pallas_call x3, Pallas kernels, finish(): pl.pallas_call(lambda *refs: finish_kernel(heads, start, steps, last, *re...  7.34 us
    pallas_call x4, Pallas kernels, down(): pl.pallas_call(lambda *refs: down_kernel(level, top, STATE // chips, half...  3.15 us
    pallas_call x4, Pallas kernels, up(): pl.pallas_call(lambda *refs: up_kernel(level, last, STATE // chips, half...  2.96 us
  transfers between devices with their start and end apart: 26, of which 10 were waited for; matrix products, arithmetic and copies ran while one was open for 0% of the time, Pallas kernels for 29%

profile of v9, /device:TPU:7, one launch (start us, length us, event | category | flops | bytes accessed | tf_op | source)
XLA Modules:
  0.0 122.8 jit_solution(9198840008394676529)
XLA Ops:
  1.2 3.8 %summary.2 = (f32[1288,128]{1,0:T(8,128)}, f32[1280,128]{1,0:T(8,128)}, f32[10,128]{1,0:T(8,128)}, f32[8,128]{1,0:T(8,128)}, f32[256,128]{1,0:T(8,128)}, /*index...) custom-call(s32[3]{0:T(128)} %pad_add_fusion.refs_0_.place, bf16[256,2560]{1,0:T(8,128)(2,1)} %refs_1_.9, ...), custom_call_target="tpu_custom_call" | custom-call | flops 1 | bytes 1 | tf_op jit(solution)/shard_map/summary/pallas_call | solution.py:187
  5.0 0.7 collective-permute-start
  5.8 3.7 %summary.3 = (f32[1288,128]{1,0:T(8,128)}, f32[1280,128]{1,0:T(8,128)}, f32[10,128]{1,0:T(8,128)}) custom-call(s32[3]{0:T(128)} %pad_add_fusion.refs_0_.place, bf16[256,2560]{1,0:T(8,128)(2,1)} %refs_1_.9, bf16[256,2560]{1,0:T(8,128)(2,1)} %refs_2_.17, bf16[256,128]{1,0:T(8,128)(2,1)} %refs_3_.17, bf16[256,128]{1,0:T(8,128)(2,1)} %refs_4_.17, ...), custom_call_target="tpu_custom_call" | custom-call | flops 1 | bytes 1 | tf_op jit(solution)/shard_map/summary/pallas_call | solution.py:187
  9.6 0.6 combine.2
  10.2 1.4 %collective-permute-start.1 = (f32[648,128]{1,0:T(8,128)S(1)}, f32[648,128]{1,0:T(8,128)S(1)}, u32[]{:S(2)}, u32[]{:S(2)}) collective-permute-start(f32[648,128]{1,0:T(8,128)S(1)} %get-tuple-element.113.refs_1_.refs_2_), channel_id=1, source_target_pairs={{0,2},{1,3},{2,0},{3,1},{4,6},{5,7},{6,4},{7,5},{8,10},{9,11},{10,... | collective-permute-start | bytes 995336 | tf_op jit(solution)/shard_map/ppermute | solution.py:685
  11.7 3.1 %intra.4 = (f32[256,2560]{1,0:T(8,128)S(1)}, f32[128,2560]{1,0:T(8,128)S(1)}, f32[128,2560]{1,0:T(8,128)S(1)}, f32[256,128]{1,0:T(8,128)S(1)}, f32[256,256]{1,0:T(8,128)S(1)}) custom-call(s32[3]{0:T(128)S(1)} %copy-done.12, f32[648,128]{1,0:T(8,128)S(1)} %get-tuple-element.113.refs_1_.refs_2_, bf16[256,2560]{1,0:T(8,128)(2,1)S(1)} %copy-done, ...), custom_call_target="tpu_custom_call" | custom-call | flops 1 | bytes 1 | tf_op jit(solution)/shard_map/intra/pallas_call | solution.py:433
  14.8 4.4 %collective-permute-done.1.refs_3_ = f32[648,128]{1,0:T(8,128)S(1)} collective-permute-done((f32[648,128]{1,0:T(8,128)S(1)}, f32[648,128]{1,0:T(8,128)S(1)}, u32[]{:S(2)}, u32[]{:S(2)}) %collective-permute-start.1) | collective-permute-done | bytes 331808 | tf_op jit(solution)/shard_map/ppermute | solution.py:685
  19.2 0.6 combine.3
  19.8 1.4 %collective-permute-start.4 = (f32[648,128]{1,0:T(8,128)S(1)}, f32[648,128]{1,0:T(8,128)S(1)}, u32[]{:S(2)}, u32[]{:S(2)}) collective-permute-start(f32[648,128]{1,0:T(8,128)S(1)} %get-tuple-element.129.refs_2_), channel_id=1, source_target_pairs={{0,2},{1,3},{2,0},{3,1},{4,6},{5,7},{6,4},{7,5},{8,10},{9,11},{10,... | collective-permute-start | bytes 995336 | tf_op jit(solution)/shard_map/ppermute | solution.py:685
  21.2 0.7 up.4
  21.9 2.4 %collective-permute-start.3 = (f32[328,128]{1,0:T(8,128)S(1)}, f32[328,128]{1,0:T(8,128)S(1)}, u32[]{:S(2)}, u32[]{:S(2)}) collective-permute-start(f32[328,128]{1,0:T(8,128)S(1)} %get-tuple-element.125.refs_1_.refs_2_), channel_id=1, source_target_pairs={{0,4},{1,5},{2,6},{3,7},{4,0},{5,1},{6,2},{7,3},{8,12},{9,13},{10,... | collective-permute-start | bytes 503816 | tf_op jit(solution)/shard_map/ppermute | solution.py:685
  24.3 5.5 %intra.5 = (f32[256,2560]{1,0:T(8,128)S(1)}, f32[128,2560]{1,0:T(8,128)S(1)}, f32[128,2560]{1,0:T(8,128)S(1)}, f32[256,128]{1,0:T(8,128)S(1)}, f32[256,256]{1,0:T(8,128)S(1)}) custom-call(s32[3]{0:T(128)S(1)} %copy-done.12, f32[328,128]{1,0:T(8,128)S(1)} %get-tuple-element.125.refs_1_.refs_2_, ...), custom_call_target="tpu_custom_call", output_to_operand_aliasing={{0}: (10, {}), {1}: (11, {}), {2}: (12, {})} | custom-call | flops 1 | bytes 1 | tf_op jit(solution)/shard_map/intra/pallas_call | solution.py:433
  29.8 0.7 collective-permute-done.3.refs_3_
  30.5 0.9 collective-permute-done.4.refs_3_
  31.5 0.7 up.5.refs_1_
  32.2 1.3 %collective-permute-start.7 = (f32[328,128]{1,0:T(8,128)S(1)}, f32[328,128]{1,0:T(8,128)S(1)}, u32[]{:S(2)}, u32[]{:S(2)}) collective-permute-start(f32[328,128]{1,0:T(8,128)S(1)} %up.5.refs_1_), channel_id=1, source_target_pairs={{1,25},{3,27},{5,29},{7,31},{24,0},{26,2},{28,4},{30,6}} | collective-permute-start | bytes 503816 | tf_op jit(solution)/shard_map/ppermute | solution.py:685
  33.5 1.3 %collective-permute-start.6 = (f32[328,128]{1,0:T(8,128)S(1)}, f32[328,128]{1,0:T(8,128)S(1)}, u32[]{:S(2)}, u32[]{:S(2)}) collective-permute-start(f32[328,128]{1,0:T(8,128)S(1)} %up.5.refs_1_), channel_id=1, source_target_pairs={{1,17},{3,19},{5,21},{7,23},{9,25},{11,27},{13,29},{15,31},{16,0},... | collective-permute-start | bytes 503816 | tf_op jit(solution)/shard_map/ppermute | solution.py:685
  34.8 1.3 %collective-permute-start.5 = (f32[328,128]{1,0:T(8,128)S(1)}, f32[328,128]{1,0:T(8,128)S(1)}, u32[]{:S(2)}, u32[]{:S(2)}) collective-permute-start(f32[328,128]{1,0:T(8,128)S(1)} %up.5.refs_1_), channel_id=1, source_target_pairs={{1,9},{3,11},{5,13},{7,15},{8,0},{9,17},{10,2},{11,19},{12,4},{13,... | collective-permute-start | bytes 503816 | tf_op jit(solution)/shard_map/ppermute | solution.py:685
  36.1 0.8 up.6
  36.9 2.0 %collective-permute-start.8 = (f32[328,128]{1,0:T(8,128)S(1)}, f32[328,128]{1,0:T(8,128)S(1)}, u32[]{:S(2)}, u32[]{:S(2)}) collective-permute-start(f32[328,128]{1,0:T(8,128)S(1)} %get-tuple-element.143.refs_2_), channel_id=1, source_target_pairs={{0,4},{1,5},{2,6},{3,7},{4,0},{5,1},{6,2},{7,3},{8,12},{9,13},{10,... | collective-permute-start | bytes 503816 | tf_op jit(solution)/shard_map/ppermute | solution.py:685
  38.8 3.1 %intra.6 = (f32[256,2560]{1,0:T(8,128)S(1)}, f32[128,2560]{1,0:T(8,128)S(1)}, f32[128,2560]{1,0:T(8,128)S(1)}, f32[256,128]{1,0:T(8,128)S(1)}, f32[256,256]{1,0:T(8,128)S(1)}) custom-call(s32[3]{0:T(128)S(1)} %copy-done.12, f32[328,128]{1,0:T(8,128)S(1)} %up.5.refs_1_, ...), custom_call_target="tpu_custom_call", output_to_operand_aliasing={{0}: (10, {}), {1}: (11, {}), {2}: (12, {})} | custom-call | flops 1 | bytes 1 | tf_op jit(solution)/shard_map/intra/pallas_call | solution.py:433
  42.0 0.7 up.7.refs_1_
  42.8 1.3 %collective-permute-start.12 = (f32[328,128]{1,0:T(8,128)S(1)}, f32[328,128]{1,0:T(8,128)S(1)}, u32[]{:S(2)}, u32[]{:S(2)}) collective-permute-start(f32[328,128]{1,0:T(8,128)S(1)} %up.7.refs_1_), channel_id=1, source_target_pairs={{1,25},{3,27},{5,29},{7,31},{24,0},{26,2},{28,4},{30,6}} | collective-permute-start | bytes 503816 | tf_op jit(solution)/shard_map/ppermute | solution.py:685
  44.1 1.3 %collective-permute-start.11 = (f32[328,128]{1,0:T(8,128)S(1)}, f32[328,128]{1,0:T(8,128)S(1)}, u32[]{:S(2)}, u32[]{:S(2)}) collective-permute-start(f32[328,128]{1,0:T(8,128)S(1)} %up.7.refs_1_), channel_id=1, source_target_pairs={{1,17},{3,19},{5,21},{7,23},{9,25},{11,27},{13,29},{15,31},{16,0},... | collective-permute-start | bytes 503816 | tf_op jit(solution)/shard_map/ppermute | solution.py:685
  45.4 1.5 %collective-permute-start.10 = (f32[328,128]{1,0:T(8,128)S(1)}, f32[328,128]{1,0:T(8,128)S(1)}, u32[]{:S(2)}, u32[]{:S(2)}) collective-permute-start(f32[328,128]{1,0:T(8,128)S(1)} %up.7.refs_1_), channel_id=1, source_target_pairs={{1,9},{3,11},{5,13},{7,15},{8,0},{9,17},{10,2},{11,19},{12,4},{13,... | collective-permute-start | bytes 503816 | tf_op jit(solution)/shard_map/ppermute | solution.py:685
  46.9 0.8 down.4
  47.7 2.1 %collective-permute-start.9 = (f32[320,128]{1,0:T(8,128)S(1)}, f32[320,128]{1,0:T(8,128)S(1)}, u32[]{:S(2)}, u32[]{:S(2)}) collective-permute-start(f32[320,128]{1,0:T(8,128)S(1)} %get-tuple-element.159), channel_id=1, source_target_pairs={{0,4},{1,5},{2,6},{3,7},{4,0},{5,1},{6,2},{7,3},{8,12},{9,13},{10,... | collective-permute-start | bytes 491528 | tf_op jit(solution)/shard_map/ppermute | solution.py:685
  49.7 3.0 %intra.7 = (f32[256,2560]{1,0:T(8,128)S(1)}, f32[128,2560]{1,0:T(8,128)S(1)}, f32[128,2560]{1,0:T(8,128)S(1)}, f32[256,128]{1,0:T(8,128)S(1)}, f32[256,128]{1,0:T(8,128)S(1)}, /*index=5*/f32[256,128]{1,0:T(8,128)S(1)}) custom-call(s32[3]{0:T(128)S(1)} %copy-done.12, ...), custom_call_target="tpu_custom_call", output_to_operand_aliasing={{0}: (10, {}), {1}: (11, {}), {2}: (12, {})} | custom-call | flops 1 | bytes 1 | tf_op jit(solution)/shard_map/intra/pallas_call | solution.py:433
  52.8 2.6 %collective-permute-done.12.refs_6_ = f32[328,128]{1,0:T(8,128)S(1)} collective-permute-done((f32[328,128]{1,0:T(8,128)S(1)}, f32[328,128]{1,0:T(8,128)S(1)}, u32[]{:S(2)}, u32[]{:S(2)}) %collective-permute-start.12) | collective-permute-done | bytes 167968 | tf_op jit(solution)/shard_map/ppermute | solution.py:685
  55.4 0.7 collective-permute-done.11.refs_5_
  56.1 10.1 %collective-permute-start.15 = (f32[128,2560]{1,0:T(8,128)S(1)}, f32[128,2560]{1,0:T(8,128)S(1)}, u32[]{:S(2)}, u32[]{:S(2)}) collective-permute-start(f32[128,2560]{1,0:T(8,128)S(1)} %get-tuple-element.183), channel_id=1, source_target_pairs={{0,1},{1,0},{2,3},{3,2},{4,5},{5,4},{6,7},{7,6},{8,9},{9,8},{10,11... | collective-permute-start | bytes 3932168 | tf_op jit(solution)/shard_map/ppermute | solution.py:685
  66.2 0.8 down.5
  67.1 0.8 down.6
  67.9 2.2 %collective-permute-start.14 = (f32[320,128]{1,0:T(8,128)S(1)}, f32[320,128]{1,0:T(8,128)S(1)}, u32[]{:S(2)}, u32[]{:S(2)}) collective-permute-start(f32[320,128]{1,0:T(8,128)S(1)} %get-tuple-element.180), channel_id=1, source_target_pairs={{0,4},{1,5},{2,6},{3,7},{4,0},{5,1},{6,2},{7,3},{8,12},{9,13},{10,... | collective-permute-start | bytes 491528 | tf_op jit(solution)/shard_map/ppermute | solution.py:685
  70.1 7.8 %collective-permute-done.14.refs_5_ = f32[320,128]{1,0:T(8,128)S(1)} collective-permute-done((f32[320,128]{1,0:T(8,128)S(1)}, f32[320,128]{1,0:T(8,128)S(1)}, u32[]{:S(2)}, u32[]{:S(2)}) %collective-permute-start.14) | collective-permute-done | bytes 163872 | tf_op jit(solution)/shard_map/ppermute | solution.py:685
  77.9 2.0 %collective-permute-done.13.got_ref = f32[640,128]{1,0:T(8,128)S(1)} collective-permute-done((f32[640,128]{1,0:T(8,128)S(1)}, f32[640,128]{1,0:T(8,128)S(1)}, u32[]{:S(2)}, u32[]{:S(2)}) %collective-permute-start.13) | collective-permute-done | bytes 327712 | tf_op jit(solution)/shard_map/ppermute | solution.py:685
  80.5 0.9 collective-permute-start.16
  81.3 0.8 down.7
  82.1 0.8 collective-permute-start.17
  82.9 1.2 tally.2.refs_1_.refs_0_
  84.1 0.9 assemble.2
  85.0 3.8 %finish.3 = (bf16[256,2560]{1,0:T(8,128)(2,1)}, f32[256,128]{1,0:T(8,128)S(1)}, f32[256,128]{1,0:T(8,128)S(1)}, f32[256,128]{1,0:T(8,128)S(1)}, f32[8,128]{1,0:T(8,128)S(1)}) custom-call(f32[8,128]{1,0:T(8,128)S(1)} %tally.2.refs_1_.refs_0_, bf16[256,2560]{1,0:T(8,128)(2,1)S(1)} %copy-done, bf16[256,2560]{1,0:T(8,128)(2,1)S(1)} %copy-done.1, ...), custom_call_target="tpu_custom_call" | custom-call | flops 1 | bytes 1 | tf_op jit(solution)/shard_map/finish/pallas_call | solution.py:625
  88.8 2.7 %collective-permute-done.17.got_ref = f32[640,128]{1,0:T(8,128)S(1)} collective-permute-done((f32[640,128]{1,0:T(8,128)S(1)}, f32[640,128]{1,0:T(8,128)S(1)}, u32[]{:S(2)}, u32[]{:S(2)}) %collective-permute-start.17) | collective-permute-done | bytes 327712 | tf_op jit(solution)/shard_map/ppermute | solution.py:685
  92.1 0.9 collective-permute-start.18
  93.0 1.2 tally.3
  94.2 2.0 %collective-permute-start.21 = (f32[8,128]{1,0:T(8,128)S(1)}, f32[8,128]{1,0:T(8,128)S(1)}, u32[]{:S(2)}, u32[]{:S(2)}) collective-permute-start(f32[8,128]{1,0:T(8,128)S(1)} %add.33.refs_1_.refs_0_), channel_id=1, source_target_pairs={{0,6},{1,7},{2,4},{3,5},{4,2},{5,3},{6,0},{7,1},{8,14},{9,15},{10,... | collective-permute-start | bytes 12296 | tf_op jit(solution)/shard_map/ppermute | solution.py:685
  96.2 1.6 %collective-permute-start.19 = (f32[8,128]{1,0:T(8,128)S(1)}, f32[8,128]{1,0:T(8,128)S(1)}, u32[]{:S(2)}, u32[]{:S(2)}) collective-permute-start(f32[8,128]{1,0:T(8,128)S(1)} %add.33.refs_1_.refs_0_), channel_id=1, source_target_pairs={{0,2},{1,3},{2,0},{3,1},{4,6},{5,7},{6,4},{7,5},{8,10},{9,11},{10,... | collective-permute-start | bytes 12296 | tf_op jit(solution)/shard_map/ppermute | solution.py:685
  97.8 0.9 assemble.3
  98.7 1.8 %finish.4 = (bf16[256,2560]{1,0:T(8,128)(2,1)}, f32[256,128]{1,0:T(8,128)S(1)}, f32[256,128]{1,0:T(8,128)S(1)}, f32[256,128]{1,0:T(8,128)S(1)}, f32[8,128]{1,0:T(8,128)S(1)}) custom-call(f32[8,128]{1,0:T(8,128)S(1)} %add.33.refs_1_.refs_0_, bf16[256,2560]{1,0:T(8,128)(2,1)S(1)} %copy-done, ...), custom_call_target="tpu_custom_call", output_to_operand_aliasing={{0}: (13, {})} | custom-call | flops 1 | bytes 1 | tf_op jit(solution)/shard_map/finish/pallas_call | solution.py:625
  100.5 0.6 copy-done.13
  101.1 0.6 copy-done.15
  101.8 0.7 copy-done.17
  102.5 3.6 %collective-permute-start.24 = (f32[8,128]{1,0:T(8,128)S(1)}, f32[8,128]{1,0:T(8,128)}, u32[]{:S(2)}, u32[]{:S(2)}) collective-permute-start(f32[8,128]{1,0:T(8,128)S(1)} %add_add_fusion.refs_0_), channel_id=1, source_target_pairs={{24,0},{25,1},{26,2},{27,3},{28,4},{29,5},{30,6},{31,7}} | collective-permute-start | bytes 12296 | tf_op jit(solution)/shard_map/ppermute | solution.py:685
  106.1 1.9 %collective-permute-start.23 = (f32[8,128]{1,0:T(8,128)S(1)}, f32[8,128]{1,0:T(8,128)}, u32[]{:S(2)}, u32[]{:S(2)}) collective-permute-start(f32[8,128]{1,0:T(8,128)S(1)} %add_add_fusion.refs_0_), channel_id=1, source_target_pairs={{16,0},{17,1},{18,2},{19,3},{20,4},{21,5},{22,6},{23,7},{24,8},{25... | collective-permute-start | bytes 12296 | tf_op jit(solution)/shard_map/ppermute | solution.py:685
  107.9 2.2 %collective-permute-start.22 = (f32[8,128]{1,0:T(8,128)S(1)}, f32[8,128]{1,0:T(8,128)}, u32[]{:S(2)}, u32[]{:S(2)}) collective-permute-start(f32[8,128]{1,0:T(8,128)S(1)} %add_add_fusion.refs_0_), channel_id=1, source_target_pairs={{8,0},{9,1},{10,2},{11,3},{12,4},{13,5},{14,6},{15,7},{16,8},{17,9... | collective-permute-start | bytes 12296 | tf_op jit(solution)/shard_map/ppermute | solution.py:685
  110.7 1.7 %copy-done.3 = f32[256,2560]{1,0:T(8,128)S(1)} copy-done((f32[256,2560]{1,0:T(8,128)S(1)}, f32[256,2560]{1,0:T(8,128)}, u32[]{:S(2)}) %copy-start.3) | copy-done | bytes 2621464
  112.4 0.9 copy-done.14
  113.3 0.9 copy-done.16
  114.2 0.9 copy-done.18
  115.2 1.8 %finish.5 = (bf16[256,2560]{1,0:T(8,128)(2,1)}, bf16[256,128]{1,0:T(8,128)(2,1)}, bf16[256,128]{1,0:T(8,128)(2,1)}, f32[40,256]{1,0:T(8,128)S(1)}, f32[8,128]{1,0:T(8,128)S(1)}) custom-call(f32[8,128]{1,0:T(8,128)S(1)} %add_add_fusion.refs_0_, bf16[256,2560]{1,0:T(8,128)(2,1)S(1)} %copy-done, ...), custom_call_target="tpu_custom_call", output_to_operand_aliasing={{0}: (13, {})} | custom-call | flops 1 | bytes 1 | tf_op jit(solution)/shard_map/finish/pallas_call | solution.py:625
  117.6 0.8 add_select_fusion.mine_ref
  118.4 1.4 %collective-permute-start.25 = (f32[8,128]{1,0:T(8,128)S(1)}, f32[8,128]{1,0:T(8,128)S(1)}, u32[]{:S(2)}, u32[]{:S(2)}) collective-permute-start(f32[8,128]{1,0:T(8,128)S(1)} %add_select_fusion.mine_ref), channel_id=1, source_target_pairs={{0,1},{1,0},{2,3},{3,2},{4,5},{5,4},{6,7},{7,6},{8,9},{9,8},{10,11... | collective-permute-start | bytes 12296 | tf_op jit(solution)/shard_map/ppermute | solution.py:685
  119.8 0.8 collective-permute-done.25.other_ref
  121.2 1.6 %add_later.1 = f32[40,256]{1,0:T(8,128)} custom-call(s32[3]{0:T(128)} %pad_add_fusion.refs_0_.place, f32[40,256]{1,0:T(8,128)} %copy-done.20, f32[8,128]{1,0:T(8,128)} %copy-done.23, f32[8,128]{1,0:T(8,128)} %copy-done.26), custom_call_target="tpu_custom_call" | custom-call | flops 1 | bytes 1 | tf_op jit(solution)/shard_map/add_later/pallas_call | solution.py:658
  (75 shorter events, 3.9 us)
Async XLA Ops:
  5.0 4.6 %collective-permute-start = (f32[1288,128]{1,0:T(8,128)}, f32[1288,128]{1,0:T(8,128)S(1)}, u32[]{:S(2)}, u32[]{:S(2)}) collective-permute-start(f32[1288,128]{1,0:T(8,128)} %get-tuple-element.108), channel_id=1, source_target_pairs={{0,1},{1,0},{2,3},{3,2},{4,5},{5,4},{6,7},{7,6},{8,9},{9,8},{10,11... | collective-permute-start | bytes 1978376 | tf_op jit(solution)/shard_map/ppermute | solution.py:685
  5.7 3.9 %copy-start.11 = (f32[1280,128]{1,0:T(8,128)S(1)}, f32[1280,128]{1,0:T(8,128)}, u32[]{:S(2)}) copy-start(f32[1280,128]{1,0:T(8,128)} %get-tuple-element.110.refs_2_) | copy-start | bytes 1966084
  5.7 3.9 %copy-start.12 = (s32[3]{0:T(128)S(1)}, s32[3]{0:T(128)}, u32[]{:S(2)}) copy-start(s32[3]{0:T(128)} %pad_add_fusion.refs_0_.place) | copy-start | bytes 40
  5.7 3.9 %copy-start.19 = (f32[8,128]{1,0:T(8,128)S(1)}, f32[8,128]{1,0:T(8,128)}, u32[]{:S(2)}) copy-start(f32[8,128]{1,0:T(8,128)} %get-tuple-element.109.refs_4_.refs_5_.after_ref) | copy-start | bytes 12292
  5.7 3.9 %copy-start.22 = (f32[10,128]{1,0:T(8,128)S(1)}, f32[10,128]{1,0:T(8,128)}, u32[]{:S(2)}) copy-start(f32[10,128]{1,0:T(8,128)} %get-tuple-element.111.refs_3_) | copy-start | bytes 15364
  5.7 5.9 %copy-start.1 = (bf16[256,2560]{1,0:T(8,128)(2,1)S(1)}, bf16[256,2560]{1,0:T(8,128)(2,1)}, u32[]{:S(2)}) copy-start(bf16[256,2560]{1,0:T(8,128)(2,1)} %refs_2_.17) | copy-start | bytes 3932164
  5.7 5.8 %copy-start.4 = (bf16[256,128]{1,0:T(8,128)(2,1)S(1)}, bf16[256,128]{1,0:T(8,128)(2,1)}, u32[]{:S(2)}) copy-start(bf16[256,128]{1,0:T(8,128)(2,1)} %refs_3_.17) | copy-start | bytes 196612
  5.8 5.8 %copy-start.5 = (bf16[256,128]{1,0:T(8,128)(2,1)S(1)}, bf16[256,128]{1,0:T(8,128)(2,1)}, u32[]{:S(2)}) copy-start(bf16[256,128]{1,0:T(8,128)(2,1)} %refs_4_.17) | copy-start | bytes 196612
  5.8 5.8 %copy-start.6 = (bf16[256,128]{1,0:T(8,128)(2,1)S(1)}, bf16[256,128]{1,0:T(8,128)(2,1)}, u32[]{:S(2)}) copy-start(bf16[256,128]{1,0:T(8,128)(2,1)} %get-tuple-element.114.refs_6_.refs_8_.refs_5_) | copy-start | bytes 196612
  5.8 5.8 %copy-start.7 = (bf16[256,128]{1,0:T(8,128)(2,1)S(1)}, bf16[256,128]{1,0:T(8,128)(2,1)}, u32[]{:S(2)}) copy-start(bf16[256,128]{1,0:T(8,128)(2,1)} %get-tuple-element.115.refs_7_.refs_9_.refs_6_) | copy-start | bytes 196612
  5.8 5.8 %copy-start.8 = (f32[256,128]{1,0:T(8,128)S(1)}, f32[256,128]{1,0:T(8,128)}, u32[]{:S(2)}) copy-start(f32[256,128]{1,0:T(8,128)} %get-tuple-element.117.refs_7_) | copy-start | bytes 393220
  5.8 5.8 %copy-start.9 = (f32[40,256]{1,0:T(8,128)S(1)}, f32[40,256]{1,0:T(8,128)}, u32[]{:S(2)}) copy-start(f32[40,256]{1,0:T(8,128)} %refs_6_.7) | copy-start | bytes 122884
  9.5 2.2 %copy-start = (bf16[256,2560]{1,0:T(8,128)(2,1)S(1)}, bf16[256,2560]{1,0:T(8,128)(2,1)}, u32[]{:S(2)}) copy-start(bf16[256,2560]{1,0:T(8,128)(2,1)} %refs_1_.9) | copy-start | bytes 3932164
  9.5 5.3 %collective-permute-start.2 = (f32[1288,128]{1,0:T(8,128)}, f32[1288,128]{1,0:T(8,128)S(1)}, u32[]{:S(2)}, u32[]{:S(2)}) collective-permute-start(f32[1288,128]{1,0:T(8,128)} %get-tuple-element.116), channel_id=1, source_target_pairs={{0,1},{1,0},{2,3},{3,2},{4,5},{5,4},{6,7},{7,6},{8,9},{9,8},{10,11... | collective-permute-start | bytes 1978376 | tf_op jit(solution)/shard_map/ppermute | solution.py:685
  10.2 9.0 %collective-permute-start.1 = (f32[648,128]{1,0:T(8,128)S(1)}, f32[648,128]{1,0:T(8,128)S(1)}, u32[]{:S(2)}, u32[]{:S(2)}) collective-permute-start(f32[648,128]{1,0:T(8,128)S(1)} %get-tuple-element.113.refs_1_.refs_2_), channel_id=1, source_target_pairs={{0,2},{1,3},{2,0},{3,1},{4,6},{5,7},{6,4},{7,5},{8,10},{9,11},{10,... | collective-permute-start | bytes 995336 | tf_op jit(solution)/shard_map/ppermute | solution.py:685
  11.6 7.6 %copy-start.10 = (f32[1280,128]{1,0:T(8,128)S(1)}, f32[1280,128]{1,0:T(8,128)}, u32[]{:S(2)}) copy-start(f32[1280,128]{1,0:T(8,128)} %get-tuple-element.127.refs_2_) | copy-start | bytes 1966084
  11.6 7.5 %copy-start.21 = (f32[10,128]{1,0:T(8,128)S(1)}, f32[10,128]{1,0:T(8,128)}, u32[]{:S(2)}) copy-start(f32[10,128]{1,0:T(8,128)} %get-tuple-element.128.refs_3_) | copy-start | bytes 15364
  19.8 11.6 %collective-permute-start.4 = (f32[648,128]{1,0:T(8,128)S(1)}, f32[648,128]{1,0:T(8,128)S(1)}, u32[]{:S(2)}, u32[]{:S(2)}) collective-permute-start(f32[648,128]{1,0:T(8,128)S(1)} %get-tuple-element.129.refs_2_), channel_id=1, source_target_pairs={{0,2},{1,3},{2,0},{3,1},{4,6},{5,7},{6,4},{7,5},{8,10},{9,11},{10,... | collective-permute-start | bytes 995336 | tf_op jit(solution)/shard_map/ppermute | solution.py:685
  21.9 8.6 %collective-permute-start.3 = (f32[328,128]{1,0:T(8,128)S(1)}, f32[328,128]{1,0:T(8,128)S(1)}, u32[]{:S(2)}, u32[]{:S(2)}) collective-permute-start(f32[328,128]{1,0:T(8,128)S(1)} %get-tuple-element.125.refs_1_.refs_2_), channel_id=1, source_target_pairs={{0,4},{1,5},{2,6},{3,7},{4,0},{5,1},{6,2},{7,3},{8,12},{9,13},{10,... | collective-permute-start | bytes 503816 | tf_op jit(solution)/shard_map/ppermute | solution.py:685
  32.2 9.7 %collective-permute-start.7 = (f32[328,128]{1,0:T(8,128)S(1)}, f32[328,128]{1,0:T(8,128)S(1)}, u32[]{:S(2)}, u32[]{:S(2)}) collective-permute-start(f32[328,128]{1,0:T(8,128)S(1)} %up.5.refs_1_), channel_id=1, source_target_pairs={{1,25},{3,27},{5,29},{7,31},{24,0},{26,2},{28,4},{30,6}} | collective-permute-start | bytes 503816 | tf_op jit(solution)/shard_map/ppermute | solution.py:685
  33.5 8.5 %collective-permute-start.6 = (f32[328,128]{1,0:T(8,128)S(1)}, f32[328,128]{1,0:T(8,128)S(1)}, u32[]{:S(2)}, u32[]{:S(2)}) collective-permute-start(f32[328,128]{1,0:T(8,128)S(1)} %up.5.refs_1_), channel_id=1, source_target_pairs={{1,17},{3,19},{5,21},{7,23},{9,25},{11,27},{13,29},{15,31},{16,0},... | collective-permute-start | bytes 503816 | tf_op jit(solution)/shard_map/ppermute | solution.py:685
  34.8 7.2 %collective-permute-start.5 = (f32[328,128]{1,0:T(8,128)S(1)}, f32[328,128]{1,0:T(8,128)S(1)}, u32[]{:S(2)}, u32[]{:S(2)}) collective-permute-start(f32[328,128]{1,0:T(8,128)S(1)} %up.5.refs_1_), channel_id=1, source_target_pairs={{1,9},{3,11},{5,13},{7,15},{8,0},{9,17},{10,2},{11,19},{12,4},{13,... | collective-permute-start | bytes 503816 | tf_op jit(solution)/shard_map/ppermute | solution.py:685
  36.9 5.2 %collective-permute-start.8 = (f32[328,128]{1,0:T(8,128)S(1)}, f32[328,128]{1,0:T(8,128)S(1)}, u32[]{:S(2)}, u32[]{:S(2)}) collective-permute-start(f32[328,128]{1,0:T(8,128)S(1)} %get-tuple-element.143.refs_2_), channel_id=1, source_target_pairs={{0,4},{1,5},{2,6},{3,7},{4,0},{5,1},{6,2},{7,3},{8,12},{9,13},{10,... | collective-permute-start | bytes 503816 | tf_op jit(solution)/shard_map/ppermute | solution.py:685
  42.8 12.6 %collective-permute-start.12 = (f32[328,128]{1,0:T(8,128)S(1)}, f32[328,128]{1,0:T(8,128)S(1)}, u32[]{:S(2)}, u32[]{:S(2)}) collective-permute-start(f32[328,128]{1,0:T(8,128)S(1)} %up.7.refs_1_), channel_id=1, source_target_pairs={{1,25},{3,27},{5,29},{7,31},{24,0},{26,2},{28,4},{30,6}} | collective-permute-start | bytes 503816 | tf_op jit(solution)/shard_map/ppermute | solution.py:685
  44.1 12.0 %collective-permute-start.11 = (f32[328,128]{1,0:T(8,128)S(1)}, f32[328,128]{1,0:T(8,128)S(1)}, u32[]{:S(2)}, u32[]{:S(2)}) collective-permute-start(f32[328,128]{1,0:T(8,128)S(1)} %up.7.refs_1_), channel_id=1, source_target_pairs={{1,17},{3,19},{5,21},{7,23},{9,25},{11,27},{13,29},{15,31},{16,0},... | collective-permute-start | bytes 503816 | tf_op jit(solution)/shard_map/ppermute | solution.py:685
  45.4 10.7 %collective-permute-start.10 = (f32[328,128]{1,0:T(8,128)S(1)}, f32[328,128]{1,0:T(8,128)S(1)}, u32[]{:S(2)}, u32[]{:S(2)}) collective-permute-start(f32[328,128]{1,0:T(8,128)S(1)} %up.7.refs_1_), channel_id=1, source_target_pairs={{1,9},{3,11},{5,13},{7,15},{8,0},{9,17},{10,2},{11,19},{12,4},{13,... | collective-permute-start | bytes 503816 | tf_op jit(solution)/shard_map/ppermute | solution.py:685
  47.7 5.1 %collective-permute-start.9 = (f32[320,128]{1,0:T(8,128)S(1)}, f32[320,128]{1,0:T(8,128)S(1)}, u32[]{:S(2)}, u32[]{:S(2)}) collective-permute-start(f32[320,128]{1,0:T(8,128)S(1)} %get-tuple-element.159), channel_id=1, source_target_pairs={{0,4},{1,5},{2,6},{3,7},{4,0},{5,1},{6,2},{7,3},{8,12},{9,13},{10,... | collective-permute-start | bytes 491528 | tf_op jit(solution)/shard_map/ppermute | solution.py:685
  52.7 46.0 %copy-start.2 = (f32[256,2560]{1,0:T(8,128)}, f32[256,2560]{1,0:T(8,128)S(1)}, u32[]{:S(2)}) copy-start(f32[256,2560]{1,0:T(8,128)S(1)} %get-tuple-element.185.refs_7_) | copy-start | bytes 7864324
  56.1 26.8 %collective-permute-start.15 = (f32[128,2560]{1,0:T(8,128)S(1)}, f32[128,2560]{1,0:T(8,128)S(1)}, u32[]{:S(2)}, u32[]{:S(2)}) collective-permute-start(f32[128,2560]{1,0:T(8,128)S(1)} %get-tuple-element.183), channel_id=1, source_target_pairs={{0,1},{1,0},{2,3},{3,2},{4,5},{5,4},{6,7},{7,6},{8,9},{9,8},{10,11... | collective-permute-start | bytes 3932168 | tf_op jit(solution)/shard_map/ppermute | solution.py:685
  67.0 12.9 %collective-permute-start.13 = (f32[640,128]{1,0:T(8,128)S(1)}, f32[640,128]{1,0:T(8,128)S(1)}, u32[]{:S(2)}, u32[]{:S(2)}) collective-permute-start(f32[640,128]{1,0:T(8,128)S(1)} %get-tuple-element.176), channel_id=1, source_target_pairs={{0,2},{1,3},{2,0},{3,1},{4,6},{5,7},{6,4},{7,5},{8,10},{9,11},{10,... | collective-permute-start | bytes 983048 | tf_op jit(solution)/shard_map/ppermute | solution.py:685
  67.9 10.0 %collective-permute-start.14 = (f32[320,128]{1,0:T(8,128)S(1)}, f32[320,128]{1,0:T(8,128)S(1)}, u32[]{:S(2)}, u32[]{:S(2)}) collective-permute-start(f32[320,128]{1,0:T(8,128)S(1)} %get-tuple-element.180), channel_id=1, source_target_pairs={{0,4},{1,5},{2,6},{3,7},{4,0},{5,1},{6,2},{7,3},{8,12},{9,13},{10,... | collective-permute-start | bytes 491528 | tf_op jit(solution)/shard_map/ppermute | solution.py:685
  80.5 3.6 %collective-permute-start.16 = (f32[1280,128]{1,0:T(8,128)S(1)}, f32[1280,128]{1,0:T(8,128)S(1)}, u32[]{:S(2)}, u32[]{:S(2)}) collective-permute-start(f32[1280,128]{1,0:T(8,128)S(1)} %order.2.refs_2_.refs_3_), channel_id=1, source_target_pairs={{0,1},{1,0},{2,3},{3,2},{4,5},{5,4},{6,7},{7,6},{8,9},{9,8},{10,11... | collective-permute-start | bytes 1966088 | tf_op jit(solution)/shard_map/ppermute | solution.py:685
  82.1 9.4 %collective-permute-start.17 = (f32[640,128]{1,0:T(8,128)S(1)}, f32[640,128]{1,0:T(8,128)S(1)}, u32[]{:S(2)}, u32[]{:S(2)}) collective-permute-start(f32[640,128]{1,0:T(8,128)S(1)} %get-tuple-element.195), channel_id=1, source_target_pairs={{0,2},{1,3},{2,0},{3,1},{4,6},{5,7},{6,4},{7,5},{8,10},{9,11},{10,... | collective-permute-start | bytes 983048 | tf_op jit(solution)/shard_map/ppermute | solution.py:685
  92.1 5.7 %collective-permute-start.18 = (f32[1280,128]{1,0:T(8,128)S(1)}, f32[1280,128]{1,0:T(8,128)S(1)}, u32[]{:S(2)}, u32[]{:S(2)}) collective-permute-start(f32[1280,128]{1,0:T(8,128)S(1)} %order.3.refs_2_.refs_3_), channel_id=1, source_target_pairs={{0,1},{1,0},{2,3},{3,2},{4,5},{5,4},{6,7},{7,6},{8,9},{9,8},{10,11... | collective-permute-start | bytes 1966088 | tf_op jit(solution)/shard_map/ppermute | solution.py:685
  94.2 8.2 %collective-permute-start.21 = (f32[8,128]{1,0:T(8,128)S(1)}, f32[8,128]{1,0:T(8,128)S(1)}, u32[]{:S(2)}, u32[]{:S(2)}) collective-permute-start(f32[8,128]{1,0:T(8,128)S(1)} %add.33.refs_1_.refs_0_), channel_id=1, source_target_pairs={{0,6},{1,7},{2,4},{3,5},{4,2},{5,3},{6,0},{7,1},{8,14},{9,15},{10,... | collective-permute-start | bytes 12296 | tf_op jit(solution)/shard_map/ppermute | solution.py:685
  96.2 6.2 %collective-permute-start.20 = (f32[8,128]{1,0:T(8,128)S(1)}, f32[8,128]{1,0:T(8,128)S(1)}, u32[]{:S(2)}, u32[]{:S(2)}) collective-permute-start(f32[8,128]{1,0:T(8,128)S(1)} %add.33.refs_1_.refs_0_), channel_id=1, source_target_pairs={{0,4},{1,5},{2,6},{3,7},{4,0},{5,1},{6,2},{7,3},{8,12},{9,13},{10,... | collective-permute-start | bytes 12296 | tf_op jit(solution)/shard_map/ppermute | solution.py:685
  96.2 6.2 %collective-permute-start.19 = (f32[8,128]{1,0:T(8,128)S(1)}, f32[8,128]{1,0:T(8,128)S(1)}, u32[]{:S(2)}, u32[]{:S(2)}) collective-permute-start(f32[8,128]{1,0:T(8,128)S(1)} %add.33.refs_1_.refs_0_), channel_id=1, source_target_pairs={{0,2},{1,3},{2,0},{3,1},{4,6},{5,7},{6,4},{7,5},{8,10},{9,11},{10,... | collective-permute-start | bytes 12296 | tf_op jit(solution)/shard_map/ppermute | solution.py:685
  100.5 0.6 copy-start.13
  101.1 0.6 copy-start.15
  101.8 0.7 copy-start.17
  102.4 3.6 %copy-start.24 = (f32[8,128]{1,0:T(8,128)}, f32[8,128]{1,0:T(8,128)S(1)}, u32[]{:S(2)}) copy-start(f32[8,128]{1,0:T(8,128)S(1)} %collective-permute-done.19) | copy-start | bytes 12292
  102.5 15.1 %collective-permute-start.24 = (f32[8,128]{1,0:T(8,128)S(1)}, f32[8,128]{1,0:T(8,128)}, u32[]{:S(2)}, u32[]{:S(2)}) collective-permute-start(f32[8,128]{1,0:T(8,128)S(1)} %add_add_fusion.refs_0_), channel_id=1, source_target_pairs={{24,0},{25,1},{26,2},{27,3},{28,4},{29,5},{30,6},{31,7}} | collective-permute-start | bytes 12296 | tf_op jit(solution)/shard_map/ppermute | solution.py:685
  106.1 11.5 %collective-permute-start.23 = (f32[8,128]{1,0:T(8,128)S(1)}, f32[8,128]{1,0:T(8,128)}, u32[]{:S(2)}, u32[]{:S(2)}) collective-permute-start(f32[8,128]{1,0:T(8,128)S(1)} %add_add_fusion.refs_0_), channel_id=1, source_target_pairs={{16,0},{17,1},{18,2},{19,3},{20,4},{21,5},{22,6},{23,7},{24,8},{25... | collective-permute-start | bytes 12296 | tf_op jit(solution)/shard_map/ppermute | solution.py:685
  107.9 9.6 %collective-permute-start.22 = (f32[8,128]{1,0:T(8,128)S(1)}, f32[8,128]{1,0:T(8,128)}, u32[]{:S(2)}, u32[]{:S(2)}) collective-permute-start(f32[8,128]{1,0:T(8,128)S(1)} %add_add_fusion.refs_0_), channel_id=1, source_target_pairs={{8,0},{9,1},{10,2},{11,3},{12,4},{13,5},{14,6},{15,7},{16,8},{17,9... | collective-permute-start | bytes 12296 | tf_op jit(solution)/shard_map/ppermute | solution.py:685
  110.7 1.7 %copy-start.3 = (f32[256,2560]{1,0:T(8,128)S(1)}, f32[256,2560]{1,0:T(8,128)}, u32[]{:S(2)}) copy-start(f32[256,2560]{1,0:T(8,128)} %copy-done.2) | copy-start | bytes 7864324
  112.4 0.9 copy-start.14
  113.3 0.9 copy-start.16
  114.2 0.9 copy-start.18
  115.1 2.4 %copy-start.25 = (f32[8,128]{1,0:T(8,128)S(1)}, f32[8,128]{1,0:T(8,128)}, u32[]{:S(2)}) copy-start(f32[8,128]{1,0:T(8,128)} %copy-done.24) | copy-start | bytes 12292
  115.2 2.4 %copy-start.27 = (pred[8]{0:T(512)(128)(4,1)S(1)}, pred[8]{0:T(512)(128)(4,1)}, u32[]{:S(2)}) copy-start(pred[8]{0:T(512)(128)(4,1)} %iota_compare_fusion) | copy-start | bytes 28
  116.9 0.6 copy-start.20
  118.4 2.3 %copy-start.23 = (f32[8,128]{1,0:T(8,128)}, f32[8,128]{1,0:T(8,128)S(1)}, u32[]{:S(2)}) copy-start(f32[8,128]{1,0:T(8,128)S(1)} %add_select_fusion.mine_ref) | copy-start | bytes 12292
  118.4 2.3 %collective-permute-start.25 = (f32[8,128]{1,0:T(8,128)S(1)}, f32[8,128]{1,0:T(8,128)S(1)}, u32[]{:S(2)}, u32[]{:S(2)}) collective-permute-start(f32[8,128]{1,0:T(8,128)S(1)} %add_select_fusion.mine_ref), channel_id=1, source_target_pairs={{0,1},{1,0},{2,3},{3,2},{4,5},{5,4},{6,7},{7,6},{8,9},{9,8},{10,11... | collective-permute-start | bytes 12296 | tf_op jit(solution)/shard_map/ppermute | solution.py:685
  120.6 0.6 copy-start.26

commit v10 on v7

--- a/solution.py
+++ b/solution.py
@@ -464,28 +464,28 @@
     )(after, x, g, write_map, read_map, rates, *shared[1:], *earlier)
 
 
-def order_kernel(place, here_ref, got_ref, out_ref):
+def order_kernel(place, after_ref, here_ref, got_ref, out_ref):
     size = here_ref.shape[0]
     bit = place[1] & 1
     out_ref[pl.ds(pl.multiple_of(bit * size, size), size), :] = here_ref[...]
     out_ref[pl.ds(pl.multiple_of((1 - bit) * size, size), size), :] = got_ref[...]
 
 
-def order(place, here, got):
+def order(place, after, here, got):
     shape = (2 * here.shape[0], STRIP)
     return pl.pallas_call(
         order_kernel,
-        in_specs=[SCALARS, whole(*here.shape), whole(*got.shape)],
+        in_specs=[SCALARS, whole(META, STRIP), whole(*here.shape), whole(*got.shape)],
         out_specs=whole(*shape),
         out_shape=jax.ShapeDtypeStruct(shape, F32),
         compiler_params=pltpu.CompilerParams(vmem_limit_bytes=SMALL_VMEM),
         cost_estimate=LITTLE,
         name="order",
-    )(place, here, got)
+    )(place, after, here, got)
 
 
 def assemble_kernel(
-    heads, chips, half, head_size, place, after, first_ref, state_own, back_own, own_ref, far_ref,
+    heads, chips, half, head_size, place, after_ref, first_ref, state_own, back_own, own_ref, far_ref,
     state_ref, back_ref, total_ref,
 ):
     lanes = state_ref.shape[1]
@@ -513,9 +513,8 @@
     row_sum = [
         jnp.broadcast_to(jnp.sum(value, axis=0, keepdims=True), (META, STRIP)) for value in sums
     ]
-    total_ref[...] = head_sums(
-        jnp.concatenate(row_sum, axis=1), head_adder(half, head_size, lanes)
-    )
+    total = head_sums(jnp.concatenate(row_sum, axis=1), head_adder(half, head_size, lanes))
+    total_ref[...] = total + after_ref[...] if half else total
 
 
 def assemble(heads, chips, half, place, after, first, state_own, back_own, own, far):
@@ -543,7 +542,7 @@
     heads, start, steps, last, x_ref, g_ref, write_ref, read_ref, tail_ref, lead_ref,
     dx_ref, db_ref, dc_ref, change_ref, state_ref, back_ref, *refs,
 ):
-    grad_ref, db_out, dc_out, change_out, db_sum, dc_sum, sum_out = refs[-7:]
+    grad_ref, db_out, dc_out, change_out, token_ref, db_sum, dc_sum, sum_out = refs[-8:]
     chunk = pl.program_id(0)
     lanes = x_ref.shape[1]
     head_size = lanes * STEPS * HALVES // heads
@@ -572,6 +571,7 @@
 
     @pl.when(chunk == steps - 1)
     def _():
+        token_ref[...] = jnp.zeros_like(token_ref)
         db_out[...] = db_sum[...].astype(db_out.dtype)
         dc_out[...] = dc_sum[...].astype(dc_out.dtype)
         if last:
@@ -580,7 +580,7 @@
             change_out[...] = sum_out[...]
 
 
-def finish(heads, start, steps, x, g, write_map, read_map, shared, dx, sums, state, back, grad):
+def finish(heads, start, steps, after, x, g, write_map, read_map, shared, dx, sums, state, back, grad):
     tokens, wide = x.shape
     lanes = wide // (STEPS * HALVES)
     strip = pl.BlockSpec((tokens, lanes), lambda c: (0, start + c))
@@ -597,36 +597,70 @@
         + [strip]
         + [whole(tokens, STATE)] * 3
         + [own, own]
-        + [pl.BlockSpec(memory_space=pl.ANY)] * len(earlier),
-        out_specs=[strip] + [whole(tokens, STATE)] * 2 + [whole(*change)],
+        + [pl.BlockSpec(memory_space=pl.ANY)] * len(earlier)
+        + [whole(META, STRIP)],
+        out_specs=[strip] + [whole(tokens, STATE)] * 2 + [whole(*change), whole(META, STRIP)],
         out_shape=[
             jax.ShapeDtypeStruct((tokens, wide), BF16),
             jax.ShapeDtypeStruct((tokens, STATE), kind),
             jax.ShapeDtypeStruct((tokens, STATE), kind),
             jax.ShapeDtypeStruct(change, F32),
+            jax.ShapeDtypeStruct((META, STRIP), F32),
         ],
         scratch_shapes=[pltpu.VMEM((tokens, STATE), F32)] * 3,
         input_output_aliases={12: 0} if earlier else {},
         compiler_params=pltpu.CompilerParams(vmem_limit_bytes=SMALL_VMEM),
         cost_estimate=LITTLE,
         name="finish",
-    )(x, g, write_map, read_map, *shared[2:], dx, *sums, state, back, *earlier)
-
-
-def add_later_kernel(suffix_ref, later_ref, out_ref):
+    )(x, g, write_map, read_map, *shared[2:], dx, *sums, state, back, *earlier, after)
+
+
+def count_kernel(place, later_ref, total_ref, after_ref, *refs):
+    got_refs, (later_out, total_out) = refs[:-2], refs[-2:]
+    later, total = later_ref[...], total_ref[...] + after_ref[...]
+    for step, ref in enumerate(got_refs, 1):
+        later = later + jnp.where((place[1] ^ step) > place[1], ref[...], 0.0)
+        total = total + ref[...]
+    later_out[...] = later
+    total_out[...] = total
+
+
+def core_kernel(place, total_ref, after_ref, got_ref, later_out, total_out):
+    later_out[...] = jnp.where(place[0] == 0, got_ref[...], 0.0)
+    total_out[...] = total_ref[...] + got_ref[...] + after_ref[...]
+
+
+def tiles(kernel, name, place, *values):
+    return pl.pallas_call(
+        kernel,
+        in_specs=[SCALARS] + [whole(META, STRIP)] * len(values),
+        out_specs=[whole(META, STRIP)] * 2,
+        out_shape=[jax.ShapeDtypeStruct((META, STRIP), F32)] * 2,
+        compiler_params=pltpu.CompilerParams(vmem_limit_bytes=SMALL_VMEM),
+        cost_estimate=LITTLE,
+        name=name,
+    )(place, *values)
+
+
+def add_later_kernel(suffix_ref, *refs):
+    out_ref = refs[-1]
     heads = out_ref.shape[0]
-    out_ref[...] = suffix_ref[...] + later_ref[...].T[:heads, 0:1]
-
-
-def add_later(suffix, later):
+    later = refs[0][...]
+    for ref in refs[1:-1]:
+        later = later + ref[...]
+    out_ref[...] = suffix_ref[...] + later.T[:heads, 0:1]
+
+
+def add_later(suffix, *parts):
     return pl.pallas_call(
         add_later_kernel,
-        in_specs=[whole(*suffix.shape), whole(*later.shape)],
+        in_specs=[whole(*value.shape) for value in (suffix, *parts)],
         out_specs=whole(*suffix.shape),
         out_shape=jax.ShapeDtypeStruct(suffix.shape, F32),
+        compiler_params=pltpu.CompilerParams(vmem_limit_bytes=SMALL_VMEM),
         cost_estimate=LITTLE,
         name="add_later",
-    )(suffix, later)
+    )(suffix, *parts)
 
 
 def per_device(inputs, out_grad, input_map, output_map, log_decay):
@@ -638,7 +672,6 @@
     chip, core = shard >> 1, shard & 1
     place = jnp.stack([core, chip, group]).astype(jnp.int32)
     strips = inputs.shape[1] // STRIP // HALVES
-    bits = groups.bit_length() - 1
     everyone = [(a, z, c) for a in range(groups) for z in range(chips) for c in range(2)]
 
     def move(value, target):
@@ -655,8 +688,8 @@
     def to_chip(value, step):
         return move(value, lambda a, z, c: (a, z ^ step, c)) if step else value
 
-    def to_group(value, step):
-        return move(value, lambda a, z, c: (a ^ step, z, c))
+    def to_earlier(value, step):
+        return move(value, lambda a, z, c: (a - step, z, c) if a >= step else None)
 
     def to_later(value, step):
         def target(a, z, c):
@@ -664,9 +697,6 @@
             return (to, z, c) if 0 <= to < groups else None
 
         return move(value, target)
-
-    def hold(value, *tokens):
-        return lax.optimization_barrier((value, tokens))[0]
 
     maps = (inputs, out_grad, input_map, output_map)
     send, keep, decay, *shared = summary(chips, 0, place, *maps, log_decay, None)
@@ -681,7 +711,7 @@
     held = [[], []]
     waiting = [None, None]
 
-    def advance(half, step):
+    def advance(half, step, after=None):
         fixed = (chips, half, strips, head_size, place)
         if step == 0:
             mine, send = combine(
@@ -704,7 +734,7 @@
             waiting[half] = to_chip(send, 1 << level)
             return send
         else:
-            send = order(place, held[half][0], waiting[half])
+            send = order(place, after, held[half][0], waiting[half])
             held[half] = send
             waiting[half] = to_core(send)
             return send
@@ -722,7 +752,7 @@
     rounds = 2 * levels + 2
     block, ready = (), 0
     for step in range(rounds):
-        token = advance(0, step)
+        token = advance(0, step, shared[0])
         if step:
             advance(1, step - 1)
         if step < 3:
@@ -735,28 +765,25 @@
         elif step < rounds - 1:
             waiting[0], waiting[1] = lax.optimization_barrier((waiting[0], waiting[1]))
     dx, state_own, back_own, change, db, dc = block
-    state, back, tally = entering(0, change)
-    grad, *sums = finish(heads, 0, STEPS, *maps, shared, dx, (db, dc, change), state, back, None)
-    waiting[1] = hold(waiting[1], sums[2])
-    advance(1, rounds - 1)
-    state, back, tally_b = entering(1, sums[2])
-    tally = tally + tally_b
-
-    def count(later, tally, got, bit, index):
-        return later + jnp.where((index >> bit) & 1 == 0, got, 0.0), tally + got
-
-    got = to_core(tally)
-    grad, *sums = finish(heads, STEPS, 1, *maps, shared, dx, sums, state, back, grad)
-    later, tally = count(0.0, tally, hold(got, sums[2]), 0, core)
-    got = to_chip(tally, 1)
-    sums = hold(sums, tally)
-    grad, *sums = finish(heads, STEPS + 1, 1, *maps, shared, dx, sums, state, back, grad)
-    later, tally = count(later, tally, hold(got, sums[2]), 0, chip)
-    for bit in range(1, chips.bit_length() - 1):
-        later, tally = count(later, tally, to_chip(tally, 1 << bit), bit, chip)
-    for bit in range(bits):
-        later, tally = count(later, tally, to_group(tally, 1 << bit), bit, group)
-    return (grad, sums[0], sums[1], add_later(sums[2], later))
+    state, back, counted = entering(0, change)
+    grad, *sums, token = finish(
+        heads, 0, STEPS, counted, *maps, shared, dx, (db, dc, change), state, back, None
+    )
+    advance(1, rounds - 1, token)
+    state, back, counted = entering(1, counted)
+
+    got = to_core(counted)
+    grad, *sums, token = finish(
+        heads, STEPS, 1, counted, *maps, shared, dx, sums, state, back, grad
+    )
+    later, counted = tiles(core_kernel, "core_sum", place, counted, token, got)
+    got = [to_chip(counted, step) for step in range(1, chips)]
+    grad, *sums, token = finish(
+        heads, STEPS + 1, 1, counted, *maps, shared, dx, sums, state, back, grad
+    )
+    later, counted = tiles(count_kernel, "chip_sum", place, later, counted, token, *got)
+    got = [to_earlier(counted, step) for step in range(1, groups)]
+    return (grad, sums[0], sums[1], add_later(sums[2], later, *got))
 
 
 def solution(mesh):

time: 116 us -> 116 us (level)
  starting transfers between devices: 26.5 us -> 29.4 us
  waiting for transfers between devices: 45.8 us -> 44.3 us
    ppermute x23 -> x25, starting transfers between devices: 26.5 us -> 29.4 us  [move(): return lax.ppermute(value, ('grp', 'seq'), pairs)]
    ppermute x23 -> x25, waiting for transfers between devices: 45.8 us -> 44.3 us  [move(): return lax.ppermute(value, ('grp', 'seq'), pairs)]
    pallas_call x3 -> x5, Pallas kernels: 2.72 us -> 3.04 us  [the longest x2 1.17 us: order(): pl.pallas_call(order_kernel, in_specs=[SCALARS, whole(META, STRIP), whole...]
  transfers between devices with their start and end apart: 23 -> 25, of which waited for: 14 -> 15; matrix products, arithmetic and copies ran while one was open for 0% -> 0% of each run, Pallas kernels for 25% -> 25%
where the time goes in v10:
time: 116 us
  waiting for transfers between devices  44.3 us (38%)
  Pallas kernels  40.3 us (35%)
  starting transfers between devices  29.4 us (25%)
    ppermute x25, waiting for transfers between devices, move(): return lax.ppermute(value, ('grp', 'seq'), pairs)  44.3 us
    ppermute x25, starting transfers between devices, move(): return lax.ppermute(value, ('grp', 'seq'), pairs)  29.4 us
    pallas_call x3, Pallas kernels, intra(): pl.pallas_call(lambda *refs: intra_kernel(heads, wide // heads, start, la...  12.5 us
    pallas_call x3, Pallas kernels, finish(): pl.pallas_call(lambda *refs: finish_kernel(heads, start, steps, last, *re...  7.4 us
    pallas_call x2, Pallas kernels, summary(): pl.pallas_call(lambda *refs: summary_kernel(heads, chips, half, *refs), g...  7.39 us
    pallas_call x4, Pallas kernels, down(): pl.pallas_call(lambda *refs: down_kernel(level, top, STATE // chips, half...  3.17 us
    pallas_call x4, Pallas kernels, up(): pl.pallas_call(lambda *refs: up_kernel(level, last, STATE // chips, half...  2.96 us
    pallas_call x2, Pallas kernels, assemble(): pl.pallas_call(lambda *refs: assemble_kernel(heads, chips, half, wide //...  2.62 us
  transfers between devices with their start and end apart: 25, of which 15 were waited for; matrix products, arithmetic and copies ran while one was open for 0% of the time, Pallas kernels for 25%

profile of v10, /device:TPU:0, one launch (start us, length us, event | category | flops | bytes accessed | tf_op | source)
XLA Modules:
  0.0 115.8 jit_solution(15236065477245479422)
XLA Ops:
  0.6 0.7 pad_add_fusion.refs_0_.place
  1.3 3.8 %summary.2 = (f32[1288,128]{1,0:T(8,128)}, f32[1280,128]{1,0:T(8,128)}, f32[10,128]{1,0:T(8,128)}, f32[8,128]{1,0:T(8,128)}, f32[256,128]{1,0:T(8,128)}, /*index...) custom-call(s32[3]{0:T(128)} %pad_add_fusion.refs_0_.place, bf16[256,2560]{1,0:T(8,128)(2,1)} %refs_0_.5, ...), custom_call_target="tpu_custom_call" | custom-call | flops 1 | bytes 1 | tf_op jit(solution)/shard_map/summary/pallas_call | solution.py:187
  5.1 0.5 collective-permute-start
  5.7 3.6 %summary.3 = (f32[1288,128]{1,0:T(8,128)}, f32[1280,128]{1,0:T(8,128)}, f32[10,128]{1,0:T(8,128)}) custom-call(s32[3]{0:T(128)} %pad_add_fusion.refs_0_.place, bf16[256,2560]{1,0:T(8,128)(2,1)} %refs_0_.5, bf16[256,2560]{1,0:T(8,128)(2,1)} %refs_1_.15, bf16[256,128]{1,0:T(8,128)(2,1)} %refs_2_.15, bf16[256,128]{1,0:T(8,128)(2,1)} %refs_3_.15, ...), custom_call_target="tpu_custom_call" | custom-call | flops 1 | bytes 1 | tf_op jit(solution)/shard_map/summary/pallas_call | solution.py:187
  9.3 0.1 collective-permute-start.2
  9.5 0.6 combine.2
  10.1 3.1 %collective-permute-start.1 = (f32[648,128]{1,0:T(8,128)S(1)}, f32[648,128]{1,0:T(8,128)S(1)}, u32[]{:S(2)}, u32[]{:S(2)}) collective-permute-start(f32[648,128]{1,0:T(8,128)S(1)} %get-tuple-element.110.refs_0_.refs_2_), channel_id=1, source_target_pairs={{0,2},{1,3},{2,0},{3,1},{4,6},{5,7},{6,4},{7,5},{8,10},{9,11},{10,... | collective-permute-start | bytes 995336 | tf_op jit(solution)/shard_map/ppermute | solution.py:683
  13.3 5.0 %intra.3 = (f32[256,2560]{1,0:T(8,128)S(1)}, f32[128,2560]{1,0:T(8,128)S(1)}, f32[128,2560]{1,0:T(8,128)S(1)}, f32[256,128]{1,0:T(8,128)S(1)}, f32[256,256]{1,0:T(8,128)S(1)}) custom-call(f32[648,128]{1,0:T(8,128)S(1)} %get-tuple-element.110.refs_0_.refs_2_, bf16[256,2560]{1,0:T(8,128)(2,1)S(1)} %copy-done, bf16[256,2560]{1,0:T(8,128)(2,1)S(1)} %copy-done.1, ...), custom_call_target="tpu_custom_call" | custom-call | flops 1 | bytes 1 | tf_op jit(solution)/shard_map/intra/pallas_call | solution.py:430
  18.3 2.9 %collective-permute-done.1.refs_3_ = f32[648,128]{1,0:T(8,128)S(1)} collective-permute-done((f32[648,128]{1,0:T(8,128)S(1)}, f32[648,128]{1,0:T(8,128)S(1)}, u32[]{:S(2)}, u32[]{:S(2)}) %collective-permute-start.1) | collective-permute-done | bytes 331808 | tf_op jit(solution)/shard_map/ppermute | solution.py:683
  21.2 0.6 combine.3
  21.9 1.8 %collective-permute-start.4 = (f32[648,128]{1,0:T(8,128)S(1)}, f32[648,128]{1,0:T(8,128)S(1)}, u32[]{:S(2)}, u32[]{:S(2)}) collective-permute-start(f32[648,128]{1,0:T(8,128)S(1)} %get-tuple-element.124.refs_2_), channel_id=1, source_target_pairs={{0,2},{1,3},{2,0},{3,1},{4,6},{5,7},{6,4},{7,5},{8,10},{9,11},{10,... | collective-permute-start | bytes 995336 | tf_op jit(solution)/shard_map/ppermute | solution.py:683
  23.7 0.8 up.4
  24.4 2.7 %collective-permute-start.3 = (f32[328,128]{1,0:T(8,128)S(1)}, f32[328,128]{1,0:T(8,128)S(1)}, u32[]{:S(2)}, u32[]{:S(2)}) collective-permute-start(f32[328,128]{1,0:T(8,128)S(1)} %get-tuple-element.120.refs_0_.refs_2_), channel_id=1, source_target_pairs={{0,4},{1,5},{2,6},{3,7},{4,0},{5,1},{6,2},{7,3},{8,12},{9,13},{10,... | collective-permute-start | bytes 503816 | tf_op jit(solution)/shard_map/ppermute | solution.py:683
  27.1 5.0 %intra.4 = (f32[256,2560]{1,0:T(8,128)S(1)}, f32[128,2560]{1,0:T(8,128)S(1)}, f32[128,2560]{1,0:T(8,128)S(1)}, f32[256,128]{1,0:T(8,128)S(1)}, f32[256,256]{1,0:T(8,128)S(1)}) custom-call(f32[328,128]{1,0:T(8,128)S(1)} %get-tuple-element.120.refs_0_.refs_2_, ...), custom_call_target="tpu_custom_call", output_to_operand_aliasing={{0}: (9, {}), {1}: (10, {}), {2}: (11, {})} | custom-call | flops 1 | bytes 1 | tf_op jit(solution)/shard_map/intra/pallas_call | solution.py:430
  32.1 1.6 %collective-permute-done.3.refs_3_ = f32[328,128]{1,0:T(8,128)S(1)} collective-permute-done((f32[328,128]{1,0:T(8,128)S(1)}, f32[328,128]{1,0:T(8,128)S(1)}, u32[]{:S(2)}, u32[]{:S(2)}) %collective-permute-start.3) | collective-permute-done | bytes 167968 | tf_op jit(solution)/shard_map/ppermute | solution.py:683
  33.7 1.1 collective-permute-done.4.refs_3_
  34.8 0.7 up.5.refs_0_
  35.5 1.3 %collective-permute-start.7 = (f32[328,128]{1,0:T(8,128)S(1)}, f32[328,128]{1,0:T(8,128)S(1)}, u32[]{:S(2)}, u32[]{:S(2)}) collective-permute-start(f32[328,128]{1,0:T(8,128)S(1)} %up.5.refs_0_), channel_id=1, source_target_pairs={{1,25},{3,27},{5,29},{7,31},{24,0},{26,2},{28,4},{30,6}} | collective-permute-start | bytes 503816 | tf_op jit(solution)/shard_map/ppermute | solution.py:683
  36.8 1.3 %collective-permute-start.6 = (f32[328,128]{1,0:T(8,128)S(1)}, f32[328,128]{1,0:T(8,128)S(1)}, u32[]{:S(2)}, u32[]{:S(2)}) collective-permute-start(f32[328,128]{1,0:T(8,128)S(1)} %up.5.refs_0_), channel_id=1, source_target_pairs={{1,17},{3,19},{5,21},{7,23},{9,25},{11,27},{13,29},{15,31},{16,0},... | collective-permute-start | bytes 503816 | tf_op jit(solution)/shard_map/ppermute | solution.py:683
  38.1 1.3 %collective-permute-start.5 = (f32[328,128]{1,0:T(8,128)S(1)}, f32[328,128]{1,0:T(8,128)S(1)}, u32[]{:S(2)}, u32[]{:S(2)}) collective-permute-start(f32[328,128]{1,0:T(8,128)S(1)} %up.5.refs_0_), channel_id=1, source_target_pairs={{1,9},{3,11},{5,13},{7,15},{8,0},{9,17},{10,2},{11,19},{12,4},{13,... | collective-permute-start | bytes 503816 | tf_op jit(solution)/shard_map/ppermute | solution.py:683
  39.4 0.7 up.6
  40.2 2.4 %collective-permute-start.8 = (f32[328,128]{1,0:T(8,128)S(1)}, f32[328,128]{1,0:T(8,128)S(1)}, u32[]{:S(2)}, u32[]{:S(2)}) collective-permute-start(f32[328,128]{1,0:T(8,128)S(1)} %get-tuple-element.138.refs_2_), channel_id=1, source_target_pairs={{0,4},{1,5},{2,6},{3,7},{4,0},{5,1},{6,2},{7,3},{8,12},{9,13},{10,... | collective-permute-start | bytes 503816 | tf_op jit(solution)/shard_map/ppermute | solution.py:683
  42.6 2.5 %intra.5 = (f32[256,2560]{1,0:T(8,128)S(1)}, f32[128,2560]{1,0:T(8,128)S(1)}, f32[128,2560]{1,0:T(8,128)S(1)}, f32[256,128]{1,0:T(8,128)S(1)}, f32[256,128]{1,0:T(8,128)S(1)}, /*index=5*/f32[256,128]{1,0:T(8,128)S(1)}) custom-call(f32[328,128]{1,0:T(8,128)S(1)} %up.5.refs_0_, ...), custom_call_target="tpu_custom_call", output_to_operand_aliasing={{0}: (9, {}), {1}: (10, {}), {2}: (11, {})} | custom-call | flops 1 | bytes 1 | tf_op jit(solution)/shard_map/intra/pallas_call | solution.py:430
  45.1 0.4 collective-permute-done.6.refs_5_
  45.5 0.5 collective-permute-done.5.refs_4_
  46.0 5.1 %collective-permute-done.8.refs_3_ = f32[328,128]{1,0:T(8,128)S(1)} collective-permute-done((f32[328,128]{1,0:T(8,128)S(1)}, f32[328,128]{1,0:T(8,128)S(1)}, u32[]{:S(2)}, u32[]{:S(2)}) %collective-permute-start.8) | collective-permute-done | bytes 167968 | tf_op jit(solution)/shard_map/ppermute | solution.py:683
  51.0 0.7 up.7
  51.8 1.3 %collective-permute-start.12 = (f32[328,128]{1,0:T(8,128)S(1)}, f32[328,128]{1,0:T(8,128)S(1)}, u32[]{:S(2)}, u32[]{:S(2)}) collective-permute-start(f32[328,128]{1,0:T(8,128)S(1)} %up.7), channel_id=1, source_target_pairs={{1,25},{3,27},{5,29},{7,31},{24,0},{26,2},{28,4},{30,6}} | collective-permute-start | bytes 503816 | tf_op jit(solution)/shard_map/ppermute | solution.py:683
  53.1 1.3 %collective-permute-start.11 = (f32[328,128]{1,0:T(8,128)S(1)}, f32[328,128]{1,0:T(8,128)S(1)}, u32[]{:S(2)}, u32[]{:S(2)}) collective-permute-start(f32[328,128]{1,0:T(8,128)S(1)} %up.7), channel_id=1, source_target_pairs={{1,17},{3,19},{5,21},{7,23},{9,25},{11,27},{13,29},{15,31},{16,0},... | collective-permute-start | bytes 503816 | tf_op jit(solution)/shard_map/ppermute | solution.py:683
  54.4 1.5 %collective-permute-start.10 = (f32[328,128]{1,0:T(8,128)S(1)}, f32[328,128]{1,0:T(8,128)S(1)}, u32[]{:S(2)}, u32[]{:S(2)}) collective-permute-start(f32[328,128]{1,0:T(8,128)S(1)} %up.7), channel_id=1, source_target_pairs={{1,9},{3,11},{5,13},{7,15},{8,0},{9,17},{10,2},{11,19},{12,4},{13,... | collective-permute-start | bytes 503816 | tf_op jit(solution)/shard_map/ppermute | solution.py:683
  55.8 0.8 down.4
  56.7 11.2 %collective-permute-done.9.refs_5_ = f32[320,128]{1,0:T(8,128)S(1)} collective-permute-done((f32[320,128]{1,0:T(8,128)S(1)}, f32[320,128]{1,0:T(8,128)S(1)}, u32[]{:S(2)}, u32[]{:S(2)}) %collective-permute-start.9) | collective-permute-done | bytes 163872 | tf_op jit(solution)/shard_map/ppermute | solution.py:683
  68.0 0.8 down.5
  68.7 0.1 collective-permute-start.13
  68.8 0.8 down.6
  69.6 1.8 %collective-permute-start.14 = (f32[320,128]{1,0:T(8,128)S(1)}, f32[320,128]{1,0:T(8,128)S(1)}, u32[]{:S(2)}, u32[]{:S(2)}) collective-permute-start(f32[320,128]{1,0:T(8,128)S(1)} %get-tuple-element.170), channel_id=1, source_target_pairs={{0,4},{1,5},{2,6},{3,7},{4,0},{5,1},{6,2},{7,3},{8,12},{9,13},{10,... | collective-permute-start | bytes 491528 | tf_op jit(solution)/shard_map/ppermute | solution.py:683
  71.4 8.2 %collective-permute-done.14.refs_5_ = f32[320,128]{1,0:T(8,128)S(1)} collective-permute-done((f32[320,128]{1,0:T(8,128)S(1)}, f32[320,128]{1,0:T(8,128)S(1)}, u32[]{:S(2)}, u32[]{:S(2)}) %collective-permute-start.14) | collective-permute-done | bytes 163872 | tf_op jit(solution)/shard_map/ppermute | solution.py:683
  79.6 2.2 %collective-permute-done.13.got_ref = f32[640,128]{1,0:T(8,128)S(1)} collective-permute-done((f32[640,128]{1,0:T(8,128)S(1)}, f32[640,128]{1,0:T(8,128)S(1)}, u32[]{:S(2)}, u32[]{:S(2)}) %collective-permute-start.13) | collective-permute-done | bytes 327712 | tf_op jit(solution)/shard_map/ppermute | solution.py:683
  81.8 0.6 order.2.refs_5_
  82.4 0.1 collective-permute-start.15
  82.5 0.8 down.7
  83.3 0.3 collective-permute-start.16
  83.6 1.0 collective-permute-done.15.refs_6_
  84.5 1.3 %assemble.2 = (bf16[128,1280]{1,0:T(8,128)(2,1)S(1)}, bf16[128,1280]{1,0:T(8,128)(2,1)S(1)}, f32[8,128]{1,0:T(8,128)S(1)}) custom-call(s32[3]{0:T(128)S(1)} %copy-done.10, f32[256,128]{1,0:T(8,128)S(1)} %get-tuple-element.154.refs_1_.refs_9_, f32[1288,128]{1,0:T(8,128)S(1)} %collective-permute-done.refs_1_.refs_2_, ...), custom_call_target="tpu_custom_call" | custom-call | flops 1 | bytes 1 | tf_op jit(solution)/shard_map/assemble/pallas_call | solution.py:524
  85.8 3.8 %finish.3 = (bf16[256,2560]{1,0:T(8,128)(2,1)}, f32[256,128]{1,0:T(8,128)S(1)}, f32[256,128]{1,0:T(8,128)S(1)}, f32[256,128]{1,0:T(8,128)S(1)}, f32[8,128]{1,0:T(8,128)S(1)}) custom-call(bf16[256,2560]{1,0:T(8,128)(2,1)S(1)} %copy-done, bf16[256,2560]{1,0:T(8,128)(2,1)S(1)} %copy-done.1, bf16[256,128]{1,0:T(8,128)(2,1)S(1)} %copy-done.2, ...), custom_call_target="tpu_custom_call" | custom-call | flops 1 | bytes 1 | tf_op jit(solution)/shard_map/finish/pallas_call | solution.py:592
  89.6 3.8 %collective-permute-done.16.got_ref = f32[640,128]{1,0:T(8,128)S(1)} collective-permute-done((f32[640,128]{1,0:T(8,128)S(1)}, f32[640,128]{1,0:T(8,128)S(1)}, u32[]{:S(2)}, u32[]{:S(2)}) %collective-permute-start.16) | collective-permute-done | bytes 327712 | tf_op jit(solution)/shard_map/ppermute | solution.py:683
  93.4 0.6 order.3.refs_5_
  94.1 2.1 %collective-permute-done.17.refs_6_ = f32[1280,128]{1,0:T(8,128)S(1)} collective-permute-done((f32[1280,128]{1,0:T(8,128)S(1)}, f32[1280,128]{1,0:T(8,128)S(1)}, u32[]{:S(2)}, u32[]{:S(2)}) %collective-permute-start.17) | collective-permute-done | bytes 655392 | tf_op jit(solution)/shard_map/ppermute | solution.py:683
  96.2 1.3 %assemble.3 = (bf16[128,1280]{1,0:T(8,128)(2,1)S(1)}, bf16[128,1280]{1,0:T(8,128)(2,1)S(1)}, f32[8,128]{1,0:T(8,128)S(1)}) custom-call(s32[3]{0:T(128)S(1)} %copy-done.10, f32[8,128]{1,0:T(8,128)S(1)} %get-tuple-element.174.refs_12_.refs_1_, f32[1288,128]{1,0:T(8,128)S(1)} %collective-permute-done.2.refs_1_.refs_2_, ...), custom_call_target="tpu_custom_call" | custom-call | flops 1 | bytes 1 | tf_op jit(solution)/shard_map/assemble/pallas_call | solution.py:524
  97.5 0.2 collective-permute-start.18
  97.7 1.8 %finish.4 = (bf16[256,2560]{1,0:T(8,128)(2,1)}, f32[256,128]{1,0:T(8,128)S(1)}, f32[256,128]{1,0:T(8,128)S(1)}, f32[256,128]{1,0:T(8,128)S(1)}, f32[8,128]{1,0:T(8,128)S(1)}) custom-call(bf16[256,2560]{1,0:T(8,128)(2,1)S(1)} %copy-done, bf16[256,2560]{1,0:T(8,128)(2,1)S(1)} %copy-done.1, ...), custom_call_target="tpu_custom_call", output_to_operand_aliasing={{0}: (12, {})} | custom-call | flops 1 | bytes 1 | tf_op jit(solution)/shard_map/finish/pallas_call | solution.py:592
  99.5 0.5 core_sum.1
  100.1 1.5 %collective-permute-start.21 = (f32[8,128]{1,0:T(8,128)S(1)}, f32[8,128]{1,0:T(8,128)S(1)}, u32[]{:S(2)}, u32[]{:S(2)}) collective-permute-start(f32[8,128]{1,0:T(8,128)S(1)} %get-tuple-element.193.refs_13_.total_ref), channel_id=1, source_target_pairs={{0,6},{1,7},{2,4},{3,5},{4,2},{5,3},{6,0},{7,1},{8,14},{9,15},{10,... | collective-permute-start | bytes 12296 | tf_op jit(solution)/shard_map/ppermute | solution.py:683
  101.6 0.3 collective-permute-start.20
  101.9 2.6 %collective-permute-start.19 = (f32[8,128]{1,0:T(8,128)S(1)}, f32[8,128]{1,0:T(8,128)S(1)}, u32[]{:S(2)}, u32[]{:S(2)}) collective-permute-start(f32[8,128]{1,0:T(8,128)S(1)} %get-tuple-element.193.refs_13_.total_ref), channel_id=1, source_target_pairs={{0,2},{1,3},{2,0},{3,1},{4,6},{5,7},{6,4},{7,5},{8,10},{9,11},{10,... | collective-permute-start | bytes 12296 | tf_op jit(solution)/shard_map/ppermute | solution.py:683
  104.5 1.8 %finish.5 = (bf16[256,2560]{1,0:T(8,128)(2,1)}, bf16[256,128]{1,0:T(8,128)(2,1)}, bf16[256,128]{1,0:T(8,128)(2,1)}, f32[40,256]{1,0:T(8,128)S(1)}, f32[8,128]{1,0:T(8,128)S(1)}) custom-call(bf16[256,2560]{1,0:T(8,128)(2,1)S(1)} %copy-done, bf16[256,2560]{1,0:T(8,128)(2,1)S(1)} %copy-done.1, ...), custom_call_target="tpu_custom_call", output_to_operand_aliasing={{0}: (12, {})} | custom-call | flops 1 | bytes 1 | tf_op jit(solution)/shard_map/finish/pallas_call | solution.py:592
  106.4 0.6 chip_sum.1
  106.9 1.3 %collective-permute-start.24 = (f32[8,128]{1,0:T(8,128)S(1)}, f32[8,128]{1,0:T(8,128)S(1)}, u32[]{:S(2)}, u32[]{:S(2)}) collective-permute-start(f32[8,128]{1,0:T(8,128)S(1)} %get-tuple-element.201), channel_id=1, source_target_pairs={{24,0},{25,1},{26,2},{27,3},{28,4},{29,5},{30,6},{31,7}} | collective-permute-start | bytes 12296 | tf_op jit(solution)/shard_map/ppermute | solution.py:683
  108.2 1.3 %collective-permute-start.23 = (f32[8,128]{1,0:T(8,128)S(1)}, f32[8,128]{1,0:T(8,128)S(1)}, u32[]{:S(2)}, u32[]{:S(2)}) collective-permute-start(f32[8,128]{1,0:T(8,128)S(1)} %get-tuple-element.201), channel_id=1, source_target_pairs={{16,0},{17,1},{18,2},{19,3},{20,4},{21,5},{22,6},{23,7},{24,8},{25... | collective-permute-start | bytes 12296 | tf_op jit(solution)/shard_map/ppermute | solution.py:683
  109.5 1.3 %collective-permute-start.22 = (f32[8,128]{1,0:T(8,128)S(1)}, f32[8,128]{1,0:T(8,128)S(1)}, u32[]{:S(2)}, u32[]{:S(2)}) collective-permute-start(f32[8,128]{1,0:T(8,128)S(1)} %get-tuple-element.201), channel_id=1, source_target_pairs={{8,0},{9,1},{10,2},{11,3},{12,4},{13,5},{14,6},{15,7},{16,8},{17,9... | collective-permute-start | bytes 12296 | tf_op jit(solution)/shard_map/ppermute | solution.py:683
  110.8 2.5 %collective-permute-done.24.refs_3_ = f32[8,128]{1,0:T(8,128)S(1)} collective-permute-done((f32[8,128]{1,0:T(8,128)S(1)}, f32[8,128]{1,0:T(8,128)S(1)}, u32[]{:S(2)}, u32[]{:S(2)}) %collective-permute-start.24) | collective-permute-done | bytes 4128 | tf_op jit(solution)/shard_map/ppermute | solution.py:683
  113.3 0.4 collective-permute-done.23.refs_2_
  113.7 1.3 %collective-permute-done.22.refs_1_ = f32[8,128]{1,0:T(8,128)S(1)} collective-permute-done((f32[8,128]{1,0:T(8,128)S(1)}, f32[8,128]{1,0:T(8,128)S(1)}, u32[]{:S(2)}, u32[]{:S(2)}) %collective-permute-start.22) | collective-permute-done | bytes 4128 | tf_op jit(solution)/shard_map/ppermute | solution.py:683
  115.0 0.8 add_later.1
  (40 shorter events, 0.2 us)
Async XLA Ops:
  5.1 4.4 %collective-permute-start = (f32[1288,128]{1,0:T(8,128)}, f32[1288,128]{1,0:T(8,128)S(1)}, u32[]{:S(2)}, u32[]{:S(2)}) collective-permute-start(f32[1288,128]{1,0:T(8,128)} %get-tuple-element.105), channel_id=1, source_target_pairs={{0,1},{1,0},{2,3},{3,2},{4,5},{5,4},{6,7},{7,6},{8,9},{9,8},{10,11... | collective-permute-start | bytes 1978376 | tf_op jit(solution)/shard_map/ppermute | solution.py:683
  5.6 3.9 %copy-start.9 = (f32[1280,128]{1,0:T(8,128)S(1)}, f32[1280,128]{1,0:T(8,128)}, u32[]{:S(2)}) copy-start(f32[1280,128]{1,0:T(8,128)} %get-tuple-element.106.refs_2_) | copy-start | bytes 1966084
  5.6 3.9 %copy-start.10 = (s32[3]{0:T(128)S(1)}, s32[3]{0:T(128)}, u32[]{:S(2)}) copy-start(s32[3]{0:T(128)} %pad_add_fusion.refs_0_.place) | copy-start | bytes 40
  5.6 3.9 %copy-start.11 = (f32[8,128]{1,0:T(8,128)S(1)}, f32[8,128]{1,0:T(8,128)}, u32[]{:S(2)}) copy-start(f32[8,128]{1,0:T(8,128)} %get-tuple-element.108.refs_4_.refs_5_.after_ref) | copy-start | bytes 12292
  5.6 3.9 %copy-start.13 = (f32[10,128]{1,0:T(8,128)S(1)}, f32[10,128]{1,0:T(8,128)}, u32[]{:S(2)}) copy-start(f32[10,128]{1,0:T(8,128)} %get-tuple-element.107.refs_3_) | copy-start | bytes 15364
  5.6 7.6 %copy-start.1 = (bf16[256,2560]{1,0:T(8,128)(2,1)S(1)}, bf16[256,2560]{1,0:T(8,128)(2,1)}, u32[]{:S(2)}) copy-start(bf16[256,2560]{1,0:T(8,128)(2,1)} %refs_1_.15) | copy-start | bytes 3932164
  5.6 7.6 %copy-start.2 = (bf16[256,128]{1,0:T(8,128)(2,1)S(1)}, bf16[256,128]{1,0:T(8,128)(2,1)}, u32[]{:S(2)}) copy-start(bf16[256,128]{1,0:T(8,128)(2,1)} %refs_2_.15) | copy-start | bytes 196612
  5.6 7.6 %copy-start.3 = (bf16[256,128]{1,0:T(8,128)(2,1)S(1)}, bf16[256,128]{1,0:T(8,128)(2,1)}, u32[]{:S(2)}) copy-start(bf16[256,128]{1,0:T(8,128)(2,1)} %refs_3_.15) | copy-start | bytes 196612
  5.6 7.6 %copy-start.4 = (bf16[256,128]{1,0:T(8,128)(2,1)S(1)}, bf16[256,128]{1,0:T(8,128)(2,1)}, u32[]{:S(2)}) copy-start(bf16[256,128]{1,0:T(8,128)(2,1)} %get-tuple-element.103.refs_6_.refs_7_.refs_4_) | copy-start | bytes 196612
  5.6 7.6 %copy-start.5 = (bf16[256,128]{1,0:T(8,128)(2,1)S(1)}, bf16[256,128]{1,0:T(8,128)(2,1)}, u32[]{:S(2)}) copy-start(bf16[256,128]{1,0:T(8,128)(2,1)} %get-tuple-element.104.refs_7_.refs_8_.refs_5_) | copy-start | bytes 196612
  5.7 7.6 %copy-start.6 = (f32[256,128]{1,0:T(8,128)S(1)}, f32[256,128]{1,0:T(8,128)}, u32[]{:S(2)}) copy-start(f32[256,128]{1,0:T(8,128)} %get-tuple-element.112.refs_6_) | copy-start | bytes 393220
  5.7 7.6 %copy-start.7 = (f32[40,256]{1,0:T(8,128)S(1)}, f32[40,256]{1,0:T(8,128)}, u32[]{:S(2)}) copy-start(f32[40,256]{1,0:T(8,128)} %refs_5_.7) | copy-start | bytes 122884
  9.3 3.9 %copy-start = (bf16[256,2560]{1,0:T(8,128)(2,1)S(1)}, bf16[256,2560]{1,0:T(8,128)(2,1)}, u32[]{:S(2)}) copy-start(bf16[256,2560]{1,0:T(8,128)(2,1)} %refs_0_.5) | copy-start | bytes 3932164
  9.3 9.0 %collective-permute-start.2 = (f32[1288,128]{1,0:T(8,128)}, f32[1288,128]{1,0:T(8,128)S(1)}, u32[]{:S(2)}, u32[]{:S(2)}) collective-permute-start(f32[1288,128]{1,0:T(8,128)} %get-tuple-element.111), channel_id=1, source_target_pairs={{0,1},{1,0},{2,3},{3,2},{4,5},{5,4},{6,7},{7,6},{8,9},{9,8},{10,11... | collective-permute-start | bytes 1978376 | tf_op jit(solution)/shard_map/ppermute | solution.py:683
  10.1 11.1 %collective-permute-start.1 = (f32[648,128]{1,0:T(8,128)S(1)}, f32[648,128]{1,0:T(8,128)S(1)}, u32[]{:S(2)}, u32[]{:S(2)}) collective-permute-start(f32[648,128]{1,0:T(8,128)S(1)} %get-tuple-element.110.refs_0_.refs_2_), channel_id=1, source_target_pairs={{0,2},{1,3},{2,0},{3,1},{4,6},{5,7},{6,4},{7,5},{8,10},{9,11},{10,... | collective-permute-start | bytes 995336 | tf_op jit(solution)/shard_map/ppermute | solution.py:683
  13.2 8.0 %copy-start.8 = (f32[1280,128]{1,0:T(8,128)S(1)}, f32[1280,128]{1,0:T(8,128)}, u32[]{:S(2)}) copy-start(f32[1280,128]{1,0:T(8,128)} %get-tuple-element.122.refs_2_) | copy-start | bytes 1966084
  13.3 8.0 %copy-start.12 = (f32[10,128]{1,0:T(8,128)S(1)}, f32[10,128]{1,0:T(8,128)}, u32[]{:S(2)}) copy-start(f32[10,128]{1,0:T(8,128)} %get-tuple-element.123.refs_3_) | copy-start | bytes 15364
  21.9 12.9 %collective-permute-start.4 = (f32[648,128]{1,0:T(8,128)S(1)}, f32[648,128]{1,0:T(8,128)S(1)}, u32[]{:S(2)}, u32[]{:S(2)}) collective-permute-start(f32[648,128]{1,0:T(8,128)S(1)} %get-tuple-element.124.refs_2_), channel_id=1, source_target_pairs={{0,2},{1,3},{2,0},{3,1},{4,6},{5,7},{6,4},{7,5},{8,10},{9,11},{10,... | collective-permute-start | bytes 995336 | tf_op jit(solution)/shard_map/ppermute | solution.py:683
  24.4 9.3 %collective-permute-start.3 = (f32[328,128]{1,0:T(8,128)S(1)}, f32[328,128]{1,0:T(8,128)S(1)}, u32[]{:S(2)}, u32[]{:S(2)}) collective-permute-start(f32[328,128]{1,0:T(8,128)S(1)} %get-tuple-element.120.refs_0_.refs_2_), channel_id=1, source_target_pairs={{0,4},{1,5},{2,6},{3,7},{4,0},{5,1},{6,2},{7,3},{8,12},{9,13},{10,... | collective-permute-start | bytes 503816 | tf_op jit(solution)/shard_map/ppermute | solution.py:683
  35.5 9.5 %collective-permute-start.7 = (f32[328,128]{1,0:T(8,128)S(1)}, f32[328,128]{1,0:T(8,128)S(1)}, u32[]{:S(2)}, u32[]{:S(2)}) collective-permute-start(f32[328,128]{1,0:T(8,128)S(1)} %up.5.refs_0_), channel_id=1, source_target_pairs={{1,25},{3,27},{5,29},{7,31},{24,0},{26,2},{28,4},{30,6}} | collective-permute-start | bytes 503816 | tf_op jit(solution)/shard_map/ppermute | solution.py:683
  36.8 8.7 %collective-permute-start.6 = (f32[328,128]{1,0:T(8,128)S(1)}, f32[328,128]{1,0:T(8,128)S(1)}, u32[]{:S(2)}, u32[]{:S(2)}) collective-permute-start(f32[328,128]{1,0:T(8,128)S(1)} %up.5.refs_0_), channel_id=1, source_target_pairs={{1,17},{3,19},{5,21},{7,23},{9,25},{11,27},{13,29},{15,31},{16,0},... | collective-permute-start | bytes 503816 | tf_op jit(solution)/shard_map/ppermute | solution.py:683
  38.1 7.9 %collective-permute-start.5 = (f32[328,128]{1,0:T(8,128)S(1)}, f32[328,128]{1,0:T(8,128)S(1)}, u32[]{:S(2)}, u32[]{:S(2)}) collective-permute-start(f32[328,128]{1,0:T(8,128)S(1)} %up.5.refs_0_), channel_id=1, source_target_pairs={{1,9},{3,11},{5,13},{7,15},{8,0},{9,17},{10,2},{11,19},{12,4},{13,... | collective-permute-start | bytes 503816 | tf_op jit(solution)/shard_map/ppermute | solution.py:683
  40.2 10.9 %collective-permute-start.8 = (f32[328,128]{1,0:T(8,128)S(1)}, f32[328,128]{1,0:T(8,128)S(1)}, u32[]{:S(2)}, u32[]{:S(2)}) collective-permute-start(f32[328,128]{1,0:T(8,128)S(1)} %get-tuple-element.138.refs_2_), channel_id=1, source_target_pairs={{0,4},{1,5},{2,6},{3,7},{4,0},{5,1},{6,2},{7,3},{8,12},{9,13},{10,... | collective-permute-start | bytes 503816 | tf_op jit(solution)/shard_map/ppermute | solution.py:683
  51.8 16.2 %collective-permute-start.12 = (f32[328,128]{1,0:T(8,128)S(1)}, f32[328,128]{1,0:T(8,128)S(1)}, u32[]{:S(2)}, u32[]{:S(2)}) collective-permute-start(f32[328,128]{1,0:T(8,128)S(1)} %up.7), channel_id=1, source_target_pairs={{1,25},{3,27},{5,29},{7,31},{24,0},{26,2},{28,4},{30,6}} | collective-permute-start | bytes 503816 | tf_op jit(solution)/shard_map/ppermute | solution.py:683
  53.1 14.9 %collective-permute-start.11 = (f32[328,128]{1,0:T(8,128)S(1)}, f32[328,128]{1,0:T(8,128)S(1)}, u32[]{:S(2)}, u32[]{:S(2)}) collective-permute-start(f32[328,128]{1,0:T(8,128)S(1)} %up.7), channel_id=1, source_target_pairs={{1,17},{3,19},{5,21},{7,23},{9,25},{11,27},{13,29},{15,31},{16,0},... | collective-permute-start | bytes 503816 | tf_op jit(solution)/shard_map/ppermute | solution.py:683
  54.4 13.6 %collective-permute-start.10 = (f32[328,128]{1,0:T(8,128)S(1)}, f32[328,128]{1,0:T(8,128)S(1)}, u32[]{:S(2)}, u32[]{:S(2)}) collective-permute-start(f32[328,128]{1,0:T(8,128)S(1)} %up.7), channel_id=1, source_target_pairs={{1,9},{3,11},{5,13},{7,15},{8,0},{9,17},{10,2},{11,19},{12,4},{13,... | collective-permute-start | bytes 503816 | tf_op jit(solution)/shard_map/ppermute | solution.py:683
  56.6 11.3 %collective-permute-start.9 = (f32[320,128]{1,0:T(8,128)S(1)}, f32[320,128]{1,0:T(8,128)S(1)}, u32[]{:S(2)}, u32[]{:S(2)}) collective-permute-start(f32[320,128]{1,0:T(8,128)S(1)} %get-tuple-element.161), channel_id=1, source_target_pairs={{0,4},{1,5},{2,6},{3,7},{4,0},{5,1},{6,2},{7,3},{8,12},{9,13},{10,... | collective-permute-start | bytes 491528 | tf_op jit(solution)/shard_map/ppermute | solution.py:683
  68.7 13.0 %collective-permute-start.13 = (f32[640,128]{1,0:T(8,128)S(1)}, f32[640,128]{1,0:T(8,128)S(1)}, u32[]{:S(2)}, u32[]{:S(2)}) collective-permute-start(f32[640,128]{1,0:T(8,128)S(1)} %get-tuple-element.166), channel_id=1, source_target_pairs={{0,2},{1,3},{2,0},{3,1},{4,6},{5,7},{6,4},{7,5},{8,10},{9,11},{10,... | collective-permute-start | bytes 983048 | tf_op jit(solution)/shard_map/ppermute | solution.py:683
  69.6 10.0 %collective-permute-start.14 = (f32[320,128]{1,0:T(8,128)S(1)}, f32[320,128]{1,0:T(8,128)S(1)}, u32[]{:S(2)}, u32[]{:S(2)}) collective-permute-start(f32[320,128]{1,0:T(8,128)S(1)} %get-tuple-element.170), channel_id=1, source_target_pairs={{0,4},{1,5},{2,6},{3,7},{4,0},{5,1},{6,2},{7,3},{8,12},{9,13},{10,... | collective-permute-start | bytes 491528 | tf_op jit(solution)/shard_map/ppermute | solution.py:683
  82.4 2.2 %collective-permute-start.15 = (f32[1280,128]{1,0:T(8,128)S(1)}, f32[1280,128]{1,0:T(8,128)S(1)}, u32[]{:S(2)}, u32[]{:S(2)}) collective-permute-start(f32[1280,128]{1,0:T(8,128)S(1)} %order.2.refs_5_), channel_id=1, source_target_pairs={{0,1},{1,0},{2,3},{3,2},{4,5},{5,4},{6,7},{7,6},{8,9},{9,8},{10,11... | collective-permute-start | bytes 1966088 | tf_op jit(solution)/shard_map/ppermute | solution.py:683
  83.3 10.2 %collective-permute-start.16 = (f32[640,128]{1,0:T(8,128)S(1)}, f32[640,128]{1,0:T(8,128)S(1)}, u32[]{:S(2)}, u32[]{:S(2)}) collective-permute-start(f32[640,128]{1,0:T(8,128)S(1)} %get-tuple-element.183), channel_id=1, source_target_pairs={{0,2},{1,3},{2,0},{3,1},{4,6},{5,7},{6,4},{7,5},{8,10},{9,11},{10,... | collective-permute-start | bytes 983048 | tf_op jit(solution)/shard_map/ppermute | solution.py:683
  94.0 2.2 %collective-permute-start.17 = (f32[1280,128]{1,0:T(8,128)S(1)}, f32[1280,128]{1,0:T(8,128)S(1)}, u32[]{:S(2)}, u32[]{:S(2)}) collective-permute-start(f32[1280,128]{1,0:T(8,128)S(1)} %order.3.refs_5_), channel_id=1, source_target_pairs={{0,1},{1,0},{2,3},{3,2},{4,5},{5,4},{6,7},{7,6},{8,9},{9,8},{10,11... | collective-permute-start | bytes 1966088 | tf_op jit(solution)/shard_map/ppermute | solution.py:683
  97.5 2.0 %collective-permute-start.18 = (f32[8,128]{1,0:T(8,128)S(1)}, f32[8,128]{1,0:T(8,128)S(1)}, u32[]{:S(2)}, u32[]{:S(2)}) collective-permute-start(f32[8,128]{1,0:T(8,128)S(1)} %get-tuple-element.187.refs_13_.total_ref), channel_id=1, source_target_pairs={{0,1},{1,0},{2,3},{3,2},{4,5},{5,4},{6,7},{7,6},{8,9},{9,8},{10,11... | collective-permute-start | bytes 12296 | tf_op jit(solution)/shard_map/ppermute | solution.py:683
  100.1 6.3 %collective-permute-start.21 = (f32[8,128]{1,0:T(8,128)S(1)}, f32[8,128]{1,0:T(8,128)S(1)}, u32[]{:S(2)}, u32[]{:S(2)}) collective-permute-start(f32[8,128]{1,0:T(8,128)S(1)} %get-tuple-element.193.refs_13_.total_ref), channel_id=1, source_target_pairs={{0,6},{1,7},{2,4},{3,5},{4,2},{5,3},{6,0},{7,1},{8,14},{9,15},{10,... | collective-permute-start | bytes 12296 | tf_op jit(solution)/shard_map/ppermute | solution.py:683
  101.6 4.8 %collective-permute-start.20 = (f32[8,128]{1,0:T(8,128)S(1)}, f32[8,128]{1,0:T(8,128)S(1)}, u32[]{:S(2)}, u32[]{:S(2)}) collective-permute-start(f32[8,128]{1,0:T(8,128)S(1)} %get-tuple-element.193.refs_13_.total_ref), channel_id=1, source_target_pairs={{0,4},{1,5},{2,6},{3,7},{4,0},{5,1},{6,2},{7,3},{8,12},{9,13},{10,... | collective-permute-start | bytes 12296 | tf_op jit(solution)/shard_map/ppermute | solution.py:683
  101.9 4.5 %collective-permute-start.19 = (f32[8,128]{1,0:T(8,128)S(1)}, f32[8,128]{1,0:T(8,128)S(1)}, u32[]{:S(2)}, u32[]{:S(2)}) collective-permute-start(f32[8,128]{1,0:T(8,128)S(1)} %get-tuple-element.193.refs_13_.total_ref), channel_id=1, source_target_pairs={{0,2},{1,3},{2,0},{3,1},{4,6},{5,7},{6,4},{7,5},{8,10},{9,11},{10,... | collective-permute-start | bytes 12296 | tf_op jit(solution)/shard_map/ppermute | solution.py:683
  106.9 6.4 %collective-permute-start.24 = (f32[8,128]{1,0:T(8,128)S(1)}, f32[8,128]{1,0:T(8,128)S(1)}, u32[]{:S(2)}, u32[]{:S(2)}) collective-permute-start(f32[8,128]{1,0:T(8,128)S(1)} %get-tuple-element.201), channel_id=1, source_target_pairs={{24,0},{25,1},{26,2},{27,3},{28,4},{29,5},{30,6},{31,7}} | collective-permute-start | bytes 12296 | tf_op jit(solution)/shard_map/ppermute | solution.py:683
  108.2 5.5 %collective-permute-start.23 = (f32[8,128]{1,0:T(8,128)S(1)}, f32[8,128]{1,0:T(8,128)S(1)}, u32[]{:S(2)}, u32[]{:S(2)}) collective-permute-start(f32[8,128]{1,0:T(8,128)S(1)} %get-tuple-element.201), channel_id=1, source_target_pairs={{16,0},{17,1},{18,2},{19,3},{20,4},{21,5},{22,6},{23,7},{24,8},{25... | collective-permute-start | bytes 12296 | tf_op jit(solution)/shard_map/ppermute | solution.py:683
  109.5 5.5 %collective-permute-start.22 = (f32[8,128]{1,0:T(8,128)S(1)}, f32[8,128]{1,0:T(8,128)S(1)}, u32[]{:S(2)}, u32[]{:S(2)}) collective-permute-start(f32[8,128]{1,0:T(8,128)S(1)} %get-tuple-element.201), channel_id=1, source_target_pairs={{8,0},{9,1},{10,2},{11,3},{12,4},{13,5},{14,6},{15,7},{16,8},{17,9... | collective-permute-start | bytes 12296 | tf_op jit(solution)/shard_map/ppermute | solution.py:683

commit v11 on v10

--- a/solution.py
+++ b/solution.py
@@ -11,6 +11,7 @@
 HALVES = 2
 STRIP = 128
 META = 8
+PAD = 2 * META
 BIG_VMEM = 56 << 20
 SMALL_VMEM = 24 << 20
 F32 = jnp.float32
@@ -218,15 +219,17 @@
             for at in range(strip * part, size, strips * part):
                 rows = pl.ds(pl.multiple_of(base + at, part), part)
                 out_ref[at : at + part, :] = first_ref[rows, :] * decay + keep_ref[rows, :]
-    send_ref[size:, :] = first_ref[2 * size :, :] + log_ref[...]
+    meta = first_ref[2 * size :, :] + log_ref[...]
+    send_ref[size : size + META, :] = meta
+    send_ref[size + META :, :] = meta
 
 
 def halves(size):
     return (
-        [whole(size, STRIP), whole(size + META, STRIP)],
+        [whole(size, STRIP), whole(size + PAD, STRIP)],
         [
             jax.ShapeDtypeStruct((size, STRIP), F32),
-            jax.ShapeDtypeStruct((size + META, STRIP), F32),
+            jax.ShapeDtypeStruct((size + PAD, STRIP), F32),
         ],
     )
 
@@ -275,7 +278,7 @@
                 out_ref[at : at + part, :] = (
                     mine_ref[rows, :] * mine_wide[one, :] + got_ref[rows, :] * got_wide[one, :]
                 )
-    outs[-1][half:, :] = jnp.broadcast_to(mine_log + got_log, (META, STRIP))
+    outs[-1][half:, :] = jnp.broadcast_to(mine_log + got_log, (META if last else PAD, STRIP))
 
 
 def up(level, chips, half, strips, head_size, place, mine, send, got):
@@ -283,13 +286,14 @@
     last = 2 << level == chips
     out_specs, out_shape = halves(size if last else size // 2)
     if last:
-        out_specs, out_shape = out_specs[1:], out_shape[1:]
+        out_specs = [whole(size + META, STRIP)]
+        out_shape = [jax.ShapeDtypeStruct((size + META, STRIP), F32)]
     return pl.pallas_call(
         lambda *refs: up_kernel(
             level, last, STATE // chips, half * strips, strips, head_size, *refs
         ),
         grid=(1,),
-        in_specs=[SCALARS, whole(size, STRIP), tail_block(send), whole(size + META, STRIP)],
+        in_specs=[SCALARS, whole(size, STRIP), tail_block(send), whole(size + PAD, STRIP)],
         out_specs=out_specs,
         out_shape=out_shape,
         compiler_params=pltpu.CompilerParams(vmem_limit_bytes=SMALL_VMEM),
@@ -333,6 +337,7 @@
                 mine = jnp.where(ahead, 0.0, mine_ref[rows, :])
                 here_ref[rows, :] = entering * here_wide[one, :] + got
                 there_ref[rows, :] = entering * there_wide[one, :] + mine
+    there_ref[size:, :] = jnp.zeros((PAD, STRIP), F32)
 
 
 def down(level, chips, half, strips, head_size, place, mine, send, got, sources):
@@ -343,10 +348,13 @@
             level, top, STATE // chips, half * strips, strips, head_size, *refs
         ),
         grid=(1,),
-        in_specs=[SCALARS, whole(size, STRIP), tail_block(send), whole(size + META, STRIP)]
+        in_specs=[SCALARS, whole(size, STRIP), tail_block(send), whole(size + PAD, STRIP)]
         + [whole(*value.shape) for value in sources],
-        out_specs=[whole(size, STRIP)] * 2,
-        out_shape=[jax.ShapeDtypeStruct((size, STRIP), F32)] * 2,
+        out_specs=[whole(size, STRIP), whole(size + PAD, STRIP)],
+        out_shape=[
+            jax.ShapeDtypeStruct((size, STRIP), F32),
+            jax.ShapeDtypeStruct((size + PAD, STRIP), F32),
+        ],
         compiler_params=pltpu.CompilerParams(vmem_limit_bytes=SMALL_VMEM),
         cost_estimate=LITTLE,
         name="down",
@@ -464,20 +472,26 @@
     )(after, x, g, write_map, read_map, rates, *shared[1:], *earlier)
 
 
-def order_kernel(place, after_ref, here_ref, got_ref, out_ref):
+def order_kernel(place, after_ref, here_ref, got_ref, *outs):
     size = here_ref.shape[0]
     bit = place[1] & 1
-    out_ref[pl.ds(pl.multiple_of(bit * size, size), size), :] = here_ref[...]
-    out_ref[pl.ds(pl.multiple_of((1 - bit) * size, size), size), :] = got_ref[...]
-
-
-def order(place, after, here, got):
-    shape = (2 * here.shape[0], STRIP)
+    if len(outs) == 1:
+        outs[0][pl.ds(pl.multiple_of(bit * size, size), size), :] = here_ref[...]
+        outs[0][pl.ds(pl.multiple_of((1 - bit) * size, size), size), :] = got_ref[:size, :]
+    else:
+        here, got = here_ref[...], got_ref[:size, :]
+        outs[0][...] = jnp.where(bit == 0, here, got)
+        outs[1][...] = jnp.where(bit == 0, got, here)
+
+
+def order(pieces, place, after, here, got):
+    shape = (2 * here.shape[0] // pieces, STRIP)
     return pl.pallas_call(
         order_kernel,
+        grid=(1,),
         in_specs=[SCALARS, whole(META, STRIP), whole(*here.shape), whole(*got.shape)],
-        out_specs=whole(*shape),
-        out_shape=jax.ShapeDtypeStruct(shape, F32),
+        out_specs=[whole(*shape)] * pieces,
+        out_shape=[jax.ShapeDtypeStruct(shape, F32)] * pieces,
         compiler_params=pltpu.CompilerParams(vmem_limit_bytes=SMALL_VMEM),
         cost_estimate=LITTLE,
         name="order",
@@ -485,9 +499,11 @@
 
 
 def assemble_kernel(
-    heads, chips, half, head_size, place, after_ref, first_ref, state_own, back_own, own_ref, far_ref,
-    state_ref, back_ref, total_ref,
+    heads, chips, half, head_size, place, after_ref, first_ref, state_own, back_own, *refs,
 ):
+    state_ref, back_ref, total_ref = refs[-3:]
+    pieces = (len(refs) - 3) // 2
+    own_refs, far_refs = refs[:pieces], refs[pieces : 2 * pieces]
     lanes = state_ref.shape[1]
     strips = lanes // STRIP
     part = STATE // chips
@@ -501,8 +517,10 @@
         for strip in range(strips):
             wide = slice(strip * STRIP, (strip + 1) * STRIP)
             here = slice(quarter * size + strip * part, quarter * size + (strip + 1) * part)
-            own = own_ref[here, :] * decay[strip : strip + 1, :] + first_ref[here, :]
-            far = far_ref[here, :]
+            piece, at = divmod(here.start, own_refs[0].shape[0])
+            there = slice(at, at + part)
+            own = own_refs[piece][there, :] * decay[strip : strip + 1, :] + first_ref[here, :]
+            far = far_refs[piece][there, :]
             state = jnp.where(is_first, far, own).astype(BF16)
             back = jnp.where(is_first, own, far).astype(BF16)
             state_ref[rows, wide] = state
@@ -525,7 +543,7 @@
         lambda *refs: assemble_kernel(heads, chips, half, wide // heads, *refs),
         grid=(1,),
         in_specs=[SCALARS, whole(META, STRIP), whole(*first.shape), mine, mine]
-        + [whole(*own.shape), whole(*far.shape)],
+        + [whole(*value.shape) for value in (*own, *far)],
         out_specs=[whole(STATE, lanes), whole(STATE, lanes), whole(META, STRIP)],
         out_shape=[
             jax.ShapeDtypeStruct((STATE, lanes), BF16),
@@ -535,7 +553,7 @@
         compiler_params=pltpu.CompilerParams(vmem_limit_bytes=SMALL_VMEM),
         cost_estimate=LITTLE,
         name="assemble",
-    )(place, after, first, state_own, back_own, own, far)
+    )(place, after, first, state_own, back_own, *own, *far)
 
 
 def finish_kernel(
@@ -734,10 +752,9 @@
             waiting[half] = to_chip(send, 1 << level)
             return send
         else:
-            send = order(place, after, held[half][0], waiting[half])
-            held[half] = send
-            waiting[half] = to_core(send)
-            return send
+            held[half] = order(2 - half, place, after, held[half][0], waiting[half])
+            waiting[half] = [to_core(value) for value in held[half]]
+            return held[half][0]
         held[half].append((mine, send))
         waiting[half] = to_chip(send, 1 << step)
         return send

time: 116 us -> 107 us (0.922)
  waiting for transfers between devices: 44.3 us -> 30.3 us
  starting transfers between devices: 29.4 us -> 34.7 us
    ppermute x25 -> x26, waiting for transfers between devices: 44.3 us -> 30.3 us  [move(): return lax.ppermute(value, ('grp', 'seq'), pairs)]
    ppermute x25 -> x26, starting transfers between devices: 29.4 us -> 34.7 us  [move(): return lax.ppermute(value, ('grp', 'seq'), pairs)]
  transfers between devices with their start and end apart: 25 -> 26, of which waited for: 15 -> 16; matrix products, arithmetic and copies ran while one was open for 0% -> 0% of each run, Pallas kernels for 25% -> 27%
where the time goes in v11:
time: 107 us
  Pallas kernels  40.3 us (38%)
  starting transfers between devices  34.7 us (32%)
  waiting for transfers between devices  30.3 us (28%)
    ppermute x26, starting transfers between devices, move(): return lax.ppermute(value, ('grp', 'seq'), pairs)  34.7 us
    ppermute x26, waiting for transfers between devices, move(): return lax.ppermute(value, ('grp', 'seq'), pairs)  30.3 us
    pallas_call x3, Pallas kernels, intra(): pl.pallas_call(lambda *refs: intra_kernel(heads, wide // heads, start, la...  12.5 us
    pallas_call x2, Pallas kernels, summary(): pl.pallas_call(lambda *refs: summary_kernel(heads, chips, half, *refs), g...  7.4 us
    pallas_call x3, Pallas kernels, finish(): pl.pallas_call(lambda *refs: finish_kernel(heads, start, steps, last, *re...  7.33 us
    pallas_call x4, Pallas kernels, down(): pl.pallas_call(lambda *refs: down_kernel(level, top, STATE // chips, half...  3.15 us
    pallas_call x4, Pallas kernels, up(): pl.pallas_call(lambda *refs: up_kernel(level, last, STATE // chips, half...  2.96 us
    pallas_call x2, Pallas kernels, assemble(): pl.pallas_call(lambda *refs: assemble_kernel(heads, chips, half, wide //...  2.62 us
  transfers between devices with their start and end apart: 26, of which 16 were waited for; matrix products, arithmetic and copies ran while one was open for 0% of the time, Pallas kernels for 27%

profile of v11, /device:TPU:0, one launch (start us, length us, event | category | flops | bytes accessed | tf_op | source)
XLA Modules:
  0.0 106.9 jit_solution(15370398995431678637)
XLA Ops:
  0.6 0.6 pad_add_fusion.refs_0_.place
  1.2 3.8 %summary.2 = (f32[1288,128]{1,0:T(8,128)}, f32[1280,128]{1,0:T(8,128)}, f32[10,128]{1,0:T(8,128)}, f32[8,128]{1,0:T(8,128)}, f32[256,128]{1,0:T(8,128)}, /*index...) custom-call(s32[3]{0:T(128)} %pad_add_fusion.refs_0_.place, bf16[256,2560]{1,0:T(8,128)(2,1)} %refs_0_.5, ...), custom_call_target="tpu_custom_call" | custom-call | flops 1 | bytes 1 | tf_op jit(solution)/shard_map/summary/pallas_call | solution.py:188
  5.0 0.5 collective-permute-start
  5.6 3.6 %summary.3 = (f32[1288,128]{1,0:T(8,128)}, f32[1280,128]{1,0:T(8,128)}, f32[10,128]{1,0:T(8,128)}) custom-call(s32[3]{0:T(128)} %pad_add_fusion.refs_0_.place, bf16[256,2560]{1,0:T(8,128)(2,1)} %refs_0_.5, bf16[256,2560]{1,0:T(8,128)(2,1)} %refs_1_.15, bf16[256,128]{1,0:T(8,128)(2,1)} %refs_2_.15, bf16[256,128]{1,0:T(8,128)(2,1)} %refs_3_.15, ...), custom_call_target="tpu_custom_call" | custom-call | flops 1 | bytes 1 | tf_op jit(solution)/shard_map/summary/pallas_call | solution.py:188
  9.4 0.7 combine.2
  10.0 3.1 %collective-permute-start.1 = (f32[656,128]{1,0:T(8,128)S(1)}, f32[656,128]{1,0:T(8,128)S(1)}, u32[]{:S(2)}, u32[]{:S(2)}) collective-permute-start(f32[656,128]{1,0:T(8,128)S(1)} %get-tuple-element.112.refs_0_.refs_2_), channel_id=1, source_target_pairs={{0,2},{1,3},{2,0},{3,1},{4,6},{5,7},{6,4},{7,5},{8,10},{9,11},{10,... | collective-permute-start | bytes 1007624 | tf_op jit(solution)/shard_map/ppermute | solution.py:701
  13.2 5.0 %intra.3 = (f32[256,2560]{1,0:T(8,128)S(1)}, f32[128,2560]{1,0:T(8,128)S(1)}, f32[128,2560]{1,0:T(8,128)S(1)}, f32[256,128]{1,0:T(8,128)S(1)}, f32[256,256]{1,0:T(8,128)S(1)}) custom-call(f32[656,128]{1,0:T(8,128)S(1)} %get-tuple-element.112.refs_0_.refs_2_, bf16[256,2560]{1,0:T(8,128)(2,1)S(1)} %copy-done, bf16[256,2560]{1,0:T(8,128)(2,1)S(1)} %copy-done.1, ...), custom_call_target="tpu_custom_call" | custom-call | flops 1 | bytes 1 | tf_op jit(solution)/shard_map/intra/pallas_call | solution.py:438
  18.2 3.0 %collective-permute-done.1.refs_3_ = f32[656,128]{1,0:T(8,128)S(1)} collective-permute-done((f32[656,128]{1,0:T(8,128)S(1)}, f32[656,128]{1,0:T(8,128)S(1)}, u32[]{:S(2)}, u32[]{:S(2)}) %collective-permute-start.1) | collective-permute-done | bytes 335904 | tf_op jit(solution)/shard_map/ppermute | solution.py:701
  21.2 0.6 combine.3
  21.8 1.8 %collective-permute-start.4 = (f32[656,128]{1,0:T(8,128)S(1)}, f32[656,128]{1,0:T(8,128)S(1)}, u32[]{:S(2)}, u32[]{:S(2)}) collective-permute-start(f32[656,128]{1,0:T(8,128)S(1)} %get-tuple-element.126.refs_2_), channel_id=1, source_target_pairs={{0,2},{1,3},{2,0},{3,1},{4,6},{5,7},{6,4},{7,5},{8,10},{9,11},{10,... | collective-permute-start | bytes 1007624 | tf_op jit(solution)/shard_map/ppermute | solution.py:701
  23.6 0.8 up.4
  24.4 2.6 %collective-permute-start.3 = (f32[336,128]{1,0:T(8,128)S(1)}, f32[336,128]{1,0:T(8,128)S(1)}, u32[]{:S(2)}, u32[]{:S(2)}) collective-permute-start(f32[336,128]{1,0:T(8,128)S(1)} %get-tuple-element.122.refs_0_.refs_2_), channel_id=1, source_target_pairs={{0,4},{1,5},{2,6},{3,7},{4,0},{5,1},{6,2},{7,3},{8,12},{9,13},{10,... | collective-permute-start | bytes 516104 | tf_op jit(solution)/shard_map/ppermute | solution.py:701
  27.0 5.0 %intra.4 = (f32[256,2560]{1,0:T(8,128)S(1)}, f32[128,2560]{1,0:T(8,128)S(1)}, f32[128,2560]{1,0:T(8,128)S(1)}, f32[256,128]{1,0:T(8,128)S(1)}, f32[256,256]{1,0:T(8,128)S(1)}) custom-call(f32[336,128]{1,0:T(8,128)S(1)} %get-tuple-element.122.refs_0_.refs_2_, ...), custom_call_target="tpu_custom_call", output_to_operand_aliasing={{0}: (9, {}), {1}: (10, {}), {2}: (11, {})} | custom-call | flops 1 | bytes 1 | tf_op jit(solution)/shard_map/intra/pallas_call | solution.py:438
  32.0 1.8 %collective-permute-done.3.refs_3_ = f32[336,128]{1,0:T(8,128)S(1)} collective-permute-done((f32[336,128]{1,0:T(8,128)S(1)}, f32[336,128]{1,0:T(8,128)S(1)}, u32[]{:S(2)}, u32[]{:S(2)}) %collective-permute-start.3) | collective-permute-done | bytes 172064 | tf_op jit(solution)/shard_map/ppermute | solution.py:701
  33.8 1.1 collective-permute-done.4.refs_3_
  34.9 0.8 up.6
  35.6 2.4 %collective-permute-start.8 = (f32[336,128]{1,0:T(8,128)S(1)}, f32[336,128]{1,0:T(8,128)S(1)}, u32[]{:S(2)}, u32[]{:S(2)}) collective-permute-start(f32[336,128]{1,0:T(8,128)S(1)} %get-tuple-element.140.refs_2_), channel_id=1, source_target_pairs={{0,4},{1,5},{2,6},{3,7},{4,0},{5,1},{6,2},{7,3},{8,12},{9,13},{10,... | collective-permute-start | bytes 516104 | tf_op jit(solution)/shard_map/ppermute | solution.py:701
  38.0 0.7 up.5.refs_0_
  38.8 1.3 %collective-permute-start.7 = (f32[328,128]{1,0:T(8,128)S(1)}, f32[328,128]{1,0:T(8,128)S(1)}, u32[]{:S(2)}, u32[]{:S(2)}) collective-permute-start(f32[328,128]{1,0:T(8,128)S(1)} %up.5.refs_0_), channel_id=1, source_target_pairs={{1,25},{3,27},{5,29},{7,31},{24,0},{26,2},{28,4},{30,6}} | collective-permute-start | bytes 503816 | tf_op jit(solution)/shard_map/ppermute | solution.py:701
  40.1 1.3 %collective-permute-start.6 = (f32[328,128]{1,0:T(8,128)S(1)}, f32[328,128]{1,0:T(8,128)S(1)}, u32[]{:S(2)}, u32[]{:S(2)}) collective-permute-start(f32[328,128]{1,0:T(8,128)S(1)} %up.5.refs_0_), channel_id=1, source_target_pairs={{1,17},{3,19},{5,21},{7,23},{9,25},{11,27},{13,29},{15,31},{16,0},... | collective-permute-start | bytes 503816 | tf_op jit(solution)/shard_map/ppermute | solution.py:701
  41.4 1.3 %collective-permute-start.5 = (f32[328,128]{1,0:T(8,128)S(1)}, f32[328,128]{1,0:T(8,128)S(1)}, u32[]{:S(2)}, u32[]{:S(2)}) collective-permute-start(f32[328,128]{1,0:T(8,128)S(1)} %up.5.refs_0_), channel_id=1, source_target_pairs={{1,9},{3,11},{5,13},{7,15},{8,0},{9,17},{10,2},{11,19},{12,4},{13,... | collective-permute-start | bytes 503816 | tf_op jit(solution)/shard_map/ppermute | solution.py:701
  42.7 2.5 %intra.5 = (f32[256,2560]{1,0:T(8,128)S(1)}, f32[128,2560]{1,0:T(8,128)S(1)}, f32[128,2560]{1,0:T(8,128)S(1)}, f32[256,128]{1,0:T(8,128)S(1)}, f32[256,128]{1,0:T(8,128)S(1)}, /*index=5*/f32[256,128]{1,0:T(8,128)S(1)}) custom-call(f32[328,128]{1,0:T(8,128)S(1)} %up.5.refs_0_, ...), custom_call_target="tpu_custom_call", output_to_operand_aliasing={{0}: (9, {}), {1}: (10, {}), {2}: (11, {})} | custom-call | flops 1 | bytes 1 | tf_op jit(solution)/shard_map/intra/pallas_call | solution.py:438
  45.2 1.9 %collective-permute-done.7.refs_6_ = f32[328,128]{1,0:T(8,128)S(1)} collective-permute-done((f32[328,128]{1,0:T(8,128)S(1)}, f32[328,128]{1,0:T(8,128)S(1)}, u32[]{:S(2)}, u32[]{:S(2)}) %collective-permute-start.7) | collective-permute-done | bytes 167968 | tf_op jit(solution)/shard_map/ppermute | solution.py:701
  47.0 1.7 %collective-permute-done.6.refs_5_ = f32[328,128]{1,0:T(8,128)S(1)} collective-permute-done((f32[328,128]{1,0:T(8,128)S(1)}, f32[328,128]{1,0:T(8,128)S(1)}, u32[]{:S(2)}, u32[]{:S(2)}) %collective-permute-start.6) | collective-permute-done | bytes 167968 | tf_op jit(solution)/shard_map/ppermute | solution.py:701
  48.8 0.8 down.4
  49.6 0.8 collective-permute-start.9
  50.4 0.7 up.7
  51.1 1.3 %collective-permute-start.12 = (f32[328,128]{1,0:T(8,128)S(1)}, f32[328,128]{1,0:T(8,128)S(1)}, u32[]{:S(2)}, u32[]{:S(2)}) collective-permute-start(f32[328,128]{1,0:T(8,128)S(1)} %up.7), channel_id=1, source_target_pairs={{1,25},{3,27},{5,29},{7,31},{24,0},{26,2},{28,4},{30,6}} | collective-permute-start | bytes 503816 | tf_op jit(solution)/shard_map/ppermute | solution.py:701
  52.4 1.3 %collective-permute-start.11 = (f32[328,128]{1,0:T(8,128)S(1)}, f32[328,128]{1,0:T(8,128)S(1)}, u32[]{:S(2)}, u32[]{:S(2)}) collective-permute-start(f32[328,128]{1,0:T(8,128)S(1)} %up.7), channel_id=1, source_target_pairs={{1,17},{3,19},{5,21},{7,23},{9,25},{11,27},{13,29},{15,31},{16,0},... | collective-permute-start | bytes 503816 | tf_op jit(solution)/shard_map/ppermute | solution.py:701
  53.7 1.5 %collective-permute-start.10 = (f32[328,128]{1,0:T(8,128)S(1)}, f32[328,128]{1,0:T(8,128)S(1)}, u32[]{:S(2)}, u32[]{:S(2)}) collective-permute-start(f32[328,128]{1,0:T(8,128)S(1)} %up.7), channel_id=1, source_target_pairs={{1,9},{3,11},{5,13},{7,15},{8,0},{9,17},{10,2},{11,19},{12,4},{13,... | collective-permute-start | bytes 503816 | tf_op jit(solution)/shard_map/ppermute | solution.py:701
  55.2 4.2 %collective-permute-done.12.refs_6_ = f32[328,128]{1,0:T(8,128)S(1)} collective-permute-done((f32[328,128]{1,0:T(8,128)S(1)}, f32[328,128]{1,0:T(8,128)S(1)}, u32[]{:S(2)}, u32[]{:S(2)}) %collective-permute-start.12) | collective-permute-done | bytes 167968 | tf_op jit(solution)/shard_map/ppermute | solution.py:701
  59.4 1.7 %collective-permute-done.11.refs_5_ = f32[328,128]{1,0:T(8,128)S(1)} collective-permute-done((f32[328,128]{1,0:T(8,128)S(1)}, f32[328,128]{1,0:T(8,128)S(1)}, u32[]{:S(2)}, u32[]{:S(2)}) %collective-permute-start.11) | collective-permute-done | bytes 167968 | tf_op jit(solution)/shard_map/ppermute | solution.py:701
  61.1 0.8 down.5
  61.9 2.4 %collective-permute-start.13 = (f32[656,128]{1,0:T(8,128)S(1)}, f32[656,128]{1,0:T(8,128)S(1)}, u32[]{:S(2)}, u32[]{:S(2)}) collective-permute-start(f32[656,128]{1,0:T(8,128)S(1)} %get-tuple-element.168), channel_id=1, source_target_pairs={{0,2},{1,3},{2,0},{3,1},{4,6},{5,7},{6,4},{7,5},{8,10},{9,11},{10,... | collective-permute-start | bytes 1007624 | tf_op jit(solution)/shard_map/ppermute | solution.py:701
  64.2 0.8 down.6
  65.0 1.9 %collective-permute-start.14 = (f32[336,128]{1,0:T(8,128)S(1)}, f32[336,128]{1,0:T(8,128)S(1)}, u32[]{:S(2)}, u32[]{:S(2)}) collective-permute-start(f32[336,128]{1,0:T(8,128)S(1)} %get-tuple-element.172), channel_id=1, source_target_pairs={{0,4},{1,5},{2,6},{3,7},{4,0},{5,1},{6,2},{7,3},{8,12},{9,13},{10,... | collective-permute-start | bytes 516104 | tf_op jit(solution)/shard_map/ppermute | solution.py:701
  67.0 5.8 %collective-permute-done.14.refs_5_ = f32[336,128]{1,0:T(8,128)S(1)} collective-permute-done((f32[336,128]{1,0:T(8,128)S(1)}, f32[336,128]{1,0:T(8,128)S(1)}, u32[]{:S(2)}, u32[]{:S(2)}) %collective-permute-start.14) | collective-permute-done | bytes 172064 | tf_op jit(solution)/shard_map/ppermute | solution.py:701
  72.9 0.8 down.7
  73.7 1.7 %collective-permute-start.17 = (f32[656,128]{1,0:T(8,128)S(1)}, f32[656,128]{1,0:T(8,128)S(1)}, u32[]{:S(2)}, u32[]{:S(2)}) collective-permute-start(f32[656,128]{1,0:T(8,128)S(1)} %get-tuple-element.187), channel_id=1, source_target_pairs={{0,2},{1,3},{2,0},{3,1},{4,6},{5,7},{6,4},{7,5},{8,10},{9,11},{10,... | collective-permute-start | bytes 1007624 | tf_op jit(solution)/shard_map/ppermute | solution.py:701
  75.4 0.6 order.2
  76.1 0.5 collective-permute-start.16
  76.6 1.1 %collective-permute-done.15.refs_7_ = f32[640,128]{1,0:T(8,128)S(1)} collective-permute-done((f32[640,128]{1,0:T(8,128)S(1)}, f32[640,128]{1,0:T(8,128)S(1)}, u32[]{:S(2)}, u32[]{:S(2)}) %collective-permute-start.15) | collective-permute-done | bytes 327712 | tf_op jit(solution)/shard_map/ppermute | solution.py:701
  77.7 0.5 collective-permute-done.16.refs_8_
  78.2 1.3 %assemble.2 = (bf16[128,1280]{1,0:T(8,128)(2,1)S(1)}, bf16[128,1280]{1,0:T(8,128)(2,1)S(1)}, f32[8,128]{1,0:T(8,128)S(1)}) custom-call(s32[3]{0:T(128)S(1)} %copy-done.10, f32[256,128]{1,0:T(8,128)S(1)} %get-tuple-element.156.refs_1_.refs_9_, f32[1288,128]{1,0:T(8,128)S(1)} %collective-permute-done.refs_1_.refs_2_, ...), custom_call_target="tpu_custom_call" | custom-call | flops 1 | bytes 1 | tf_op jit(solution)/shard_map/assemble/pallas_call | solution.py:542
  79.5 3.8 %finish.3 = (bf16[256,2560]{1,0:T(8,128)(2,1)}, f32[256,128]{1,0:T(8,128)S(1)}, f32[256,128]{1,0:T(8,128)S(1)}, f32[256,128]{1,0:T(8,128)S(1)}, f32[8,128]{1,0:T(8,128)S(1)}) custom-call(bf16[256,2560]{1,0:T(8,128)(2,1)S(1)} %copy-done, bf16[256,2560]{1,0:T(8,128)(2,1)S(1)} %copy-done.1, bf16[256,128]{1,0:T(8,128)(2,1)S(1)} %copy-done.2, ...), custom_call_target="tpu_custom_call" | custom-call | flops 1 | bytes 1 | tf_op jit(solution)/shard_map/finish/pallas_call | solution.py:610
  83.3 0.6 order.3.refs_5_
  83.9 0.2 collective-permute-start.18
  84.1 2.0 %collective-permute-done.18.refs_6_ = f32[1280,128]{1,0:T(8,128)S(1)} collective-permute-done((f32[1280,128]{1,0:T(8,128)S(1)}, f32[1280,128]{1,0:T(8,128)S(1)}, u32[]{:S(2)}, u32[]{:S(2)}) %collective-permute-start.18) | collective-permute-done | bytes 655392 | tf_op jit(solution)/shard_map/ppermute | solution.py:701
  86.0 1.3 %assemble.3 = (bf16[128,1280]{1,0:T(8,128)(2,1)S(1)}, bf16[128,1280]{1,0:T(8,128)(2,1)S(1)}, f32[8,128]{1,0:T(8,128)S(1)}) custom-call(s32[3]{0:T(128)S(1)} %copy-done.10, f32[8,128]{1,0:T(8,128)S(1)} %get-tuple-element.178.refs_12_.refs_1_, f32[1288,128]{1,0:T(8,128)S(1)} %collective-permute-done.2.refs_1_.refs_2_, ...), custom_call_target="tpu_custom_call" | custom-call | flops 1 | bytes 1 | tf_op jit(solution)/shard_map/assemble/pallas_call | solution.py:542
  87.4 0.2 collective-permute-start.19
  87.6 1.7 %finish.4 = (bf16[256,2560]{1,0:T(8,128)(2,1)}, f32[256,128]{1,0:T(8,128)S(1)}, f32[256,128]{1,0:T(8,128)S(1)}, f32[256,128]{1,0:T(8,128)S(1)}, f32[8,128]{1,0:T(8,128)S(1)}) custom-call(bf16[256,2560]{1,0:T(8,128)(2,1)S(1)} %copy-done, bf16[256,2560]{1,0:T(8,128)(2,1)S(1)} %copy-done.1, ...), custom_call_target="tpu_custom_call", output_to_operand_aliasing={{0}: (12, {})} | custom-call | flops 1 | bytes 1 | tf_op jit(solution)/shard_map/finish/pallas_call | solution.py:610
  89.3 0.5 core_sum.1
  89.9 3.1 %collective-permute-start.22 = (f32[8,128]{1,0:T(8,128)S(1)}, f32[8,128]{1,0:T(8,128)S(1)}, u32[]{:S(2)}, u32[]{:S(2)}) collective-permute-start(f32[8,128]{1,0:T(8,128)S(1)} %get-tuple-element.197.refs_13_.total_ref), channel_id=1, source_target_pairs={{0,6},{1,7},{2,4},{3,5},{4,2},{5,3},{6,0},{7,1},{8,14},{9,15},{10,... | collective-permute-start | bytes 12296 | tf_op jit(solution)/shard_map/ppermute | solution.py:701
  93.0 1.4 %collective-permute-start.20 = (f32[8,128]{1,0:T(8,128)S(1)}, f32[8,128]{1,0:T(8,128)S(1)}, u32[]{:S(2)}, u32[]{:S(2)}) collective-permute-start(f32[8,128]{1,0:T(8,128)S(1)} %get-tuple-element.197.refs_13_.total_ref), channel_id=1, source_target_pairs={{0,2},{1,3},{2,0},{3,1},{4,6},{5,7},{6,4},{7,5},{8,10},{9,11},{10,... | collective-permute-start | bytes 12296 | tf_op jit(solution)/shard_map/ppermute | solution.py:701
  94.3 1.8 %finish.5 = (bf16[256,2560]{1,0:T(8,128)(2,1)}, bf16[256,128]{1,0:T(8,128)(2,1)}, bf16[256,128]{1,0:T(8,128)(2,1)}, f32[40,256]{1,0:T(8,128)S(1)}, f32[8,128]{1,0:T(8,128)S(1)}) custom-call(bf16[256,2560]{1,0:T(8,128)(2,1)S(1)} %copy-done, bf16[256,2560]{1,0:T(8,128)(2,1)S(1)} %copy-done.1, ...), custom_call_target="tpu_custom_call", output_to_operand_aliasing={{0}: (12, {})} | custom-call | flops 1 | bytes 1 | tf_op jit(solution)/shard_map/finish/pallas_call | solution.py:610
  96.1 1.3 %collective-permute-done.21.refs_1_ = f32[8,128]{1,0:T(8,128)S(1)} collective-permute-done((f32[8,128]{1,0:T(8,128)S(1)}, f32[8,128]{1,0:T(8,128)S(1)}, u32[]{:S(2)}, u32[]{:S(2)}) %collective-permute-start.21) | collective-permute-done | bytes 4128 | tf_op jit(solution)/shard_map/ppermute | solution.py:701
  97.5 0.6 chip_sum.1
  98.0 1.3 %collective-permute-start.25 = (f32[8,128]{1,0:T(8,128)S(1)}, f32[8,128]{1,0:T(8,128)S(1)}, u32[]{:S(2)}, u32[]{:S(2)}) collective-permute-start(f32[8,128]{1,0:T(8,128)S(1)} %get-tuple-element.205), channel_id=1, source_target_pairs={{24,0},{25,1},{26,2},{27,3},{28,4},{29,5},{30,6},{31,7}} | collective-permute-start | bytes 12296 | tf_op jit(solution)/shard_map/ppermute | solution.py:701
  99.3 1.3 %collective-permute-start.24 = (f32[8,128]{1,0:T(8,128)S(1)}, f32[8,128]{1,0:T(8,128)S(1)}, u32[]{:S(2)}, u32[]{:S(2)}) collective-permute-start(f32[8,128]{1,0:T(8,128)S(1)} %get-tuple-element.205), channel_id=1, source_target_pairs={{16,0},{17,1},{18,2},{19,3},{20,4},{21,5},{22,6},{23,7},{24,8},{25... | collective-permute-start | bytes 12296 | tf_op jit(solution)/shard_map/ppermute | solution.py:701
  100.6 1.3 %collective-permute-start.23 = (f32[8,128]{1,0:T(8,128)S(1)}, f32[8,128]{1,0:T(8,128)S(1)}, u32[]{:S(2)}, u32[]{:S(2)}) collective-permute-start(f32[8,128]{1,0:T(8,128)S(1)} %get-tuple-element.205), channel_id=1, source_target_pairs={{8,0},{9,1},{10,2},{11,3},{12,4},{13,5},{14,6},{15,7},{16,8},{17,9... | collective-permute-start | bytes 12296 | tf_op jit(solution)/shard_map/ppermute | solution.py:701
  101.9 2.5 %collective-permute-done.25.refs_3_ = f32[8,128]{1,0:T(8,128)S(1)} collective-permute-done((f32[8,128]{1,0:T(8,128)S(1)}, f32[8,128]{1,0:T(8,128)S(1)}, u32[]{:S(2)}, u32[]{:S(2)}) %collective-permute-start.25) | collective-permute-done | bytes 4128 | tf_op jit(solution)/shard_map/ppermute | solution.py:701
  104.4 0.4 collective-permute-done.24.refs_2_
  104.8 1.3 %collective-permute-done.23.refs_1_ = f32[8,128]{1,0:T(8,128)S(1)} collective-permute-done((f32[8,128]{1,0:T(8,128)S(1)}, f32[8,128]{1,0:T(8,128)S(1)}, u32[]{:S(2)}, u32[]{:S(2)}) %collective-permute-start.23) | collective-permute-done | bytes 4128 | tf_op jit(solution)/shard_map/ppermute | solution.py:701
  106.1 0.8 add_later.1
  (42 shorter events, 0.5 us)
Async XLA Ops:
  5.0 4.4 %collective-permute-start = (f32[1288,128]{1,0:T(8,128)}, f32[1288,128]{1,0:T(8,128)S(1)}, u32[]{:S(2)}, u32[]{:S(2)}) collective-permute-start(f32[1288,128]{1,0:T(8,128)} %get-tuple-element.107), channel_id=1, source_target_pairs={{0,1},{1,0},{2,3},{3,2},{4,5},{5,4},{6,7},{7,6},{8,9},{9,8},{10,11... | collective-permute-start | bytes 1978376 | tf_op jit(solution)/shard_map/ppermute | solution.py:701
  5.5 3.9 %copy-start.8 = (f32[1280,128]{1,0:T(8,128)S(1)}, f32[1280,128]{1,0:T(8,128)}, u32[]{:S(2)}) copy-start(f32[1280,128]{1,0:T(8,128)} %get-tuple-element.108.refs_2_) | copy-start | bytes 1966084
  5.5 3.9 %copy-start.10 = (s32[3]{0:T(128)S(1)}, s32[3]{0:T(128)}, u32[]{:S(2)}) copy-start(s32[3]{0:T(128)} %pad_add_fusion.refs_0_.place) | copy-start | bytes 40
  5.5 3.9 %copy-start.11 = (f32[8,128]{1,0:T(8,128)S(1)}, f32[8,128]{1,0:T(8,128)}, u32[]{:S(2)}) copy-start(f32[8,128]{1,0:T(8,128)} %get-tuple-element.110.refs_4_.refs_5_.after_ref) | copy-start | bytes 12292
  5.5 3.9 %copy-start.13 = (f32[10,128]{1,0:T(8,128)S(1)}, f32[10,128]{1,0:T(8,128)}, u32[]{:S(2)}) copy-start(f32[10,128]{1,0:T(8,128)} %get-tuple-element.109.refs_3_) | copy-start | bytes 15364
  5.5 7.6 %copy-start.1 = (bf16[256,2560]{1,0:T(8,128)(2,1)S(1)}, bf16[256,2560]{1,0:T(8,128)(2,1)}, u32[]{:S(2)}) copy-start(bf16[256,2560]{1,0:T(8,128)(2,1)} %refs_1_.15) | copy-start | bytes 3932164
  5.5 7.6 %copy-start.2 = (bf16[256,128]{1,0:T(8,128)(2,1)S(1)}, bf16[256,128]{1,0:T(8,128)(2,1)}, u32[]{:S(2)}) copy-start(bf16[256,128]{1,0:T(8,128)(2,1)} %refs_2_.15) | copy-start | bytes 196612
  5.5 7.6 %copy-start.3 = (bf16[256,128]{1,0:T(8,128)(2,1)S(1)}, bf16[256,128]{1,0:T(8,128)(2,1)}, u32[]{:S(2)}) copy-start(bf16[256,128]{1,0:T(8,128)(2,1)} %refs_3_.15) | copy-start | bytes 196612
  5.5 7.6 %copy-start.4 = (bf16[256,128]{1,0:T(8,128)(2,1)S(1)}, bf16[256,128]{1,0:T(8,128)(2,1)}, u32[]{:S(2)}) copy-start(bf16[256,128]{1,0:T(8,128)(2,1)} %get-tuple-element.105.refs_6_.refs_7_.refs_4_) | copy-start | bytes 196612
  5.5 7.6 %copy-start.5 = (bf16[256,128]{1,0:T(8,128)(2,1)S(1)}, bf16[256,128]{1,0:T(8,128)(2,1)}, u32[]{:S(2)}) copy-start(bf16[256,128]{1,0:T(8,128)(2,1)} %get-tuple-element.106.refs_7_.refs_8_.refs_5_) | copy-start | bytes 196612
  5.5 7.6 %copy-start.6 = (f32[256,128]{1,0:T(8,128)S(1)}, f32[256,128]{1,0:T(8,128)}, u32[]{:S(2)}) copy-start(f32[256,128]{1,0:T(8,128)} %get-tuple-element.114.refs_6_) | copy-start | bytes 393220
  5.6 7.6 %copy-start.9 = (f32[40,256]{1,0:T(8,128)S(1)}, f32[40,256]{1,0:T(8,128)}, u32[]{:S(2)}) copy-start(f32[40,256]{1,0:T(8,128)} %refs_5_.7) | copy-start | bytes 122884
  9.2 4.0 %copy-start = (bf16[256,2560]{1,0:T(8,128)(2,1)S(1)}, bf16[256,2560]{1,0:T(8,128)(2,1)}, u32[]{:S(2)}) copy-start(bf16[256,2560]{1,0:T(8,128)(2,1)} %refs_0_.5) | copy-start | bytes 3932164
  9.2 9.0 %collective-permute-start.2 = (f32[1288,128]{1,0:T(8,128)}, f32[1288,128]{1,0:T(8,128)S(1)}, u32[]{:S(2)}, u32[]{:S(2)}) collective-permute-start(f32[1288,128]{1,0:T(8,128)} %get-tuple-element.113), channel_id=1, source_target_pairs={{0,1},{1,0},{2,3},{3,2},{4,5},{5,4},{6,7},{7,6},{8,9},{9,8},{10,11... | collective-permute-start | bytes 1978376 | tf_op jit(solution)/shard_map/ppermute | solution.py:701
  10.0 11.2 %collective-permute-start.1 = (f32[656,128]{1,0:T(8,128)S(1)}, f32[656,128]{1,0:T(8,128)S(1)}, u32[]{:S(2)}, u32[]{:S(2)}) collective-permute-start(f32[656,128]{1,0:T(8,128)S(1)} %get-tuple-element.112.refs_0_.refs_2_), channel_id=1, source_target_pairs={{0,2},{1,3},{2,0},{3,1},{4,6},{5,7},{6,4},{7,5},{8,10},{9,11},{10,... | collective-permute-start | bytes 1007624 | tf_op jit(solution)/shard_map/ppermute | solution.py:701
  13.2 8.0 %copy-start.7 = (f32[1280,128]{1,0:T(8,128)S(1)}, f32[1280,128]{1,0:T(8,128)}, u32[]{:S(2)}) copy-start(f32[1280,128]{1,0:T(8,128)} %get-tuple-element.124.refs_2_) | copy-start | bytes 1966084
  13.2 8.0 %copy-start.12 = (f32[10,128]{1,0:T(8,128)S(1)}, f32[10,128]{1,0:T(8,128)}, u32[]{:S(2)}) copy-start(f32[10,128]{1,0:T(8,128)} %get-tuple-element.125.refs_3_) | copy-start | bytes 15364
  21.8 13.1 %collective-permute-start.4 = (f32[656,128]{1,0:T(8,128)S(1)}, f32[656,128]{1,0:T(8,128)S(1)}, u32[]{:S(2)}, u32[]{:S(2)}) collective-permute-start(f32[656,128]{1,0:T(8,128)S(1)} %get-tuple-element.126.refs_2_), channel_id=1, source_target_pairs={{0,2},{1,3},{2,0},{3,1},{4,6},{5,7},{6,4},{7,5},{8,10},{9,11},{10,... | collective-permute-start | bytes 1007624 | tf_op jit(solution)/shard_map/ppermute | solution.py:701
  24.4 9.4 %collective-permute-start.3 = (f32[336,128]{1,0:T(8,128)S(1)}, f32[336,128]{1,0:T(8,128)S(1)}, u32[]{:S(2)}, u32[]{:S(2)}) collective-permute-start(f32[336,128]{1,0:T(8,128)S(1)} %get-tuple-element.122.refs_0_.refs_2_), channel_id=1, source_target_pairs={{0,4},{1,5},{2,6},{3,7},{4,0},{5,1},{6,2},{7,3},{8,12},{9,13},{10,... | collective-permute-start | bytes 516104 | tf_op jit(solution)/shard_map/ppermute | solution.py:701
  35.6 13.1 %collective-permute-start.8 = (f32[336,128]{1,0:T(8,128)S(1)}, f32[336,128]{1,0:T(8,128)S(1)}, u32[]{:S(2)}, u32[]{:S(2)}) collective-permute-start(f32[336,128]{1,0:T(8,128)S(1)} %get-tuple-element.140.refs_2_), channel_id=1, source_target_pairs={{0,4},{1,5},{2,6},{3,7},{4,0},{5,1},{6,2},{7,3},{8,12},{9,13},{10,... | collective-permute-start | bytes 516104 | tf_op jit(solution)/shard_map/ppermute | solution.py:701
  38.8 8.3 %collective-permute-start.7 = (f32[328,128]{1,0:T(8,128)S(1)}, f32[328,128]{1,0:T(8,128)S(1)}, u32[]{:S(2)}, u32[]{:S(2)}) collective-permute-start(f32[328,128]{1,0:T(8,128)S(1)} %up.5.refs_0_), channel_id=1, source_target_pairs={{1,25},{3,27},{5,29},{7,31},{24,0},{26,2},{28,4},{30,6}} | collective-permute-start | bytes 503816 | tf_op jit(solution)/shard_map/ppermute | solution.py:701
  40.1 8.7 %collective-permute-start.6 = (f32[328,128]{1,0:T(8,128)S(1)}, f32[328,128]{1,0:T(8,128)S(1)}, u32[]{:S(2)}, u32[]{:S(2)}) collective-permute-start(f32[328,128]{1,0:T(8,128)S(1)} %up.5.refs_0_), channel_id=1, source_target_pairs={{1,17},{3,19},{5,21},{7,23},{9,25},{11,27},{13,29},{15,31},{16,0},... | collective-permute-start | bytes 503816 | tf_op jit(solution)/shard_map/ppermute | solution.py:701
  41.4 7.4 %collective-permute-start.5 = (f32[328,128]{1,0:T(8,128)S(1)}, f32[328,128]{1,0:T(8,128)S(1)}, u32[]{:S(2)}, u32[]{:S(2)}) collective-permute-start(f32[328,128]{1,0:T(8,128)S(1)} %up.5.refs_0_), channel_id=1, source_target_pairs={{1,9},{3,11},{5,13},{7,15},{8,0},{9,17},{10,2},{11,19},{12,4},{13,... | collective-permute-start | bytes 503816 | tf_op jit(solution)/shard_map/ppermute | solution.py:701
  49.6 11.5 %collective-permute-start.9 = (f32[336,128]{1,0:T(8,128)S(1)}, f32[336,128]{1,0:T(8,128)S(1)}, u32[]{:S(2)}, u32[]{:S(2)}) collective-permute-start(f32[336,128]{1,0:T(8,128)S(1)} %get-tuple-element.163), channel_id=1, source_target_pairs={{0,4},{1,5},{2,6},{3,7},{4,0},{5,1},{6,2},{7,3},{8,12},{9,13},{10,... | collective-permute-start | bytes 516104 | tf_op jit(solution)/shard_map/ppermute | solution.py:701
  51.1 8.3 %collective-permute-start.12 = (f32[328,128]{1,0:T(8,128)S(1)}, f32[328,128]{1,0:T(8,128)S(1)}, u32[]{:S(2)}, u32[]{:S(2)}) collective-permute-start(f32[328,128]{1,0:T(8,128)S(1)} %up.7), channel_id=1, source_target_pairs={{1,25},{3,27},{5,29},{7,31},{24,0},{26,2},{28,4},{30,6}} | collective-permute-start | bytes 503816 | tf_op jit(solution)/shard_map/ppermute | solution.py:701
  52.4 8.7 %collective-permute-start.11 = (f32[328,128]{1,0:T(8,128)S(1)}, f32[328,128]{1,0:T(8,128)S(1)}, u32[]{:S(2)}, u32[]{:S(2)}) collective-permute-start(f32[328,128]{1,0:T(8,128)S(1)} %up.7), channel_id=1, source_target_pairs={{1,17},{3,19},{5,21},{7,23},{9,25},{11,27},{13,29},{15,31},{16,0},... | collective-permute-start | bytes 503816 | tf_op jit(solution)/shard_map/ppermute | solution.py:701
  53.7 7.4 %collective-permute-start.10 = (f32[328,128]{1,0:T(8,128)S(1)}, f32[328,128]{1,0:T(8,128)S(1)}, u32[]{:S(2)}, u32[]{:S(2)}) collective-permute-start(f32[328,128]{1,0:T(8,128)S(1)} %up.7), channel_id=1, source_target_pairs={{1,9},{3,11},{5,13},{7,15},{8,0},{9,17},{10,2},{11,19},{12,4},{13,... | collective-permute-start | bytes 503816 | tf_op jit(solution)/shard_map/ppermute | solution.py:701
  61.9 11.1 %collective-permute-start.13 = (f32[656,128]{1,0:T(8,128)S(1)}, f32[656,128]{1,0:T(8,128)S(1)}, u32[]{:S(2)}, u32[]{:S(2)}) collective-permute-start(f32[656,128]{1,0:T(8,128)S(1)} %get-tuple-element.168), channel_id=1, source_target_pairs={{0,2},{1,3},{2,0},{3,1},{4,6},{5,7},{6,4},{7,5},{8,10},{9,11},{10,... | collective-permute-start | bytes 1007624 | tf_op jit(solution)/shard_map/ppermute | solution.py:701
  65.0 7.7 %collective-permute-start.14 = (f32[336,128]{1,0:T(8,128)S(1)}, f32[336,128]{1,0:T(8,128)S(1)}, u32[]{:S(2)}, u32[]{:S(2)}) collective-permute-start(f32[336,128]{1,0:T(8,128)S(1)} %get-tuple-element.172), channel_id=1, source_target_pairs={{0,4},{1,5},{2,6},{3,7},{4,0},{5,1},{6,2},{7,3},{8,12},{9,13},{10,... | collective-permute-start | bytes 516104 | tf_op jit(solution)/shard_map/ppermute | solution.py:701
  73.7 9.6 %collective-permute-start.17 = (f32[656,128]{1,0:T(8,128)S(1)}, f32[656,128]{1,0:T(8,128)S(1)}, u32[]{:S(2)}, u32[]{:S(2)}) collective-permute-start(f32[656,128]{1,0:T(8,128)S(1)} %get-tuple-element.187), channel_id=1, source_target_pairs={{0,2},{1,3},{2,0},{3,1},{4,6},{5,7},{6,4},{7,5},{8,10},{9,11},{10,... | collective-permute-start | bytes 1007624 | tf_op jit(solution)/shard_map/ppermute | solution.py:701
  76.0 1.7 %collective-permute-start.15 = (f32[640,128]{1,0:T(8,128)S(1)}, f32[640,128]{1,0:T(8,128)S(1)}, u32[]{:S(2)}, u32[]{:S(2)}) collective-permute-start(f32[640,128]{1,0:T(8,128)S(1)} %get-tuple-element.174.refs_5_), channel_id=1, source_target_pairs={{0,1},{1,0},{2,3},{3,2},{4,5},{5,4},{6,7},{7,6},{8,9},{9,8},{10,11... | collective-permute-start | bytes 983048 | tf_op jit(solution)/shard_map/ppermute | solution.py:701
  76.1 2.1 %collective-permute-start.16 = (f32[640,128]{1,0:T(8,128)S(1)}, f32[640,128]{1,0:T(8,128)S(1)}, u32[]{:S(2)}, u32[]{:S(2)}) collective-permute-start(f32[640,128]{1,0:T(8,128)S(1)} %get-tuple-element.175.refs_6_), channel_id=1, source_target_pairs={{0,1},{1,0},{2,3},{3,2},{4,5},{5,4},{6,7},{7,6},{8,9},{9,8},{10,11... | collective-permute-start | bytes 983048 | tf_op jit(solution)/shard_map/ppermute | solution.py:701
  83.9 2.2 %collective-permute-start.18 = (f32[1280,128]{1,0:T(8,128)S(1)}, f32[1280,128]{1,0:T(8,128)S(1)}, u32[]{:S(2)}, u32[]{:S(2)}) collective-permute-start(f32[1280,128]{1,0:T(8,128)S(1)} %order.3.refs_5_), channel_id=1, source_target_pairs={{0,1},{1,0},{2,3},{3,2},{4,5},{5,4},{6,7},{7,6},{8,9},{9,8},{10,11... | collective-permute-start | bytes 1966088 | tf_op jit(solution)/shard_map/ppermute | solution.py:701
  87.4 1.9 %collective-permute-start.19 = (f32[8,128]{1,0:T(8,128)S(1)}, f32[8,128]{1,0:T(8,128)S(1)}, u32[]{:S(2)}, u32[]{:S(2)}) collective-permute-start(f32[8,128]{1,0:T(8,128)S(1)} %get-tuple-element.191.refs_13_.total_ref), channel_id=1, source_target_pairs={{0,1},{1,0},{2,3},{3,2},{4,5},{5,4},{6,7},{7,6},{8,9},{9,8},{10,11... | collective-permute-start | bytes 12296 | tf_op jit(solution)/shard_map/ppermute | solution.py:701
  89.9 6.3 %collective-permute-start.22 = (f32[8,128]{1,0:T(8,128)S(1)}, f32[8,128]{1,0:T(8,128)S(1)}, u32[]{:S(2)}, u32[]{:S(2)}) collective-permute-start(f32[8,128]{1,0:T(8,128)S(1)} %get-tuple-element.197.refs_13_.total_ref), channel_id=1, source_target_pairs={{0,6},{1,7},{2,4},{3,5},{4,2},{5,3},{6,0},{7,1},{8,14},{9,15},{10,... | collective-permute-start | bytes 12296 | tf_op jit(solution)/shard_map/ppermute | solution.py:701
  93.0 4.5 %collective-permute-start.21 = (f32[8,128]{1,0:T(8,128)S(1)}, f32[8,128]{1,0:T(8,128)S(1)}, u32[]{:S(2)}, u32[]{:S(2)}) collective-permute-start(f32[8,128]{1,0:T(8,128)S(1)} %get-tuple-element.197.refs_13_.total_ref), channel_id=1, source_target_pairs={{0,4},{1,5},{2,6},{3,7},{4,0},{5,1},{6,2},{7,3},{8,12},{9,13},{10,... | collective-permute-start | bytes 12296 | tf_op jit(solution)/shard_map/ppermute | solution.py:701
  93.0 4.5 %collective-permute-start.20 = (f32[8,128]{1,0:T(8,128)S(1)}, f32[8,128]{1,0:T(8,128)S(1)}, u32[]{:S(2)}, u32[]{:S(2)}) collective-permute-start(f32[8,128]{1,0:T(8,128)S(1)} %get-tuple-element.197.refs_13_.total_ref), channel_id=1, source_target_pairs={{0,2},{1,3},{2,0},{3,1},{4,6},{5,7},{6,4},{7,5},{8,10},{9,11},{10,... | collective-permute-start | bytes 12296 | tf_op jit(solution)/shard_map/ppermute | solution.py:701
  98.0 6.4 %collective-permute-start.25 = (f32[8,128]{1,0:T(8,128)S(1)}, f32[8,128]{1,0:T(8,128)S(1)}, u32[]{:S(2)}, u32[]{:S(2)}) collective-permute-start(f32[8,128]{1,0:T(8,128)S(1)} %get-tuple-element.205), channel_id=1, source_target_pairs={{24,0},{25,1},{26,2},{27,3},{28,4},{29,5},{30,6},{31,7}} | collective-permute-start | bytes 12296 | tf_op jit(solution)/shard_map/ppermute | solution.py:701
  99.3 5.5 %collective-permute-start.24 = (f32[8,128]{1,0:T(8,128)S(1)}, f32[8,128]{1,0:T(8,128)S(1)}, u32[]{:S(2)}, u32[]{:S(2)}) collective-permute-start(f32[8,128]{1,0:T(8,128)S(1)} %get-tuple-element.205), channel_id=1, source_target_pairs={{16,0},{17,1},{18,2},{19,3},{20,4},{21,5},{22,6},{23,7},{24,8},{25... | collective-permute-start | bytes 12296 | tf_op jit(solution)/shard_map/ppermute | solution.py:701
  100.6 5.5 %collective-permute-start.23 = (f32[8,128]{1,0:T(8,128)S(1)}, f32[8,128]{1,0:T(8,128)S(1)}, u32[]{:S(2)}, u32[]{:S(2)}) collective-permute-start(f32[8,128]{1,0:T(8,128)S(1)} %get-tuple-element.205), channel_id=1, source_target_pairs={{8,0},{9,1},{10,2},{11,3},{12,4},{13,5},{14,6},{15,7},{16,8},{17,9... | collective-permute-start | bytes 12296 | tf_op jit(solution)/shard_map/ppermute | solution.py:701

commit v12 on v11

--- a/solution.py
+++ b/solution.py
@@ -472,38 +472,31 @@
     )(after, x, g, write_map, read_map, rates, *shared[1:], *earlier)
 
 
-def order_kernel(place, after_ref, here_ref, got_ref, *outs):
-    size = here_ref.shape[0]
+def order_kernel(place, here_ref, got_ref, low_ref, high_ref):
     bit = place[1] & 1
-    if len(outs) == 1:
-        outs[0][pl.ds(pl.multiple_of(bit * size, size), size), :] = here_ref[...]
-        outs[0][pl.ds(pl.multiple_of((1 - bit) * size, size), size), :] = got_ref[:size, :]
-    else:
-        here, got = here_ref[...], got_ref[:size, :]
-        outs[0][...] = jnp.where(bit == 0, here, got)
-        outs[1][...] = jnp.where(bit == 0, got, here)
-
-
-def order(pieces, place, after, here, got):
-    shape = (2 * here.shape[0] // pieces, STRIP)
+    here, got = here_ref[...], got_ref[: here_ref.shape[0], :]
+    low_ref[...] = jnp.where(bit == 0, here, got)
+    high_ref[...] = jnp.where(bit == 0, got, here)
+
+
+def order(place, here, got):
     return pl.pallas_call(
         order_kernel,
-        grid=(1,),
-        in_specs=[SCALARS, whole(META, STRIP), whole(*here.shape), whole(*got.shape)],
-        out_specs=[whole(*shape)] * pieces,
-        out_shape=[jax.ShapeDtypeStruct(shape, F32)] * pieces,
+        in_specs=[SCALARS, whole(*here.shape), whole(*got.shape)],
+        out_specs=[whole(*here.shape)] * 2,
+        out_shape=[jax.ShapeDtypeStruct(here.shape, F32)] * 2,
         compiler_params=pltpu.CompilerParams(vmem_limit_bytes=SMALL_VMEM),
         cost_estimate=LITTLE,
         name="order",
-    )(place, after, here, got)
+    )(place, here, got)
 
 
 def assemble_kernel(
-    heads, chips, half, head_size, place, after_ref, first_ref, state_own, back_own, *refs,
+    heads, chips, half, head_size, ordered,
+    place, after_ref, first_ref, state_own, back_own, *refs,
 ):
-    state_ref, back_ref, total_ref = refs[-3:]
-    pieces = (len(refs) - 3) // 2
-    own_refs, far_refs = refs[:pieces], refs[pieces : 2 * pieces]
+    own_refs, far_refs, (state_ref, back_ref, total_ref) = refs[:2], refs[2:4], refs[4:]
+    bit = 0 if ordered else place[1] & 1
     lanes = state_ref.shape[1]
     strips = lanes // STRIP
     part = STATE // chips
@@ -517,10 +510,13 @@
         for strip in range(strips):
             wide = slice(strip * STRIP, (strip + 1) * STRIP)
             here = slice(quarter * size + strip * part, quarter * size + (strip + 1) * part)
-            piece, at = divmod(here.start, own_refs[0].shape[0])
+            piece, at = divmod(here.start, chips // 2 * size)
             there = slice(at, at + part)
-            own = own_refs[piece][there, :] * decay[strip : strip + 1, :] + first_ref[here, :]
-            far = far_refs[piece][there, :]
+            own, far = own_refs[piece][there, :], far_refs[piece][there, :]
+            if not ordered:
+                own = jnp.where(bit == 0, own, own_refs[1 - piece][there, :])
+                far = jnp.where(bit == 0, far, far_refs[1 - piece][there, :])
+            own = own * decay[strip : strip + 1, :] + first_ref[here, :]
             state = jnp.where(is_first, far, own).astype(BF16)
             back = jnp.where(is_first, own, far).astype(BF16)
             state_ref[rows, wide] = state
@@ -535,12 +531,12 @@
     total_ref[...] = total + after_ref[...] if half else total
 
 
-def assemble(heads, chips, half, place, after, first, state_own, back_own, own, far):
+def assemble(heads, chips, half, ordered, place, after, first, state_own, back_own, own, far):
     wide = state_own.shape[1]
     lanes = wide // HALVES
     mine = pl.BlockSpec((STATE, lanes), lambda c: (0, half))
     return pl.pallas_call(
-        lambda *refs: assemble_kernel(heads, chips, half, wide // heads, *refs),
+        lambda *refs: assemble_kernel(heads, chips, half, wide // heads, ordered, *refs),
         grid=(1,),
         in_specs=[SCALARS, whole(META, STRIP), whole(*first.shape), mine, mine]
         + [whole(*value.shape) for value in (*own, *far)],
@@ -589,7 +585,7 @@
 
     @pl.when(chunk == steps - 1)
     def _():
-        token_ref[...] = jnp.zeros_like(token_ref)
+        token_ref[...] = refs[-9][...]
         db_out[...] = db_sum[...].astype(db_out.dtype)
         dc_out[...] = dc_sum[...].astype(dc_out.dtype)
         if last:
@@ -633,9 +629,9 @@
     )(x, g, write_map, read_map, *shared[2:], dx, *sums, state, back, *earlier, after)
 
 
-def count_kernel(place, later_ref, total_ref, after_ref, *refs):
+def count_kernel(place, after_ref, later_ref, total_ref, *refs):
     got_refs, (later_out, total_out) = refs[:-2], refs[-2:]
-    later, total = later_ref[...], total_ref[...] + after_ref[...]
+    later, total = later_ref[...], total_ref[...]
     for step, ref in enumerate(got_refs, 1):
         later = later + jnp.where((place[1] ^ step) > place[1], ref[...], 0.0)
         total = total + ref[...]
@@ -643,9 +639,9 @@
     total_out[...] = total
 
 
-def core_kernel(place, total_ref, after_ref, got_ref, later_out, total_out):
+def core_kernel(place, total_ref, got_ref, later_out, total_out):
     later_out[...] = jnp.where(place[0] == 0, got_ref[...], 0.0)
-    total_out[...] = total_ref[...] + got_ref[...] + after_ref[...]
+    total_out[...] = total_ref[...] + got_ref[...]
 
 
 def tiles(kernel, name, place, *values):
@@ -729,7 +725,7 @@
     held = [[], []]
     waiting = [None, None]
 
-    def advance(half, step, after=None):
+    def advance(half, step):
         fixed = (chips, half, strips, head_size, place)
         if step == 0:
             mine, send = combine(
@@ -752,24 +748,18 @@
             waiting[half] = to_chip(send, 1 << level)
             return send
         else:
-            held[half] = order(2 - half, place, after, held[half][0], waiting[half])
+            held[half] = order(place, held[half][0], waiting[half])
             waiting[half] = [to_core(value) for value in held[half]]
             return held[half][0]
         held[half].append((mine, send))
         waiting[half] = to_chip(send, 1 << step)
         return send
 
-    def entering(half, token):
-        return assemble(
-            heads, chips, half, place, token, first[half], state_own, back_own,
-            held[half], waiting[half],
-        )
-
     chunks = inputs.shape[1] // LANES
     rounds = 2 * levels + 2
     block, ready = (), 0
     for step in range(rounds):
-        token = advance(0, step, shared[0])
+        token = advance(0, step)
         if step:
             advance(1, step - 1)
         if step < 3:
@@ -782,24 +772,30 @@
         elif step < rounds - 1:
             waiting[0], waiting[1] = lax.optimization_barrier((waiting[0], waiting[1]))
     dx, state_own, back_own, change, db, dc = block
-    state, back, counted = entering(0, change)
-    grad, *sums, token = finish(
+    own_b = held[1][0]
+    far_b = to_core(own_b)
+    state, back, counted = assemble(
+        heads, chips, 0, True, place, change, first[0], state_own, back_own, held[0], waiting[0]
+    )
+    grad, *sums, counted = finish(
         heads, 0, STEPS, counted, *maps, shared, dx, (db, dc, change), state, back, None
     )
-    advance(1, rounds - 1, token)
-    state, back, counted = entering(1, counted)
-
-    got = to_core(counted)
+    got, far_b, counted = lax.optimization_barrier((waiting[1], far_b, counted))
+    own_b, far_b = (own_b, got), (far_b, to_core(got))
+    state, back, counted = assemble(
+        heads, chips, 1, False, place, counted, first[1], state_own, back_own, own_b, far_b
+    )
+
+    later, counted = tiles(core_kernel, "core_sum", place, counted, to_core(counted))
+    got = [to_chip(counted, step) for step in range(1, chips)]
     grad, *sums, token = finish(
         heads, STEPS, 1, counted, *maps, shared, dx, sums, state, back, grad
     )
-    later, counted = tiles(core_kernel, "core_sum", place, counted, token, got)
-    got = [to_chip(counted, step) for step in range(1, chips)]
-    grad, *sums, token = finish(
+    later, counted = tiles(count_kernel, "chip_sum", place, token, later, counted, *got)
+    got = [to_earlier(counted, step) for step in range(1, groups)]
+    grad, *sums, _ = finish(
         heads, STEPS + 1, 1, counted, *maps, shared, dx, sums, state, back, grad
     )
-    later, counted = tiles(count_kernel, "chip_sum", place, later, counted, token, *got)
-    got = [to_earlier(counted, step) for step in range(1, groups)]
     return (grad, sums[0], sums[1], add_later(sums[2], later, *got))
 
 

time: 107 us -> 105 us (0.981)
  waiting for transfers between devices: 30.3 us -> 29.1 us
    ppermute x26 -> x27, waiting for transfers between devices: 30.3 us -> 29.1 us  [move(): return lax.ppermute(value, ('grp', 'seq'), pairs)]
    ppermute x26 -> x27, starting transfers between devices: 34.7 us -> 34.7 us  [move(): return lax.ppermute(value, ('grp', 'seq'), pairs)]
  transfers between devices with their start and end apart: 26 -> 27, of which waited for: 16 -> 17; matrix products, arithmetic and copies ran while one was open for 0% -> 0% of each run, Pallas kernels for 27% -> 28%
where the time goes in v12:
time: 105 us
  Pallas kernels  39.7 us (38%)
  starting transfers between devices  34.7 us (33%)
  waiting for transfers between devices  29.1 us (28%)
    ppermute x27, starting transfers between devices, move(): return lax.ppermute(value, ('grp', 'seq'), pairs)  34.7 us
    ppermute x27, waiting for transfers between devices, move(): return lax.ppermute(value, ('grp', 'seq'), pairs)  29.1 us
    pallas_call x3, Pallas kernels, intra(): pl.pallas_call(lambda *refs: intra_kernel(heads, wide // heads, start, la...  12.5 us
    pallas_call x2, Pallas kernels, summary(): pl.pallas_call(lambda *refs: summary_kernel(heads, chips, half, *refs), g...  7.41 us
    pallas_call x3, Pallas kernels, finish(): pl.pallas_call(lambda *refs: finish_kernel(heads, start, steps, last, *re...  7.27 us
    pallas_call x4, Pallas kernels, down(): pl.pallas_call(lambda *refs: down_kernel(level, top, STATE // chips, half...  3.15 us
    pallas_call x4, Pallas kernels, up(): pl.pallas_call(lambda *refs: up_kernel(level, last, STATE // chips, half...  2.96 us
    pallas_call x2, Pallas kernels, assemble(): pl.pallas_call(lambda *refs: assemble_kernel(heads, chips, half, wide //...  2.65 us
  transfers between devices with their start and end apart: 27, of which 17 were waited for; matrix products, arithmetic and copies ran while one was open for 0% of the time, Pallas kernels for 28%

profile of v12, /device:TPU:0, one launch (start us, length us, event | category | flops | bytes accessed | tf_op | source)
XLA Modules:
  0.0 105.1 jit_solution(694327580777280068)
XLA Ops:
  0.6 0.6 pad_add_fusion.refs_0_.place
  1.2 3.8 %summary.2 = (f32[1288,128]{1,0:T(8,128)}, f32[1280,128]{1,0:T(8,128)}, f32[10,128]{1,0:T(8,128)}, f32[8,128]{1,0:T(8,128)}, f32[256,128]{1,0:T(8,128)}, /*index...) custom-call(s32[3]{0:T(128)} %pad_add_fusion.refs_0_.place, bf16[256,2560]{1,0:T(8,128)(2,1)} %refs_0_.5, ...), custom_call_target="tpu_custom_call" | custom-call | flops 1 | bytes 1 | tf_op jit(solution)/shard_map/summary/pallas_call | solution.py:188
  5.0 0.5 collective-permute-start
  5.6 3.7 %summary.3 = (f32[1288,128]{1,0:T(8,128)}, f32[1280,128]{1,0:T(8,128)}, f32[10,128]{1,0:T(8,128)}) custom-call(s32[3]{0:T(128)} %pad_add_fusion.refs_0_.place, bf16[256,2560]{1,0:T(8,128)(2,1)} %refs_0_.5, bf16[256,2560]{1,0:T(8,128)(2,1)} %refs_1_.15, bf16[256,128]{1,0:T(8,128)(2,1)} %refs_2_.15, bf16[256,128]{1,0:T(8,128)(2,1)} %refs_3_.15, ...), custom_call_target="tpu_custom_call" | custom-call | flops 1 | bytes 1 | tf_op jit(solution)/shard_map/summary/pallas_call | solution.py:188
  9.4 0.7 combine.2
  10.1 3.1 %collective-permute-start.1 = (f32[656,128]{1,0:T(8,128)S(1)}, f32[656,128]{1,0:T(8,128)S(1)}, u32[]{:S(2)}, u32[]{:S(2)}) collective-permute-start(f32[656,128]{1,0:T(8,128)S(1)} %get-tuple-element.114.refs_0_.refs_2_), channel_id=1, source_target_pairs={{0,2},{1,3},{2,0},{3,1},{4,6},{5,7},{6,4},{7,5},{8,10},{9,11},{10,... | collective-permute-start | bytes 1007624 | tf_op jit(solution)/shard_map/ppermute | solution.py:697
  13.2 5.0 %intra.3 = (f32[256,2560]{1,0:T(8,128)S(1)}, f32[128,2560]{1,0:T(8,128)S(1)}, f32[128,2560]{1,0:T(8,128)S(1)}, f32[256,128]{1,0:T(8,128)S(1)}, f32[256,256]{1,0:T(8,128)S(1)}) custom-call(f32[656,128]{1,0:T(8,128)S(1)} %get-tuple-element.114.refs_0_.refs_2_, bf16[256,2560]{1,0:T(8,128)(2,1)S(1)} %copy-done, bf16[256,2560]{1,0:T(8,128)(2,1)S(1)} %copy-done.1, ...), custom_call_target="tpu_custom_call" | custom-call | flops 1 | bytes 1 | tf_op jit(solution)/shard_map/intra/pallas_call | solution.py:438
  18.3 3.0 %collective-permute-done.1.refs_3_ = f32[656,128]{1,0:T(8,128)S(1)} collective-permute-done((f32[656,128]{1,0:T(8,128)S(1)}, f32[656,128]{1,0:T(8,128)S(1)}, u32[]{:S(2)}, u32[]{:S(2)}) %collective-permute-start.1) | collective-permute-done | bytes 335904 | tf_op jit(solution)/shard_map/ppermute | solution.py:697
  21.3 0.6 combine.3
  21.9 1.8 %collective-permute-start.4 = (f32[656,128]{1,0:T(8,128)S(1)}, f32[656,128]{1,0:T(8,128)S(1)}, u32[]{:S(2)}, u32[]{:S(2)}) collective-permute-start(f32[656,128]{1,0:T(8,128)S(1)} %get-tuple-element.128.refs_2_), channel_id=1, source_target_pairs={{0,2},{1,3},{2,0},{3,1},{4,6},{5,7},{6,4},{7,5},{8,10},{9,11},{10,... | collective-permute-start | bytes 1007624 | tf_op jit(solution)/shard_map/ppermute | solution.py:697
  23.7 0.8 up.4
  24.4 2.7 %collective-permute-start.3 = (f32[336,128]{1,0:T(8,128)S(1)}, f32[336,128]{1,0:T(8,128)S(1)}, u32[]{:S(2)}, u32[]{:S(2)}) collective-permute-start(f32[336,128]{1,0:T(8,128)S(1)} %get-tuple-element.124.refs_0_.refs_2_), channel_id=1, source_target_pairs={{0,4},{1,5},{2,6},{3,7},{4,0},{5,1},{6,2},{7,3},{8,12},{9,13},{10,... | collective-permute-start | bytes 516104 | tf_op jit(solution)/shard_map/ppermute | solution.py:697
  27.1 5.0 %intra.4 = (f32[256,2560]{1,0:T(8,128)S(1)}, f32[128,2560]{1,0:T(8,128)S(1)}, f32[128,2560]{1,0:T(8,128)S(1)}, f32[256,128]{1,0:T(8,128)S(1)}, f32[256,256]{1,0:T(8,128)S(1)}) custom-call(f32[336,128]{1,0:T(8,128)S(1)} %get-tuple-element.124.refs_0_.refs_2_, ...), custom_call_target="tpu_custom_call", output_to_operand_aliasing={{0}: (9, {}), {1}: (10, {}), {2}: (11, {})} | custom-call | flops 1 | bytes 1 | tf_op jit(solution)/shard_map/intra/pallas_call | solution.py:438
  32.1 1.8 %collective-permute-done.3.refs_3_ = f32[336,128]{1,0:T(8,128)S(1)} collective-permute-done((f32[336,128]{1,0:T(8,128)S(1)}, f32[336,128]{1,0:T(8,128)S(1)}, u32[]{:S(2)}, u32[]{:S(2)}) %collective-permute-start.3) | collective-permute-done | bytes 172064 | tf_op jit(solution)/shard_map/ppermute | solution.py:697
  33.9 1.1 %collective-permute-done.4.refs_3_ = f32[656,128]{1,0:T(8,128)S(1)} collective-permute-done((f32[656,128]{1,0:T(8,128)S(1)}, f32[656,128]{1,0:T(8,128)S(1)}, u32[]{:S(2)}, u32[]{:S(2)}) %collective-permute-start.4) | collective-permute-done | bytes 335904 | tf_op jit(solution)/shard_map/ppermute | solution.py:697
  34.9 0.8 up.6
  35.7 2.4 %collective-permute-start.8 = (f32[336,128]{1,0:T(8,128)S(1)}, f32[336,128]{1,0:T(8,128)S(1)}, u32[]{:S(2)}, u32[]{:S(2)}) collective-permute-start(f32[336,128]{1,0:T(8,128)S(1)} %get-tuple-element.142.refs_2_), channel_id=1, source_target_pairs={{0,4},{1,5},{2,6},{3,7},{4,0},{5,1},{6,2},{7,3},{8,12},{9,13},{10,... | collective-permute-start | bytes 516104 | tf_op jit(solution)/shard_map/ppermute | solution.py:697
  38.1 0.7 up.5.refs_0_
  38.8 1.3 %collective-permute-start.7 = (f32[328,128]{1,0:T(8,128)S(1)}, f32[328,128]{1,0:T(8,128)S(1)}, u32[]{:S(2)}, u32[]{:S(2)}) collective-permute-start(f32[328,128]{1,0:T(8,128)S(1)} %up.5.refs_0_), channel_id=1, source_target_pairs={{1,25},{3,27},{5,29},{7,31},{24,0},{26,2},{28,4},{30,6}} | collective-permute-start | bytes 503816 | tf_op jit(solution)/shard_map/ppermute | solution.py:697
  40.1 1.3 %collective-permute-start.6 = (f32[328,128]{1,0:T(8,128)S(1)}, f32[328,128]{1,0:T(8,128)S(1)}, u32[]{:S(2)}, u32[]{:S(2)}) collective-permute-start(f32[328,128]{1,0:T(8,128)S(1)} %up.5.refs_0_), channel_id=1, source_target_pairs={{1,17},{3,19},{5,21},{7,23},{9,25},{11,27},{13,29},{15,31},{16,0},... | collective-permute-start | bytes 503816 | tf_op jit(solution)/shard_map/ppermute | solution.py:697
  41.4 1.3 %collective-permute-start.5 = (f32[328,128]{1,0:T(8,128)S(1)}, f32[328,128]{1,0:T(8,128)S(1)}, u32[]{:S(2)}, u32[]{:S(2)}) collective-permute-start(f32[328,128]{1,0:T(8,128)S(1)} %up.5.refs_0_), channel_id=1, source_target_pairs={{1,9},{3,11},{5,13},{7,15},{8,0},{9,17},{10,2},{11,19},{12,4},{13,... | collective-permute-start | bytes 503816 | tf_op jit(solution)/shard_map/ppermute | solution.py:697
  42.7 2.5 %intra.5 = (f32[256,2560]{1,0:T(8,128)S(1)}, f32[128,2560]{1,0:T(8,128)S(1)}, f32[128,2560]{1,0:T(8,128)S(1)}, f32[256,128]{1,0:T(8,128)S(1)}, f32[256,128]{1,0:T(8,128)S(1)}, /*index=5*/f32[256,128]{1,0:T(8,128)S(1)}) custom-call(f32[328,128]{1,0:T(8,128)S(1)} %up.5.refs_0_, ...), custom_call_target="tpu_custom_call", output_to_operand_aliasing={{0}: (9, {}), {1}: (10, {}), {2}: (11, {})} | custom-call | flops 1 | bytes 1 | tf_op jit(solution)/shard_map/intra/pallas_call | solution.py:438
  45.2 1.9 %collective-permute-done.7.refs_6_ = f32[328,128]{1,0:T(8,128)S(1)} collective-permute-done((f32[328,128]{1,0:T(8,128)S(1)}, f32[328,128]{1,0:T(8,128)S(1)}, u32[]{:S(2)}, u32[]{:S(2)}) %collective-permute-start.7) | collective-permute-done | bytes 167968 | tf_op jit(solution)/shard_map/ppermute | solution.py:697
  47.1 1.7 %collective-permute-done.6.refs_5_ = f32[328,128]{1,0:T(8,128)S(1)} collective-permute-done((f32[328,128]{1,0:T(8,128)S(1)}, f32[328,128]{1,0:T(8,128)S(1)}, u32[]{:S(2)}, u32[]{:S(2)}) %collective-permute-start.6) | collective-permute-done | bytes 167968 | tf_op jit(solution)/shard_map/ppermute | solution.py:697
  48.8 0.8 down.4
  49.6 0.8 collective-permute-start.9
  50.4 0.7 up.7
  51.2 1.3 %collective-permute-start.12 = (f32[328,128]{1,0:T(8,128)S(1)}, f32[328,128]{1,0:T(8,128)S(1)}, u32[]{:S(2)}, u32[]{:S(2)}) collective-permute-start(f32[328,128]{1,0:T(8,128)S(1)} %up.7), channel_id=1, source_target_pairs={{1,25},{3,27},{5,29},{7,31},{24,0},{26,2},{28,4},{30,6}} | collective-permute-start | bytes 503816 | tf_op jit(solution)/shard_map/ppermute | solution.py:697
  52.5 1.3 %collective-permute-start.11 = (f32[328,128]{1,0:T(8,128)S(1)}, f32[328,128]{1,0:T(8,128)S(1)}, u32[]{:S(2)}, u32[]{:S(2)}) collective-permute-start(f32[328,128]{1,0:T(8,128)S(1)} %up.7), channel_id=1, source_target_pairs={{1,17},{3,19},{5,21},{7,23},{9,25},{11,27},{13,29},{15,31},{16,0},... | collective-permute-start | bytes 503816 | tf_op jit(solution)/shard_map/ppermute | solution.py:697
  53.8 1.5 %collective-permute-start.10 = (f32[328,128]{1,0:T(8,128)S(1)}, f32[328,128]{1,0:T(8,128)S(1)}, u32[]{:S(2)}, u32[]{:S(2)}) collective-permute-start(f32[328,128]{1,0:T(8,128)S(1)} %up.7), channel_id=1, source_target_pairs={{1,9},{3,11},{5,13},{7,15},{8,0},{9,17},{10,2},{11,19},{12,4},{13,... | collective-permute-start | bytes 503816 | tf_op jit(solution)/shard_map/ppermute | solution.py:697
  55.2 4.2 %collective-permute-done.12.refs_6_ = f32[328,128]{1,0:T(8,128)S(1)} collective-permute-done((f32[328,128]{1,0:T(8,128)S(1)}, f32[328,128]{1,0:T(8,128)S(1)}, u32[]{:S(2)}, u32[]{:S(2)}) %collective-permute-start.12) | collective-permute-done | bytes 167968 | tf_op jit(solution)/shard_map/ppermute | solution.py:697
  59.4 1.7 %collective-permute-done.11.refs_5_ = f32[328,128]{1,0:T(8,128)S(1)} collective-permute-done((f32[328,128]{1,0:T(8,128)S(1)}, f32[328,128]{1,0:T(8,128)S(1)}, u32[]{:S(2)}, u32[]{:S(2)}) %collective-permute-start.11) | collective-permute-done | bytes 167968 | tf_op jit(solution)/shard_map/ppermute | solution.py:697
  61.1 0.8 down.5
  61.9 2.4 %collective-permute-start.13 = (f32[656,128]{1,0:T(8,128)S(1)}, f32[656,128]{1,0:T(8,128)S(1)}, u32[]{:S(2)}, u32[]{:S(2)}) collective-permute-start(f32[656,128]{1,0:T(8,128)S(1)} %get-tuple-element.170), channel_id=1, source_target_pairs={{0,2},{1,3},{2,0},{3,1},{4,6},{5,7},{6,4},{7,5},{8,10},{9,11},{10,... | collective-permute-start | bytes 1007624 | tf_op jit(solution)/shard_map/ppermute | solution.py:697
  64.3 0.8 down.6
  65.1 1.9 %collective-permute-start.14 = (f32[336,128]{1,0:T(8,128)S(1)}, f32[336,128]{1,0:T(8,128)S(1)}, u32[]{:S(2)}, u32[]{:S(2)}) collective-permute-start(f32[336,128]{1,0:T(8,128)S(1)} %get-tuple-element.174), channel_id=1, source_target_pairs={{0,4},{1,5},{2,6},{3,7},{4,0},{5,1},{6,2},{7,3},{8,12},{9,13},{10,... | collective-permute-start | bytes 516104 | tf_op jit(solution)/shard_map/ppermute | solution.py:697
  67.0 5.8 %collective-permute-done.14.refs_5_ = f32[336,128]{1,0:T(8,128)S(1)} collective-permute-done((f32[336,128]{1,0:T(8,128)S(1)}, f32[336,128]{1,0:T(8,128)S(1)}, u32[]{:S(2)}, u32[]{:S(2)}) %collective-permute-start.14) | collective-permute-done | bytes 172064 | tf_op jit(solution)/shard_map/ppermute | solution.py:697
  72.8 0.2 collective-permute-done.13.got_ref
  73.0 0.8 down.7
  73.8 1.7 %collective-permute-start.17 = (f32[656,128]{1,0:T(8,128)S(1)}, f32[656,128]{1,0:T(8,128)S(1)}, u32[]{:S(2)}, u32[]{:S(2)}) collective-permute-start(f32[656,128]{1,0:T(8,128)S(1)} %get-tuple-element.186), channel_id=1, source_target_pairs={{0,2},{1,3},{2,0},{3,1},{4,6},{5,7},{6,4},{7,5},{8,10},{9,11},{10,... | collective-permute-start | bytes 1007624 | tf_op jit(solution)/shard_map/ppermute | solution.py:697
  75.5 0.6 order.1
  76.2 0.5 collective-permute-start.16
  76.7 1.0 collective-permute-done.15.refs_7_
  77.8 0.5 collective-permute-done.16.refs_8_
  78.2 1.3 %assemble.2 = (bf16[128,1280]{1,0:T(8,128)(2,1)S(1)}, bf16[128,1280]{1,0:T(8,128)(2,1)S(1)}, f32[8,128]{1,0:T(8,128)S(1)}) custom-call(s32[3]{0:T(128)S(1)} %copy-done.10, f32[256,128]{1,0:T(8,128)S(1)} %get-tuple-element.158.refs_1_.refs_9_, f32[1288,128]{1,0:T(8,128)S(1)} %collective-permute-done.refs_1_.refs_2_, ...), custom_call_target="tpu_custom_call" | custom-call | flops 1 | bytes 1 | tf_op jit(solution)/shard_map/assemble/pallas_call | solution.py:538
  79.5 3.8 %finish.3 = (bf16[256,2560]{1,0:T(8,128)(2,1)}, f32[256,128]{1,0:T(8,128)S(1)}, f32[256,128]{1,0:T(8,128)S(1)}, f32[256,128]{1,0:T(8,128)S(1)}, f32[8,128]{1,0:T(8,128)S(1)}) custom-call(bf16[256,2560]{1,0:T(8,128)(2,1)S(1)} %copy-done, bf16[256,2560]{1,0:T(8,128)(2,1)S(1)} %copy-done.1, bf16[256,128]{1,0:T(8,128)(2,1)S(1)} %copy-done.2, ...), custom_call_target="tpu_custom_call" | custom-call | flops 1 | bytes 1 | tf_op jit(solution)/shard_map/finish/pallas_call | solution.py:606
  83.5 1.5 %collective-permute-done.19.refs_8_ = f32[656,128]{1,0:T(8,128)S(1)} collective-permute-done((f32[656,128]{1,0:T(8,128)S(1)}, f32[656,128]{1,0:T(8,128)S(1)}, u32[]{:S(2)}, u32[]{:S(2)}) %collective-permute-start.19) | collective-permute-done | bytes 335904 | tf_op jit(solution)/shard_map/ppermute | solution.py:697
  85.0 1.4 %assemble.3 = (bf16[128,1280]{1,0:T(8,128)(2,1)S(1)}, bf16[128,1280]{1,0:T(8,128)(2,1)S(1)}, f32[8,128]{1,0:T(8,128)S(1)}) custom-call(s32[3]{0:T(128)S(1)} %copy-done.10, f32[8,128]{1,0:T(8,128)S(1)} %get-tuple-element.189.refs_1_, f32[1288,128]{1,0:T(8,128)S(1)} %collective-permute-done.2.refs_1_.refs_2_, f32[128,2560]{1,0:T(8,128)S(1)} %get-tuple-element.159.refs_3_, ...), custom_call_target="tpu_custom_call" | custom-call | flops 1 | bytes 1 | tf_op jit(solution)/shard_map/assemble/pallas_call | solution.py:538
  86.3 0.2 collective-permute-start.20
  86.5 1.0 collective-permute-done.20.got_ref
  87.6 0.5 core_sum.1
  88.1 3.1 %collective-permute-start.23 = (f32[8,128]{1,0:T(8,128)S(1)}, f32[8,128]{1,0:T(8,128)S(1)}, u32[]{:S(2)}, u32[]{:S(2)}) collective-permute-start(f32[8,128]{1,0:T(8,128)S(1)} %get-tuple-element.197.refs_13_.total_ref), channel_id=1, source_target_pairs={{0,6},{1,7},{2,4},{3,5},{4,2},{5,3},{6,0},{7,1},{8,14},{9,15},{10,... | collective-permute-start | bytes 12296 | tf_op jit(solution)/shard_map/ppermute | solution.py:697
  91.2 1.4 %collective-permute-start.21 = (f32[8,128]{1,0:T(8,128)S(1)}, f32[8,128]{1,0:T(8,128)S(1)}, u32[]{:S(2)}, u32[]{:S(2)}) collective-permute-start(f32[8,128]{1,0:T(8,128)S(1)} %get-tuple-element.197.refs_13_.total_ref), channel_id=1, source_target_pairs={{0,2},{1,3},{2,0},{3,1},{4,6},{5,7},{6,4},{7,5},{8,10},{9,11},{10,... | collective-permute-start | bytes 12296 | tf_op jit(solution)/shard_map/ppermute | solution.py:697
  92.6 1.5 %finish.4 = (bf16[256,2560]{1,0:T(8,128)(2,1)}, f32[256,128]{1,0:T(8,128)S(1)}, f32[256,128]{1,0:T(8,128)S(1)}, f32[256,128]{1,0:T(8,128)S(1)}, f32[8,128]{1,0:T(8,128)S(1)}) custom-call(bf16[256,2560]{1,0:T(8,128)(2,1)S(1)} %copy-done, bf16[256,2560]{1,0:T(8,128)(2,1)S(1)} %copy-done.1, ...), custom_call_target="tpu_custom_call", output_to_operand_aliasing={{0}: (12, {})} | custom-call | flops 1 | bytes 1 | tf_op jit(solution)/shard_map/finish/pallas_call | solution.py:606
  94.1 1.6 %collective-permute-done.22.refs_1_ = f32[8,128]{1,0:T(8,128)S(1)} collective-permute-done((f32[8,128]{1,0:T(8,128)S(1)}, f32[8,128]{1,0:T(8,128)S(1)}, u32[]{:S(2)}, u32[]{:S(2)}) %collective-permute-start.22) | collective-permute-done | bytes 4128 | tf_op jit(solution)/shard_map/ppermute | solution.py:697
  95.7 0.6 chip_sum.1
  96.3 1.3 %collective-permute-start.26 = (f32[8,128]{1,0:T(8,128)S(1)}, f32[8,128]{1,0:T(8,128)S(1)}, u32[]{:S(2)}, u32[]{:S(2)}) collective-permute-start(f32[8,128]{1,0:T(8,128)S(1)} %get-tuple-element.204.refs_13_), channel_id=1, source_target_pairs={{24,0},{25,1},{26,2},{27,3},{28,4},{29,5},{30,6},{31,7}} | collective-permute-start | bytes 12296 | tf_op jit(solution)/shard_map/ppermute | solution.py:697
  97.6 1.3 %collective-permute-start.25 = (f32[8,128]{1,0:T(8,128)S(1)}, f32[8,128]{1,0:T(8,128)S(1)}, u32[]{:S(2)}, u32[]{:S(2)}) collective-permute-start(f32[8,128]{1,0:T(8,128)S(1)} %get-tuple-element.204.refs_13_), channel_id=1, source_target_pairs={{16,0},{17,1},{18,2},{19,3},{20,4},{21,5},{22,6},{23,7},{24,8},{25... | collective-permute-start | bytes 12296 | tf_op jit(solution)/shard_map/ppermute | solution.py:697
  98.9 1.3 %collective-permute-start.24 = (f32[8,128]{1,0:T(8,128)S(1)}, f32[8,128]{1,0:T(8,128)S(1)}, u32[]{:S(2)}, u32[]{:S(2)}) collective-permute-start(f32[8,128]{1,0:T(8,128)S(1)} %get-tuple-element.204.refs_13_), channel_id=1, source_target_pairs={{8,0},{9,1},{10,2},{11,3},{12,4},{13,5},{14,6},{15,7},{16,8},{17,9... | collective-permute-start | bytes 12296 | tf_op jit(solution)/shard_map/ppermute | solution.py:697
  100.2 2.0 %finish.5 = (bf16[256,2560]{1,0:T(8,128)(2,1)}, bf16[256,128]{1,0:T(8,128)(2,1)}, bf16[256,128]{1,0:T(8,128)(2,1)}, f32[40,256]{1,0:T(8,128)S(1)}, f32[8,128]{1,0:T(8,128)}) custom-call(bf16[256,2560]{1,0:T(8,128)(2,1)S(1)} %copy-done, bf16[256,2560]{1,0:T(8,128)(2,1)S(1)} %copy-done.1, ...), custom_call_target="tpu_custom_call", output_to_operand_aliasing={{0}: (12, {})} | custom-call | flops 1 | bytes 1 | tf_op jit(solution)/shard_map/finish/pallas_call | solution.py:606
  102.1 0.5 collective-permute-done.26.refs_3_
  102.7 0.4 collective-permute-done.25.refs_2_
  103.1 1.3 %collective-permute-done.24.refs_1_ = f32[8,128]{1,0:T(8,128)S(1)} collective-permute-done((f32[8,128]{1,0:T(8,128)S(1)}, f32[8,128]{1,0:T(8,128)S(1)}, u32[]{:S(2)}, u32[]{:S(2)}) %collective-permute-start.24) | collective-permute-done | bytes 4128 | tf_op jit(solution)/shard_map/ppermute | solution.py:697
  104.4 0.8 add_later.1
  (43 shorter events, 0.5 us)
Async XLA Ops:
  5.0 4.4 %collective-permute-start = (f32[1288,128]{1,0:T(8,128)}, f32[1288,128]{1,0:T(8,128)S(1)}, u32[]{:S(2)}, u32[]{:S(2)}) collective-permute-start(f32[1288,128]{1,0:T(8,128)} %get-tuple-element.109), channel_id=1, source_target_pairs={{0,1},{1,0},{2,3},{3,2},{4,5},{5,4},{6,7},{7,6},{8,9},{9,8},{10,11... | collective-permute-start | bytes 1978376 | tf_op jit(solution)/shard_map/ppermute | solution.py:697
  5.5 3.9 %copy-start.8 = (f32[1280,128]{1,0:T(8,128)S(1)}, f32[1280,128]{1,0:T(8,128)}, u32[]{:S(2)}) copy-start(f32[1280,128]{1,0:T(8,128)} %get-tuple-element.110.refs_2_) | copy-start | bytes 1966084
  5.5 3.9 %copy-start.10 = (s32[3]{0:T(128)S(1)}, s32[3]{0:T(128)}, u32[]{:S(2)}) copy-start(s32[3]{0:T(128)} %pad_add_fusion.refs_0_.place) | copy-start | bytes 40
  5.5 3.9 %copy-start.11 = (f32[8,128]{1,0:T(8,128)S(1)}, f32[8,128]{1,0:T(8,128)}, u32[]{:S(2)}) copy-start(f32[8,128]{1,0:T(8,128)} %get-tuple-element.112.refs_4_.refs_5_) | copy-start | bytes 12292
  5.5 3.9 %copy-start.13 = (f32[10,128]{1,0:T(8,128)S(1)}, f32[10,128]{1,0:T(8,128)}, u32[]{:S(2)}) copy-start(f32[10,128]{1,0:T(8,128)} %get-tuple-element.111.refs_3_) | copy-start | bytes 15364
  5.5 7.6 %copy-start.1 = (bf16[256,2560]{1,0:T(8,128)(2,1)S(1)}, bf16[256,2560]{1,0:T(8,128)(2,1)}, u32[]{:S(2)}) copy-start(bf16[256,2560]{1,0:T(8,128)(2,1)} %refs_1_.15) | copy-start | bytes 3932164
  5.5 7.6 %copy-start.2 = (bf16[256,128]{1,0:T(8,128)(2,1)S(1)}, bf16[256,128]{1,0:T(8,128)(2,1)}, u32[]{:S(2)}) copy-start(bf16[256,128]{1,0:T(8,128)(2,1)} %refs_2_.15) | copy-start | bytes 196612
  5.6 7.6 %copy-start.3 = (bf16[256,128]{1,0:T(8,128)(2,1)S(1)}, bf16[256,128]{1,0:T(8,128)(2,1)}, u32[]{:S(2)}) copy-start(bf16[256,128]{1,0:T(8,128)(2,1)} %refs_3_.15) | copy-start | bytes 196612
  5.6 7.6 %copy-start.4 = (bf16[256,128]{1,0:T(8,128)(2,1)S(1)}, bf16[256,128]{1,0:T(8,128)(2,1)}, u32[]{:S(2)}) copy-start(bf16[256,128]{1,0:T(8,128)(2,1)} %get-tuple-element.107.refs_6_.refs_7_.refs_4_) | copy-start | bytes 196612
  5.6 7.6 %copy-start.5 = (bf16[256,128]{1,0:T(8,128)(2,1)S(1)}, bf16[256,128]{1,0:T(8,128)(2,1)}, u32[]{:S(2)}) copy-start(bf16[256,128]{1,0:T(8,128)(2,1)} %get-tuple-element.108.refs_7_.refs_8_.refs_5_) | copy-start | bytes 196612
  5.6 7.6 %copy-start.6 = (f32[256,128]{1,0:T(8,128)S(1)}, f32[256,128]{1,0:T(8,128)}, u32[]{:S(2)}) copy-start(f32[256,128]{1,0:T(8,128)} %get-tuple-element.116.refs_6_) | copy-start | bytes 393220
  5.6 7.6 %copy-start.9 = (f32[40,256]{1,0:T(8,128)S(1)}, f32[40,256]{1,0:T(8,128)}, u32[]{:S(2)}) copy-start(f32[40,256]{1,0:T(8,128)} %refs_5_.7) | copy-start | bytes 122884
  9.3 3.9 %copy-start = (bf16[256,2560]{1,0:T(8,128)(2,1)S(1)}, bf16[256,2560]{1,0:T(8,128)(2,1)}, u32[]{:S(2)}) copy-start(bf16[256,2560]{1,0:T(8,128)(2,1)} %refs_0_.5) | copy-start | bytes 3932164
  9.3 9.0 %collective-permute-start.2 = (f32[1288,128]{1,0:T(8,128)}, f32[1288,128]{1,0:T(8,128)S(1)}, u32[]{:S(2)}, u32[]{:S(2)}) collective-permute-start(f32[1288,128]{1,0:T(8,128)} %get-tuple-element.115), channel_id=1, source_target_pairs={{0,1},{1,0},{2,3},{3,2},{4,5},{5,4},{6,7},{7,6},{8,9},{9,8},{10,11... | collective-permute-start | bytes 1978376 | tf_op jit(solution)/shard_map/ppermute | solution.py:697
  10.1 11.2 %collective-permute-start.1 = (f32[656,128]{1,0:T(8,128)S(1)}, f32[656,128]{1,0:T(8,128)S(1)}, u32[]{:S(2)}, u32[]{:S(2)}) collective-permute-start(f32[656,128]{1,0:T(8,128)S(1)} %get-tuple-element.114.refs_0_.refs_2_), channel_id=1, source_target_pairs={{0,2},{1,3},{2,0},{3,1},{4,6},{5,7},{6,4},{7,5},{8,10},{9,11},{10,... | collective-permute-start | bytes 1007624 | tf_op jit(solution)/shard_map/ppermute | solution.py:697
  13.2 8.0 %copy-start.7 = (f32[1280,128]{1,0:T(8,128)S(1)}, f32[1280,128]{1,0:T(8,128)}, u32[]{:S(2)}) copy-start(f32[1280,128]{1,0:T(8,128)} %get-tuple-element.126.refs_2_) | copy-start | bytes 1966084
  13.2 8.0 %copy-start.12 = (f32[10,128]{1,0:T(8,128)S(1)}, f32[10,128]{1,0:T(8,128)}, u32[]{:S(2)}) copy-start(f32[10,128]{1,0:T(8,128)} %get-tuple-element.127.refs_3_) | copy-start | bytes 15364
  21.9 13.1 %collective-permute-start.4 = (f32[656,128]{1,0:T(8,128)S(1)}, f32[656,128]{1,0:T(8,128)S(1)}, u32[]{:S(2)}, u32[]{:S(2)}) collective-permute-start(f32[656,128]{1,0:T(8,128)S(1)} %get-tuple-element.128.refs_2_), channel_id=1, source_target_pairs={{0,2},{1,3},{2,0},{3,1},{4,6},{5,7},{6,4},{7,5},{8,10},{9,11},{10,... | collective-permute-start | bytes 1007624 | tf_op jit(solution)/shard_map/ppermute | solution.py:697
  24.4 9.4 %collective-permute-start.3 = (f32[336,128]{1,0:T(8,128)S(1)}, f32[336,128]{1,0:T(8,128)S(1)}, u32[]{:S(2)}, u32[]{:S(2)}) collective-permute-start(f32[336,128]{1,0:T(8,128)S(1)} %get-tuple-element.124.refs_0_.refs_2_), channel_id=1, source_target_pairs={{0,4},{1,5},{2,6},{3,7},{4,0},{5,1},{6,2},{7,3},{8,12},{9,13},{10,... | collective-permute-start | bytes 516104 | tf_op jit(solution)/shard_map/ppermute | solution.py:697
  35.7 13.1 %collective-permute-start.8 = (f32[336,128]{1,0:T(8,128)S(1)}, f32[336,128]{1,0:T(8,128)S(1)}, u32[]{:S(2)}, u32[]{:S(2)}) collective-permute-start(f32[336,128]{1,0:T(8,128)S(1)} %get-tuple-element.142.refs_2_), channel_id=1, source_target_pairs={{0,4},{1,5},{2,6},{3,7},{4,0},{5,1},{6,2},{7,3},{8,12},{9,13},{10,... | collective-permute-start | bytes 516104 | tf_op jit(solution)/shard_map/ppermute | solution.py:697
  38.8 8.3 %collective-permute-start.7 = (f32[328,128]{1,0:T(8,128)S(1)}, f32[328,128]{1,0:T(8,128)S(1)}, u32[]{:S(2)}, u32[]{:S(2)}) collective-permute-start(f32[328,128]{1,0:T(8,128)S(1)} %up.5.refs_0_), channel_id=1, source_target_pairs={{1,25},{3,27},{5,29},{7,31},{24,0},{26,2},{28,4},{30,6}} | collective-permute-start | bytes 503816 | tf_op jit(solution)/shard_map/ppermute | solution.py:697
  40.1 8.7 %collective-permute-start.6 = (f32[328,128]{1,0:T(8,128)S(1)}, f32[328,128]{1,0:T(8,128)S(1)}, u32[]{:S(2)}, u32[]{:S(2)}) collective-permute-start(f32[328,128]{1,0:T(8,128)S(1)} %up.5.refs_0_), channel_id=1, source_target_pairs={{1,17},{3,19},{5,21},{7,23},{9,25},{11,27},{13,29},{15,31},{16,0},... | collective-permute-start | bytes 503816 | tf_op jit(solution)/shard_map/ppermute | solution.py:697
  41.4 7.4 %collective-permute-start.5 = (f32[328,128]{1,0:T(8,128)S(1)}, f32[328,128]{1,0:T(8,128)S(1)}, u32[]{:S(2)}, u32[]{:S(2)}) collective-permute-start(f32[328,128]{1,0:T(8,128)S(1)} %up.5.refs_0_), channel_id=1, source_target_pairs={{1,9},{3,11},{5,13},{7,15},{8,0},{9,17},{10,2},{11,19},{12,4},{13,... | collective-permute-start | bytes 503816 | tf_op jit(solution)/shard_map/ppermute | solution.py:697
  49.6 11.5 %collective-permute-start.9 = (f32[336,128]{1,0:T(8,128)S(1)}, f32[336,128]{1,0:T(8,128)S(1)}, u32[]{:S(2)}, u32[]{:S(2)}) collective-permute-start(f32[336,128]{1,0:T(8,128)S(1)} %get-tuple-element.165), channel_id=1, source_target_pairs={{0,4},{1,5},{2,6},{3,7},{4,0},{5,1},{6,2},{7,3},{8,12},{9,13},{10,... | collective-permute-start | bytes 516104 | tf_op jit(solution)/shard_map/ppermute | solution.py:697
  51.2 8.3 %collective-permute-start.12 = (f32[328,128]{1,0:T(8,128)S(1)}, f32[328,128]{1,0:T(8,128)S(1)}, u32[]{:S(2)}, u32[]{:S(2)}) collective-permute-start(f32[328,128]{1,0:T(8,128)S(1)} %up.7), channel_id=1, source_target_pairs={{1,25},{3,27},{5,29},{7,31},{24,0},{26,2},{28,4},{30,6}} | collective-permute-start | bytes 503816 | tf_op jit(solution)/shard_map/ppermute | solution.py:697
  52.5 8.7 %collective-permute-start.11 = (f32[328,128]{1,0:T(8,128)S(1)}, f32[328,128]{1,0:T(8,128)S(1)}, u32[]{:S(2)}, u32[]{:S(2)}) collective-permute-start(f32[328,128]{1,0:T(8,128)S(1)} %up.7), channel_id=1, source_target_pairs={{1,17},{3,19},{5,21},{7,23},{9,25},{11,27},{13,29},{15,31},{16,0},... | collective-permute-start | bytes 503816 | tf_op jit(solution)/shard_map/ppermute | solution.py:697
  53.8 7.4 %collective-permute-start.10 = (f32[328,128]{1,0:T(8,128)S(1)}, f32[328,128]{1,0:T(8,128)S(1)}, u32[]{:S(2)}, u32[]{:S(2)}) collective-permute-start(f32[328,128]{1,0:T(8,128)S(1)} %up.7), channel_id=1, source_target_pairs={{1,9},{3,11},{5,13},{7,15},{8,0},{9,17},{10,2},{11,19},{12,4},{13,... | collective-permute-start | bytes 503816 | tf_op jit(solution)/shard_map/ppermute | solution.py:697
  61.9 11.1 %collective-permute-start.13 = (f32[656,128]{1,0:T(8,128)S(1)}, f32[656,128]{1,0:T(8,128)S(1)}, u32[]{:S(2)}, u32[]{:S(2)}) collective-permute-start(f32[656,128]{1,0:T(8,128)S(1)} %get-tuple-element.170), channel_id=1, source_target_pairs={{0,2},{1,3},{2,0},{3,1},{4,6},{5,7},{6,4},{7,5},{8,10},{9,11},{10,... | collective-permute-start | bytes 1007624 | tf_op jit(solution)/shard_map/ppermute | solution.py:697
  65.1 7.7 %collective-permute-start.14 = (f32[336,128]{1,0:T(8,128)S(1)}, f32[336,128]{1,0:T(8,128)S(1)}, u32[]{:S(2)}, u32[]{:S(2)}) collective-permute-start(f32[336,128]{1,0:T(8,128)S(1)} %get-tuple-element.174), channel_id=1, source_target_pairs={{0,4},{1,5},{2,6},{3,7},{4,0},{5,1},{6,2},{7,3},{8,12},{9,13},{10,... | collective-permute-start | bytes 516104 | tf_op jit(solution)/shard_map/ppermute | solution.py:697
  73.8 9.6 %collective-permute-start.17 = (f32[656,128]{1,0:T(8,128)S(1)}, f32[656,128]{1,0:T(8,128)S(1)}, u32[]{:S(2)}, u32[]{:S(2)}) collective-permute-start(f32[656,128]{1,0:T(8,128)S(1)} %get-tuple-element.186), channel_id=1, source_target_pairs={{0,2},{1,3},{2,0},{3,1},{4,6},{5,7},{6,4},{7,5},{8,10},{9,11},{10,... | collective-permute-start | bytes 1007624 | tf_op jit(solution)/shard_map/ppermute | solution.py:697
  76.1 1.7 %collective-permute-start.15 = (f32[640,128]{1,0:T(8,128)S(1)}, f32[640,128]{1,0:T(8,128)S(1)}, u32[]{:S(2)}, u32[]{:S(2)}) collective-permute-start(f32[640,128]{1,0:T(8,128)S(1)} %get-tuple-element.176.refs_5_), channel_id=1, source_target_pairs={{0,1},{1,0},{2,3},{3,2},{4,5},{5,4},{6,7},{7,6},{8,9},{9,8},{10,11... | collective-permute-start | bytes 983048 | tf_op jit(solution)/shard_map/ppermute | solution.py:697
  76.2 2.1 %collective-permute-start.16 = (f32[640,128]{1,0:T(8,128)S(1)}, f32[640,128]{1,0:T(8,128)S(1)}, u32[]{:S(2)}, u32[]{:S(2)}) collective-permute-start(f32[640,128]{1,0:T(8,128)S(1)} %get-tuple-element.177.refs_6_), channel_id=1, source_target_pairs={{0,1},{1,0},{2,3},{3,2},{4,5},{5,4},{6,7},{7,6},{8,9},{9,8},{10,11... | collective-permute-start | bytes 983048 | tf_op jit(solution)/shard_map/ppermute | solution.py:697
  76.7 6.7 %collective-permute-start.18 = (f32[640,128]{1,0:T(8,128)S(1)}, f32[640,128]{1,0:T(8,128)S(1)}, u32[]{:S(2)}, u32[]{:S(2)}) collective-permute-start(f32[640,128]{1,0:T(8,128)S(1)} %get-tuple-element.187.refs_5_), channel_id=1, source_target_pairs={{0,1},{1,0},{2,3},{3,2},{4,5},{5,4},{6,7},{7,6},{8,9},{9,8},{10,11... | collective-permute-start | bytes 983048 | tf_op jit(solution)/shard_map/ppermute | solution.py:697
  83.3 1.6 %collective-permute-start.19 = (f32[656,128]{1,0:T(8,128)S(1)}, f32[656,128]{1,0:T(8,128)S(1)}, u32[]{:S(2)}, u32[]{:S(2)}) collective-permute-start(f32[656,128]{1,0:T(8,128)S(1)} %collective-permute-done.17.refs_6_), channel_id=1, source_target_pairs={{0,1},{1,0},{2,3},{3,2},{4,5},{5,4},{6,7},{7,6},{8,9},{9,8},{10,11... | collective-permute-start | bytes 1007624 | tf_op jit(solution)/shard_map/ppermute | solution.py:697
  86.3 1.2 %collective-permute-start.20 = (f32[8,128]{1,0:T(8,128)S(1)}, f32[8,128]{1,0:T(8,128)S(1)}, u32[]{:S(2)}, u32[]{:S(2)}) collective-permute-start(f32[8,128]{1,0:T(8,128)S(1)} %get-tuple-element.196.total_ref), channel_id=1, source_target_pairs={{0,1},{1,0},{2,3},{3,2},{4,5},{5,4},{6,7},{7,6},{8,9},{9,8},{10,11... | collective-permute-start | bytes 12296 | tf_op jit(solution)/shard_map/ppermute | solution.py:697
  88.1 6.0 %collective-permute-start.23 = (f32[8,128]{1,0:T(8,128)S(1)}, f32[8,128]{1,0:T(8,128)S(1)}, u32[]{:S(2)}, u32[]{:S(2)}) collective-permute-start(f32[8,128]{1,0:T(8,128)S(1)} %get-tuple-element.197.refs_13_.total_ref), channel_id=1, source_target_pairs={{0,6},{1,7},{2,4},{3,5},{4,2},{5,3},{6,0},{7,1},{8,14},{9,15},{10,... | collective-permute-start | bytes 12296 | tf_op jit(solution)/shard_map/ppermute | solution.py:697
  91.2 4.5 %collective-permute-start.22 = (f32[8,128]{1,0:T(8,128)S(1)}, f32[8,128]{1,0:T(8,128)S(1)}, u32[]{:S(2)}, u32[]{:S(2)}) collective-permute-start(f32[8,128]{1,0:T(8,128)S(1)} %get-tuple-element.197.refs_13_.total_ref), channel_id=1, source_target_pairs={{0,4},{1,5},{2,6},{3,7},{4,0},{5,1},{6,2},{7,3},{8,12},{9,13},{10,... | collective-permute-start | bytes 12296 | tf_op jit(solution)/shard_map/ppermute | solution.py:697
  91.2 4.5 %collective-permute-start.21 = (f32[8,128]{1,0:T(8,128)S(1)}, f32[8,128]{1,0:T(8,128)S(1)}, u32[]{:S(2)}, u32[]{:S(2)}) collective-permute-start(f32[8,128]{1,0:T(8,128)S(1)} %get-tuple-element.197.refs_13_.total_ref), channel_id=1, source_target_pairs={{0,2},{1,3},{2,0},{3,1},{4,6},{5,7},{6,4},{7,5},{8,10},{9,11},{10,... | collective-permute-start | bytes 12296 | tf_op jit(solution)/shard_map/ppermute | solution.py:697
  96.3 6.4 %collective-permute-start.26 = (f32[8,128]{1,0:T(8,128)S(1)}, f32[8,128]{1,0:T(8,128)S(1)}, u32[]{:S(2)}, u32[]{:S(2)}) collective-permute-start(f32[8,128]{1,0:T(8,128)S(1)} %get-tuple-element.204.refs_13_), channel_id=1, source_target_pairs={{24,0},{25,1},{26,2},{27,3},{28,4},{29,5},{30,6},{31,7}} | collective-permute-start | bytes 12296 | tf_op jit(solution)/shard_map/ppermute | solution.py:697
  97.6 5.5 %collective-permute-start.25 = (f32[8,128]{1,0:T(8,128)S(1)}, f32[8,128]{1,0:T(8,128)S(1)}, u32[]{:S(2)}, u32[]{:S(2)}) collective-permute-start(f32[8,128]{1,0:T(8,128)S(1)} %get-tuple-element.204.refs_13_), channel_id=1, source_target_pairs={{16,0},{17,1},{18,2},{19,3},{20,4},{21,5},{22,6},{23,7},{24,8},{25... | collective-permute-start | bytes 12296 | tf_op jit(solution)/shard_map/ppermute | solution.py:697
  98.9 5.5 %collective-permute-start.24 = (f32[8,128]{1,0:T(8,128)S(1)}, f32[8,128]{1,0:T(8,128)S(1)}, u32[]{:S(2)}, u32[]{:S(2)}) collective-permute-start(f32[8,128]{1,0:T(8,128)S(1)} %get-tuple-element.204.refs_13_), channel_id=1, source_target_pairs={{8,0},{9,1},{10,2},{11,3},{12,4},{13,5},{14,6},{15,7},{16,8},{17,9... | collective-permute-start | bytes 12296 | tf_op jit(solution)/shard_map/ppermute | solution.py:697

commit v13 on v12

--- a/solution.py
+++ b/solution.py
@@ -114,11 +114,18 @@
 
 
 LITTLE = pl.CostEstimate(flops=1, bytes_accessed=1, transcendentals=0)
-SCALARS = pl.BlockSpec(memory_space=pltpu.SMEM)
+
+
+def position():
+    shard = lax.axis_index("seq")
+    return shard & 1, shard >> 1
+
+
 STEPS = 2
 
 
-def summary_kernel(heads, chips, half, place, x_ref, g_ref, write_ref, read_ref, *refs):
+def summary_kernel(heads, chips, half, x_ref, g_ref, write_ref, read_ref, *refs):
+    place = position()
     chunk = pl.program_id(0)
     lanes = x_ref.shape[1]
     strips = lanes // STRIP
@@ -164,7 +171,7 @@
             keep_ref[rows, :] = keep[mine, wide]
 
 
-def summary(chips, half, place, x, g, write_map, read_map, rates, shared):
+def summary(chips, half, x, g, write_map, read_map, rates, shared):
     tokens, wide = x.shape
     heads = rates.shape[0]
     lanes = wide // (STEPS * HALVES)
@@ -189,7 +196,6 @@
         lambda *refs: summary_kernel(heads, chips, half, *refs),
         grid=(STEPS,),
         in_specs=[
-            SCALARS,
             half_lanes(tokens, lanes, half, STEPS),
             half_lanes(tokens, lanes, half, STEPS),
             whole(tokens, STATE),
@@ -205,10 +211,11 @@
         compiler_params=pltpu.CompilerParams(vmem_limit_bytes=BIG_VMEM),
         cost_estimate=LITTLE,
         name="summary",
-    )(place, x, g, write_map, read_map, *extra)
-
-
-def combine_kernel(chips, place, first_ref, keep_ref, decay_ref, log_ref, mine_ref, send_ref):
+    )(x, g, write_map, read_map, *extra)
+
+
+def combine_kernel(chips, first_ref, keep_ref, decay_ref, log_ref, mine_ref, send_ref):
+    place = position()
     strips = decay_ref.shape[0]
     part = STATE // chips
     size = mine_ref.shape[0]
@@ -234,31 +241,28 @@
     )
 
 
-def combine(chips, place, first, keep, decay, log):
+def combine(chips, first, keep, decay, log):
     out_specs, out_shape = halves(keep.shape[0] // 2)
     return pl.pallas_call(
         lambda *refs: combine_kernel(chips, *refs),
-        in_specs=[SCALARS] + [whole(*value.shape) for value in (first, keep, decay, log)],
+        in_specs=[whole(*value.shape) for value in (first, keep, decay, log)],
         out_specs=out_specs,
         out_shape=out_shape,
         compiler_params=pltpu.CompilerParams(vmem_limit_bytes=SMALL_VMEM),
         cost_estimate=LITTLE,
         name="combine",
-    )(place, first, keep, decay, log)
+    )(first, keep, decay, log)
 
 
 def is_ahead(place, level):
     return ((place[1] >> level) & 1) == place[0]
 
 
-def tail_block(value):
-    return pl.BlockSpec((META, STRIP), lambda c: (value.shape[0] // META - 1, 0))
-
-
-def up_kernel(level, last, part, offset, strips, head_size, place, mine_ref, log_ref, got_ref, *outs):
+def up_kernel(level, last, part, offset, strips, head_size, mine_ref, log_ref, got_ref, *outs):
+    place = position()
     size = mine_ref.shape[0]
     ahead = is_ahead(place, level)
-    mine_log, got_log = log_ref[0:1, :], got_ref[size : size + 1, :]
+    mine_log, got_log = log_ref[size : size + 1, :], got_ref[size : size + 1, :]
     mine_wide, got_wide = spread_rows(
         [jnp.where(ahead, 1.0, jnp.exp(got_log)), jnp.where(ahead, jnp.exp(mine_log), 1.0)],
         offset,
@@ -281,7 +285,7 @@
     outs[-1][half:, :] = jnp.broadcast_to(mine_log + got_log, (META if last else PAD, STRIP))
 
 
-def up(level, chips, half, strips, head_size, place, mine, send, got):
+def up(level, chips, half, strips, head_size, mine, send, got):
     size = mine.shape[0]
     last = 2 << level == chips
     out_specs, out_shape = halves(size if last else size // 2)
@@ -292,23 +296,23 @@
         lambda *refs: up_kernel(
             level, last, STATE // chips, half * strips, strips, head_size, *refs
         ),
-        grid=(1,),
-        in_specs=[SCALARS, whole(size, STRIP), tail_block(send), whole(size + PAD, STRIP)],
+        in_specs=[whole(size, STRIP), whole(*send.shape), whole(size + PAD, STRIP)],
         out_specs=out_specs,
         out_shape=out_shape,
         compiler_params=pltpu.CompilerParams(vmem_limit_bytes=SMALL_VMEM),
         cost_estimate=LITTLE,
         name="up",
-    )(place, mine, send, got)
-
-
-def down_kernel(level, top, part, offset, strips, head_size, place, mine_ref, log_ref, got_ref, *refs):
+    )(mine, send, got)
+
+
+def down_kernel(level, top, part, offset, strips, head_size, mine_ref, log_ref, got_ref, *refs):
+    place = position()
     sources, (here_ref, there_ref) = refs[:-2], refs[-2:]
     size = mine_ref.shape[0]
     ahead = is_ahead(place, level)
     rows_of = [
         jnp.where(ahead, jnp.exp(got_ref[size : size + 1, :]), 1.0),
-        jnp.where(ahead, 1.0, jnp.exp(log_ref[0:1, :])),
+        jnp.where(ahead, 1.0, jnp.exp(log_ref[size : size + 1, :])),
     ]
     if top:
         passed = jnp.zeros_like(rows_of[0])
@@ -340,15 +344,14 @@
     there_ref[size:, :] = jnp.zeros((PAD, STRIP), F32)
 
 
-def down(level, chips, half, strips, head_size, place, mine, send, got, sources):
+def down(level, chips, half, strips, head_size, mine, send, got, sources):
     size = mine.shape[0]
     top = 2 << level == chips
     return pl.pallas_call(
         lambda *refs: down_kernel(
             level, top, STATE // chips, half * strips, strips, head_size, *refs
         ),
-        grid=(1,),
-        in_specs=[SCALARS, whole(size, STRIP), tail_block(send), whole(size + PAD, STRIP)]
+        in_specs=[whole(size, STRIP), whole(*send.shape), whole(size + PAD, STRIP)]
         + [whole(*value.shape) for value in sources],
         out_specs=[whole(size, STRIP), whole(size + PAD, STRIP)],
         out_shape=[
@@ -358,7 +361,7 @@
         compiler_params=pltpu.CompilerParams(vmem_limit_bytes=SMALL_VMEM),
         cost_estimate=LITTLE,
         name="down",
-    )(place, mine, send, got, *sources)
+    )(mine, send, got, *sources)
 
 
 def intra_kernel(
@@ -472,29 +475,31 @@
     )(after, x, g, write_map, read_map, rates, *shared[1:], *earlier)
 
 
-def order_kernel(place, here_ref, got_ref, low_ref, high_ref):
+def order_kernel(here_ref, got_ref, low_ref, high_ref):
+    place = position()
     bit = place[1] & 1
     here, got = here_ref[...], got_ref[: here_ref.shape[0], :]
     low_ref[...] = jnp.where(bit == 0, here, got)
     high_ref[...] = jnp.where(bit == 0, got, here)
 
 
-def order(place, here, got):
+def order(here, got):
     return pl.pallas_call(
         order_kernel,
-        in_specs=[SCALARS, whole(*here.shape), whole(*got.shape)],
+        in_specs=[whole(*here.shape), whole(*got.shape)],
         out_specs=[whole(*here.shape)] * 2,
         out_shape=[jax.ShapeDtypeStruct(here.shape, F32)] * 2,
         compiler_params=pltpu.CompilerParams(vmem_limit_bytes=SMALL_VMEM),
         cost_estimate=LITTLE,
         name="order",
-    )(place, here, got)
+    )(here, got)
 
 
 def assemble_kernel(
     heads, chips, half, head_size, ordered,
-    place, after_ref, first_ref, state_own, back_own, *refs,
+    after_ref, first_ref, state_own, back_own, *refs,
 ):
+    place = position()
     own_refs, far_refs, (state_ref, back_ref, total_ref) = refs[:2], refs[2:4], refs[4:]
     bit = 0 if ordered else place[1] & 1
     lanes = state_ref.shape[1]
@@ -531,14 +536,14 @@
     total_ref[...] = total + after_ref[...] if half else total
 
 
-def assemble(heads, chips, half, ordered, place, after, first, state_own, back_own, own, far):
+def assemble(heads, chips, half, ordered, after, first, state_own, back_own, own, far):
     wide = state_own.shape[1]
     lanes = wide // HALVES
     mine = pl.BlockSpec((STATE, lanes), lambda c: (0, half))
     return pl.pallas_call(
         lambda *refs: assemble_kernel(heads, chips, half, wide // heads, ordered, *refs),
         grid=(1,),
-        in_specs=[SCALARS, whole(META, STRIP), whole(*first.shape), mine, mine]
+        in_specs=[whole(META, STRIP), whole(*first.shape), mine, mine]
         + [whole(*value.shape) for value in (*own, *far)],
         out_specs=[whole(STATE, lanes), whole(STATE, lanes), whole(META, STRIP)],
         out_shape=[
@@ -549,7 +554,7 @@
         compiler_params=pltpu.CompilerParams(vmem_limit_bytes=SMALL_VMEM),
         cost_estimate=LITTLE,
         name="assemble",
-    )(place, after, first, state_own, back_own, *own, *far)
+    )(after, first, state_own, back_own, *own, *far)
 
 
 def finish_kernel(
@@ -629,7 +634,8 @@
     )(x, g, write_map, read_map, *shared[2:], dx, *sums, state, back, *earlier, after)
 
 
-def count_kernel(place, after_ref, later_ref, total_ref, *refs):
+def count_kernel(after_ref, later_ref, total_ref, *refs):
+    place = position()
     got_refs, (later_out, total_out) = refs[:-2], refs[-2:]
     later, total = later_ref[...], total_ref[...]
     for step, ref in enumerate(got_refs, 1):
@@ -639,21 +645,22 @@
     total_out[...] = total
 
 
-def core_kernel(place, total_ref, got_ref, later_out, total_out):
+def core_kernel(total_ref, got_ref, later_out, total_out):
+    place = position()
     later_out[...] = jnp.where(place[0] == 0, got_ref[...], 0.0)
     total_out[...] = total_ref[...] + got_ref[...]
 
 
-def tiles(kernel, name, place, *values):
+def tiles(kernel, name, *values):
     return pl.pallas_call(
         kernel,
-        in_specs=[SCALARS] + [whole(META, STRIP)] * len(values),
+        in_specs=[whole(META, STRIP)] * len(values),
         out_specs=[whole(META, STRIP)] * 2,
         out_shape=[jax.ShapeDtypeStruct((META, STRIP), F32)] * 2,
         compiler_params=pltpu.CompilerParams(vmem_limit_bytes=SMALL_VMEM),
         cost_estimate=LITTLE,
         name=name,
-    )(place, *values)
+    )(*values)
 
 
 def add_later_kernel(suffix_ref, *refs):
@@ -682,9 +689,6 @@
     head_size = inputs.shape[1] // heads
     groups, shards = lax.axis_size("grp"), lax.axis_size("seq")
     chips = shards // 2
-    shard, group = lax.axis_index("seq"), lax.axis_index("grp")
-    chip, core = shard >> 1, shard & 1
-    place = jnp.stack([core, chip, group]).astype(jnp.int32)
     strips = inputs.shape[1] // STRIP // HALVES
     everyone = [(a, z, c) for a in range(groups) for z in range(chips) for c in range(2)]
 
@@ -713,10 +717,10 @@
         return move(value, target)
 
     maps = (inputs, out_grad, input_map, output_map)
-    send, keep, decay, *shared = summary(chips, 0, place, *maps, log_decay, None)
+    send, keep, decay, *shared = summary(chips, 0, *maps, log_decay, None)
     first = [to_core(send)]
     kept, decays = [keep], [decay]
-    send, keep, decay = summary(chips, 1, place, *maps, log_decay, shared)
+    send, keep, decay = summary(chips, 1, *maps, log_decay, shared)
     first.append(to_core(send))
     kept.append(keep)
     decays.append(decay)
@@ -726,10 +730,10 @@
     waiting = [None, None]
 
     def advance(half, step):
-        fixed = (chips, half, strips, head_size, place)
+        fixed = (chips, half, strips, head_size)
         if step == 0:
             mine, send = combine(
-                chips, place, first[half], kept[half], decays[half], shared[0]
+                chips, first[half], kept[half], decays[half], shared[0]
             )
         elif step < levels:
             held[half][-1] += (waiting[half],)
@@ -748,7 +752,7 @@
             waiting[half] = to_chip(send, 1 << level)
             return send
         else:
-            held[half] = order(place, held[half][0], waiting[half])
+            held[half] = order(held[half][0], waiting[half])
             waiting[half] = [to_core(value) for value in held[half]]
             return held[half][0]
         held[half].append((mine, send))
@@ -775,7 +779,7 @@
     own_b = held[1][0]
     far_b = to_core(own_b)
     state, back, counted = assemble(
-        heads, chips, 0, True, place, change, first[0], state_own, back_own, held[0], waiting[0]
+        heads, chips, 0, True, change, first[0], state_own, back_own, held[0], waiting[0]
     )
     grad, *sums, counted = finish(
         heads, 0, STEPS, counted, *maps, shared, dx, (db, dc, change), state, back, None
@@ -783,15 +787,15 @@
     got, far_b, counted = lax.optimization_barrier((waiting[1], far_b, counted))
     own_b, far_b = (own_b, got), (far_b, to_core(got))
     state, back, counted = assemble(
-        heads, chips, 1, False, place, counted, first[1], state_own, back_own, own_b, far_b
-    )
-
-    later, counted = tiles(core_kernel, "core_sum", place, counted, to_core(counted))
+        heads, chips, 1, False, counted, first[1], state_own, back_own, own_b, far_b
+    )
+
+    later, counted = tiles(core_kernel, "core_sum", counted, to_core(counted))
     got = [to_chip(counted, step) for step in range(1, chips)]
     grad, *sums, token = finish(
         heads, STEPS, 1, counted, *maps, shared, dx, sums, state, back, grad
     )
-    later, counted = tiles(count_kernel, "chip_sum", place, token, later, counted, *got)
+    later, counted = tiles(count_kernel, "chip_sum", token, later, counted, *got)
     got = [to_earlier(counted, step) for step in range(1, groups)]
     grad, *sums, _ = finish(
         heads, STEPS + 1, 1, counted, *maps, shared, dx, sums, state, back, grad

time: 105 us -> 98.3 us (0.936)
  Pallas kernels: 39.7 us -> 31.6 us
  waiting for transfers between devices: 29.1 us -> 30.5 us
    pallas_call x5, Pallas kernels: 2.96 us -> 0.27 us  [the longest x2 0.19 us: combine(): pl.pallas_call(lambda *refs: combine_kernel(chips, *refs), in_specs=[whol...]
    pallas_call x4, Pallas kernels: 3.15 us -> 0.99 us  [down(): pl.pallas_call(lambda *refs: down_kernel(level, top, STATE // chips, half...]
    pallas_call x4, Pallas kernels: 2.96 us -> 0.8 us  [up(): pl.pallas_call(lambda *refs: up_kernel(level, last, STATE // chips, half...]
    ppermute x27, waiting for transfers between devices: 29.1 us -> 30.5 us  [move(): return lax.ppermute(value, ('grp', 'seq'), pairs)]
    pallas_call x2, Pallas kernels: 2.65 us -> 1.59 us  [assemble(): pl.pallas_call(lambda *refs: assemble_kernel(heads, chips, half, wide //...]
  transfers between devices with their start and end apart: 27 -> 27, of which waited for: 17 -> 17; matrix products, arithmetic and copies ran while one was open for 0% -> 0% of each run, Pallas kernels for 28% -> 26%
where the time goes in v13:
time: 98.3 us; the launch traced here: 98 us
  starting transfers between devices  34.9 us (36%)
  Pallas kernels  31.6 us (32%)
  waiting for transfers between devices  30.5 us (31%)
    ppermute x27, starting transfers between devices, move(): return lax.ppermute(value, ('grp', 'seq'), pairs)  34.9 us
    ppermute x27, waiting for transfers between devices, move(): return lax.ppermute(value, ('grp', 'seq'), pairs)  30.5 us
    pallas_call x3, Pallas kernels, intra(): pl.pallas_call(lambda *refs: intra_kernel(heads, wide // heads, start, la...  12.5 us
    pallas_call x2, Pallas kernels, summary(): pl.pallas_call(lambda *refs: summary_kernel(heads, chips, half, *refs), g...  7.38 us
    pallas_call x3, Pallas kernels, finish(): pl.pallas_call(lambda *refs: finish_kernel(heads, start, steps, last, *re...  7.27 us
  transfers between devices with their start and end apart: 27, of which 17 were waited for; matrix products, arithmetic and copies ran while one was open for 0% of the time, Pallas kernels for 26%

profile of v13, /device:TPU:0, one launch (start us, length us, event | category | flops | bytes accessed | tf_op | source)
XLA Modules:
  0.0 98.0 jit_solution(17097457351653227584)
XLA Ops:
  0.6 3.8 %summary.2 = (f32[1288,128]{1,0:T(8,128)}, f32[1280,128]{1,0:T(8,128)}, f32[10,128]{1,0:T(8,128)}, f32[8,128]{1,0:T(8,128)}, f32[256,128]{1,0:T(8,128)}, /*index...) custom-call(bf16[256,2560]{1,0:T(8,128)(2,1)} %refs_0_.9, bf16[256,2560]{1,0:T(8,128)(2,1)} %refs_1_.15, ...), custom_call_target="tpu_custom_call" | custom-call | flops 1 | bytes 1 | tf_op jit(solution)/shard_map/summary/pallas_call | solution.py:195
  4.4 0.5 collective-permute-start
  5.0 3.6 %summary.3 = (f32[1288,128]{1,0:T(8,128)}, f32[1280,128]{1,0:T(8,128)}, f32[10,128]{1,0:T(8,128)}) custom-call(bf16[256,2560]{1,0:T(8,128)(2,1)} %refs_0_.9, bf16[256,2560]{1,0:T(8,128)(2,1)} %refs_1_.15, bf16[256,128]{1,0:T(8,128)(2,1)} %refs_2_.15, bf16[256,128]{1,0:T(8,128)(2,1)} %refs_3_.15, f32[8,128]{1,0:T(8,128)} %get-tuple-element.112.refs_3_.refs_4_, ...), custom_call_target="tpu_custom_call" | custom-call | flops 1 | bytes 1 | tf_op jit(solution)/shard_map/summary/pallas_call | solution.py:195
  8.6 0.1 collective-permute-start.2
  8.8 0.1 combine.2
  8.9 3.1 %collective-permute-start.1 = (f32[656,128]{1,0:T(8,128)S(1)}, f32[656,128]{1,0:T(8,128)S(1)}, u32[]{:S(2)}, u32[]{:S(2)}) collective-permute-start(f32[656,128]{1,0:T(8,128)S(1)} %get-tuple-element.114.refs_0_.refs_1_), channel_id=1, source_target_pairs={{0,2},{1,3},{2,0},{3,1},{4,6},{5,7},{6,4},{7,5},{8,10},{9,11},{10,... | collective-permute-start | bytes 1007624 | tf_op jit(solution)/shard_map/ppermute | solution.py:701
  12.0 5.1 %intra.3 = (f32[256,2560]{1,0:T(8,128)S(1)}, f32[128,2560]{1,0:T(8,128)S(1)}, f32[128,2560]{1,0:T(8,128)S(1)}, f32[256,128]{1,0:T(8,128)S(1)}, f32[256,256]{1,0:T(8,128)S(1)}) custom-call(f32[656,128]{1,0:T(8,128)S(1)} %get-tuple-element.114.refs_0_.refs_1_, bf16[256,2560]{1,0:T(8,128)(2,1)S(1)} %copy-done, bf16[256,2560]{1,0:T(8,128)(2,1)S(1)} %copy-done.1, ...), custom_call_target="tpu_custom_call" | custom-call | flops 1 | bytes 1 | tf_op jit(solution)/shard_map/intra/pallas_call | solution.py:441
  17.1 2.9 %collective-permute-done.1.refs_2_ = f32[656,128]{1,0:T(8,128)S(1)} collective-permute-done((f32[656,128]{1,0:T(8,128)S(1)}, f32[656,128]{1,0:T(8,128)S(1)}, u32[]{:S(2)}, u32[]{:S(2)}) %collective-permute-start.1) | collective-permute-done | bytes 335904 | tf_op jit(solution)/shard_map/ppermute | solution.py:701
  20.1 0.1 combine.3
  20.1 1.8 %collective-permute-start.4 = (f32[656,128]{1,0:T(8,128)S(1)}, f32[656,128]{1,0:T(8,128)S(1)}, u32[]{:S(2)}, u32[]{:S(2)}) collective-permute-start(f32[656,128]{1,0:T(8,128)S(1)} %get-tuple-element.128.refs_1_), channel_id=1, source_target_pairs={{0,2},{1,3},{2,0},{3,1},{4,6},{5,7},{6,4},{7,5},{8,10},{9,11},{10,... | collective-permute-start | bytes 1007624 | tf_op jit(solution)/shard_map/ppermute | solution.py:701
  22.0 0.2 up.4
  22.2 2.7 %collective-permute-start.3 = (f32[336,128]{1,0:T(8,128)S(1)}, f32[336,128]{1,0:T(8,128)S(1)}, u32[]{:S(2)}, u32[]{:S(2)}) collective-permute-start(f32[336,128]{1,0:T(8,128)S(1)} %get-tuple-element.124.refs_0_.refs_1_), channel_id=1, source_target_pairs={{0,4},{1,5},{2,6},{3,7},{4,0},{5,1},{6,2},{7,3},{8,12},{9,13},{10,... | collective-permute-start | bytes 516104 | tf_op jit(solution)/shard_map/ppermute | solution.py:701
  24.8 5.0 %intra.4 = (f32[256,2560]{1,0:T(8,128)S(1)}, f32[128,2560]{1,0:T(8,128)S(1)}, f32[128,2560]{1,0:T(8,128)S(1)}, f32[256,128]{1,0:T(8,128)S(1)}, f32[256,256]{1,0:T(8,128)S(1)}) custom-call(f32[336,128]{1,0:T(8,128)S(1)} %get-tuple-element.124.refs_0_.refs_1_, ...), custom_call_target="tpu_custom_call", output_to_operand_aliasing={{0}: (9, {}), {1}: (10, {}), {2}: (11, {})} | custom-call | flops 1 | bytes 1 | tf_op jit(solution)/shard_map/intra/pallas_call | solution.py:441
  29.8 2.3 %collective-permute-done.3.refs_2_ = f32[336,128]{1,0:T(8,128)S(1)} collective-permute-done((f32[336,128]{1,0:T(8,128)S(1)}, f32[336,128]{1,0:T(8,128)S(1)}, u32[]{:S(2)}, u32[]{:S(2)}) %collective-permute-start.3) | collective-permute-done | bytes 172064 | tf_op jit(solution)/shard_map/ppermute | solution.py:701
  32.1 1.1 %collective-permute-done.4.refs_2_ = f32[656,128]{1,0:T(8,128)S(1)} collective-permute-done((f32[656,128]{1,0:T(8,128)S(1)}, f32[656,128]{1,0:T(8,128)S(1)}, u32[]{:S(2)}, u32[]{:S(2)}) %collective-permute-start.4) | collective-permute-done | bytes 335904 | tf_op jit(solution)/shard_map/ppermute | solution.py:701
  33.2 0.2 up.6
  33.4 2.4 %collective-permute-start.8 = (f32[336,128]{1,0:T(8,128)S(1)}, f32[336,128]{1,0:T(8,128)S(1)}, u32[]{:S(2)}, u32[]{:S(2)}) collective-permute-start(f32[336,128]{1,0:T(8,128)S(1)} %get-tuple-element.142.refs_1_), channel_id=1, source_target_pairs={{0,4},{1,5},{2,6},{3,7},{4,0},{5,1},{6,2},{7,3},{8,12},{9,13},{10,... | collective-permute-start | bytes 516104 | tf_op jit(solution)/shard_map/ppermute | solution.py:701
  35.8 0.2 up.5.refs_0_
  36.0 1.3 %collective-permute-start.7 = (f32[328,128]{1,0:T(8,128)S(1)}, f32[328,128]{1,0:T(8,128)S(1)}, u32[]{:S(2)}, u32[]{:S(2)}) collective-permute-start(f32[328,128]{1,0:T(8,128)S(1)} %up.5.refs_0_), channel_id=1, source_target_pairs={{1,25},{3,27},{5,29},{7,31},{24,0},{26,2},{28,4},{30,6}} | collective-permute-start | bytes 503816 | tf_op jit(solution)/shard_map/ppermute | solution.py:701
  37.3 1.3 %collective-permute-start.6 = (f32[328,128]{1,0:T(8,128)S(1)}, f32[328,128]{1,0:T(8,128)S(1)}, u32[]{:S(2)}, u32[]{:S(2)}) collective-permute-start(f32[328,128]{1,0:T(8,128)S(1)} %up.5.refs_0_), channel_id=1, source_target_pairs={{1,17},{3,19},{5,21},{7,23},{9,25},{11,27},{13,29},{15,31},{16,0},... | collective-permute-start | bytes 503816 | tf_op jit(solution)/shard_map/ppermute | solution.py:701
  38.6 1.3 %collective-permute-start.5 = (f32[328,128]{1,0:T(8,128)S(1)}, f32[328,128]{1,0:T(8,128)S(1)}, u32[]{:S(2)}, u32[]{:S(2)}) collective-permute-start(f32[328,128]{1,0:T(8,128)S(1)} %up.5.refs_0_), channel_id=1, source_target_pairs={{1,9},{3,11},{5,13},{7,15},{8,0},{9,17},{10,2},{11,19},{12,4},{13,... | collective-permute-start | bytes 503816 | tf_op jit(solution)/shard_map/ppermute | solution.py:701
  39.9 2.5 %intra.5 = (f32[256,2560]{1,0:T(8,128)S(1)}, f32[128,2560]{1,0:T(8,128)S(1)}, f32[128,2560]{1,0:T(8,128)S(1)}, f32[256,128]{1,0:T(8,128)S(1)}, f32[256,128]{1,0:T(8,128)S(1)}, /*index=5*/f32[256,128]{1,0:T(8,128)S(1)}) custom-call(f32[328,128]{1,0:T(8,128)S(1)} %up.5.refs_0_, ...), custom_call_target="tpu_custom_call", output_to_operand_aliasing={{0}: (9, {}), {1}: (10, {}), {2}: (11, {})} | custom-call | flops 1 | bytes 1 | tf_op jit(solution)/shard_map/intra/pallas_call | solution.py:441
  42.4 1.9 %collective-permute-done.7.refs_5_ = f32[328,128]{1,0:T(8,128)S(1)} collective-permute-done((f32[328,128]{1,0:T(8,128)S(1)}, f32[328,128]{1,0:T(8,128)S(1)}, u32[]{:S(2)}, u32[]{:S(2)}) %collective-permute-start.7) | collective-permute-done | bytes 167968 | tf_op jit(solution)/shard_map/ppermute | solution.py:701
  44.3 1.7 %collective-permute-done.6.refs_4_ = f32[328,128]{1,0:T(8,128)S(1)} collective-permute-done((f32[328,128]{1,0:T(8,128)S(1)}, f32[328,128]{1,0:T(8,128)S(1)}, u32[]{:S(2)}, u32[]{:S(2)}) %collective-permute-start.6) | collective-permute-done | bytes 167968 | tf_op jit(solution)/shard_map/ppermute | solution.py:701
  46.0 0.3 down.4
  46.3 0.8 collective-permute-start.9
  47.1 0.2 up.7
  47.3 1.3 %collective-permute-start.12 = (f32[328,128]{1,0:T(8,128)S(1)}, f32[328,128]{1,0:T(8,128)S(1)}, u32[]{:S(2)}, u32[]{:S(2)}) collective-permute-start(f32[328,128]{1,0:T(8,128)S(1)} %up.7), channel_id=1, source_target_pairs={{1,25},{3,27},{5,29},{7,31},{24,0},{26,2},{28,4},{30,6}} | collective-permute-start | bytes 503816 | tf_op jit(solution)/shard_map/ppermute | solution.py:701
  48.6 1.3 %collective-permute-start.11 = (f32[328,128]{1,0:T(8,128)S(1)}, f32[328,128]{1,0:T(8,128)S(1)}, u32[]{:S(2)}, u32[]{:S(2)}) collective-permute-start(f32[328,128]{1,0:T(8,128)S(1)} %up.7), channel_id=1, source_target_pairs={{1,17},{3,19},{5,21},{7,23},{9,25},{11,27},{13,29},{15,31},{16,0},... | collective-permute-start | bytes 503816 | tf_op jit(solution)/shard_map/ppermute | solution.py:701
  49.9 1.5 %collective-permute-start.10 = (f32[328,128]{1,0:T(8,128)S(1)}, f32[328,128]{1,0:T(8,128)S(1)}, u32[]{:S(2)}, u32[]{:S(2)}) collective-permute-start(f32[328,128]{1,0:T(8,128)S(1)} %up.7), channel_id=1, source_target_pairs={{1,9},{3,11},{5,13},{7,15},{8,0},{9,17},{10,2},{11,19},{12,4},{13,... | collective-permute-start | bytes 503816 | tf_op jit(solution)/shard_map/ppermute | solution.py:701
  51.4 4.2 %collective-permute-done.12.refs_5_ = f32[328,128]{1,0:T(8,128)S(1)} collective-permute-done((f32[328,128]{1,0:T(8,128)S(1)}, f32[328,128]{1,0:T(8,128)S(1)}, u32[]{:S(2)}, u32[]{:S(2)}) %collective-permute-start.12) | collective-permute-done | bytes 167968 | tf_op jit(solution)/shard_map/ppermute | solution.py:701
  55.5 1.7 %collective-permute-done.11.refs_4_ = f32[328,128]{1,0:T(8,128)S(1)} collective-permute-done((f32[328,128]{1,0:T(8,128)S(1)}, f32[328,128]{1,0:T(8,128)S(1)}, u32[]{:S(2)}, u32[]{:S(2)}) %collective-permute-start.11) | collective-permute-done | bytes 167968 | tf_op jit(solution)/shard_map/ppermute | solution.py:701
  57.2 0.2 down.5
  57.5 2.4 %collective-permute-start.13 = (f32[656,128]{1,0:T(8,128)S(1)}, f32[656,128]{1,0:T(8,128)S(1)}, u32[]{:S(2)}, u32[]{:S(2)}) collective-permute-start(f32[656,128]{1,0:T(8,128)S(1)} %get-tuple-element.170), channel_id=1, source_target_pairs={{0,2},{1,3},{2,0},{3,1},{4,6},{5,7},{6,4},{7,5},{8,10},{9,11},{10,... | collective-permute-start | bytes 1007624 | tf_op jit(solution)/shard_map/ppermute | solution.py:701
  59.9 0.2 down.6
  60.1 2.2 %collective-permute-start.14 = (f32[336,128]{1,0:T(8,128)S(1)}, f32[336,128]{1,0:T(8,128)S(1)}, u32[]{:S(2)}, u32[]{:S(2)}) collective-permute-start(f32[336,128]{1,0:T(8,128)S(1)} %get-tuple-element.174), channel_id=1, source_target_pairs={{0,4},{1,5},{2,6},{3,7},{4,0},{5,1},{6,2},{7,3},{8,12},{9,13},{10,... | collective-permute-start | bytes 516104 | tf_op jit(solution)/shard_map/ppermute | solution.py:701
  62.4 6.6 %collective-permute-done.14.refs_4_ = f32[336,128]{1,0:T(8,128)S(1)} collective-permute-done((f32[336,128]{1,0:T(8,128)S(1)}, f32[336,128]{1,0:T(8,128)S(1)}, u32[]{:S(2)}, u32[]{:S(2)}) %collective-permute-start.14) | collective-permute-done | bytes 172064 | tf_op jit(solution)/shard_map/ppermute | solution.py:701
  68.9 0.4 collective-permute-done.13.got_ref
  69.4 0.2 down.7
  69.6 1.7 %collective-permute-start.17 = (f32[656,128]{1,0:T(8,128)S(1)}, f32[656,128]{1,0:T(8,128)S(1)}, u32[]{:S(2)}, u32[]{:S(2)}) collective-permute-start(f32[656,128]{1,0:T(8,128)S(1)} %get-tuple-element.186), channel_id=1, source_target_pairs={{0,2},{1,3},{2,0},{3,1},{4,6},{5,7},{6,4},{7,5},{8,10},{9,11},{10,... | collective-permute-start | bytes 1007624 | tf_op jit(solution)/shard_map/ppermute | solution.py:701
  71.4 0.1 collective-permute-start.15
  71.4 0.5 collective-permute-start.16
  71.9 0.1 collective-permute-start.18
  72.0 1.0 %collective-permute-done.15.refs_6_ = f32[640,128]{1,0:T(8,128)S(1)} collective-permute-done((f32[640,128]{1,0:T(8,128)S(1)}, f32[640,128]{1,0:T(8,128)S(1)}, u32[]{:S(2)}, u32[]{:S(2)}) %collective-permute-start.15) | collective-permute-done | bytes 327712 | tf_op jit(solution)/shard_map/ppermute | solution.py:701
  73.0 0.5 collective-permute-done.16.refs_7_
  73.5 0.8 assemble.2
  74.3 3.8 %finish.3 = (bf16[256,2560]{1,0:T(8,128)(2,1)}, f32[256,128]{1,0:T(8,128)S(1)}, f32[256,128]{1,0:T(8,128)S(1)}, f32[256,128]{1,0:T(8,128)S(1)}, f32[8,128]{1,0:T(8,128)S(1)}) custom-call(bf16[256,2560]{1,0:T(8,128)(2,1)S(1)} %copy-done, bf16[256,2560]{1,0:T(8,128)(2,1)S(1)} %copy-done.1, bf16[256,128]{1,0:T(8,128)(2,1)S(1)} %copy-done.2, ...), custom_call_target="tpu_custom_call" | custom-call | flops 1 | bytes 1 | tf_op jit(solution)/shard_map/finish/pallas_call | solution.py:611
  78.1 0.1 collective-permute-start.19
  78.2 1.5 %collective-permute-done.19.refs_7_ = f32[656,128]{1,0:T(8,128)S(1)} collective-permute-done((f32[656,128]{1,0:T(8,128)S(1)}, f32[656,128]{1,0:T(8,128)S(1)}, u32[]{:S(2)}, u32[]{:S(2)}) %collective-permute-start.19) | collective-permute-done | bytes 335904 | tf_op jit(solution)/shard_map/ppermute | solution.py:701
  79.7 0.8 assemble.3
  80.5 0.2 collective-permute-start.20
  80.7 1.0 %collective-permute-done.20.got_ref = f32[8,128]{1,0:T(8,128)S(1)} collective-permute-done((f32[8,128]{1,0:T(8,128)S(1)}, f32[8,128]{1,0:T(8,128)S(1)}, u32[]{:S(2)}, u32[]{:S(2)}) %collective-permute-start.20) | collective-permute-done | bytes 4128 | tf_op jit(solution)/shard_map/ppermute | solution.py:701
  81.8 2.8 %collective-permute-start.23 = (f32[8,128]{1,0:T(8,128)S(1)}, f32[8,128]{1,0:T(8,128)S(1)}, u32[]{:S(2)}, u32[]{:S(2)}) collective-permute-start(f32[8,128]{1,0:T(8,128)S(1)} %get-tuple-element.197.refs_13_.total_ref), channel_id=1, source_target_pairs={{0,6},{1,7},{2,4},{3,5},{4,2},{5,3},{6,0},{7,1},{8,14},{9,15},{10,... | collective-permute-start | bytes 12296 | tf_op jit(solution)/shard_map/ppermute | solution.py:701
  84.6 1.6 %collective-permute-start.21 = (f32[8,128]{1,0:T(8,128)S(1)}, f32[8,128]{1,0:T(8,128)S(1)}, u32[]{:S(2)}, u32[]{:S(2)}) collective-permute-start(f32[8,128]{1,0:T(8,128)S(1)} %get-tuple-element.197.refs_13_.total_ref), channel_id=1, source_target_pairs={{0,2},{1,3},{2,0},{3,1},{4,6},{5,7},{6,4},{7,5},{8,10},{9,11},{10,... | collective-permute-start | bytes 12296 | tf_op jit(solution)/shard_map/ppermute | solution.py:701
  86.2 1.5 %finish.4 = (bf16[256,2560]{1,0:T(8,128)(2,1)}, f32[256,128]{1,0:T(8,128)S(1)}, f32[256,128]{1,0:T(8,128)S(1)}, f32[256,128]{1,0:T(8,128)S(1)}, f32[8,128]{1,0:T(8,128)S(1)}) custom-call(bf16[256,2560]{1,0:T(8,128)(2,1)S(1)} %copy-done, bf16[256,2560]{1,0:T(8,128)(2,1)S(1)} %copy-done.1, ...), custom_call_target="tpu_custom_call", output_to_operand_aliasing={{0}: (12, {})} | custom-call | flops 1 | bytes 1 | tf_op jit(solution)/shard_map/finish/pallas_call | solution.py:611
  87.7 1.4 %collective-permute-done.22.refs_1_ = f32[8,128]{1,0:T(8,128)S(1)} collective-permute-done((f32[8,128]{1,0:T(8,128)S(1)}, f32[8,128]{1,0:T(8,128)S(1)}, u32[]{:S(2)}, u32[]{:S(2)}) %collective-permute-start.22) | collective-permute-done | bytes 4128 | tf_op jit(solution)/shard_map/ppermute | solution.py:701
  89.1 1.3 %collective-permute-start.26 = (f32[8,128]{1,0:T(8,128)S(1)}, f32[8,128]{1,0:T(8,128)S(1)}, u32[]{:S(2)}, u32[]{:S(2)}) collective-permute-start(f32[8,128]{1,0:T(8,128)S(1)} %get-tuple-element.204.refs_13_), channel_id=1, source_target_pairs={{24,0},{25,1},{26,2},{27,3},{28,4},{29,5},{30,6},{31,7}} | collective-permute-start | bytes 12296 | tf_op jit(solution)/shard_map/ppermute | solution.py:701
  90.4 1.3 %collective-permute-start.25 = (f32[8,128]{1,0:T(8,128)S(1)}, f32[8,128]{1,0:T(8,128)S(1)}, u32[]{:S(2)}, u32[]{:S(2)}) collective-permute-start(f32[8,128]{1,0:T(8,128)S(1)} %get-tuple-element.204.refs_13_), channel_id=1, source_target_pairs={{16,0},{17,1},{18,2},{19,3},{20,4},{21,5},{22,6},{23,7},{24,8},{25... | collective-permute-start | bytes 12296 | tf_op jit(solution)/shard_map/ppermute | solution.py:701
  91.7 1.3 %collective-permute-start.24 = (f32[8,128]{1,0:T(8,128)S(1)}, f32[8,128]{1,0:T(8,128)S(1)}, u32[]{:S(2)}, u32[]{:S(2)}) collective-permute-start(f32[8,128]{1,0:T(8,128)S(1)} %get-tuple-element.204.refs_13_), channel_id=1, source_target_pairs={{8,0},{9,1},{10,2},{11,3},{12,4},{13,5},{14,6},{15,7},{16,8},{17,9... | collective-permute-start | bytes 12296 | tf_op jit(solution)/shard_map/ppermute | solution.py:701
  93.0 2.0 %finish.5 = (bf16[256,2560]{1,0:T(8,128)(2,1)}, bf16[256,128]{1,0:T(8,128)(2,1)}, bf16[256,128]{1,0:T(8,128)(2,1)}, f32[40,256]{1,0:T(8,128)S(1)}, f32[8,128]{1,0:T(8,128)}) custom-call(bf16[256,2560]{1,0:T(8,128)(2,1)S(1)} %copy-done, bf16[256,2560]{1,0:T(8,128)(2,1)S(1)} %copy-done.1, ...), custom_call_target="tpu_custom_call", output_to_operand_aliasing={{0}: (12, {})} | custom-call | flops 1 | bytes 1 | tf_op jit(solution)/shard_map/finish/pallas_call | solution.py:611
  95.0 0.5 collective-permute-done.26.refs_3_
  95.5 0.4 collective-permute-done.25.refs_2_
  95.9 1.3 %collective-permute-done.24.refs_1_ = f32[8,128]{1,0:T(8,128)S(1)} collective-permute-done((f32[8,128]{1,0:T(8,128)S(1)}, f32[8,128]{1,0:T(8,128)S(1)}, u32[]{:S(2)}, u32[]{:S(2)}) %collective-permute-start.24) | collective-permute-done | bytes 4128 | tf_op jit(solution)/shard_map/ppermute | solution.py:701
  97.2 0.8 add_later.1
  (40 shorter events, 0.2 us)
Async XLA Ops:
  4.4 4.3 %collective-permute-start = (f32[1288,128]{1,0:T(8,128)}, f32[1288,128]{1,0:T(8,128)S(1)}, u32[]{:S(2)}, u32[]{:S(2)}) collective-permute-start(f32[1288,128]{1,0:T(8,128)} %get-tuple-element.109), channel_id=1, source_target_pairs={{0,1},{1,0},{2,3},{3,2},{4,5},{5,4},{6,7},{7,6},{8,9},{9,8},{10,11... | collective-permute-start | bytes 1978376 | tf_op jit(solution)/shard_map/ppermute | solution.py:701
  4.9 3.8 %copy-start.8 = (f32[1280,128]{1,0:T(8,128)S(1)}, f32[1280,128]{1,0:T(8,128)}, u32[]{:S(2)}) copy-start(f32[1280,128]{1,0:T(8,128)} %get-tuple-element.110.refs_1_) | copy-start | bytes 1966084
  4.9 3.8 %copy-start.10 = (f32[8,128]{1,0:T(8,128)S(1)}, f32[8,128]{1,0:T(8,128)}, u32[]{:S(2)}) copy-start(f32[8,128]{1,0:T(8,128)} %get-tuple-element.112.refs_3_.refs_4_) | copy-start | bytes 12292
  4.9 3.8 %copy-start.12 = (f32[10,128]{1,0:T(8,128)S(1)}, f32[10,128]{1,0:T(8,128)}, u32[]{:S(2)}) copy-start(f32[10,128]{1,0:T(8,128)} %get-tuple-element.111.refs_2_) | copy-start | bytes 15364
  4.9 7.0 %copy-start.1 = (bf16[256,2560]{1,0:T(8,128)(2,1)S(1)}, bf16[256,2560]{1,0:T(8,128)(2,1)}, u32[]{:S(2)}) copy-start(bf16[256,2560]{1,0:T(8,128)(2,1)} %refs_1_.15) | copy-start | bytes 3932164
  4.9 7.0 %copy-start.2 = (bf16[256,128]{1,0:T(8,128)(2,1)S(1)}, bf16[256,128]{1,0:T(8,128)(2,1)}, u32[]{:S(2)}) copy-start(bf16[256,128]{1,0:T(8,128)(2,1)} %refs_2_.15) | copy-start | bytes 196612
  4.9 7.0 %copy-start.3 = (bf16[256,128]{1,0:T(8,128)(2,1)S(1)}, bf16[256,128]{1,0:T(8,128)(2,1)}, u32[]{:S(2)}) copy-start(bf16[256,128]{1,0:T(8,128)(2,1)} %refs_3_.15) | copy-start | bytes 196612
  5.0 7.0 %copy-start.4 = (bf16[256,128]{1,0:T(8,128)(2,1)S(1)}, bf16[256,128]{1,0:T(8,128)(2,1)}, u32[]{:S(2)}) copy-start(bf16[256,128]{1,0:T(8,128)(2,1)} %get-tuple-element.107.refs_5_.refs_7_.refs_4_) | copy-start | bytes 196612
  5.0 7.0 %copy-start.5 = (bf16[256,128]{1,0:T(8,128)(2,1)S(1)}, bf16[256,128]{1,0:T(8,128)(2,1)}, u32[]{:S(2)}) copy-start(bf16[256,128]{1,0:T(8,128)(2,1)} %get-tuple-element.108.refs_6_.refs_8_.refs_5_) | copy-start | bytes 196612
  5.0 7.0 %copy-start.6 = (f32[256,128]{1,0:T(8,128)S(1)}, f32[256,128]{1,0:T(8,128)}, u32[]{:S(2)}) copy-start(f32[256,128]{1,0:T(8,128)} %get-tuple-element.116.refs_6_) | copy-start | bytes 393220
  5.0 7.0 %copy-start.9 = (f32[40,256]{1,0:T(8,128)S(1)}, f32[40,256]{1,0:T(8,128)}, u32[]{:S(2)}) copy-start(f32[40,256]{1,0:T(8,128)} %refs_5_.5) | copy-start | bytes 122884
  8.6 3.4 %copy-start = (bf16[256,2560]{1,0:T(8,128)(2,1)S(1)}, bf16[256,2560]{1,0:T(8,128)(2,1)}, u32[]{:S(2)}) copy-start(bf16[256,2560]{1,0:T(8,128)(2,1)} %refs_0_.9) | copy-start | bytes 3932164
  8.6 8.5 %collective-permute-start.2 = (f32[1288,128]{1,0:T(8,128)}, f32[1288,128]{1,0:T(8,128)S(1)}, u32[]{:S(2)}, u32[]{:S(2)}) collective-permute-start(f32[1288,128]{1,0:T(8,128)} %get-tuple-element.115), channel_id=1, source_target_pairs={{0,1},{1,0},{2,3},{3,2},{4,5},{5,4},{6,7},{7,6},{8,9},{9,8},{10,11... | collective-permute-start | bytes 1978376 | tf_op jit(solution)/shard_map/ppermute | solution.py:701
  8.9 11.2 %collective-permute-start.1 = (f32[656,128]{1,0:T(8,128)S(1)}, f32[656,128]{1,0:T(8,128)S(1)}, u32[]{:S(2)}, u32[]{:S(2)}) collective-permute-start(f32[656,128]{1,0:T(8,128)S(1)} %get-tuple-element.114.refs_0_.refs_1_), channel_id=1, source_target_pairs={{0,2},{1,3},{2,0},{3,1},{4,6},{5,7},{6,4},{7,5},{8,10},{9,11},{10,... | collective-permute-start | bytes 1007624 | tf_op jit(solution)/shard_map/ppermute | solution.py:701
  12.0 8.0 %copy-start.7 = (f32[1280,128]{1,0:T(8,128)S(1)}, f32[1280,128]{1,0:T(8,128)}, u32[]{:S(2)}) copy-start(f32[1280,128]{1,0:T(8,128)} %get-tuple-element.126.refs_1_) | copy-start | bytes 1966084
  12.0 8.0 %copy-start.11 = (f32[10,128]{1,0:T(8,128)S(1)}, f32[10,128]{1,0:T(8,128)}, u32[]{:S(2)}) copy-start(f32[10,128]{1,0:T(8,128)} %get-tuple-element.127.refs_2_) | copy-start | bytes 15364
  20.1 13.1 %collective-permute-start.4 = (f32[656,128]{1,0:T(8,128)S(1)}, f32[656,128]{1,0:T(8,128)S(1)}, u32[]{:S(2)}, u32[]{:S(2)}) collective-permute-start(f32[656,128]{1,0:T(8,128)S(1)} %get-tuple-element.128.refs_1_), channel_id=1, source_target_pairs={{0,2},{1,3},{2,0},{3,1},{4,6},{5,7},{6,4},{7,5},{8,10},{9,11},{10,... | collective-permute-start | bytes 1007624 | tf_op jit(solution)/shard_map/ppermute | solution.py:701
  22.2 10.0 %collective-permute-start.3 = (f32[336,128]{1,0:T(8,128)S(1)}, f32[336,128]{1,0:T(8,128)S(1)}, u32[]{:S(2)}, u32[]{:S(2)}) collective-permute-start(f32[336,128]{1,0:T(8,128)S(1)} %get-tuple-element.124.refs_0_.refs_1_), channel_id=1, source_target_pairs={{0,4},{1,5},{2,6},{3,7},{4,0},{5,1},{6,2},{7,3},{8,12},{9,13},{10,... | collective-permute-start | bytes 516104 | tf_op jit(solution)/shard_map/ppermute | solution.py:701
  33.4 12.6 %collective-permute-start.8 = (f32[336,128]{1,0:T(8,128)S(1)}, f32[336,128]{1,0:T(8,128)S(1)}, u32[]{:S(2)}, u32[]{:S(2)}) collective-permute-start(f32[336,128]{1,0:T(8,128)S(1)} %get-tuple-element.142.refs_1_), channel_id=1, source_target_pairs={{0,4},{1,5},{2,6},{3,7},{4,0},{5,1},{6,2},{7,3},{8,12},{9,13},{10,... | collective-permute-start | bytes 516104 | tf_op jit(solution)/shard_map/ppermute | solution.py:701
  36.0 8.3 %collective-permute-start.7 = (f32[328,128]{1,0:T(8,128)S(1)}, f32[328,128]{1,0:T(8,128)S(1)}, u32[]{:S(2)}, u32[]{:S(2)}) collective-permute-start(f32[328,128]{1,0:T(8,128)S(1)} %up.5.refs_0_), channel_id=1, source_target_pairs={{1,25},{3,27},{5,29},{7,31},{24,0},{26,2},{28,4},{30,6}} | collective-permute-start | bytes 503816 | tf_op jit(solution)/shard_map/ppermute | solution.py:701
  37.3 8.7 %collective-permute-start.6 = (f32[328,128]{1,0:T(8,128)S(1)}, f32[328,128]{1,0:T(8,128)S(1)}, u32[]{:S(2)}, u32[]{:S(2)}) collective-permute-start(f32[328,128]{1,0:T(8,128)S(1)} %up.5.refs_0_), channel_id=1, source_target_pairs={{1,17},{3,19},{5,21},{7,23},{9,25},{11,27},{13,29},{15,31},{16,0},... | collective-permute-start | bytes 503816 | tf_op jit(solution)/shard_map/ppermute | solution.py:701
  38.6 7.4 %collective-permute-start.5 = (f32[328,128]{1,0:T(8,128)S(1)}, f32[328,128]{1,0:T(8,128)S(1)}, u32[]{:S(2)}, u32[]{:S(2)}) collective-permute-start(f32[328,128]{1,0:T(8,128)S(1)} %up.5.refs_0_), channel_id=1, source_target_pairs={{1,9},{3,11},{5,13},{7,15},{8,0},{9,17},{10,2},{11,19},{12,4},{13,... | collective-permute-start | bytes 503816 | tf_op jit(solution)/shard_map/ppermute | solution.py:701
  46.3 11.0 %collective-permute-start.9 = (f32[336,128]{1,0:T(8,128)S(1)}, f32[336,128]{1,0:T(8,128)S(1)}, u32[]{:S(2)}, u32[]{:S(2)}) collective-permute-start(f32[336,128]{1,0:T(8,128)S(1)} %get-tuple-element.165), channel_id=1, source_target_pairs={{0,4},{1,5},{2,6},{3,7},{4,0},{5,1},{6,2},{7,3},{8,12},{9,13},{10,... | collective-permute-start | bytes 516104 | tf_op jit(solution)/shard_map/ppermute | solution.py:701
  47.3 8.3 %collective-permute-start.12 = (f32[328,128]{1,0:T(8,128)S(1)}, f32[328,128]{1,0:T(8,128)S(1)}, u32[]{:S(2)}, u32[]{:S(2)}) collective-permute-start(f32[328,128]{1,0:T(8,128)S(1)} %up.7), channel_id=1, source_target_pairs={{1,25},{3,27},{5,29},{7,31},{24,0},{26,2},{28,4},{30,6}} | collective-permute-start | bytes 503816 | tf_op jit(solution)/shard_map/ppermute | solution.py:701
  48.6 8.7 %collective-permute-start.11 = (f32[328,128]{1,0:T(8,128)S(1)}, f32[328,128]{1,0:T(8,128)S(1)}, u32[]{:S(2)}, u32[]{:S(2)}) collective-permute-start(f32[328,128]{1,0:T(8,128)S(1)} %up.7), channel_id=1, source_target_pairs={{1,17},{3,19},{5,21},{7,23},{9,25},{11,27},{13,29},{15,31},{16,0},... | collective-permute-start | bytes 503816 | tf_op jit(solution)/shard_map/ppermute | solution.py:701
  49.9 7.4 %collective-permute-start.10 = (f32[328,128]{1,0:T(8,128)S(1)}, f32[328,128]{1,0:T(8,128)S(1)}, u32[]{:S(2)}, u32[]{:S(2)}) collective-permute-start(f32[328,128]{1,0:T(8,128)S(1)} %up.7), channel_id=1, source_target_pairs={{1,9},{3,11},{5,13},{7,15},{8,0},{9,17},{10,2},{11,19},{12,4},{13,... | collective-permute-start | bytes 503816 | tf_op jit(solution)/shard_map/ppermute | solution.py:701
  57.5 11.8 %collective-permute-start.13 = (f32[656,128]{1,0:T(8,128)S(1)}, f32[656,128]{1,0:T(8,128)S(1)}, u32[]{:S(2)}, u32[]{:S(2)}) collective-permute-start(f32[656,128]{1,0:T(8,128)S(1)} %get-tuple-element.170), channel_id=1, source_target_pairs={{0,2},{1,3},{2,0},{3,1},{4,6},{5,7},{6,4},{7,5},{8,10},{9,11},{10,... | collective-permute-start | bytes 1007624 | tf_op jit(solution)/shard_map/ppermute | solution.py:701
  60.1 8.8 %collective-permute-start.14 = (f32[336,128]{1,0:T(8,128)S(1)}, f32[336,128]{1,0:T(8,128)S(1)}, u32[]{:S(2)}, u32[]{:S(2)}) collective-permute-start(f32[336,128]{1,0:T(8,128)S(1)} %get-tuple-element.174), channel_id=1, source_target_pairs={{0,4},{1,5},{2,6},{3,7},{4,0},{5,1},{6,2},{7,3},{8,12},{9,13},{10,... | collective-permute-start | bytes 516104 | tf_op jit(solution)/shard_map/ppermute | solution.py:701
  69.6 8.5 %collective-permute-start.17 = (f32[656,128]{1,0:T(8,128)S(1)}, f32[656,128]{1,0:T(8,128)S(1)}, u32[]{:S(2)}, u32[]{:S(2)}) collective-permute-start(f32[656,128]{1,0:T(8,128)S(1)} %get-tuple-element.186), channel_id=1, source_target_pairs={{0,2},{1,3},{2,0},{3,1},{4,6},{5,7},{6,4},{7,5},{8,10},{9,11},{10,... | collective-permute-start | bytes 1007624 | tf_op jit(solution)/shard_map/ppermute | solution.py:701
  71.4 1.7 %collective-permute-start.15 = (f32[640,128]{1,0:T(8,128)S(1)}, f32[640,128]{1,0:T(8,128)S(1)}, u32[]{:S(2)}, u32[]{:S(2)}) collective-permute-start(f32[640,128]{1,0:T(8,128)S(1)} %get-tuple-element.176.refs_4_), channel_id=1, source_target_pairs={{0,1},{1,0},{2,3},{3,2},{4,5},{5,4},{6,7},{7,6},{8,9},{9,8},{10,11... | collective-permute-start | bytes 983048 | tf_op jit(solution)/shard_map/ppermute | solution.py:701
  71.4 2.1 %collective-permute-start.16 = (f32[640,128]{1,0:T(8,128)S(1)}, f32[640,128]{1,0:T(8,128)S(1)}, u32[]{:S(2)}, u32[]{:S(2)}) collective-permute-start(f32[640,128]{1,0:T(8,128)S(1)} %get-tuple-element.177.refs_5_), channel_id=1, source_target_pairs={{0,1},{1,0},{2,3},{3,2},{4,5},{5,4},{6,7},{7,6},{8,9},{9,8},{10,11... | collective-permute-start | bytes 983048 | tf_op jit(solution)/shard_map/ppermute | solution.py:701
  71.9 6.1 %collective-permute-start.18 = (f32[640,128]{1,0:T(8,128)S(1)}, f32[640,128]{1,0:T(8,128)S(1)}, u32[]{:S(2)}, u32[]{:S(2)}) collective-permute-start(f32[640,128]{1,0:T(8,128)S(1)} %get-tuple-element.187.refs_4_), channel_id=1, source_target_pairs={{0,1},{1,0},{2,3},{3,2},{4,5},{5,4},{6,7},{7,6},{8,9},{9,8},{10,11... | collective-permute-start | bytes 983048 | tf_op jit(solution)/shard_map/ppermute | solution.py:701
  78.1 1.6 %collective-permute-start.19 = (f32[656,128]{1,0:T(8,128)S(1)}, f32[656,128]{1,0:T(8,128)S(1)}, u32[]{:S(2)}, u32[]{:S(2)}) collective-permute-start(f32[656,128]{1,0:T(8,128)S(1)} %collective-permute-done.17.refs_5_), channel_id=1, source_target_pairs={{0,1},{1,0},{2,3},{3,2},{4,5},{5,4},{6,7},{7,6},{8,9},{9,8},{10,11... | collective-permute-start | bytes 1007624 | tf_op jit(solution)/shard_map/ppermute | solution.py:701
  80.5 1.2 %collective-permute-start.20 = (f32[8,128]{1,0:T(8,128)S(1)}, f32[8,128]{1,0:T(8,128)S(1)}, u32[]{:S(2)}, u32[]{:S(2)}) collective-permute-start(f32[8,128]{1,0:T(8,128)S(1)} %get-tuple-element.196.total_ref), channel_id=1, source_target_pairs={{0,1},{1,0},{2,3},{3,2},{4,5},{5,4},{6,7},{7,6},{8,9},{9,8},{10,11... | collective-permute-start | bytes 12296 | tf_op jit(solution)/shard_map/ppermute | solution.py:701
  81.8 5.9 %collective-permute-start.23 = (f32[8,128]{1,0:T(8,128)S(1)}, f32[8,128]{1,0:T(8,128)S(1)}, u32[]{:S(2)}, u32[]{:S(2)}) collective-permute-start(f32[8,128]{1,0:T(8,128)S(1)} %get-tuple-element.197.refs_13_.total_ref), channel_id=1, source_target_pairs={{0,6},{1,7},{2,4},{3,5},{4,2},{5,3},{6,0},{7,1},{8,14},{9,15},{10,... | collective-permute-start | bytes 12296 | tf_op jit(solution)/shard_map/ppermute | solution.py:701
  84.6 4.5 %collective-permute-start.22 = (f32[8,128]{1,0:T(8,128)S(1)}, f32[8,128]{1,0:T(8,128)S(1)}, u32[]{:S(2)}, u32[]{:S(2)}) collective-permute-start(f32[8,128]{1,0:T(8,128)S(1)} %get-tuple-element.197.refs_13_.total_ref), channel_id=1, source_target_pairs={{0,4},{1,5},{2,6},{3,7},{4,0},{5,1},{6,2},{7,3},{8,12},{9,13},{10,... | collective-permute-start | bytes 12296 | tf_op jit(solution)/shard_map/ppermute | solution.py:701
  84.6 4.5 %collective-permute-start.21 = (f32[8,128]{1,0:T(8,128)S(1)}, f32[8,128]{1,0:T(8,128)S(1)}, u32[]{:S(2)}, u32[]{:S(2)}) collective-permute-start(f32[8,128]{1,0:T(8,128)S(1)} %get-tuple-element.197.refs_13_.total_ref), channel_id=1, source_target_pairs={{0,2},{1,3},{2,0},{3,1},{4,6},{5,7},{6,4},{7,5},{8,10},{9,11},{10,... | collective-permute-start | bytes 12296 | tf_op jit(solution)/shard_map/ppermute | solution.py:701
  89.1 6.4 %collective-permute-start.26 = (f32[8,128]{1,0:T(8,128)S(1)}, f32[8,128]{1,0:T(8,128)S(1)}, u32[]{:S(2)}, u32[]{:S(2)}) collective-permute-start(f32[8,128]{1,0:T(8,128)S(1)} %get-tuple-element.204.refs_13_), channel_id=1, source_target_pairs={{24,0},{25,1},{26,2},{27,3},{28,4},{29,5},{30,6},{31,7}} | collective-permute-start | bytes 12296 | tf_op jit(solution)/shard_map/ppermute | solution.py:701
  90.4 5.5 %collective-permute-start.25 = (f32[8,128]{1,0:T(8,128)S(1)}, f32[8,128]{1,0:T(8,128)S(1)}, u32[]{:S(2)}, u32[]{:S(2)}) collective-permute-start(f32[8,128]{1,0:T(8,128)S(1)} %get-tuple-element.204.refs_13_), channel_id=1, source_target_pairs={{16,0},{17,1},{18,2},{19,3},{20,4},{21,5},{22,6},{23,7},{24,8},{25... | collective-permute-start | bytes 12296 | tf_op jit(solution)/shard_map/ppermute | solution.py:701
  91.7 5.5 %collective-permute-start.24 = (f32[8,128]{1,0:T(8,128)S(1)}, f32[8,128]{1,0:T(8,128)S(1)}, u32[]{:S(2)}, u32[]{:S(2)}) collective-permute-start(f32[8,128]{1,0:T(8,128)S(1)} %get-tuple-element.204.refs_13_), channel_id=1, source_target_pairs={{8,0},{9,1},{10,2},{11,3},{12,4},{13,5},{14,6},{15,7},{16,8},{17,9... | collective-permute-start | bytes 12296 | tf_op jit(solution)/shard_map/ppermute | solution.py:701

commit v14 on v13

--- a/solution.py
+++ b/solution.py
@@ -773,7 +773,7 @@
             waiting[0], waiting[1], first[1], block = lax.optimization_barrier(
                 (waiting[0], waiting[1], first[1], block)
             )
-        elif step < rounds - 1:
+        elif levels + 1 < step < rounds - 1:
             waiting[0], waiting[1] = lax.optimization_barrier((waiting[0], waiting[1]))
     dx, state_own, back_own, change, db, dc = block
     own_b = held[1][0]

time: 98.3 us -> 95.3 us (0.969)
  starting transfers between devices: 34.9 us -> 33 us
  waiting for transfers between devices: 30.5 us -> 29.4 us
    ppermute x27, starting transfers between devices: 34.9 us -> 33 us  [move(): return lax.ppermute(value, ('grp', 'seq'), pairs)]
    ppermute x27, waiting for transfers between devices: 30.5 us -> 29.4 us  [move(): return lax.ppermute(value, ('grp', 'seq'), pairs)]
  transfers between devices with their start and end apart: 27 -> 27, of which waited for: 17 -> 18; matrix products, arithmetic and copies ran while one was open for 0% -> 0% of each run, Pallas kernels for 26% -> 27%
where the time goes in v14:
time: 95.3 us; the launch traced here: 95 us
  starting transfers between devices  33 us (35%)
  Pallas kernels  31.6 us (33%)
  waiting for transfers between devices  29.4 us (31%)
  between operations  0.96 us (1%)
    ppermute x27, starting transfers between devices, move(): return lax.ppermute(value, ('grp', 'seq'), pairs)  33 us
    ppermute x27, waiting for transfers between devices, move(): return lax.ppermute(value, ('grp', 'seq'), pairs)  29.4 us
    pallas_call x3, Pallas kernels, intra(): pl.pallas_call(lambda *refs: intra_kernel(heads, wide // heads, start, la...  12.5 us
    pallas_call x2, Pallas kernels, summary(): pl.pallas_call(lambda *refs: summary_kernel(heads, chips, half, *refs), g...  7.38 us
    pallas_call x3, Pallas kernels, finish(): pl.pallas_call(lambda *refs: finish_kernel(heads, start, steps, last, *re...  7.27 us
  transfers between devices with their start and end apart: 27, of which 18 were waited for; matrix products, arithmetic and copies ran while one was open for 0% of the time, Pallas kernels for 27%

profile of v14, /device:TPU:0, one launch (start us, length us, event | category | flops | bytes accessed | tf_op | source)
XLA Modules:
  0.0 95.0 jit_solution(11522296624287856024)
XLA Ops:
  0.6 3.8 %summary.2 = (f32[1288,128]{1,0:T(8,128)}, f32[1280,128]{1,0:T(8,128)}, f32[10,128]{1,0:T(8,128)}, f32[8,128]{1,0:T(8,128)}, f32[256,128]{1,0:T(8,128)}, /*index...) custom-call(bf16[256,2560]{1,0:T(8,128)(2,1)} %refs_0_.9, bf16[256,2560]{1,0:T(8,128)(2,1)} %refs_1_.15, ...), custom_call_target="tpu_custom_call" | custom-call | flops 1 | bytes 1 | tf_op jit(solution)/shard_map/summary/pallas_call | solution.py:195
  4.4 0.5 collective-permute-start
  5.0 3.6 %summary.3 = (f32[1288,128]{1,0:T(8,128)}, f32[1280,128]{1,0:T(8,128)}, f32[10,128]{1,0:T(8,128)}) custom-call(bf16[256,2560]{1,0:T(8,128)(2,1)} %refs_0_.9, bf16[256,2560]{1,0:T(8,128)(2,1)} %refs_1_.15, bf16[256,128]{1,0:T(8,128)(2,1)} %refs_2_.15, bf16[256,128]{1,0:T(8,128)(2,1)} %refs_3_.15, f32[8,128]{1,0:T(8,128)} %get-tuple-element.108.refs_3_.refs_4_, ...), custom_call_target="tpu_custom_call" | custom-call | flops 1 | bytes 1 | tf_op jit(solution)/shard_map/summary/pallas_call | solution.py:195
  8.6 0.1 collective-permute-start.2
  8.8 0.1 combine.2
  8.9 3.1 %collective-permute-start.1 = (f32[656,128]{1,0:T(8,128)S(1)}, f32[656,128]{1,0:T(8,128)S(1)}, u32[]{:S(2)}, u32[]{:S(2)}) collective-permute-start(f32[656,128]{1,0:T(8,128)S(1)} %get-tuple-element.110.refs_0_.refs_1_), channel_id=1, source_target_pairs={{0,2},{1,3},{2,0},{3,1},{4,6},{5,7},{6,4},{7,5},{8,10},{9,11},{10,... | collective-permute-start | bytes 1007624 | tf_op jit(solution)/shard_map/ppermute | solution.py:701
  12.0 5.1 %intra.3 = (f32[256,2560]{1,0:T(8,128)S(1)}, f32[128,2560]{1,0:T(8,128)S(1)}, f32[128,2560]{1,0:T(8,128)S(1)}, f32[256,128]{1,0:T(8,128)S(1)}, f32[256,256]{1,0:T(8,128)S(1)}) custom-call(f32[656,128]{1,0:T(8,128)S(1)} %get-tuple-element.110.refs_0_.refs_1_, bf16[256,2560]{1,0:T(8,128)(2,1)S(1)} %copy-done, bf16[256,2560]{1,0:T(8,128)(2,1)S(1)} %copy-done.1, ...), custom_call_target="tpu_custom_call" | custom-call | flops 1 | bytes 1 | tf_op jit(solution)/shard_map/intra/pallas_call | solution.py:441
  17.1 2.9 %collective-permute-done.1.refs_2_ = f32[656,128]{1,0:T(8,128)S(1)} collective-permute-done((f32[656,128]{1,0:T(8,128)S(1)}, f32[656,128]{1,0:T(8,128)S(1)}, u32[]{:S(2)}, u32[]{:S(2)}) %collective-permute-start.1) | collective-permute-done | bytes 335904 | tf_op jit(solution)/shard_map/ppermute | solution.py:701
  20.1 1.8 %collective-permute-start.4 = (f32[656,128]{1,0:T(8,128)S(1)}, f32[656,128]{1,0:T(8,128)S(1)}, u32[]{:S(2)}, u32[]{:S(2)}) collective-permute-start(f32[656,128]{1,0:T(8,128)S(1)} %get-tuple-element.124.refs_1_), channel_id=1, source_target_pairs={{0,2},{1,3},{2,0},{3,1},{4,6},{5,7},{6,4},{7,5},{8,10},{9,11},{10,... | collective-permute-start | bytes 1007624 | tf_op jit(solution)/shard_map/ppermute | solution.py:701
  22.0 0.2 up.4
  22.2 2.7 %collective-permute-start.3 = (f32[336,128]{1,0:T(8,128)S(1)}, f32[336,128]{1,0:T(8,128)S(1)}, u32[]{:S(2)}, u32[]{:S(2)}) collective-permute-start(f32[336,128]{1,0:T(8,128)S(1)} %get-tuple-element.120.refs_0_.refs_1_), channel_id=1, source_target_pairs={{0,4},{1,5},{2,6},{3,7},{4,0},{5,1},{6,2},{7,3},{8,12},{9,13},{10,... | collective-permute-start | bytes 516104 | tf_op jit(solution)/shard_map/ppermute | solution.py:701
  24.8 5.0 %intra.4 = (f32[256,2560]{1,0:T(8,128)S(1)}, f32[128,2560]{1,0:T(8,128)S(1)}, f32[128,2560]{1,0:T(8,128)S(1)}, f32[256,128]{1,0:T(8,128)S(1)}, f32[256,256]{1,0:T(8,128)S(1)}) custom-call(f32[336,128]{1,0:T(8,128)S(1)} %get-tuple-element.120.refs_0_.refs_1_, ...), custom_call_target="tpu_custom_call", output_to_operand_aliasing={{0}: (9, {}), {1}: (10, {}), {2}: (11, {})} | custom-call | flops 1 | bytes 1 | tf_op jit(solution)/shard_map/intra/pallas_call | solution.py:441
  29.8 2.3 %collective-permute-done.3.refs_2_ = f32[336,128]{1,0:T(8,128)S(1)} collective-permute-done((f32[336,128]{1,0:T(8,128)S(1)}, f32[336,128]{1,0:T(8,128)S(1)}, u32[]{:S(2)}, u32[]{:S(2)}) %collective-permute-start.3) | collective-permute-done | bytes 172064 | tf_op jit(solution)/shard_map/ppermute | solution.py:701
  32.1 1.1 %collective-permute-done.4.refs_2_ = f32[656,128]{1,0:T(8,128)S(1)} collective-permute-done((f32[656,128]{1,0:T(8,128)S(1)}, f32[656,128]{1,0:T(8,128)S(1)}, u32[]{:S(2)}, u32[]{:S(2)}) %collective-permute-start.4) | collective-permute-done | bytes 335904 | tf_op jit(solution)/shard_map/ppermute | solution.py:701
  33.2 0.2 up.6
  33.4 2.4 %collective-permute-start.8 = (f32[336,128]{1,0:T(8,128)S(1)}, f32[336,128]{1,0:T(8,128)S(1)}, u32[]{:S(2)}, u32[]{:S(2)}) collective-permute-start(f32[336,128]{1,0:T(8,128)S(1)} %get-tuple-element.138.refs_1_), channel_id=1, source_target_pairs={{0,4},{1,5},{2,6},{3,7},{4,0},{5,1},{6,2},{7,3},{8,12},{9,13},{10,... | collective-permute-start | bytes 516104 | tf_op jit(solution)/shard_map/ppermute | solution.py:701
  35.8 0.2 up.5.refs_0_
  36.0 1.3 %collective-permute-start.7 = (f32[328,128]{1,0:T(8,128)S(1)}, f32[328,128]{1,0:T(8,128)S(1)}, u32[]{:S(2)}, u32[]{:S(2)}) collective-permute-start(f32[328,128]{1,0:T(8,128)S(1)} %up.5.refs_0_), channel_id=1, source_target_pairs={{1,25},{3,27},{5,29},{7,31},{24,0},{26,2},{28,4},{30,6}} | collective-permute-start | bytes 503816 | tf_op jit(solution)/shard_map/ppermute | solution.py:701
  37.3 1.3 %collective-permute-start.6 = (f32[328,128]{1,0:T(8,128)S(1)}, f32[328,128]{1,0:T(8,128)S(1)}, u32[]{:S(2)}, u32[]{:S(2)}) collective-permute-start(f32[328,128]{1,0:T(8,128)S(1)} %up.5.refs_0_), channel_id=1, source_target_pairs={{1,17},{3,19},{5,21},{7,23},{9,25},{11,27},{13,29},{15,31},{16,0},... | collective-permute-start | bytes 503816 | tf_op jit(solution)/shard_map/ppermute | solution.py:701
  38.6 1.3 %collective-permute-start.5 = (f32[328,128]{1,0:T(8,128)S(1)}, f32[328,128]{1,0:T(8,128)S(1)}, u32[]{:S(2)}, u32[]{:S(2)}) collective-permute-start(f32[328,128]{1,0:T(8,128)S(1)} %up.5.refs_0_), channel_id=1, source_target_pairs={{1,9},{3,11},{5,13},{7,15},{8,0},{9,17},{10,2},{11,19},{12,4},{13,... | collective-permute-start | bytes 503816 | tf_op jit(solution)/shard_map/ppermute | solution.py:701
  39.9 2.5 %intra.5 = (f32[256,2560]{1,0:T(8,128)S(1)}, f32[128,2560]{1,0:T(8,128)S(1)}, f32[128,2560]{1,0:T(8,128)S(1)}, f32[256,128]{1,0:T(8,128)S(1)}, f32[256,128]{1,0:T(8,128)S(1)}, /*index=5*/f32[256,128]{1,0:T(8,128)S(1)}) custom-call(f32[328,128]{1,0:T(8,128)S(1)} %up.5.refs_0_, ...), custom_call_target="tpu_custom_call", output_to_operand_aliasing={{0}: (9, {}), {1}: (10, {}), {2}: (11, {})} | custom-call | flops 1 | bytes 1 | tf_op jit(solution)/shard_map/intra/pallas_call | solution.py:441
  42.4 1.9 %collective-permute-done.7.refs_5_ = f32[328,128]{1,0:T(8,128)S(1)} collective-permute-done((f32[328,128]{1,0:T(8,128)S(1)}, f32[328,128]{1,0:T(8,128)S(1)}, u32[]{:S(2)}, u32[]{:S(2)}) %collective-permute-start.7) | collective-permute-done | bytes 167968 | tf_op jit(solution)/shard_map/ppermute | solution.py:701
  44.3 1.7 %collective-permute-done.6.refs_4_ = f32[328,128]{1,0:T(8,128)S(1)} collective-permute-done((f32[328,128]{1,0:T(8,128)S(1)}, f32[328,128]{1,0:T(8,128)S(1)}, u32[]{:S(2)}, u32[]{:S(2)}) %collective-permute-start.6) | collective-permute-done | bytes 167968 | tf_op jit(solution)/shard_map/ppermute | solution.py:701
  46.0 0.3 down.4
  46.3 0.8 collective-permute-start.9
  47.1 0.2 up.7
  47.3 1.3 %collective-permute-start.13 = (f32[328,128]{1,0:T(8,128)S(1)}, f32[328,128]{1,0:T(8,128)S(1)}, u32[]{:S(2)}, u32[]{:S(2)}) collective-permute-start(f32[328,128]{1,0:T(8,128)S(1)} %up.7), channel_id=1, source_target_pairs={{1,25},{3,27},{5,29},{7,31},{24,0},{26,2},{28,4},{30,6}} | collective-permute-start | bytes 503816 | tf_op jit(solution)/shard_map/ppermute | solution.py:701
  48.6 1.3 %collective-permute-start.12 = (f32[328,128]{1,0:T(8,128)S(1)}, f32[328,128]{1,0:T(8,128)S(1)}, u32[]{:S(2)}, u32[]{:S(2)}) collective-permute-start(f32[328,128]{1,0:T(8,128)S(1)} %up.7), channel_id=1, source_target_pairs={{1,17},{3,19},{5,21},{7,23},{9,25},{11,27},{13,29},{15,31},{16,0},... | collective-permute-start | bytes 503816 | tf_op jit(solution)/shard_map/ppermute | solution.py:701
  49.9 1.5 %collective-permute-start.11 = (f32[328,128]{1,0:T(8,128)S(1)}, f32[328,128]{1,0:T(8,128)S(1)}, u32[]{:S(2)}, u32[]{:S(2)}) collective-permute-start(f32[328,128]{1,0:T(8,128)S(1)} %up.7), channel_id=1, source_target_pairs={{1,9},{3,11},{5,13},{7,15},{8,0},{9,17},{10,2},{11,19},{12,4},{13,... | collective-permute-start | bytes 503816 | tf_op jit(solution)/shard_map/ppermute | solution.py:701
  51.4 3.6 %collective-permute-done.9.refs_4_ = f32[336,128]{1,0:T(8,128)S(1)} collective-permute-done((f32[336,128]{1,0:T(8,128)S(1)}, f32[336,128]{1,0:T(8,128)S(1)}, u32[]{:S(2)}, u32[]{:S(2)}) %collective-permute-start.9) | collective-permute-done | bytes 172064 | tf_op jit(solution)/shard_map/ppermute | solution.py:701
  55.0 0.2 down.5
  55.3 0.1 collective-permute-start.10
  55.4 0.2 collective-permute-done.13.refs_5_
  55.5 1.7 %collective-permute-done.12.refs_4_ = f32[328,128]{1,0:T(8,128)S(1)} collective-permute-done((f32[328,128]{1,0:T(8,128)S(1)}, f32[328,128]{1,0:T(8,128)S(1)}, u32[]{:S(2)}, u32[]{:S(2)}) %collective-permute-start.12) | collective-permute-done | bytes 167968 | tf_op jit(solution)/shard_map/ppermute | solution.py:701
  57.2 0.3 down.6
  57.5 2.2 %collective-permute-start.14 = (f32[336,128]{1,0:T(8,128)S(1)}, f32[336,128]{1,0:T(8,128)S(1)}, u32[]{:S(2)}, u32[]{:S(2)}) collective-permute-start(f32[336,128]{1,0:T(8,128)S(1)} %get-tuple-element.166), channel_id=1, source_target_pairs={{0,4},{1,5},{2,6},{3,7},{4,0},{5,1},{6,2},{7,3},{8,12},{9,13},{10,... | collective-permute-start | bytes 516104 | tf_op jit(solution)/shard_map/ppermute | solution.py:701
  59.7 5.9 %collective-permute-done.14.refs_4_ = f32[336,128]{1,0:T(8,128)S(1)} collective-permute-done((f32[336,128]{1,0:T(8,128)S(1)}, f32[336,128]{1,0:T(8,128)S(1)}, u32[]{:S(2)}, u32[]{:S(2)}) %collective-permute-start.14) | collective-permute-done | bytes 172064 | tf_op jit(solution)/shard_map/ppermute | solution.py:701
  65.6 0.3 collective-permute-done.10.got_ref
  65.9 0.2 down.7
  66.2 2.1 %collective-permute-start.17 = (f32[656,128]{1,0:T(8,128)S(1)}, f32[656,128]{1,0:T(8,128)S(1)}, u32[]{:S(2)}, u32[]{:S(2)}) collective-permute-start(f32[656,128]{1,0:T(8,128)S(1)} %get-tuple-element.178), channel_id=1, source_target_pairs={{0,2},{1,3},{2,0},{3,1},{4,6},{5,7},{6,4},{7,5},{8,10},{9,11},{10,... | collective-permute-start | bytes 1007624 | tf_op jit(solution)/shard_map/ppermute | solution.py:701
  68.4 0.5 collective-permute-start.16
  68.9 0.1 collective-permute-start.18
  69.0 1.0 %collective-permute-done.15.refs_6_ = f32[640,128]{1,0:T(8,128)S(1)} collective-permute-done((f32[640,128]{1,0:T(8,128)S(1)}, f32[640,128]{1,0:T(8,128)S(1)}, u32[]{:S(2)}, u32[]{:S(2)}) %collective-permute-start.15) | collective-permute-done | bytes 327712 | tf_op jit(solution)/shard_map/ppermute | solution.py:701
  70.0 0.5 collective-permute-done.16.refs_7_
  70.5 0.8 assemble.2
  71.3 3.8 %finish.3 = (bf16[256,2560]{1,0:T(8,128)(2,1)}, f32[256,128]{1,0:T(8,128)S(1)}, f32[256,128]{1,0:T(8,128)S(1)}, f32[256,128]{1,0:T(8,128)S(1)}, f32[8,128]{1,0:T(8,128)S(1)}) custom-call(bf16[256,2560]{1,0:T(8,128)(2,1)S(1)} %copy-done, bf16[256,2560]{1,0:T(8,128)(2,1)S(1)} %copy-done.1, bf16[256,128]{1,0:T(8,128)(2,1)S(1)} %copy-done.2, ...), custom_call_target="tpu_custom_call" | custom-call | flops 1 | bytes 1 | tf_op jit(solution)/shard_map/finish/pallas_call | solution.py:611
  75.0 0.1 collective-permute-start.19
  75.2 1.5 %collective-permute-done.19.refs_7_ = f32[656,128]{1,0:T(8,128)S(1)} collective-permute-done((f32[656,128]{1,0:T(8,128)S(1)}, f32[656,128]{1,0:T(8,128)S(1)}, u32[]{:S(2)}, u32[]{:S(2)}) %collective-permute-start.19) | collective-permute-done | bytes 335904 | tf_op jit(solution)/shard_map/ppermute | solution.py:701
  76.7 0.8 assemble.3
  77.5 0.2 collective-permute-start.20
  77.7 1.0 %collective-permute-done.20.got_ref = f32[8,128]{1,0:T(8,128)S(1)} collective-permute-done((f32[8,128]{1,0:T(8,128)S(1)}, f32[8,128]{1,0:T(8,128)S(1)}, u32[]{:S(2)}, u32[]{:S(2)}) %collective-permute-start.20) | collective-permute-done | bytes 4128 | tf_op jit(solution)/shard_map/ppermute | solution.py:701
  78.8 2.8 %collective-permute-start.23 = (f32[8,128]{1,0:T(8,128)S(1)}, f32[8,128]{1,0:T(8,128)S(1)}, u32[]{:S(2)}, u32[]{:S(2)}) collective-permute-start(f32[8,128]{1,0:T(8,128)S(1)} %get-tuple-element.189.refs_13_.total_ref), channel_id=1, source_target_pairs={{0,6},{1,7},{2,4},{3,5},{4,2},{5,3},{6,0},{7,1},{8,14},{9,15},{10,... | collective-permute-start | bytes 12296 | tf_op jit(solution)/shard_map/ppermute | solution.py:701
  81.6 0.3 collective-permute-start.22
  81.9 1.3 %collective-permute-start.21 = (f32[8,128]{1,0:T(8,128)S(1)}, f32[8,128]{1,0:T(8,128)S(1)}, u32[]{:S(2)}, u32[]{:S(2)}) collective-permute-start(f32[8,128]{1,0:T(8,128)S(1)} %get-tuple-element.189.refs_13_.total_ref), channel_id=1, source_target_pairs={{0,2},{1,3},{2,0},{3,1},{4,6},{5,7},{6,4},{7,5},{8,10},{9,11},{10,... | collective-permute-start | bytes 12296 | tf_op jit(solution)/shard_map/ppermute | solution.py:701
  83.1 1.5 %finish.4 = (bf16[256,2560]{1,0:T(8,128)(2,1)}, f32[256,128]{1,0:T(8,128)S(1)}, f32[256,128]{1,0:T(8,128)S(1)}, f32[256,128]{1,0:T(8,128)S(1)}, f32[8,128]{1,0:T(8,128)S(1)}) custom-call(bf16[256,2560]{1,0:T(8,128)(2,1)S(1)} %copy-done, bf16[256,2560]{1,0:T(8,128)(2,1)S(1)} %copy-done.1, ...), custom_call_target="tpu_custom_call", output_to_operand_aliasing={{0}: (12, {})} | custom-call | flops 1 | bytes 1 | tf_op jit(solution)/shard_map/finish/pallas_call | solution.py:611
  84.7 1.4 %collective-permute-done.22.refs_1_ = f32[8,128]{1,0:T(8,128)S(1)} collective-permute-done((f32[8,128]{1,0:T(8,128)S(1)}, f32[8,128]{1,0:T(8,128)S(1)}, u32[]{:S(2)}, u32[]{:S(2)}) %collective-permute-start.22) | collective-permute-done | bytes 4128 | tf_op jit(solution)/shard_map/ppermute | solution.py:701
  86.1 1.3 %collective-permute-start.26 = (f32[8,128]{1,0:T(8,128)S(1)}, f32[8,128]{1,0:T(8,128)S(1)}, u32[]{:S(2)}, u32[]{:S(2)}) collective-permute-start(f32[8,128]{1,0:T(8,128)S(1)} %get-tuple-element.196.refs_13_), channel_id=1, source_target_pairs={{24,0},{25,1},{26,2},{27,3},{28,4},{29,5},{30,6},{31,7}} | collective-permute-start | bytes 12296 | tf_op jit(solution)/shard_map/ppermute | solution.py:701
  87.4 1.3 %collective-permute-start.25 = (f32[8,128]{1,0:T(8,128)S(1)}, f32[8,128]{1,0:T(8,128)S(1)}, u32[]{:S(2)}, u32[]{:S(2)}) collective-permute-start(f32[8,128]{1,0:T(8,128)S(1)} %get-tuple-element.196.refs_13_), channel_id=1, source_target_pairs={{16,0},{17,1},{18,2},{19,3},{20,4},{21,5},{22,6},{23,7},{24,8},{25... | collective-permute-start | bytes 12296 | tf_op jit(solution)/shard_map/ppermute | solution.py:701
  88.7 1.3 %collective-permute-start.24 = (f32[8,128]{1,0:T(8,128)S(1)}, f32[8,128]{1,0:T(8,128)S(1)}, u32[]{:S(2)}, u32[]{:S(2)}) collective-permute-start(f32[8,128]{1,0:T(8,128)S(1)} %get-tuple-element.196.refs_13_), channel_id=1, source_target_pairs={{8,0},{9,1},{10,2},{11,3},{12,4},{13,5},{14,6},{15,7},{16,8},{17,9... | collective-permute-start | bytes 12296 | tf_op jit(solution)/shard_map/ppermute | solution.py:701
  90.0 2.0 %finish.5 = (bf16[256,2560]{1,0:T(8,128)(2,1)}, bf16[256,128]{1,0:T(8,128)(2,1)}, bf16[256,128]{1,0:T(8,128)(2,1)}, f32[40,256]{1,0:T(8,128)S(1)}, f32[8,128]{1,0:T(8,128)}) custom-call(bf16[256,2560]{1,0:T(8,128)(2,1)S(1)} %copy-done, bf16[256,2560]{1,0:T(8,128)(2,1)S(1)} %copy-done.1, ...), custom_call_target="tpu_custom_call", output_to_operand_aliasing={{0}: (12, {})} | custom-call | flops 1 | bytes 1 | tf_op jit(solution)/shard_map/finish/pallas_call | solution.py:611
  92.0 0.5 collective-permute-done.26.refs_3_
  92.5 0.4 collective-permute-done.25.refs_2_
  92.9 1.3 %collective-permute-done.24.refs_1_ = f32[8,128]{1,0:T(8,128)S(1)} collective-permute-done((f32[8,128]{1,0:T(8,128)S(1)}, f32[8,128]{1,0:T(8,128)S(1)}, u32[]{:S(2)}, u32[]{:S(2)}) %collective-permute-start.24) | collective-permute-done | bytes 4128 | tf_op jit(solution)/shard_map/ppermute | solution.py:701
  94.2 0.8 add_later.1
  (40 shorter events, 0.3 us)
Async XLA Ops:
  4.4 4.3 %collective-permute-start = (f32[1288,128]{1,0:T(8,128)}, f32[1288,128]{1,0:T(8,128)S(1)}, u32[]{:S(2)}, u32[]{:S(2)}) collective-permute-start(f32[1288,128]{1,0:T(8,128)} %get-tuple-element.105), channel_id=1, source_target_pairs={{0,1},{1,0},{2,3},{3,2},{4,5},{5,4},{6,7},{7,6},{8,9},{9,8},{10,11... | collective-permute-start | bytes 1978376 | tf_op jit(solution)/shard_map/ppermute | solution.py:701
  4.9 3.8 %copy-start.8 = (f32[1280,128]{1,0:T(8,128)S(1)}, f32[1280,128]{1,0:T(8,128)}, u32[]{:S(2)}) copy-start(f32[1280,128]{1,0:T(8,128)} %get-tuple-element.106.refs_1_) | copy-start | bytes 1966084
  4.9 3.8 %copy-start.10 = (f32[8,128]{1,0:T(8,128)S(1)}, f32[8,128]{1,0:T(8,128)}, u32[]{:S(2)}) copy-start(f32[8,128]{1,0:T(8,128)} %get-tuple-element.108.refs_3_.refs_4_) | copy-start | bytes 12292
  4.9 3.8 %copy-start.12 = (f32[10,128]{1,0:T(8,128)S(1)}, f32[10,128]{1,0:T(8,128)}, u32[]{:S(2)}) copy-start(f32[10,128]{1,0:T(8,128)} %get-tuple-element.107.refs_2_) | copy-start | bytes 15364
  4.9 7.0 %copy-start.1 = (bf16[256,2560]{1,0:T(8,128)(2,1)S(1)}, bf16[256,2560]{1,0:T(8,128)(2,1)}, u32[]{:S(2)}) copy-start(bf16[256,2560]{1,0:T(8,128)(2,1)} %refs_1_.15) | copy-start | bytes 3932164
  4.9 7.0 %copy-start.2 = (bf16[256,128]{1,0:T(8,128)(2,1)S(1)}, bf16[256,128]{1,0:T(8,128)(2,1)}, u32[]{:S(2)}) copy-start(bf16[256,128]{1,0:T(8,128)(2,1)} %refs_2_.15) | copy-start | bytes 196612
  4.9 7.0 %copy-start.3 = (bf16[256,128]{1,0:T(8,128)(2,1)S(1)}, bf16[256,128]{1,0:T(8,128)(2,1)}, u32[]{:S(2)}) copy-start(bf16[256,128]{1,0:T(8,128)(2,1)} %refs_3_.15) | copy-start | bytes 196612
  5.0 7.0 %copy-start.4 = (bf16[256,128]{1,0:T(8,128)(2,1)S(1)}, bf16[256,128]{1,0:T(8,128)(2,1)}, u32[]{:S(2)}) copy-start(bf16[256,128]{1,0:T(8,128)(2,1)} %get-tuple-element.103.refs_5_.refs_7_.refs_4_) | copy-start | bytes 196612
  5.0 7.0 %copy-start.5 = (bf16[256,128]{1,0:T(8,128)(2,1)S(1)}, bf16[256,128]{1,0:T(8,128)(2,1)}, u32[]{:S(2)}) copy-start(bf16[256,128]{1,0:T(8,128)(2,1)} %get-tuple-element.104.refs_6_.refs_8_.refs_5_) | copy-start | bytes 196612
  5.0 7.0 %copy-start.6 = (f32[256,128]{1,0:T(8,128)S(1)}, f32[256,128]{1,0:T(8,128)}, u32[]{:S(2)}) copy-start(f32[256,128]{1,0:T(8,128)} %get-tuple-element.112.refs_6_) | copy-start | bytes 393220
  5.0 7.0 %copy-start.9 = (f32[40,256]{1,0:T(8,128)S(1)}, f32[40,256]{1,0:T(8,128)}, u32[]{:S(2)}) copy-start(f32[40,256]{1,0:T(8,128)} %refs_5_.5) | copy-start | bytes 122884
  8.6 3.4 %copy-start = (bf16[256,2560]{1,0:T(8,128)(2,1)S(1)}, bf16[256,2560]{1,0:T(8,128)(2,1)}, u32[]{:S(2)}) copy-start(bf16[256,2560]{1,0:T(8,128)(2,1)} %refs_0_.9) | copy-start | bytes 3932164
  8.6 8.5 %collective-permute-start.2 = (f32[1288,128]{1,0:T(8,128)}, f32[1288,128]{1,0:T(8,128)S(1)}, u32[]{:S(2)}, u32[]{:S(2)}) collective-permute-start(f32[1288,128]{1,0:T(8,128)} %get-tuple-element.111), channel_id=1, source_target_pairs={{0,1},{1,0},{2,3},{3,2},{4,5},{5,4},{6,7},{7,6},{8,9},{9,8},{10,11... | collective-permute-start | bytes 1978376 | tf_op jit(solution)/shard_map/ppermute | solution.py:701
  8.9 11.2 %collective-permute-start.1 = (f32[656,128]{1,0:T(8,128)S(1)}, f32[656,128]{1,0:T(8,128)S(1)}, u32[]{:S(2)}, u32[]{:S(2)}) collective-permute-start(f32[656,128]{1,0:T(8,128)S(1)} %get-tuple-element.110.refs_0_.refs_1_), channel_id=1, source_target_pairs={{0,2},{1,3},{2,0},{3,1},{4,6},{5,7},{6,4},{7,5},{8,10},{9,11},{10,... | collective-permute-start | bytes 1007624 | tf_op jit(solution)/shard_map/ppermute | solution.py:701
  12.0 8.0 %copy-start.7 = (f32[1280,128]{1,0:T(8,128)S(1)}, f32[1280,128]{1,0:T(8,128)}, u32[]{:S(2)}) copy-start(f32[1280,128]{1,0:T(8,128)} %get-tuple-element.122.refs_1_) | copy-start | bytes 1966084
  12.0 8.0 %copy-start.11 = (f32[10,128]{1,0:T(8,128)S(1)}, f32[10,128]{1,0:T(8,128)}, u32[]{:S(2)}) copy-start(f32[10,128]{1,0:T(8,128)} %get-tuple-element.123.refs_2_) | copy-start | bytes 15364
  20.1 13.1 %collective-permute-start.4 = (f32[656,128]{1,0:T(8,128)S(1)}, f32[656,128]{1,0:T(8,128)S(1)}, u32[]{:S(2)}, u32[]{:S(2)}) collective-permute-start(f32[656,128]{1,0:T(8,128)S(1)} %get-tuple-element.124.refs_1_), channel_id=1, source_target_pairs={{0,2},{1,3},{2,0},{3,1},{4,6},{5,7},{6,4},{7,5},{8,10},{9,11},{10,... | collective-permute-start | bytes 1007624 | tf_op jit(solution)/shard_map/ppermute | solution.py:701
  22.2 10.0 %collective-permute-start.3 = (f32[336,128]{1,0:T(8,128)S(1)}, f32[336,128]{1,0:T(8,128)S(1)}, u32[]{:S(2)}, u32[]{:S(2)}) collective-permute-start(f32[336,128]{1,0:T(8,128)S(1)} %get-tuple-element.120.refs_0_.refs_1_), channel_id=1, source_target_pairs={{0,4},{1,5},{2,6},{3,7},{4,0},{5,1},{6,2},{7,3},{8,12},{9,13},{10,... | collective-permute-start | bytes 516104 | tf_op jit(solution)/shard_map/ppermute | solution.py:701
  33.4 12.6 %collective-permute-start.8 = (f32[336,128]{1,0:T(8,128)S(1)}, f32[336,128]{1,0:T(8,128)S(1)}, u32[]{:S(2)}, u32[]{:S(2)}) collective-permute-start(f32[336,128]{1,0:T(8,128)S(1)} %get-tuple-element.138.refs_1_), channel_id=1, source_target_pairs={{0,4},{1,5},{2,6},{3,7},{4,0},{5,1},{6,2},{7,3},{8,12},{9,13},{10,... | collective-permute-start | bytes 516104 | tf_op jit(solution)/shard_map/ppermute | solution.py:701
  36.0 8.3 %collective-permute-start.7 = (f32[328,128]{1,0:T(8,128)S(1)}, f32[328,128]{1,0:T(8,128)S(1)}, u32[]{:S(2)}, u32[]{:S(2)}) collective-permute-start(f32[328,128]{1,0:T(8,128)S(1)} %up.5.refs_0_), channel_id=1, source_target_pairs={{1,25},{3,27},{5,29},{7,31},{24,0},{26,2},{28,4},{30,6}} | collective-permute-start | bytes 503816 | tf_op jit(solution)/shard_map/ppermute | solution.py:701
  37.3 8.7 %collective-permute-start.6 = (f32[328,128]{1,0:T(8,128)S(1)}, f32[328,128]{1,0:T(8,128)S(1)}, u32[]{:S(2)}, u32[]{:S(2)}) collective-permute-start(f32[328,128]{1,0:T(8,128)S(1)} %up.5.refs_0_), channel_id=1, source_target_pairs={{1,17},{3,19},{5,21},{7,23},{9,25},{11,27},{13,29},{15,31},{16,0},... | collective-permute-start | bytes 503816 | tf_op jit(solution)/shard_map/ppermute | solution.py:701
  38.6 7.4 %collective-permute-start.5 = (f32[328,128]{1,0:T(8,128)S(1)}, f32[328,128]{1,0:T(8,128)S(1)}, u32[]{:S(2)}, u32[]{:S(2)}) collective-permute-start(f32[328,128]{1,0:T(8,128)S(1)} %up.5.refs_0_), channel_id=1, source_target_pairs={{1,9},{3,11},{5,13},{7,15},{8,0},{9,17},{10,2},{11,19},{12,4},{13,... | collective-permute-start | bytes 503816 | tf_op jit(solution)/shard_map/ppermute | solution.py:701
  46.3 8.8 %collective-permute-start.9 = (f32[336,128]{1,0:T(8,128)S(1)}, f32[336,128]{1,0:T(8,128)S(1)}, u32[]{:S(2)}, u32[]{:S(2)}) collective-permute-start(f32[336,128]{1,0:T(8,128)S(1)} %get-tuple-element.161), channel_id=1, source_target_pairs={{0,4},{1,5},{2,6},{3,7},{4,0},{5,1},{6,2},{7,3},{8,12},{9,13},{10,... | collective-permute-start | bytes 516104 | tf_op jit(solution)/shard_map/ppermute | solution.py:701
  47.3 8.3 %collective-permute-start.13 = (f32[328,128]{1,0:T(8,128)S(1)}, f32[328,128]{1,0:T(8,128)S(1)}, u32[]{:S(2)}, u32[]{:S(2)}) collective-permute-start(f32[328,128]{1,0:T(8,128)S(1)} %up.7), channel_id=1, source_target_pairs={{1,25},{3,27},{5,29},{7,31},{24,0},{26,2},{28,4},{30,6}} | collective-permute-start | bytes 503816 | tf_op jit(solution)/shard_map/ppermute | solution.py:701
  48.6 8.7 %collective-permute-start.12 = (f32[328,128]{1,0:T(8,128)S(1)}, f32[328,128]{1,0:T(8,128)S(1)}, u32[]{:S(2)}, u32[]{:S(2)}) collective-permute-start(f32[328,128]{1,0:T(8,128)S(1)} %up.7), channel_id=1, source_target_pairs={{1,17},{3,19},{5,21},{7,23},{9,25},{11,27},{13,29},{15,31},{16,0},... | collective-permute-start | bytes 503816 | tf_op jit(solution)/shard_map/ppermute | solution.py:701
  49.9 7.4 %collective-permute-start.11 = (f32[328,128]{1,0:T(8,128)S(1)}, f32[328,128]{1,0:T(8,128)S(1)}, u32[]{:S(2)}, u32[]{:S(2)}) collective-permute-start(f32[328,128]{1,0:T(8,128)S(1)} %up.7), channel_id=1, source_target_pairs={{1,9},{3,11},{5,13},{7,15},{8,0},{9,17},{10,2},{11,19},{12,4},{13,... | collective-permute-start | bytes 503816 | tf_op jit(solution)/shard_map/ppermute | solution.py:701
  55.3 10.7 %collective-permute-start.10 = (f32[656,128]{1,0:T(8,128)S(1)}, f32[656,128]{1,0:T(8,128)S(1)}, u32[]{:S(2)}, u32[]{:S(2)}) collective-permute-start(f32[656,128]{1,0:T(8,128)S(1)} %get-tuple-element.163), channel_id=1, source_target_pairs={{0,2},{1,3},{2,0},{3,1},{4,6},{5,7},{6,4},{7,5},{8,10},{9,11},{10,... | collective-permute-start | bytes 1007624 | tf_op jit(solution)/shard_map/ppermute | solution.py:701
  57.5 8.1 %collective-permute-start.14 = (f32[336,128]{1,0:T(8,128)S(1)}, f32[336,128]{1,0:T(8,128)S(1)}, u32[]{:S(2)}, u32[]{:S(2)}) collective-permute-start(f32[336,128]{1,0:T(8,128)S(1)} %get-tuple-element.166), channel_id=1, source_target_pairs={{0,4},{1,5},{2,6},{3,7},{4,0},{5,1},{6,2},{7,3},{8,12},{9,13},{10,... | collective-permute-start | bytes 516104 | tf_op jit(solution)/shard_map/ppermute | solution.py:701
  66.2 8.9 %collective-permute-start.17 = (f32[656,128]{1,0:T(8,128)S(1)}, f32[656,128]{1,0:T(8,128)S(1)}, u32[]{:S(2)}, u32[]{:S(2)}) collective-permute-start(f32[656,128]{1,0:T(8,128)S(1)} %get-tuple-element.178), channel_id=1, source_target_pairs={{0,2},{1,3},{2,0},{3,1},{4,6},{5,7},{6,4},{7,5},{8,10},{9,11},{10,... | collective-permute-start | bytes 1007624 | tf_op jit(solution)/shard_map/ppermute | solution.py:701
  68.3 1.7 %collective-permute-start.15 = (f32[640,128]{1,0:T(8,128)S(1)}, f32[640,128]{1,0:T(8,128)S(1)}, u32[]{:S(2)}, u32[]{:S(2)}) collective-permute-start(f32[640,128]{1,0:T(8,128)S(1)} %get-tuple-element.168.refs_4_), channel_id=1, source_target_pairs={{0,1},{1,0},{2,3},{3,2},{4,5},{5,4},{6,7},{7,6},{8,9},{9,8},{10,11... | collective-permute-start | bytes 983048 | tf_op jit(solution)/shard_map/ppermute | solution.py:701
  68.4 2.1 %collective-permute-start.16 = (f32[640,128]{1,0:T(8,128)S(1)}, f32[640,128]{1,0:T(8,128)S(1)}, u32[]{:S(2)}, u32[]{:S(2)}) collective-permute-start(f32[640,128]{1,0:T(8,128)S(1)} %get-tuple-element.169.refs_5_), channel_id=1, source_target_pairs={{0,1},{1,0},{2,3},{3,2},{4,5},{5,4},{6,7},{7,6},{8,9},{9,8},{10,11... | collective-permute-start | bytes 983048 | tf_op jit(solution)/shard_map/ppermute | solution.py:701
  68.9 6.1 %collective-permute-start.18 = (f32[640,128]{1,0:T(8,128)S(1)}, f32[640,128]{1,0:T(8,128)S(1)}, u32[]{:S(2)}, u32[]{:S(2)}) collective-permute-start(f32[640,128]{1,0:T(8,128)S(1)} %get-tuple-element.179.refs_4_), channel_id=1, source_target_pairs={{0,1},{1,0},{2,3},{3,2},{4,5},{5,4},{6,7},{7,6},{8,9},{9,8},{10,11... | collective-permute-start | bytes 983048 | tf_op jit(solution)/shard_map/ppermute | solution.py:701
  75.0 1.6 %collective-permute-start.19 = (f32[656,128]{1,0:T(8,128)S(1)}, f32[656,128]{1,0:T(8,128)S(1)}, u32[]{:S(2)}, u32[]{:S(2)}) collective-permute-start(f32[656,128]{1,0:T(8,128)S(1)} %collective-permute-done.17.refs_5_), channel_id=1, source_target_pairs={{0,1},{1,0},{2,3},{3,2},{4,5},{5,4},{6,7},{7,6},{8,9},{9,8},{10,11... | collective-permute-start | bytes 1007624 | tf_op jit(solution)/shard_map/ppermute | solution.py:701
  77.5 1.2 %collective-permute-start.20 = (f32[8,128]{1,0:T(8,128)S(1)}, f32[8,128]{1,0:T(8,128)S(1)}, u32[]{:S(2)}, u32[]{:S(2)}) collective-permute-start(f32[8,128]{1,0:T(8,128)S(1)} %get-tuple-element.188.total_ref), channel_id=1, source_target_pairs={{0,1},{1,0},{2,3},{3,2},{4,5},{5,4},{6,7},{7,6},{8,9},{9,8},{10,11... | collective-permute-start | bytes 12296 | tf_op jit(solution)/shard_map/ppermute | solution.py:701
  78.8 5.9 %collective-permute-start.23 = (f32[8,128]{1,0:T(8,128)S(1)}, f32[8,128]{1,0:T(8,128)S(1)}, u32[]{:S(2)}, u32[]{:S(2)}) collective-permute-start(f32[8,128]{1,0:T(8,128)S(1)} %get-tuple-element.189.refs_13_.total_ref), channel_id=1, source_target_pairs={{0,6},{1,7},{2,4},{3,5},{4,2},{5,3},{6,0},{7,1},{8,14},{9,15},{10,... | collective-permute-start | bytes 12296 | tf_op jit(solution)/shard_map/ppermute | solution.py:701
  81.6 4.5 %collective-permute-start.22 = (f32[8,128]{1,0:T(8,128)S(1)}, f32[8,128]{1,0:T(8,128)S(1)}, u32[]{:S(2)}, u32[]{:S(2)}) collective-permute-start(f32[8,128]{1,0:T(8,128)S(1)} %get-tuple-element.189.refs_13_.total_ref), channel_id=1, source_target_pairs={{0,4},{1,5},{2,6},{3,7},{4,0},{5,1},{6,2},{7,3},{8,12},{9,13},{10,... | collective-permute-start | bytes 12296 | tf_op jit(solution)/shard_map/ppermute | solution.py:701
  81.9 4.2 %collective-permute-start.21 = (f32[8,128]{1,0:T(8,128)S(1)}, f32[8,128]{1,0:T(8,128)S(1)}, u32[]{:S(2)}, u32[]{:S(2)}) collective-permute-start(f32[8,128]{1,0:T(8,128)S(1)} %get-tuple-element.189.refs_13_.total_ref), channel_id=1, source_target_pairs={{0,2},{1,3},{2,0},{3,1},{4,6},{5,7},{6,4},{7,5},{8,10},{9,11},{10,... | collective-permute-start | bytes 12296 | tf_op jit(solution)/shard_map/ppermute | solution.py:701
  86.1 6.4 %collective-permute-start.26 = (f32[8,128]{1,0:T(8,128)S(1)}, f32[8,128]{1,0:T(8,128)S(1)}, u32[]{:S(2)}, u32[]{:S(2)}) collective-permute-start(f32[8,128]{1,0:T(8,128)S(1)} %get-tuple-element.196.refs_13_), channel_id=1, source_target_pairs={{24,0},{25,1},{26,2},{27,3},{28,4},{29,5},{30,6},{31,7}} | collective-permute-start | bytes 12296 | tf_op jit(solution)/shard_map/ppermute | solution.py:701
  87.4 5.5 %collective-permute-start.25 = (f32[8,128]{1,0:T(8,128)S(1)}, f32[8,128]{1,0:T(8,128)S(1)}, u32[]{:S(2)}, u32[]{:S(2)}) collective-permute-start(f32[8,128]{1,0:T(8,128)S(1)} %get-tuple-element.196.refs_13_), channel_id=1, source_target_pairs={{16,0},{17,1},{18,2},{19,3},{20,4},{21,5},{22,6},{23,7},{24,8},{25... | collective-permute-start | bytes 12296 | tf_op jit(solution)/shard_map/ppermute | solution.py:701
  88.7 5.5 %collective-permute-start.24 = (f32[8,128]{1,0:T(8,128)S(1)}, f32[8,128]{1,0:T(8,128)S(1)}, u32[]{:S(2)}, u32[]{:S(2)}) collective-permute-start(f32[8,128]{1,0:T(8,128)S(1)} %get-tuple-element.196.refs_13_), channel_id=1, source_target_pairs={{8,0},{9,1},{10,2},{11,3},{12,4},{13,5},{14,6},{15,7},{16,8},{17,9... | collective-permute-start | bytes 12296 | tf_op jit(solution)/shard_map/ppermute | solution.py:701

commit v15 on v14

--- a/solution.py
+++ b/solution.py
@@ -770,9 +770,12 @@
             more = pl.cdiv(chunks - ready, 3 - step)
             block = intra(ready, more, token, *maps, log_decay, shared, block)
             ready += more
-            waiting[0], waiting[1], first[1], block = lax.optimization_barrier(
-                (waiting[0], waiting[1], first[1], block)
-            )
+            if step == 0:
+                first[1], block = lax.optimization_barrier((first[1], block))
+            elif step == 1:
+                waiting[0], block = lax.optimization_barrier((waiting[0], block))
+            else:
+                waiting[1], block = lax.optimization_barrier((waiting[1], block))
         elif levels + 1 < step < rounds - 1:
             waiting[0], waiting[1] = lax.optimization_barrier((waiting[0], waiting[1]))
     dx, state_own, back_own, change, db, dc = block

time: 95.3 us -> 99.5 us (1.044)
  waiting for transfers between devices: 29.4 us -> 33.1 us
    ppermute x27, waiting for transfers between devices: 29.4 us -> 33.1 us  [move(): return lax.ppermute(value, ('grp', 'seq'), pairs)]
  transfers between devices with their start and end apart: 27 -> 27, of which waited for: 18 -> 20; matrix products, arithmetic and copies ran while one was open for 0% -> 0% of each run, Pallas kernels for 27% -> 26%
where the time goes in v15:
time: 99.5 us; the launch traced here: 99.2 us
  starting transfers between devices  33.4 us (34%)
  waiting for transfers between devices  33.1 us (33%)
  Pallas kernels  31.6 us (32%)
  between operations  1.01 us (1%)
    ppermute x27, starting transfers between devices, move(): return lax.ppermute(value, ('grp', 'seq'), pairs)  33.4 us
    ppermute x27, waiting for transfers between devices, move(): return lax.ppermute(value, ('grp', 'seq'), pairs)  33.1 us
    pallas_call x3, Pallas kernels, intra(): pl.pallas_call(lambda *refs: intra_kernel(heads, wide // heads, start, la...  12.5 us
    pallas_call x2, Pallas kernels, summary(): pl.pallas_call(lambda *refs: summary_kernel(heads, chips, half, *refs), g...  7.38 us
    pallas_call x3, Pallas kernels, finish(): pl.pallas_call(lambda *refs: finish_kernel(heads, start, steps, last, *re...  7.27 us
  transfers between devices with their start and end apart: 27, of which 20 were waited for; matrix products, arithmetic and copies ran while one was open for 0% of the time, Pallas kernels for 26%

profile of v15, /device:TPU:0, one launch (start us, length us, event | category | flops | bytes accessed | tf_op | source)
XLA Modules:
  0.0 99.2 jit_solution(7534136029986950590)
XLA Ops:
  0.6 3.8 %summary.2 = (f32[1288,128]{1,0:T(8,128)}, f32[1280,128]{1,0:T(8,128)}, f32[10,128]{1,0:T(8,128)}, f32[8,128]{1,0:T(8,128)}, f32[256,128]{1,0:T(8,128)}, /*index...) custom-call(bf16[256,2560]{1,0:T(8,128)(2,1)} %refs_0_.9, bf16[256,2560]{1,0:T(8,128)(2,1)} %refs_1_.15, ...), custom_call_target="tpu_custom_call" | custom-call | flops 1 | bytes 1 | tf_op jit(solution)/shard_map/summary/pallas_call | solution.py:195
  4.4 0.5 collective-permute-start.1
  5.0 3.6 %summary.3 = (f32[1288,128]{1,0:T(8,128)}, f32[1280,128]{1,0:T(8,128)}, f32[10,128]{1,0:T(8,128)}) custom-call(bf16[256,2560]{1,0:T(8,128)(2,1)} %refs_0_.9, bf16[256,2560]{1,0:T(8,128)(2,1)} %refs_1_.15, bf16[256,128]{1,0:T(8,128)(2,1)} %refs_2_.15, bf16[256,128]{1,0:T(8,128)(2,1)} %refs_3_.15, f32[8,128]{1,0:T(8,128)} %get-tuple-element.98.refs_4_.refs_3_, ...), custom_call_target="tpu_custom_call" | custom-call | flops 1 | bytes 1 | tf_op jit(solution)/shard_map/summary/pallas_call | solution.py:195
  8.6 0.1 collective-permute-start
  8.8 0.1 combine.2
  8.9 3.1 %collective-permute-start.4 = (f32[656,128]{1,0:T(8,128)S(1)}, f32[656,128]{1,0:T(8,128)S(1)}, u32[]{:S(2)}, u32[]{:S(2)}) collective-permute-start(f32[656,128]{1,0:T(8,128)S(1)} %get-tuple-element.103.refs_0_.refs_1_), channel_id=1, source_target_pairs={{0,2},{1,3},{2,0},{3,1},{4,6},{5,7},{6,4},{7,5},{8,10},{9,11},{10,... | collective-permute-start | bytes 1007624 | tf_op jit(solution)/shard_map/ppermute | solution.py:701
  12.0 5.1 %intra.3 = (f32[256,2560]{1,0:T(8,128)S(1)}, f32[128,2560]{1,0:T(8,128)S(1)}, f32[128,2560]{1,0:T(8,128)S(1)}, f32[256,128]{1,0:T(8,128)S(1)}, f32[256,256]{1,0:T(8,128)S(1)}) custom-call(f32[656,128]{1,0:T(8,128)S(1)} %get-tuple-element.103.refs_0_.refs_1_, bf16[256,2560]{1,0:T(8,128)(2,1)S(1)} %copy-done, bf16[256,2560]{1,0:T(8,128)(2,1)S(1)} %copy-done.1, ...), custom_call_target="tpu_custom_call" | custom-call | flops 1 | bytes 1 | tf_op jit(solution)/shard_map/intra/pallas_call | solution.py:441
  17.1 0.1 combine.3
  17.2 0.5 collective-permute-start.2
  17.8 2.6 %collective-permute-done.4.refs_2_ = f32[656,128]{1,0:T(8,128)S(1)} collective-permute-done((f32[656,128]{1,0:T(8,128)S(1)}, f32[656,128]{1,0:T(8,128)S(1)}, u32[]{:S(2)}, u32[]{:S(2)}) %collective-permute-start.4) | collective-permute-done | bytes 335904 | tf_op jit(solution)/shard_map/ppermute | solution.py:701
  20.4 0.2 up.5
  20.6 3.0 %collective-permute-start.5 = (f32[336,128]{1,0:T(8,128)S(1)}, f32[336,128]{1,0:T(8,128)S(1)}, u32[]{:S(2)}, u32[]{:S(2)}) collective-permute-start(f32[336,128]{1,0:T(8,128)S(1)} %get-tuple-element.118.refs_0_.refs_1_), channel_id=1, source_target_pairs={{0,4},{1,5},{2,6},{3,7},{4,0},{5,1},{6,2},{7,3},{8,12},{9,13},{10,... | collective-permute-start | bytes 516104 | tf_op jit(solution)/shard_map/ppermute | solution.py:701
  23.6 5.0 %intra.4 = (f32[256,2560]{1,0:T(8,128)S(1)}, f32[128,2560]{1,0:T(8,128)S(1)}, f32[128,2560]{1,0:T(8,128)S(1)}, f32[256,128]{1,0:T(8,128)S(1)}, f32[256,256]{1,0:T(8,128)S(1)}) custom-call(f32[336,128]{1,0:T(8,128)S(1)} %get-tuple-element.118.refs_0_.refs_1_, ...), custom_call_target="tpu_custom_call", output_to_operand_aliasing={{0}: (9, {}), {1}: (10, {}), {2}: (11, {})} | custom-call | flops 1 | bytes 1 | tf_op jit(solution)/shard_map/intra/pallas_call | solution.py:441
  28.6 1.6 %collective-permute-done.5.refs_2_ = f32[336,128]{1,0:T(8,128)S(1)} collective-permute-done((f32[336,128]{1,0:T(8,128)S(1)}, f32[336,128]{1,0:T(8,128)S(1)}, u32[]{:S(2)}, u32[]{:S(2)}) %collective-permute-start.5) | collective-permute-done | bytes 172064 | tf_op jit(solution)/shard_map/ppermute | solution.py:701
  30.2 0.2 up.6.refs_0_
  30.4 1.3 %collective-permute-start.8 = (f32[328,128]{1,0:T(8,128)S(1)}, f32[328,128]{1,0:T(8,128)S(1)}, u32[]{:S(2)}, u32[]{:S(2)}) collective-permute-start(f32[328,128]{1,0:T(8,128)S(1)} %up.6.refs_0_), channel_id=1, source_target_pairs={{1,25},{3,27},{5,29},{7,31},{24,0},{26,2},{28,4},{30,6}} | collective-permute-start | bytes 503816 | tf_op jit(solution)/shard_map/ppermute | solution.py:701
  31.7 1.3 %collective-permute-start.7 = (f32[328,128]{1,0:T(8,128)S(1)}, f32[328,128]{1,0:T(8,128)S(1)}, u32[]{:S(2)}, u32[]{:S(2)}) collective-permute-start(f32[328,128]{1,0:T(8,128)S(1)} %up.6.refs_0_), channel_id=1, source_target_pairs={{1,17},{3,19},{5,21},{7,23},{9,25},{11,27},{13,29},{15,31},{16,0},... | collective-permute-start | bytes 503816 | tf_op jit(solution)/shard_map/ppermute | solution.py:701
  33.0 1.3 %collective-permute-start.6 = (f32[328,128]{1,0:T(8,128)S(1)}, f32[328,128]{1,0:T(8,128)S(1)}, u32[]{:S(2)}, u32[]{:S(2)}) collective-permute-start(f32[328,128]{1,0:T(8,128)S(1)} %up.6.refs_0_), channel_id=1, source_target_pairs={{1,9},{3,11},{5,13},{7,15},{8,0},{9,17},{10,2},{11,19},{12,4},{13,... | collective-permute-start | bytes 503816 | tf_op jit(solution)/shard_map/ppermute | solution.py:701
  34.4 0.2 up.4
  34.6 3.5 %collective-permute-start.3 = (f32[336,128]{1,0:T(8,128)S(1)}, f32[336,128]{1,0:T(8,128)S(1)}, u32[]{:S(2)}, u32[]{:S(2)}) collective-permute-start(f32[336,128]{1,0:T(8,128)S(1)} %get-tuple-element.115.refs_1_), channel_id=1, source_target_pairs={{0,4},{1,5},{2,6},{3,7},{4,0},{5,1},{6,2},{7,3},{8,12},{9,13},{10,... | collective-permute-start | bytes 516104 | tf_op jit(solution)/shard_map/ppermute | solution.py:701
  38.1 0.6 collective-permute-done.8.refs_5_
  38.7 1.7 %collective-permute-done.7.refs_4_ = f32[328,128]{1,0:T(8,128)S(1)} collective-permute-done((f32[328,128]{1,0:T(8,128)S(1)}, f32[328,128]{1,0:T(8,128)S(1)}, u32[]{:S(2)}, u32[]{:S(2)}) %collective-permute-start.7) | collective-permute-done | bytes 167968 | tf_op jit(solution)/shard_map/ppermute | solution.py:701
  40.4 1.5 %collective-permute-done.6.refs_3_ = f32[328,128]{1,0:T(8,128)S(1)} collective-permute-done((f32[328,128]{1,0:T(8,128)S(1)}, f32[328,128]{1,0:T(8,128)S(1)}, u32[]{:S(2)}, u32[]{:S(2)}) %collective-permute-start.6) | collective-permute-done | bytes 167968 | tf_op jit(solution)/shard_map/ppermute | solution.py:701
  41.9 0.2 down.4
  42.2 3.4 %collective-permute-start.9 = (f32[336,128]{1,0:T(8,128)S(1)}, f32[336,128]{1,0:T(8,128)S(1)}, u32[]{:S(2)}, u32[]{:S(2)}) collective-permute-start(f32[336,128]{1,0:T(8,128)S(1)} %get-tuple-element.148), channel_id=1, source_target_pairs={{0,4},{1,5},{2,6},{3,7},{4,0},{5,1},{6,2},{7,3},{8,12},{9,13},{10,... | collective-permute-start | bytes 516104 | tf_op jit(solution)/shard_map/ppermute | solution.py:701
  45.6 2.5 %intra.5 = (f32[256,2560]{1,0:T(8,128)S(1)}, f32[128,2560]{1,0:T(8,128)S(1)}, f32[128,2560]{1,0:T(8,128)S(1)}, f32[256,128]{1,0:T(8,128)S(1)}, f32[256,128]{1,0:T(8,128)S(1)}, /*index=5*/f32[256,128]{1,0:T(8,128)S(1)}) custom-call(f32[328,128]{1,0:T(8,128)S(1)} %up.6.refs_0_, ...), custom_call_target="tpu_custom_call", output_to_operand_aliasing={{0}: (9, {}), {1}: (10, {}), {2}: (11, {})} | custom-call | flops 1 | bytes 1 | tf_op jit(solution)/shard_map/intra/pallas_call | solution.py:441
  48.1 0.2 up.7
  48.3 1.3 %collective-permute-start.13 = (f32[328,128]{1,0:T(8,128)S(1)}, f32[328,128]{1,0:T(8,128)S(1)}, u32[]{:S(2)}, u32[]{:S(2)}) collective-permute-start(f32[328,128]{1,0:T(8,128)S(1)} %up.7), channel_id=1, source_target_pairs={{1,25},{3,27},{5,29},{7,31},{24,0},{26,2},{28,4},{30,6}} | collective-permute-start | bytes 503816 | tf_op jit(solution)/shard_map/ppermute | solution.py:701
  49.6 1.3 %collective-permute-start.12 = (f32[328,128]{1,0:T(8,128)S(1)}, f32[328,128]{1,0:T(8,128)S(1)}, u32[]{:S(2)}, u32[]{:S(2)}) collective-permute-start(f32[328,128]{1,0:T(8,128)S(1)} %up.7), channel_id=1, source_target_pairs={{1,17},{3,19},{5,21},{7,23},{9,25},{11,27},{13,29},{15,31},{16,0},... | collective-permute-start | bytes 503816 | tf_op jit(solution)/shard_map/ppermute | solution.py:701
  50.9 1.5 %collective-permute-start.11 = (f32[328,128]{1,0:T(8,128)S(1)}, f32[328,128]{1,0:T(8,128)S(1)}, u32[]{:S(2)}, u32[]{:S(2)}) collective-permute-start(f32[328,128]{1,0:T(8,128)S(1)} %up.7), channel_id=1, source_target_pairs={{1,9},{3,11},{5,13},{7,15},{8,0},{9,17},{10,2},{11,19},{12,4},{13,... | collective-permute-start | bytes 503816 | tf_op jit(solution)/shard_map/ppermute | solution.py:701
  52.4 1.6 %collective-permute-done.9.refs_4_ = f32[336,128]{1,0:T(8,128)S(1)} collective-permute-done((f32[336,128]{1,0:T(8,128)S(1)}, f32[336,128]{1,0:T(8,128)S(1)}, u32[]{:S(2)}, u32[]{:S(2)}) %collective-permute-start.9) | collective-permute-done | bytes 172064 | tf_op jit(solution)/shard_map/ppermute | solution.py:701
  54.0 0.2 down.5
  54.3 2.0 %collective-permute-start.10 = (f32[656,128]{1,0:T(8,128)S(1)}, f32[656,128]{1,0:T(8,128)S(1)}, u32[]{:S(2)}, u32[]{:S(2)}) collective-permute-start(f32[656,128]{1,0:T(8,128)S(1)} %get-tuple-element.150), channel_id=1, source_target_pairs={{0,2},{1,3},{2,0},{3,1},{4,6},{5,7},{6,4},{7,5},{8,10},{9,11},{10,... | collective-permute-start | bytes 1007624 | tf_op jit(solution)/shard_map/ppermute | solution.py:701
  56.2 1.8 %collective-permute-done.13.refs_5_ = f32[328,128]{1,0:T(8,128)S(1)} collective-permute-done((f32[328,128]{1,0:T(8,128)S(1)}, f32[328,128]{1,0:T(8,128)S(1)}, u32[]{:S(2)}, u32[]{:S(2)}) %collective-permute-start.13) | collective-permute-done | bytes 167968 | tf_op jit(solution)/shard_map/ppermute | solution.py:701
  58.1 0.6 collective-permute-done.12.refs_4_
  58.7 2.8 %collective-permute-done.11.refs_3_ = f32[328,128]{1,0:T(8,128)S(1)} collective-permute-done((f32[328,128]{1,0:T(8,128)S(1)}, f32[328,128]{1,0:T(8,128)S(1)}, u32[]{:S(2)}, u32[]{:S(2)}) %collective-permute-start.11) | collective-permute-done | bytes 167968 | tf_op jit(solution)/shard_map/ppermute | solution.py:701
  61.5 0.3 down.6
  61.9 10.0 %collective-permute-done.14.refs_4_ = f32[336,128]{1,0:T(8,128)S(1)} collective-permute-done((f32[336,128]{1,0:T(8,128)S(1)}, f32[336,128]{1,0:T(8,128)S(1)}, u32[]{:S(2)}, u32[]{:S(2)}) %collective-permute-start.14) | collective-permute-done | bytes 172064 | tf_op jit(solution)/shard_map/ppermute | solution.py:701
  71.8 0.2 down.7
  72.3 0.5 collective-permute-start.16
  72.8 0.1 collective-permute-start.18
  72.9 1.0 %collective-permute-done.15.refs_6_ = f32[640,128]{1,0:T(8,128)S(1)} collective-permute-done((f32[640,128]{1,0:T(8,128)S(1)}, f32[640,128]{1,0:T(8,128)S(1)}, u32[]{:S(2)}, u32[]{:S(2)}) %collective-permute-start.15) | collective-permute-done | bytes 327712 | tf_op jit(solution)/shard_map/ppermute | solution.py:701
  74.0 0.5 collective-permute-done.16.refs_7_
  74.4 0.8 assemble.2
  75.2 3.8 %finish.3 = (bf16[256,2560]{1,0:T(8,128)(2,1)}, f32[256,128]{1,0:T(8,128)S(1)}, f32[256,128]{1,0:T(8,128)S(1)}, f32[256,128]{1,0:T(8,128)S(1)}, f32[8,128]{1,0:T(8,128)S(1)}) custom-call(bf16[256,2560]{1,0:T(8,128)(2,1)S(1)} %copy-done, bf16[256,2560]{1,0:T(8,128)(2,1)S(1)} %copy-done.1, bf16[256,128]{1,0:T(8,128)(2,1)S(1)} %copy-done.2, ...), custom_call_target="tpu_custom_call" | custom-call | flops 1 | bytes 1 | tf_op jit(solution)/shard_map/finish/pallas_call | solution.py:611
  79.0 0.8 collective-permute-done.17.refs_5_
  79.8 1.6 %collective-permute-done.19.refs_7_ = f32[656,128]{1,0:T(8,128)S(1)} collective-permute-done((f32[656,128]{1,0:T(8,128)S(1)}, f32[656,128]{1,0:T(8,128)S(1)}, u32[]{:S(2)}, u32[]{:S(2)}) %collective-permute-start.19) | collective-permute-done | bytes 335904 | tf_op jit(solution)/shard_map/ppermute | solution.py:701
  81.4 0.8 assemble.3
  82.2 0.2 collective-permute-start.20
  82.4 1.0 %collective-permute-done.20.got_ref = f32[8,128]{1,0:T(8,128)S(1)} collective-permute-done((f32[8,128]{1,0:T(8,128)S(1)}, f32[8,128]{1,0:T(8,128)S(1)}, u32[]{:S(2)}, u32[]{:S(2)}) %collective-permute-start.20) | collective-permute-done | bytes 4128 | tf_op jit(solution)/shard_map/ppermute | solution.py:701
  83.5 2.1 %collective-permute-start.23 = (f32[8,128]{1,0:T(8,128)S(1)}, f32[8,128]{1,0:T(8,128)S(1)}, u32[]{:S(2)}, u32[]{:S(2)}) collective-permute-start(f32[8,128]{1,0:T(8,128)S(1)} %get-tuple-element.175.refs_13_.total_ref), channel_id=1, source_target_pairs={{0,6},{1,7},{2,4},{3,5},{4,2},{5,3},{6,0},{7,1},{8,14},{9,15},{10,... | collective-permute-start | bytes 12296 | tf_op jit(solution)/shard_map/ppermute | solution.py:701
  85.5 1.1 %collective-permute-start.22 = (f32[8,128]{1,0:T(8,128)S(1)}, f32[8,128]{1,0:T(8,128)S(1)}, u32[]{:S(2)}, u32[]{:S(2)}) collective-permute-start(f32[8,128]{1,0:T(8,128)S(1)} %get-tuple-element.175.refs_13_.total_ref), channel_id=1, source_target_pairs={{0,4},{1,5},{2,6},{3,7},{4,0},{5,1},{6,2},{7,3},{8,12},{9,13},{10,... | collective-permute-start | bytes 12296 | tf_op jit(solution)/shard_map/ppermute | solution.py:701
  86.7 1.2 %collective-permute-start.21 = (f32[8,128]{1,0:T(8,128)S(1)}, f32[8,128]{1,0:T(8,128)S(1)}, u32[]{:S(2)}, u32[]{:S(2)}) collective-permute-start(f32[8,128]{1,0:T(8,128)S(1)} %get-tuple-element.175.refs_13_.total_ref), channel_id=1, source_target_pairs={{0,2},{1,3},{2,0},{3,1},{4,6},{5,7},{6,4},{7,5},{8,10},{9,11},{10,... | collective-permute-start | bytes 12296 | tf_op jit(solution)/shard_map/ppermute | solution.py:701
  87.9 1.5 %finish.4 = (bf16[256,2560]{1,0:T(8,128)(2,1)}, f32[256,128]{1,0:T(8,128)S(1)}, f32[256,128]{1,0:T(8,128)S(1)}, f32[256,128]{1,0:T(8,128)S(1)}, f32[8,128]{1,0:T(8,128)S(1)}) custom-call(bf16[256,2560]{1,0:T(8,128)(2,1)S(1)} %copy-done, bf16[256,2560]{1,0:T(8,128)(2,1)S(1)} %copy-done.1, ...), custom_call_target="tpu_custom_call", output_to_operand_aliasing={{0}: (12, {})} | custom-call | flops 1 | bytes 1 | tf_op jit(solution)/shard_map/finish/pallas_call | solution.py:611
  89.4 0.7 collective-permute-done.22.refs_1_
  90.0 0.2 collective-permute-done.21.refs_0_
  90.3 1.3 %collective-permute-start.26 = (f32[8,128]{1,0:T(8,128)S(1)}, f32[8,128]{1,0:T(8,128)S(1)}, u32[]{:S(2)}, u32[]{:S(2)}) collective-permute-start(f32[8,128]{1,0:T(8,128)S(1)} %get-tuple-element.182.refs_13_), channel_id=1, source_target_pairs={{24,0},{25,1},{26,2},{27,3},{28,4},{29,5},{30,6},{31,7}} | collective-permute-start | bytes 12296 | tf_op jit(solution)/shard_map/ppermute | solution.py:701
  91.6 1.3 %collective-permute-start.25 = (f32[8,128]{1,0:T(8,128)S(1)}, f32[8,128]{1,0:T(8,128)S(1)}, u32[]{:S(2)}, u32[]{:S(2)}) collective-permute-start(f32[8,128]{1,0:T(8,128)S(1)} %get-tuple-element.182.refs_13_), channel_id=1, source_target_pairs={{16,0},{17,1},{18,2},{19,3},{20,4},{21,5},{22,6},{23,7},{24,8},{25... | collective-permute-start | bytes 12296 | tf_op jit(solution)/shard_map/ppermute | solution.py:701
  92.9 1.3 %collective-permute-start.24 = (f32[8,128]{1,0:T(8,128)S(1)}, f32[8,128]{1,0:T(8,128)S(1)}, u32[]{:S(2)}, u32[]{:S(2)}) collective-permute-start(f32[8,128]{1,0:T(8,128)S(1)} %get-tuple-element.182.refs_13_), channel_id=1, source_target_pairs={{8,0},{9,1},{10,2},{11,3},{12,4},{13,5},{14,6},{15,7},{16,8},{17,9... | collective-permute-start | bytes 12296 | tf_op jit(solution)/shard_map/ppermute | solution.py:701
  94.2 2.0 %finish.5 = (bf16[256,2560]{1,0:T(8,128)(2,1)}, bf16[256,128]{1,0:T(8,128)(2,1)}, bf16[256,128]{1,0:T(8,128)(2,1)}, f32[40,256]{1,0:T(8,128)S(1)}, f32[8,128]{1,0:T(8,128)}) custom-call(bf16[256,2560]{1,0:T(8,128)(2,1)S(1)} %copy-done, bf16[256,2560]{1,0:T(8,128)(2,1)S(1)} %copy-done.1, ...), custom_call_target="tpu_custom_call", output_to_operand_aliasing={{0}: (12, {})} | custom-call | flops 1 | bytes 1 | tf_op jit(solution)/shard_map/finish/pallas_call | solution.py:611
  96.2 0.5 collective-permute-done.26.refs_3_
  96.7 0.4 collective-permute-done.25.refs_2_
  97.1 1.3 %collective-permute-done.24.refs_1_ = f32[8,128]{1,0:T(8,128)S(1)} collective-permute-done((f32[8,128]{1,0:T(8,128)S(1)}, f32[8,128]{1,0:T(8,128)S(1)}, u32[]{:S(2)}, u32[]{:S(2)}) %collective-permute-start.24) | collective-permute-done | bytes 4128 | tf_op jit(solution)/shard_map/ppermute | solution.py:701
  98.4 0.8 add_later.1
  (40 shorter events, 0.4 us)
Async XLA Ops:
  4.4 4.3 %collective-permute-start.1 = (f32[1288,128]{1,0:T(8,128)}, f32[1288,128]{1,0:T(8,128)S(1)}, u32[]{:S(2)}, u32[]{:S(2)}) collective-permute-start(f32[1288,128]{1,0:T(8,128)} %get-tuple-element.100), channel_id=1, source_target_pairs={{0,1},{1,0},{2,3},{3,2},{4,5},{5,4},{6,7},{7,6},{8,9},{9,8},{10,11... | collective-permute-start | bytes 1978376 | tf_op jit(solution)/shard_map/ppermute | solution.py:701
  4.9 3.8 %copy-start.8 = (f32[1280,128]{1,0:T(8,128)S(1)}, f32[1280,128]{1,0:T(8,128)}, u32[]{:S(2)}) copy-start(f32[1280,128]{1,0:T(8,128)} %get-tuple-element.101.refs_1_) | copy-start | bytes 1966084
  4.9 3.8 %copy-start.10 = (f32[8,128]{1,0:T(8,128)S(1)}, f32[8,128]{1,0:T(8,128)}, u32[]{:S(2)}) copy-start(f32[8,128]{1,0:T(8,128)} %get-tuple-element.98.refs_4_.refs_3_) | copy-start | bytes 12292
  4.9 3.8 %copy-start.12 = (f32[10,128]{1,0:T(8,128)S(1)}, f32[10,128]{1,0:T(8,128)}, u32[]{:S(2)}) copy-start(f32[10,128]{1,0:T(8,128)} %get-tuple-element.102.refs_2_) | copy-start | bytes 15364
  4.9 7.0 %copy-start.1 = (bf16[256,2560]{1,0:T(8,128)(2,1)S(1)}, bf16[256,2560]{1,0:T(8,128)(2,1)}, u32[]{:S(2)}) copy-start(bf16[256,2560]{1,0:T(8,128)(2,1)} %refs_1_.15) | copy-start | bytes 3932164
  4.9 7.0 %copy-start.2 = (bf16[256,128]{1,0:T(8,128)(2,1)S(1)}, bf16[256,128]{1,0:T(8,128)(2,1)}, u32[]{:S(2)}) copy-start(bf16[256,128]{1,0:T(8,128)(2,1)} %refs_2_.15) | copy-start | bytes 196612
  4.9 7.0 %copy-start.3 = (bf16[256,128]{1,0:T(8,128)(2,1)S(1)}, bf16[256,128]{1,0:T(8,128)(2,1)}, u32[]{:S(2)}) copy-start(bf16[256,128]{1,0:T(8,128)(2,1)} %refs_3_.15) | copy-start | bytes 196612
  5.0 7.0 %copy-start.4 = (bf16[256,128]{1,0:T(8,128)(2,1)S(1)}, bf16[256,128]{1,0:T(8,128)(2,1)}, u32[]{:S(2)}) copy-start(bf16[256,128]{1,0:T(8,128)(2,1)} %get-tuple-element.96.refs_5_.refs_7_.refs_4_) | copy-start | bytes 196612
  5.0 7.0 %copy-start.5 = (bf16[256,128]{1,0:T(8,128)(2,1)S(1)}, bf16[256,128]{1,0:T(8,128)(2,1)}, u32[]{:S(2)}) copy-start(bf16[256,128]{1,0:T(8,128)(2,1)} %get-tuple-element.97.refs_6_.refs_8_.refs_5_) | copy-start | bytes 196612
  5.0 7.0 %copy-start.6 = (f32[256,128]{1,0:T(8,128)S(1)}, f32[256,128]{1,0:T(8,128)}, u32[]{:S(2)}) copy-start(f32[256,128]{1,0:T(8,128)} %get-tuple-element.104.refs_6_) | copy-start | bytes 393220
  5.0 7.0 %copy-start.9 = (f32[40,256]{1,0:T(8,128)S(1)}, f32[40,256]{1,0:T(8,128)}, u32[]{:S(2)}) copy-start(f32[40,256]{1,0:T(8,128)} %refs_5_.5) | copy-start | bytes 122884
  8.6 3.4 %copy-start = (bf16[256,2560]{1,0:T(8,128)(2,1)S(1)}, bf16[256,2560]{1,0:T(8,128)(2,1)}, u32[]{:S(2)}) copy-start(bf16[256,2560]{1,0:T(8,128)(2,1)} %refs_0_.9) | copy-start | bytes 3932164
  8.6 8.5 %collective-permute-start = (f32[1288,128]{1,0:T(8,128)}, f32[1288,128]{1,0:T(8,128)S(1)}, u32[]{:S(2)}, u32[]{:S(2)}) collective-permute-start(f32[1288,128]{1,0:T(8,128)} %get-tuple-element.99), channel_id=1, source_target_pairs={{0,1},{1,0},{2,3},{3,2},{4,5},{5,4},{6,7},{7,6},{8,9},{9,8},{10,11... | collective-permute-start | bytes 1978376 | tf_op jit(solution)/shard_map/ppermute | solution.py:701
  8.9 11.5 %collective-permute-start.4 = (f32[656,128]{1,0:T(8,128)S(1)}, f32[656,128]{1,0:T(8,128)S(1)}, u32[]{:S(2)}, u32[]{:S(2)}) collective-permute-start(f32[656,128]{1,0:T(8,128)S(1)} %get-tuple-element.103.refs_0_.refs_1_), channel_id=1, source_target_pairs={{0,2},{1,3},{2,0},{3,1},{4,6},{5,7},{6,4},{7,5},{8,10},{9,11},{10,... | collective-permute-start | bytes 1007624 | tf_op jit(solution)/shard_map/ppermute | solution.py:701
  12.0 5.1 %copy-start.7 = (f32[1280,128]{1,0:T(8,128)S(1)}, f32[1280,128]{1,0:T(8,128)}, u32[]{:S(2)}) copy-start(f32[1280,128]{1,0:T(8,128)} %get-tuple-element.111.refs_1_) | copy-start | bytes 1966084
  12.0 5.1 %copy-start.11 = (f32[10,128]{1,0:T(8,128)S(1)}, f32[10,128]{1,0:T(8,128)}, u32[]{:S(2)}) copy-start(f32[10,128]{1,0:T(8,128)} %get-tuple-element.112.refs_2_) | copy-start | bytes 15364
  17.2 17.1 %collective-permute-start.2 = (f32[656,128]{1,0:T(8,128)S(1)}, f32[656,128]{1,0:T(8,128)S(1)}, u32[]{:S(2)}, u32[]{:S(2)}) collective-permute-start(f32[656,128]{1,0:T(8,128)S(1)} %get-tuple-element.114.refs_1_), channel_id=1, source_target_pairs={{0,2},{1,3},{2,0},{3,1},{4,6},{5,7},{6,4},{7,5},{8,10},{9,11},{10,... | collective-permute-start | bytes 1007624 | tf_op jit(solution)/shard_map/ppermute | solution.py:701
  20.6 9.6 %collective-permute-start.5 = (f32[336,128]{1,0:T(8,128)S(1)}, f32[336,128]{1,0:T(8,128)S(1)}, u32[]{:S(2)}, u32[]{:S(2)}) collective-permute-start(f32[336,128]{1,0:T(8,128)S(1)} %get-tuple-element.118.refs_0_.refs_1_), channel_id=1, source_target_pairs={{0,4},{1,5},{2,6},{3,7},{4,0},{5,1},{6,2},{7,3},{8,12},{9,13},{10,... | collective-permute-start | bytes 516104 | tf_op jit(solution)/shard_map/ppermute | solution.py:701
  30.4 8.3 %collective-permute-start.8 = (f32[328,128]{1,0:T(8,128)S(1)}, f32[328,128]{1,0:T(8,128)S(1)}, u32[]{:S(2)}, u32[]{:S(2)}) collective-permute-start(f32[328,128]{1,0:T(8,128)S(1)} %up.6.refs_0_), channel_id=1, source_target_pairs={{1,25},{3,27},{5,29},{7,31},{24,0},{26,2},{28,4},{30,6}} | collective-permute-start | bytes 503816 | tf_op jit(solution)/shard_map/ppermute | solution.py:701
  31.7 8.7 %collective-permute-start.7 = (f32[328,128]{1,0:T(8,128)S(1)}, f32[328,128]{1,0:T(8,128)S(1)}, u32[]{:S(2)}, u32[]{:S(2)}) collective-permute-start(f32[328,128]{1,0:T(8,128)S(1)} %up.6.refs_0_), channel_id=1, source_target_pairs={{1,17},{3,19},{5,21},{7,23},{9,25},{11,27},{13,29},{15,31},{16,0},... | collective-permute-start | bytes 503816 | tf_op jit(solution)/shard_map/ppermute | solution.py:701
  33.0 8.9 %collective-permute-start.6 = (f32[328,128]{1,0:T(8,128)S(1)}, f32[328,128]{1,0:T(8,128)S(1)}, u32[]{:S(2)}, u32[]{:S(2)}) collective-permute-start(f32[328,128]{1,0:T(8,128)S(1)} %up.6.refs_0_), channel_id=1, source_target_pairs={{1,9},{3,11},{5,13},{7,15},{8,0},{9,17},{10,2},{11,19},{12,4},{13,... | collective-permute-start | bytes 503816 | tf_op jit(solution)/shard_map/ppermute | solution.py:701
  34.6 13.5 %collective-permute-start.3 = (f32[336,128]{1,0:T(8,128)S(1)}, f32[336,128]{1,0:T(8,128)S(1)}, u32[]{:S(2)}, u32[]{:S(2)}) collective-permute-start(f32[336,128]{1,0:T(8,128)S(1)} %get-tuple-element.115.refs_1_), channel_id=1, source_target_pairs={{0,4},{1,5},{2,6},{3,7},{4,0},{5,1},{6,2},{7,3},{8,12},{9,13},{10,... | collective-permute-start | bytes 516104 | tf_op jit(solution)/shard_map/ppermute | solution.py:701
  42.2 11.8 %collective-permute-start.9 = (f32[336,128]{1,0:T(8,128)S(1)}, f32[336,128]{1,0:T(8,128)S(1)}, u32[]{:S(2)}, u32[]{:S(2)}) collective-permute-start(f32[336,128]{1,0:T(8,128)S(1)} %get-tuple-element.148), channel_id=1, source_target_pairs={{0,4},{1,5},{2,6},{3,7},{4,0},{5,1},{6,2},{7,3},{8,12},{9,13},{10,... | collective-permute-start | bytes 516104 | tf_op jit(solution)/shard_map/ppermute | solution.py:701
  48.3 9.7 %collective-permute-start.13 = (f32[328,128]{1,0:T(8,128)S(1)}, f32[328,128]{1,0:T(8,128)S(1)}, u32[]{:S(2)}, u32[]{:S(2)}) collective-permute-start(f32[328,128]{1,0:T(8,128)S(1)} %up.7), channel_id=1, source_target_pairs={{1,25},{3,27},{5,29},{7,31},{24,0},{26,2},{28,4},{30,6}} | collective-permute-start | bytes 503816 | tf_op jit(solution)/shard_map/ppermute | solution.py:701
  49.6 9.1 %collective-permute-start.12 = (f32[328,128]{1,0:T(8,128)S(1)}, f32[328,128]{1,0:T(8,128)S(1)}, u32[]{:S(2)}, u32[]{:S(2)}) collective-permute-start(f32[328,128]{1,0:T(8,128)S(1)} %up.7), channel_id=1, source_target_pairs={{1,17},{3,19},{5,21},{7,23},{9,25},{11,27},{13,29},{15,31},{16,0},... | collective-permute-start | bytes 503816 | tf_op jit(solution)/shard_map/ppermute | solution.py:701
  50.9 10.6 %collective-permute-start.11 = (f32[328,128]{1,0:T(8,128)S(1)}, f32[328,128]{1,0:T(8,128)S(1)}, u32[]{:S(2)}, u32[]{:S(2)}) collective-permute-start(f32[328,128]{1,0:T(8,128)S(1)} %up.7), channel_id=1, source_target_pairs={{1,9},{3,11},{5,13},{7,15},{8,0},{9,17},{10,2},{11,19},{12,4},{13,... | collective-permute-start | bytes 503816 | tf_op jit(solution)/shard_map/ppermute | solution.py:701
  54.3 17.6 %collective-permute-start.10 = (f32[656,128]{1,0:T(8,128)S(1)}, f32[656,128]{1,0:T(8,128)S(1)}, u32[]{:S(2)}, u32[]{:S(2)}) collective-permute-start(f32[656,128]{1,0:T(8,128)S(1)} %get-tuple-element.150), channel_id=1, source_target_pairs={{0,2},{1,3},{2,0},{3,1},{4,6},{5,7},{6,4},{7,5},{8,10},{9,11},{10,... | collective-permute-start | bytes 1007624 | tf_op jit(solution)/shard_map/ppermute | solution.py:701
  61.8 10.1 %collective-permute-start.14 = (f32[336,128]{1,0:T(8,128)S(1)}, f32[336,128]{1,0:T(8,128)S(1)}, u32[]{:S(2)}, u32[]{:S(2)}) collective-permute-start(f32[336,128]{1,0:T(8,128)S(1)} %get-tuple-element.153), channel_id=1, source_target_pairs={{0,4},{1,5},{2,6},{3,7},{4,0},{5,1},{6,2},{7,3},{8,12},{9,13},{10,... | collective-permute-start | bytes 516104 | tf_op jit(solution)/shard_map/ppermute | solution.py:701
  72.1 7.7 %collective-permute-start.17 = (f32[656,128]{1,0:T(8,128)S(1)}, f32[656,128]{1,0:T(8,128)S(1)}, u32[]{:S(2)}, u32[]{:S(2)}) collective-permute-start(f32[656,128]{1,0:T(8,128)S(1)} %get-tuple-element.165), channel_id=1, source_target_pairs={{0,2},{1,3},{2,0},{3,1},{4,6},{5,7},{6,4},{7,5},{8,10},{9,11},{10,... | collective-permute-start | bytes 1007624 | tf_op jit(solution)/shard_map/ppermute | solution.py:701
  72.3 1.7 %collective-permute-start.15 = (f32[640,128]{1,0:T(8,128)S(1)}, f32[640,128]{1,0:T(8,128)S(1)}, u32[]{:S(2)}, u32[]{:S(2)}) collective-permute-start(f32[640,128]{1,0:T(8,128)S(1)} %get-tuple-element.155.refs_4_), channel_id=1, source_target_pairs={{0,1},{1,0},{2,3},{3,2},{4,5},{5,4},{6,7},{7,6},{8,9},{9,8},{10,11... | collective-permute-start | bytes 983048 | tf_op jit(solution)/shard_map/ppermute | solution.py:701
  72.3 2.1 %collective-permute-start.16 = (f32[640,128]{1,0:T(8,128)S(1)}, f32[640,128]{1,0:T(8,128)S(1)}, u32[]{:S(2)}, u32[]{:S(2)}) collective-permute-start(f32[640,128]{1,0:T(8,128)S(1)} %get-tuple-element.156.refs_5_), channel_id=1, source_target_pairs={{0,1},{1,0},{2,3},{3,2},{4,5},{5,4},{6,7},{7,6},{8,9},{9,8},{10,11... | collective-permute-start | bytes 983048 | tf_op jit(solution)/shard_map/ppermute | solution.py:701
  72.8 6.1 %collective-permute-start.18 = (f32[640,128]{1,0:T(8,128)S(1)}, f32[640,128]{1,0:T(8,128)S(1)}, u32[]{:S(2)}, u32[]{:S(2)}) collective-permute-start(f32[640,128]{1,0:T(8,128)S(1)} %get-tuple-element.166.refs_4_), channel_id=1, source_target_pairs={{0,1},{1,0},{2,3},{3,2},{4,5},{5,4},{6,7},{7,6},{8,9},{9,8},{10,11... | collective-permute-start | bytes 983048 | tf_op jit(solution)/shard_map/ppermute | solution.py:701
  79.8 1.6 %collective-permute-start.19 = (f32[656,128]{1,0:T(8,128)S(1)}, f32[656,128]{1,0:T(8,128)S(1)}, u32[]{:S(2)}, u32[]{:S(2)}) collective-permute-start(f32[656,128]{1,0:T(8,128)S(1)} %collective-permute-done.17.refs_5_), channel_id=1, source_target_pairs={{0,1},{1,0},{2,3},{3,2},{4,5},{5,4},{6,7},{7,6},{8,9},{9,8},{10,11... | collective-permute-start | bytes 1007624 | tf_op jit(solution)/shard_map/ppermute | solution.py:701
  82.2 1.2 %collective-permute-start.20 = (f32[8,128]{1,0:T(8,128)S(1)}, f32[8,128]{1,0:T(8,128)S(1)}, u32[]{:S(2)}, u32[]{:S(2)}) collective-permute-start(f32[8,128]{1,0:T(8,128)S(1)} %get-tuple-element.174.total_ref), channel_id=1, source_target_pairs={{0,1},{1,0},{2,3},{3,2},{4,5},{5,4},{6,7},{7,6},{8,9},{9,8},{10,11... | collective-permute-start | bytes 12296 | tf_op jit(solution)/shard_map/ppermute | solution.py:701
  83.5 5.9 %collective-permute-start.23 = (f32[8,128]{1,0:T(8,128)S(1)}, f32[8,128]{1,0:T(8,128)S(1)}, u32[]{:S(2)}, u32[]{:S(2)}) collective-permute-start(f32[8,128]{1,0:T(8,128)S(1)} %get-tuple-element.175.refs_13_.total_ref), channel_id=1, source_target_pairs={{0,6},{1,7},{2,4},{3,5},{4,2},{5,3},{6,0},{7,1},{8,14},{9,15},{10,... | collective-permute-start | bytes 12296 | tf_op jit(solution)/shard_map/ppermute | solution.py:701
  85.5 4.5 %collective-permute-start.22 = (f32[8,128]{1,0:T(8,128)S(1)}, f32[8,128]{1,0:T(8,128)S(1)}, u32[]{:S(2)}, u32[]{:S(2)}) collective-permute-start(f32[8,128]{1,0:T(8,128)S(1)} %get-tuple-element.175.refs_13_.total_ref), channel_id=1, source_target_pairs={{0,4},{1,5},{2,6},{3,7},{4,0},{5,1},{6,2},{7,3},{8,12},{9,13},{10,... | collective-permute-start | bytes 12296 | tf_op jit(solution)/shard_map/ppermute | solution.py:701
  86.7 3.6 %collective-permute-start.21 = (f32[8,128]{1,0:T(8,128)S(1)}, f32[8,128]{1,0:T(8,128)S(1)}, u32[]{:S(2)}, u32[]{:S(2)}) collective-permute-start(f32[8,128]{1,0:T(8,128)S(1)} %get-tuple-element.175.refs_13_.total_ref), channel_id=1, source_target_pairs={{0,2},{1,3},{2,0},{3,1},{4,6},{5,7},{6,4},{7,5},{8,10},{9,11},{10,... | collective-permute-start | bytes 12296 | tf_op jit(solution)/shard_map/ppermute | solution.py:701
  90.3 6.4 %collective-permute-start.26 = (f32[8,128]{1,0:T(8,128)S(1)}, f32[8,128]{1,0:T(8,128)S(1)}, u32[]{:S(2)}, u32[]{:S(2)}) collective-permute-start(f32[8,128]{1,0:T(8,128)S(1)} %get-tuple-element.182.refs_13_), channel_id=1, source_target_pairs={{24,0},{25,1},{26,2},{27,3},{28,4},{29,5},{30,6},{31,7}} | collective-permute-start | bytes 12296 | tf_op jit(solution)/shard_map/ppermute | solution.py:701
  91.6 5.5 %collective-permute-start.25 = (f32[8,128]{1,0:T(8,128)S(1)}, f32[8,128]{1,0:T(8,128)S(1)}, u32[]{:S(2)}, u32[]{:S(2)}) collective-permute-start(f32[8,128]{1,0:T(8,128)S(1)} %get-tuple-element.182.refs_13_), channel_id=1, source_target_pairs={{16,0},{17,1},{18,2},{19,3},{20,4},{21,5},{22,6},{23,7},{24,8},{25... | collective-permute-start | bytes 12296 | tf_op jit(solution)/shard_map/ppermute | solution.py:701
  92.9 5.5 %collective-permute-start.24 = (f32[8,128]{1,0:T(8,128)S(1)}, f32[8,128]{1,0:T(8,128)S(1)}, u32[]{:S(2)}, u32[]{:S(2)}) collective-permute-start(f32[8,128]{1,0:T(8,128)S(1)} %get-tuple-element.182.refs_13_), channel_id=1, source_target_pairs={{8,0},{9,1},{10,2},{11,3},{12,4},{13,5},{14,6},{15,7},{16,8},{17,9... | collective-permute-start | bytes 12296 | tf_op jit(solution)/shard_map/ppermute | solution.py:701

commit v16 on v15

--- a/solution.py
+++ b/solution.py
@@ -772,10 +772,10 @@
             ready += more
             if step == 0:
                 first[1], block = lax.optimization_barrier((first[1], block))
-            elif step == 1:
-                waiting[0], block = lax.optimization_barrier((waiting[0], block))
             else:
-                waiting[1], block = lax.optimization_barrier((waiting[1], block))
+                waiting[0], waiting[1], block = lax.optimization_barrier(
+                    (waiting[0], waiting[1], block)
+                )
         elif levels + 1 < step < rounds - 1:
             waiting[0], waiting[1] = lax.optimization_barrier((waiting[0], waiting[1]))
     dx, state_own, back_own, change, db, dc = block

time: 99.5 us -> 96.3 us (0.968)
  starting transfers between devices: 33.4 us -> 30.2 us
    ppermute x27, starting transfers between devices: 33.4 us -> 30.2 us  [move(): return lax.ppermute(value, ('grp', 'seq'), pairs)]
  transfers between devices with their start and end apart: 27 -> 27, of which waited for: 20 -> 19; matrix products, arithmetic and copies ran while one was open for 0% -> 0% of each run, Pallas kernels for 26% -> 27%
where the time goes in v16:
time: 96.3 us; the launch traced here: 95.7 us
  waiting for transfers between devices  32.8 us (34%)
  Pallas kernels  31.6 us (33%)
  starting transfers between devices  30.2 us (31%)
  between operations  0.99 us (1%)
    ppermute x27, waiting for transfers between devices, move(): return lax.ppermute(value, ('grp', 'seq'), pairs)  32.8 us
    ppermute x27, starting transfers between devices, move(): return lax.ppermute(value, ('grp', 'seq'), pairs)  30.2 us
    pallas_call x3, Pallas kernels, intra(): pl.pallas_call(lambda *refs: intra_kernel(heads, wide // heads, start, la...  12.5 us
    pallas_call x2, Pallas kernels, summary(): pl.pallas_call(lambda *refs: summary_kernel(heads, chips, half, *refs), g...  7.38 us
    pallas_call x3, Pallas kernels, finish(): pl.pallas_call(lambda *refs: finish_kernel(heads, start, steps, last, *re...  7.27 us
  transfers between devices with their start and end apart: 27, of which 19 were waited for; matrix products, arithmetic and copies ran while one was open for 0% of the time, Pallas kernels for 27%

profile of v16, /device:TPU:0, one launch (start us, length us, event | category | flops | bytes accessed | tf_op | source)
XLA Modules:
  0.0 95.7 jit_solution(7089204007104064537)
XLA Ops:
  0.6 3.8 %summary.2 = (f32[1288,128]{1,0:T(8,128)}, f32[1280,128]{1,0:T(8,128)}, f32[10,128]{1,0:T(8,128)}, f32[8,128]{1,0:T(8,128)}, f32[256,128]{1,0:T(8,128)}, /*index...) custom-call(bf16[256,2560]{1,0:T(8,128)(2,1)} %refs_0_.9, bf16[256,2560]{1,0:T(8,128)(2,1)} %refs_1_.15, ...), custom_call_target="tpu_custom_call" | custom-call | flops 1 | bytes 1 | tf_op jit(solution)/shard_map/summary/pallas_call | solution.py:195
  4.4 0.5 collective-permute-start
  5.0 3.6 %summary.3 = (f32[1288,128]{1,0:T(8,128)}, f32[1280,128]{1,0:T(8,128)}, f32[10,128]{1,0:T(8,128)}) custom-call(bf16[256,2560]{1,0:T(8,128)(2,1)} %refs_0_.9, bf16[256,2560]{1,0:T(8,128)(2,1)} %refs_1_.15, bf16[256,128]{1,0:T(8,128)(2,1)} %refs_2_.15, bf16[256,128]{1,0:T(8,128)(2,1)} %refs_3_.15, f32[8,128]{1,0:T(8,128)} %get-tuple-element.105.refs_3_.refs_4_, ...), custom_call_target="tpu_custom_call" | custom-call | flops 1 | bytes 1 | tf_op jit(solution)/shard_map/summary/pallas_call | solution.py:195
  8.6 0.1 collective-permute-start.3
  8.8 0.1 combine.2
  8.9 3.1 %collective-permute-start.1 = (f32[656,128]{1,0:T(8,128)S(1)}, f32[656,128]{1,0:T(8,128)S(1)}, u32[]{:S(2)}, u32[]{:S(2)}) collective-permute-start(f32[656,128]{1,0:T(8,128)S(1)} %get-tuple-element.107.refs_1_.refs_0_), channel_id=1, source_target_pairs={{0,2},{1,3},{2,0},{3,1},{4,6},{5,7},{6,4},{7,5},{8,10},{9,11},{10,... | collective-permute-start | bytes 1007624 | tf_op jit(solution)/shard_map/ppermute | solution.py:701
  12.0 5.1 %intra.3 = (f32[256,2560]{1,0:T(8,128)S(1)}, f32[128,2560]{1,0:T(8,128)S(1)}, f32[128,2560]{1,0:T(8,128)S(1)}, f32[256,128]{1,0:T(8,128)S(1)}, f32[256,256]{1,0:T(8,128)S(1)}) custom-call(f32[656,128]{1,0:T(8,128)S(1)} %get-tuple-element.107.refs_1_.refs_0_, bf16[256,2560]{1,0:T(8,128)(2,1)S(1)} %copy-done, bf16[256,2560]{1,0:T(8,128)(2,1)S(1)} %copy-done.1, ...), custom_call_target="tpu_custom_call" | custom-call | flops 1 | bytes 1 | tf_op jit(solution)/shard_map/intra/pallas_call | solution.py:441
  17.1 0.1 combine.3
  17.2 0.5 collective-permute-start.4
  17.8 2.6 %collective-permute-done.1.refs_2_ = f32[656,128]{1,0:T(8,128)S(1)} collective-permute-done((f32[656,128]{1,0:T(8,128)S(1)}, f32[656,128]{1,0:T(8,128)S(1)}, u32[]{:S(2)}, u32[]{:S(2)}) %collective-permute-start.1) | collective-permute-done | bytes 335904 | tf_op jit(solution)/shard_map/ppermute | solution.py:701
  20.4 0.2 up.4
  20.6 3.0 %collective-permute-start.2 = (f32[336,128]{1,0:T(8,128)S(1)}, f32[336,128]{1,0:T(8,128)S(1)}, u32[]{:S(2)}, u32[]{:S(2)}) collective-permute-start(f32[336,128]{1,0:T(8,128)S(1)} %get-tuple-element.109.refs_0_.refs_1_), channel_id=1, source_target_pairs={{0,4},{1,5},{2,6},{3,7},{4,0},{5,1},{6,2},{7,3},{8,12},{9,13},{10,... | collective-permute-start | bytes 516104 | tf_op jit(solution)/shard_map/ppermute | solution.py:701
  23.6 5.0 %intra.4 = (f32[256,2560]{1,0:T(8,128)S(1)}, f32[128,2560]{1,0:T(8,128)S(1)}, f32[128,2560]{1,0:T(8,128)S(1)}, f32[256,128]{1,0:T(8,128)S(1)}, f32[256,256]{1,0:T(8,128)S(1)}) custom-call(f32[336,128]{1,0:T(8,128)S(1)} %get-tuple-element.109.refs_0_.refs_1_, ...), custom_call_target="tpu_custom_call", output_to_operand_aliasing={{0}: (9, {}), {1}: (10, {}), {2}: (11, {})} | custom-call | flops 1 | bytes 1 | tf_op jit(solution)/shard_map/intra/pallas_call | solution.py:441
  28.6 2.3 %collective-permute-done.4.refs_2_ = f32[656,128]{1,0:T(8,128)S(1)} collective-permute-done((f32[656,128]{1,0:T(8,128)S(1)}, f32[656,128]{1,0:T(8,128)S(1)}, u32[]{:S(2)}, u32[]{:S(2)}) %collective-permute-start.4) | collective-permute-done | bytes 335904 | tf_op jit(solution)/shard_map/ppermute | solution.py:701
  30.9 0.2 up.6
  31.2 2.8 %collective-permute-start.8 = (f32[336,128]{1,0:T(8,128)S(1)}, f32[336,128]{1,0:T(8,128)S(1)}, u32[]{:S(2)}, u32[]{:S(2)}) collective-permute-start(f32[336,128]{1,0:T(8,128)S(1)} %get-tuple-element.134.refs_1_), channel_id=1, source_target_pairs={{0,4},{1,5},{2,6},{3,7},{4,0},{5,1},{6,2},{7,3},{8,12},{9,13},{10,... | collective-permute-start | bytes 516104 | tf_op jit(solution)/shard_map/ppermute | solution.py:701
  34.0 0.2 up.5.refs_0_
  34.2 1.3 %collective-permute-start.7 = (f32[328,128]{1,0:T(8,128)S(1)}, f32[328,128]{1,0:T(8,128)S(1)}, u32[]{:S(2)}, u32[]{:S(2)}) collective-permute-start(f32[328,128]{1,0:T(8,128)S(1)} %up.5.refs_0_), channel_id=1, source_target_pairs={{1,25},{3,27},{5,29},{7,31},{24,0},{26,2},{28,4},{30,6}} | collective-permute-start | bytes 503816 | tf_op jit(solution)/shard_map/ppermute | solution.py:701
  35.5 1.3 %collective-permute-start.6 = (f32[328,128]{1,0:T(8,128)S(1)}, f32[328,128]{1,0:T(8,128)S(1)}, u32[]{:S(2)}, u32[]{:S(2)}) collective-permute-start(f32[328,128]{1,0:T(8,128)S(1)} %up.5.refs_0_), channel_id=1, source_target_pairs={{1,17},{3,19},{5,21},{7,23},{9,25},{11,27},{13,29},{15,31},{16,0},... | collective-permute-start | bytes 503816 | tf_op jit(solution)/shard_map/ppermute | solution.py:701
  36.8 1.3 %collective-permute-start.5 = (f32[328,128]{1,0:T(8,128)S(1)}, f32[328,128]{1,0:T(8,128)S(1)}, u32[]{:S(2)}, u32[]{:S(2)}) collective-permute-start(f32[328,128]{1,0:T(8,128)S(1)} %up.5.refs_0_), channel_id=1, source_target_pairs={{1,9},{3,11},{5,13},{7,15},{8,0},{9,17},{10,2},{11,19},{12,4},{13,... | collective-permute-start | bytes 503816 | tf_op jit(solution)/shard_map/ppermute | solution.py:701
  38.1 2.5 %intra.5 = (f32[256,2560]{1,0:T(8,128)S(1)}, f32[128,2560]{1,0:T(8,128)S(1)}, f32[128,2560]{1,0:T(8,128)S(1)}, f32[256,128]{1,0:T(8,128)S(1)}, f32[256,128]{1,0:T(8,128)S(1)}, /*index=5*/f32[256,128]{1,0:T(8,128)S(1)}) custom-call(f32[328,128]{1,0:T(8,128)S(1)} %up.5.refs_0_, ...), custom_call_target="tpu_custom_call", output_to_operand_aliasing={{0}: (9, {}), {1}: (10, {}), {2}: (11, {})} | custom-call | flops 1 | bytes 1 | tf_op jit(solution)/shard_map/intra/pallas_call | solution.py:441
  40.6 1.9 %collective-permute-done.7.refs_5_ = f32[328,128]{1,0:T(8,128)S(1)} collective-permute-done((f32[328,128]{1,0:T(8,128)S(1)}, f32[328,128]{1,0:T(8,128)S(1)}, u32[]{:S(2)}, u32[]{:S(2)}) %collective-permute-start.7) | collective-permute-done | bytes 167968 | tf_op jit(solution)/shard_map/ppermute | solution.py:701
  42.4 1.7 %collective-permute-done.6.refs_4_ = f32[328,128]{1,0:T(8,128)S(1)} collective-permute-done((f32[328,128]{1,0:T(8,128)S(1)}, f32[328,128]{1,0:T(8,128)S(1)}, u32[]{:S(2)}, u32[]{:S(2)}) %collective-permute-start.6) | collective-permute-done | bytes 167968 | tf_op jit(solution)/shard_map/ppermute | solution.py:701
  44.1 1.2 %collective-permute-done.5.refs_3_ = f32[328,128]{1,0:T(8,128)S(1)} collective-permute-done((f32[328,128]{1,0:T(8,128)S(1)}, f32[328,128]{1,0:T(8,128)S(1)}, u32[]{:S(2)}, u32[]{:S(2)}) %collective-permute-start.5) | collective-permute-done | bytes 167968 | tf_op jit(solution)/shard_map/ppermute | solution.py:701
  45.3 0.2 down.4
  45.6 0.8 collective-permute-start.9
  46.3 0.2 up.7
  46.5 1.3 %collective-permute-start.13 = (f32[328,128]{1,0:T(8,128)S(1)}, f32[328,128]{1,0:T(8,128)S(1)}, u32[]{:S(2)}, u32[]{:S(2)}) collective-permute-start(f32[328,128]{1,0:T(8,128)S(1)} %up.7), channel_id=1, source_target_pairs={{1,25},{3,27},{5,29},{7,31},{24,0},{26,2},{28,4},{30,6}} | collective-permute-start | bytes 503816 | tf_op jit(solution)/shard_map/ppermute | solution.py:701
  47.8 1.3 %collective-permute-start.12 = (f32[328,128]{1,0:T(8,128)S(1)}, f32[328,128]{1,0:T(8,128)S(1)}, u32[]{:S(2)}, u32[]{:S(2)}) collective-permute-start(f32[328,128]{1,0:T(8,128)S(1)} %up.7), channel_id=1, source_target_pairs={{1,17},{3,19},{5,21},{7,23},{9,25},{11,27},{13,29},{15,31},{16,0},... | collective-permute-start | bytes 503816 | tf_op jit(solution)/shard_map/ppermute | solution.py:701
  49.1 1.5 %collective-permute-start.11 = (f32[328,128]{1,0:T(8,128)S(1)}, f32[328,128]{1,0:T(8,128)S(1)}, u32[]{:S(2)}, u32[]{:S(2)}) collective-permute-start(f32[328,128]{1,0:T(8,128)S(1)} %up.7), channel_id=1, source_target_pairs={{1,9},{3,11},{5,13},{7,15},{8,0},{9,17},{10,2},{11,19},{12,4},{13,... | collective-permute-start | bytes 503816 | tf_op jit(solution)/shard_map/ppermute | solution.py:701
  50.6 3.7 %collective-permute-done.9.refs_4_ = f32[336,128]{1,0:T(8,128)S(1)} collective-permute-done((f32[336,128]{1,0:T(8,128)S(1)}, f32[336,128]{1,0:T(8,128)S(1)}, u32[]{:S(2)}, u32[]{:S(2)}) %collective-permute-start.9) | collective-permute-done | bytes 172064 | tf_op jit(solution)/shard_map/ppermute | solution.py:701
  54.3 0.2 down.5
  54.7 0.1 collective-permute-done.13.refs_5_
  54.8 1.7 %collective-permute-done.12.refs_4_ = f32[328,128]{1,0:T(8,128)S(1)} collective-permute-done((f32[328,128]{1,0:T(8,128)S(1)}, f32[328,128]{1,0:T(8,128)S(1)}, u32[]{:S(2)}, u32[]{:S(2)}) %collective-permute-start.12) | collective-permute-done | bytes 167968 | tf_op jit(solution)/shard_map/ppermute | solution.py:701
  56.5 0.6 collective-permute-done.11.refs_3_
  57.0 0.3 down.6
  57.3 1.9 %collective-permute-start.14 = (f32[336,128]{1,0:T(8,128)S(1)}, f32[336,128]{1,0:T(8,128)S(1)}, u32[]{:S(2)}, u32[]{:S(2)}) collective-permute-start(f32[336,128]{1,0:T(8,128)S(1)} %get-tuple-element.161), channel_id=1, source_target_pairs={{0,4},{1,5},{2,6},{3,7},{4,0},{5,1},{6,2},{7,3},{8,12},{9,13},{10,... | collective-permute-start | bytes 516104 | tf_op jit(solution)/shard_map/ppermute | solution.py:701
  59.2 7.7 %collective-permute-done.14.refs_4_ = f32[336,128]{1,0:T(8,128)S(1)} collective-permute-done((f32[336,128]{1,0:T(8,128)S(1)}, f32[336,128]{1,0:T(8,128)S(1)}, u32[]{:S(2)}, u32[]{:S(2)}) %collective-permute-start.14) | collective-permute-done | bytes 172064 | tf_op jit(solution)/shard_map/ppermute | solution.py:701
  66.9 0.2 down.7
  67.1 0.5 collective-permute-start.17
  67.7 0.5 collective-permute-start.16
  68.2 0.1 collective-permute-start.18
  68.3 1.0 %collective-permute-done.15.refs_6_ = f32[640,128]{1,0:T(8,128)S(1)} collective-permute-done((f32[640,128]{1,0:T(8,128)S(1)}, f32[640,128]{1,0:T(8,128)S(1)}, u32[]{:S(2)}, u32[]{:S(2)}) %collective-permute-start.15) | collective-permute-done | bytes 327712 | tf_op jit(solution)/shard_map/ppermute | solution.py:701
  69.4 0.5 collective-permute-done.16.refs_7_
  69.8 0.8 assemble.2
  70.6 3.8 %finish.3 = (bf16[256,2560]{1,0:T(8,128)(2,1)}, f32[256,128]{1,0:T(8,128)S(1)}, f32[256,128]{1,0:T(8,128)S(1)}, f32[256,128]{1,0:T(8,128)S(1)}, f32[8,128]{1,0:T(8,128)S(1)}) custom-call(bf16[256,2560]{1,0:T(8,128)(2,1)S(1)} %copy-done, bf16[256,2560]{1,0:T(8,128)(2,1)S(1)} %copy-done.1, bf16[256,128]{1,0:T(8,128)(2,1)S(1)} %copy-done.2, ...), custom_call_target="tpu_custom_call" | custom-call | flops 1 | bytes 1 | tf_op jit(solution)/shard_map/finish/pallas_call | solution.py:611
  74.4 0.4 collective-permute-done.17.refs_5_
  74.8 1.6 %collective-permute-done.19.refs_7_ = f32[656,128]{1,0:T(8,128)S(1)} collective-permute-done((f32[656,128]{1,0:T(8,128)S(1)}, f32[656,128]{1,0:T(8,128)S(1)}, u32[]{:S(2)}, u32[]{:S(2)}) %collective-permute-start.19) | collective-permute-done | bytes 335904 | tf_op jit(solution)/shard_map/ppermute | solution.py:701
  76.4 0.8 assemble.3
  77.3 0.2 collective-permute-start.20
  77.5 1.0 %collective-permute-done.20.got_ref = f32[8,128]{1,0:T(8,128)S(1)} collective-permute-done((f32[8,128]{1,0:T(8,128)S(1)}, f32[8,128]{1,0:T(8,128)S(1)}, u32[]{:S(2)}, u32[]{:S(2)}) %collective-permute-start.20) | collective-permute-done | bytes 4128 | tf_op jit(solution)/shard_map/ppermute | solution.py:701
  78.5 2.3 %collective-permute-start.23 = (f32[8,128]{1,0:T(8,128)S(1)}, f32[8,128]{1,0:T(8,128)S(1)}, u32[]{:S(2)}, u32[]{:S(2)}) collective-permute-start(f32[8,128]{1,0:T(8,128)S(1)} %get-tuple-element.183.refs_13_.total_ref), channel_id=1, source_target_pairs={{0,6},{1,7},{2,4},{3,5},{4,2},{5,3},{6,0},{7,1},{8,14},{9,15},{10,... | collective-permute-start | bytes 12296 | tf_op jit(solution)/shard_map/ppermute | solution.py:701
  80.8 0.3 collective-permute-start.22
  81.2 1.7 %collective-permute-start.21 = (f32[8,128]{1,0:T(8,128)S(1)}, f32[8,128]{1,0:T(8,128)S(1)}, u32[]{:S(2)}, u32[]{:S(2)}) collective-permute-start(f32[8,128]{1,0:T(8,128)S(1)} %get-tuple-element.183.refs_13_.total_ref), channel_id=1, source_target_pairs={{0,2},{1,3},{2,0},{3,1},{4,6},{5,7},{6,4},{7,5},{8,10},{9,11},{10,... | collective-permute-start | bytes 12296 | tf_op jit(solution)/shard_map/ppermute | solution.py:701
  82.9 1.5 %finish.4 = (bf16[256,2560]{1,0:T(8,128)(2,1)}, f32[256,128]{1,0:T(8,128)S(1)}, f32[256,128]{1,0:T(8,128)S(1)}, f32[256,128]{1,0:T(8,128)S(1)}, f32[8,128]{1,0:T(8,128)S(1)}) custom-call(bf16[256,2560]{1,0:T(8,128)(2,1)S(1)} %copy-done, bf16[256,2560]{1,0:T(8,128)(2,1)S(1)} %copy-done.1, ...), custom_call_target="tpu_custom_call", output_to_operand_aliasing={{0}: (12, {})} | custom-call | flops 1 | bytes 1 | tf_op jit(solution)/shard_map/finish/pallas_call | solution.py:611
  84.4 0.9 collective-permute-done.22.refs_1_
  85.4 1.3 %collective-permute-start.26 = (f32[8,128]{1,0:T(8,128)S(1)}, f32[8,128]{1,0:T(8,128)S(1)}, u32[]{:S(2)}, u32[]{:S(2)}) collective-permute-start(f32[8,128]{1,0:T(8,128)S(1)} %get-tuple-element.190.refs_13_), channel_id=1, source_target_pairs={{24,0},{25,1},{26,2},{27,3},{28,4},{29,5},{30,6},{31,7}} | collective-permute-start | bytes 12296 | tf_op jit(solution)/shard_map/ppermute | solution.py:701
  86.7 1.3 %collective-permute-start.25 = (f32[8,128]{1,0:T(8,128)S(1)}, f32[8,128]{1,0:T(8,128)S(1)}, u32[]{:S(2)}, u32[]{:S(2)}) collective-permute-start(f32[8,128]{1,0:T(8,128)S(1)} %get-tuple-element.190.refs_13_), channel_id=1, source_target_pairs={{16,0},{17,1},{18,2},{19,3},{20,4},{21,5},{22,6},{23,7},{24,8},{25... | collective-permute-start | bytes 12296 | tf_op jit(solution)/shard_map/ppermute | solution.py:701
  88.0 1.3 %collective-permute-start.24 = (f32[8,128]{1,0:T(8,128)S(1)}, f32[8,128]{1,0:T(8,128)S(1)}, u32[]{:S(2)}, u32[]{:S(2)}) collective-permute-start(f32[8,128]{1,0:T(8,128)S(1)} %get-tuple-element.190.refs_13_), channel_id=1, source_target_pairs={{8,0},{9,1},{10,2},{11,3},{12,4},{13,5},{14,6},{15,7},{16,8},{17,9... | collective-permute-start | bytes 12296 | tf_op jit(solution)/shard_map/ppermute | solution.py:701
  89.3 2.0 %finish.5 = (bf16[256,2560]{1,0:T(8,128)(2,1)}, bf16[256,128]{1,0:T(8,128)(2,1)}, bf16[256,128]{1,0:T(8,128)(2,1)}, f32[40,256]{1,0:T(8,128)S(1)}, f32[8,128]{1,0:T(8,128)}) custom-call(bf16[256,2560]{1,0:T(8,128)(2,1)S(1)} %copy-done, bf16[256,2560]{1,0:T(8,128)(2,1)S(1)} %copy-done.1, ...), custom_call_target="tpu_custom_call", output_to_operand_aliasing={{0}: (12, {})} | custom-call | flops 1 | bytes 1 | tf_op jit(solution)/shard_map/finish/pallas_call | solution.py:611
  91.2 0.5 collective-permute-done.26.refs_3_
  91.8 2.5 %collective-permute-done.25.refs_2_ = f32[8,128]{1,0:T(8,128)S(1)} collective-permute-done((f32[8,128]{1,0:T(8,128)S(1)}, f32[8,128]{1,0:T(8,128)S(1)}, u32[]{:S(2)}, u32[]{:S(2)}) %collective-permute-start.25) | collective-permute-done | bytes 4128 | tf_op jit(solution)/shard_map/ppermute | solution.py:701
  94.3 0.7 collective-permute-done.24.refs_1_
  94.9 0.8 add_later.1
  (40 shorter events, 0.3 us)
Async XLA Ops:
  4.4 4.3 %collective-permute-start = (f32[1288,128]{1,0:T(8,128)}, f32[1288,128]{1,0:T(8,128)S(1)}, u32[]{:S(2)}, u32[]{:S(2)}) collective-permute-start(f32[1288,128]{1,0:T(8,128)} %get-tuple-element.102), channel_id=1, source_target_pairs={{0,1},{1,0},{2,3},{3,2},{4,5},{5,4},{6,7},{7,6},{8,9},{9,8},{10,11... | collective-permute-start | bytes 1978376 | tf_op jit(solution)/shard_map/ppermute | solution.py:701
  4.9 3.8 %copy-start.8 = (f32[1280,128]{1,0:T(8,128)S(1)}, f32[1280,128]{1,0:T(8,128)}, u32[]{:S(2)}) copy-start(f32[1280,128]{1,0:T(8,128)} %get-tuple-element.103.refs_1_) | copy-start | bytes 1966084
  4.9 3.8 %copy-start.10 = (f32[8,128]{1,0:T(8,128)S(1)}, f32[8,128]{1,0:T(8,128)}, u32[]{:S(2)}) copy-start(f32[8,128]{1,0:T(8,128)} %get-tuple-element.105.refs_3_.refs_4_) | copy-start | bytes 12292
  4.9 3.8 %copy-start.12 = (f32[10,128]{1,0:T(8,128)S(1)}, f32[10,128]{1,0:T(8,128)}, u32[]{:S(2)}) copy-start(f32[10,128]{1,0:T(8,128)} %get-tuple-element.104.refs_2_) | copy-start | bytes 15364
  4.9 7.0 %copy-start.1 = (bf16[256,2560]{1,0:T(8,128)(2,1)S(1)}, bf16[256,2560]{1,0:T(8,128)(2,1)}, u32[]{:S(2)}) copy-start(bf16[256,2560]{1,0:T(8,128)(2,1)} %refs_1_.15) | copy-start | bytes 3932164
  4.9 7.0 %copy-start.2 = (bf16[256,128]{1,0:T(8,128)(2,1)S(1)}, bf16[256,128]{1,0:T(8,128)(2,1)}, u32[]{:S(2)}) copy-start(bf16[256,128]{1,0:T(8,128)(2,1)} %refs_2_.15) | copy-start | bytes 196612
  4.9 7.0 %copy-start.3 = (bf16[256,128]{1,0:T(8,128)(2,1)S(1)}, bf16[256,128]{1,0:T(8,128)(2,1)}, u32[]{:S(2)}) copy-start(bf16[256,128]{1,0:T(8,128)(2,1)} %refs_3_.15) | copy-start | bytes 196612
  5.0 7.0 %copy-start.4 = (bf16[256,128]{1,0:T(8,128)(2,1)S(1)}, bf16[256,128]{1,0:T(8,128)(2,1)}, u32[]{:S(2)}) copy-start(bf16[256,128]{1,0:T(8,128)(2,1)} %get-tuple-element.100.refs_5_.refs_7_.refs_4_) | copy-start | bytes 196612
  5.0 7.0 %copy-start.5 = (bf16[256,128]{1,0:T(8,128)(2,1)S(1)}, bf16[256,128]{1,0:T(8,128)(2,1)}, u32[]{:S(2)}) copy-start(bf16[256,128]{1,0:T(8,128)(2,1)} %get-tuple-element.101.refs_6_.refs_8_.refs_5_) | copy-start | bytes 196612
  5.0 7.0 %copy-start.6 = (f32[256,128]{1,0:T(8,128)S(1)}, f32[256,128]{1,0:T(8,128)}, u32[]{:S(2)}) copy-start(f32[256,128]{1,0:T(8,128)} %get-tuple-element.111.refs_6_) | copy-start | bytes 393220
  5.0 7.0 %copy-start.9 = (f32[40,256]{1,0:T(8,128)S(1)}, f32[40,256]{1,0:T(8,128)}, u32[]{:S(2)}) copy-start(f32[40,256]{1,0:T(8,128)} %refs_5_.5) | copy-start | bytes 122884
  8.6 3.4 %copy-start = (bf16[256,2560]{1,0:T(8,128)(2,1)S(1)}, bf16[256,2560]{1,0:T(8,128)(2,1)}, u32[]{:S(2)}) copy-start(bf16[256,2560]{1,0:T(8,128)(2,1)} %refs_0_.9) | copy-start | bytes 3932164
  8.6 8.5 %collective-permute-start.3 = (f32[1288,128]{1,0:T(8,128)}, f32[1288,128]{1,0:T(8,128)S(1)}, u32[]{:S(2)}, u32[]{:S(2)}) collective-permute-start(f32[1288,128]{1,0:T(8,128)} %get-tuple-element.110), channel_id=1, source_target_pairs={{0,1},{1,0},{2,3},{3,2},{4,5},{5,4},{6,7},{7,6},{8,9},{9,8},{10,11... | collective-permute-start | bytes 1978376 | tf_op jit(solution)/shard_map/ppermute | solution.py:701
  8.9 11.5 %collective-permute-start.1 = (f32[656,128]{1,0:T(8,128)S(1)}, f32[656,128]{1,0:T(8,128)S(1)}, u32[]{:S(2)}, u32[]{:S(2)}) collective-permute-start(f32[656,128]{1,0:T(8,128)S(1)} %get-tuple-element.107.refs_1_.refs_0_), channel_id=1, source_target_pairs={{0,2},{1,3},{2,0},{3,1},{4,6},{5,7},{6,4},{7,5},{8,10},{9,11},{10,... | collective-permute-start | bytes 1007624 | tf_op jit(solution)/shard_map/ppermute | solution.py:701
  12.0 5.1 %copy-start.7 = (f32[1280,128]{1,0:T(8,128)S(1)}, f32[1280,128]{1,0:T(8,128)}, u32[]{:S(2)}) copy-start(f32[1280,128]{1,0:T(8,128)} %get-tuple-element.118.refs_1_) | copy-start | bytes 1966084
  12.0 5.1 %copy-start.11 = (f32[10,128]{1,0:T(8,128)S(1)}, f32[10,128]{1,0:T(8,128)}, u32[]{:S(2)}) copy-start(f32[10,128]{1,0:T(8,128)} %get-tuple-element.119.refs_2_) | copy-start | bytes 15364
  17.2 13.7 %collective-permute-start.4 = (f32[656,128]{1,0:T(8,128)S(1)}, f32[656,128]{1,0:T(8,128)S(1)}, u32[]{:S(2)}, u32[]{:S(2)}) collective-permute-start(f32[656,128]{1,0:T(8,128)S(1)} %get-tuple-element.120.refs_1_), channel_id=1, source_target_pairs={{0,2},{1,3},{2,0},{3,1},{4,6},{5,7},{6,4},{7,5},{8,10},{9,11},{10,... | collective-permute-start | bytes 1007624 | tf_op jit(solution)/shard_map/ppermute | solution.py:701
  20.6 10.3 %collective-permute-start.2 = (f32[336,128]{1,0:T(8,128)S(1)}, f32[336,128]{1,0:T(8,128)S(1)}, u32[]{:S(2)}, u32[]{:S(2)}) collective-permute-start(f32[336,128]{1,0:T(8,128)S(1)} %get-tuple-element.109.refs_0_.refs_1_), channel_id=1, source_target_pairs={{0,4},{1,5},{2,6},{3,7},{4,0},{5,1},{6,2},{7,3},{8,12},{9,13},{10,... | collective-permute-start | bytes 516104 | tf_op jit(solution)/shard_map/ppermute | solution.py:701
  31.2 14.2 %collective-permute-start.8 = (f32[336,128]{1,0:T(8,128)S(1)}, f32[336,128]{1,0:T(8,128)S(1)}, u32[]{:S(2)}, u32[]{:S(2)}) collective-permute-start(f32[336,128]{1,0:T(8,128)S(1)} %get-tuple-element.134.refs_1_), channel_id=1, source_target_pairs={{0,4},{1,5},{2,6},{3,7},{4,0},{5,1},{6,2},{7,3},{8,12},{9,13},{10,... | collective-permute-start | bytes 516104 | tf_op jit(solution)/shard_map/ppermute | solution.py:701
  34.2 8.3 %collective-permute-start.7 = (f32[328,128]{1,0:T(8,128)S(1)}, f32[328,128]{1,0:T(8,128)S(1)}, u32[]{:S(2)}, u32[]{:S(2)}) collective-permute-start(f32[328,128]{1,0:T(8,128)S(1)} %up.5.refs_0_), channel_id=1, source_target_pairs={{1,25},{3,27},{5,29},{7,31},{24,0},{26,2},{28,4},{30,6}} | collective-permute-start | bytes 503816 | tf_op jit(solution)/shard_map/ppermute | solution.py:701
  35.5 8.7 %collective-permute-start.6 = (f32[328,128]{1,0:T(8,128)S(1)}, f32[328,128]{1,0:T(8,128)S(1)}, u32[]{:S(2)}, u32[]{:S(2)}) collective-permute-start(f32[328,128]{1,0:T(8,128)S(1)} %up.5.refs_0_), channel_id=1, source_target_pairs={{1,17},{3,19},{5,21},{7,23},{9,25},{11,27},{13,29},{15,31},{16,0},... | collective-permute-start | bytes 503816 | tf_op jit(solution)/shard_map/ppermute | solution.py:701
  36.8 8.6 %collective-permute-start.5 = (f32[328,128]{1,0:T(8,128)S(1)}, f32[328,128]{1,0:T(8,128)S(1)}, u32[]{:S(2)}, u32[]{:S(2)}) collective-permute-start(f32[328,128]{1,0:T(8,128)S(1)} %up.5.refs_0_), channel_id=1, source_target_pairs={{1,9},{3,11},{5,13},{7,15},{8,0},{9,17},{10,2},{11,19},{12,4},{13,... | collective-permute-start | bytes 503816 | tf_op jit(solution)/shard_map/ppermute | solution.py:701
  45.6 8.8 %collective-permute-start.9 = (f32[336,128]{1,0:T(8,128)S(1)}, f32[336,128]{1,0:T(8,128)S(1)}, u32[]{:S(2)}, u32[]{:S(2)}) collective-permute-start(f32[336,128]{1,0:T(8,128)S(1)} %get-tuple-element.156), channel_id=1, source_target_pairs={{0,4},{1,5},{2,6},{3,7},{4,0},{5,1},{6,2},{7,3},{8,12},{9,13},{10,... | collective-permute-start | bytes 516104 | tf_op jit(solution)/shard_map/ppermute | solution.py:701
  46.5 8.3 %collective-permute-start.13 = (f32[328,128]{1,0:T(8,128)S(1)}, f32[328,128]{1,0:T(8,128)S(1)}, u32[]{:S(2)}, u32[]{:S(2)}) collective-permute-start(f32[328,128]{1,0:T(8,128)S(1)} %up.7), channel_id=1, source_target_pairs={{1,25},{3,27},{5,29},{7,31},{24,0},{26,2},{28,4},{30,6}} | collective-permute-start | bytes 503816 | tf_op jit(solution)/shard_map/ppermute | solution.py:701
  47.8 8.7 %collective-permute-start.12 = (f32[328,128]{1,0:T(8,128)S(1)}, f32[328,128]{1,0:T(8,128)S(1)}, u32[]{:S(2)}, u32[]{:S(2)}) collective-permute-start(f32[328,128]{1,0:T(8,128)S(1)} %up.7), channel_id=1, source_target_pairs={{1,17},{3,19},{5,21},{7,23},{9,25},{11,27},{13,29},{15,31},{16,0},... | collective-permute-start | bytes 503816 | tf_op jit(solution)/shard_map/ppermute | solution.py:701
  49.1 7.9 %collective-permute-start.11 = (f32[328,128]{1,0:T(8,128)S(1)}, f32[328,128]{1,0:T(8,128)S(1)}, u32[]{:S(2)}, u32[]{:S(2)}) collective-permute-start(f32[328,128]{1,0:T(8,128)S(1)} %up.7), channel_id=1, source_target_pairs={{1,9},{3,11},{5,13},{7,15},{8,0},{9,17},{10,2},{11,19},{12,4},{13,... | collective-permute-start | bytes 503816 | tf_op jit(solution)/shard_map/ppermute | solution.py:701
  54.6 12.3 %collective-permute-start.10 = (f32[656,128]{1,0:T(8,128)S(1)}, f32[656,128]{1,0:T(8,128)S(1)}, u32[]{:S(2)}, u32[]{:S(2)}) collective-permute-start(f32[656,128]{1,0:T(8,128)S(1)} %get-tuple-element.158), channel_id=1, source_target_pairs={{0,2},{1,3},{2,0},{3,1},{4,6},{5,7},{6,4},{7,5},{8,10},{9,11},{10,... | collective-permute-start | bytes 1007624 | tf_op jit(solution)/shard_map/ppermute | solution.py:701
  57.3 9.6 %collective-permute-start.14 = (f32[336,128]{1,0:T(8,128)S(1)}, f32[336,128]{1,0:T(8,128)S(1)}, u32[]{:S(2)}, u32[]{:S(2)}) collective-permute-start(f32[336,128]{1,0:T(8,128)S(1)} %get-tuple-element.161), channel_id=1, source_target_pairs={{0,4},{1,5},{2,6},{3,7},{4,0},{5,1},{6,2},{7,3},{8,12},{9,13},{10,... | collective-permute-start | bytes 516104 | tf_op jit(solution)/shard_map/ppermute | solution.py:701
  67.1 7.7 %collective-permute-start.17 = (f32[656,128]{1,0:T(8,128)S(1)}, f32[656,128]{1,0:T(8,128)S(1)}, u32[]{:S(2)}, u32[]{:S(2)}) collective-permute-start(f32[656,128]{1,0:T(8,128)S(1)} %get-tuple-element.173), channel_id=1, source_target_pairs={{0,2},{1,3},{2,0},{3,1},{4,6},{5,7},{6,4},{7,5},{8,10},{9,11},{10,... | collective-permute-start | bytes 1007624 | tf_op jit(solution)/shard_map/ppermute | solution.py:701
  67.7 1.7 %collective-permute-start.15 = (f32[640,128]{1,0:T(8,128)S(1)}, f32[640,128]{1,0:T(8,128)S(1)}, u32[]{:S(2)}, u32[]{:S(2)}) collective-permute-start(f32[640,128]{1,0:T(8,128)S(1)} %get-tuple-element.163.refs_4_), channel_id=1, source_target_pairs={{0,1},{1,0},{2,3},{3,2},{4,5},{5,4},{6,7},{7,6},{8,9},{9,8},{10,11... | collective-permute-start | bytes 983048 | tf_op jit(solution)/shard_map/ppermute | solution.py:701
  67.7 2.1 %collective-permute-start.16 = (f32[640,128]{1,0:T(8,128)S(1)}, f32[640,128]{1,0:T(8,128)S(1)}, u32[]{:S(2)}, u32[]{:S(2)}) collective-permute-start(f32[640,128]{1,0:T(8,128)S(1)} %get-tuple-element.164.refs_5_), channel_id=1, source_target_pairs={{0,1},{1,0},{2,3},{3,2},{4,5},{5,4},{6,7},{7,6},{8,9},{9,8},{10,11... | collective-permute-start | bytes 983048 | tf_op jit(solution)/shard_map/ppermute | solution.py:701
  68.2 6.1 %collective-permute-start.18 = (f32[640,128]{1,0:T(8,128)S(1)}, f32[640,128]{1,0:T(8,128)S(1)}, u32[]{:S(2)}, u32[]{:S(2)}) collective-permute-start(f32[640,128]{1,0:T(8,128)S(1)} %get-tuple-element.174.refs_4_), channel_id=1, source_target_pairs={{0,1},{1,0},{2,3},{3,2},{4,5},{5,4},{6,7},{7,6},{8,9},{9,8},{10,11... | collective-permute-start | bytes 983048 | tf_op jit(solution)/shard_map/ppermute | solution.py:701
  74.8 1.6 %collective-permute-start.19 = (f32[656,128]{1,0:T(8,128)S(1)}, f32[656,128]{1,0:T(8,128)S(1)}, u32[]{:S(2)}, u32[]{:S(2)}) collective-permute-start(f32[656,128]{1,0:T(8,128)S(1)} %collective-permute-done.17.refs_5_), channel_id=1, source_target_pairs={{0,1},{1,0},{2,3},{3,2},{4,5},{5,4},{6,7},{7,6},{8,9},{9,8},{10,11... | collective-permute-start | bytes 1007624 | tf_op jit(solution)/shard_map/ppermute | solution.py:701
  77.3 1.2 %collective-permute-start.20 = (f32[8,128]{1,0:T(8,128)S(1)}, f32[8,128]{1,0:T(8,128)S(1)}, u32[]{:S(2)}, u32[]{:S(2)}) collective-permute-start(f32[8,128]{1,0:T(8,128)S(1)} %get-tuple-element.182.total_ref), channel_id=1, source_target_pairs={{0,1},{1,0},{2,3},{3,2},{4,5},{5,4},{6,7},{7,6},{8,9},{9,8},{10,11... | collective-permute-start | bytes 12296 | tf_op jit(solution)/shard_map/ppermute | solution.py:701
  78.5 5.9 %collective-permute-start.23 = (f32[8,128]{1,0:T(8,128)S(1)}, f32[8,128]{1,0:T(8,128)S(1)}, u32[]{:S(2)}, u32[]{:S(2)}) collective-permute-start(f32[8,128]{1,0:T(8,128)S(1)} %get-tuple-element.183.refs_13_.total_ref), channel_id=1, source_target_pairs={{0,6},{1,7},{2,4},{3,5},{4,2},{5,3},{6,0},{7,1},{8,14},{9,15},{10,... | collective-permute-start | bytes 12296 | tf_op jit(solution)/shard_map/ppermute | solution.py:701
  80.8 4.5 %collective-permute-start.22 = (f32[8,128]{1,0:T(8,128)S(1)}, f32[8,128]{1,0:T(8,128)S(1)}, u32[]{:S(2)}, u32[]{:S(2)}) collective-permute-start(f32[8,128]{1,0:T(8,128)S(1)} %get-tuple-element.183.refs_13_.total_ref), channel_id=1, source_target_pairs={{0,4},{1,5},{2,6},{3,7},{4,0},{5,1},{6,2},{7,3},{8,12},{9,13},{10,... | collective-permute-start | bytes 12296 | tf_op jit(solution)/shard_map/ppermute | solution.py:701
  81.2 4.2 %collective-permute-start.21 = (f32[8,128]{1,0:T(8,128)S(1)}, f32[8,128]{1,0:T(8,128)S(1)}, u32[]{:S(2)}, u32[]{:S(2)}) collective-permute-start(f32[8,128]{1,0:T(8,128)S(1)} %get-tuple-element.183.refs_13_.total_ref), channel_id=1, source_target_pairs={{0,2},{1,3},{2,0},{3,1},{4,6},{5,7},{6,4},{7,5},{8,10},{9,11},{10,... | collective-permute-start | bytes 12296 | tf_op jit(solution)/shard_map/ppermute | solution.py:701
  85.4 6.4 %collective-permute-start.26 = (f32[8,128]{1,0:T(8,128)S(1)}, f32[8,128]{1,0:T(8,128)S(1)}, u32[]{:S(2)}, u32[]{:S(2)}) collective-permute-start(f32[8,128]{1,0:T(8,128)S(1)} %get-tuple-element.190.refs_13_), channel_id=1, source_target_pairs={{24,0},{25,1},{26,2},{27,3},{28,4},{29,5},{30,6},{31,7}} | collective-permute-start | bytes 12296 | tf_op jit(solution)/shard_map/ppermute | solution.py:701
  86.7 7.6 %collective-permute-start.25 = (f32[8,128]{1,0:T(8,128)S(1)}, f32[8,128]{1,0:T(8,128)S(1)}, u32[]{:S(2)}, u32[]{:S(2)}) collective-permute-start(f32[8,128]{1,0:T(8,128)S(1)} %get-tuple-element.190.refs_13_), channel_id=1, source_target_pairs={{16,0},{17,1},{18,2},{19,3},{20,4},{21,5},{22,6},{23,7},{24,8},{25... | collective-permute-start | bytes 12296 | tf_op jit(solution)/shard_map/ppermute | solution.py:701
  88.0 7.0 %collective-permute-start.24 = (f32[8,128]{1,0:T(8,128)S(1)}, f32[8,128]{1,0:T(8,128)S(1)}, u32[]{:S(2)}, u32[]{:S(2)}) collective-permute-start(f32[8,128]{1,0:T(8,128)S(1)} %get-tuple-element.190.refs_13_), channel_id=1, source_target_pairs={{8,0},{9,1},{10,2},{11,3},{12,4},{13,5},{14,6},{15,7},{16,8},{17,9... | collective-permute-start | bytes 12296 | tf_op jit(solution)/shard_map/ppermute | solution.py:701

commit v17 on v14

--- a/solution.py
+++ b/solution.py
@@ -122,6 +122,7 @@
 
 
 STEPS = 2
+SUMMARY_STEPS = 5
 
 
 def summary_kernel(heads, chips, half, x_ref, g_ref, write_ref, read_ref, *refs):
@@ -129,8 +130,8 @@
     chunk = pl.program_id(0)
     lanes = x_ref.shape[1]
     strips = lanes // STRIP
-    half_strips = strips * STEPS
-    head_size = lanes * STEPS * HALVES // heads
+    half_strips = strips * SUMMARY_STEPS
+    head_size = lanes * SUMMARY_STEPS * HALVES // heads
     part = STATE // chips
     if half == 0:
         rates_ref, send_ref, keep_ref, decay_ref, log_ref, run_ref, tail_ref, lead_ref = refs[:8]
@@ -150,7 +151,7 @@
         write_t[...] = write_ref[...].astype(F32).T.astype(BF16)
         read_t[...] = read_ref[...].astype(F32).T.astype(BF16)
 
-    spread = spreader(half * STEPS + chunk, heads, head_size, lanes)
+    spread = spreader(half * SUMMARY_STEPS + chunk, heads, head_size, lanes)
     tail = dot(tail_ref[...], spread, 1, 0)
     lead = dot(lead_ref[...], spread, 1, 0)
     inputs_tail = (x_ref[...].astype(F32) * tail).astype(BF16)
@@ -174,7 +175,7 @@
 def summary(chips, half, x, g, write_map, read_map, rates, shared):
     tokens, wide = x.shape
     heads = rates.shape[0]
-    lanes = wide // (STEPS * HALVES)
+    lanes = wide // (SUMMARY_STEPS * HALVES)
     strips = wide // STRIP // HALVES
     terms = [
         jax.ShapeDtypeStruct((META, STRIP), F32),
@@ -194,10 +195,10 @@
         extra = [shared[0], shared[2], shared[3]]
     return pl.pallas_call(
         lambda *refs: summary_kernel(heads, chips, half, *refs),
-        grid=(STEPS,),
+        grid=(SUMMARY_STEPS,),
         in_specs=[
-            half_lanes(tokens, lanes, half, STEPS),
-            half_lanes(tokens, lanes, half, STEPS),
+            half_lanes(tokens, lanes, half, SUMMARY_STEPS),
+            half_lanes(tokens, lanes, half, SUMMARY_STEPS),
             whole(tokens, STATE),
             whole(tokens, STATE),
         ]

time: 95.3 us -> 99.4 us (1.043)
  Pallas kernels: 31.6 us -> 35.6 us
    pallas_call x2, Pallas kernels: 7.38 us -> 11.4 us  [summary(): pl.pallas_call(lambda *refs: summary_kernel(heads, chips, half, *refs), g...]
  transfers between devices with their start and end apart: 27 -> 27, of which waited for: 18 -> 18; matrix products, arithmetic and copies ran while one was open for 0% -> 0% of each run, Pallas kernels for 27% -> 28%
where the time goes in v17:
time: 99.4 us; the launch traced here: 99 us
  Pallas kernels  35.6 us (36%)
  starting transfers between devices  33 us (33%)
  waiting for transfers between devices  29.4 us (30%)
    ppermute x27, starting transfers between devices, move(): return lax.ppermute(value, ('grp', 'seq'), pairs)  33 us
    ppermute x27, waiting for transfers between devices, move(): return lax.ppermute(value, ('grp', 'seq'), pairs)  29.4 us
    pallas_call x3, Pallas kernels, intra(): pl.pallas_call(lambda *refs: intra_kernel(heads, wide // heads, start, la...  12.5 us
    pallas_call x2, Pallas kernels, summary(): pl.pallas_call(lambda *refs: summary_kernel(heads, chips, half, *refs), g...  11.4 us
    pallas_call x3, Pallas kernels, finish(): pl.pallas_call(lambda *refs: finish_kernel(heads, start, steps, last, *re...  7.27 us
  transfers between devices with their start and end apart: 27, of which 18 were waited for; matrix products, arithmetic and copies ran while one was open for 0% of the time, Pallas kernels for 28%

profile of v17, /device:TPU:0, one launch (start us, length us, event | category | flops | bytes accessed | tf_op | source)
XLA Modules:
  0.0 99.0 jit_solution(2260977436558798702)
XLA Ops:
  0.6 5.7 %summary.2 = (f32[1288,128]{1,0:T(8,128)}, f32[1280,128]{1,0:T(8,128)}, f32[10,128]{1,0:T(8,128)}, f32[8,128]{1,0:T(8,128)}, f32[256,128]{1,0:T(8,128)}, /*index...) custom-call(bf16[256,2560]{1,0:T(8,128)(2,1)} %refs_0_.9, bf16[256,2560]{1,0:T(8,128)(2,1)} %refs_1_.15, ...), custom_call_target="tpu_custom_call" | custom-call | flops 1 | bytes 1 | tf_op jit(solution)/shard_map/summary/pallas_call | solution.py:196
  6.4 0.5 collective-permute-start
  7.0 5.6 %summary.3 = (f32[1288,128]{1,0:T(8,128)}, f32[1280,128]{1,0:T(8,128)}, f32[10,128]{1,0:T(8,128)}) custom-call(bf16[256,2560]{1,0:T(8,128)(2,1)} %refs_0_.9, bf16[256,2560]{1,0:T(8,128)(2,1)} %refs_1_.15, bf16[256,128]{1,0:T(8,128)(2,1)} %refs_2_.15, bf16[256,128]{1,0:T(8,128)(2,1)} %refs_3_.15, f32[8,128]{1,0:T(8,128)} %get-tuple-element.108.refs_3_.refs_4_, ...), custom_call_target="tpu_custom_call" | custom-call | flops 1 | bytes 1 | tf_op jit(solution)/shard_map/summary/pallas_call | solution.py:196
  12.6 0.1 collective-permute-start.2
  12.8 0.1 combine.2
  12.9 3.1 %collective-permute-start.1 = (f32[656,128]{1,0:T(8,128)S(1)}, f32[656,128]{1,0:T(8,128)S(1)}, u32[]{:S(2)}, u32[]{:S(2)}) collective-permute-start(f32[656,128]{1,0:T(8,128)S(1)} %get-tuple-element.110.refs_0_.refs_1_), channel_id=1, source_target_pairs={{0,2},{1,3},{2,0},{3,1},{4,6},{5,7},{6,4},{7,5},{8,10},{9,11},{10,... | collective-permute-start | bytes 1007624 | tf_op jit(solution)/shard_map/ppermute | solution.py:702
  16.0 5.1 %intra.3 = (f32[256,2560]{1,0:T(8,128)S(1)}, f32[128,2560]{1,0:T(8,128)S(1)}, f32[128,2560]{1,0:T(8,128)S(1)}, f32[256,128]{1,0:T(8,128)S(1)}, f32[256,256]{1,0:T(8,128)S(1)}) custom-call(f32[656,128]{1,0:T(8,128)S(1)} %get-tuple-element.110.refs_0_.refs_1_, bf16[256,2560]{1,0:T(8,128)(2,1)S(1)} %copy-done, bf16[256,2560]{1,0:T(8,128)(2,1)S(1)} %copy-done.1, ...), custom_call_target="tpu_custom_call" | custom-call | flops 1 | bytes 1 | tf_op jit(solution)/shard_map/intra/pallas_call | solution.py:442
  21.1 2.9 %collective-permute-done.1.refs_2_ = f32[656,128]{1,0:T(8,128)S(1)} collective-permute-done((f32[656,128]{1,0:T(8,128)S(1)}, f32[656,128]{1,0:T(8,128)S(1)}, u32[]{:S(2)}, u32[]{:S(2)}) %collective-permute-start.1) | collective-permute-done | bytes 335904 | tf_op jit(solution)/shard_map/ppermute | solution.py:702
  24.1 1.8 %collective-permute-start.4 = (f32[656,128]{1,0:T(8,128)S(1)}, f32[656,128]{1,0:T(8,128)S(1)}, u32[]{:S(2)}, u32[]{:S(2)}) collective-permute-start(f32[656,128]{1,0:T(8,128)S(1)} %get-tuple-element.124.refs_1_), channel_id=1, source_target_pairs={{0,2},{1,3},{2,0},{3,1},{4,6},{5,7},{6,4},{7,5},{8,10},{9,11},{10,... | collective-permute-start | bytes 1007624 | tf_op jit(solution)/shard_map/ppermute | solution.py:702
  25.9 0.2 up.4
  26.1 2.7 %collective-permute-start.3 = (f32[336,128]{1,0:T(8,128)S(1)}, f32[336,128]{1,0:T(8,128)S(1)}, u32[]{:S(2)}, u32[]{:S(2)}) collective-permute-start(f32[336,128]{1,0:T(8,128)S(1)} %get-tuple-element.120.refs_0_.refs_1_), channel_id=1, source_target_pairs={{0,4},{1,5},{2,6},{3,7},{4,0},{5,1},{6,2},{7,3},{8,12},{9,13},{10,... | collective-permute-start | bytes 516104 | tf_op jit(solution)/shard_map/ppermute | solution.py:702
  28.8 5.0 %intra.4 = (f32[256,2560]{1,0:T(8,128)S(1)}, f32[128,2560]{1,0:T(8,128)S(1)}, f32[128,2560]{1,0:T(8,128)S(1)}, f32[256,128]{1,0:T(8,128)S(1)}, f32[256,256]{1,0:T(8,128)S(1)}) custom-call(f32[336,128]{1,0:T(8,128)S(1)} %get-tuple-element.120.refs_0_.refs_1_, ...), custom_call_target="tpu_custom_call", output_to_operand_aliasing={{0}: (9, {}), {1}: (10, {}), {2}: (11, {})} | custom-call | flops 1 | bytes 1 | tf_op jit(solution)/shard_map/intra/pallas_call | solution.py:442
  33.8 2.3 %collective-permute-done.3.refs_2_ = f32[336,128]{1,0:T(8,128)S(1)} collective-permute-done((f32[336,128]{1,0:T(8,128)S(1)}, f32[336,128]{1,0:T(8,128)S(1)}, u32[]{:S(2)}, u32[]{:S(2)}) %collective-permute-start.3) | collective-permute-done | bytes 172064 | tf_op jit(solution)/shard_map/ppermute | solution.py:702
  36.1 1.1 %collective-permute-done.4.refs_2_ = f32[656,128]{1,0:T(8,128)S(1)} collective-permute-done((f32[656,128]{1,0:T(8,128)S(1)}, f32[656,128]{1,0:T(8,128)S(1)}, u32[]{:S(2)}, u32[]{:S(2)}) %collective-permute-start.4) | collective-permute-done | bytes 335904 | tf_op jit(solution)/shard_map/ppermute | solution.py:702
  37.2 0.2 up.6
  37.4 2.4 %collective-permute-start.8 = (f32[336,128]{1,0:T(8,128)S(1)}, f32[336,128]{1,0:T(8,128)S(1)}, u32[]{:S(2)}, u32[]{:S(2)}) collective-permute-start(f32[336,128]{1,0:T(8,128)S(1)} %get-tuple-element.138.refs_1_), channel_id=1, source_target_pairs={{0,4},{1,5},{2,6},{3,7},{4,0},{5,1},{6,2},{7,3},{8,12},{9,13},{10,... | collective-permute-start | bytes 516104 | tf_op jit(solution)/shard_map/ppermute | solution.py:702
  39.8 0.2 up.5.refs_0_
  40.0 1.3 %collective-permute-start.7 = (f32[328,128]{1,0:T(8,128)S(1)}, f32[328,128]{1,0:T(8,128)S(1)}, u32[]{:S(2)}, u32[]{:S(2)}) collective-permute-start(f32[328,128]{1,0:T(8,128)S(1)} %up.5.refs_0_), channel_id=1, source_target_pairs={{1,25},{3,27},{5,29},{7,31},{24,0},{26,2},{28,4},{30,6}} | collective-permute-start | bytes 503816 | tf_op jit(solution)/shard_map/ppermute | solution.py:702
  41.3 1.3 %collective-permute-start.6 = (f32[328,128]{1,0:T(8,128)S(1)}, f32[328,128]{1,0:T(8,128)S(1)}, u32[]{:S(2)}, u32[]{:S(2)}) collective-permute-start(f32[328,128]{1,0:T(8,128)S(1)} %up.5.refs_0_), channel_id=1, source_target_pairs={{1,17},{3,19},{5,21},{7,23},{9,25},{11,27},{13,29},{15,31},{16,0},... | collective-permute-start | bytes 503816 | tf_op jit(solution)/shard_map/ppermute | solution.py:702
  42.6 1.3 %collective-permute-start.5 = (f32[328,128]{1,0:T(8,128)S(1)}, f32[328,128]{1,0:T(8,128)S(1)}, u32[]{:S(2)}, u32[]{:S(2)}) collective-permute-start(f32[328,128]{1,0:T(8,128)S(1)} %up.5.refs_0_), channel_id=1, source_target_pairs={{1,9},{3,11},{5,13},{7,15},{8,0},{9,17},{10,2},{11,19},{12,4},{13,... | collective-permute-start | bytes 503816 | tf_op jit(solution)/shard_map/ppermute | solution.py:702
  43.9 2.5 %intra.5 = (f32[256,2560]{1,0:T(8,128)S(1)}, f32[128,2560]{1,0:T(8,128)S(1)}, f32[128,2560]{1,0:T(8,128)S(1)}, f32[256,128]{1,0:T(8,128)S(1)}, f32[256,128]{1,0:T(8,128)S(1)}, /*index=5*/f32[256,128]{1,0:T(8,128)S(1)}) custom-call(f32[328,128]{1,0:T(8,128)S(1)} %up.5.refs_0_, ...), custom_call_target="tpu_custom_call", output_to_operand_aliasing={{0}: (9, {}), {1}: (10, {}), {2}: (11, {})} | custom-call | flops 1 | bytes 1 | tf_op jit(solution)/shard_map/intra/pallas_call | solution.py:442
  46.4 1.9 %collective-permute-done.7.refs_5_ = f32[328,128]{1,0:T(8,128)S(1)} collective-permute-done((f32[328,128]{1,0:T(8,128)S(1)}, f32[328,128]{1,0:T(8,128)S(1)}, u32[]{:S(2)}, u32[]{:S(2)}) %collective-permute-start.7) | collective-permute-done | bytes 167968 | tf_op jit(solution)/shard_map/ppermute | solution.py:702
  48.2 1.7 %collective-permute-done.6.refs_4_ = f32[328,128]{1,0:T(8,128)S(1)} collective-permute-done((f32[328,128]{1,0:T(8,128)S(1)}, f32[328,128]{1,0:T(8,128)S(1)}, u32[]{:S(2)}, u32[]{:S(2)}) %collective-permute-start.6) | collective-permute-done | bytes 167968 | tf_op jit(solution)/shard_map/ppermute | solution.py:702
  50.0 0.2 down.4
  50.2 0.8 collective-permute-start.9
  51.0 0.2 up.7
  51.2 1.3 %collective-permute-start.13 = (f32[328,128]{1,0:T(8,128)S(1)}, f32[328,128]{1,0:T(8,128)S(1)}, u32[]{:S(2)}, u32[]{:S(2)}) collective-permute-start(f32[328,128]{1,0:T(8,128)S(1)} %up.7), channel_id=1, source_target_pairs={{1,25},{3,27},{5,29},{7,31},{24,0},{26,2},{28,4},{30,6}} | collective-permute-start | bytes 503816 | tf_op jit(solution)/shard_map/ppermute | solution.py:702
  52.5 1.3 %collective-permute-start.12 = (f32[328,128]{1,0:T(8,128)S(1)}, f32[328,128]{1,0:T(8,128)S(1)}, u32[]{:S(2)}, u32[]{:S(2)}) collective-permute-start(f32[328,128]{1,0:T(8,128)S(1)} %up.7), channel_id=1, source_target_pairs={{1,17},{3,19},{5,21},{7,23},{9,25},{11,27},{13,29},{15,31},{16,0},... | collective-permute-start | bytes 503816 | tf_op jit(solution)/shard_map/ppermute | solution.py:702
  53.8 1.5 %collective-permute-start.11 = (f32[328,128]{1,0:T(8,128)S(1)}, f32[328,128]{1,0:T(8,128)S(1)}, u32[]{:S(2)}, u32[]{:S(2)}) collective-permute-start(f32[328,128]{1,0:T(8,128)S(1)} %up.7), channel_id=1, source_target_pairs={{1,9},{3,11},{5,13},{7,15},{8,0},{9,17},{10,2},{11,19},{12,4},{13,... | collective-permute-start | bytes 503816 | tf_op jit(solution)/shard_map/ppermute | solution.py:702
  55.3 3.7 %collective-permute-done.9.refs_4_ = f32[336,128]{1,0:T(8,128)S(1)} collective-permute-done((f32[336,128]{1,0:T(8,128)S(1)}, f32[336,128]{1,0:T(8,128)S(1)}, u32[]{:S(2)}, u32[]{:S(2)}) %collective-permute-start.9) | collective-permute-done | bytes 172064 | tf_op jit(solution)/shard_map/ppermute | solution.py:702
  59.0 0.2 down.5
  59.2 0.1 collective-permute-start.10
  59.3 0.2 collective-permute-done.13.refs_5_
  59.5 1.7 %collective-permute-done.12.refs_4_ = f32[328,128]{1,0:T(8,128)S(1)} collective-permute-done((f32[328,128]{1,0:T(8,128)S(1)}, f32[328,128]{1,0:T(8,128)S(1)}, u32[]{:S(2)}, u32[]{:S(2)}) %collective-permute-start.12) | collective-permute-done | bytes 167968 | tf_op jit(solution)/shard_map/ppermute | solution.py:702
  61.2 0.3 down.6
  61.5 2.2 %collective-permute-start.14 = (f32[336,128]{1,0:T(8,128)S(1)}, f32[336,128]{1,0:T(8,128)S(1)}, u32[]{:S(2)}, u32[]{:S(2)}) collective-permute-start(f32[336,128]{1,0:T(8,128)S(1)} %get-tuple-element.166), channel_id=1, source_target_pairs={{0,4},{1,5},{2,6},{3,7},{4,0},{5,1},{6,2},{7,3},{8,12},{9,13},{10,... | collective-permute-start | bytes 516104 | tf_op jit(solution)/shard_map/ppermute | solution.py:702
  63.7 5.8 %collective-permute-done.14.refs_4_ = f32[336,128]{1,0:T(8,128)S(1)} collective-permute-done((f32[336,128]{1,0:T(8,128)S(1)}, f32[336,128]{1,0:T(8,128)S(1)}, u32[]{:S(2)}, u32[]{:S(2)}) %collective-permute-start.14) | collective-permute-done | bytes 172064 | tf_op jit(solution)/shard_map/ppermute | solution.py:702
  69.5 0.4 collective-permute-done.10.got_ref
  69.9 0.2 down.7
  70.2 2.1 %collective-permute-start.17 = (f32[656,128]{1,0:T(8,128)S(1)}, f32[656,128]{1,0:T(8,128)S(1)}, u32[]{:S(2)}, u32[]{:S(2)}) collective-permute-start(f32[656,128]{1,0:T(8,128)S(1)} %get-tuple-element.178), channel_id=1, source_target_pairs={{0,2},{1,3},{2,0},{3,1},{4,6},{5,7},{6,4},{7,5},{8,10},{9,11},{10,... | collective-permute-start | bytes 1007624 | tf_op jit(solution)/shard_map/ppermute | solution.py:702
  72.4 0.5 collective-permute-start.16
  72.9 0.1 collective-permute-start.18
  72.9 1.0 %collective-permute-done.15.refs_6_ = f32[640,128]{1,0:T(8,128)S(1)} collective-permute-done((f32[640,128]{1,0:T(8,128)S(1)}, f32[640,128]{1,0:T(8,128)S(1)}, u32[]{:S(2)}, u32[]{:S(2)}) %collective-permute-start.15) | collective-permute-done | bytes 327712 | tf_op jit(solution)/shard_map/ppermute | solution.py:702
  74.0 0.5 collective-permute-done.16.refs_7_
  74.5 0.8 assemble.2
  75.2 3.8 %finish.3 = (bf16[256,2560]{1,0:T(8,128)(2,1)}, f32[256,128]{1,0:T(8,128)S(1)}, f32[256,128]{1,0:T(8,128)S(1)}, f32[256,128]{1,0:T(8,128)S(1)}, f32[8,128]{1,0:T(8,128)S(1)}) custom-call(bf16[256,2560]{1,0:T(8,128)(2,1)S(1)} %copy-done, bf16[256,2560]{1,0:T(8,128)(2,1)S(1)} %copy-done.1, bf16[256,128]{1,0:T(8,128)(2,1)S(1)} %copy-done.2, ...), custom_call_target="tpu_custom_call" | custom-call | flops 1 | bytes 1 | tf_op jit(solution)/shard_map/finish/pallas_call | solution.py:612
  79.0 0.1 collective-permute-start.19
  79.1 1.5 %collective-permute-done.19.refs_7_ = f32[656,128]{1,0:T(8,128)S(1)} collective-permute-done((f32[656,128]{1,0:T(8,128)S(1)}, f32[656,128]{1,0:T(8,128)S(1)}, u32[]{:S(2)}, u32[]{:S(2)}) %collective-permute-start.19) | collective-permute-done | bytes 335904 | tf_op jit(solution)/shard_map/ppermute | solution.py:702
  80.7 0.8 assemble.3
  81.5 0.2 collective-permute-start.20
  81.7 1.0 %collective-permute-done.20.got_ref = f32[8,128]{1,0:T(8,128)S(1)} collective-permute-done((f32[8,128]{1,0:T(8,128)S(1)}, f32[8,128]{1,0:T(8,128)S(1)}, u32[]{:S(2)}, u32[]{:S(2)}) %collective-permute-start.20) | collective-permute-done | bytes 4128 | tf_op jit(solution)/shard_map/ppermute | solution.py:702
  82.7 2.8 %collective-permute-start.23 = (f32[8,128]{1,0:T(8,128)S(1)}, f32[8,128]{1,0:T(8,128)S(1)}, u32[]{:S(2)}, u32[]{:S(2)}) collective-permute-start(f32[8,128]{1,0:T(8,128)S(1)} %get-tuple-element.189.refs_13_.total_ref), channel_id=1, source_target_pairs={{0,6},{1,7},{2,4},{3,5},{4,2},{5,3},{6,0},{7,1},{8,14},{9,15},{10,... | collective-permute-start | bytes 12296 | tf_op jit(solution)/shard_map/ppermute | solution.py:702
  85.6 0.3 collective-permute-start.22
  85.8 1.3 %collective-permute-start.21 = (f32[8,128]{1,0:T(8,128)S(1)}, f32[8,128]{1,0:T(8,128)S(1)}, u32[]{:S(2)}, u32[]{:S(2)}) collective-permute-start(f32[8,128]{1,0:T(8,128)S(1)} %get-tuple-element.189.refs_13_.total_ref), channel_id=1, source_target_pairs={{0,2},{1,3},{2,0},{3,1},{4,6},{5,7},{6,4},{7,5},{8,10},{9,11},{10,... | collective-permute-start | bytes 12296 | tf_op jit(solution)/shard_map/ppermute | solution.py:702
  87.1 1.5 %finish.4 = (bf16[256,2560]{1,0:T(8,128)(2,1)}, f32[256,128]{1,0:T(8,128)S(1)}, f32[256,128]{1,0:T(8,128)S(1)}, f32[256,128]{1,0:T(8,128)S(1)}, f32[8,128]{1,0:T(8,128)S(1)}) custom-call(bf16[256,2560]{1,0:T(8,128)(2,1)S(1)} %copy-done, bf16[256,2560]{1,0:T(8,128)(2,1)S(1)} %copy-done.1, ...), custom_call_target="tpu_custom_call", output_to_operand_aliasing={{0}: (12, {})} | custom-call | flops 1 | bytes 1 | tf_op jit(solution)/shard_map/finish/pallas_call | solution.py:612
  88.6 1.4 %collective-permute-done.22.refs_1_ = f32[8,128]{1,0:T(8,128)S(1)} collective-permute-done((f32[8,128]{1,0:T(8,128)S(1)}, f32[8,128]{1,0:T(8,128)S(1)}, u32[]{:S(2)}, u32[]{:S(2)}) %collective-permute-start.22) | collective-permute-done | bytes 4128 | tf_op jit(solution)/shard_map/ppermute | solution.py:702
  90.1 1.3 %collective-permute-start.26 = (f32[8,128]{1,0:T(8,128)S(1)}, f32[8,128]{1,0:T(8,128)S(1)}, u32[]{:S(2)}, u32[]{:S(2)}) collective-permute-start(f32[8,128]{1,0:T(8,128)S(1)} %get-tuple-element.196.refs_13_), channel_id=1, source_target_pairs={{24,0},{25,1},{26,2},{27,3},{28,4},{29,5},{30,6},{31,7}} | collective-permute-start | bytes 12296 | tf_op jit(solution)/shard_map/ppermute | solution.py:702
  91.4 1.3 %collective-permute-start.25 = (f32[8,128]{1,0:T(8,128)S(1)}, f32[8,128]{1,0:T(8,128)S(1)}, u32[]{:S(2)}, u32[]{:S(2)}) collective-permute-start(f32[8,128]{1,0:T(8,128)S(1)} %get-tuple-element.196.refs_13_), channel_id=1, source_target_pairs={{16,0},{17,1},{18,2},{19,3},{20,4},{21,5},{22,6},{23,7},{24,8},{25... | collective-permute-start | bytes 12296 | tf_op jit(solution)/shard_map/ppermute | solution.py:702
  92.7 1.3 %collective-permute-start.24 = (f32[8,128]{1,0:T(8,128)S(1)}, f32[8,128]{1,0:T(8,128)S(1)}, u32[]{:S(2)}, u32[]{:S(2)}) collective-permute-start(f32[8,128]{1,0:T(8,128)S(1)} %get-tuple-element.196.refs_13_), channel_id=1, source_target_pairs={{8,0},{9,1},{10,2},{11,3},{12,4},{13,5},{14,6},{15,7},{16,8},{17,9... | collective-permute-start | bytes 12296 | tf_op jit(solution)/shard_map/ppermute | solution.py:702
  94.0 2.0 %finish.5 = (bf16[256,2560]{1,0:T(8,128)(2,1)}, bf16[256,128]{1,0:T(8,128)(2,1)}, bf16[256,128]{1,0:T(8,128)(2,1)}, f32[40,256]{1,0:T(8,128)S(1)}, f32[8,128]{1,0:T(8,128)}) custom-call(bf16[256,2560]{1,0:T(8,128)(2,1)S(1)} %copy-done, bf16[256,2560]{1,0:T(8,128)(2,1)S(1)} %copy-done.1, ...), custom_call_target="tpu_custom_call", output_to_operand_aliasing={{0}: (12, {})} | custom-call | flops 1 | bytes 1 | tf_op jit(solution)/shard_map/finish/pallas_call | solution.py:612
  96.0 0.5 collective-permute-done.26.refs_3_
  96.5 0.4 collective-permute-done.25.refs_2_
  96.9 1.3 %collective-permute-done.24.refs_1_ = f32[8,128]{1,0:T(8,128)S(1)} collective-permute-done((f32[8,128]{1,0:T(8,128)S(1)}, f32[8,128]{1,0:T(8,128)S(1)}, u32[]{:S(2)}, u32[]{:S(2)}) %collective-permute-start.24) | collective-permute-done | bytes 4128 | tf_op jit(solution)/shard_map/ppermute | solution.py:702
  98.2 0.8 add_later.1
  (40 shorter events, 0.3 us)
Async XLA Ops:
  6.4 6.4 %collective-permute-start = (f32[1288,128]{1,0:T(8,128)}, f32[1288,128]{1,0:T(8,128)S(1)}, u32[]{:S(2)}, u32[]{:S(2)}) collective-permute-start(f32[1288,128]{1,0:T(8,128)} %get-tuple-element.105), channel_id=1, source_target_pairs={{0,1},{1,0},{2,3},{3,2},{4,5},{5,4},{6,7},{7,6},{8,9},{9,8},{10,11... | collective-permute-start | bytes 1978376 | tf_op jit(solution)/shard_map/ppermute | solution.py:702
  6.9 5.8 %copy-start.8 = (f32[1280,128]{1,0:T(8,128)S(1)}, f32[1280,128]{1,0:T(8,128)}, u32[]{:S(2)}) copy-start(f32[1280,128]{1,0:T(8,128)} %get-tuple-element.106.refs_1_) | copy-start | bytes 1966084
  6.9 5.8 %copy-start.10 = (f32[8,128]{1,0:T(8,128)S(1)}, f32[8,128]{1,0:T(8,128)}, u32[]{:S(2)}) copy-start(f32[8,128]{1,0:T(8,128)} %get-tuple-element.108.refs_3_.refs_4_) | copy-start | bytes 12292
  6.9 5.8 %copy-start.12 = (f32[10,128]{1,0:T(8,128)S(1)}, f32[10,128]{1,0:T(8,128)}, u32[]{:S(2)}) copy-start(f32[10,128]{1,0:T(8,128)} %get-tuple-element.107.refs_2_) | copy-start | bytes 15364
  6.9 9.0 %copy-start.1 = (bf16[256,2560]{1,0:T(8,128)(2,1)S(1)}, bf16[256,2560]{1,0:T(8,128)(2,1)}, u32[]{:S(2)}) copy-start(bf16[256,2560]{1,0:T(8,128)(2,1)} %refs_1_.15) | copy-start | bytes 3932164
  6.9 9.0 %copy-start.2 = (bf16[256,128]{1,0:T(8,128)(2,1)S(1)}, bf16[256,128]{1,0:T(8,128)(2,1)}, u32[]{:S(2)}) copy-start(bf16[256,128]{1,0:T(8,128)(2,1)} %refs_2_.15) | copy-start | bytes 196612
  6.9 9.0 %copy-start.3 = (bf16[256,128]{1,0:T(8,128)(2,1)S(1)}, bf16[256,128]{1,0:T(8,128)(2,1)}, u32[]{:S(2)}) copy-start(bf16[256,128]{1,0:T(8,128)(2,1)} %refs_3_.15) | copy-start | bytes 196612
  6.9 9.0 %copy-start.4 = (bf16[256,128]{1,0:T(8,128)(2,1)S(1)}, bf16[256,128]{1,0:T(8,128)(2,1)}, u32[]{:S(2)}) copy-start(bf16[256,128]{1,0:T(8,128)(2,1)} %get-tuple-element.103.refs_5_.refs_7_.refs_4_) | copy-start | bytes 196612
  7.0 9.0 %copy-start.5 = (bf16[256,128]{1,0:T(8,128)(2,1)S(1)}, bf16[256,128]{1,0:T(8,128)(2,1)}, u32[]{:S(2)}) copy-start(bf16[256,128]{1,0:T(8,128)(2,1)} %get-tuple-element.104.refs_6_.refs_8_.refs_5_) | copy-start | bytes 196612
  7.0 9.0 %copy-start.6 = (f32[256,128]{1,0:T(8,128)S(1)}, f32[256,128]{1,0:T(8,128)}, u32[]{:S(2)}) copy-start(f32[256,128]{1,0:T(8,128)} %get-tuple-element.112.refs_6_) | copy-start | bytes 393220
  7.0 9.0 %copy-start.9 = (f32[40,256]{1,0:T(8,128)S(1)}, f32[40,256]{1,0:T(8,128)}, u32[]{:S(2)}) copy-start(f32[40,256]{1,0:T(8,128)} %refs_5_.5) | copy-start | bytes 122884
  12.6 3.4 %copy-start = (bf16[256,2560]{1,0:T(8,128)(2,1)S(1)}, bf16[256,2560]{1,0:T(8,128)(2,1)}, u32[]{:S(2)}) copy-start(bf16[256,2560]{1,0:T(8,128)(2,1)} %refs_0_.9) | copy-start | bytes 3932164
  12.6 8.5 %collective-permute-start.2 = (f32[1288,128]{1,0:T(8,128)}, f32[1288,128]{1,0:T(8,128)S(1)}, u32[]{:S(2)}, u32[]{:S(2)}) collective-permute-start(f32[1288,128]{1,0:T(8,128)} %get-tuple-element.111), channel_id=1, source_target_pairs={{0,1},{1,0},{2,3},{3,2},{4,5},{5,4},{6,7},{7,6},{8,9},{9,8},{10,11... | collective-permute-start | bytes 1978376 | tf_op jit(solution)/shard_map/ppermute | solution.py:702
  12.9 11.2 %collective-permute-start.1 = (f32[656,128]{1,0:T(8,128)S(1)}, f32[656,128]{1,0:T(8,128)S(1)}, u32[]{:S(2)}, u32[]{:S(2)}) collective-permute-start(f32[656,128]{1,0:T(8,128)S(1)} %get-tuple-element.110.refs_0_.refs_1_), channel_id=1, source_target_pairs={{0,2},{1,3},{2,0},{3,1},{4,6},{5,7},{6,4},{7,5},{8,10},{9,11},{10,... | collective-permute-start | bytes 1007624 | tf_op jit(solution)/shard_map/ppermute | solution.py:702
  16.0 8.0 %copy-start.7 = (f32[1280,128]{1,0:T(8,128)S(1)}, f32[1280,128]{1,0:T(8,128)}, u32[]{:S(2)}) copy-start(f32[1280,128]{1,0:T(8,128)} %get-tuple-element.122.refs_1_) | copy-start | bytes 1966084
  16.0 8.0 %copy-start.11 = (f32[10,128]{1,0:T(8,128)S(1)}, f32[10,128]{1,0:T(8,128)}, u32[]{:S(2)}) copy-start(f32[10,128]{1,0:T(8,128)} %get-tuple-element.123.refs_2_) | copy-start | bytes 15364
  24.1 13.0 %collective-permute-start.4 = (f32[656,128]{1,0:T(8,128)S(1)}, f32[656,128]{1,0:T(8,128)S(1)}, u32[]{:S(2)}, u32[]{:S(2)}) collective-permute-start(f32[656,128]{1,0:T(8,128)S(1)} %get-tuple-element.124.refs_1_), channel_id=1, source_target_pairs={{0,2},{1,3},{2,0},{3,1},{4,6},{5,7},{6,4},{7,5},{8,10},{9,11},{10,... | collective-permute-start | bytes 1007624 | tf_op jit(solution)/shard_map/ppermute | solution.py:702
  26.1 10.0 %collective-permute-start.3 = (f32[336,128]{1,0:T(8,128)S(1)}, f32[336,128]{1,0:T(8,128)S(1)}, u32[]{:S(2)}, u32[]{:S(2)}) collective-permute-start(f32[336,128]{1,0:T(8,128)S(1)} %get-tuple-element.120.refs_0_.refs_1_), channel_id=1, source_target_pairs={{0,4},{1,5},{2,6},{3,7},{4,0},{5,1},{6,2},{7,3},{8,12},{9,13},{10,... | collective-permute-start | bytes 516104 | tf_op jit(solution)/shard_map/ppermute | solution.py:702
  37.4 12.6 %collective-permute-start.8 = (f32[336,128]{1,0:T(8,128)S(1)}, f32[336,128]{1,0:T(8,128)S(1)}, u32[]{:S(2)}, u32[]{:S(2)}) collective-permute-start(f32[336,128]{1,0:T(8,128)S(1)} %get-tuple-element.138.refs_1_), channel_id=1, source_target_pairs={{0,4},{1,5},{2,6},{3,7},{4,0},{5,1},{6,2},{7,3},{8,12},{9,13},{10,... | collective-permute-start | bytes 516104 | tf_op jit(solution)/shard_map/ppermute | solution.py:702
  40.0 8.3 %collective-permute-start.7 = (f32[328,128]{1,0:T(8,128)S(1)}, f32[328,128]{1,0:T(8,128)S(1)}, u32[]{:S(2)}, u32[]{:S(2)}) collective-permute-start(f32[328,128]{1,0:T(8,128)S(1)} %up.5.refs_0_), channel_id=1, source_target_pairs={{1,25},{3,27},{5,29},{7,31},{24,0},{26,2},{28,4},{30,6}} | collective-permute-start | bytes 503816 | tf_op jit(solution)/shard_map/ppermute | solution.py:702
  41.3 8.7 %collective-permute-start.6 = (f32[328,128]{1,0:T(8,128)S(1)}, f32[328,128]{1,0:T(8,128)S(1)}, u32[]{:S(2)}, u32[]{:S(2)}) collective-permute-start(f32[328,128]{1,0:T(8,128)S(1)} %up.5.refs_0_), channel_id=1, source_target_pairs={{1,17},{3,19},{5,21},{7,23},{9,25},{11,27},{13,29},{15,31},{16,0},... | collective-permute-start | bytes 503816 | tf_op jit(solution)/shard_map/ppermute | solution.py:702
  42.6 7.4 %collective-permute-start.5 = (f32[328,128]{1,0:T(8,128)S(1)}, f32[328,128]{1,0:T(8,128)S(1)}, u32[]{:S(2)}, u32[]{:S(2)}) collective-permute-start(f32[328,128]{1,0:T(8,128)S(1)} %up.5.refs_0_), channel_id=1, source_target_pairs={{1,9},{3,11},{5,13},{7,15},{8,0},{9,17},{10,2},{11,19},{12,4},{13,... | collective-permute-start | bytes 503816 | tf_op jit(solution)/shard_map/ppermute | solution.py:702
  50.2 8.8 %collective-permute-start.9 = (f32[336,128]{1,0:T(8,128)S(1)}, f32[336,128]{1,0:T(8,128)S(1)}, u32[]{:S(2)}, u32[]{:S(2)}) collective-permute-start(f32[336,128]{1,0:T(8,128)S(1)} %get-tuple-element.161), channel_id=1, source_target_pairs={{0,4},{1,5},{2,6},{3,7},{4,0},{5,1},{6,2},{7,3},{8,12},{9,13},{10,... | collective-permute-start | bytes 516104 | tf_op jit(solution)/shard_map/ppermute | solution.py:702
  51.2 8.3 %collective-permute-start.13 = (f32[328,128]{1,0:T(8,128)S(1)}, f32[328,128]{1,0:T(8,128)S(1)}, u32[]{:S(2)}, u32[]{:S(2)}) collective-permute-start(f32[328,128]{1,0:T(8,128)S(1)} %up.7), channel_id=1, source_target_pairs={{1,25},{3,27},{5,29},{7,31},{24,0},{26,2},{28,4},{30,6}} | collective-permute-start | bytes 503816 | tf_op jit(solution)/shard_map/ppermute | solution.py:702
  52.5 8.7 %collective-permute-start.12 = (f32[328,128]{1,0:T(8,128)S(1)}, f32[328,128]{1,0:T(8,128)S(1)}, u32[]{:S(2)}, u32[]{:S(2)}) collective-permute-start(f32[328,128]{1,0:T(8,128)S(1)} %up.7), channel_id=1, source_target_pairs={{1,17},{3,19},{5,21},{7,23},{9,25},{11,27},{13,29},{15,31},{16,0},... | collective-permute-start | bytes 503816 | tf_op jit(solution)/shard_map/ppermute | solution.py:702
  53.8 7.4 %collective-permute-start.11 = (f32[328,128]{1,0:T(8,128)S(1)}, f32[328,128]{1,0:T(8,128)S(1)}, u32[]{:S(2)}, u32[]{:S(2)}) collective-permute-start(f32[328,128]{1,0:T(8,128)S(1)} %up.7), channel_id=1, source_target_pairs={{1,9},{3,11},{5,13},{7,15},{8,0},{9,17},{10,2},{11,19},{12,4},{13,... | collective-permute-start | bytes 503816 | tf_op jit(solution)/shard_map/ppermute | solution.py:702
  59.2 10.7 %collective-permute-start.10 = (f32[656,128]{1,0:T(8,128)S(1)}, f32[656,128]{1,0:T(8,128)S(1)}, u32[]{:S(2)}, u32[]{:S(2)}) collective-permute-start(f32[656,128]{1,0:T(8,128)S(1)} %get-tuple-element.163), channel_id=1, source_target_pairs={{0,2},{1,3},{2,0},{3,1},{4,6},{5,7},{6,4},{7,5},{8,10},{9,11},{10,... | collective-permute-start | bytes 1007624 | tf_op jit(solution)/shard_map/ppermute | solution.py:702
  61.5 8.1 %collective-permute-start.14 = (f32[336,128]{1,0:T(8,128)S(1)}, f32[336,128]{1,0:T(8,128)S(1)}, u32[]{:S(2)}, u32[]{:S(2)}) collective-permute-start(f32[336,128]{1,0:T(8,128)S(1)} %get-tuple-element.166), channel_id=1, source_target_pairs={{0,4},{1,5},{2,6},{3,7},{4,0},{5,1},{6,2},{7,3},{8,12},{9,13},{10,... | collective-permute-start | bytes 516104 | tf_op jit(solution)/shard_map/ppermute | solution.py:702
  70.2 8.8 %collective-permute-start.17 = (f32[656,128]{1,0:T(8,128)S(1)}, f32[656,128]{1,0:T(8,128)S(1)}, u32[]{:S(2)}, u32[]{:S(2)}) collective-permute-start(f32[656,128]{1,0:T(8,128)S(1)} %get-tuple-element.178), channel_id=1, source_target_pairs={{0,2},{1,3},{2,0},{3,1},{4,6},{5,7},{6,4},{7,5},{8,10},{9,11},{10,... | collective-permute-start | bytes 1007624 | tf_op jit(solution)/shard_map/ppermute | solution.py:702
  72.3 1.7 %collective-permute-start.15 = (f32[640,128]{1,0:T(8,128)S(1)}, f32[640,128]{1,0:T(8,128)S(1)}, u32[]{:S(2)}, u32[]{:S(2)}) collective-permute-start(f32[640,128]{1,0:T(8,128)S(1)} %get-tuple-element.168.refs_4_), channel_id=1, source_target_pairs={{0,1},{1,0},{2,3},{3,2},{4,5},{5,4},{6,7},{7,6},{8,9},{9,8},{10,11... | collective-permute-start | bytes 983048 | tf_op jit(solution)/shard_map/ppermute | solution.py:702
  72.4 2.1 %collective-permute-start.16 = (f32[640,128]{1,0:T(8,128)S(1)}, f32[640,128]{1,0:T(8,128)S(1)}, u32[]{:S(2)}, u32[]{:S(2)}) collective-permute-start(f32[640,128]{1,0:T(8,128)S(1)} %get-tuple-element.169.refs_5_), channel_id=1, source_target_pairs={{0,1},{1,0},{2,3},{3,2},{4,5},{5,4},{6,7},{7,6},{8,9},{9,8},{10,11... | collective-permute-start | bytes 983048 | tf_op jit(solution)/shard_map/ppermute | solution.py:702
  72.9 6.1 %collective-permute-start.18 = (f32[640,128]{1,0:T(8,128)S(1)}, f32[640,128]{1,0:T(8,128)S(1)}, u32[]{:S(2)}, u32[]{:S(2)}) collective-permute-start(f32[640,128]{1,0:T(8,128)S(1)} %get-tuple-element.179.refs_4_), channel_id=1, source_target_pairs={{0,1},{1,0},{2,3},{3,2},{4,5},{5,4},{6,7},{7,6},{8,9},{9,8},{10,11... | collective-permute-start | bytes 983048 | tf_op jit(solution)/shard_map/ppermute | solution.py:702
  79.0 1.6 %collective-permute-start.19 = (f32[656,128]{1,0:T(8,128)S(1)}, f32[656,128]{1,0:T(8,128)S(1)}, u32[]{:S(2)}, u32[]{:S(2)}) collective-permute-start(f32[656,128]{1,0:T(8,128)S(1)} %collective-permute-done.17.refs_5_), channel_id=1, source_target_pairs={{0,1},{1,0},{2,3},{3,2},{4,5},{5,4},{6,7},{7,6},{8,9},{9,8},{10,11... | collective-permute-start | bytes 1007624 | tf_op jit(solution)/shard_map/ppermute | solution.py:702
  81.5 1.2 %collective-permute-start.20 = (f32[8,128]{1,0:T(8,128)S(1)}, f32[8,128]{1,0:T(8,128)S(1)}, u32[]{:S(2)}, u32[]{:S(2)}) collective-permute-start(f32[8,128]{1,0:T(8,128)S(1)} %get-tuple-element.188.total_ref), channel_id=1, source_target_pairs={{0,1},{1,0},{2,3},{3,2},{4,5},{5,4},{6,7},{7,6},{8,9},{9,8},{10,11... | collective-permute-start | bytes 12296 | tf_op jit(solution)/shard_map/ppermute | solution.py:702
  82.7 5.9 %collective-permute-start.23 = (f32[8,128]{1,0:T(8,128)S(1)}, f32[8,128]{1,0:T(8,128)S(1)}, u32[]{:S(2)}, u32[]{:S(2)}) collective-permute-start(f32[8,128]{1,0:T(8,128)S(1)} %get-tuple-element.189.refs_13_.total_ref), channel_id=1, source_target_pairs={{0,6},{1,7},{2,4},{3,5},{4,2},{5,3},{6,0},{7,1},{8,14},{9,15},{10,... | collective-permute-start | bytes 12296 | tf_op jit(solution)/shard_map/ppermute | solution.py:702
  85.6 4.5 %collective-permute-start.22 = (f32[8,128]{1,0:T(8,128)S(1)}, f32[8,128]{1,0:T(8,128)S(1)}, u32[]{:S(2)}, u32[]{:S(2)}) collective-permute-start(f32[8,128]{1,0:T(8,128)S(1)} %get-tuple-element.189.refs_13_.total_ref), channel_id=1, source_target_pairs={{0,4},{1,5},{2,6},{3,7},{4,0},{5,1},{6,2},{7,3},{8,12},{9,13},{10,... | collective-permute-start | bytes 12296 | tf_op jit(solution)/shard_map/ppermute | solution.py:702
  85.8 4.2 %collective-permute-start.21 = (f32[8,128]{1,0:T(8,128)S(1)}, f32[8,128]{1,0:T(8,128)S(1)}, u32[]{:S(2)}, u32[]{:S(2)}) collective-permute-start(f32[8,128]{1,0:T(8,128)S(1)} %get-tuple-element.189.refs_13_.total_ref), channel_id=1, source_target_pairs={{0,2},{1,3},{2,0},{3,1},{4,6},{5,7},{6,4},{7,5},{8,10},{9,11},{10,... | collective-permute-start | bytes 12296 | tf_op jit(solution)/shard_map/ppermute | solution.py:702
  90.1 6.4 %collective-permute-start.26 = (f32[8,128]{1,0:T(8,128)S(1)}, f32[8,128]{1,0:T(8,128)S(1)}, u32[]{:S(2)}, u32[]{:S(2)}) collective-permute-start(f32[8,128]{1,0:T(8,128)S(1)} %get-tuple-element.196.refs_13_), channel_id=1, source_target_pairs={{24,0},{25,1},{26,2},{27,3},{28,4},{29,5},{30,6},{31,7}} | collective-permute-start | bytes 12296 | tf_op jit(solution)/shard_map/ppermute | solution.py:702
  91.4 5.5 %collective-permute-start.25 = (f32[8,128]{1,0:T(8,128)S(1)}, f32[8,128]{1,0:T(8,128)S(1)}, u32[]{:S(2)}, u32[]{:S(2)}) collective-permute-start(f32[8,128]{1,0:T(8,128)S(1)} %get-tuple-element.196.refs_13_), channel_id=1, source_target_pairs={{16,0},{17,1},{18,2},{19,3},{20,4},{21,5},{22,6},{23,7},{24,8},{25... | collective-permute-start | bytes 12296 | tf_op jit(solution)/shard_map/ppermute | solution.py:702
  92.7 5.5 %collective-permute-start.24 = (f32[8,128]{1,0:T(8,128)S(1)}, f32[8,128]{1,0:T(8,128)S(1)}, u32[]{:S(2)}, u32[]{:S(2)}) collective-permute-start(f32[8,128]{1,0:T(8,128)S(1)} %get-tuple-element.196.refs_13_), channel_id=1, source_target_pairs={{8,0},{9,1},{10,2},{11,3},{12,4},{13,5},{14,6},{15,7},{16,8},{17,9... | collective-permute-start | bytes 12296 | tf_op jit(solution)/shard_map/ppermute | solution.py:702

commit v18 on v17

--- a/solution.py
+++ b/solution.py
@@ -122,7 +122,7 @@
 
 
 STEPS = 2
-SUMMARY_STEPS = 5
+SUMMARY_STEPS = 1
 
 
 def summary_kernel(heads, chips, half, x_ref, g_ref, write_ref, read_ref, *refs):
@@ -559,13 +559,12 @@
 
 
 def finish_kernel(
-    heads, start, steps, last, x_ref, g_ref, write_ref, read_ref, tail_ref, lead_ref,
+    heads, head_size, start, steps, last, x_ref, g_ref, write_ref, read_ref, tail_ref, lead_ref,
     dx_ref, db_ref, dc_ref, change_ref, state_ref, back_ref, *refs,
 ):
     grad_ref, db_out, dc_out, change_out, token_ref, db_sum, dc_sum, sum_out = refs[-8:]
     chunk = pl.program_id(0)
     lanes = x_ref.shape[1]
-    head_size = lanes * STEPS * HALVES // heads
     wide = start + chunk
 
     @pl.when(chunk == 0)
@@ -600,17 +599,17 @@
             change_out[...] = sum_out[...]
 
 
-def finish(heads, start, steps, after, x, g, write_map, read_map, shared, dx, sums, state, back, grad):
+def finish(heads, lanes, start, steps, after, x, g, write_map, read_map, shared, dx, sums, state, back, grad):
     tokens, wide = x.shape
-    lanes = wide // (STEPS * HALVES)
     strip = pl.BlockSpec((tokens, lanes), lambda c: (0, start + c))
-    own = pl.BlockSpec((STATE, lanes), lambda c: (0, start % STEPS + c))
-    last = start + steps == STEPS * HALVES
+    first = start % (wide // HALVES // lanes)
+    own = pl.BlockSpec((STATE, lanes), lambda c: (0, first + c))
+    last = (start + steps) * lanes == wide
     kind = BF16 if last else F32
     change = (heads, tokens) if last else (tokens, STATE)
     earlier = [] if grad is None else [grad]
     return pl.pallas_call(
-        lambda *refs: finish_kernel(heads, start, steps, last, *refs),
+        lambda *refs: finish_kernel(heads, wide // heads, start, steps, last, *refs),
         grid=(steps,),
         in_specs=[strip, strip]
         + [whole(tokens, STATE)] * 4
@@ -777,13 +776,14 @@
         elif levels + 1 < step < rounds - 1:
             waiting[0], waiting[1] = lax.optimization_barrier((waiting[0], waiting[1]))
     dx, state_own, back_own, change, db, dc = block
+    lanes = inputs.shape[1] // HALVES // STEPS
     own_b = held[1][0]
     far_b = to_core(own_b)
     state, back, counted = assemble(
         heads, chips, 0, True, change, first[0], state_own, back_own, held[0], waiting[0]
     )
     grad, *sums, counted = finish(
-        heads, 0, STEPS, counted, *maps, shared, dx, (db, dc, change), state, back, None
+        heads, lanes * STEPS, 0, 1, counted, *maps, shared, dx, (db, dc, change), state, back, None
     )
     got, far_b, counted = lax.optimization_barrier((waiting[1], far_b, counted))
     own_b, far_b = (own_b, got), (far_b, to_core(got))
@@ -794,12 +794,12 @@
     later, counted = tiles(core_kernel, "core_sum", counted, to_core(counted))
     got = [to_chip(counted, step) for step in range(1, chips)]
     grad, *sums, token = finish(
-        heads, STEPS, 1, counted, *maps, shared, dx, sums, state, back, grad
+        heads, lanes, STEPS, 1, counted, *maps, shared, dx, sums, state, back, grad
     )
     later, counted = tiles(count_kernel, "chip_sum", token, later, counted, *got)
     got = [to_earlier(counted, step) for step in range(1, groups)]
     grad, *sums, _ = finish(
-        heads, STEPS + 1, 1, counted, *maps, shared, dx, sums, state, back, grad
+        heads, lanes, STEPS + 1, 1, counted, *maps, shared, dx, sums, state, back, grad
     )
     return (grad, sums[0], sums[1], add_later(sums[2], later, *got))
 

time: 99.4 us -> 94.9 us (0.955)
  Pallas kernels: 35.6 us -> 30.5 us
    pallas_call x2, Pallas kernels: 11.4 us -> 7.13 us  [summary(): pl.pallas_call(lambda *refs: summary_kernel(heads, chips, half, *refs), g...]
  transfers between devices with their start and end apart: 27 -> 27, of which waited for: 18 -> 18; matrix products, arithmetic and copies ran while one was open for 0% -> 0% of each run, Pallas kernels for 28% -> 26%
where the time goes in v18:
time: 94.9 us; the launch traced here: 94.6 us
  starting transfers between devices  32.8 us (35%)
  Pallas kernels  30.5 us (32%)
  waiting for transfers between devices  30.3 us (32%)
  between operations  0.96 us (1%)
    ppermute x27, starting transfers between devices, move(): return lax.ppermute(value, ('grp', 'seq'), pairs)  32.8 us
    ppermute x27, waiting for transfers between devices, move(): return lax.ppermute(value, ('grp', 'seq'), pairs)  30.3 us
    pallas_call x3, Pallas kernels, intra(): pl.pallas_call(lambda *refs: intra_kernel(heads, wide // heads, start, la...  12.5 us
    pallas_call x2, Pallas kernels, summary(): pl.pallas_call(lambda *refs: summary_kernel(heads, chips, half, *refs), g...  7.13 us
    pallas_call x3, Pallas kernels, finish(): pl.pallas_call(lambda *refs: finish_kernel(heads, wide // heads, start, s...  6.38 us
  transfers between devices with their start and end apart: 27, of which 18 were waited for; matrix products, arithmetic and copies ran while one was open for 0% of the time, Pallas kernels for 26%

profile of v18, /device:TPU:0, one launch (start us, length us, event | category | flops | bytes accessed | tf_op | source)
XLA Modules:
  0.0 94.6 jit_solution(759218022377795127)
XLA Ops:
  0.6 3.9 %summary.2 = (f32[1288,128]{1,0:T(8,128)}, f32[1280,128]{1,0:T(8,128)}, f32[10,128]{1,0:T(8,128)}, f32[8,128]{1,0:T(8,128)}, f32[256,128]{1,0:T(8,128)}, /*index...) custom-call(bf16[256,2560]{1,0:T(8,128)(2,1)} %refs_0_.9, bf16[256,2560]{1,0:T(8,128)(2,1)} %refs_1_.15, ...), custom_call_target="tpu_custom_call" | custom-call | flops 1 | bytes 1 | tf_op jit(solution)/shard_map/summary/pallas_call | solution.py:196
  4.5 0.5 collective-permute-start
  5.0 3.3 %summary.3 = (f32[1288,128]{1,0:T(8,128)}, f32[1280,128]{1,0:T(8,128)}, f32[10,128]{1,0:T(8,128)}) custom-call(bf16[256,2560]{1,0:T(8,128)(2,1)} %refs_0_.9, bf16[256,2560]{1,0:T(8,128)(2,1)} %refs_1_.15, bf16[256,128]{1,0:T(8,128)(2,1)} %refs_2_.15, bf16[256,128]{1,0:T(8,128)(2,1)} %refs_3_.15, f32[8,128]{1,0:T(8,128)} %get-tuple-element.108.refs_3_.refs_4_, ...), custom_call_target="tpu_custom_call" | custom-call | flops 1 | bytes 1 | tf_op jit(solution)/shard_map/summary/pallas_call | solution.py:196
  8.4 0.1 combine.2
  8.5 3.1 %collective-permute-start.1 = (f32[656,128]{1,0:T(8,128)S(1)}, f32[656,128]{1,0:T(8,128)S(1)}, u32[]{:S(2)}, u32[]{:S(2)}) collective-permute-start(f32[656,128]{1,0:T(8,128)S(1)} %get-tuple-element.110.refs_0_.refs_1_), channel_id=1, source_target_pairs={{0,2},{1,3},{2,0},{3,1},{4,6},{5,7},{6,4},{7,5},{8,10},{9,11},{10,... | collective-permute-start | bytes 1007624 | tf_op jit(solution)/shard_map/ppermute | solution.py:701
  11.7 5.1 %intra.3 = (f32[256,2560]{1,0:T(8,128)S(1)}, f32[128,2560]{1,0:T(8,128)S(1)}, f32[128,2560]{1,0:T(8,128)S(1)}, f32[256,128]{1,0:T(8,128)S(1)}, f32[256,256]{1,0:T(8,128)S(1)}) custom-call(f32[656,128]{1,0:T(8,128)S(1)} %get-tuple-element.110.refs_0_.refs_1_, bf16[256,2560]{1,0:T(8,128)(2,1)S(1)} %copy-done, bf16[256,2560]{1,0:T(8,128)(2,1)S(1)} %copy-done.1, ...), custom_call_target="tpu_custom_call" | custom-call | flops 1 | bytes 1 | tf_op jit(solution)/shard_map/intra/pallas_call | solution.py:442
  16.7 2.9 %collective-permute-done.1.refs_2_ = f32[656,128]{1,0:T(8,128)S(1)} collective-permute-done((f32[656,128]{1,0:T(8,128)S(1)}, f32[656,128]{1,0:T(8,128)S(1)}, u32[]{:S(2)}, u32[]{:S(2)}) %collective-permute-start.1) | collective-permute-done | bytes 335904 | tf_op jit(solution)/shard_map/ppermute | solution.py:701
  19.7 0.1 combine.3
  19.8 1.8 %collective-permute-start.4 = (f32[656,128]{1,0:T(8,128)S(1)}, f32[656,128]{1,0:T(8,128)S(1)}, u32[]{:S(2)}, u32[]{:S(2)}) collective-permute-start(f32[656,128]{1,0:T(8,128)S(1)} %get-tuple-element.124.refs_1_), channel_id=1, source_target_pairs={{0,2},{1,3},{2,0},{3,1},{4,6},{5,7},{6,4},{7,5},{8,10},{9,11},{10,... | collective-permute-start | bytes 1007624 | tf_op jit(solution)/shard_map/ppermute | solution.py:701
  21.6 0.2 up.4
  21.8 2.7 %collective-permute-start.3 = (f32[336,128]{1,0:T(8,128)S(1)}, f32[336,128]{1,0:T(8,128)S(1)}, u32[]{:S(2)}, u32[]{:S(2)}) collective-permute-start(f32[336,128]{1,0:T(8,128)S(1)} %get-tuple-element.120.refs_0_.refs_1_), channel_id=1, source_target_pairs={{0,4},{1,5},{2,6},{3,7},{4,0},{5,1},{6,2},{7,3},{8,12},{9,13},{10,... | collective-permute-start | bytes 516104 | tf_op jit(solution)/shard_map/ppermute | solution.py:701
  24.4 5.0 %intra.4 = (f32[256,2560]{1,0:T(8,128)S(1)}, f32[128,2560]{1,0:T(8,128)S(1)}, f32[128,2560]{1,0:T(8,128)S(1)}, f32[256,128]{1,0:T(8,128)S(1)}, f32[256,256]{1,0:T(8,128)S(1)}) custom-call(f32[336,128]{1,0:T(8,128)S(1)} %get-tuple-element.120.refs_0_.refs_1_, ...), custom_call_target="tpu_custom_call", output_to_operand_aliasing={{0}: (9, {}), {1}: (10, {}), {2}: (11, {})} | custom-call | flops 1 | bytes 1 | tf_op jit(solution)/shard_map/intra/pallas_call | solution.py:442
  29.4 2.3 %collective-permute-done.3.refs_2_ = f32[336,128]{1,0:T(8,128)S(1)} collective-permute-done((f32[336,128]{1,0:T(8,128)S(1)}, f32[336,128]{1,0:T(8,128)S(1)}, u32[]{:S(2)}, u32[]{:S(2)}) %collective-permute-start.3) | collective-permute-done | bytes 172064 | tf_op jit(solution)/shard_map/ppermute | solution.py:701
  31.7 1.1 %collective-permute-done.4.refs_2_ = f32[656,128]{1,0:T(8,128)S(1)} collective-permute-done((f32[656,128]{1,0:T(8,128)S(1)}, f32[656,128]{1,0:T(8,128)S(1)}, u32[]{:S(2)}, u32[]{:S(2)}) %collective-permute-start.4) | collective-permute-done | bytes 335904 | tf_op jit(solution)/shard_map/ppermute | solution.py:701
  32.8 0.2 up.6
  33.0 2.4 %collective-permute-start.8 = (f32[336,128]{1,0:T(8,128)S(1)}, f32[336,128]{1,0:T(8,128)S(1)}, u32[]{:S(2)}, u32[]{:S(2)}) collective-permute-start(f32[336,128]{1,0:T(8,128)S(1)} %get-tuple-element.138.refs_1_), channel_id=1, source_target_pairs={{0,4},{1,5},{2,6},{3,7},{4,0},{5,1},{6,2},{7,3},{8,12},{9,13},{10,... | collective-permute-start | bytes 516104 | tf_op jit(solution)/shard_map/ppermute | solution.py:701
  35.4 0.2 up.5.refs_0_
  35.6 1.3 %collective-permute-start.7 = (f32[328,128]{1,0:T(8,128)S(1)}, f32[328,128]{1,0:T(8,128)S(1)}, u32[]{:S(2)}, u32[]{:S(2)}) collective-permute-start(f32[328,128]{1,0:T(8,128)S(1)} %up.5.refs_0_), channel_id=1, source_target_pairs={{1,25},{3,27},{5,29},{7,31},{24,0},{26,2},{28,4},{30,6}} | collective-permute-start | bytes 503816 | tf_op jit(solution)/shard_map/ppermute | solution.py:701
  36.9 1.3 %collective-permute-start.6 = (f32[328,128]{1,0:T(8,128)S(1)}, f32[328,128]{1,0:T(8,128)S(1)}, u32[]{:S(2)}, u32[]{:S(2)}) collective-permute-start(f32[328,128]{1,0:T(8,128)S(1)} %up.5.refs_0_), channel_id=1, source_target_pairs={{1,17},{3,19},{5,21},{7,23},{9,25},{11,27},{13,29},{15,31},{16,0},... | collective-permute-start | bytes 503816 | tf_op jit(solution)/shard_map/ppermute | solution.py:701
  38.2 1.3 %collective-permute-start.5 = (f32[328,128]{1,0:T(8,128)S(1)}, f32[328,128]{1,0:T(8,128)S(1)}, u32[]{:S(2)}, u32[]{:S(2)}) collective-permute-start(f32[328,128]{1,0:T(8,128)S(1)} %up.5.refs_0_), channel_id=1, source_target_pairs={{1,9},{3,11},{5,13},{7,15},{8,0},{9,17},{10,2},{11,19},{12,4},{13,... | collective-permute-start | bytes 503816 | tf_op jit(solution)/shard_map/ppermute | solution.py:701
  39.5 2.5 %intra.5 = (f32[256,2560]{1,0:T(8,128)S(1)}, f32[128,2560]{1,0:T(8,128)S(1)}, f32[128,2560]{1,0:T(8,128)S(1)}, f32[256,128]{1,0:T(8,128)S(1)}, f32[256,128]{1,0:T(8,128)S(1)}, /*index=5*/f32[256,128]{1,0:T(8,128)S(1)}) custom-call(f32[328,128]{1,0:T(8,128)S(1)} %up.5.refs_0_, ...), custom_call_target="tpu_custom_call", output_to_operand_aliasing={{0}: (9, {}), {1}: (10, {}), {2}: (11, {})} | custom-call | flops 1 | bytes 1 | tf_op jit(solution)/shard_map/intra/pallas_call | solution.py:442
  42.0 1.9 %collective-permute-done.7.refs_5_ = f32[328,128]{1,0:T(8,128)S(1)} collective-permute-done((f32[328,128]{1,0:T(8,128)S(1)}, f32[328,128]{1,0:T(8,128)S(1)}, u32[]{:S(2)}, u32[]{:S(2)}) %collective-permute-start.7) | collective-permute-done | bytes 167968 | tf_op jit(solution)/shard_map/ppermute | solution.py:701
  43.9 1.7 %collective-permute-done.6.refs_4_ = f32[328,128]{1,0:T(8,128)S(1)} collective-permute-done((f32[328,128]{1,0:T(8,128)S(1)}, f32[328,128]{1,0:T(8,128)S(1)}, u32[]{:S(2)}, u32[]{:S(2)}) %collective-permute-start.6) | collective-permute-done | bytes 167968 | tf_op jit(solution)/shard_map/ppermute | solution.py:701
  45.6 0.2 down.4
  45.9 0.8 collective-permute-start.9
  46.7 0.2 up.7
  46.9 1.3 %collective-permute-start.13 = (f32[328,128]{1,0:T(8,128)S(1)}, f32[328,128]{1,0:T(8,128)S(1)}, u32[]{:S(2)}, u32[]{:S(2)}) collective-permute-start(f32[328,128]{1,0:T(8,128)S(1)} %up.7), channel_id=1, source_target_pairs={{1,25},{3,27},{5,29},{7,31},{24,0},{26,2},{28,4},{30,6}} | collective-permute-start | bytes 503816 | tf_op jit(solution)/shard_map/ppermute | solution.py:701
  48.2 1.3 %collective-permute-start.12 = (f32[328,128]{1,0:T(8,128)S(1)}, f32[328,128]{1,0:T(8,128)S(1)}, u32[]{:S(2)}, u32[]{:S(2)}) collective-permute-start(f32[328,128]{1,0:T(8,128)S(1)} %up.7), channel_id=1, source_target_pairs={{1,17},{3,19},{5,21},{7,23},{9,25},{11,27},{13,29},{15,31},{16,0},... | collective-permute-start | bytes 503816 | tf_op jit(solution)/shard_map/ppermute | solution.py:701
  49.5 1.5 %collective-permute-start.11 = (f32[328,128]{1,0:T(8,128)S(1)}, f32[328,128]{1,0:T(8,128)S(1)}, u32[]{:S(2)}, u32[]{:S(2)}) collective-permute-start(f32[328,128]{1,0:T(8,128)S(1)} %up.7), channel_id=1, source_target_pairs={{1,9},{3,11},{5,13},{7,15},{8,0},{9,17},{10,2},{11,19},{12,4},{13,... | collective-permute-start | bytes 503816 | tf_op jit(solution)/shard_map/ppermute | solution.py:701
  51.0 3.7 %collective-permute-done.9.refs_4_ = f32[336,128]{1,0:T(8,128)S(1)} collective-permute-done((f32[336,128]{1,0:T(8,128)S(1)}, f32[336,128]{1,0:T(8,128)S(1)}, u32[]{:S(2)}, u32[]{:S(2)}) %collective-permute-start.9) | collective-permute-done | bytes 172064 | tf_op jit(solution)/shard_map/ppermute | solution.py:701
  54.6 0.2 down.5
  54.9 0.1 collective-permute-start.10
  55.0 0.2 collective-permute-done.13.refs_5_
  55.1 1.7 %collective-permute-done.12.refs_4_ = f32[328,128]{1,0:T(8,128)S(1)} collective-permute-done((f32[328,128]{1,0:T(8,128)S(1)}, f32[328,128]{1,0:T(8,128)S(1)}, u32[]{:S(2)}, u32[]{:S(2)}) %collective-permute-start.12) | collective-permute-done | bytes 167968 | tf_op jit(solution)/shard_map/ppermute | solution.py:701
  56.8 0.3 down.6
  57.1 2.3 %collective-permute-start.14 = (f32[336,128]{1,0:T(8,128)S(1)}, f32[336,128]{1,0:T(8,128)S(1)}, u32[]{:S(2)}, u32[]{:S(2)}) collective-permute-start(f32[336,128]{1,0:T(8,128)S(1)} %get-tuple-element.166), channel_id=1, source_target_pairs={{0,4},{1,5},{2,6},{3,7},{4,0},{5,1},{6,2},{7,3},{8,12},{9,13},{10,... | collective-permute-start | bytes 516104 | tf_op jit(solution)/shard_map/ppermute | solution.py:701
  59.3 5.8 %collective-permute-done.14.refs_4_ = f32[336,128]{1,0:T(8,128)S(1)} collective-permute-done((f32[336,128]{1,0:T(8,128)S(1)}, f32[336,128]{1,0:T(8,128)S(1)}, u32[]{:S(2)}, u32[]{:S(2)}) %collective-permute-start.14) | collective-permute-done | bytes 172064 | tf_op jit(solution)/shard_map/ppermute | solution.py:701
  65.2 0.4 collective-permute-done.10.got_ref
  65.5 0.2 down.7
  65.8 2.0 %collective-permute-start.17 = (f32[656,128]{1,0:T(8,128)S(1)}, f32[656,128]{1,0:T(8,128)S(1)}, u32[]{:S(2)}, u32[]{:S(2)}) collective-permute-start(f32[656,128]{1,0:T(8,128)S(1)} %get-tuple-element.178), channel_id=1, source_target_pairs={{0,2},{1,3},{2,0},{3,1},{4,6},{5,7},{6,4},{7,5},{8,10},{9,11},{10,... | collective-permute-start | bytes 1007624 | tf_op jit(solution)/shard_map/ppermute | solution.py:701
  67.9 0.1 collective-permute-start.15
  68.0 0.5 collective-permute-start.16
  68.5 0.1 collective-permute-start.18
  68.6 1.0 %collective-permute-done.15.refs_6_ = f32[640,128]{1,0:T(8,128)S(1)} collective-permute-done((f32[640,128]{1,0:T(8,128)S(1)}, f32[640,128]{1,0:T(8,128)S(1)}, u32[]{:S(2)}, u32[]{:S(2)}) %collective-permute-start.15) | collective-permute-done | bytes 327712 | tf_op jit(solution)/shard_map/ppermute | solution.py:701
  69.6 0.5 collective-permute-done.16.refs_7_
  70.1 0.8 assemble.2
  70.8 2.9 %finish.3 = (bf16[256,2560]{1,0:T(8,128)(2,1)}, f32[256,128]{1,0:T(8,128)S(1)}, f32[256,128]{1,0:T(8,128)S(1)}, f32[256,128]{1,0:T(8,128)S(1)}, f32[8,128]{1,0:T(8,128)S(1)}) custom-call(bf16[256,2560]{1,0:T(8,128)(2,1)S(1)} %copy-done, bf16[256,2560]{1,0:T(8,128)(2,1)S(1)} %copy-done.1, bf16[256,128]{1,0:T(8,128)(2,1)S(1)} %copy-done.2, ...), custom_call_target="tpu_custom_call" | custom-call | flops 1 | bytes 1 | tf_op jit(solution)/shard_map/finish/pallas_call | solution.py:611
  73.7 0.1 collective-permute-start.19
  73.9 1.5 %collective-permute-done.19.refs_7_ = f32[656,128]{1,0:T(8,128)S(1)} collective-permute-done((f32[656,128]{1,0:T(8,128)S(1)}, f32[656,128]{1,0:T(8,128)S(1)}, u32[]{:S(2)}, u32[]{:S(2)}) %collective-permute-start.19) | collective-permute-done | bytes 335904 | tf_op jit(solution)/shard_map/ppermute | solution.py:701
  75.4 0.8 assemble.3
  76.2 0.2 collective-permute-start.20
  76.4 1.0 %collective-permute-done.20.got_ref = f32[8,128]{1,0:T(8,128)S(1)} collective-permute-done((f32[8,128]{1,0:T(8,128)S(1)}, f32[8,128]{1,0:T(8,128)S(1)}, u32[]{:S(2)}, u32[]{:S(2)}) %collective-permute-start.20) | collective-permute-done | bytes 4128 | tf_op jit(solution)/shard_map/ppermute | solution.py:701
  77.4 3.8 %collective-permute-start.23 = (f32[8,128]{1,0:T(8,128)S(1)}, f32[8,128]{1,0:T(8,128)S(1)}, u32[]{:S(2)}, u32[]{:S(2)}) collective-permute-start(f32[8,128]{1,0:T(8,128)S(1)} %get-tuple-element.189.refs_13_.total_ref), channel_id=1, source_target_pairs={{0,6},{1,7},{2,4},{3,5},{4,2},{5,3},{6,0},{7,1},{8,14},{9,15},{10,... | collective-permute-start | bytes 12296 | tf_op jit(solution)/shard_map/ppermute | solution.py:701
  81.2 0.6 collective-permute-start.21
  81.8 1.5 %finish.4 = (bf16[256,2560]{1,0:T(8,128)(2,1)}, f32[256,128]{1,0:T(8,128)S(1)}, f32[256,128]{1,0:T(8,128)S(1)}, f32[256,128]{1,0:T(8,128)S(1)}, f32[8,128]{1,0:T(8,128)S(1)}) custom-call(bf16[256,2560]{1,0:T(8,128)(2,1)S(1)} %copy-done, bf16[256,2560]{1,0:T(8,128)(2,1)S(1)} %copy-done.1, ...), custom_call_target="tpu_custom_call", output_to_operand_aliasing={{0}: (12, {})} | custom-call | flops 1 | bytes 1 | tf_op jit(solution)/shard_map/finish/pallas_call | solution.py:611
  83.3 2.4 %collective-permute-done.22.refs_1_ = f32[8,128]{1,0:T(8,128)S(1)} collective-permute-done((f32[8,128]{1,0:T(8,128)S(1)}, f32[8,128]{1,0:T(8,128)S(1)}, u32[]{:S(2)}, u32[]{:S(2)}) %collective-permute-start.22) | collective-permute-done | bytes 4128 | tf_op jit(solution)/shard_map/ppermute | solution.py:701
  85.7 1.3 %collective-permute-start.26 = (f32[8,128]{1,0:T(8,128)S(1)}, f32[8,128]{1,0:T(8,128)S(1)}, u32[]{:S(2)}, u32[]{:S(2)}) collective-permute-start(f32[8,128]{1,0:T(8,128)S(1)} %get-tuple-element.196.refs_13_), channel_id=1, source_target_pairs={{24,0},{25,1},{26,2},{27,3},{28,4},{29,5},{30,6},{31,7}} | collective-permute-start | bytes 12296 | tf_op jit(solution)/shard_map/ppermute | solution.py:701
  87.0 1.3 %collective-permute-start.25 = (f32[8,128]{1,0:T(8,128)S(1)}, f32[8,128]{1,0:T(8,128)S(1)}, u32[]{:S(2)}, u32[]{:S(2)}) collective-permute-start(f32[8,128]{1,0:T(8,128)S(1)} %get-tuple-element.196.refs_13_), channel_id=1, source_target_pairs={{16,0},{17,1},{18,2},{19,3},{20,4},{21,5},{22,6},{23,7},{24,8},{25... | collective-permute-start | bytes 12296 | tf_op jit(solution)/shard_map/ppermute | solution.py:701
  88.3 1.3 %collective-permute-start.24 = (f32[8,128]{1,0:T(8,128)S(1)}, f32[8,128]{1,0:T(8,128)S(1)}, u32[]{:S(2)}, u32[]{:S(2)}) collective-permute-start(f32[8,128]{1,0:T(8,128)S(1)} %get-tuple-element.196.refs_13_), channel_id=1, source_target_pairs={{8,0},{9,1},{10,2},{11,3},{12,4},{13,5},{14,6},{15,7},{16,8},{17,9... | collective-permute-start | bytes 12296 | tf_op jit(solution)/shard_map/ppermute | solution.py:701
  89.6 2.0 %finish.5 = (bf16[256,2560]{1,0:T(8,128)(2,1)}, bf16[256,128]{1,0:T(8,128)(2,1)}, bf16[256,128]{1,0:T(8,128)(2,1)}, f32[40,256]{1,0:T(8,128)S(1)}, f32[8,128]{1,0:T(8,128)}) custom-call(bf16[256,2560]{1,0:T(8,128)(2,1)S(1)} %copy-done, bf16[256,2560]{1,0:T(8,128)(2,1)S(1)} %copy-done.1, ...), custom_call_target="tpu_custom_call", output_to_operand_aliasing={{0}: (12, {})} | custom-call | flops 1 | bytes 1 | tf_op jit(solution)/shard_map/finish/pallas_call | solution.py:611
  91.6 0.5 collective-permute-done.26.refs_3_
  92.1 0.4 collective-permute-done.25.refs_2_
  92.5 1.3 %collective-permute-done.24.refs_1_ = f32[8,128]{1,0:T(8,128)S(1)} collective-permute-done((f32[8,128]{1,0:T(8,128)S(1)}, f32[8,128]{1,0:T(8,128)S(1)}, u32[]{:S(2)}, u32[]{:S(2)}) %collective-permute-start.24) | collective-permute-done | bytes 4128 | tf_op jit(solution)/shard_map/ppermute | solution.py:701
  93.8 0.8 add_later.1
  (40 shorter events, 0.3 us)
Async XLA Ops:
  4.5 3.9 %collective-permute-start = (f32[1288,128]{1,0:T(8,128)}, f32[1288,128]{1,0:T(8,128)S(1)}, u32[]{:S(2)}, u32[]{:S(2)}) collective-permute-start(f32[1288,128]{1,0:T(8,128)} %get-tuple-element.105), channel_id=1, source_target_pairs={{0,1},{1,0},{2,3},{3,2},{4,5},{5,4},{6,7},{7,6},{8,9},{9,8},{10,11... | collective-permute-start | bytes 1978376 | tf_op jit(solution)/shard_map/ppermute | solution.py:701
  4.9 3.4 %copy-start.8 = (f32[1280,128]{1,0:T(8,128)S(1)}, f32[1280,128]{1,0:T(8,128)}, u32[]{:S(2)}) copy-start(f32[1280,128]{1,0:T(8,128)} %get-tuple-element.106.refs_1_) | copy-start | bytes 1966084
  5.0 3.4 %copy-start.10 = (f32[8,128]{1,0:T(8,128)S(1)}, f32[8,128]{1,0:T(8,128)}, u32[]{:S(2)}) copy-start(f32[8,128]{1,0:T(8,128)} %get-tuple-element.108.refs_3_.refs_4_) | copy-start | bytes 12292
  5.0 3.4 %copy-start.12 = (f32[10,128]{1,0:T(8,128)S(1)}, f32[10,128]{1,0:T(8,128)}, u32[]{:S(2)}) copy-start(f32[10,128]{1,0:T(8,128)} %get-tuple-element.107.refs_2_) | copy-start | bytes 15364
  5.0 6.6 %copy-start.1 = (bf16[256,2560]{1,0:T(8,128)(2,1)S(1)}, bf16[256,2560]{1,0:T(8,128)(2,1)}, u32[]{:S(2)}) copy-start(bf16[256,2560]{1,0:T(8,128)(2,1)} %refs_1_.15) | copy-start | bytes 3932164
  5.0 6.6 %copy-start.2 = (bf16[256,128]{1,0:T(8,128)(2,1)S(1)}, bf16[256,128]{1,0:T(8,128)(2,1)}, u32[]{:S(2)}) copy-start(bf16[256,128]{1,0:T(8,128)(2,1)} %refs_2_.15) | copy-start | bytes 196612
  5.0 6.6 %copy-start.3 = (bf16[256,128]{1,0:T(8,128)(2,1)S(1)}, bf16[256,128]{1,0:T(8,128)(2,1)}, u32[]{:S(2)}) copy-start(bf16[256,128]{1,0:T(8,128)(2,1)} %refs_3_.15) | copy-start | bytes 196612
  5.0 6.6 %copy-start.4 = (bf16[256,128]{1,0:T(8,128)(2,1)S(1)}, bf16[256,128]{1,0:T(8,128)(2,1)}, u32[]{:S(2)}) copy-start(bf16[256,128]{1,0:T(8,128)(2,1)} %get-tuple-element.103.refs_5_.refs_7_.refs_4_) | copy-start | bytes 196612
  5.0 6.6 %copy-start.5 = (bf16[256,128]{1,0:T(8,128)(2,1)S(1)}, bf16[256,128]{1,0:T(8,128)(2,1)}, u32[]{:S(2)}) copy-start(bf16[256,128]{1,0:T(8,128)(2,1)} %get-tuple-element.104.refs_6_.refs_8_.refs_5_) | copy-start | bytes 196612
  5.0 6.6 %copy-start.6 = (f32[256,128]{1,0:T(8,128)S(1)}, f32[256,128]{1,0:T(8,128)}, u32[]{:S(2)}) copy-start(f32[256,128]{1,0:T(8,128)} %get-tuple-element.112.refs_6_) | copy-start | bytes 393220
  5.0 6.6 %copy-start.9 = (f32[40,256]{1,0:T(8,128)S(1)}, f32[40,256]{1,0:T(8,128)}, u32[]{:S(2)}) copy-start(f32[40,256]{1,0:T(8,128)} %refs_5_.5) | copy-start | bytes 122884
  8.3 3.3 %copy-start = (bf16[256,2560]{1,0:T(8,128)(2,1)S(1)}, bf16[256,2560]{1,0:T(8,128)(2,1)}, u32[]{:S(2)}) copy-start(bf16[256,2560]{1,0:T(8,128)(2,1)} %refs_0_.9) | copy-start | bytes 3932164
  8.3 8.4 %collective-permute-start.2 = (f32[1288,128]{1,0:T(8,128)}, f32[1288,128]{1,0:T(8,128)S(1)}, u32[]{:S(2)}, u32[]{:S(2)}) collective-permute-start(f32[1288,128]{1,0:T(8,128)} %get-tuple-element.111), channel_id=1, source_target_pairs={{0,1},{1,0},{2,3},{3,2},{4,5},{5,4},{6,7},{7,6},{8,9},{9,8},{10,11... | collective-permute-start | bytes 1978376 | tf_op jit(solution)/shard_map/ppermute | solution.py:701
  8.5 11.2 %collective-permute-start.1 = (f32[656,128]{1,0:T(8,128)S(1)}, f32[656,128]{1,0:T(8,128)S(1)}, u32[]{:S(2)}, u32[]{:S(2)}) collective-permute-start(f32[656,128]{1,0:T(8,128)S(1)} %get-tuple-element.110.refs_0_.refs_1_), channel_id=1, source_target_pairs={{0,2},{1,3},{2,0},{3,1},{4,6},{5,7},{6,4},{7,5},{8,10},{9,11},{10,... | collective-permute-start | bytes 1007624 | tf_op jit(solution)/shard_map/ppermute | solution.py:701
  11.6 8.0 %copy-start.7 = (f32[1280,128]{1,0:T(8,128)S(1)}, f32[1280,128]{1,0:T(8,128)}, u32[]{:S(2)}) copy-start(f32[1280,128]{1,0:T(8,128)} %get-tuple-element.122.refs_1_) | copy-start | bytes 1966084
  11.6 8.0 %copy-start.11 = (f32[10,128]{1,0:T(8,128)S(1)}, f32[10,128]{1,0:T(8,128)}, u32[]{:S(2)}) copy-start(f32[10,128]{1,0:T(8,128)} %get-tuple-element.123.refs_2_) | copy-start | bytes 15364
  19.8 13.0 %collective-permute-start.4 = (f32[656,128]{1,0:T(8,128)S(1)}, f32[656,128]{1,0:T(8,128)S(1)}, u32[]{:S(2)}, u32[]{:S(2)}) collective-permute-start(f32[656,128]{1,0:T(8,128)S(1)} %get-tuple-element.124.refs_1_), channel_id=1, source_target_pairs={{0,2},{1,3},{2,0},{3,1},{4,6},{5,7},{6,4},{7,5},{8,10},{9,11},{10,... | collective-permute-start | bytes 1007624 | tf_op jit(solution)/shard_map/ppermute | solution.py:701
  21.8 10.0 %collective-permute-start.3 = (f32[336,128]{1,0:T(8,128)S(1)}, f32[336,128]{1,0:T(8,128)S(1)}, u32[]{:S(2)}, u32[]{:S(2)}) collective-permute-start(f32[336,128]{1,0:T(8,128)S(1)} %get-tuple-element.120.refs_0_.refs_1_), channel_id=1, source_target_pairs={{0,4},{1,5},{2,6},{3,7},{4,0},{5,1},{6,2},{7,3},{8,12},{9,13},{10,... | collective-permute-start | bytes 516104 | tf_op jit(solution)/shard_map/ppermute | solution.py:701
  33.0 12.6 %collective-permute-start.8 = (f32[336,128]{1,0:T(8,128)S(1)}, f32[336,128]{1,0:T(8,128)S(1)}, u32[]{:S(2)}, u32[]{:S(2)}) collective-permute-start(f32[336,128]{1,0:T(8,128)S(1)} %get-tuple-element.138.refs_1_), channel_id=1, source_target_pairs={{0,4},{1,5},{2,6},{3,7},{4,0},{5,1},{6,2},{7,3},{8,12},{9,13},{10,... | collective-permute-start | bytes 516104 | tf_op jit(solution)/shard_map/ppermute | solution.py:701
  35.6 8.3 %collective-permute-start.7 = (f32[328,128]{1,0:T(8,128)S(1)}, f32[328,128]{1,0:T(8,128)S(1)}, u32[]{:S(2)}, u32[]{:S(2)}) collective-permute-start(f32[328,128]{1,0:T(8,128)S(1)} %up.5.refs_0_), channel_id=1, source_target_pairs={{1,25},{3,27},{5,29},{7,31},{24,0},{26,2},{28,4},{30,6}} | collective-permute-start | bytes 503816 | tf_op jit(solution)/shard_map/ppermute | solution.py:701
  36.9 8.7 %collective-permute-start.6 = (f32[328,128]{1,0:T(8,128)S(1)}, f32[328,128]{1,0:T(8,128)S(1)}, u32[]{:S(2)}, u32[]{:S(2)}) collective-permute-start(f32[328,128]{1,0:T(8,128)S(1)} %up.5.refs_0_), channel_id=1, source_target_pairs={{1,17},{3,19},{5,21},{7,23},{9,25},{11,27},{13,29},{15,31},{16,0},... | collective-permute-start | bytes 503816 | tf_op jit(solution)/shard_map/ppermute | solution.py:701
  38.2 7.4 %collective-permute-start.5 = (f32[328,128]{1,0:T(8,128)S(1)}, f32[328,128]{1,0:T(8,128)S(1)}, u32[]{:S(2)}, u32[]{:S(2)}) collective-permute-start(f32[328,128]{1,0:T(8,128)S(1)} %up.5.refs_0_), channel_id=1, source_target_pairs={{1,9},{3,11},{5,13},{7,15},{8,0},{9,17},{10,2},{11,19},{12,4},{13,... | collective-permute-start | bytes 503816 | tf_op jit(solution)/shard_map/ppermute | solution.py:701
  45.9 8.7 %collective-permute-start.9 = (f32[336,128]{1,0:T(8,128)S(1)}, f32[336,128]{1,0:T(8,128)S(1)}, u32[]{:S(2)}, u32[]{:S(2)}) collective-permute-start(f32[336,128]{1,0:T(8,128)S(1)} %get-tuple-element.161), channel_id=1, source_target_pairs={{0,4},{1,5},{2,6},{3,7},{4,0},{5,1},{6,2},{7,3},{8,12},{9,13},{10,... | collective-permute-start | bytes 516104 | tf_op jit(solution)/shard_map/ppermute | solution.py:701
  46.9 8.3 %collective-permute-start.13 = (f32[328,128]{1,0:T(8,128)S(1)}, f32[328,128]{1,0:T(8,128)S(1)}, u32[]{:S(2)}, u32[]{:S(2)}) collective-permute-start(f32[328,128]{1,0:T(8,128)S(1)} %up.7), channel_id=1, source_target_pairs={{1,25},{3,27},{5,29},{7,31},{24,0},{26,2},{28,4},{30,6}} | collective-permute-start | bytes 503816 | tf_op jit(solution)/shard_map/ppermute | solution.py:701
  48.2 8.7 %collective-permute-start.12 = (f32[328,128]{1,0:T(8,128)S(1)}, f32[328,128]{1,0:T(8,128)S(1)}, u32[]{:S(2)}, u32[]{:S(2)}) collective-permute-start(f32[328,128]{1,0:T(8,128)S(1)} %up.7), channel_id=1, source_target_pairs={{1,17},{3,19},{5,21},{7,23},{9,25},{11,27},{13,29},{15,31},{16,0},... | collective-permute-start | bytes 503816 | tf_op jit(solution)/shard_map/ppermute | solution.py:701
  49.5 7.4 %collective-permute-start.11 = (f32[328,128]{1,0:T(8,128)S(1)}, f32[328,128]{1,0:T(8,128)S(1)}, u32[]{:S(2)}, u32[]{:S(2)}) collective-permute-start(f32[328,128]{1,0:T(8,128)S(1)} %up.7), channel_id=1, source_target_pairs={{1,9},{3,11},{5,13},{7,15},{8,0},{9,17},{10,2},{11,19},{12,4},{13,... | collective-permute-start | bytes 503816 | tf_op jit(solution)/shard_map/ppermute | solution.py:701
  54.9 10.7 %collective-permute-start.10 = (f32[656,128]{1,0:T(8,128)S(1)}, f32[656,128]{1,0:T(8,128)S(1)}, u32[]{:S(2)}, u32[]{:S(2)}) collective-permute-start(f32[656,128]{1,0:T(8,128)S(1)} %get-tuple-element.163), channel_id=1, source_target_pairs={{0,2},{1,3},{2,0},{3,1},{4,6},{5,7},{6,4},{7,5},{8,10},{9,11},{10,... | collective-permute-start | bytes 1007624 | tf_op jit(solution)/shard_map/ppermute | solution.py:701
  57.1 8.1 %collective-permute-start.14 = (f32[336,128]{1,0:T(8,128)S(1)}, f32[336,128]{1,0:T(8,128)S(1)}, u32[]{:S(2)}, u32[]{:S(2)}) collective-permute-start(f32[336,128]{1,0:T(8,128)S(1)} %get-tuple-element.166), channel_id=1, source_target_pairs={{0,4},{1,5},{2,6},{3,7},{4,0},{5,1},{6,2},{7,3},{8,12},{9,13},{10,... | collective-permute-start | bytes 516104 | tf_op jit(solution)/shard_map/ppermute | solution.py:701
  65.8 7.9 %collective-permute-start.17 = (f32[656,128]{1,0:T(8,128)S(1)}, f32[656,128]{1,0:T(8,128)S(1)}, u32[]{:S(2)}, u32[]{:S(2)}) collective-permute-start(f32[656,128]{1,0:T(8,128)S(1)} %get-tuple-element.178), channel_id=1, source_target_pairs={{0,2},{1,3},{2,0},{3,1},{4,6},{5,7},{6,4},{7,5},{8,10},{9,11},{10,... | collective-permute-start | bytes 1007624 | tf_op jit(solution)/shard_map/ppermute | solution.py:701
  67.9 1.7 %collective-permute-start.15 = (f32[640,128]{1,0:T(8,128)S(1)}, f32[640,128]{1,0:T(8,128)S(1)}, u32[]{:S(2)}, u32[]{:S(2)}) collective-permute-start(f32[640,128]{1,0:T(8,128)S(1)} %get-tuple-element.168.refs_4_), channel_id=1, source_target_pairs={{0,1},{1,0},{2,3},{3,2},{4,5},{5,4},{6,7},{7,6},{8,9},{9,8},{10,11... | collective-permute-start | bytes 983048 | tf_op jit(solution)/shard_map/ppermute | solution.py:701
  68.0 2.1 %collective-permute-start.16 = (f32[640,128]{1,0:T(8,128)S(1)}, f32[640,128]{1,0:T(8,128)S(1)}, u32[]{:S(2)}, u32[]{:S(2)}) collective-permute-start(f32[640,128]{1,0:T(8,128)S(1)} %get-tuple-element.169.refs_5_), channel_id=1, source_target_pairs={{0,1},{1,0},{2,3},{3,2},{4,5},{5,4},{6,7},{7,6},{8,9},{9,8},{10,11... | collective-permute-start | bytes 983048 | tf_op jit(solution)/shard_map/ppermute | solution.py:701
  68.5 5.2 %collective-permute-start.18 = (f32[640,128]{1,0:T(8,128)S(1)}, f32[640,128]{1,0:T(8,128)S(1)}, u32[]{:S(2)}, u32[]{:S(2)}) collective-permute-start(f32[640,128]{1,0:T(8,128)S(1)} %get-tuple-element.179.refs_4_), channel_id=1, source_target_pairs={{0,1},{1,0},{2,3},{3,2},{4,5},{5,4},{6,7},{7,6},{8,9},{9,8},{10,11... | collective-permute-start | bytes 983048 | tf_op jit(solution)/shard_map/ppermute | solution.py:701
  73.7 1.6 %collective-permute-start.19 = (f32[656,128]{1,0:T(8,128)S(1)}, f32[656,128]{1,0:T(8,128)S(1)}, u32[]{:S(2)}, u32[]{:S(2)}) collective-permute-start(f32[656,128]{1,0:T(8,128)S(1)} %collective-permute-done.17.refs_5_), channel_id=1, source_target_pairs={{0,1},{1,0},{2,3},{3,2},{4,5},{5,4},{6,7},{7,6},{8,9},{9,8},{10,11... | collective-permute-start | bytes 1007624 | tf_op jit(solution)/shard_map/ppermute | solution.py:701
  76.2 1.2 %collective-permute-start.20 = (f32[8,128]{1,0:T(8,128)S(1)}, f32[8,128]{1,0:T(8,128)S(1)}, u32[]{:S(2)}, u32[]{:S(2)}) collective-permute-start(f32[8,128]{1,0:T(8,128)S(1)} %get-tuple-element.188.total_ref), channel_id=1, source_target_pairs={{0,1},{1,0},{2,3},{3,2},{4,5},{5,4},{6,7},{7,6},{8,9},{9,8},{10,11... | collective-permute-start | bytes 12296 | tf_op jit(solution)/shard_map/ppermute | solution.py:701
  77.4 5.9 %collective-permute-start.23 = (f32[8,128]{1,0:T(8,128)S(1)}, f32[8,128]{1,0:T(8,128)S(1)}, u32[]{:S(2)}, u32[]{:S(2)}) collective-permute-start(f32[8,128]{1,0:T(8,128)S(1)} %get-tuple-element.189.refs_13_.total_ref), channel_id=1, source_target_pairs={{0,6},{1,7},{2,4},{3,5},{4,2},{5,3},{6,0},{7,1},{8,14},{9,15},{10,... | collective-permute-start | bytes 12296 | tf_op jit(solution)/shard_map/ppermute | solution.py:701
  81.2 4.5 %collective-permute-start.22 = (f32[8,128]{1,0:T(8,128)S(1)}, f32[8,128]{1,0:T(8,128)S(1)}, u32[]{:S(2)}, u32[]{:S(2)}) collective-permute-start(f32[8,128]{1,0:T(8,128)S(1)} %get-tuple-element.189.refs_13_.total_ref), channel_id=1, source_target_pairs={{0,4},{1,5},{2,6},{3,7},{4,0},{5,1},{6,2},{7,3},{8,12},{9,13},{10,... | collective-permute-start | bytes 12296 | tf_op jit(solution)/shard_map/ppermute | solution.py:701
  81.2 4.5 %collective-permute-start.21 = (f32[8,128]{1,0:T(8,128)S(1)}, f32[8,128]{1,0:T(8,128)S(1)}, u32[]{:S(2)}, u32[]{:S(2)}) collective-permute-start(f32[8,128]{1,0:T(8,128)S(1)} %get-tuple-element.189.refs_13_.total_ref), channel_id=1, source_target_pairs={{0,2},{1,3},{2,0},{3,1},{4,6},{5,7},{6,4},{7,5},{8,10},{9,11},{10,... | collective-permute-start | bytes 12296 | tf_op jit(solution)/shard_map/ppermute | solution.py:701
  85.7 6.4 %collective-permute-start.26 = (f32[8,128]{1,0:T(8,128)S(1)}, f32[8,128]{1,0:T(8,128)S(1)}, u32[]{:S(2)}, u32[]{:S(2)}) collective-permute-start(f32[8,128]{1,0:T(8,128)S(1)} %get-tuple-element.196.refs_13_), channel_id=1, source_target_pairs={{24,0},{25,1},{26,2},{27,3},{28,4},{29,5},{30,6},{31,7}} | collective-permute-start | bytes 12296 | tf_op jit(solution)/shard_map/ppermute | solution.py:701
  87.0 5.5 %collective-permute-start.25 = (f32[8,128]{1,0:T(8,128)S(1)}, f32[8,128]{1,0:T(8,128)S(1)}, u32[]{:S(2)}, u32[]{:S(2)}) collective-permute-start(f32[8,128]{1,0:T(8,128)S(1)} %get-tuple-element.196.refs_13_), channel_id=1, source_target_pairs={{16,0},{17,1},{18,2},{19,3},{20,4},{21,5},{22,6},{23,7},{24,8},{25... | collective-permute-start | bytes 12296 | tf_op jit(solution)/shard_map/ppermute | solution.py:701
  88.3 5.5 %collective-permute-start.24 = (f32[8,128]{1,0:T(8,128)S(1)}, f32[8,128]{1,0:T(8,128)S(1)}, u32[]{:S(2)}, u32[]{:S(2)}) collective-permute-start(f32[8,128]{1,0:T(8,128)S(1)} %get-tuple-element.196.refs_13_), channel_id=1, source_target_pairs={{8,0},{9,1},{10,2},{11,3},{12,4},{13,5},{14,6},{15,7},{16,8},{17,9... | collective-permute-start | bytes 12296 | tf_op jit(solution)/shard_map/ppermute | solution.py:701

commit v19 on v18

--- a/solution.py
+++ b/solution.py
@@ -770,9 +770,12 @@
             more = pl.cdiv(chunks - ready, 3 - step)
             block = intra(ready, more, token, *maps, log_decay, shared, block)
             ready += more
-            waiting[0], waiting[1], first[1], block = lax.optimization_barrier(
-                (waiting[0], waiting[1], first[1], block)
-            )
+            if step < 2:
+                waiting[0], waiting[1], first[1], block = lax.optimization_barrier(
+                    (waiting[0], waiting[1], first[1], block)
+                )
+            else:
+                waiting[1], block = lax.optimization_barrier((waiting[1], block))
         elif levels + 1 < step < rounds - 1:
             waiting[0], waiting[1] = lax.optimization_barrier((waiting[0], waiting[1]))
     dx, state_own, back_own, change, db, dc = block

time: 94.9 us -> 102 us (1.075)
  waiting for transfers between devices: 30.3 us -> 38.5 us
  starting transfers between devices: 32.8 us -> 31.3 us
    ppermute x27, waiting for transfers between devices: 30.3 us -> 38.5 us  [move(): return lax.ppermute(value, ('grp', 'seq'), pairs)]
    ppermute x27, starting transfers between devices: 32.8 us -> 31.3 us  [move(): return lax.ppermute(value, ('grp', 'seq'), pairs)]
  transfers between devices with their start and end apart: 27 -> 27, of which waited for: 18 -> 20; matrix products, arithmetic and copies ran while one was open for 0% -> 0% of each run, Pallas kernels for 26% -> 24%
where the time goes in v19:
time: 102 us; the launch traced here: 101 us
  waiting for transfers between devices  38.5 us (38%)
  starting transfers between devices  31.3 us (31%)
  Pallas kernels  30.5 us (30%)
    ppermute x27, waiting for transfers between devices, move(): return lax.ppermute(value, ('grp', 'seq'), pairs)  38.5 us
    ppermute x27, starting transfers between devices, move(): return lax.ppermute(value, ('grp', 'seq'), pairs)  31.3 us
    pallas_call x3, Pallas kernels, intra(): pl.pallas_call(lambda *refs: intra_kernel(heads, wide // heads, start, la...  12.5 us
    pallas_call x2, Pallas kernels, summary(): pl.pallas_call(lambda *refs: summary_kernel(heads, chips, half, *refs), g...  7.13 us
    pallas_call x3, Pallas kernels, finish(): pl.pallas_call(lambda *refs: finish_kernel(heads, wide // heads, start, s...  6.38 us
  transfers between devices with their start and end apart: 27, of which 20 were waited for; matrix products, arithmetic and copies ran while one was open for 0% of the time, Pallas kernels for 24%

profile of v19, /device:TPU:0, one launch (start us, length us, event | category | flops | bytes accessed | tf_op | source)
XLA Modules:
  0.0 101.2 jit_solution(9270590313654337663)
XLA Ops:
  0.6 3.9 %summary.2 = (f32[1288,128]{1,0:T(8,128)}, f32[1280,128]{1,0:T(8,128)}, f32[10,128]{1,0:T(8,128)}, f32[8,128]{1,0:T(8,128)}, f32[256,128]{1,0:T(8,128)}, /*index...) custom-call(bf16[256,2560]{1,0:T(8,128)(2,1)} %refs_0_.9, bf16[256,2560]{1,0:T(8,128)(2,1)} %refs_1_.15, ...), custom_call_target="tpu_custom_call" | custom-call | flops 1 | bytes 1 | tf_op jit(solution)/shard_map/summary/pallas_call | solution.py:196
  4.5 0.5 collective-permute-start
  5.0 3.3 %summary.3 = (f32[1288,128]{1,0:T(8,128)}, f32[1280,128]{1,0:T(8,128)}, f32[10,128]{1,0:T(8,128)}) custom-call(bf16[256,2560]{1,0:T(8,128)(2,1)} %refs_0_.9, bf16[256,2560]{1,0:T(8,128)(2,1)} %refs_1_.15, bf16[256,128]{1,0:T(8,128)(2,1)} %refs_2_.15, bf16[256,128]{1,0:T(8,128)(2,1)} %refs_3_.15, f32[8,128]{1,0:T(8,128)} %get-tuple-element.104.refs_3_.refs_4_, ...), custom_call_target="tpu_custom_call" | custom-call | flops 1 | bytes 1 | tf_op jit(solution)/shard_map/summary/pallas_call | solution.py:196
  8.4 0.1 combine.2
  8.5 3.1 %collective-permute-start.1 = (f32[656,128]{1,0:T(8,128)S(1)}, f32[656,128]{1,0:T(8,128)S(1)}, u32[]{:S(2)}, u32[]{:S(2)}) collective-permute-start(f32[656,128]{1,0:T(8,128)S(1)} %get-tuple-element.105.refs_0_.refs_1_), channel_id=1, source_target_pairs={{0,2},{1,3},{2,0},{3,1},{4,6},{5,7},{6,4},{7,5},{8,10},{9,11},{10,... | collective-permute-start | bytes 1007624 | tf_op jit(solution)/shard_map/ppermute | solution.py:701
  11.7 5.1 %intra.3 = (f32[256,2560]{1,0:T(8,128)S(1)}, f32[128,2560]{1,0:T(8,128)S(1)}, f32[128,2560]{1,0:T(8,128)S(1)}, f32[256,128]{1,0:T(8,128)S(1)}, f32[256,256]{1,0:T(8,128)S(1)}) custom-call(f32[656,128]{1,0:T(8,128)S(1)} %get-tuple-element.105.refs_0_.refs_1_, bf16[256,2560]{1,0:T(8,128)(2,1)S(1)} %copy-done, bf16[256,2560]{1,0:T(8,128)(2,1)S(1)} %copy-done.1, ...), custom_call_target="tpu_custom_call" | custom-call | flops 1 | bytes 1 | tf_op jit(solution)/shard_map/intra/pallas_call | solution.py:442
  16.7 2.9 %collective-permute-done.1.refs_2_ = f32[656,128]{1,0:T(8,128)S(1)} collective-permute-done((f32[656,128]{1,0:T(8,128)S(1)}, f32[656,128]{1,0:T(8,128)S(1)}, u32[]{:S(2)}, u32[]{:S(2)}) %collective-permute-start.1) | collective-permute-done | bytes 335904 | tf_op jit(solution)/shard_map/ppermute | solution.py:701
  19.7 0.1 combine.3
  19.8 1.8 %collective-permute-start.4 = (f32[656,128]{1,0:T(8,128)S(1)}, f32[656,128]{1,0:T(8,128)S(1)}, u32[]{:S(2)}, u32[]{:S(2)}) collective-permute-start(f32[656,128]{1,0:T(8,128)S(1)} %get-tuple-element.117.refs_1_), channel_id=1, source_target_pairs={{0,2},{1,3},{2,0},{3,1},{4,6},{5,7},{6,4},{7,5},{8,10},{9,11},{10,... | collective-permute-start | bytes 1007624 | tf_op jit(solution)/shard_map/ppermute | solution.py:701
  21.6 0.2 up.4
  21.8 2.7 %collective-permute-start.3 = (f32[336,128]{1,0:T(8,128)S(1)}, f32[336,128]{1,0:T(8,128)S(1)}, u32[]{:S(2)}, u32[]{:S(2)}) collective-permute-start(f32[336,128]{1,0:T(8,128)S(1)} %get-tuple-element.120.refs_0_.refs_1_), channel_id=1, source_target_pairs={{0,4},{1,5},{2,6},{3,7},{4,0},{5,1},{6,2},{7,3},{8,12},{9,13},{10,... | collective-permute-start | bytes 516104 | tf_op jit(solution)/shard_map/ppermute | solution.py:701
  24.4 5.0 %intra.4 = (f32[256,2560]{1,0:T(8,128)S(1)}, f32[128,2560]{1,0:T(8,128)S(1)}, f32[128,2560]{1,0:T(8,128)S(1)}, f32[256,128]{1,0:T(8,128)S(1)}, f32[256,256]{1,0:T(8,128)S(1)}) custom-call(f32[336,128]{1,0:T(8,128)S(1)} %get-tuple-element.120.refs_0_.refs_1_, ...), custom_call_target="tpu_custom_call", output_to_operand_aliasing={{0}: (9, {}), {1}: (10, {}), {2}: (11, {})} | custom-call | flops 1 | bytes 1 | tf_op jit(solution)/shard_map/intra/pallas_call | solution.py:442
  29.4 2.3 %collective-permute-done.3.refs_2_ = f32[336,128]{1,0:T(8,128)S(1)} collective-permute-done((f32[336,128]{1,0:T(8,128)S(1)}, f32[336,128]{1,0:T(8,128)S(1)}, u32[]{:S(2)}, u32[]{:S(2)}) %collective-permute-start.3) | collective-permute-done | bytes 172064 | tf_op jit(solution)/shard_map/ppermute | solution.py:701
  31.7 1.1 %collective-permute-done.4.refs_2_ = f32[656,128]{1,0:T(8,128)S(1)} collective-permute-done((f32[656,128]{1,0:T(8,128)S(1)}, f32[656,128]{1,0:T(8,128)S(1)}, u32[]{:S(2)}, u32[]{:S(2)}) %collective-permute-start.4) | collective-permute-done | bytes 335904 | tf_op jit(solution)/shard_map/ppermute | solution.py:701
  32.8 0.2 up.6.refs_0_
  33.0 1.3 %collective-permute-start.8 = (f32[328,128]{1,0:T(8,128)S(1)}, f32[328,128]{1,0:T(8,128)S(1)}, u32[]{:S(2)}, u32[]{:S(2)}) collective-permute-start(f32[328,128]{1,0:T(8,128)S(1)} %up.6.refs_0_), channel_id=1, source_target_pairs={{1,25},{3,27},{5,29},{7,31},{24,0},{26,2},{28,4},{30,6}} | collective-permute-start | bytes 503816 | tf_op jit(solution)/shard_map/ppermute | solution.py:701
  34.3 1.3 %collective-permute-start.7 = (f32[328,128]{1,0:T(8,128)S(1)}, f32[328,128]{1,0:T(8,128)S(1)}, u32[]{:S(2)}, u32[]{:S(2)}) collective-permute-start(f32[328,128]{1,0:T(8,128)S(1)} %up.6.refs_0_), channel_id=1, source_target_pairs={{1,17},{3,19},{5,21},{7,23},{9,25},{11,27},{13,29},{15,31},{16,0},... | collective-permute-start | bytes 503816 | tf_op jit(solution)/shard_map/ppermute | solution.py:701
  35.6 1.3 %collective-permute-start.6 = (f32[328,128]{1,0:T(8,128)S(1)}, f32[328,128]{1,0:T(8,128)S(1)}, u32[]{:S(2)}, u32[]{:S(2)}) collective-permute-start(f32[328,128]{1,0:T(8,128)S(1)} %up.6.refs_0_), channel_id=1, source_target_pairs={{1,9},{3,11},{5,13},{7,15},{8,0},{9,17},{10,2},{11,19},{12,4},{13,... | collective-permute-start | bytes 503816 | tf_op jit(solution)/shard_map/ppermute | solution.py:701
  36.9 0.2 up.5
  37.1 2.4 %collective-permute-start.5 = (f32[336,128]{1,0:T(8,128)S(1)}, f32[336,128]{1,0:T(8,128)S(1)}, u32[]{:S(2)}, u32[]{:S(2)}) collective-permute-start(f32[336,128]{1,0:T(8,128)S(1)} %get-tuple-element.132.refs_1_), channel_id=1, source_target_pairs={{0,4},{1,5},{2,6},{3,7},{4,0},{5,1},{6,2},{7,3},{8,12},{9,13},{10,... | collective-permute-start | bytes 516104 | tf_op jit(solution)/shard_map/ppermute | solution.py:701
  39.5 1.7 %collective-permute-done.8.refs_5_ = f32[328,128]{1,0:T(8,128)S(1)} collective-permute-done((f32[328,128]{1,0:T(8,128)S(1)}, f32[328,128]{1,0:T(8,128)S(1)}, u32[]{:S(2)}, u32[]{:S(2)}) %collective-permute-start.8) | collective-permute-done | bytes 167968 | tf_op jit(solution)/shard_map/ppermute | solution.py:701
  41.3 1.7 %collective-permute-done.7.refs_4_ = f32[328,128]{1,0:T(8,128)S(1)} collective-permute-done((f32[328,128]{1,0:T(8,128)S(1)}, f32[328,128]{1,0:T(8,128)S(1)}, u32[]{:S(2)}, u32[]{:S(2)}) %collective-permute-start.7) | collective-permute-done | bytes 167968 | tf_op jit(solution)/shard_map/ppermute | solution.py:701
  43.0 0.5 collective-permute-done.6.refs_3_
  43.4 0.2 down.4
  43.7 2.3 %collective-permute-start.9 = (f32[336,128]{1,0:T(8,128)S(1)}, f32[336,128]{1,0:T(8,128)S(1)}, u32[]{:S(2)}, u32[]{:S(2)}) collective-permute-start(f32[336,128]{1,0:T(8,128)S(1)} %get-tuple-element.153), channel_id=1, source_target_pairs={{0,4},{1,5},{2,6},{3,7},{4,0},{5,1},{6,2},{7,3},{8,12},{9,13},{10,... | collective-permute-start | bytes 516104 | tf_op jit(solution)/shard_map/ppermute | solution.py:701
  45.9 2.5 %intra.5 = (f32[256,2560]{1,0:T(8,128)S(1)}, f32[128,2560]{1,0:T(8,128)S(1)}, f32[128,2560]{1,0:T(8,128)S(1)}, f32[256,128]{1,0:T(8,128)S(1)}, f32[256,128]{1,0:T(8,128)S(1)}, /*index=5*/f32[256,128]{1,0:T(8,128)S(1)}) custom-call(f32[328,128]{1,0:T(8,128)S(1)} %up.6.refs_0_, ...), custom_call_target="tpu_custom_call", output_to_operand_aliasing={{0}: (9, {}), {1}: (10, {}), {2}: (11, {})} | custom-call | flops 1 | bytes 1 | tf_op jit(solution)/shard_map/intra/pallas_call | solution.py:442
  48.4 3.5 %collective-permute-done.5.refs_2_ = f32[336,128]{1,0:T(8,128)S(1)} collective-permute-done((f32[336,128]{1,0:T(8,128)S(1)}, f32[336,128]{1,0:T(8,128)S(1)}, u32[]{:S(2)}, u32[]{:S(2)}) %collective-permute-start.5) | collective-permute-done | bytes 172064 | tf_op jit(solution)/shard_map/ppermute | solution.py:701
  51.9 0.2 up.7
  52.1 1.3 %collective-permute-start.13 = (f32[328,128]{1,0:T(8,128)S(1)}, f32[328,128]{1,0:T(8,128)S(1)}, u32[]{:S(2)}, u32[]{:S(2)}) collective-permute-start(f32[328,128]{1,0:T(8,128)S(1)} %up.7), channel_id=1, source_target_pairs={{1,25},{3,27},{5,29},{7,31},{24,0},{26,2},{28,4},{30,6}} | collective-permute-start | bytes 503816 | tf_op jit(solution)/shard_map/ppermute | solution.py:701
  53.4 1.3 %collective-permute-start.12 = (f32[328,128]{1,0:T(8,128)S(1)}, f32[328,128]{1,0:T(8,128)S(1)}, u32[]{:S(2)}, u32[]{:S(2)}) collective-permute-start(f32[328,128]{1,0:T(8,128)S(1)} %up.7), channel_id=1, source_target_pairs={{1,17},{3,19},{5,21},{7,23},{9,25},{11,27},{13,29},{15,31},{16,0},... | collective-permute-start | bytes 503816 | tf_op jit(solution)/shard_map/ppermute | solution.py:701
  54.7 1.5 %collective-permute-start.11 = (f32[328,128]{1,0:T(8,128)S(1)}, f32[328,128]{1,0:T(8,128)S(1)}, u32[]{:S(2)}, u32[]{:S(2)}) collective-permute-start(f32[328,128]{1,0:T(8,128)S(1)} %up.7), channel_id=1, source_target_pairs={{1,9},{3,11},{5,13},{7,15},{8,0},{9,17},{10,2},{11,19},{12,4},{13,... | collective-permute-start | bytes 503816 | tf_op jit(solution)/shard_map/ppermute | solution.py:701
  56.2 0.2 down.5
  56.4 1.2 %collective-permute-start.10 = (f32[656,128]{1,0:T(8,128)S(1)}, f32[656,128]{1,0:T(8,128)S(1)}, u32[]{:S(2)}, u32[]{:S(2)}) collective-permute-start(f32[656,128]{1,0:T(8,128)S(1)} %get-tuple-element.155), channel_id=1, source_target_pairs={{0,2},{1,3},{2,0},{3,1},{4,6},{5,7},{6,4},{7,5},{8,10},{9,11},{10,... | collective-permute-start | bytes 1007624 | tf_op jit(solution)/shard_map/ppermute | solution.py:701
  57.6 2.7 %collective-permute-done.13.refs_5_ = f32[328,128]{1,0:T(8,128)S(1)} collective-permute-done((f32[328,128]{1,0:T(8,128)S(1)}, f32[328,128]{1,0:T(8,128)S(1)}, u32[]{:S(2)}, u32[]{:S(2)}) %collective-permute-start.13) | collective-permute-done | bytes 167968 | tf_op jit(solution)/shard_map/ppermute | solution.py:701
  60.4 1.7 %collective-permute-done.12.refs_4_ = f32[328,128]{1,0:T(8,128)S(1)} collective-permute-done((f32[328,128]{1,0:T(8,128)S(1)}, f32[328,128]{1,0:T(8,128)S(1)}, u32[]{:S(2)}, u32[]{:S(2)}) %collective-permute-start.12) | collective-permute-done | bytes 167968 | tf_op jit(solution)/shard_map/ppermute | solution.py:701
  62.0 0.8 collective-permute-done.11.refs_3_
  62.8 0.3 down.6
  63.2 10.0 %collective-permute-done.14.refs_4_ = f32[336,128]{1,0:T(8,128)S(1)} collective-permute-done((f32[336,128]{1,0:T(8,128)S(1)}, f32[336,128]{1,0:T(8,128)S(1)}, u32[]{:S(2)}, u32[]{:S(2)}) %collective-permute-start.14) | collective-permute-done | bytes 172064 | tf_op jit(solution)/shard_map/ppermute | solution.py:701
  73.2 0.2 down.7
  73.5 0.3 collective-permute-start.17
  73.9 0.5 collective-permute-start.16
  74.4 0.1 collective-permute-start.18
  74.5 1.0 %collective-permute-done.15.refs_6_ = f32[640,128]{1,0:T(8,128)S(1)} collective-permute-done((f32[640,128]{1,0:T(8,128)S(1)}, f32[640,128]{1,0:T(8,128)S(1)}, u32[]{:S(2)}, u32[]{:S(2)}) %collective-permute-start.15) | collective-permute-done | bytes 327712 | tf_op jit(solution)/shard_map/ppermute | solution.py:701
  75.5 0.5 collective-permute-done.16.refs_7_
  76.0 0.8 assemble.2
  76.7 2.9 %finish.3 = (bf16[256,2560]{1,0:T(8,128)(2,1)}, f32[256,128]{1,0:T(8,128)S(1)}, f32[256,128]{1,0:T(8,128)S(1)}, f32[256,128]{1,0:T(8,128)S(1)}, f32[8,128]{1,0:T(8,128)S(1)}) custom-call(bf16[256,2560]{1,0:T(8,128)(2,1)S(1)} %copy-done, bf16[256,2560]{1,0:T(8,128)(2,1)S(1)} %copy-done.1, bf16[256,128]{1,0:T(8,128)(2,1)S(1)} %copy-done.2, ...), custom_call_target="tpu_custom_call" | custom-call | flops 1 | bytes 1 | tf_op jit(solution)/shard_map/finish/pallas_call | solution.py:611
  79.6 2.2 %collective-permute-done.17.refs_5_ = f32[656,128]{1,0:T(8,128)S(1)} collective-permute-done((f32[656,128]{1,0:T(8,128)S(1)}, f32[656,128]{1,0:T(8,128)S(1)}, u32[]{:S(2)}, u32[]{:S(2)}) %collective-permute-start.17) | collective-permute-done | bytes 335904 | tf_op jit(solution)/shard_map/ppermute | solution.py:701
  81.8 1.6 %collective-permute-done.19.refs_7_ = f32[656,128]{1,0:T(8,128)S(1)} collective-permute-done((f32[656,128]{1,0:T(8,128)S(1)}, f32[656,128]{1,0:T(8,128)S(1)}, u32[]{:S(2)}, u32[]{:S(2)}) %collective-permute-start.19) | collective-permute-done | bytes 335904 | tf_op jit(solution)/shard_map/ppermute | solution.py:701
  83.5 0.8 assemble.3
  84.3 0.2 collective-permute-start.20
  84.5 1.0 %collective-permute-done.20.got_ref = f32[8,128]{1,0:T(8,128)S(1)} collective-permute-done((f32[8,128]{1,0:T(8,128)S(1)}, f32[8,128]{1,0:T(8,128)S(1)}, u32[]{:S(2)}, u32[]{:S(2)}) %collective-permute-start.20) | collective-permute-done | bytes 4128 | tf_op jit(solution)/shard_map/ppermute | solution.py:701
  85.5 1.3 %collective-permute-start.23 = (f32[8,128]{1,0:T(8,128)S(1)}, f32[8,128]{1,0:T(8,128)S(1)}, u32[]{:S(2)}, u32[]{:S(2)}) collective-permute-start(f32[8,128]{1,0:T(8,128)S(1)} %get-tuple-element.181.refs_13_.total_ref), channel_id=1, source_target_pairs={{0,6},{1,7},{2,4},{3,5},{4,2},{5,3},{6,0},{7,1},{8,14},{9,15},{10,... | collective-permute-start | bytes 12296 | tf_op jit(solution)/shard_map/ppermute | solution.py:701
  86.9 1.9 %collective-permute-start.22 = (f32[8,128]{1,0:T(8,128)S(1)}, f32[8,128]{1,0:T(8,128)S(1)}, u32[]{:S(2)}, u32[]{:S(2)}) collective-permute-start(f32[8,128]{1,0:T(8,128)S(1)} %get-tuple-element.181.refs_13_.total_ref), channel_id=1, source_target_pairs={{0,4},{1,5},{2,6},{3,7},{4,0},{5,1},{6,2},{7,3},{8,12},{9,13},{10,... | collective-permute-start | bytes 12296 | tf_op jit(solution)/shard_map/ppermute | solution.py:701
  88.7 1.2 %collective-permute-start.21 = (f32[8,128]{1,0:T(8,128)S(1)}, f32[8,128]{1,0:T(8,128)S(1)}, u32[]{:S(2)}, u32[]{:S(2)}) collective-permute-start(f32[8,128]{1,0:T(8,128)S(1)} %get-tuple-element.181.refs_13_.total_ref), channel_id=1, source_target_pairs={{0,2},{1,3},{2,0},{3,1},{4,6},{5,7},{6,4},{7,5},{8,10},{9,11},{10,... | collective-permute-start | bytes 12296 | tf_op jit(solution)/shard_map/ppermute | solution.py:701
  89.9 1.5 %finish.4 = (bf16[256,2560]{1,0:T(8,128)(2,1)}, f32[256,128]{1,0:T(8,128)S(1)}, f32[256,128]{1,0:T(8,128)S(1)}, f32[256,128]{1,0:T(8,128)S(1)}, f32[8,128]{1,0:T(8,128)S(1)}) custom-call(bf16[256,2560]{1,0:T(8,128)(2,1)S(1)} %copy-done, bf16[256,2560]{1,0:T(8,128)(2,1)S(1)} %copy-done.1, ...), custom_call_target="tpu_custom_call", output_to_operand_aliasing={{0}: (12, {})} | custom-call | flops 1 | bytes 1 | tf_op jit(solution)/shard_map/finish/pallas_call | solution.py:611
  91.5 0.9 collective-permute-done.21.refs_0_
  92.4 1.3 %collective-permute-start.26 = (f32[8,128]{1,0:T(8,128)S(1)}, f32[8,128]{1,0:T(8,128)S(1)}, u32[]{:S(2)}, u32[]{:S(2)}) collective-permute-start(f32[8,128]{1,0:T(8,128)S(1)} %get-tuple-element.188.refs_13_), channel_id=1, source_target_pairs={{24,0},{25,1},{26,2},{27,3},{28,4},{29,5},{30,6},{31,7}} | collective-permute-start | bytes 12296 | tf_op jit(solution)/shard_map/ppermute | solution.py:701
  93.7 1.3 %collective-permute-start.25 = (f32[8,128]{1,0:T(8,128)S(1)}, f32[8,128]{1,0:T(8,128)S(1)}, u32[]{:S(2)}, u32[]{:S(2)}) collective-permute-start(f32[8,128]{1,0:T(8,128)S(1)} %get-tuple-element.188.refs_13_), channel_id=1, source_target_pairs={{16,0},{17,1},{18,2},{19,3},{20,4},{21,5},{22,6},{23,7},{24,8},{25... | collective-permute-start | bytes 12296 | tf_op jit(solution)/shard_map/ppermute | solution.py:701
  95.0 1.3 %collective-permute-start.24 = (f32[8,128]{1,0:T(8,128)S(1)}, f32[8,128]{1,0:T(8,128)S(1)}, u32[]{:S(2)}, u32[]{:S(2)}) collective-permute-start(f32[8,128]{1,0:T(8,128)S(1)} %get-tuple-element.188.refs_13_), channel_id=1, source_target_pairs={{8,0},{9,1},{10,2},{11,3},{12,4},{13,5},{14,6},{15,7},{16,8},{17,9... | collective-permute-start | bytes 12296 | tf_op jit(solution)/shard_map/ppermute | solution.py:701
  96.3 2.0 %finish.5 = (bf16[256,2560]{1,0:T(8,128)(2,1)}, bf16[256,128]{1,0:T(8,128)(2,1)}, bf16[256,128]{1,0:T(8,128)(2,1)}, f32[40,256]{1,0:T(8,128)S(1)}, f32[8,128]{1,0:T(8,128)}) custom-call(bf16[256,2560]{1,0:T(8,128)(2,1)S(1)} %copy-done, bf16[256,2560]{1,0:T(8,128)(2,1)S(1)} %copy-done.1, ...), custom_call_target="tpu_custom_call", output_to_operand_aliasing={{0}: (12, {})} | custom-call | flops 1 | bytes 1 | tf_op jit(solution)/shard_map/finish/pallas_call | solution.py:611
  98.2 0.5 collective-permute-done.26.refs_3_
  98.8 0.4 collective-permute-done.25.refs_2_
  99.2 1.3 %collective-permute-done.24.refs_1_ = f32[8,128]{1,0:T(8,128)S(1)} collective-permute-done((f32[8,128]{1,0:T(8,128)S(1)}, f32[8,128]{1,0:T(8,128)S(1)}, u32[]{:S(2)}, u32[]{:S(2)}) %collective-permute-start.24) | collective-permute-done | bytes 4128 | tf_op jit(solution)/shard_map/ppermute | solution.py:701
  100.5 0.8 add_later.1
  (40 shorter events, 0.4 us)
Async XLA Ops:
  4.5 3.9 %collective-permute-start = (f32[1288,128]{1,0:T(8,128)}, f32[1288,128]{1,0:T(8,128)S(1)}, u32[]{:S(2)}, u32[]{:S(2)}) collective-permute-start(f32[1288,128]{1,0:T(8,128)} %get-tuple-element.101), channel_id=1, source_target_pairs={{0,1},{1,0},{2,3},{3,2},{4,5},{5,4},{6,7},{7,6},{8,9},{9,8},{10,11... | collective-permute-start | bytes 1978376 | tf_op jit(solution)/shard_map/ppermute | solution.py:701
  4.9 3.4 %copy-start.8 = (f32[1280,128]{1,0:T(8,128)S(1)}, f32[1280,128]{1,0:T(8,128)}, u32[]{:S(2)}) copy-start(f32[1280,128]{1,0:T(8,128)} %get-tuple-element.102.refs_1_) | copy-start | bytes 1966084
  5.0 3.4 %copy-start.10 = (f32[8,128]{1,0:T(8,128)S(1)}, f32[8,128]{1,0:T(8,128)}, u32[]{:S(2)}) copy-start(f32[8,128]{1,0:T(8,128)} %get-tuple-element.104.refs_3_.refs_4_) | copy-start | bytes 12292
  5.0 3.4 %copy-start.12 = (f32[10,128]{1,0:T(8,128)S(1)}, f32[10,128]{1,0:T(8,128)}, u32[]{:S(2)}) copy-start(f32[10,128]{1,0:T(8,128)} %get-tuple-element.103.refs_2_) | copy-start | bytes 15364
  5.0 6.6 %copy-start.1 = (bf16[256,2560]{1,0:T(8,128)(2,1)S(1)}, bf16[256,2560]{1,0:T(8,128)(2,1)}, u32[]{:S(2)}) copy-start(bf16[256,2560]{1,0:T(8,128)(2,1)} %refs_1_.15) | copy-start | bytes 3932164
  5.0 6.6 %copy-start.2 = (bf16[256,128]{1,0:T(8,128)(2,1)S(1)}, bf16[256,128]{1,0:T(8,128)(2,1)}, u32[]{:S(2)}) copy-start(bf16[256,128]{1,0:T(8,128)(2,1)} %refs_2_.15) | copy-start | bytes 196612
  5.0 6.6 %copy-start.3 = (bf16[256,128]{1,0:T(8,128)(2,1)S(1)}, bf16[256,128]{1,0:T(8,128)(2,1)}, u32[]{:S(2)}) copy-start(bf16[256,128]{1,0:T(8,128)(2,1)} %refs_3_.15) | copy-start | bytes 196612
  5.0 6.6 %copy-start.4 = (bf16[256,128]{1,0:T(8,128)(2,1)S(1)}, bf16[256,128]{1,0:T(8,128)(2,1)}, u32[]{:S(2)}) copy-start(bf16[256,128]{1,0:T(8,128)(2,1)} %get-tuple-element.99.refs_5_.refs_7_.refs_4_) | copy-start | bytes 196612
  5.0 6.6 %copy-start.5 = (bf16[256,128]{1,0:T(8,128)(2,1)S(1)}, bf16[256,128]{1,0:T(8,128)(2,1)}, u32[]{:S(2)}) copy-start(bf16[256,128]{1,0:T(8,128)(2,1)} %get-tuple-element.100.refs_6_.refs_8_.refs_5_) | copy-start | bytes 196612
  5.0 6.6 %copy-start.6 = (f32[256,128]{1,0:T(8,128)S(1)}, f32[256,128]{1,0:T(8,128)}, u32[]{:S(2)}) copy-start(f32[256,128]{1,0:T(8,128)} %get-tuple-element.107.refs_6_) | copy-start | bytes 393220
  5.0 6.6 %copy-start.9 = (f32[40,256]{1,0:T(8,128)S(1)}, f32[40,256]{1,0:T(8,128)}, u32[]{:S(2)}) copy-start(f32[40,256]{1,0:T(8,128)} %refs_5_.5) | copy-start | bytes 122884
  8.3 3.3 %copy-start = (bf16[256,2560]{1,0:T(8,128)(2,1)S(1)}, bf16[256,2560]{1,0:T(8,128)(2,1)}, u32[]{:S(2)}) copy-start(bf16[256,2560]{1,0:T(8,128)(2,1)} %refs_0_.9) | copy-start | bytes 3932164
  8.3 8.4 %collective-permute-start.2 = (f32[1288,128]{1,0:T(8,128)}, f32[1288,128]{1,0:T(8,128)S(1)}, u32[]{:S(2)}, u32[]{:S(2)}) collective-permute-start(f32[1288,128]{1,0:T(8,128)} %get-tuple-element.106), channel_id=1, source_target_pairs={{0,1},{1,0},{2,3},{3,2},{4,5},{5,4},{6,7},{7,6},{8,9},{9,8},{10,11... | collective-permute-start | bytes 1978376 | tf_op jit(solution)/shard_map/ppermute | solution.py:701
  8.5 11.2 %collective-permute-start.1 = (f32[656,128]{1,0:T(8,128)S(1)}, f32[656,128]{1,0:T(8,128)S(1)}, u32[]{:S(2)}, u32[]{:S(2)}) collective-permute-start(f32[656,128]{1,0:T(8,128)S(1)} %get-tuple-element.105.refs_0_.refs_1_), channel_id=1, source_target_pairs={{0,2},{1,3},{2,0},{3,1},{4,6},{5,7},{6,4},{7,5},{8,10},{9,11},{10,... | collective-permute-start | bytes 1007624 | tf_op jit(solution)/shard_map/ppermute | solution.py:701
  11.6 8.0 %copy-start.7 = (f32[1280,128]{1,0:T(8,128)S(1)}, f32[1280,128]{1,0:T(8,128)}, u32[]{:S(2)}) copy-start(f32[1280,128]{1,0:T(8,128)} %get-tuple-element.114.refs_1_) | copy-start | bytes 1966084
  11.6 8.0 %copy-start.11 = (f32[10,128]{1,0:T(8,128)S(1)}, f32[10,128]{1,0:T(8,128)}, u32[]{:S(2)}) copy-start(f32[10,128]{1,0:T(8,128)} %get-tuple-element.115.refs_2_) | copy-start | bytes 15364
  19.8 13.0 %collective-permute-start.4 = (f32[656,128]{1,0:T(8,128)S(1)}, f32[656,128]{1,0:T(8,128)S(1)}, u32[]{:S(2)}, u32[]{:S(2)}) collective-permute-start(f32[656,128]{1,0:T(8,128)S(1)} %get-tuple-element.117.refs_1_), channel_id=1, source_target_pairs={{0,2},{1,3},{2,0},{3,1},{4,6},{5,7},{6,4},{7,5},{8,10},{9,11},{10,... | collective-permute-start | bytes 1007624 | tf_op jit(solution)/shard_map/ppermute | solution.py:701
  21.8 10.0 %collective-permute-start.3 = (f32[336,128]{1,0:T(8,128)S(1)}, f32[336,128]{1,0:T(8,128)S(1)}, u32[]{:S(2)}, u32[]{:S(2)}) collective-permute-start(f32[336,128]{1,0:T(8,128)S(1)} %get-tuple-element.120.refs_0_.refs_1_), channel_id=1, source_target_pairs={{0,4},{1,5},{2,6},{3,7},{4,0},{5,1},{6,2},{7,3},{8,12},{9,13},{10,... | collective-permute-start | bytes 516104 | tf_op jit(solution)/shard_map/ppermute | solution.py:701
  33.0 8.3 %collective-permute-start.8 = (f32[328,128]{1,0:T(8,128)S(1)}, f32[328,128]{1,0:T(8,128)S(1)}, u32[]{:S(2)}, u32[]{:S(2)}) collective-permute-start(f32[328,128]{1,0:T(8,128)S(1)} %up.6.refs_0_), channel_id=1, source_target_pairs={{1,25},{3,27},{5,29},{7,31},{24,0},{26,2},{28,4},{30,6}} | collective-permute-start | bytes 503816 | tf_op jit(solution)/shard_map/ppermute | solution.py:701
  34.3 8.7 %collective-permute-start.7 = (f32[328,128]{1,0:T(8,128)S(1)}, f32[328,128]{1,0:T(8,128)S(1)}, u32[]{:S(2)}, u32[]{:S(2)}) collective-permute-start(f32[328,128]{1,0:T(8,128)S(1)} %up.6.refs_0_), channel_id=1, source_target_pairs={{1,17},{3,19},{5,21},{7,23},{9,25},{11,27},{13,29},{15,31},{16,0},... | collective-permute-start | bytes 503816 | tf_op jit(solution)/shard_map/ppermute | solution.py:701
  35.6 7.8 %collective-permute-start.6 = (f32[328,128]{1,0:T(8,128)S(1)}, f32[328,128]{1,0:T(8,128)S(1)}, u32[]{:S(2)}, u32[]{:S(2)}) collective-permute-start(f32[328,128]{1,0:T(8,128)S(1)} %up.6.refs_0_), channel_id=1, source_target_pairs={{1,9},{3,11},{5,13},{7,15},{8,0},{9,17},{10,2},{11,19},{12,4},{13,... | collective-permute-start | bytes 503816 | tf_op jit(solution)/shard_map/ppermute | solution.py:701
  37.1 14.8 %collective-permute-start.5 = (f32[336,128]{1,0:T(8,128)S(1)}, f32[336,128]{1,0:T(8,128)S(1)}, u32[]{:S(2)}, u32[]{:S(2)}) collective-permute-start(f32[336,128]{1,0:T(8,128)S(1)} %get-tuple-element.132.refs_1_), channel_id=1, source_target_pairs={{0,4},{1,5},{2,6},{3,7},{4,0},{5,1},{6,2},{7,3},{8,12},{9,13},{10,... | collective-permute-start | bytes 516104 | tf_op jit(solution)/shard_map/ppermute | solution.py:701
  43.7 12.5 %collective-permute-start.9 = (f32[336,128]{1,0:T(8,128)S(1)}, f32[336,128]{1,0:T(8,128)S(1)}, u32[]{:S(2)}, u32[]{:S(2)}) collective-permute-start(f32[336,128]{1,0:T(8,128)S(1)} %get-tuple-element.153), channel_id=1, source_target_pairs={{0,4},{1,5},{2,6},{3,7},{4,0},{5,1},{6,2},{7,3},{8,12},{9,13},{10,... | collective-permute-start | bytes 516104 | tf_op jit(solution)/shard_map/ppermute | solution.py:701
  52.1 8.3 %collective-permute-start.13 = (f32[328,128]{1,0:T(8,128)S(1)}, f32[328,128]{1,0:T(8,128)S(1)}, u32[]{:S(2)}, u32[]{:S(2)}) collective-permute-start(f32[328,128]{1,0:T(8,128)S(1)} %up.7), channel_id=1, source_target_pairs={{1,25},{3,27},{5,29},{7,31},{24,0},{26,2},{28,4},{30,6}} | collective-permute-start | bytes 503816 | tf_op jit(solution)/shard_map/ppermute | solution.py:701
  53.4 8.7 %collective-permute-start.12 = (f32[328,128]{1,0:T(8,128)S(1)}, f32[328,128]{1,0:T(8,128)S(1)}, u32[]{:S(2)}, u32[]{:S(2)}) collective-permute-start(f32[328,128]{1,0:T(8,128)S(1)} %up.7), channel_id=1, source_target_pairs={{1,17},{3,19},{5,21},{7,23},{9,25},{11,27},{13,29},{15,31},{16,0},... | collective-permute-start | bytes 503816 | tf_op jit(solution)/shard_map/ppermute | solution.py:701
  54.7 8.1 %collective-permute-start.11 = (f32[328,128]{1,0:T(8,128)S(1)}, f32[328,128]{1,0:T(8,128)S(1)}, u32[]{:S(2)}, u32[]{:S(2)}) collective-permute-start(f32[328,128]{1,0:T(8,128)S(1)} %up.7), channel_id=1, source_target_pairs={{1,9},{3,11},{5,13},{7,15},{8,0},{9,17},{10,2},{11,19},{12,4},{13,... | collective-permute-start | bytes 503816 | tf_op jit(solution)/shard_map/ppermute | solution.py:701
  56.4 16.8 %collective-permute-start.10 = (f32[656,128]{1,0:T(8,128)S(1)}, f32[656,128]{1,0:T(8,128)S(1)}, u32[]{:S(2)}, u32[]{:S(2)}) collective-permute-start(f32[656,128]{1,0:T(8,128)S(1)} %get-tuple-element.155), channel_id=1, source_target_pairs={{0,2},{1,3},{2,0},{3,1},{4,6},{5,7},{6,4},{7,5},{8,10},{9,11},{10,... | collective-permute-start | bytes 1007624 | tf_op jit(solution)/shard_map/ppermute | solution.py:701
  63.1 10.1 %collective-permute-start.14 = (f32[336,128]{1,0:T(8,128)S(1)}, f32[336,128]{1,0:T(8,128)S(1)}, u32[]{:S(2)}, u32[]{:S(2)}) collective-permute-start(f32[336,128]{1,0:T(8,128)S(1)} %get-tuple-element.158), channel_id=1, source_target_pairs={{0,4},{1,5},{2,6},{3,7},{4,0},{5,1},{6,2},{7,3},{8,12},{9,13},{10,... | collective-permute-start | bytes 516104 | tf_op jit(solution)/shard_map/ppermute | solution.py:701
  73.5 8.4 %collective-permute-start.17 = (f32[656,128]{1,0:T(8,128)S(1)}, f32[656,128]{1,0:T(8,128)S(1)}, u32[]{:S(2)}, u32[]{:S(2)}) collective-permute-start(f32[656,128]{1,0:T(8,128)S(1)} %get-tuple-element.170), channel_id=1, source_target_pairs={{0,2},{1,3},{2,0},{3,1},{4,6},{5,7},{6,4},{7,5},{8,10},{9,11},{10,... | collective-permute-start | bytes 1007624 | tf_op jit(solution)/shard_map/ppermute | solution.py:701
  73.8 1.7 %collective-permute-start.15 = (f32[640,128]{1,0:T(8,128)S(1)}, f32[640,128]{1,0:T(8,128)S(1)}, u32[]{:S(2)}, u32[]{:S(2)}) collective-permute-start(f32[640,128]{1,0:T(8,128)S(1)} %get-tuple-element.160.refs_4_), channel_id=1, source_target_pairs={{0,1},{1,0},{2,3},{3,2},{4,5},{5,4},{6,7},{7,6},{8,9},{9,8},{10,11... | collective-permute-start | bytes 983048 | tf_op jit(solution)/shard_map/ppermute | solution.py:701
  73.9 2.1 %collective-permute-start.16 = (f32[640,128]{1,0:T(8,128)S(1)}, f32[640,128]{1,0:T(8,128)S(1)}, u32[]{:S(2)}, u32[]{:S(2)}) collective-permute-start(f32[640,128]{1,0:T(8,128)S(1)} %get-tuple-element.161.refs_5_), channel_id=1, source_target_pairs={{0,1},{1,0},{2,3},{3,2},{4,5},{5,4},{6,7},{7,6},{8,9},{9,8},{10,11... | collective-permute-start | bytes 983048 | tf_op jit(solution)/shard_map/ppermute | solution.py:701
  74.4 5.2 %collective-permute-start.18 = (f32[640,128]{1,0:T(8,128)S(1)}, f32[640,128]{1,0:T(8,128)S(1)}, u32[]{:S(2)}, u32[]{:S(2)}) collective-permute-start(f32[640,128]{1,0:T(8,128)S(1)} %get-tuple-element.171.refs_4_), channel_id=1, source_target_pairs={{0,1},{1,0},{2,3},{3,2},{4,5},{5,4},{6,7},{7,6},{8,9},{9,8},{10,11... | collective-permute-start | bytes 983048 | tf_op jit(solution)/shard_map/ppermute | solution.py:701
  81.8 1.6 %collective-permute-start.19 = (f32[656,128]{1,0:T(8,128)S(1)}, f32[656,128]{1,0:T(8,128)S(1)}, u32[]{:S(2)}, u32[]{:S(2)}) collective-permute-start(f32[656,128]{1,0:T(8,128)S(1)} %collective-permute-done.17.refs_5_), channel_id=1, source_target_pairs={{0,1},{1,0},{2,3},{3,2},{4,5},{5,4},{6,7},{7,6},{8,9},{9,8},{10,11... | collective-permute-start | bytes 1007624 | tf_op jit(solution)/shard_map/ppermute | solution.py:701
  84.3 1.2 %collective-permute-start.20 = (f32[8,128]{1,0:T(8,128)S(1)}, f32[8,128]{1,0:T(8,128)S(1)}, u32[]{:S(2)}, u32[]{:S(2)}) collective-permute-start(f32[8,128]{1,0:T(8,128)S(1)} %get-tuple-element.180.total_ref), channel_id=1, source_target_pairs={{0,1},{1,0},{2,3},{3,2},{4,5},{5,4},{6,7},{7,6},{8,9},{9,8},{10,11... | collective-permute-start | bytes 12296 | tf_op jit(solution)/shard_map/ppermute | solution.py:701
  85.5 5.9 %collective-permute-start.23 = (f32[8,128]{1,0:T(8,128)S(1)}, f32[8,128]{1,0:T(8,128)S(1)}, u32[]{:S(2)}, u32[]{:S(2)}) collective-permute-start(f32[8,128]{1,0:T(8,128)S(1)} %get-tuple-element.181.refs_13_.total_ref), channel_id=1, source_target_pairs={{0,6},{1,7},{2,4},{3,5},{4,2},{5,3},{6,0},{7,1},{8,14},{9,15},{10,... | collective-permute-start | bytes 12296 | tf_op jit(solution)/shard_map/ppermute | solution.py:701
  86.9 4.6 %collective-permute-start.22 = (f32[8,128]{1,0:T(8,128)S(1)}, f32[8,128]{1,0:T(8,128)S(1)}, u32[]{:S(2)}, u32[]{:S(2)}) collective-permute-start(f32[8,128]{1,0:T(8,128)S(1)} %get-tuple-element.181.refs_13_.total_ref), channel_id=1, source_target_pairs={{0,4},{1,5},{2,6},{3,7},{4,0},{5,1},{6,2},{7,3},{8,12},{9,13},{10,... | collective-permute-start | bytes 12296 | tf_op jit(solution)/shard_map/ppermute | solution.py:701
  88.7 3.6 %collective-permute-start.21 = (f32[8,128]{1,0:T(8,128)S(1)}, f32[8,128]{1,0:T(8,128)S(1)}, u32[]{:S(2)}, u32[]{:S(2)}) collective-permute-start(f32[8,128]{1,0:T(8,128)S(1)} %get-tuple-element.181.refs_13_.total_ref), channel_id=1, source_target_pairs={{0,2},{1,3},{2,0},{3,1},{4,6},{5,7},{6,4},{7,5},{8,10},{9,11},{10,... | collective-permute-start | bytes 12296 | tf_op jit(solution)/shard_map/ppermute | solution.py:701
  92.4 6.4 %collective-permute-start.26 = (f32[8,128]{1,0:T(8,128)S(1)}, f32[8,128]{1,0:T(8,128)S(1)}, u32[]{:S(2)}, u32[]{:S(2)}) collective-permute-start(f32[8,128]{1,0:T(8,128)S(1)} %get-tuple-element.188.refs_13_), channel_id=1, source_target_pairs={{24,0},{25,1},{26,2},{27,3},{28,4},{29,5},{30,6},{31,7}} | collective-permute-start | bytes 12296 | tf_op jit(solution)/shard_map/ppermute | solution.py:701
  93.7 5.5 %collective-permute-start.25 = (f32[8,128]{1,0:T(8,128)S(1)}, f32[8,128]{1,0:T(8,128)S(1)}, u32[]{:S(2)}, u32[]{:S(2)}) collective-permute-start(f32[8,128]{1,0:T(8,128)S(1)} %get-tuple-element.188.refs_13_), channel_id=1, source_target_pairs={{16,0},{17,1},{18,2},{19,3},{20,4},{21,5},{22,6},{23,7},{24,8},{25... | collective-permute-start | bytes 12296 | tf_op jit(solution)/shard_map/ppermute | solution.py:701
  95.0 5.5 %collective-permute-start.24 = (f32[8,128]{1,0:T(8,128)S(1)}, f32[8,128]{1,0:T(8,128)S(1)}, u32[]{:S(2)}, u32[]{:S(2)}) collective-permute-start(f32[8,128]{1,0:T(8,128)S(1)} %get-tuple-element.188.refs_13_), channel_id=1, source_target_pairs={{8,0},{9,1},{10,2},{11,3},{12,4},{13,5},{14,6},{15,7},{16,8},{17,9... | collective-permute-start | bytes 12296 | tf_op jit(solution)/shard_map/ppermute | solution.py:701

commit v20 on v18

--- a/solution.py
+++ b/solution.py
@@ -527,8 +527,9 @@
             back = jnp.where(is_first, own, far).astype(BF16)
             state_ref[rows, wide] = state
             back_ref[rows, wide] = back
-            gain = state.astype(F32) * back_own[rows, wide]
-            gain = gain - back.astype(F32) * state_own[rows, wide]
+            whole_at = slice(half * lanes + wide.start, half * lanes + wide.stop)
+            gain = state.astype(F32) * back_own[rows, whole_at]
+            gain = gain - back.astype(F32) * state_own[rows, whole_at]
             sums[strip] = gain if sums[strip] is None else sums[strip] + gain
     row_sum = [
         jnp.broadcast_to(jnp.sum(value, axis=0, keepdims=True), (META, STRIP)) for value in sums
@@ -540,12 +541,11 @@
 def assemble(heads, chips, half, ordered, after, first, state_own, back_own, own, far):
     wide = state_own.shape[1]
     lanes = wide // HALVES
-    mine = pl.BlockSpec((STATE, lanes), lambda c: (0, half))
     return pl.pallas_call(
         lambda *refs: assemble_kernel(heads, chips, half, wide // heads, ordered, *refs),
-        grid=(1,),
-        in_specs=[whole(META, STRIP), whole(*first.shape), mine, mine]
-        + [whole(*value.shape) for value in (*own, *far)],
+        in_specs=[
+            whole(*value.shape) for value in (after, first, state_own, back_own, *own, *far)
+        ],
         out_specs=[whole(STATE, lanes), whole(STATE, lanes), whole(META, STRIP)],
         out_shape=[
             jax.ShapeDtypeStruct((STATE, lanes), BF16),
@@ -780,7 +780,7 @@
     own_b = held[1][0]
     far_b = to_core(own_b)
     state, back, counted = assemble(
-        heads, chips, 0, True, change, first[0], state_own, back_own, held[0], waiting[0]
+        heads, chips, 0, True, shared[0], first[0], state_own, back_own, held[0], waiting[0]
     )
     grad, *sums, counted = finish(
         heads, lanes * STEPS, 0, 1, counted, *maps, shared, dx, (db, dc, change), state, back, None

time: 94.9 us -> 94.9 us (level)
  no operation moved by 1% of the time
where the time goes in v20:
time: 94.9 us; the launch traced here: 94.6 us
  starting transfers between devices  32.9 us (35%)
  Pallas kernels  30.4 us (32%)
  waiting for transfers between devices  30.3 us (32%)
  between operations  0.96 us (1%)
    ppermute x27, starting transfers between devices, move(): return lax.ppermute(value, ('grp', 'seq'), pairs)  32.9 us
    ppermute x27, waiting for transfers between devices, move(): return lax.ppermute(value, ('grp', 'seq'), pairs)  30.3 us
    pallas_call x3, Pallas kernels, intra(): pl.pallas_call(lambda *refs: intra_kernel(heads, wide // heads, start, la...  12.5 us
    pallas_call x2, Pallas kernels, summary(): pl.pallas_call(lambda *refs: summary_kernel(heads, chips, half, *refs), g...  7.13 us
    pallas_call x3, Pallas kernels, finish(): pl.pallas_call(lambda *refs: finish_kernel(heads, wide // heads, start, s...  6.33 us
  transfers between devices with their start and end apart: 27, of which 18 were waited for; matrix products, arithmetic and copies ran while one was open for 0% of the time, Pallas kernels for 26%

profile of v20, /device:TPU:0, one launch (start us, length us, event | category | flops | bytes accessed | tf_op | source)
XLA Modules:
  0.0 94.6 jit_solution(3488759414116829756)
XLA Ops:
  0.6 3.9 %summary.2 = (f32[1288,128]{1,0:T(8,128)}, f32[1280,128]{1,0:T(8,128)}, f32[10,128]{1,0:T(8,128)}, f32[8,128]{1,0:T(8,128)}, f32[256,128]{1,0:T(8,128)}, /*index...) custom-call(bf16[256,2560]{1,0:T(8,128)(2,1)} %refs_0_.9, bf16[256,2560]{1,0:T(8,128)(2,1)} %refs_1_.15, ...), custom_call_target="tpu_custom_call" | custom-call | flops 1 | bytes 1 | tf_op jit(solution)/shard_map/summary/pallas_call | solution.py:196
  4.5 0.5 collective-permute-start
  5.0 3.3 %summary.3 = (f32[1288,128]{1,0:T(8,128)}, f32[1280,128]{1,0:T(8,128)}, f32[10,128]{1,0:T(8,128)}) custom-call(bf16[256,2560]{1,0:T(8,128)(2,1)} %refs_0_.9, bf16[256,2560]{1,0:T(8,128)(2,1)} %refs_1_.15, bf16[256,128]{1,0:T(8,128)(2,1)} %refs_2_.15, bf16[256,128]{1,0:T(8,128)(2,1)} %refs_3_.15, f32[8,128]{1,0:T(8,128)} %get-tuple-element.108.refs_3_.refs_4_.refs_0_, ...), custom_call_target="tpu_custom_call" | custom-call | flops 1 | bytes 1 | tf_op jit(solution)/shard_map/summary/pallas_call | solution.py:196
  8.4 0.1 combine.2
  8.5 3.1 %collective-permute-start.1 = (f32[656,128]{1,0:T(8,128)S(1)}, f32[656,128]{1,0:T(8,128)S(1)}, u32[]{:S(2)}, u32[]{:S(2)}) collective-permute-start(f32[656,128]{1,0:T(8,128)S(1)} %get-tuple-element.110.refs_0_.refs_1_), channel_id=1, source_target_pairs={{0,2},{1,3},{2,0},{3,1},{4,6},{5,7},{6,4},{7,5},{8,10},{9,11},{10,... | collective-permute-start | bytes 1007624 | tf_op jit(solution)/shard_map/ppermute | solution.py:701
  11.7 5.1 %intra.3 = (f32[256,2560]{1,0:T(8,128)S(1)}, f32[128,2560]{1,0:T(8,128)S(1)}, f32[128,2560]{1,0:T(8,128)S(1)}, f32[256,128]{1,0:T(8,128)S(1)}, f32[256,256]{1,0:T(8,128)S(1)}) custom-call(f32[656,128]{1,0:T(8,128)S(1)} %get-tuple-element.110.refs_0_.refs_1_, bf16[256,2560]{1,0:T(8,128)(2,1)S(1)} %copy-done, bf16[256,2560]{1,0:T(8,128)(2,1)S(1)} %copy-done.1, ...), custom_call_target="tpu_custom_call" | custom-call | flops 1 | bytes 1 | tf_op jit(solution)/shard_map/intra/pallas_call | solution.py:442
  16.7 2.9 %collective-permute-done.1.refs_2_ = f32[656,128]{1,0:T(8,128)S(1)} collective-permute-done((f32[656,128]{1,0:T(8,128)S(1)}, f32[656,128]{1,0:T(8,128)S(1)}, u32[]{:S(2)}, u32[]{:S(2)}) %collective-permute-start.1) | collective-permute-done | bytes 335904 | tf_op jit(solution)/shard_map/ppermute | solution.py:701
  19.7 0.1 combine.3
  19.8 1.8 %collective-permute-start.4 = (f32[656,128]{1,0:T(8,128)S(1)}, f32[656,128]{1,0:T(8,128)S(1)}, u32[]{:S(2)}, u32[]{:S(2)}) collective-permute-start(f32[656,128]{1,0:T(8,128)S(1)} %get-tuple-element.124.refs_1_), channel_id=1, source_target_pairs={{0,2},{1,3},{2,0},{3,1},{4,6},{5,7},{6,4},{7,5},{8,10},{9,11},{10,... | collective-permute-start | bytes 1007624 | tf_op jit(solution)/shard_map/ppermute | solution.py:701
  21.6 0.2 up.4
  21.8 2.7 %collective-permute-start.3 = (f32[336,128]{1,0:T(8,128)S(1)}, f32[336,128]{1,0:T(8,128)S(1)}, u32[]{:S(2)}, u32[]{:S(2)}) collective-permute-start(f32[336,128]{1,0:T(8,128)S(1)} %get-tuple-element.120.refs_0_.refs_1_), channel_id=1, source_target_pairs={{0,4},{1,5},{2,6},{3,7},{4,0},{5,1},{6,2},{7,3},{8,12},{9,13},{10,... | collective-permute-start | bytes 516104 | tf_op jit(solution)/shard_map/ppermute | solution.py:701
  24.4 5.0 %intra.4 = (f32[256,2560]{1,0:T(8,128)S(1)}, f32[128,2560]{1,0:T(8,128)S(1)}, f32[128,2560]{1,0:T(8,128)S(1)}, f32[256,128]{1,0:T(8,128)S(1)}, f32[256,256]{1,0:T(8,128)S(1)}) custom-call(f32[336,128]{1,0:T(8,128)S(1)} %get-tuple-element.120.refs_0_.refs_1_, ...), custom_call_target="tpu_custom_call", output_to_operand_aliasing={{0}: (9, {}), {1}: (10, {}), {2}: (11, {})} | custom-call | flops 1 | bytes 1 | tf_op jit(solution)/shard_map/intra/pallas_call | solution.py:442
  29.4 2.3 %collective-permute-done.3.refs_2_ = f32[336,128]{1,0:T(8,128)S(1)} collective-permute-done((f32[336,128]{1,0:T(8,128)S(1)}, f32[336,128]{1,0:T(8,128)S(1)}, u32[]{:S(2)}, u32[]{:S(2)}) %collective-permute-start.3) | collective-permute-done | bytes 172064 | tf_op jit(solution)/shard_map/ppermute | solution.py:701
  31.7 1.1 %collective-permute-done.4.refs_2_ = f32[656,128]{1,0:T(8,128)S(1)} collective-permute-done((f32[656,128]{1,0:T(8,128)S(1)}, f32[656,128]{1,0:T(8,128)S(1)}, u32[]{:S(2)}, u32[]{:S(2)}) %collective-permute-start.4) | collective-permute-done | bytes 335904 | tf_op jit(solution)/shard_map/ppermute | solution.py:701
  32.8 0.2 up.6
  33.0 2.4 %collective-permute-start.8 = (f32[336,128]{1,0:T(8,128)S(1)}, f32[336,128]{1,0:T(8,128)S(1)}, u32[]{:S(2)}, u32[]{:S(2)}) collective-permute-start(f32[336,128]{1,0:T(8,128)S(1)} %get-tuple-element.138.refs_1_), channel_id=1, source_target_pairs={{0,4},{1,5},{2,6},{3,7},{4,0},{5,1},{6,2},{7,3},{8,12},{9,13},{10,... | collective-permute-start | bytes 516104 | tf_op jit(solution)/shard_map/ppermute | solution.py:701
  35.4 0.2 up.5.refs_0_
  35.6 1.3 %collective-permute-start.7 = (f32[328,128]{1,0:T(8,128)S(1)}, f32[328,128]{1,0:T(8,128)S(1)}, u32[]{:S(2)}, u32[]{:S(2)}) collective-permute-start(f32[328,128]{1,0:T(8,128)S(1)} %up.5.refs_0_), channel_id=1, source_target_pairs={{1,25},{3,27},{5,29},{7,31},{24,0},{26,2},{28,4},{30,6}} | collective-permute-start | bytes 503816 | tf_op jit(solution)/shard_map/ppermute | solution.py:701
  36.9 1.3 %collective-permute-start.6 = (f32[328,128]{1,0:T(8,128)S(1)}, f32[328,128]{1,0:T(8,128)S(1)}, u32[]{:S(2)}, u32[]{:S(2)}) collective-permute-start(f32[328,128]{1,0:T(8,128)S(1)} %up.5.refs_0_), channel_id=1, source_target_pairs={{1,17},{3,19},{5,21},{7,23},{9,25},{11,27},{13,29},{15,31},{16,0},... | collective-permute-start | bytes 503816 | tf_op jit(solution)/shard_map/ppermute | solution.py:701
  38.2 1.3 %collective-permute-start.5 = (f32[328,128]{1,0:T(8,128)S(1)}, f32[328,128]{1,0:T(8,128)S(1)}, u32[]{:S(2)}, u32[]{:S(2)}) collective-permute-start(f32[328,128]{1,0:T(8,128)S(1)} %up.5.refs_0_), channel_id=1, source_target_pairs={{1,9},{3,11},{5,13},{7,15},{8,0},{9,17},{10,2},{11,19},{12,4},{13,... | collective-permute-start | bytes 503816 | tf_op jit(solution)/shard_map/ppermute | solution.py:701
  39.5 2.5 %intra.5 = (f32[256,2560]{1,0:T(8,128)S(1)}, f32[128,2560]{1,0:T(8,128)S(1)}, f32[128,2560]{1,0:T(8,128)S(1)}, f32[256,128]{1,0:T(8,128)S(1)}, f32[256,128]{1,0:T(8,128)S(1)}, /*index=5*/f32[256,128]{1,0:T(8,128)S(1)}) custom-call(f32[328,128]{1,0:T(8,128)S(1)} %up.5.refs_0_, ...), custom_call_target="tpu_custom_call", output_to_operand_aliasing={{0}: (9, {}), {1}: (10, {}), {2}: (11, {})} | custom-call | flops 1 | bytes 1 | tf_op jit(solution)/shard_map/intra/pallas_call | solution.py:442
  42.0 1.9 %collective-permute-done.7.refs_5_ = f32[328,128]{1,0:T(8,128)S(1)} collective-permute-done((f32[328,128]{1,0:T(8,128)S(1)}, f32[328,128]{1,0:T(8,128)S(1)}, u32[]{:S(2)}, u32[]{:S(2)}) %collective-permute-start.7) | collective-permute-done | bytes 167968 | tf_op jit(solution)/shard_map/ppermute | solution.py:701
  43.9 1.7 %collective-permute-done.6.refs_4_ = f32[328,128]{1,0:T(8,128)S(1)} collective-permute-done((f32[328,128]{1,0:T(8,128)S(1)}, f32[328,128]{1,0:T(8,128)S(1)}, u32[]{:S(2)}, u32[]{:S(2)}) %collective-permute-start.6) | collective-permute-done | bytes 167968 | tf_op jit(solution)/shard_map/ppermute | solution.py:701
  45.6 0.2 down.4
  45.9 0.8 collective-permute-start.9
  46.7 0.2 up.7
  46.9 1.3 %collective-permute-start.13 = (f32[328,128]{1,0:T(8,128)S(1)}, f32[328,128]{1,0:T(8,128)S(1)}, u32[]{:S(2)}, u32[]{:S(2)}) collective-permute-start(f32[328,128]{1,0:T(8,128)S(1)} %up.7), channel_id=1, source_target_pairs={{1,25},{3,27},{5,29},{7,31},{24,0},{26,2},{28,4},{30,6}} | collective-permute-start | bytes 503816 | tf_op jit(solution)/shard_map/ppermute | solution.py:701
  48.2 1.3 %collective-permute-start.12 = (f32[328,128]{1,0:T(8,128)S(1)}, f32[328,128]{1,0:T(8,128)S(1)}, u32[]{:S(2)}, u32[]{:S(2)}) collective-permute-start(f32[328,128]{1,0:T(8,128)S(1)} %up.7), channel_id=1, source_target_pairs={{1,17},{3,19},{5,21},{7,23},{9,25},{11,27},{13,29},{15,31},{16,0},... | collective-permute-start | bytes 503816 | tf_op jit(solution)/shard_map/ppermute | solution.py:701
  49.5 1.5 %collective-permute-start.11 = (f32[328,128]{1,0:T(8,128)S(1)}, f32[328,128]{1,0:T(8,128)S(1)}, u32[]{:S(2)}, u32[]{:S(2)}) collective-permute-start(f32[328,128]{1,0:T(8,128)S(1)} %up.7), channel_id=1, source_target_pairs={{1,9},{3,11},{5,13},{7,15},{8,0},{9,17},{10,2},{11,19},{12,4},{13,... | collective-permute-start | bytes 503816 | tf_op jit(solution)/shard_map/ppermute | solution.py:701
  51.0 3.7 %collective-permute-done.9.refs_4_ = f32[336,128]{1,0:T(8,128)S(1)} collective-permute-done((f32[336,128]{1,0:T(8,128)S(1)}, f32[336,128]{1,0:T(8,128)S(1)}, u32[]{:S(2)}, u32[]{:S(2)}) %collective-permute-start.9) | collective-permute-done | bytes 172064 | tf_op jit(solution)/shard_map/ppermute | solution.py:701
  54.6 0.2 down.5
  54.9 0.1 collective-permute-start.10
  55.0 0.2 collective-permute-done.13.refs_5_
  55.1 1.7 %collective-permute-done.12.refs_4_ = f32[328,128]{1,0:T(8,128)S(1)} collective-permute-done((f32[328,128]{1,0:T(8,128)S(1)}, f32[328,128]{1,0:T(8,128)S(1)}, u32[]{:S(2)}, u32[]{:S(2)}) %collective-permute-start.12) | collective-permute-done | bytes 167968 | tf_op jit(solution)/shard_map/ppermute | solution.py:701
  56.8 0.3 down.6
  57.1 2.3 %collective-permute-start.14 = (f32[336,128]{1,0:T(8,128)S(1)}, f32[336,128]{1,0:T(8,128)S(1)}, u32[]{:S(2)}, u32[]{:S(2)}) collective-permute-start(f32[336,128]{1,0:T(8,128)S(1)} %get-tuple-element.166), channel_id=1, source_target_pairs={{0,4},{1,5},{2,6},{3,7},{4,0},{5,1},{6,2},{7,3},{8,12},{9,13},{10,... | collective-permute-start | bytes 516104 | tf_op jit(solution)/shard_map/ppermute | solution.py:701
  59.3 5.8 %collective-permute-done.14.refs_4_ = f32[336,128]{1,0:T(8,128)S(1)} collective-permute-done((f32[336,128]{1,0:T(8,128)S(1)}, f32[336,128]{1,0:T(8,128)S(1)}, u32[]{:S(2)}, u32[]{:S(2)}) %collective-permute-start.14) | collective-permute-done | bytes 172064 | tf_op jit(solution)/shard_map/ppermute | solution.py:701
  65.2 0.4 collective-permute-done.10.got_ref
  65.5 0.2 down.7
  65.8 2.0 %collective-permute-start.17 = (f32[656,128]{1,0:T(8,128)S(1)}, f32[656,128]{1,0:T(8,128)S(1)}, u32[]{:S(2)}, u32[]{:S(2)}) collective-permute-start(f32[656,128]{1,0:T(8,128)S(1)} %get-tuple-element.178), channel_id=1, source_target_pairs={{0,2},{1,3},{2,0},{3,1},{4,6},{5,7},{6,4},{7,5},{8,10},{9,11},{10,... | collective-permute-start | bytes 1007624 | tf_op jit(solution)/shard_map/ppermute | solution.py:701
  67.8 0.1 order.1
  68.0 0.5 collective-permute-start.16
  68.5 0.1 collective-permute-start.18
  68.6 1.0 %collective-permute-done.15.refs_6_ = f32[640,128]{1,0:T(8,128)S(1)} collective-permute-done((f32[640,128]{1,0:T(8,128)S(1)}, f32[640,128]{1,0:T(8,128)S(1)}, u32[]{:S(2)}, u32[]{:S(2)}) %collective-permute-start.15) | collective-permute-done | bytes 327712 | tf_op jit(solution)/shard_map/ppermute | solution.py:701
  69.6 0.5 collective-permute-done.16.refs_7_
  70.1 0.7 assemble.2
  70.8 2.8 %finish.3 = (bf16[256,2560]{1,0:T(8,128)(2,1)}, f32[256,128]{1,0:T(8,128)S(1)}, f32[256,128]{1,0:T(8,128)S(1)}, f32[256,128]{1,0:T(8,128)S(1)}, f32[8,128]{1,0:T(8,128)S(1)}) custom-call(bf16[256,2560]{1,0:T(8,128)(2,1)S(1)} %copy-done, bf16[256,2560]{1,0:T(8,128)(2,1)S(1)} %copy-done.1, bf16[256,128]{1,0:T(8,128)(2,1)S(1)} %copy-done.2, ...), custom_call_target="tpu_custom_call" | custom-call | flops 1 | bytes 1 | tf_op jit(solution)/shard_map/finish/pallas_call | solution.py:611
  73.7 0.1 collective-permute-start.19
  73.8 1.5 %collective-permute-done.19.refs_7_ = f32[656,128]{1,0:T(8,128)S(1)} collective-permute-done((f32[656,128]{1,0:T(8,128)S(1)}, f32[656,128]{1,0:T(8,128)S(1)}, u32[]{:S(2)}, u32[]{:S(2)}) %collective-permute-start.19) | collective-permute-done | bytes 335904 | tf_op jit(solution)/shard_map/ppermute | solution.py:701
  75.3 0.8 assemble.3
  76.2 0.2 collective-permute-start.20
  76.3 1.0 %collective-permute-done.20.got_ref = f32[8,128]{1,0:T(8,128)S(1)} collective-permute-done((f32[8,128]{1,0:T(8,128)S(1)}, f32[8,128]{1,0:T(8,128)S(1)}, u32[]{:S(2)}, u32[]{:S(2)}) %collective-permute-start.20) | collective-permute-done | bytes 4128 | tf_op jit(solution)/shard_map/ppermute | solution.py:701
  77.4 3.8 %collective-permute-start.23 = (f32[8,128]{1,0:T(8,128)S(1)}, f32[8,128]{1,0:T(8,128)S(1)}, u32[]{:S(2)}, u32[]{:S(2)}) collective-permute-start(f32[8,128]{1,0:T(8,128)S(1)} %get-tuple-element.189.refs_13_.total_ref), channel_id=1, source_target_pairs={{0,6},{1,7},{2,4},{3,5},{4,2},{5,3},{6,0},{7,1},{8,14},{9,15},{10,... | collective-permute-start | bytes 12296 | tf_op jit(solution)/shard_map/ppermute | solution.py:701
  81.2 0.6 collective-permute-start.21
  81.8 1.5 %finish.4 = (bf16[256,2560]{1,0:T(8,128)(2,1)}, f32[256,128]{1,0:T(8,128)S(1)}, f32[256,128]{1,0:T(8,128)S(1)}, f32[256,128]{1,0:T(8,128)S(1)}, f32[8,128]{1,0:T(8,128)S(1)}) custom-call(bf16[256,2560]{1,0:T(8,128)(2,1)S(1)} %copy-done, bf16[256,2560]{1,0:T(8,128)(2,1)S(1)} %copy-done.1, ...), custom_call_target="tpu_custom_call", output_to_operand_aliasing={{0}: (12, {})} | custom-call | flops 1 | bytes 1 | tf_op jit(solution)/shard_map/finish/pallas_call | solution.py:611
  83.4 2.4 %collective-permute-done.22.refs_1_ = f32[8,128]{1,0:T(8,128)S(1)} collective-permute-done((f32[8,128]{1,0:T(8,128)S(1)}, f32[8,128]{1,0:T(8,128)S(1)}, u32[]{:S(2)}, u32[]{:S(2)}) %collective-permute-start.22) | collective-permute-done | bytes 4128 | tf_op jit(solution)/shard_map/ppermute | solution.py:701
  85.7 1.3 %collective-permute-start.26 = (f32[8,128]{1,0:T(8,128)S(1)}, f32[8,128]{1,0:T(8,128)S(1)}, u32[]{:S(2)}, u32[]{:S(2)}) collective-permute-start(f32[8,128]{1,0:T(8,128)S(1)} %get-tuple-element.196.refs_13_), channel_id=1, source_target_pairs={{24,0},{25,1},{26,2},{27,3},{28,4},{29,5},{30,6},{31,7}} | collective-permute-start | bytes 12296 | tf_op jit(solution)/shard_map/ppermute | solution.py:701
  87.0 1.3 %collective-permute-start.25 = (f32[8,128]{1,0:T(8,128)S(1)}, f32[8,128]{1,0:T(8,128)S(1)}, u32[]{:S(2)}, u32[]{:S(2)}) collective-permute-start(f32[8,128]{1,0:T(8,128)S(1)} %get-tuple-element.196.refs_13_), channel_id=1, source_target_pairs={{16,0},{17,1},{18,2},{19,3},{20,4},{21,5},{22,6},{23,7},{24,8},{25... | collective-permute-start | bytes 12296 | tf_op jit(solution)/shard_map/ppermute | solution.py:701
  88.3 1.3 %collective-permute-start.24 = (f32[8,128]{1,0:T(8,128)S(1)}, f32[8,128]{1,0:T(8,128)S(1)}, u32[]{:S(2)}, u32[]{:S(2)}) collective-permute-start(f32[8,128]{1,0:T(8,128)S(1)} %get-tuple-element.196.refs_13_), channel_id=1, source_target_pairs={{8,0},{9,1},{10,2},{11,3},{12,4},{13,5},{14,6},{15,7},{16,8},{17,9... | collective-permute-start | bytes 12296 | tf_op jit(solution)/shard_map/ppermute | solution.py:701
  89.6 2.0 %finish.5 = (bf16[256,2560]{1,0:T(8,128)(2,1)}, bf16[256,128]{1,0:T(8,128)(2,1)}, bf16[256,128]{1,0:T(8,128)(2,1)}, f32[40,256]{1,0:T(8,128)S(1)}, f32[8,128]{1,0:T(8,128)}) custom-call(bf16[256,2560]{1,0:T(8,128)(2,1)S(1)} %copy-done, bf16[256,2560]{1,0:T(8,128)(2,1)S(1)} %copy-done.1, ...), custom_call_target="tpu_custom_call", output_to_operand_aliasing={{0}: (12, {})} | custom-call | flops 1 | bytes 1 | tf_op jit(solution)/shard_map/finish/pallas_call | solution.py:611
  91.6 0.5 collective-permute-done.26.refs_3_
  92.1 0.4 collective-permute-done.25.refs_2_
  92.5 1.3 %collective-permute-done.24.refs_1_ = f32[8,128]{1,0:T(8,128)S(1)} collective-permute-done((f32[8,128]{1,0:T(8,128)S(1)}, f32[8,128]{1,0:T(8,128)S(1)}, u32[]{:S(2)}, u32[]{:S(2)}) %collective-permute-start.24) | collective-permute-done | bytes 4128 | tf_op jit(solution)/shard_map/ppermute | solution.py:701
  93.8 0.8 add_later.1
  (40 shorter events, 0.3 us)
Async XLA Ops:
  4.5 3.9 %collective-permute-start = (f32[1288,128]{1,0:T(8,128)}, f32[1288,128]{1,0:T(8,128)S(1)}, u32[]{:S(2)}, u32[]{:S(2)}) collective-permute-start(f32[1288,128]{1,0:T(8,128)} %get-tuple-element.105), channel_id=1, source_target_pairs={{0,1},{1,0},{2,3},{3,2},{4,5},{5,4},{6,7},{7,6},{8,9},{9,8},{10,11... | collective-permute-start | bytes 1978376 | tf_op jit(solution)/shard_map/ppermute | solution.py:701
  4.9 3.4 %copy-start.8 = (f32[1280,128]{1,0:T(8,128)S(1)}, f32[1280,128]{1,0:T(8,128)}, u32[]{:S(2)}) copy-start(f32[1280,128]{1,0:T(8,128)} %get-tuple-element.106.refs_1_) | copy-start | bytes 1966084
  5.0 3.4 %copy-start.10 = (f32[8,128]{1,0:T(8,128)S(1)}, f32[8,128]{1,0:T(8,128)}, u32[]{:S(2)}) copy-start(f32[8,128]{1,0:T(8,128)} %get-tuple-element.108.refs_3_.refs_4_.refs_0_) | copy-start | bytes 12292
  5.0 3.4 %copy-start.12 = (f32[10,128]{1,0:T(8,128)S(1)}, f32[10,128]{1,0:T(8,128)}, u32[]{:S(2)}) copy-start(f32[10,128]{1,0:T(8,128)} %get-tuple-element.107.refs_2_) | copy-start | bytes 15364
  5.0 6.6 %copy-start.1 = (bf16[256,2560]{1,0:T(8,128)(2,1)S(1)}, bf16[256,2560]{1,0:T(8,128)(2,1)}, u32[]{:S(2)}) copy-start(bf16[256,2560]{1,0:T(8,128)(2,1)} %refs_1_.15) | copy-start | bytes 3932164
  5.0 6.6 %copy-start.2 = (bf16[256,128]{1,0:T(8,128)(2,1)S(1)}, bf16[256,128]{1,0:T(8,128)(2,1)}, u32[]{:S(2)}) copy-start(bf16[256,128]{1,0:T(8,128)(2,1)} %refs_2_.15) | copy-start | bytes 196612
  5.0 6.6 %copy-start.3 = (bf16[256,128]{1,0:T(8,128)(2,1)S(1)}, bf16[256,128]{1,0:T(8,128)(2,1)}, u32[]{:S(2)}) copy-start(bf16[256,128]{1,0:T(8,128)(2,1)} %refs_3_.15) | copy-start | bytes 196612
  5.0 6.6 %copy-start.4 = (bf16[256,128]{1,0:T(8,128)(2,1)S(1)}, bf16[256,128]{1,0:T(8,128)(2,1)}, u32[]{:S(2)}) copy-start(bf16[256,128]{1,0:T(8,128)(2,1)} %get-tuple-element.103.refs_5_.refs_7_.refs_4_) | copy-start | bytes 196612
  5.0 6.6 %copy-start.5 = (bf16[256,128]{1,0:T(8,128)(2,1)S(1)}, bf16[256,128]{1,0:T(8,128)(2,1)}, u32[]{:S(2)}) copy-start(bf16[256,128]{1,0:T(8,128)(2,1)} %get-tuple-element.104.refs_6_.refs_8_.refs_5_) | copy-start | bytes 196612
  5.0 6.6 %copy-start.6 = (f32[256,128]{1,0:T(8,128)S(1)}, f32[256,128]{1,0:T(8,128)}, u32[]{:S(2)}) copy-start(f32[256,128]{1,0:T(8,128)} %get-tuple-element.112.refs_6_) | copy-start | bytes 393220
  5.0 6.6 %copy-start.9 = (f32[40,256]{1,0:T(8,128)S(1)}, f32[40,256]{1,0:T(8,128)}, u32[]{:S(2)}) copy-start(f32[40,256]{1,0:T(8,128)} %refs_5_.5) | copy-start | bytes 122884
  8.3 3.3 %copy-start = (bf16[256,2560]{1,0:T(8,128)(2,1)S(1)}, bf16[256,2560]{1,0:T(8,128)(2,1)}, u32[]{:S(2)}) copy-start(bf16[256,2560]{1,0:T(8,128)(2,1)} %refs_0_.9) | copy-start | bytes 3932164
  8.3 8.4 %collective-permute-start.2 = (f32[1288,128]{1,0:T(8,128)}, f32[1288,128]{1,0:T(8,128)S(1)}, u32[]{:S(2)}, u32[]{:S(2)}) collective-permute-start(f32[1288,128]{1,0:T(8,128)} %get-tuple-element.111), channel_id=1, source_target_pairs={{0,1},{1,0},{2,3},{3,2},{4,5},{5,4},{6,7},{7,6},{8,9},{9,8},{10,11... | collective-permute-start | bytes 1978376 | tf_op jit(solution)/shard_map/ppermute | solution.py:701
  8.5 11.2 %collective-permute-start.1 = (f32[656,128]{1,0:T(8,128)S(1)}, f32[656,128]{1,0:T(8,128)S(1)}, u32[]{:S(2)}, u32[]{:S(2)}) collective-permute-start(f32[656,128]{1,0:T(8,128)S(1)} %get-tuple-element.110.refs_0_.refs_1_), channel_id=1, source_target_pairs={{0,2},{1,3},{2,0},{3,1},{4,6},{5,7},{6,4},{7,5},{8,10},{9,11},{10,... | collective-permute-start | bytes 1007624 | tf_op jit(solution)/shard_map/ppermute | solution.py:701
  11.6 8.0 %copy-start.7 = (f32[1280,128]{1,0:T(8,128)S(1)}, f32[1280,128]{1,0:T(8,128)}, u32[]{:S(2)}) copy-start(f32[1280,128]{1,0:T(8,128)} %get-tuple-element.122.refs_1_) | copy-start | bytes 1966084
  11.6 8.0 %copy-start.11 = (f32[10,128]{1,0:T(8,128)S(1)}, f32[10,128]{1,0:T(8,128)}, u32[]{:S(2)}) copy-start(f32[10,128]{1,0:T(8,128)} %get-tuple-element.123.refs_2_) | copy-start | bytes 15364
  19.8 13.0 %collective-permute-start.4 = (f32[656,128]{1,0:T(8,128)S(1)}, f32[656,128]{1,0:T(8,128)S(1)}, u32[]{:S(2)}, u32[]{:S(2)}) collective-permute-start(f32[656,128]{1,0:T(8,128)S(1)} %get-tuple-element.124.refs_1_), channel_id=1, source_target_pairs={{0,2},{1,3},{2,0},{3,1},{4,6},{5,7},{6,4},{7,5},{8,10},{9,11},{10,... | collective-permute-start | bytes 1007624 | tf_op jit(solution)/shard_map/ppermute | solution.py:701
  21.8 10.0 %collective-permute-start.3 = (f32[336,128]{1,0:T(8,128)S(1)}, f32[336,128]{1,0:T(8,128)S(1)}, u32[]{:S(2)}, u32[]{:S(2)}) collective-permute-start(f32[336,128]{1,0:T(8,128)S(1)} %get-tuple-element.120.refs_0_.refs_1_), channel_id=1, source_target_pairs={{0,4},{1,5},{2,6},{3,7},{4,0},{5,1},{6,2},{7,3},{8,12},{9,13},{10,... | collective-permute-start | bytes 516104 | tf_op jit(solution)/shard_map/ppermute | solution.py:701
  33.0 12.6 %collective-permute-start.8 = (f32[336,128]{1,0:T(8,128)S(1)}, f32[336,128]{1,0:T(8,128)S(1)}, u32[]{:S(2)}, u32[]{:S(2)}) collective-permute-start(f32[336,128]{1,0:T(8,128)S(1)} %get-tuple-element.138.refs_1_), channel_id=1, source_target_pairs={{0,4},{1,5},{2,6},{3,7},{4,0},{5,1},{6,2},{7,3},{8,12},{9,13},{10,... | collective-permute-start | bytes 516104 | tf_op jit(solution)/shard_map/ppermute | solution.py:701
  35.6 8.3 %collective-permute-start.7 = (f32[328,128]{1,0:T(8,128)S(1)}, f32[328,128]{1,0:T(8,128)S(1)}, u32[]{:S(2)}, u32[]{:S(2)}) collective-permute-start(f32[328,128]{1,0:T(8,128)S(1)} %up.5.refs_0_), channel_id=1, source_target_pairs={{1,25},{3,27},{5,29},{7,31},{24,0},{26,2},{28,4},{30,6}} | collective-permute-start | bytes 503816 | tf_op jit(solution)/shard_map/ppermute | solution.py:701
  36.9 8.7 %collective-permute-start.6 = (f32[328,128]{1,0:T(8,128)S(1)}, f32[328,128]{1,0:T(8,128)S(1)}, u32[]{:S(2)}, u32[]{:S(2)}) collective-permute-start(f32[328,128]{1,0:T(8,128)S(1)} %up.5.refs_0_), channel_id=1, source_target_pairs={{1,17},{3,19},{5,21},{7,23},{9,25},{11,27},{13,29},{15,31},{16,0},... | collective-permute-start | bytes 503816 | tf_op jit(solution)/shard_map/ppermute | solution.py:701
  38.2 7.4 %collective-permute-start.5 = (f32[328,128]{1,0:T(8,128)S(1)}, f32[328,128]{1,0:T(8,128)S(1)}, u32[]{:S(2)}, u32[]{:S(2)}) collective-permute-start(f32[328,128]{1,0:T(8,128)S(1)} %up.5.refs_0_), channel_id=1, source_target_pairs={{1,9},{3,11},{5,13},{7,15},{8,0},{9,17},{10,2},{11,19},{12,4},{13,... | collective-permute-start | bytes 503816 | tf_op jit(solution)/shard_map/ppermute | solution.py:701
  45.9 8.7 %collective-permute-start.9 = (f32[336,128]{1,0:T(8,128)S(1)}, f32[336,128]{1,0:T(8,128)S(1)}, u32[]{:S(2)}, u32[]{:S(2)}) collective-permute-start(f32[336,128]{1,0:T(8,128)S(1)} %get-tuple-element.161), channel_id=1, source_target_pairs={{0,4},{1,5},{2,6},{3,7},{4,0},{5,1},{6,2},{7,3},{8,12},{9,13},{10,... | collective-permute-start | bytes 516104 | tf_op jit(solution)/shard_map/ppermute | solution.py:701
  46.9 8.3 %collective-permute-start.13 = (f32[328,128]{1,0:T(8,128)S(1)}, f32[328,128]{1,0:T(8,128)S(1)}, u32[]{:S(2)}, u32[]{:S(2)}) collective-permute-start(f32[328,128]{1,0:T(8,128)S(1)} %up.7), channel_id=1, source_target_pairs={{1,25},{3,27},{5,29},{7,31},{24,0},{26,2},{28,4},{30,6}} | collective-permute-start | bytes 503816 | tf_op jit(solution)/shard_map/ppermute | solution.py:701
  48.2 8.7 %collective-permute-start.12 = (f32[328,128]{1,0:T(8,128)S(1)}, f32[328,128]{1,0:T(8,128)S(1)}, u32[]{:S(2)}, u32[]{:S(2)}) collective-permute-start(f32[328,128]{1,0:T(8,128)S(1)} %up.7), channel_id=1, source_target_pairs={{1,17},{3,19},{5,21},{7,23},{9,25},{11,27},{13,29},{15,31},{16,0},... | collective-permute-start | bytes 503816 | tf_op jit(solution)/shard_map/ppermute | solution.py:701
  49.5 7.4 %collective-permute-start.11 = (f32[328,128]{1,0:T(8,128)S(1)}, f32[328,128]{1,0:T(8,128)S(1)}, u32[]{:S(2)}, u32[]{:S(2)}) collective-permute-start(f32[328,128]{1,0:T(8,128)S(1)} %up.7), channel_id=1, source_target_pairs={{1,9},{3,11},{5,13},{7,15},{8,0},{9,17},{10,2},{11,19},{12,4},{13,... | collective-permute-start | bytes 503816 | tf_op jit(solution)/shard_map/ppermute | solution.py:701
  54.9 10.7 %collective-permute-start.10 = (f32[656,128]{1,0:T(8,128)S(1)}, f32[656,128]{1,0:T(8,128)S(1)}, u32[]{:S(2)}, u32[]{:S(2)}) collective-permute-start(f32[656,128]{1,0:T(8,128)S(1)} %get-tuple-element.163), channel_id=1, source_target_pairs={{0,2},{1,3},{2,0},{3,1},{4,6},{5,7},{6,4},{7,5},{8,10},{9,11},{10,... | collective-permute-start | bytes 1007624 | tf_op jit(solution)/shard_map/ppermute | solution.py:701
  57.1 8.1 %collective-permute-start.14 = (f32[336,128]{1,0:T(8,128)S(1)}, f32[336,128]{1,0:T(8,128)S(1)}, u32[]{:S(2)}, u32[]{:S(2)}) collective-permute-start(f32[336,128]{1,0:T(8,128)S(1)} %get-tuple-element.166), channel_id=1, source_target_pairs={{0,4},{1,5},{2,6},{3,7},{4,0},{5,1},{6,2},{7,3},{8,12},{9,13},{10,... | collective-permute-start | bytes 516104 | tf_op jit(solution)/shard_map/ppermute | solution.py:701
  65.8 7.9 %collective-permute-start.17 = (f32[656,128]{1,0:T(8,128)S(1)}, f32[656,128]{1,0:T(8,128)S(1)}, u32[]{:S(2)}, u32[]{:S(2)}) collective-permute-start(f32[656,128]{1,0:T(8,128)S(1)} %get-tuple-element.178), channel_id=1, source_target_pairs={{0,2},{1,3},{2,0},{3,1},{4,6},{5,7},{6,4},{7,5},{8,10},{9,11},{10,... | collective-permute-start | bytes 1007624 | tf_op jit(solution)/shard_map/ppermute | solution.py:701
  67.9 1.7 %collective-permute-start.15 = (f32[640,128]{1,0:T(8,128)S(1)}, f32[640,128]{1,0:T(8,128)S(1)}, u32[]{:S(2)}, u32[]{:S(2)}) collective-permute-start(f32[640,128]{1,0:T(8,128)S(1)} %get-tuple-element.168.refs_4_), channel_id=1, source_target_pairs={{0,1},{1,0},{2,3},{3,2},{4,5},{5,4},{6,7},{7,6},{8,9},{9,8},{10,11... | collective-permute-start | bytes 983048 | tf_op jit(solution)/shard_map/ppermute | solution.py:701
  68.0 2.1 %collective-permute-start.16 = (f32[640,128]{1,0:T(8,128)S(1)}, f32[640,128]{1,0:T(8,128)S(1)}, u32[]{:S(2)}, u32[]{:S(2)}) collective-permute-start(f32[640,128]{1,0:T(8,128)S(1)} %get-tuple-element.169.refs_5_), channel_id=1, source_target_pairs={{0,1},{1,0},{2,3},{3,2},{4,5},{5,4},{6,7},{7,6},{8,9},{9,8},{10,11... | collective-permute-start | bytes 983048 | tf_op jit(solution)/shard_map/ppermute | solution.py:701
  68.5 5.2 %collective-permute-start.18 = (f32[640,128]{1,0:T(8,128)S(1)}, f32[640,128]{1,0:T(8,128)S(1)}, u32[]{:S(2)}, u32[]{:S(2)}) collective-permute-start(f32[640,128]{1,0:T(8,128)S(1)} %get-tuple-element.179.refs_4_), channel_id=1, source_target_pairs={{0,1},{1,0},{2,3},{3,2},{4,5},{5,4},{6,7},{7,6},{8,9},{9,8},{10,11... | collective-permute-start | bytes 983048 | tf_op jit(solution)/shard_map/ppermute | solution.py:701
  73.7 1.6 %collective-permute-start.19 = (f32[656,128]{1,0:T(8,128)S(1)}, f32[656,128]{1,0:T(8,128)S(1)}, u32[]{:S(2)}, u32[]{:S(2)}) collective-permute-start(f32[656,128]{1,0:T(8,128)S(1)} %collective-permute-done.17.refs_5_), channel_id=1, source_target_pairs={{0,1},{1,0},{2,3},{3,2},{4,5},{5,4},{6,7},{7,6},{8,9},{9,8},{10,11... | collective-permute-start | bytes 1007624 | tf_op jit(solution)/shard_map/ppermute | solution.py:701
  76.2 1.2 %collective-permute-start.20 = (f32[8,128]{1,0:T(8,128)S(1)}, f32[8,128]{1,0:T(8,128)S(1)}, u32[]{:S(2)}, u32[]{:S(2)}) collective-permute-start(f32[8,128]{1,0:T(8,128)S(1)} %get-tuple-element.188.total_ref), channel_id=1, source_target_pairs={{0,1},{1,0},{2,3},{3,2},{4,5},{5,4},{6,7},{7,6},{8,9},{9,8},{10,11... | collective-permute-start | bytes 12296 | tf_op jit(solution)/shard_map/ppermute | solution.py:701
  77.4 6.0 %collective-permute-start.23 = (f32[8,128]{1,0:T(8,128)S(1)}, f32[8,128]{1,0:T(8,128)S(1)}, u32[]{:S(2)}, u32[]{:S(2)}) collective-permute-start(f32[8,128]{1,0:T(8,128)S(1)} %get-tuple-element.189.refs_13_.total_ref), channel_id=1, source_target_pairs={{0,6},{1,7},{2,4},{3,5},{4,2},{5,3},{6,0},{7,1},{8,14},{9,15},{10,... | collective-permute-start | bytes 12296 | tf_op jit(solution)/shard_map/ppermute | solution.py:701
  81.2 4.5 %collective-permute-start.22 = (f32[8,128]{1,0:T(8,128)S(1)}, f32[8,128]{1,0:T(8,128)S(1)}, u32[]{:S(2)}, u32[]{:S(2)}) collective-permute-start(f32[8,128]{1,0:T(8,128)S(1)} %get-tuple-element.189.refs_13_.total_ref), channel_id=1, source_target_pairs={{0,4},{1,5},{2,6},{3,7},{4,0},{5,1},{6,2},{7,3},{8,12},{9,13},{10,... | collective-permute-start | bytes 12296 | tf_op jit(solution)/shard_map/ppermute | solution.py:701
  81.2 4.5 %collective-permute-start.21 = (f32[8,128]{1,0:T(8,128)S(1)}, f32[8,128]{1,0:T(8,128)S(1)}, u32[]{:S(2)}, u32[]{:S(2)}) collective-permute-start(f32[8,128]{1,0:T(8,128)S(1)} %get-tuple-element.189.refs_13_.total_ref), channel_id=1, source_target_pairs={{0,2},{1,3},{2,0},{3,1},{4,6},{5,7},{6,4},{7,5},{8,10},{9,11},{10,... | collective-permute-start | bytes 12296 | tf_op jit(solution)/shard_map/ppermute | solution.py:701
  85.7 6.4 %collective-permute-start.26 = (f32[8,128]{1,0:T(8,128)S(1)}, f32[8,128]{1,0:T(8,128)S(1)}, u32[]{:S(2)}, u32[]{:S(2)}) collective-permute-start(f32[8,128]{1,0:T(8,128)S(1)} %get-tuple-element.196.refs_13_), channel_id=1, source_target_pairs={{24,0},{25,1},{26,2},{27,3},{28,4},{29,5},{30,6},{31,7}} | collective-permute-start | bytes 12296 | tf_op jit(solution)/shard_map/ppermute | solution.py:701
  87.0 5.5 %collective-permute-start.25 = (f32[8,128]{1,0:T(8,128)S(1)}, f32[8,128]{1,0:T(8,128)S(1)}, u32[]{:S(2)}, u32[]{:S(2)}) collective-permute-start(f32[8,128]{1,0:T(8,128)S(1)} %get-tuple-element.196.refs_13_), channel_id=1, source_target_pairs={{16,0},{17,1},{18,2},{19,3},{20,4},{21,5},{22,6},{23,7},{24,8},{25... | collective-permute-start | bytes 12296 | tf_op jit(solution)/shard_map/ppermute | solution.py:701
  88.3 5.5 %collective-permute-start.24 = (f32[8,128]{1,0:T(8,128)S(1)}, f32[8,128]{1,0:T(8,128)S(1)}, u32[]{:S(2)}, u32[]{:S(2)}) collective-permute-start(f32[8,128]{1,0:T(8,128)S(1)} %get-tuple-element.196.refs_13_), channel_id=1, source_target_pairs={{8,0},{9,1},{10,2},{11,3},{12,4},{13,5},{14,6},{15,7},{16,8},{17,9... | collective-permute-start | bytes 12296 | tf_op jit(solution)/shard_map/ppermute | solution.py:701

commit v21 on v20

--- a/solution.py
+++ b/solution.py
@@ -121,7 +121,6 @@
     return shard & 1, shard >> 1
 
 
-STEPS = 2
 SUMMARY_STEPS = 1
 
 
@@ -776,14 +775,14 @@
         elif levels + 1 < step < rounds - 1:
             waiting[0], waiting[1] = lax.optimization_barrier((waiting[0], waiting[1]))
     dx, state_own, back_own, change, db, dc = block
-    lanes = inputs.shape[1] // HALVES // STEPS
+    lanes = inputs.shape[1] // HALVES
     own_b = held[1][0]
     far_b = to_core(own_b)
     state, back, counted = assemble(
         heads, chips, 0, True, shared[0], first[0], state_own, back_own, held[0], waiting[0]
     )
     grad, *sums, counted = finish(
-        heads, lanes * STEPS, 0, 1, counted, *maps, shared, dx, (db, dc, change), state, back, None
+        heads, lanes, 0, 1, counted, *maps, shared, dx, (db, dc, change), state, back, None
     )
     got, far_b, counted = lax.optimization_barrier((waiting[1], far_b, counted))
     own_b, far_b = (own_b, got), (far_b, to_core(got))
@@ -793,13 +792,10 @@
 
     later, counted = tiles(core_kernel, "core_sum", counted, to_core(counted))
     got = [to_chip(counted, step) for step in range(1, chips)]
-    grad, *sums, token = finish(
-        heads, lanes, STEPS, 1, counted, *maps, shared, dx, sums, state, back, grad
-    )
-    later, counted = tiles(count_kernel, "chip_sum", token, later, counted, *got)
+    later, counted = tiles(count_kernel, "chip_sum", counted, later, counted, *got)
     got = [to_earlier(counted, step) for step in range(1, groups)]
     grad, *sums, _ = finish(
-        heads, lanes, STEPS + 1, 1, counted, *maps, shared, dx, sums, state, back, grad
+        heads, lanes, 1, 1, counted, *maps, shared, dx, sums, state, back, grad
     )
     return (grad, sums[0], sums[1], add_later(sums[2], later, *got))
 

time: 94.9 us -> 94.9 us (level)
    pallas_call x3 -> x2, Pallas kernels: 6.33 us -> 5.79 us  [finish(): pl.pallas_call(lambda *refs: finish_kernel(heads, wide // heads, start, s...]
  transfers between devices with their start and end apart: 27 -> 27, of which waited for: 18 -> 17; matrix products, arithmetic and copies ran while one was open for 0% -> 0% of each run, Pallas kernels for 26% -> 25%
where the time goes in v21:
time: 94.9 us; the launch traced here: 94.6 us
  starting transfers between devices  32.9 us (35%)
  waiting for transfers between devices  30.8 us (32%)
  Pallas kernels  29.9 us (32%)
  between operations  0.96 us (1%)
    ppermute x27, starting transfers between devices, move(): return lax.ppermute(value, ('grp', 'seq'), pairs)  32.9 us
    ppermute x27, waiting for transfers between devices, move(): return lax.ppermute(value, ('grp', 'seq'), pairs)  30.8 us
    pallas_call x3, Pallas kernels, intra(): pl.pallas_call(lambda *refs: intra_kernel(heads, wide // heads, start, la...  12.5 us
    pallas_call x2, Pallas kernels, summary(): pl.pallas_call(lambda *refs: summary_kernel(heads, chips, half, *refs), g...  7.15 us
    pallas_call x2, Pallas kernels, finish(): pl.pallas_call(lambda *refs: finish_kernel(heads, wide // heads, start, s...  5.79 us
  transfers between devices with their start and end apart: 27, of which 17 were waited for; matrix products, arithmetic and copies ran while one was open for 0% of the time, Pallas kernels for 25%

profile of v21, /device:TPU:0, one launch (start us, length us, event | category | flops | bytes accessed | tf_op | source)
XLA Modules:
  0.0 94.6 jit_solution(10940758331423799953)
XLA Ops:
  0.6 3.9 %summary.2 = (f32[1288,128]{1,0:T(8,128)}, f32[1280,128]{1,0:T(8,128)}, f32[10,128]{1,0:T(8,128)}, f32[8,128]{1,0:T(8,128)}, f32[256,128]{1,0:T(8,128)}, /*index...) custom-call(bf16[256,2560]{1,0:T(8,128)(2,1)} %refs_0_.7, bf16[256,2560]{1,0:T(8,128)(2,1)} %refs_1_.13, ...), custom_call_target="tpu_custom_call" | custom-call | flops 1 | bytes 1 | tf_op jit(solution)/shard_map/summary/pallas_call | solution.py:195
  4.5 0.5 collective-permute-start
  5.0 3.3 %summary.3 = (f32[1288,128]{1,0:T(8,128)}, f32[1280,128]{1,0:T(8,128)}, f32[10,128]{1,0:T(8,128)}) custom-call(bf16[256,2560]{1,0:T(8,128)(2,1)} %refs_0_.7, bf16[256,2560]{1,0:T(8,128)(2,1)} %refs_1_.13, bf16[256,128]{1,0:T(8,128)(2,1)} %refs_2_.13, bf16[256,128]{1,0:T(8,128)(2,1)} %refs_3_.13, f32[8,128]{1,0:T(8,128)} %get-tuple-element.103.refs_3_.refs_4_.refs_0_, ...), custom_call_target="tpu_custom_call" | custom-call | flops 1 | bytes 1 | tf_op jit(solution)/shard_map/summary/pallas_call | solution.py:195
  8.3 0.1 collective-permute-start.2
  8.4 0.1 combine.2
  8.5 3.1 %collective-permute-start.1 = (f32[656,128]{1,0:T(8,128)S(1)}, f32[656,128]{1,0:T(8,128)S(1)}, u32[]{:S(2)}, u32[]{:S(2)}) collective-permute-start(f32[656,128]{1,0:T(8,128)S(1)} %get-tuple-element.105.refs_0_.refs_1_), channel_id=1, source_target_pairs={{0,2},{1,3},{2,0},{3,1},{4,6},{5,7},{6,4},{7,5},{8,10},{9,11},{10,... | collective-permute-start | bytes 1007624 | tf_op jit(solution)/shard_map/ppermute | solution.py:700
  11.7 5.0 %intra.3 = (f32[256,2560]{1,0:T(8,128)S(1)}, f32[128,2560]{1,0:T(8,128)S(1)}, f32[128,2560]{1,0:T(8,128)S(1)}, f32[256,128]{1,0:T(8,128)S(1)}, f32[256,256]{1,0:T(8,128)S(1)}) custom-call(f32[656,128]{1,0:T(8,128)S(1)} %get-tuple-element.105.refs_0_.refs_1_, bf16[256,2560]{1,0:T(8,128)(2,1)S(1)} %copy-done, bf16[256,2560]{1,0:T(8,128)(2,1)S(1)} %copy-done.1, ...), custom_call_target="tpu_custom_call" | custom-call | flops 1 | bytes 1 | tf_op jit(solution)/shard_map/intra/pallas_call | solution.py:441
  16.7 2.9 %collective-permute-done.1.refs_2_ = f32[656,128]{1,0:T(8,128)S(1)} collective-permute-done((f32[656,128]{1,0:T(8,128)S(1)}, f32[656,128]{1,0:T(8,128)S(1)}, u32[]{:S(2)}, u32[]{:S(2)}) %collective-permute-start.1) | collective-permute-done | bytes 335904 | tf_op jit(solution)/shard_map/ppermute | solution.py:700
  19.7 0.1 combine.3
  19.8 1.8 %collective-permute-start.4 = (f32[656,128]{1,0:T(8,128)S(1)}, f32[656,128]{1,0:T(8,128)S(1)}, u32[]{:S(2)}, u32[]{:S(2)}) collective-permute-start(f32[656,128]{1,0:T(8,128)S(1)} %get-tuple-element.119.refs_1_), channel_id=1, source_target_pairs={{0,2},{1,3},{2,0},{3,1},{4,6},{5,7},{6,4},{7,5},{8,10},{9,11},{10,... | collective-permute-start | bytes 1007624 | tf_op jit(solution)/shard_map/ppermute | solution.py:700
  21.6 0.2 up.4
  21.8 2.7 %collective-permute-start.3 = (f32[336,128]{1,0:T(8,128)S(1)}, f32[336,128]{1,0:T(8,128)S(1)}, u32[]{:S(2)}, u32[]{:S(2)}) collective-permute-start(f32[336,128]{1,0:T(8,128)S(1)} %get-tuple-element.115.refs_0_.refs_1_), channel_id=1, source_target_pairs={{0,4},{1,5},{2,6},{3,7},{4,0},{5,1},{6,2},{7,3},{8,12},{9,13},{10,... | collective-permute-start | bytes 516104 | tf_op jit(solution)/shard_map/ppermute | solution.py:700
  24.5 5.0 %intra.4 = (f32[256,2560]{1,0:T(8,128)S(1)}, f32[128,2560]{1,0:T(8,128)S(1)}, f32[128,2560]{1,0:T(8,128)S(1)}, f32[256,128]{1,0:T(8,128)S(1)}, f32[256,256]{1,0:T(8,128)S(1)}) custom-call(f32[336,128]{1,0:T(8,128)S(1)} %get-tuple-element.115.refs_0_.refs_1_, ...), custom_call_target="tpu_custom_call", output_to_operand_aliasing={{0}: (9, {}), {1}: (10, {}), {2}: (11, {})} | custom-call | flops 1 | bytes 1 | tf_op jit(solution)/shard_map/intra/pallas_call | solution.py:441
  29.4 2.3 %collective-permute-done.3.refs_2_ = f32[336,128]{1,0:T(8,128)S(1)} collective-permute-done((f32[336,128]{1,0:T(8,128)S(1)}, f32[336,128]{1,0:T(8,128)S(1)}, u32[]{:S(2)}, u32[]{:S(2)}) %collective-permute-start.3) | collective-permute-done | bytes 172064 | tf_op jit(solution)/shard_map/ppermute | solution.py:700
  31.8 1.1 %collective-permute-done.4.refs_2_ = f32[656,128]{1,0:T(8,128)S(1)} collective-permute-done((f32[656,128]{1,0:T(8,128)S(1)}, f32[656,128]{1,0:T(8,128)S(1)}, u32[]{:S(2)}, u32[]{:S(2)}) %collective-permute-start.4) | collective-permute-done | bytes 335904 | tf_op jit(solution)/shard_map/ppermute | solution.py:700
  32.8 0.2 up.6
  33.0 2.4 %collective-permute-start.8 = (f32[336,128]{1,0:T(8,128)S(1)}, f32[336,128]{1,0:T(8,128)S(1)}, u32[]{:S(2)}, u32[]{:S(2)}) collective-permute-start(f32[336,128]{1,0:T(8,128)S(1)} %get-tuple-element.133.refs_1_), channel_id=1, source_target_pairs={{0,4},{1,5},{2,6},{3,7},{4,0},{5,1},{6,2},{7,3},{8,12},{9,13},{10,... | collective-permute-start | bytes 516104 | tf_op jit(solution)/shard_map/ppermute | solution.py:700
  35.4 0.2 up.5.refs_0_
  35.6 1.3 %collective-permute-start.7 = (f32[328,128]{1,0:T(8,128)S(1)}, f32[328,128]{1,0:T(8,128)S(1)}, u32[]{:S(2)}, u32[]{:S(2)}) collective-permute-start(f32[328,128]{1,0:T(8,128)S(1)} %up.5.refs_0_), channel_id=1, source_target_pairs={{1,25},{3,27},{5,29},{7,31},{24,0},{26,2},{28,4},{30,6}} | collective-permute-start | bytes 503816 | tf_op jit(solution)/shard_map/ppermute | solution.py:700
  36.9 1.3 %collective-permute-start.6 = (f32[328,128]{1,0:T(8,128)S(1)}, f32[328,128]{1,0:T(8,128)S(1)}, u32[]{:S(2)}, u32[]{:S(2)}) collective-permute-start(f32[328,128]{1,0:T(8,128)S(1)} %up.5.refs_0_), channel_id=1, source_target_pairs={{1,17},{3,19},{5,21},{7,23},{9,25},{11,27},{13,29},{15,31},{16,0},... | collective-permute-start | bytes 503816 | tf_op jit(solution)/shard_map/ppermute | solution.py:700
  38.2 1.3 %collective-permute-start.5 = (f32[328,128]{1,0:T(8,128)S(1)}, f32[328,128]{1,0:T(8,128)S(1)}, u32[]{:S(2)}, u32[]{:S(2)}) collective-permute-start(f32[328,128]{1,0:T(8,128)S(1)} %up.5.refs_0_), channel_id=1, source_target_pairs={{1,9},{3,11},{5,13},{7,15},{8,0},{9,17},{10,2},{11,19},{12,4},{13,... | collective-permute-start | bytes 503816 | tf_op jit(solution)/shard_map/ppermute | solution.py:700
  39.5 2.5 %intra.5 = (f32[256,2560]{1,0:T(8,128)S(1)}, f32[128,2560]{1,0:T(8,128)S(1)}, f32[128,2560]{1,0:T(8,128)S(1)}, f32[256,128]{1,0:T(8,128)S(1)}, f32[256,128]{1,0:T(8,128)S(1)}, /*index=5*/f32[256,128]{1,0:T(8,128)S(1)}) custom-call(f32[328,128]{1,0:T(8,128)S(1)} %up.5.refs_0_, ...), custom_call_target="tpu_custom_call", output_to_operand_aliasing={{0}: (9, {}), {1}: (10, {}), {2}: (11, {})} | custom-call | flops 1 | bytes 1 | tf_op jit(solution)/shard_map/intra/pallas_call | solution.py:441
  42.0 1.9 %collective-permute-done.7.refs_5_ = f32[328,128]{1,0:T(8,128)S(1)} collective-permute-done((f32[328,128]{1,0:T(8,128)S(1)}, f32[328,128]{1,0:T(8,128)S(1)}, u32[]{:S(2)}, u32[]{:S(2)}) %collective-permute-start.7) | collective-permute-done | bytes 167968 | tf_op jit(solution)/shard_map/ppermute | solution.py:700
  43.9 1.7 %collective-permute-done.6.refs_4_ = f32[328,128]{1,0:T(8,128)S(1)} collective-permute-done((f32[328,128]{1,0:T(8,128)S(1)}, f32[328,128]{1,0:T(8,128)S(1)}, u32[]{:S(2)}, u32[]{:S(2)}) %collective-permute-start.6) | collective-permute-done | bytes 167968 | tf_op jit(solution)/shard_map/ppermute | solution.py:700
  45.6 0.2 down.4
  45.9 0.8 collective-permute-start.9
  46.7 0.2 up.7
  46.9 1.3 %collective-permute-start.13 = (f32[328,128]{1,0:T(8,128)S(1)}, f32[328,128]{1,0:T(8,128)S(1)}, u32[]{:S(2)}, u32[]{:S(2)}) collective-permute-start(f32[328,128]{1,0:T(8,128)S(1)} %up.7), channel_id=1, source_target_pairs={{1,25},{3,27},{5,29},{7,31},{24,0},{26,2},{28,4},{30,6}} | collective-permute-start | bytes 503816 | tf_op jit(solution)/shard_map/ppermute | solution.py:700
  48.2 1.3 %collective-permute-start.12 = (f32[328,128]{1,0:T(8,128)S(1)}, f32[328,128]{1,0:T(8,128)S(1)}, u32[]{:S(2)}, u32[]{:S(2)}) collective-permute-start(f32[328,128]{1,0:T(8,128)S(1)} %up.7), channel_id=1, source_target_pairs={{1,17},{3,19},{5,21},{7,23},{9,25},{11,27},{13,29},{15,31},{16,0},... | collective-permute-start | bytes 503816 | tf_op jit(solution)/shard_map/ppermute | solution.py:700
  49.5 1.5 %collective-permute-start.11 = (f32[328,128]{1,0:T(8,128)S(1)}, f32[328,128]{1,0:T(8,128)S(1)}, u32[]{:S(2)}, u32[]{:S(2)}) collective-permute-start(f32[328,128]{1,0:T(8,128)S(1)} %up.7), channel_id=1, source_target_pairs={{1,9},{3,11},{5,13},{7,15},{8,0},{9,17},{10,2},{11,19},{12,4},{13,... | collective-permute-start | bytes 503816 | tf_op jit(solution)/shard_map/ppermute | solution.py:700
  51.0 3.7 %collective-permute-done.9.refs_4_ = f32[336,128]{1,0:T(8,128)S(1)} collective-permute-done((f32[336,128]{1,0:T(8,128)S(1)}, f32[336,128]{1,0:T(8,128)S(1)}, u32[]{:S(2)}, u32[]{:S(2)}) %collective-permute-start.9) | collective-permute-done | bytes 172064 | tf_op jit(solution)/shard_map/ppermute | solution.py:700
  54.6 0.2 down.5
  54.9 0.1 collective-permute-start.10
  55.0 0.2 collective-permute-done.13.refs_5_
  55.2 1.7 %collective-permute-done.12.refs_4_ = f32[328,128]{1,0:T(8,128)S(1)} collective-permute-done((f32[328,128]{1,0:T(8,128)S(1)}, f32[328,128]{1,0:T(8,128)S(1)}, u32[]{:S(2)}, u32[]{:S(2)}) %collective-permute-start.12) | collective-permute-done | bytes 167968 | tf_op jit(solution)/shard_map/ppermute | solution.py:700
  56.8 0.3 down.6
  57.1 2.3 %collective-permute-start.14 = (f32[336,128]{1,0:T(8,128)S(1)}, f32[336,128]{1,0:T(8,128)S(1)}, u32[]{:S(2)}, u32[]{:S(2)}) collective-permute-start(f32[336,128]{1,0:T(8,128)S(1)} %get-tuple-element.161), channel_id=1, source_target_pairs={{0,4},{1,5},{2,6},{3,7},{4,0},{5,1},{6,2},{7,3},{8,12},{9,13},{10,... | collective-permute-start | bytes 516104 | tf_op jit(solution)/shard_map/ppermute | solution.py:700
  59.4 5.8 %collective-permute-done.14.refs_4_ = f32[336,128]{1,0:T(8,128)S(1)} collective-permute-done((f32[336,128]{1,0:T(8,128)S(1)}, f32[336,128]{1,0:T(8,128)S(1)}, u32[]{:S(2)}, u32[]{:S(2)}) %collective-permute-start.14) | collective-permute-done | bytes 172064 | tf_op jit(solution)/shard_map/ppermute | solution.py:700
  65.2 0.4 collective-permute-done.10.got_ref
  65.6 0.2 down.7
  65.8 2.1 %collective-permute-start.17 = (f32[656,128]{1,0:T(8,128)S(1)}, f32[656,128]{1,0:T(8,128)S(1)}, u32[]{:S(2)}, u32[]{:S(2)}) collective-permute-start(f32[656,128]{1,0:T(8,128)S(1)} %get-tuple-element.173), channel_id=1, source_target_pairs={{0,2},{1,3},{2,0},{3,1},{4,6},{5,7},{6,4},{7,5},{8,10},{9,11},{10,... | collective-permute-start | bytes 1007624 | tf_op jit(solution)/shard_map/ppermute | solution.py:700
  67.9 0.1 order.1
  67.9 0.1 collective-permute-start.15
  68.0 0.5 collective-permute-start.16
  68.5 0.1 collective-permute-start.18
  68.6 1.0 %collective-permute-done.15.refs_6_ = f32[640,128]{1,0:T(8,128)S(1)} collective-permute-done((f32[640,128]{1,0:T(8,128)S(1)}, f32[640,128]{1,0:T(8,128)S(1)}, u32[]{:S(2)}, u32[]{:S(2)}) %collective-permute-start.15) | collective-permute-done | bytes 327712 | tf_op jit(solution)/shard_map/ppermute | solution.py:700
  69.6 0.5 collective-permute-done.16.refs_7_
  70.1 0.7 assemble.2
  70.8 2.9 %finish.2 = (bf16[256,2560]{1,0:T(8,128)(2,1)}, f32[256,128]{1,0:T(8,128)S(1)}, f32[256,128]{1,0:T(8,128)S(1)}, f32[256,128]{1,0:T(8,128)S(1)}, f32[8,128]{1,0:T(8,128)S(1)}) custom-call(bf16[256,2560]{1,0:T(8,128)(2,1)S(1)} %copy-done, bf16[256,2560]{1,0:T(8,128)(2,1)S(1)} %copy-done.1, bf16[256,128]{1,0:T(8,128)(2,1)S(1)} %copy-done.2, ...), custom_call_target="tpu_custom_call" | custom-call | flops 1 | bytes 1 | tf_op jit(solution)/shard_map/finish/pallas_call | solution.py:610
  73.7 0.1 collective-permute-start.19
  73.8 1.5 %collective-permute-done.19.refs_7_ = f32[656,128]{1,0:T(8,128)S(1)} collective-permute-done((f32[656,128]{1,0:T(8,128)S(1)}, f32[656,128]{1,0:T(8,128)S(1)}, u32[]{:S(2)}, u32[]{:S(2)}) %collective-permute-start.19) | collective-permute-done | bytes 335904 | tf_op jit(solution)/shard_map/ppermute | solution.py:700
  75.3 0.8 assemble.3
  76.2 0.2 collective-permute-start.20
  76.4 1.0 %collective-permute-done.20.got_ref = f32[8,128]{1,0:T(8,128)S(1)} collective-permute-done((f32[8,128]{1,0:T(8,128)S(1)}, f32[8,128]{1,0:T(8,128)S(1)}, u32[]{:S(2)}, u32[]{:S(2)}) %collective-permute-start.20) | collective-permute-done | bytes 4128 | tf_op jit(solution)/shard_map/ppermute | solution.py:700
  77.4 3.8 %collective-permute-start.23 = (f32[8,128]{1,0:T(8,128)S(1)}, f32[8,128]{1,0:T(8,128)S(1)}, u32[]{:S(2)}, u32[]{:S(2)}) collective-permute-start(f32[8,128]{1,0:T(8,128)S(1)} %get-tuple-element.184.after_ref.total_ref), channel_id=1, source_target_pairs={{0,6},{1,7},{2,4},{3,5},{4,2},{5,3},{6,0},{7,1},{8,14},{9,15},{10,... | collective-permute-start | bytes 12296 | tf_op jit(solution)/shard_map/ppermute | solution.py:700
  81.2 0.6 collective-permute-start.21
  81.8 1.0 %collective-permute-done.23.refs_2_ = f32[8,128]{1,0:T(8,128)S(1)} collective-permute-done((f32[8,128]{1,0:T(8,128)S(1)}, f32[8,128]{1,0:T(8,128)S(1)}, u32[]{:S(2)}, u32[]{:S(2)}) %collective-permute-start.23) | collective-permute-done | bytes 4128 | tf_op jit(solution)/shard_map/ppermute | solution.py:700
  82.8 2.9 %collective-permute-done.22.refs_1_ = f32[8,128]{1,0:T(8,128)S(1)} collective-permute-done((f32[8,128]{1,0:T(8,128)S(1)}, f32[8,128]{1,0:T(8,128)S(1)}, u32[]{:S(2)}, u32[]{:S(2)}) %collective-permute-start.22) | collective-permute-done | bytes 4128 | tf_op jit(solution)/shard_map/ppermute | solution.py:700
  85.7 1.3 %collective-permute-start.26 = (f32[8,128]{1,0:T(8,128)S(1)}, f32[8,128]{1,0:T(8,128)S(1)}, u32[]{:S(2)}, u32[]{:S(2)}) collective-permute-start(f32[8,128]{1,0:T(8,128)S(1)} %get-tuple-element.186.refs_13_), channel_id=1, source_target_pairs={{24,0},{25,1},{26,2},{27,3},{28,4},{29,5},{30,6},{31,7}} | collective-permute-start | bytes 12296 | tf_op jit(solution)/shard_map/ppermute | solution.py:700
  87.0 1.3 %collective-permute-start.25 = (f32[8,128]{1,0:T(8,128)S(1)}, f32[8,128]{1,0:T(8,128)S(1)}, u32[]{:S(2)}, u32[]{:S(2)}) collective-permute-start(f32[8,128]{1,0:T(8,128)S(1)} %get-tuple-element.186.refs_13_), channel_id=1, source_target_pairs={{16,0},{17,1},{18,2},{19,3},{20,4},{21,5},{22,6},{23,7},{24,8},{25... | collective-permute-start | bytes 12296 | tf_op jit(solution)/shard_map/ppermute | solution.py:700
  88.3 1.3 %collective-permute-start.24 = (f32[8,128]{1,0:T(8,128)S(1)}, f32[8,128]{1,0:T(8,128)S(1)}, u32[]{:S(2)}, u32[]{:S(2)}) collective-permute-start(f32[8,128]{1,0:T(8,128)S(1)} %get-tuple-element.186.refs_13_), channel_id=1, source_target_pairs={{8,0},{9,1},{10,2},{11,3},{12,4},{13,5},{14,6},{15,7},{16,8},{17,9... | collective-permute-start | bytes 12296 | tf_op jit(solution)/shard_map/ppermute | solution.py:700
  89.6 2.9 %finish.3 = (bf16[256,2560]{1,0:T(8,128)(2,1)}, bf16[256,128]{1,0:T(8,128)(2,1)}, bf16[256,128]{1,0:T(8,128)(2,1)}, f32[40,256]{1,0:T(8,128)S(1)}, f32[8,128]{1,0:T(8,128)}) custom-call(bf16[256,2560]{1,0:T(8,128)(2,1)S(1)} %copy-done, bf16[256,2560]{1,0:T(8,128)(2,1)S(1)} %copy-done.1, ...), custom_call_target="tpu_custom_call", output_to_operand_aliasing={{0}: (12, {})} | custom-call | flops 1 | bytes 1 | tf_op jit(solution)/shard_map/finish/pallas_call | solution.py:610
  92.6 1.3 %collective-permute-done.24.refs_1_ = f32[8,128]{1,0:T(8,128)S(1)} collective-permute-done((f32[8,128]{1,0:T(8,128)S(1)}, f32[8,128]{1,0:T(8,128)S(1)}, u32[]{:S(2)}, u32[]{:S(2)}) %collective-permute-start.24) | collective-permute-done | bytes 4128 | tf_op jit(solution)/shard_map/ppermute | solution.py:700
  93.8 0.8 add_later.1
  (39 shorter events, 0.1 us)
Async XLA Ops:
  4.5 3.9 %collective-permute-start = (f32[1288,128]{1,0:T(8,128)}, f32[1288,128]{1,0:T(8,128)S(1)}, u32[]{:S(2)}, u32[]{:S(2)}) collective-permute-start(f32[1288,128]{1,0:T(8,128)} %get-tuple-element.100), channel_id=1, source_target_pairs={{0,1},{1,0},{2,3},{3,2},{4,5},{5,4},{6,7},{7,6},{8,9},{9,8},{10,11... | collective-permute-start | bytes 1978376 | tf_op jit(solution)/shard_map/ppermute | solution.py:700
  4.9 3.4 %copy-start.8 = (f32[1280,128]{1,0:T(8,128)S(1)}, f32[1280,128]{1,0:T(8,128)}, u32[]{:S(2)}) copy-start(f32[1280,128]{1,0:T(8,128)} %get-tuple-element.101.refs_1_) | copy-start | bytes 1966084
  5.0 3.4 %copy-start.10 = (f32[8,128]{1,0:T(8,128)S(1)}, f32[8,128]{1,0:T(8,128)}, u32[]{:S(2)}) copy-start(f32[8,128]{1,0:T(8,128)} %get-tuple-element.103.refs_3_.refs_4_.refs_0_) | copy-start | bytes 12292
  5.0 3.4 %copy-start.12 = (f32[10,128]{1,0:T(8,128)S(1)}, f32[10,128]{1,0:T(8,128)}, u32[]{:S(2)}) copy-start(f32[10,128]{1,0:T(8,128)} %get-tuple-element.102.refs_2_) | copy-start | bytes 15364
  5.0 6.7 %copy-start.1 = (bf16[256,2560]{1,0:T(8,128)(2,1)S(1)}, bf16[256,2560]{1,0:T(8,128)(2,1)}, u32[]{:S(2)}) copy-start(bf16[256,2560]{1,0:T(8,128)(2,1)} %refs_1_.13) | copy-start | bytes 3932164
  5.0 6.7 %copy-start.2 = (bf16[256,128]{1,0:T(8,128)(2,1)S(1)}, bf16[256,128]{1,0:T(8,128)(2,1)}, u32[]{:S(2)}) copy-start(bf16[256,128]{1,0:T(8,128)(2,1)} %refs_2_.13) | copy-start | bytes 196612
  5.0 6.6 %copy-start.3 = (bf16[256,128]{1,0:T(8,128)(2,1)S(1)}, bf16[256,128]{1,0:T(8,128)(2,1)}, u32[]{:S(2)}) copy-start(bf16[256,128]{1,0:T(8,128)(2,1)} %refs_3_.13) | copy-start | bytes 196612
  5.0 6.6 %copy-start.4 = (bf16[256,128]{1,0:T(8,128)(2,1)S(1)}, bf16[256,128]{1,0:T(8,128)(2,1)}, u32[]{:S(2)}) copy-start(bf16[256,128]{1,0:T(8,128)(2,1)} %get-tuple-element.98.refs_5_.refs_7_.refs_4_) | copy-start | bytes 196612
  5.0 6.6 %copy-start.5 = (bf16[256,128]{1,0:T(8,128)(2,1)S(1)}, bf16[256,128]{1,0:T(8,128)(2,1)}, u32[]{:S(2)}) copy-start(bf16[256,128]{1,0:T(8,128)(2,1)} %get-tuple-element.99.refs_6_.refs_8_.refs_5_) | copy-start | bytes 196612
  5.0 6.6 %copy-start.6 = (f32[256,128]{1,0:T(8,128)S(1)}, f32[256,128]{1,0:T(8,128)}, u32[]{:S(2)}) copy-start(f32[256,128]{1,0:T(8,128)} %get-tuple-element.107.refs_6_) | copy-start | bytes 393220
  5.0 6.6 %copy-start.9 = (f32[40,256]{1,0:T(8,128)S(1)}, f32[40,256]{1,0:T(8,128)}, u32[]{:S(2)}) copy-start(f32[40,256]{1,0:T(8,128)} %refs_5_.5) | copy-start | bytes 122884
  8.3 3.3 %copy-start = (bf16[256,2560]{1,0:T(8,128)(2,1)S(1)}, bf16[256,2560]{1,0:T(8,128)(2,1)}, u32[]{:S(2)}) copy-start(bf16[256,2560]{1,0:T(8,128)(2,1)} %refs_0_.7) | copy-start | bytes 3932164
  8.3 8.4 %collective-permute-start.2 = (f32[1288,128]{1,0:T(8,128)}, f32[1288,128]{1,0:T(8,128)S(1)}, u32[]{:S(2)}, u32[]{:S(2)}) collective-permute-start(f32[1288,128]{1,0:T(8,128)} %get-tuple-element.106), channel_id=1, source_target_pairs={{0,1},{1,0},{2,3},{3,2},{4,5},{5,4},{6,7},{7,6},{8,9},{9,8},{10,11... | collective-permute-start | bytes 1978376 | tf_op jit(solution)/shard_map/ppermute | solution.py:700
  8.5 11.2 %collective-permute-start.1 = (f32[656,128]{1,0:T(8,128)S(1)}, f32[656,128]{1,0:T(8,128)S(1)}, u32[]{:S(2)}, u32[]{:S(2)}) collective-permute-start(f32[656,128]{1,0:T(8,128)S(1)} %get-tuple-element.105.refs_0_.refs_1_), channel_id=1, source_target_pairs={{0,2},{1,3},{2,0},{3,1},{4,6},{5,7},{6,4},{7,5},{8,10},{9,11},{10,... | collective-permute-start | bytes 1007624 | tf_op jit(solution)/shard_map/ppermute | solution.py:700
  11.7 8.0 %copy-start.7 = (f32[1280,128]{1,0:T(8,128)S(1)}, f32[1280,128]{1,0:T(8,128)}, u32[]{:S(2)}) copy-start(f32[1280,128]{1,0:T(8,128)} %get-tuple-element.117.refs_1_) | copy-start | bytes 1966084
  11.7 8.0 %copy-start.11 = (f32[10,128]{1,0:T(8,128)S(1)}, f32[10,128]{1,0:T(8,128)}, u32[]{:S(2)}) copy-start(f32[10,128]{1,0:T(8,128)} %get-tuple-element.118.refs_2_) | copy-start | bytes 15364
  19.8 13.0 %collective-permute-start.4 = (f32[656,128]{1,0:T(8,128)S(1)}, f32[656,128]{1,0:T(8,128)S(1)}, u32[]{:S(2)}, u32[]{:S(2)}) collective-permute-start(f32[656,128]{1,0:T(8,128)S(1)} %get-tuple-element.119.refs_1_), channel_id=1, source_target_pairs={{0,2},{1,3},{2,0},{3,1},{4,6},{5,7},{6,4},{7,5},{8,10},{9,11},{10,... | collective-permute-start | bytes 1007624 | tf_op jit(solution)/shard_map/ppermute | solution.py:700
  21.8 10.0 %collective-permute-start.3 = (f32[336,128]{1,0:T(8,128)S(1)}, f32[336,128]{1,0:T(8,128)S(1)}, u32[]{:S(2)}, u32[]{:S(2)}) collective-permute-start(f32[336,128]{1,0:T(8,128)S(1)} %get-tuple-element.115.refs_0_.refs_1_), channel_id=1, source_target_pairs={{0,4},{1,5},{2,6},{3,7},{4,0},{5,1},{6,2},{7,3},{8,12},{9,13},{10,... | collective-permute-start | bytes 516104 | tf_op jit(solution)/shard_map/ppermute | solution.py:700
  33.0 12.6 %collective-permute-start.8 = (f32[336,128]{1,0:T(8,128)S(1)}, f32[336,128]{1,0:T(8,128)S(1)}, u32[]{:S(2)}, u32[]{:S(2)}) collective-permute-start(f32[336,128]{1,0:T(8,128)S(1)} %get-tuple-element.133.refs_1_), channel_id=1, source_target_pairs={{0,4},{1,5},{2,6},{3,7},{4,0},{5,1},{6,2},{7,3},{8,12},{9,13},{10,... | collective-permute-start | bytes 516104 | tf_op jit(solution)/shard_map/ppermute | solution.py:700
  35.6 8.3 %collective-permute-start.7 = (f32[328,128]{1,0:T(8,128)S(1)}, f32[328,128]{1,0:T(8,128)S(1)}, u32[]{:S(2)}, u32[]{:S(2)}) collective-permute-start(f32[328,128]{1,0:T(8,128)S(1)} %up.5.refs_0_), channel_id=1, source_target_pairs={{1,25},{3,27},{5,29},{7,31},{24,0},{26,2},{28,4},{30,6}} | collective-permute-start | bytes 503816 | tf_op jit(solution)/shard_map/ppermute | solution.py:700
  36.9 8.7 %collective-permute-start.6 = (f32[328,128]{1,0:T(8,128)S(1)}, f32[328,128]{1,0:T(8,128)S(1)}, u32[]{:S(2)}, u32[]{:S(2)}) collective-permute-start(f32[328,128]{1,0:T(8,128)S(1)} %up.5.refs_0_), channel_id=1, source_target_pairs={{1,17},{3,19},{5,21},{7,23},{9,25},{11,27},{13,29},{15,31},{16,0},... | collective-permute-start | bytes 503816 | tf_op jit(solution)/shard_map/ppermute | solution.py:700
  38.2 7.4 %collective-permute-start.5 = (f32[328,128]{1,0:T(8,128)S(1)}, f32[328,128]{1,0:T(8,128)S(1)}, u32[]{:S(2)}, u32[]{:S(2)}) collective-permute-start(f32[328,128]{1,0:T(8,128)S(1)} %up.5.refs_0_), channel_id=1, source_target_pairs={{1,9},{3,11},{5,13},{7,15},{8,0},{9,17},{10,2},{11,19},{12,4},{13,... | collective-permute-start | bytes 503816 | tf_op jit(solution)/shard_map/ppermute | solution.py:700
  45.9 8.8 %collective-permute-start.9 = (f32[336,128]{1,0:T(8,128)S(1)}, f32[336,128]{1,0:T(8,128)S(1)}, u32[]{:S(2)}, u32[]{:S(2)}) collective-permute-start(f32[336,128]{1,0:T(8,128)S(1)} %get-tuple-element.156), channel_id=1, source_target_pairs={{0,4},{1,5},{2,6},{3,7},{4,0},{5,1},{6,2},{7,3},{8,12},{9,13},{10,... | collective-permute-start | bytes 516104 | tf_op jit(solution)/shard_map/ppermute | solution.py:700
  46.9 8.3 %collective-permute-start.13 = (f32[328,128]{1,0:T(8,128)S(1)}, f32[328,128]{1,0:T(8,128)S(1)}, u32[]{:S(2)}, u32[]{:S(2)}) collective-permute-start(f32[328,128]{1,0:T(8,128)S(1)} %up.7), channel_id=1, source_target_pairs={{1,25},{3,27},{5,29},{7,31},{24,0},{26,2},{28,4},{30,6}} | collective-permute-start | bytes 503816 | tf_op jit(solution)/shard_map/ppermute | solution.py:700
  48.2 8.7 %collective-permute-start.12 = (f32[328,128]{1,0:T(8,128)S(1)}, f32[328,128]{1,0:T(8,128)S(1)}, u32[]{:S(2)}, u32[]{:S(2)}) collective-permute-start(f32[328,128]{1,0:T(8,128)S(1)} %up.7), channel_id=1, source_target_pairs={{1,17},{3,19},{5,21},{7,23},{9,25},{11,27},{13,29},{15,31},{16,0},... | collective-permute-start | bytes 503816 | tf_op jit(solution)/shard_map/ppermute | solution.py:700
  49.5 7.4 %collective-permute-start.11 = (f32[328,128]{1,0:T(8,128)S(1)}, f32[328,128]{1,0:T(8,128)S(1)}, u32[]{:S(2)}, u32[]{:S(2)}) collective-permute-start(f32[328,128]{1,0:T(8,128)S(1)} %up.7), channel_id=1, source_target_pairs={{1,9},{3,11},{5,13},{7,15},{8,0},{9,17},{10,2},{11,19},{12,4},{13,... | collective-permute-start | bytes 503816 | tf_op jit(solution)/shard_map/ppermute | solution.py:700
  54.9 10.7 %collective-permute-start.10 = (f32[656,128]{1,0:T(8,128)S(1)}, f32[656,128]{1,0:T(8,128)S(1)}, u32[]{:S(2)}, u32[]{:S(2)}) collective-permute-start(f32[656,128]{1,0:T(8,128)S(1)} %get-tuple-element.158), channel_id=1, source_target_pairs={{0,2},{1,3},{2,0},{3,1},{4,6},{5,7},{6,4},{7,5},{8,10},{9,11},{10,... | collective-permute-start | bytes 1007624 | tf_op jit(solution)/shard_map/ppermute | solution.py:700
  57.1 8.1 %collective-permute-start.14 = (f32[336,128]{1,0:T(8,128)S(1)}, f32[336,128]{1,0:T(8,128)S(1)}, u32[]{:S(2)}, u32[]{:S(2)}) collective-permute-start(f32[336,128]{1,0:T(8,128)S(1)} %get-tuple-element.161), channel_id=1, source_target_pairs={{0,4},{1,5},{2,6},{3,7},{4,0},{5,1},{6,2},{7,3},{8,12},{9,13},{10,... | collective-permute-start | bytes 516104 | tf_op jit(solution)/shard_map/ppermute | solution.py:700
  65.8 7.9 %collective-permute-start.17 = (f32[656,128]{1,0:T(8,128)S(1)}, f32[656,128]{1,0:T(8,128)S(1)}, u32[]{:S(2)}, u32[]{:S(2)}) collective-permute-start(f32[656,128]{1,0:T(8,128)S(1)} %get-tuple-element.173), channel_id=1, source_target_pairs={{0,2},{1,3},{2,0},{3,1},{4,6},{5,7},{6,4},{7,5},{8,10},{9,11},{10,... | collective-permute-start | bytes 1007624 | tf_op jit(solution)/shard_map/ppermute | solution.py:700
  67.9 1.7 %collective-permute-start.15 = (f32[640,128]{1,0:T(8,128)S(1)}, f32[640,128]{1,0:T(8,128)S(1)}, u32[]{:S(2)}, u32[]{:S(2)}) collective-permute-start(f32[640,128]{1,0:T(8,128)S(1)} %get-tuple-element.163.refs_4_), channel_id=1, source_target_pairs={{0,1},{1,0},{2,3},{3,2},{4,5},{5,4},{6,7},{7,6},{8,9},{9,8},{10,11... | collective-permute-start | bytes 983048 | tf_op jit(solution)/shard_map/ppermute | solution.py:700
  68.0 2.1 %collective-permute-start.16 = (f32[640,128]{1,0:T(8,128)S(1)}, f32[640,128]{1,0:T(8,128)S(1)}, u32[]{:S(2)}, u32[]{:S(2)}) collective-permute-start(f32[640,128]{1,0:T(8,128)S(1)} %get-tuple-element.164.refs_5_), channel_id=1, source_target_pairs={{0,1},{1,0},{2,3},{3,2},{4,5},{5,4},{6,7},{7,6},{8,9},{9,8},{10,11... | collective-permute-start | bytes 983048 | tf_op jit(solution)/shard_map/ppermute | solution.py:700
  68.5 5.2 %collective-permute-start.18 = (f32[640,128]{1,0:T(8,128)S(1)}, f32[640,128]{1,0:T(8,128)S(1)}, u32[]{:S(2)}, u32[]{:S(2)}) collective-permute-start(f32[640,128]{1,0:T(8,128)S(1)} %get-tuple-element.174.refs_4_), channel_id=1, source_target_pairs={{0,1},{1,0},{2,3},{3,2},{4,5},{5,4},{6,7},{7,6},{8,9},{9,8},{10,11... | collective-permute-start | bytes 983048 | tf_op jit(solution)/shard_map/ppermute | solution.py:700
  73.7 1.6 %collective-permute-start.19 = (f32[656,128]{1,0:T(8,128)S(1)}, f32[656,128]{1,0:T(8,128)S(1)}, u32[]{:S(2)}, u32[]{:S(2)}) collective-permute-start(f32[656,128]{1,0:T(8,128)S(1)} %collective-permute-done.17.refs_5_), channel_id=1, source_target_pairs={{0,1},{1,0},{2,3},{3,2},{4,5},{5,4},{6,7},{7,6},{8,9},{9,8},{10,11... | collective-permute-start | bytes 1007624 | tf_op jit(solution)/shard_map/ppermute | solution.py:700
  76.2 1.2 %collective-permute-start.20 = (f32[8,128]{1,0:T(8,128)S(1)}, f32[8,128]{1,0:T(8,128)S(1)}, u32[]{:S(2)}, u32[]{:S(2)}) collective-permute-start(f32[8,128]{1,0:T(8,128)S(1)} %get-tuple-element.183.total_ref), channel_id=1, source_target_pairs={{0,1},{1,0},{2,3},{3,2},{4,5},{5,4},{6,7},{7,6},{8,9},{9,8},{10,11... | collective-permute-start | bytes 12296 | tf_op jit(solution)/shard_map/ppermute | solution.py:700
  77.4 5.4 %collective-permute-start.23 = (f32[8,128]{1,0:T(8,128)S(1)}, f32[8,128]{1,0:T(8,128)S(1)}, u32[]{:S(2)}, u32[]{:S(2)}) collective-permute-start(f32[8,128]{1,0:T(8,128)S(1)} %get-tuple-element.184.after_ref.total_ref), channel_id=1, source_target_pairs={{0,6},{1,7},{2,4},{3,5},{4,2},{5,3},{6,0},{7,1},{8,14},{9,15},{10,... | collective-permute-start | bytes 12296 | tf_op jit(solution)/shard_map/ppermute | solution.py:700
  81.2 4.5 %collective-permute-start.22 = (f32[8,128]{1,0:T(8,128)S(1)}, f32[8,128]{1,0:T(8,128)S(1)}, u32[]{:S(2)}, u32[]{:S(2)}) collective-permute-start(f32[8,128]{1,0:T(8,128)S(1)} %get-tuple-element.184.after_ref.total_ref), channel_id=1, source_target_pairs={{0,4},{1,5},{2,6},{3,7},{4,0},{5,1},{6,2},{7,3},{8,12},{9,13},{10,... | collective-permute-start | bytes 12296 | tf_op jit(solution)/shard_map/ppermute | solution.py:700
  81.2 4.5 %collective-permute-start.21 = (f32[8,128]{1,0:T(8,128)S(1)}, f32[8,128]{1,0:T(8,128)S(1)}, u32[]{:S(2)}, u32[]{:S(2)}) collective-permute-start(f32[8,128]{1,0:T(8,128)S(1)} %get-tuple-element.184.after_ref.total_ref), channel_id=1, source_target_pairs={{0,2},{1,3},{2,0},{3,1},{4,6},{5,7},{6,4},{7,5},{8,10},{9,11},{10,... | collective-permute-start | bytes 12296 | tf_op jit(solution)/shard_map/ppermute | solution.py:700
  85.7 6.8 %collective-permute-start.26 = (f32[8,128]{1,0:T(8,128)S(1)}, f32[8,128]{1,0:T(8,128)S(1)}, u32[]{:S(2)}, u32[]{:S(2)}) collective-permute-start(f32[8,128]{1,0:T(8,128)S(1)} %get-tuple-element.186.refs_13_), channel_id=1, source_target_pairs={{24,0},{25,1},{26,2},{27,3},{28,4},{29,5},{30,6},{31,7}} | collective-permute-start | bytes 12296 | tf_op jit(solution)/shard_map/ppermute | solution.py:700
  87.0 5.5 %collective-permute-start.25 = (f32[8,128]{1,0:T(8,128)S(1)}, f32[8,128]{1,0:T(8,128)S(1)}, u32[]{:S(2)}, u32[]{:S(2)}) collective-permute-start(f32[8,128]{1,0:T(8,128)S(1)} %get-tuple-element.186.refs_13_), channel_id=1, source_target_pairs={{16,0},{17,1},{18,2},{19,3},{20,4},{21,5},{22,6},{23,7},{24,8},{25... | collective-permute-start | bytes 12296 | tf_op jit(solution)/shard_map/ppermute | solution.py:700
  88.3 5.5 %collective-permute-start.24 = (f32[8,128]{1,0:T(8,128)S(1)}, f32[8,128]{1,0:T(8,128)S(1)}, u32[]{:S(2)}, u32[]{:S(2)}) collective-permute-start(f32[8,128]{1,0:T(8,128)S(1)} %get-tuple-element.186.refs_13_), channel_id=1, source_target_pairs={{8,0},{9,1},{10,2},{11,3},{12,4},{13,5},{14,6},{15,7},{16,8},{17,9... | collective-permute-start | bytes 12296 | tf_op jit(solution)/shard_map/ppermute | solution.py:700
